TPU v7x, 256 devices: a whole 4x4x8 slice. The times are simulated.
256 devices in a mesh: tm: 16 (over z, core), blk: 16 (over y, x).
Axes of the slice: x: 4, y: 4, z: 8, core: 2. Of those that a mesh axis runs over, the one named last changes fastest.
Arguments:
- interior_inverse: bfloat16 [16, 2048, 2048], P('tm', 'blk'), may hold values from -1 to 2
- coupling: bfloat16 [16, 2048, 2048], P('tm', 'blk'), may hold values from -0.125 to 0.125
- separator: float32 [16, 2048, 2048], P('tm', 'blk'), may hold values from -1 to 5
- link: bfloat16 [16, 2048, 2048], P('tm', 'blk'), may hold values from -0.125 to 0.125
- source: float32 [16, 64, 2048], P('tm', None, 'blk'), may hold values from -3 to 3
- weights: float32 [16, 2048], P('tm', 'blk'), may hold values from 0.5 to 1.5
Outputs:
- schur: float32 [16, 2048, 2048], P('tm', 'blk')
- sweep: float32 [16, 64, 2048], P('tm', None, 'blk')
- residual: float32 [16, 64, 2048], P('tm', None, 'blk')
All inputs are finite; a program needn't handle non-finite values.
Results may differ from a plain program's by a relative error of at most 0.024.
Values may be sent and summed in bfloat16 or wider, within the bound.
No kernel may reach another device: no remote copies, remote signals or barrier semaphores. Data moves between devices by JAX's collectives and lax.ppermute only.
A program may use at most 128 MiB of HBM per device.

v0:
```python
import jax
import jax.numpy as jnp
from jax import lax
from jax.sharding import PartitionSpec as P


def from_behind(value, axis, steps):
    count = lax.axis_size(axis)
    first, last = (max(0, -steps), min(count, count - steps))
    return lax.ppermute(value, axis, [(source, source + steps) for source in range(first, last)])


def shards(interior_inverse, coupling, separator, link, source, weights):
    inverse_rows = interior_inverse[0]
    coupling_rows = coupling[0]
    separator_rows = separator[0]
    link_rows = link[0]
    source_rows = source[0]
    weight_rows = weights[0]
    row_count = coupling_rows.shape[0]
    key_count = source_rows.shape[0]
    highest = lax.Precision.HIGHEST
    inner_rows = jnp.dot(
        inverse_rows,
        lax.all_gather(coupling_rows, "blk", axis=0, tiled=True).T,
        preferred_element_type=jnp.float32,
    )
    schur_rows = separator_rows - jnp.dot(
        coupling_rows,
        lax.all_gather(inner_rows.astype(jnp.bfloat16), "blk", axis=0, tiled=True).astype(
            jnp.float32
        ),
        precision=highest,
        preferred_element_type=jnp.float32,
    )

    def add_link(segment):
        return jnp.dot(segment, link_rows.T, preferred_element_type=jnp.float32)

    def sweep_turn(turn_index, carried):
        rounded, current, product = carried
        previous = from_behind(rounded, "tm", 1)
        product = add_link(lax.all_gather(previous, "blk", axis=1, tiled=True))
        current = weight_rows[None, :] * (source_rows - product)
        return (current.astype(jnp.bfloat16), current, product)

    zero_state = jnp.zeros((key_count, row_count), jnp.float32)
    start_state = (zero_state.astype(jnp.bfloat16), zero_state, zero_state)
    rounded, current, product = lax.fori_loop(0, lax.axis_size("tm"), sweep_turn, start_state)
    own_terms = jnp.dot(
        lax.all_gather(rounded, "blk", axis=1, tiled=True),
        schur_rows.T,
        precision=highest,
        preferred_element_type=jnp.float32,
    )
    backward = lax.psum_scatter(
        jnp.dot(link_rows.T, rounded.T, preferred_element_type=jnp.float32).astype(jnp.bfloat16),
        "blk",
        scatter_dimension=0,
        tiled=True,
    ).astype(jnp.float32)
    following = from_behind(backward.T.astype(jnp.bfloat16), "tm", -1).astype(jnp.float32)
    residual = source_rows - own_terms - product - following
    return (schur_rows[None], current[None], residual[None])


def solution(mesh):
    in_specs = (
        P("tm", "blk", None),
        P("tm", "blk", None),
        P("tm", "blk", None),
        P("tm", "blk", None),
        P("tm", None, "blk"),
        P("tm", "blk"),
    )
    out_specs = (P("tm", "blk", None), P("tm", None, "blk"), P("tm", None, "blk"))
    return jax.shard_map(shards, mesh=mesh, in_specs=in_specs, out_specs=out_specs, check_vma=False)
```

profile of v0, /device:TPU:224, one launch (start us, length us, event | category | flops | bytes accessed | tf_op | source)
XLA Modules:
  0.0 675.5 jit_solution(15455990416318762849)
XLA Ops:
  8.0 477.5 %while.15 = (s32[]{:T(128)}, bf16[64,128]{1,0:T(8,128)(2,1)S(1)}, f32[64,128]{1,0:T(8,128)}, f32[64,128]{1,0:T(8,128)}, f32[1,128]{1,0:T(1,128)}, /*index=5*/bf1...) while((s32[]{:T(128)}, bf16[64,128]{1,0:T(8,128)(2,1)S(1)}, ...), condition=%wide.region_1.0_spmd.clone, body=%wide.region_0.0_spmd.clone.sunk | while | flops 33587200 | bytes 1278607 | solution.py:49
  8.0 2.1 collective-permute-start
  10.1 3.1 collective-permute-done
  13.2 24.9 %all_gather.17 = bf16[64,2048]{1,0:T(8,128)(2,1)S(1)} all-gather(bf16[64,128]{1,0:T(8,128)(2,1)S(1)} %collective-permute-done), channel_id=1, replica_groups=mesh['tm'=16,'blk'=16] {'blk'}, dimensions={1}, use_global_device_ids=true | all-gather | bytes 278528 | tf_op jit(solution)/shard_map/while/body/eval_jaxpr/all_gather | solution.py:43
  38.1 2.0 fusion.23
  40.1 1.9 collective-permute-start
  42.0 3.1 collective-permute-done
  45.1 24.5 %all_gather.17 = bf16[64,2048]{1,0:T(8,128)(2,1)S(1)} all-gather(bf16[64,128]{1,0:T(8,128)(2,1)S(1)} %collective-permute-done), channel_id=1, replica_groups=mesh['tm'=16,'blk'=16] {'blk'}, dimensions={1}, use_global_device_ids=true | all-gather | bytes 278528 | tf_op jit(solution)/shard_map/while/body/eval_jaxpr/all_gather | solution.py:43
  69.6 2.0 fusion.23
  71.6 1.9 collective-permute-start
  73.6 3.1 collective-permute-done
  76.7 21.9 %all_gather.17 = bf16[64,2048]{1,0:T(8,128)(2,1)S(1)} all-gather(bf16[64,128]{1,0:T(8,128)(2,1)S(1)} %collective-permute-done), channel_id=1, replica_groups=mesh['tm'=16,'blk'=16] {'blk'}, dimensions={1}, use_global_device_ids=true | all-gather | bytes 278528 | tf_op jit(solution)/shard_map/while/body/eval_jaxpr/all_gather | solution.py:43
  98.6 2.0 fusion.23
  100.6 1.9 collective-permute-start
  102.5 3.1 collective-permute-done
  105.6 23.2 %all_gather.17 = bf16[64,2048]{1,0:T(8,128)(2,1)S(1)} all-gather(bf16[64,128]{1,0:T(8,128)(2,1)S(1)} %collective-permute-done), channel_id=1, replica_groups=mesh['tm'=16,'blk'=16] {'blk'}, dimensions={1}, use_global_device_ids=true | all-gather | bytes 278528 | tf_op jit(solution)/shard_map/while/body/eval_jaxpr/all_gather | solution.py:43
  128.9 2.0 fusion.23
  130.9 1.9 collective-permute-start
  132.8 3.1 collective-permute-done
  135.9 21.8 %all_gather.17 = bf16[64,2048]{1,0:T(8,128)(2,1)S(1)} all-gather(bf16[64,128]{1,0:T(8,128)(2,1)S(1)} %collective-permute-done), channel_id=1, replica_groups=mesh['tm'=16,'blk'=16] {'blk'}, dimensions={1}, use_global_device_ids=true | all-gather | bytes 278528 | tf_op jit(solution)/shard_map/while/body/eval_jaxpr/all_gather | solution.py:43
  157.7 2.0 fusion.23
  159.7 1.9 collective-permute-start
  161.6 3.1 collective-permute-done
  164.7 23.2 %all_gather.17 = bf16[64,2048]{1,0:T(8,128)(2,1)S(1)} all-gather(bf16[64,128]{1,0:T(8,128)(2,1)S(1)} %collective-permute-done), channel_id=1, replica_groups=mesh['tm'=16,'blk'=16] {'blk'}, dimensions={1}, use_global_device_ids=true | all-gather | bytes 278528 | tf_op jit(solution)/shard_map/while/body/eval_jaxpr/all_gather | solution.py:43
  188.0 2.0 fusion.23
  190.0 1.9 collective-permute-start
  191.9 3.1 collective-permute-done
  195.0 21.8 %all_gather.17 = bf16[64,2048]{1,0:T(8,128)(2,1)S(1)} all-gather(bf16[64,128]{1,0:T(8,128)(2,1)S(1)} %collective-permute-done), channel_id=1, replica_groups=mesh['tm'=16,'blk'=16] {'blk'}, dimensions={1}, use_global_device_ids=true | all-gather | bytes 278528 | tf_op jit(solution)/shard_map/while/body/eval_jaxpr/all_gather | solution.py:43
  216.8 2.0 fusion.23
  218.8 1.9 collective-permute-start
  220.7 3.1 collective-permute-done
  223.8 23.3 %all_gather.17 = bf16[64,2048]{1,0:T(8,128)(2,1)S(1)} all-gather(bf16[64,128]{1,0:T(8,128)(2,1)S(1)} %collective-permute-done), channel_id=1, replica_groups=mesh['tm'=16,'blk'=16] {'blk'}, dimensions={1}, use_global_device_ids=true | all-gather | bytes 278528 | tf_op jit(solution)/shard_map/while/body/eval_jaxpr/all_gather | solution.py:43
  247.1 2.0 fusion.23
  249.1 1.9 collective-permute-start
  251.0 3.1 collective-permute-done
  254.1 21.8 %all_gather.17 = bf16[64,2048]{1,0:T(8,128)(2,1)S(1)} all-gather(bf16[64,128]{1,0:T(8,128)(2,1)S(1)} %collective-permute-done), channel_id=1, replica_groups=mesh['tm'=16,'blk'=16] {'blk'}, dimensions={1}, use_global_device_ids=true | all-gather | bytes 278528 | tf_op jit(solution)/shard_map/while/body/eval_jaxpr/all_gather | solution.py:43
  275.9 2.0 fusion.23
  279.8 3.1 collective-permute-done
  282.9 23.3 %all_gather.17 = bf16[64,2048]{1,0:T(8,128)(2,1)S(1)} all-gather(bf16[64,128]{1,0:T(8,128)(2,1)S(1)} %collective-permute-done), channel_id=1, replica_groups=mesh['tm'=16,'blk'=16] {'blk'}, dimensions={1}, use_global_device_ids=true | all-gather | bytes 278528 | tf_op jit(solution)/shard_map/while/body/eval_jaxpr/all_gather | solution.py:43
  306.2 2.0 fusion.23
  310.1 3.1 collective-permute-done
  313.2 21.8 %all_gather.17 = bf16[64,2048]{1,0:T(8,128)(2,1)S(1)} all-gather(bf16[64,128]{1,0:T(8,128)(2,1)S(1)} %collective-permute-done), channel_id=1, replica_groups=mesh['tm'=16,'blk'=16] {'blk'}, dimensions={1}, use_global_device_ids=true | all-gather | bytes 278528 | tf_op jit(solution)/shard_map/while/body/eval_jaxpr/all_gather | solution.py:43
  335.0 2.0 fusion.23
  338.9 3.1 collective-permute-done
  342.1 23.2 %all_gather.17 = bf16[64,2048]{1,0:T(8,128)(2,1)S(1)} all-gather(bf16[64,128]{1,0:T(8,128)(2,1)S(1)} %collective-permute-done), channel_id=1, replica_groups=mesh['tm'=16,'blk'=16] {'blk'}, dimensions={1}, use_global_device_ids=true | all-gather | bytes 278528 | tf_op jit(solution)/shard_map/while/body/eval_jaxpr/all_gather | solution.py:43
  365.3 2.0 fusion.23
  369.2 3.1 collective-permute-done
  372.4 21.8 %all_gather.17 = bf16[64,2048]{1,0:T(8,128)(2,1)S(1)} all-gather(bf16[64,128]{1,0:T(8,128)(2,1)S(1)} %collective-permute-done), channel_id=1, replica_groups=mesh['tm'=16,'blk'=16] {'blk'}, dimensions={1}, use_global_device_ids=true | all-gather | bytes 278528 | tf_op jit(solution)/shard_map/while/body/eval_jaxpr/all_gather | solution.py:43
  394.1 2.0 fusion.23
  398.0 3.1 collective-permute-done
  401.2 23.2 %all_gather.17 = bf16[64,2048]{1,0:T(8,128)(2,1)S(1)} all-gather(bf16[64,128]{1,0:T(8,128)(2,1)S(1)} %collective-permute-done), channel_id=1, replica_groups=mesh['tm'=16,'blk'=16] {'blk'}, dimensions={1}, use_global_device_ids=true | all-gather | bytes 278528 | tf_op jit(solution)/shard_map/while/body/eval_jaxpr/all_gather | solution.py:43
  424.4 2.0 fusion.23
  428.3 3.1 collective-permute-done
  431.5 21.8 %all_gather.17 = bf16[64,2048]{1,0:T(8,128)(2,1)S(1)} all-gather(bf16[64,128]{1,0:T(8,128)(2,1)S(1)} %collective-permute-done), channel_id=1, replica_groups=mesh['tm'=16,'blk'=16] {'blk'}, dimensions={1}, use_global_device_ids=true | all-gather | bytes 278528 | tf_op jit(solution)/shard_map/while/body/eval_jaxpr/all_gather | solution.py:43
  453.2 2.0 fusion.23
  457.1 3.1 collective-permute-done
  460.3 23.2 %all_gather.17 = bf16[64,2048]{1,0:T(8,128)(2,1)S(1)} all-gather(bf16[64,128]{1,0:T(8,128)(2,1)S(1)} %collective-permute-done), channel_id=1, replica_groups=mesh['tm'=16,'blk'=16] {'blk'}, dimensions={1}, use_global_device_ids=true | all-gather | bytes 278528 | tf_op jit(solution)/shard_map/while/body/eval_jaxpr/all_gather | solution.py:43
  483.5 2.0 fusion.23
  488.0 7.1 %fusion.3 = bf16[128,2048]{1,0:T(8,128)(2,1)} fusion(bf16[1,2048,2048]{2,1,0:T(8,128)(2,1)} %all-gather.6.cloned.1.call-done, bf16[1,128,2048]{2,1,0:T(8,128)(2,1)S(1)} %copy-done), kind=kOutput, calls=%fused_computation.6 | convolution fusion | flops 1074003968 | bytes 9437184 | tf_op jit(solution)/shard_map/dot_general | solution.py:23
  495.5 21.8 %all_gather.14 = bf16[64,2048]{1,0:T(8,128)(2,1)S(1)} all-gather(bf16[64,128]{1,0:T(8,128)(2,1)S(1)} %get-tuple-element.41), channel_id=1, replica_groups=mesh['tm'=16,'blk'=16] {'blk'}, dimensions={1}, use_global_device_ids=true | all-gather | bytes 278528 | tf_op jit(solution)/shard_map/all_gather | solution.py:51
  517.2 65.0 %reduce-scatter.4.cloned.1.call-done = bf16[128,64]{1,0:T(8,128)(2,1)} async-done(((bf16[2048,64]{1,0:T(8,128)(2,1)}), bf16[128,64]{1,0:T(8,128)(2,1)}) %reduce-scatter.4.cloned.1.call-update) | async-done | bytes 16400
  583.1 1.9 collective-permute-start.1
  585.0 75.7 %all-gather.4.cloned.1.call-done = bf16[2048,2048]{1,0:T(8,128)(2,1)} async-done(((bf16[128,2048]{1,0:T(8,128)(2,1)}), bf16[2048,2048]{1,0:T(8,128)(2,1)}) %all-gather.4.cloned.1.call-update) | async-done | bytes 8388624 | tf_op jit(solution)/shard_map/all_gather | solution.py:30
  660.8 5.8 fusion.2
  (50 shorter events, 20.3 us)
Async XLA Ops:
  7.2 480.8 %copy-start = (bf16[1,128,2048]{2,1,0:T(8,128)(2,1)S(1)}, bf16[1,128,2048]{2,1,0:T(8,128)(2,1)}, u32[]{:S(2)}) copy-start(bf16[1,128,2048]{2,1,0:T(8,128)(2,1)} %param.8) | copy-start | bytes 1572868
  7.2 480.8 %all-gather.6.cloned.1.call-start = ((), (), s32[]{:S(2)}) async-start(), calls=%async_computation.2 | async-start | bytes 8912896 | tf_op jit(solution)/shard_map/all_gather | solution.py:25
  7.9 574.3 %reduce-scatter.4.cloned.1.call-start = ((), (), s32[]{:S(2)}) async-start(), calls=%async_computation.3 | async-start | bytes 557056
  8.0 487.1 %copy-start.3 = (f32[1,128,2048]{2,1,0:T(8,128)S(1)}, f32[1,128,2048]{2,1,0:T(8,128)}, u32[]{:S(2)}) copy-start(f32[1,128,2048]{2,1,0:T(8,128)} %param.10) | copy-start | bytes 3145732
  8.0 5.2 collective-permute-start
  40.1 5.0 collective-permute-start
  71.6 5.0 collective-permute-start
  100.6 5.0 collective-permute-start
  130.9 5.0 collective-permute-start
  159.7 5.0 collective-permute-start
  190.0 5.0 collective-permute-start
  218.8 5.0 collective-permute-start
  249.1 5.0 collective-permute-start
  277.9 5.0 collective-permute-start
  308.2 5.0 collective-permute-start
  337.0 5.0 collective-permute-start
  367.3 5.0 collective-permute-start
  396.1 5.0 collective-permute-start
  426.4 5.0 collective-permute-start
  455.2 5.0 collective-permute-start
  485.5 175.2 %copy-start.1 = (bf16[1,128,2048]{2,1,0:T(8,128)(2,1)S(1)}, bf16[1,128,2048]{2,1,0:T(8,128)(2,1)}, u32[]{:S(2)}) copy-start(bf16[1,128,2048]{2,1,0:T(8,128)(2,1)} %param.9) | copy-start | bytes 1572868
  487.9 172.8 %all-gather.4.cloned.1.call-start = ((), (), s32[]{:S(2)}) async-start(), calls=%async_computation.1 | async-start | bytes 8912896 | tf_op jit(solution)/shard_map/all_gather | solution.py:30
  495.1 172.8 %copy-start.2 = (f32[64,128]{1,0:T(8,128)S(1)}, f32[64,128]{1,0:T(8,128)}, u32[]{:S(2)}) copy-start(f32[64,128]{1,0:T(8,128)} %get-tuple-element.172) | copy-start | bytes 98308
  495.1 172.7 %copy-start.4 = (f32[64,128]{1,0:T(8,128)S(1)}, f32[64,128]{1,0:T(8,128)}, u32[]{:S(2)}) copy-start(f32[64,128]{1,0:T(8,128)} %get-tuple-element.42) | copy-start | bytes 98308
  583.1 84.8 %collective-permute-start.1 = (bf16[64,128]{1,0:T(8,128)(2,1)S(1)}, bf16[64,128]{1,0:T(8,128)(2,1)S(1)}, u32[]{:S(2)}, u32[]{:S(2)}) collective-permute-start(bf16[64,128]{1,0:T(8,128)(2,1)S(1)} %bitcast.50), channel_id=1, source_target_pairs={{16,0},{32,16},{48,32},{64,48},{80,64},{96,80},{112,96},{128,112},... | collective-permute-start | bytes 49160 | tf_op jit(solution)/shard_map/ppermute | solution.py:10
Sparse Core Ops, SparseCore 0:
  10.4 78.2 all-gather.5
  488.0 94.1 reduce-scatter.3
  585.6 75.1 all-gather.3
where the time goes:
time: 680 us; the launch traced here: 676 us
  blocking collectives  386 us (57%)
  waiting for transfers between devices  192 us (28%)
  matrix products  47.2 us (7%)
  starting transfers between devices  32.7 us (5%)
  between operations  13.9 us (2%)
    all_gather x16, blocking collectives, sweep_turn(): product = add_link(lax.all_gather(previous, 'blk', axis=1, tiled=True))  365 us
    all_gather x1, waiting for transfers between devices, shards(): lax.all_gather(inner_rows.astype(jnp.bfloat16), 'blk', axis=0, tiled=True)  75.7 us
    unnamed x4, waiting for transfers between devices  65.7 us
    ppermute x17, waiting for transfers between devices, from_behind(): lax.ppermute(value, axis, [(source, source + steps) for source in range(f...  50.1 us
    ppermute x17, starting transfers between devices, from_behind(): lax.ppermute(value, axis, [(source, source + steps) for source in range(f...  32.6 us
    dot_general x16, matrix products, add_link(): return jnp.dot(segment, link_rows.T, preferred_element_type=jnp.float32)  31.9 us
    all_gather x1, blocking collectives, shards(): lax.all_gather(rounded, 'blk', axis=1, tiled=True)  21.8 us
  transfers between devices with their start and end apart: 20, of which 18 were waited for; matrix products, arithmetic and copies ran while one was open for 7% of the time, Pallas kernels for 0%

commit v1 on v0

v1 whole, which is shorter than its diff:
```python
import jax
import jax.numpy as jnp
from jax import lax
from jax.sharding import PartitionSpec as P

AXES = ("tm", "blk")
SIDE = 4


def moved(p, b, along_reduce, step):
    y, x = divmod(b, SIDE)
    if (p % 2 == 0) == along_reduce:
        x ^= step
    else:
        y ^= step
    return y * SIDE + x


def send(value, partitions, shift, along_reduce, step):
    plane = SIDE * SIDE
    pairs = [
        (p * plane + b, (p + shift) * plane + moved(p, b, along_reduce, step))
        for p in partitions
        for b in range(plane)
    ]
    return lax.ppermute(value, AXES, pairs)


def shards(interior_inverse, coupling, separator, link, source, weights):
    f32, bf16 = jnp.float32, jnp.bfloat16
    count = lax.axis_size("tm")
    everyone = range(count)
    inverse_rows, coupling_rows, separator_rows = interior_inverse[0], coupling[0], separator[0]
    source_rows, weight_row = source[0], weights[0]
    rows, nodes = link.shape[1:]
    keys = source_rows.shape[0]
    group = SIDE * rows
    p = lax.axis_index("tm")
    b = lax.axis_index("blk")
    y, x = b // SIDE, b % SIDE
    even = p % 2 == 0
    r = jnp.where(even, x, y)
    q = jnp.where(even, y, x)

    coupling_all = lax.all_gather(coupling_rows, "blk", axis=0, tiled=True)
    inverse_all = lax.all_gather(inverse_rows, "blk", axis=0, tiled=True)

    shaped = link[0].reshape(rows, SIDE, SIDE, rows)
    chunks = jnp.where(
        even,
        shaped.transpose(2, 0, 1, 3).reshape(SIDE, rows, group),
        shaped.transpose(1, 0, 2, 3).reshape(SIDE, rows, group),
    )
    high = weight_row.astype(bf16)
    rest = weight_row - high.astype(f32)
    middle = rest.astype(bf16)
    low = (rest - middle.astype(f32)).astype(bf16)
    packed = jnp.zeros((16, group), bf16)
    packed = packed.at[:3, :rows].set(jnp.stack([high, middle, low]))

    def chunk(step):
        part = lax.dynamic_index_in_dim(chunks, r ^ step, 0, keepdims=False)
        return jnp.concatenate([part, packed], axis=0)

    pieces = [chunk(0)]
    for step in range(1, SIDE):
        pieces.append(send(chunk(step), everyone, 0, True, step))
    pieces = jnp.stack(pieces)
    order = r ^ jnp.arange(SIDE)
    pieces = pieces[order]
    block = pieces[:, :rows].reshape(group, group)
    weight_group = pieces[:, rows : rows + 3, :rows].astype(f32).sum(axis=1).reshape(1, group)

    own = lax.dynamic_update_slice(
        jnp.zeros((keys, group), f32), weight_row[None, :] * source_rows, (0, r * rows)
    )

    message = own.astype(bf16)
    final = message
    for turn in range(1, count):
        parts = [send(message, [turn - 1], 1, True, step).astype(f32) for step in range(SIDE)]
        previous = (parts[0] + parts[1] + parts[2] + parts[3]).astype(bf16)
        product = lax.dot_general(
            previous, block, (((1,), (1,)), ((), ())), preferred_element_type=f32
        )
        message = (own - weight_group * product).astype(bf16)
        final = jnp.where(p == turn, message, final)

    total = final.astype(f32)
    for step in range(1, SIDE):
        total = total + send(final, everyone, 0, True, step).astype(f32)
    rounded = total.astype(bf16)
    sweep = lax.dynamic_slice(total, (0, r * rows), (keys, rows))

    back = jnp.dot(rounded, block, preferred_element_type=f32).astype(bf16)
    back = back.reshape(keys, SIDE, rows)
    following = jnp.zeros((keys, rows), f32)
    for step in range(SIDE):
        piece = lax.dynamic_index_in_dim(back, q ^ step, 1, keepdims=False)
        following = following + send(piece, range(1, count), -1, False, step).astype(f32)

    folded = jnp.dot(coupling_rows, inverse_all, preferred_element_type=f32).astype(bf16)
    schur_rows = separator_rows - lax.dot_general(
        folded, coupling_all, (((1,), (1,)), ((), ())), preferred_element_type=f32
    )
    columns = schur_rows.astype(bf16).reshape(rows, SIDE, SIDE, rows)
    columns = jnp.where(
        even,
        columns.reshape(rows, SIDE, group).transpose(1, 0, 2),
        columns.transpose(2, 0, 1, 3).reshape(SIDE, rows, group),
    )
    own_terms = jnp.zeros((keys, rows), f32)
    for step in range(SIDE):
        seen = rounded if step == 0 else send(rounded, everyone, 0, False, step)
        part = lax.dynamic_index_in_dim(columns, q ^ step, 0, keepdims=False)
        own_terms = own_terms + lax.dot_general(
            seen, part, (((1,), (1,)), ((), ())), preferred_element_type=f32
        )
    residual = sweep / weight_row[None, :] - own_terms - following
    return schur_rows[None], sweep[None], residual[None]


def solution(mesh):
    in_specs = (
        P("tm", "blk", None),
        P("tm", "blk", None),
        P("tm", "blk", None),
        P("tm", "blk", None),
        P("tm", None, "blk"),
        P("tm", "blk"),
    )
    out_specs = (P("tm", "blk", None), P("tm", None, "blk"), P("tm", None, "blk"))
    return jax.shard_map(shards, mesh=mesh, in_specs=in_specs, out_specs=out_specs, check_vma=False)
```

time: 680 us -> 561 us (0.82)
  starting transfers between devices: 32.7 us -> 503 us
  blocking collectives: 386 us -> 0 us
  waiting for transfers between devices: 192 us -> 16 us
  matrix products: 47.2 us -> 16.6 us
    ppermute x17 -> x73, starting transfers between devices: 32.6 us -> 502 us  [send(): return lax.ppermute(value, AXES, pairs)]
    all_gather x17 -> x0, blocking collectives: 386 us -> none  [the longest x16 365 us: sweep_turn(): product = add_link(lax.all_gather(previous, 'blk', axis=1, tiled=True))]
    all_gather x2, waiting for transfers between devices: 75.8 us -> 0.01 us  [the longest x1 0.01 us: shards(): coupling_all = lax.all_gather(coupling_rows, 'blk', axis=0, tiled=True)]
    unnamed x4 -> x2, waiting for transfers between devices: 65.7 us -> 1.38 us
    ppermute x17 -> x73, waiting for transfers between devices: 50.1 us -> 14.6 us  [send(): return lax.ppermute(value, AXES, pairs)]
    dot_general x20 -> x21, matrix products: 47.2 us -> 16.6 us  [the longest x1 10.8 us: shards(): lax.dot_general(folded, coupling_all, (((1,), (1,)), ((), ())), preferred...]
  transfers between devices with their start and end apart: 20 -> 75, of which waited for: 18 -> 7; matrix products, arithmetic and copies ran while one was open for 7% -> 4% of each run, Pallas kernels for 0% -> 0%
where the time goes in v1:
time: 561 us; the launch traced here: 556 us
  starting transfers between devices  503 us (90%)
  matrix products  16.6 us (3%)
  waiting for transfers between devices  16 us (3%)
  between operations  15.2 us (3%)
    ppermute x73, starting transfers between devices, send(): return lax.ppermute(value, AXES, pairs)  502 us
    ppermute x73, waiting for transfers between devices, send(): return lax.ppermute(value, AXES, pairs)  14.6 us
  transfers between devices with their start and end apart: 75, of which 7 were waited for; matrix products, arithmetic and copies ran while one was open for 4% of the time, Pallas kernels for 0%

profile of v1, /device:TPU:224, one launch (start us, length us, event | category | flops | bytes accessed | tf_op | source)
XLA Modules:
  0.0 556.2 jit_solution(2317026306751637825)
XLA Ops:
  7.2 0.7 all-gather.7.cloned.1.call-update
  7.9 0.7 all-gather.5.cloned.1.call-update
  8.7 0.8 fusion.64
  9.5 0.7 collective-permute-start.6
  10.2 0.7 collective-permute-start.5
  10.9 1.4 reshape_squeeze.3
  12.8 0.7 fusion.79
  13.7 2.8 collective-permute-start.2
  16.5 0.8 collective-permute-start.1
  17.9 2.9 collective-permute-done.2
  21.5 1.7 collective-permute-done.1
  25.0 0.8 collective-permute-start.10
  25.8 0.7 collective-permute-start.9
  26.4 0.7 collective-permute-start.8
  27.1 0.7 collective-permute-start.7
  28.8 0.7 collective-permute-start.13
  30.1 0.7 collective-permute-start.11
  31.8 0.7 collective-permute-start.17
  33.1 0.7 collective-permute-start.15
  34.8 0.7 collective-permute-start.21
  36.2 0.7 collective-permute-start.19
  46.2 51.8 %collective-permute-start.38 = (bf16[64,512]{1,0:T(8,128)(2,1)S(1)}, bf16[64,512]{1,0:T(8,128)(2,1)S(1)}, u32[]{:S(2)}, u32[]{:S(2)}) collective-permute-start(bf16[64,512]{1,0:T(8,128)(2,1)S(1)} %fusion.32), channel_id=1, source_target_pairs={{128,147},{129,146},{130,145},{131,144},{132,151},{133,150},{134,1... | collective-permute-start | bytes 196616 | tf_op jit(solution)/shard_map/ppermute | solution.py:26
  98.0 13.1 %collective-permute-start.37 = (bf16[64,512]{1,0:T(8,128)(2,1)S(1)}, bf16[64,512]{1,0:T(8,128)(2,1)S(1)}, u32[]{:S(2)}, u32[]{:S(2)}) collective-permute-start(bf16[64,512]{1,0:T(8,128)(2,1)S(1)} %fusion.32), channel_id=1, source_target_pairs={{128,146},{129,147},{130,144},{131,145},{132,150},{133,151},{134,1... | collective-permute-start | bytes 196616 | tf_op jit(solution)/shard_map/ppermute | solution.py:26
  111.1 13.1 %collective-permute-start.36 = (bf16[64,512]{1,0:T(8,128)(2,1)S(1)}, bf16[64,512]{1,0:T(8,128)(2,1)S(1)}, u32[]{:S(2)}, u32[]{:S(2)}) collective-permute-start(bf16[64,512]{1,0:T(8,128)(2,1)S(1)} %fusion.32), channel_id=1, source_target_pairs={{128,145},{129,144},{130,147},{131,146},{132,149},{133,148},{134,1... | collective-permute-start | bytes 196616 | tf_op jit(solution)/shard_map/ppermute | solution.py:26
  125.3 15.3 %collective-permute-start.42 = (bf16[64,512]{1,0:T(8,128)(2,1)S(1)}, bf16[64,512]{1,0:T(8,128)(2,1)S(1)}, u32[]{:S(2)}, u32[]{:S(2)}) collective-permute-start(bf16[64,512]{1,0:T(8,128)(2,1)S(1)} %fusion.33), channel_id=1, source_target_pairs={{144,172},{145,173},{146,174},{147,175},{148,168},{149,169},{150,1... | collective-permute-start | bytes 196616 | tf_op jit(solution)/shard_map/ppermute | solution.py:26
  140.5 12.9 %collective-permute-start.41 = (bf16[64,512]{1,0:T(8,128)(2,1)S(1)}, bf16[64,512]{1,0:T(8,128)(2,1)S(1)}, u32[]{:S(2)}, u32[]{:S(2)}) collective-permute-start(bf16[64,512]{1,0:T(8,128)(2,1)S(1)} %fusion.33), channel_id=1, source_target_pairs={{144,168},{145,169},{146,170},{147,171},{148,172},{149,173},{150,1... | collective-permute-start | bytes 196616 | tf_op jit(solution)/shard_map/ppermute | solution.py:26
  153.4 12.9 %collective-permute-start.40 = (bf16[64,512]{1,0:T(8,128)(2,1)S(1)}, bf16[64,512]{1,0:T(8,128)(2,1)S(1)}, u32[]{:S(2)}, u32[]{:S(2)}) collective-permute-start(bf16[64,512]{1,0:T(8,128)(2,1)S(1)} %fusion.33), channel_id=1, source_target_pairs={{144,164},{145,165},{146,166},{147,167},{148,160},{149,161},{150,1... | collective-permute-start | bytes 196616 | tf_op jit(solution)/shard_map/ppermute | solution.py:26
  166.3 12.9 %collective-permute-start.39 = (bf16[64,512]{1,0:T(8,128)(2,1)S(1)}, bf16[64,512]{1,0:T(8,128)(2,1)S(1)}, u32[]{:S(2)}, u32[]{:S(2)}) collective-permute-start(bf16[64,512]{1,0:T(8,128)(2,1)S(1)} %fusion.33), channel_id=1, source_target_pairs={{144,160},{145,161},{146,162},{147,163},{148,164},{149,165},{150,1... | collective-permute-start | bytes 196616 | tf_op jit(solution)/shard_map/ppermute | solution.py:26
  179.5 15.3 %collective-permute-start.46 = (bf16[64,512]{1,0:T(8,128)(2,1)S(1)}, bf16[64,512]{1,0:T(8,128)(2,1)S(1)}, u32[]{:S(2)}, u32[]{:S(2)}) collective-permute-start(bf16[64,512]{1,0:T(8,128)(2,1)S(1)} %fusion.34), channel_id=1, source_target_pairs={{160,179},{161,178},{162,177},{163,176},{164,183},{165,182},{166,1... | collective-permute-start | bytes 196616 | tf_op jit(solution)/shard_map/ppermute | solution.py:26
  194.8 12.5 %collective-permute-start.45 = (bf16[64,512]{1,0:T(8,128)(2,1)S(1)}, bf16[64,512]{1,0:T(8,128)(2,1)S(1)}, u32[]{:S(2)}, u32[]{:S(2)}) collective-permute-start(bf16[64,512]{1,0:T(8,128)(2,1)S(1)} %fusion.34), channel_id=1, source_target_pairs={{160,178},{161,179},{162,176},{163,177},{164,182},{165,183},{166,1... | collective-permute-start | bytes 196616 | tf_op jit(solution)/shard_map/ppermute | solution.py:26
  207.3 12.5 %collective-permute-start.44 = (bf16[64,512]{1,0:T(8,128)(2,1)S(1)}, bf16[64,512]{1,0:T(8,128)(2,1)S(1)}, u32[]{:S(2)}, u32[]{:S(2)}) collective-permute-start(bf16[64,512]{1,0:T(8,128)(2,1)S(1)} %fusion.34), channel_id=1, source_target_pairs={{160,177},{161,176},{162,179},{163,178},{164,181},{165,180},{166,1... | collective-permute-start | bytes 196616 | tf_op jit(solution)/shard_map/ppermute | solution.py:26
  219.8 12.5 %collective-permute-start.43 = (bf16[64,512]{1,0:T(8,128)(2,1)S(1)}, bf16[64,512]{1,0:T(8,128)(2,1)S(1)}, u32[]{:S(2)}, u32[]{:S(2)}) collective-permute-start(bf16[64,512]{1,0:T(8,128)(2,1)S(1)} %fusion.34), channel_id=1, source_target_pairs={{160,176},{161,177},{162,178},{163,179},{164,180},{165,181},{166,1... | collective-permute-start | bytes 196616 | tf_op jit(solution)/shard_map/ppermute | solution.py:26
  232.6 13.3 %collective-permute-start.50 = (bf16[64,512]{1,0:T(8,128)(2,1)S(1)}, bf16[64,512]{1,0:T(8,128)(2,1)S(1)}, u32[]{:S(2)}, u32[]{:S(2)}) collective-permute-start(bf16[64,512]{1,0:T(8,128)(2,1)S(1)} %fusion.35), channel_id=1, source_target_pairs={{176,204},{177,205},{178,206},{179,207},{180,200},{181,201},{182,2... | collective-permute-start | bytes 196616 | tf_op jit(solution)/shard_map/ppermute | solution.py:26
  246.0 12.5 %collective-permute-start.49 = (bf16[64,512]{1,0:T(8,128)(2,1)S(1)}, bf16[64,512]{1,0:T(8,128)(2,1)S(1)}, u32[]{:S(2)}, u32[]{:S(2)}) collective-permute-start(bf16[64,512]{1,0:T(8,128)(2,1)S(1)} %fusion.35), channel_id=1, source_target_pairs={{176,200},{177,201},{178,202},{179,203},{180,204},{181,205},{182,2... | collective-permute-start | bytes 196616 | tf_op jit(solution)/shard_map/ppermute | solution.py:26
  258.5 12.5 %collective-permute-start.48 = (bf16[64,512]{1,0:T(8,128)(2,1)S(1)}, bf16[64,512]{1,0:T(8,128)(2,1)S(1)}, u32[]{:S(2)}, u32[]{:S(2)}) collective-permute-start(bf16[64,512]{1,0:T(8,128)(2,1)S(1)} %fusion.35), channel_id=1, source_target_pairs={{176,196},{177,197},{178,198},{179,199},{180,192},{181,193},{182,1... | collective-permute-start | bytes 196616 | tf_op jit(solution)/shard_map/ppermute | solution.py:26
  270.9 12.5 %collective-permute-start.47 = (bf16[64,512]{1,0:T(8,128)(2,1)S(1)}, bf16[64,512]{1,0:T(8,128)(2,1)S(1)}, u32[]{:S(2)}, u32[]{:S(2)}) collective-permute-start(bf16[64,512]{1,0:T(8,128)(2,1)S(1)} %fusion.35), channel_id=1, source_target_pairs={{176,192},{177,193},{178,194},{179,195},{180,196},{181,197},{182,1... | collective-permute-start | bytes 196616 | tf_op jit(solution)/shard_map/ppermute | solution.py:26
  283.7 14.7 %collective-permute-start.54 = (bf16[64,512]{1,0:T(8,128)(2,1)S(1)}, bf16[64,512]{1,0:T(8,128)(2,1)S(1)}, u32[]{:S(2)}, u32[]{:S(2)}) collective-permute-start(bf16[64,512]{1,0:T(8,128)(2,1)S(1)} %fusion.36), channel_id=1, source_target_pairs={{192,211},{193,210},{194,209},{195,208},{196,215},{197,214},{198,2... | collective-permute-start | bytes 196616 | tf_op jit(solution)/shard_map/ppermute | solution.py:26
  298.4 12.5 %collective-permute-start.53 = (bf16[64,512]{1,0:T(8,128)(2,1)S(1)}, bf16[64,512]{1,0:T(8,128)(2,1)S(1)}, u32[]{:S(2)}, u32[]{:S(2)}) collective-permute-start(bf16[64,512]{1,0:T(8,128)(2,1)S(1)} %fusion.36), channel_id=1, source_target_pairs={{192,210},{193,211},{194,208},{195,209},{196,214},{197,215},{198,2... | collective-permute-start | bytes 196616 | tf_op jit(solution)/shard_map/ppermute | solution.py:26
  310.9 12.5 %collective-permute-start.52 = (bf16[64,512]{1,0:T(8,128)(2,1)S(1)}, bf16[64,512]{1,0:T(8,128)(2,1)S(1)}, u32[]{:S(2)}, u32[]{:S(2)}) collective-permute-start(bf16[64,512]{1,0:T(8,128)(2,1)S(1)} %fusion.36), channel_id=1, source_target_pairs={{192,209},{193,208},{194,211},{195,210},{196,213},{197,212},{198,2... | collective-permute-start | bytes 196616 | tf_op jit(solution)/shard_map/ppermute | solution.py:26
  323.4 12.5 %collective-permute-start.51 = (bf16[64,512]{1,0:T(8,128)(2,1)S(1)}, bf16[64,512]{1,0:T(8,128)(2,1)S(1)}, u32[]{:S(2)}, u32[]{:S(2)}) collective-permute-start(bf16[64,512]{1,0:T(8,128)(2,1)S(1)} %fusion.36), channel_id=1, source_target_pairs={{192,208},{193,209},{194,210},{195,211},{196,212},{197,213},{198,2... | collective-permute-start | bytes 196616 | tf_op jit(solution)/shard_map/ppermute | solution.py:26
  336.2 12.7 %collective-permute-start.58 = (bf16[64,512]{1,0:T(8,128)(2,1)S(1)}, bf16[64,512]{1,0:T(8,128)(2,1)S(1)}, u32[]{:S(2)}, u32[]{:S(2)}) collective-permute-start(bf16[64,512]{1,0:T(8,128)(2,1)S(1)} %fusion.37), channel_id=1, source_target_pairs={{208,236},{209,237},{210,238},{211,239},{212,232},{213,233},{214,2... | collective-permute-start | bytes 196616 | tf_op jit(solution)/shard_map/ppermute | solution.py:26
  348.9 12.5 %collective-permute-start.57 = (bf16[64,512]{1,0:T(8,128)(2,1)S(1)}, bf16[64,512]{1,0:T(8,128)(2,1)S(1)}, u32[]{:S(2)}, u32[]{:S(2)}) collective-permute-start(bf16[64,512]{1,0:T(8,128)(2,1)S(1)} %fusion.37), channel_id=1, source_target_pairs={{208,232},{209,233},{210,234},{211,235},{212,236},{213,237},{214,2... | collective-permute-start | bytes 196616 | tf_op jit(solution)/shard_map/ppermute | solution.py:26
  361.4 12.5 %collective-permute-start.56 = (bf16[64,512]{1,0:T(8,128)(2,1)S(1)}, bf16[64,512]{1,0:T(8,128)(2,1)S(1)}, u32[]{:S(2)}, u32[]{:S(2)}) collective-permute-start(bf16[64,512]{1,0:T(8,128)(2,1)S(1)} %fusion.37), channel_id=1, source_target_pairs={{208,228},{209,229},{210,230},{211,231},{212,224},{213,225},{214,2... | collective-permute-start | bytes 196616 | tf_op jit(solution)/shard_map/ppermute | solution.py:26
  373.8 12.5 %collective-permute-start.55 = (bf16[64,512]{1,0:T(8,128)(2,1)S(1)}, bf16[64,512]{1,0:T(8,128)(2,1)S(1)}, u32[]{:S(2)}, u32[]{:S(2)}) collective-permute-start(bf16[64,512]{1,0:T(8,128)(2,1)S(1)} %fusion.37), channel_id=1, source_target_pairs={{208,224},{209,225},{210,226},{211,227},{212,228},{213,229},{214,2... | collective-permute-start | bytes 196616 | tf_op jit(solution)/shard_map/ppermute | solution.py:26
  386.3 3.5 collective-permute-done.55
  390.1 11.2 %collective-permute-start.62 = (bf16[64,512]{1,0:T(8,128)(2,1)S(1)}, bf16[64,512]{1,0:T(8,128)(2,1)S(1)}, u32[]{:S(2)}, u32[]{:S(2)}) collective-permute-start(bf16[64,512]{1,0:T(8,128)(2,1)S(1)} %fusion.38), channel_id=1, source_target_pairs={{224,243},{225,242},{226,241},{227,240},{228,247},{229,246},{230,2... | collective-permute-start | bytes 196616 | tf_op jit(solution)/shard_map/ppermute | solution.py:26
  401.3 12.5 %collective-permute-start.61 = (bf16[64,512]{1,0:T(8,128)(2,1)S(1)}, bf16[64,512]{1,0:T(8,128)(2,1)S(1)}, u32[]{:S(2)}, u32[]{:S(2)}) collective-permute-start(bf16[64,512]{1,0:T(8,128)(2,1)S(1)} %fusion.38), channel_id=1, source_target_pairs={{224,242},{225,243},{226,240},{227,241},{228,246},{229,247},{230,2... | collective-permute-start | bytes 196616 | tf_op jit(solution)/shard_map/ppermute | solution.py:26
  413.8 12.5 %collective-permute-start.60 = (bf16[64,512]{1,0:T(8,128)(2,1)S(1)}, bf16[64,512]{1,0:T(8,128)(2,1)S(1)}, u32[]{:S(2)}, u32[]{:S(2)}) collective-permute-start(bf16[64,512]{1,0:T(8,128)(2,1)S(1)} %fusion.38), channel_id=1, source_target_pairs={{224,241},{225,240},{226,243},{227,242},{228,245},{229,244},{230,2... | collective-permute-start | bytes 196616 | tf_op jit(solution)/shard_map/ppermute | solution.py:26
  426.3 12.5 %collective-permute-start.59 = (bf16[64,512]{1,0:T(8,128)(2,1)S(1)}, bf16[64,512]{1,0:T(8,128)(2,1)S(1)}, u32[]{:S(2)}, u32[]{:S(2)}) collective-permute-start(bf16[64,512]{1,0:T(8,128)(2,1)S(1)} %fusion.38), channel_id=1, source_target_pairs={{224,240},{225,241},{226,242},{227,243},{228,244},{229,245},{230,2... | collective-permute-start | bytes 196616 | tf_op jit(solution)/shard_map/ppermute | solution.py:26
  438.8 0.8 collective-permute-done.59
  440.0 2.8 collective-permute-start.65
  442.8 0.8 collective-permute-start.64
  444.2 1.4 collective-permute-done.65
  445.5 3.0 collective-permute-done.64
  448.6 9.5 %collective-permute-start.68 = (bf16[64,512]{1,0:T(8,128)(2,1)S(1)}, bf16[64,512]{1,0:T(8,128)(2,1)S(1)}, u32[]{:S(2)}, u32[]{:S(2)}) collective-permute-start(bf16[64,512]{1,0:T(8,128)(2,1)S(1)} %get-tuple-element.15), channel_id=1, source_target_pairs={{0,12},{1,13},{2,14},{3,15},{4,8},{5,9},{6,10},{7,11},{8,4},{9,5},... | collective-permute-start | bytes 196616 | tf_op jit(solution)/shard_map/ppermute | solution.py:26
  458.1 11.8 %collective-permute-start.67 = (bf16[64,512]{1,0:T(8,128)(2,1)S(1)}, bf16[64,512]{1,0:T(8,128)(2,1)S(1)}, u32[]{:S(2)}, u32[]{:S(2)}) collective-permute-start(bf16[64,512]{1,0:T(8,128)(2,1)S(1)} %get-tuple-element.15), channel_id=1, source_target_pairs={{0,8},{1,9},{2,10},{3,11},{4,12},{5,13},{6,14},{7,15},{8,0},{9,1},... | collective-permute-start | bytes 196616 | tf_op jit(solution)/shard_map/ppermute | solution.py:26
  469.9 11.8 %collective-permute-start.66 = (bf16[64,512]{1,0:T(8,128)(2,1)S(1)}, bf16[64,512]{1,0:T(8,128)(2,1)S(1)}, u32[]{:S(2)}, u32[]{:S(2)}) collective-permute-start(bf16[64,512]{1,0:T(8,128)(2,1)S(1)} %get-tuple-element.15), channel_id=1, source_target_pairs={{0,4},{1,5},{2,6},{3,7},{4,0},{5,1},{6,2},{7,3},{8,12},{9,13},{10,... | collective-permute-start | bytes 196616 | tf_op jit(solution)/shard_map/ppermute | solution.py:26
  482.2 13.1 %collective-permute-start.72 = (bf16[64,128]{1,0:T(8,128)(2,1)S(1)}, bf16[64,128]{1,0:T(8,128)(2,1)S(1)}, u32[]{:S(2)}, u32[]{:S(2)}) collective-permute-start(bf16[64,128]{1,0:T(8,128)(2,1)S(1)} %bitcast.149), channel_id=1, source_target_pairs={{16,3},{17,2},{18,1},{19,0},{20,7},{21,6},{22,5},{23,4},{24,11},{2... | collective-permute-start | bytes 49160 | tf_op jit(solution)/shard_map/ppermute | solution.py:26
  495.3 13.1 %collective-permute-start.71 = (bf16[64,128]{1,0:T(8,128)(2,1)S(1)}, bf16[64,128]{1,0:T(8,128)(2,1)S(1)}, u32[]{:S(2)}, u32[]{:S(2)}) collective-permute-start(bf16[64,128]{1,0:T(8,128)(2,1)S(1)} %bitcast.150), channel_id=1, source_target_pairs={{16,2},{17,3},{18,0},{19,1},{20,6},{21,7},{22,4},{23,5},{24,10},{2... | collective-permute-start | bytes 49160 | tf_op jit(solution)/shard_map/ppermute | solution.py:26
  509.1 10.8 %fusion.80 = (bf16[128,2048]{1,0:T(8,128)(2,1)S(1)}, f32[128,2048]{1,0:T(8,128)}) fusion(bf16[1,2048,2048]{2,1,0:T(8,128)(2,1)} %all-gather.7.cloned.1.call-done, bf16[1,2048,2048]{2,1,0:T(8,128)(2,1)} %all-gather.5.cloned.1.call-done, bf16[1,128,2048]{2,1,0:T(8,128)(2,1)S(1)} %copy-done, f32[1,128,2048]{2,1,0:T(8,128)S(1)} %copy-done.1), kind=kOutput, calls=%fused_computation.134 | convolution fusion | flops 2148270080 | bytes 19922944 | tf_op jit(solution)/shard_map/dot_general | solution.py:103
  520.7 13.1 %collective-permute-start.70 = (bf16[64,128]{1,0:T(8,128)(2,1)S(1)}, bf16[64,128]{1,0:T(8,128)(2,1)S(1)}, u32[]{:S(2)}, u32[]{:S(2)}) collective-permute-start(bf16[64,128]{1,0:T(8,128)(2,1)S(1)} %bitcast.152), channel_id=1, source_target_pairs={{16,1},{17,0},{18,3},{19,2},{20,5},{21,4},{22,7},{23,6},{24,9},{25... | collective-permute-start | bytes 49160 | tf_op jit(solution)/shard_map/ppermute | solution.py:26
  534.0 13.1 %collective-permute-start.69 = (bf16[64,128]{1,0:T(8,128)(2,1)S(1)}, bf16[64,128]{1,0:T(8,128)(2,1)S(1)}, u32[]{:S(2)}, u32[]{:S(2)}) collective-permute-start(bf16[64,128]{1,0:T(8,128)(2,1)S(1)} %bitcast.151), channel_id=1, source_target_pairs={{16,0},{17,1},{18,2},{19,3},{20,4},{21,5},{22,6},{23,7},{24,8},{25... | collective-permute-start | bytes 49160 | tf_op jit(solution)/shard_map/ppermute | solution.py:26
  547.6 1.0 collective-permute-done.69
  548.6 0.8 subtract_bitcast_fusion
  (143 shorter events, 23.4 us)
Async XLA Ops:
  7.2 501.9 %all-gather.7.cloned.1.call-start = ((), (), s32[]{:S(2)}) async-start(), calls=%async_computation.1 | async-start | bytes 8912896 | tf_op jit(solution)/shard_map/all_gather | solution.py:45
  7.9 501.2 %all-gather.5.cloned.1.call-start = ((), (), s32[]{:S(2)}) async-start(), calls=%async_computation | async-start | bytes 8912896 | tf_op jit(solution)/shard_map/all_gather | solution.py:46
  9.5 15.1 %collective-permute-start.6 = (bf16[64,512]{1,0:T(8,128)(2,1)S(1)}, bf16[64,512]{1,0:T(8,128)(2,1)S(1)}, u32[]{:S(2)}, u32[]{:S(2)}) collective-permute-start(bf16[64,512]{1,0:T(8,128)(2,1)S(1)} %convert_element_type.343), channel_id=1, source_target_pairs={{0,19},{1,18},{2,17},{3,16},{4,23},{5,22},{6,21},{7,20},{8,27},{9,... | collective-permute-start | bytes 196616 | tf_op jit(solution)/shard_map/ppermute | solution.py:26
  10.2 14.5 %collective-permute-start.5 = (bf16[64,512]{1,0:T(8,128)(2,1)S(1)}, bf16[64,512]{1,0:T(8,128)(2,1)S(1)}, u32[]{:S(2)}, u32[]{:S(2)}) collective-permute-start(bf16[64,512]{1,0:T(8,128)(2,1)S(1)} %convert_element_type.343), channel_id=1, source_target_pairs={{0,18},{1,19},{2,16},{3,17},{4,22},{5,23},{6,20},{7,21},{8,26},{9,... | collective-permute-start | bytes 196616 | tf_op jit(solution)/shard_map/ppermute | solution.py:26
  13.7 7.1 %collective-permute-start.2 = (bf16[144,512]{1,0:T(8,128)(2,1)S(1)}, bf16[144,512]{1,0:T(8,128)(2,1)S(1)}, u32[]{:S(2)}, u32[]{:S(2)}) collective-permute-start(bf16[144,512]{1,0:T(8,128)(2,1)S(1)} %get-tuple-element.28), channel_id=1, source_target_pairs={{0,3},{1,2},{2,1},{3,0},{4,7},{5,6},{6,5},{7,4},{8,11},{9,10},{10,... | collective-permute-start | bytes 442376 | tf_op jit(solution)/shard_map/ppermute | solution.py:26
  16.5 6.6 %collective-permute-start.1 = (bf16[144,512]{1,0:T(8,128)(2,1)S(1)}, bf16[144,512]{1,0:T(8,128)(2,1)S(1)}, u32[]{:S(2)}, u32[]{:S(2)}) collective-permute-start(bf16[144,512]{1,0:T(8,128)(2,1)S(1)} %get-tuple-element.27), channel_id=1, source_target_pairs={{0,2},{1,3},{2,0},{3,1},{4,6},{5,7},{6,4},{7,5},{8,10},{9,11},{10,... | collective-permute-start | bytes 442376 | tf_op jit(solution)/shard_map/ppermute | solution.py:26
  17.3 6.5 %collective-permute-start = (bf16[144,512]{1,0:T(8,128)(2,1)S(1)}, bf16[144,512]{1,0:T(8,128)(2,1)S(1)}, u32[]{:S(2)}, u32[]{:S(2)}) collective-permute-start(bf16[144,512]{1,0:T(8,128)(2,1)S(1)} %get-tuple-element.26), channel_id=1, source_target_pairs={{0,1},{1,0},{2,3},{3,2},{4,5},{5,4},{6,7},{7,6},{8,9},{9,8},{10,11... | collective-permute-start | bytes 442376 | tf_op jit(solution)/shard_map/ppermute | solution.py:26
  20.8 3.8 collective-permute-start.4
  23.2 1.5 collective-permute-start.3
  25.0 2.8 collective-permute-start.10
  25.8 2.0 collective-permute-start.9
  26.4 1.4 collective-permute-start.8
  28.1 2.7 collective-permute-start.14
  28.8 2.0 collective-permute-start.13
  31.1 2.7 collective-permute-start.18
  31.8 2.0 collective-permute-start.17
  34.1 2.7 collective-permute-start.22
  34.8 2.0 collective-permute-start.21
  37.2 2.7 collective-permute-start.26
  37.8 2.0 collective-permute-start.25
  38.5 1.4 collective-permute-start.24
  40.2 2.7 collective-permute-start.30
  40.9 2.0 collective-permute-start.29
  41.5 1.4 collective-permute-start.28
  43.2 2.7 collective-permute-start.34
  43.9 2.0 collective-permute-start.33
  44.5 1.4 collective-permute-start.32
  46.2 78.7 %collective-permute-start.38 = (bf16[64,512]{1,0:T(8,128)(2,1)S(1)}, bf16[64,512]{1,0:T(8,128)(2,1)S(1)}, u32[]{:S(2)}, u32[]{:S(2)}) collective-permute-start(bf16[64,512]{1,0:T(8,128)(2,1)S(1)} %fusion.32), channel_id=1, source_target_pairs={{128,147},{129,146},{130,145},{131,144},{132,151},{133,150},{134,1... | collective-permute-start | bytes 196616 | tf_op jit(solution)/shard_map/ppermute | solution.py:26
  98.0 26.9 %collective-permute-start.37 = (bf16[64,512]{1,0:T(8,128)(2,1)S(1)}, bf16[64,512]{1,0:T(8,128)(2,1)S(1)}, u32[]{:S(2)}, u32[]{:S(2)}) collective-permute-start(bf16[64,512]{1,0:T(8,128)(2,1)S(1)} %fusion.32), channel_id=1, source_target_pairs={{128,146},{129,147},{130,144},{131,145},{132,150},{133,151},{134,1... | collective-permute-start | bytes 196616 | tf_op jit(solution)/shard_map/ppermute | solution.py:26
  111.1 13.8 %collective-permute-start.36 = (bf16[64,512]{1,0:T(8,128)(2,1)S(1)}, bf16[64,512]{1,0:T(8,128)(2,1)S(1)}, u32[]{:S(2)}, u32[]{:S(2)}) collective-permute-start(bf16[64,512]{1,0:T(8,128)(2,1)S(1)} %fusion.32), channel_id=1, source_target_pairs={{128,145},{129,144},{130,147},{131,146},{132,149},{133,148},{134,1... | collective-permute-start | bytes 196616 | tf_op jit(solution)/shard_map/ppermute | solution.py:26
  125.3 53.9 %collective-permute-start.42 = (bf16[64,512]{1,0:T(8,128)(2,1)S(1)}, bf16[64,512]{1,0:T(8,128)(2,1)S(1)}, u32[]{:S(2)}, u32[]{:S(2)}) collective-permute-start(bf16[64,512]{1,0:T(8,128)(2,1)S(1)} %fusion.33), channel_id=1, source_target_pairs={{144,172},{145,173},{146,174},{147,175},{148,168},{149,169},{150,1... | collective-permute-start | bytes 196616 | tf_op jit(solution)/shard_map/ppermute | solution.py:26
  140.5 38.7 %collective-permute-start.41 = (bf16[64,512]{1,0:T(8,128)(2,1)S(1)}, bf16[64,512]{1,0:T(8,128)(2,1)S(1)}, u32[]{:S(2)}, u32[]{:S(2)}) collective-permute-start(bf16[64,512]{1,0:T(8,128)(2,1)S(1)} %fusion.33), channel_id=1, source_target_pairs={{144,168},{145,169},{146,170},{147,171},{148,172},{149,173},{150,1... | collective-permute-start | bytes 196616 | tf_op jit(solution)/shard_map/ppermute | solution.py:26
  153.4 25.8 %collective-permute-start.40 = (bf16[64,512]{1,0:T(8,128)(2,1)S(1)}, bf16[64,512]{1,0:T(8,128)(2,1)S(1)}, u32[]{:S(2)}, u32[]{:S(2)}) collective-permute-start(bf16[64,512]{1,0:T(8,128)(2,1)S(1)} %fusion.33), channel_id=1, source_target_pairs={{144,164},{145,165},{146,166},{147,167},{148,160},{149,161},{150,1... | collective-permute-start | bytes 196616 | tf_op jit(solution)/shard_map/ppermute | solution.py:26
  166.3 12.9 %collective-permute-start.39 = (bf16[64,512]{1,0:T(8,128)(2,1)S(1)}, bf16[64,512]{1,0:T(8,128)(2,1)S(1)}, u32[]{:S(2)}, u32[]{:S(2)}) collective-permute-start(bf16[64,512]{1,0:T(8,128)(2,1)S(1)} %fusion.33), channel_id=1, source_target_pairs={{144,160},{145,161},{146,162},{147,163},{148,164},{149,165},{150,1... | collective-permute-start | bytes 196616 | tf_op jit(solution)/shard_map/ppermute | solution.py:26
  179.5 52.8 %collective-permute-start.46 = (bf16[64,512]{1,0:T(8,128)(2,1)S(1)}, bf16[64,512]{1,0:T(8,128)(2,1)S(1)}, u32[]{:S(2)}, u32[]{:S(2)}) collective-permute-start(bf16[64,512]{1,0:T(8,128)(2,1)S(1)} %fusion.34), channel_id=1, source_target_pairs={{160,179},{161,178},{162,177},{163,176},{164,183},{165,182},{166,1... | collective-permute-start | bytes 196616 | tf_op jit(solution)/shard_map/ppermute | solution.py:26
  194.8 37.5 %collective-permute-start.45 = (bf16[64,512]{1,0:T(8,128)(2,1)S(1)}, bf16[64,512]{1,0:T(8,128)(2,1)S(1)}, u32[]{:S(2)}, u32[]{:S(2)}) collective-permute-start(bf16[64,512]{1,0:T(8,128)(2,1)S(1)} %fusion.34), channel_id=1, source_target_pairs={{160,178},{161,179},{162,176},{163,177},{164,182},{165,183},{166,1... | collective-permute-start | bytes 196616 | tf_op jit(solution)/shard_map/ppermute | solution.py:26
  207.3 25.0 %collective-permute-start.44 = (bf16[64,512]{1,0:T(8,128)(2,1)S(1)}, bf16[64,512]{1,0:T(8,128)(2,1)S(1)}, u32[]{:S(2)}, u32[]{:S(2)}) collective-permute-start(bf16[64,512]{1,0:T(8,128)(2,1)S(1)} %fusion.34), channel_id=1, source_target_pairs={{160,177},{161,176},{162,179},{163,178},{164,181},{165,180},{166,1... | collective-permute-start | bytes 196616 | tf_op jit(solution)/shard_map/ppermute | solution.py:26
  219.8 12.5 %collective-permute-start.43 = (bf16[64,512]{1,0:T(8,128)(2,1)S(1)}, bf16[64,512]{1,0:T(8,128)(2,1)S(1)}, u32[]{:S(2)}, u32[]{:S(2)}) collective-permute-start(bf16[64,512]{1,0:T(8,128)(2,1)S(1)} %fusion.34), channel_id=1, source_target_pairs={{160,176},{161,177},{162,178},{163,179},{164,180},{165,181},{166,1... | collective-permute-start | bytes 196616 | tf_op jit(solution)/shard_map/ppermute | solution.py:26
  232.6 50.8 %collective-permute-start.50 = (bf16[64,512]{1,0:T(8,128)(2,1)S(1)}, bf16[64,512]{1,0:T(8,128)(2,1)S(1)}, u32[]{:S(2)}, u32[]{:S(2)}) collective-permute-start(bf16[64,512]{1,0:T(8,128)(2,1)S(1)} %fusion.35), channel_id=1, source_target_pairs={{176,204},{177,205},{178,206},{179,207},{180,200},{181,201},{182,2... | collective-permute-start | bytes 196616 | tf_op jit(solution)/shard_map/ppermute | solution.py:26
  246.0 37.4 %collective-permute-start.49 = (bf16[64,512]{1,0:T(8,128)(2,1)S(1)}, bf16[64,512]{1,0:T(8,128)(2,1)S(1)}, u32[]{:S(2)}, u32[]{:S(2)}) collective-permute-start(bf16[64,512]{1,0:T(8,128)(2,1)S(1)} %fusion.35), channel_id=1, source_target_pairs={{176,200},{177,201},{178,202},{179,203},{180,204},{181,205},{182,2... | collective-permute-start | bytes 196616 | tf_op jit(solution)/shard_map/ppermute | solution.py:26
  258.5 25.0 %collective-permute-start.48 = (bf16[64,512]{1,0:T(8,128)(2,1)S(1)}, bf16[64,512]{1,0:T(8,128)(2,1)S(1)}, u32[]{:S(2)}, u32[]{:S(2)}) collective-permute-start(bf16[64,512]{1,0:T(8,128)(2,1)S(1)} %fusion.35), channel_id=1, source_target_pairs={{176,196},{177,197},{178,198},{179,199},{180,192},{181,193},{182,1... | collective-permute-start | bytes 196616 | tf_op jit(solution)/shard_map/ppermute | solution.py:26
  270.9 12.5 %collective-permute-start.47 = (bf16[64,512]{1,0:T(8,128)(2,1)S(1)}, bf16[64,512]{1,0:T(8,128)(2,1)S(1)}, u32[]{:S(2)}, u32[]{:S(2)}) collective-permute-start(bf16[64,512]{1,0:T(8,128)(2,1)S(1)} %fusion.35), channel_id=1, source_target_pairs={{176,192},{177,193},{178,194},{179,195},{180,196},{181,197},{182,1... | collective-permute-start | bytes 196616 | tf_op jit(solution)/shard_map/ppermute | solution.py:26
  283.7 52.1 %collective-permute-start.54 = (bf16[64,512]{1,0:T(8,128)(2,1)S(1)}, bf16[64,512]{1,0:T(8,128)(2,1)S(1)}, u32[]{:S(2)}, u32[]{:S(2)}) collective-permute-start(bf16[64,512]{1,0:T(8,128)(2,1)S(1)} %fusion.36), channel_id=1, source_target_pairs={{192,211},{193,210},{194,209},{195,208},{196,215},{197,214},{198,2... | collective-permute-start | bytes 196616 | tf_op jit(solution)/shard_map/ppermute | solution.py:26
  298.4 37.4 %collective-permute-start.53 = (bf16[64,512]{1,0:T(8,128)(2,1)S(1)}, bf16[64,512]{1,0:T(8,128)(2,1)S(1)}, u32[]{:S(2)}, u32[]{:S(2)}) collective-permute-start(bf16[64,512]{1,0:T(8,128)(2,1)S(1)} %fusion.36), channel_id=1, source_target_pairs={{192,210},{193,211},{194,208},{195,209},{196,214},{197,215},{198,2... | collective-permute-start | bytes 196616 | tf_op jit(solution)/shard_map/ppermute | solution.py:26
  310.9 25.0 %collective-permute-start.52 = (bf16[64,512]{1,0:T(8,128)(2,1)S(1)}, bf16[64,512]{1,0:T(8,128)(2,1)S(1)}, u32[]{:S(2)}, u32[]{:S(2)}) collective-permute-start(bf16[64,512]{1,0:T(8,128)(2,1)S(1)} %fusion.36), channel_id=1, source_target_pairs={{192,209},{193,208},{194,211},{195,210},{196,213},{197,212},{198,2... | collective-permute-start | bytes 196616 | tf_op jit(solution)/shard_map/ppermute | solution.py:26
  323.4 12.5 %collective-permute-start.51 = (bf16[64,512]{1,0:T(8,128)(2,1)S(1)}, bf16[64,512]{1,0:T(8,128)(2,1)S(1)}, u32[]{:S(2)}, u32[]{:S(2)}) collective-permute-start(bf16[64,512]{1,0:T(8,128)(2,1)S(1)} %fusion.36), channel_id=1, source_target_pairs={{192,208},{193,209},{194,210},{195,211},{196,212},{197,213},{198,2... | collective-permute-start | bytes 196616 | tf_op jit(solution)/shard_map/ppermute | solution.py:26
  336.2 50.1 %collective-permute-start.58 = (bf16[64,512]{1,0:T(8,128)(2,1)S(1)}, bf16[64,512]{1,0:T(8,128)(2,1)S(1)}, u32[]{:S(2)}, u32[]{:S(2)}) collective-permute-start(bf16[64,512]{1,0:T(8,128)(2,1)S(1)} %fusion.37), channel_id=1, source_target_pairs={{208,236},{209,237},{210,238},{211,239},{212,232},{213,233},{214,2... | collective-permute-start | bytes 196616 | tf_op jit(solution)/shard_map/ppermute | solution.py:26
  348.9 37.4 %collective-permute-start.57 = (bf16[64,512]{1,0:T(8,128)(2,1)S(1)}, bf16[64,512]{1,0:T(8,128)(2,1)S(1)}, u32[]{:S(2)}, u32[]{:S(2)}) collective-permute-start(bf16[64,512]{1,0:T(8,128)(2,1)S(1)} %fusion.37), channel_id=1, source_target_pairs={{208,232},{209,233},{210,234},{211,235},{212,236},{213,237},{214,2... | collective-permute-start | bytes 196616 | tf_op jit(solution)/shard_map/ppermute | solution.py:26
  361.4 25.0 %collective-permute-start.56 = (bf16[64,512]{1,0:T(8,128)(2,1)S(1)}, bf16[64,512]{1,0:T(8,128)(2,1)S(1)}, u32[]{:S(2)}, u32[]{:S(2)}) collective-permute-start(bf16[64,512]{1,0:T(8,128)(2,1)S(1)} %fusion.37), channel_id=1, source_target_pairs={{208,228},{209,229},{210,230},{211,231},{212,224},{213,225},{214,2... | collective-permute-start | bytes 196616 | tf_op jit(solution)/shard_map/ppermute | solution.py:26
  373.8 16.0 %collective-permute-start.55 = (bf16[64,512]{1,0:T(8,128)(2,1)S(1)}, bf16[64,512]{1,0:T(8,128)(2,1)S(1)}, u32[]{:S(2)}, u32[]{:S(2)}) collective-permute-start(bf16[64,512]{1,0:T(8,128)(2,1)S(1)} %fusion.37), channel_id=1, source_target_pairs={{208,224},{209,225},{210,226},{211,227},{212,228},{213,229},{214,2... | collective-permute-start | bytes 196616 | tf_op jit(solution)/shard_map/ppermute | solution.py:26
  390.1 48.7 %collective-permute-start.62 = (bf16[64,512]{1,0:T(8,128)(2,1)S(1)}, bf16[64,512]{1,0:T(8,128)(2,1)S(1)}, u32[]{:S(2)}, u32[]{:S(2)}) collective-permute-start(bf16[64,512]{1,0:T(8,128)(2,1)S(1)} %fusion.38), channel_id=1, source_target_pairs={{224,243},{225,242},{226,241},{227,240},{228,247},{229,246},{230,2... | collective-permute-start | bytes 196616 | tf_op jit(solution)/shard_map/ppermute | solution.py:26
  401.3 37.5 %collective-permute-start.61 = (bf16[64,512]{1,0:T(8,128)(2,1)S(1)}, bf16[64,512]{1,0:T(8,128)(2,1)S(1)}, u32[]{:S(2)}, u32[]{:S(2)}) collective-permute-start(bf16[64,512]{1,0:T(8,128)(2,1)S(1)} %fusion.38), channel_id=1, source_target_pairs={{224,242},{225,243},{226,240},{227,241},{228,246},{229,247},{230,2... | collective-permute-start | bytes 196616 | tf_op jit(solution)/shard_map/ppermute | solution.py:26
  413.8 25.0 %collective-permute-start.60 = (bf16[64,512]{1,0:T(8,128)(2,1)S(1)}, bf16[64,512]{1,0:T(8,128)(2,1)S(1)}, u32[]{:S(2)}, u32[]{:S(2)}) collective-permute-start(bf16[64,512]{1,0:T(8,128)(2,1)S(1)} %fusion.38), channel_id=1, source_target_pairs={{224,241},{225,240},{226,243},{227,242},{228,245},{229,244},{230,2... | collective-permute-start | bytes 196616 | tf_op jit(solution)/shard_map/ppermute | solution.py:26
  426.3 13.4 %collective-permute-start.59 = (bf16[64,512]{1,0:T(8,128)(2,1)S(1)}, bf16[64,512]{1,0:T(8,128)(2,1)S(1)}, u32[]{:S(2)}, u32[]{:S(2)}) collective-permute-start(bf16[64,512]{1,0:T(8,128)(2,1)S(1)} %fusion.38), channel_id=1, source_target_pairs={{224,240},{225,241},{226,242},{227,243},{228,244},{229,245},{230,2... | collective-permute-start | bytes 196616 | tf_op jit(solution)/shard_map/ppermute | solution.py:26
  440.0 5.6 %collective-permute-start.65 = (bf16[64,512]{1,0:T(8,128)(2,1)S(1)}, bf16[64,512]{1,0:T(8,128)(2,1)S(1)}, u32[]{:S(2)}, u32[]{:S(2)}) collective-permute-start(bf16[64,512]{1,0:T(8,128)(2,1)S(1)} %fusion.40), channel_id=1, source_target_pairs={{0,3},{1,2},{2,1},{3,0},{4,7},{5,6},{6,5},{7,4},{8,11},{9,10},{10,... | collective-permute-start | bytes 196616 | tf_op jit(solution)/shard_map/ppermute | solution.py:26
  442.8 5.8 %collective-permute-start.64 = (bf16[64,512]{1,0:T(8,128)(2,1)S(1)}, bf16[64,512]{1,0:T(8,128)(2,1)S(1)}, u32[]{:S(2)}, u32[]{:S(2)}) collective-permute-start(bf16[64,512]{1,0:T(8,128)(2,1)S(1)} %fusion.40), channel_id=1, source_target_pairs={{0,2},{1,3},{2,0},{3,1},{4,6},{5,7},{6,4},{7,5},{8,10},{9,11},{10,... | collective-permute-start | bytes 196616 | tf_op jit(solution)/shard_map/ppermute | solution.py:26
  443.6 4.9 collective-permute-start.63
  448.6 72.1 %collective-permute-start.68 = (bf16[64,512]{1,0:T(8,128)(2,1)S(1)}, bf16[64,512]{1,0:T(8,128)(2,1)S(1)}, u32[]{:S(2)}, u32[]{:S(2)}) collective-permute-start(bf16[64,512]{1,0:T(8,128)(2,1)S(1)} %get-tuple-element.15), channel_id=1, source_target_pairs={{0,12},{1,13},{2,14},{3,15},{4,8},{5,9},{6,10},{7,11},{8,4},{9,5},... | collective-permute-start | bytes 196616 | tf_op jit(solution)/shard_map/ppermute | solution.py:26
  458.1 76.0 %collective-permute-start.67 = (bf16[64,512]{1,0:T(8,128)(2,1)S(1)}, bf16[64,512]{1,0:T(8,128)(2,1)S(1)}, u32[]{:S(2)}, u32[]{:S(2)}) collective-permute-start(bf16[64,512]{1,0:T(8,128)(2,1)S(1)} %get-tuple-element.15), channel_id=1, source_target_pairs={{0,8},{1,9},{2,10},{3,11},{4,12},{5,13},{6,14},{7,15},{8,0},{9,1},... | collective-permute-start | bytes 196616 | tf_op jit(solution)/shard_map/ppermute | solution.py:26
  469.9 77.4 %collective-permute-start.66 = (bf16[64,512]{1,0:T(8,128)(2,1)S(1)}, bf16[64,512]{1,0:T(8,128)(2,1)S(1)}, u32[]{:S(2)}, u32[]{:S(2)}) collective-permute-start(bf16[64,512]{1,0:T(8,128)(2,1)S(1)} %get-tuple-element.15), channel_id=1, source_target_pairs={{0,4},{1,5},{2,6},{3,7},{4,0},{5,1},{6,2},{7,3},{8,12},{9,13},{10,... | collective-permute-start | bytes 196616 | tf_op jit(solution)/shard_map/ppermute | solution.py:26
  482.2 65.4 %collective-permute-start.72 = (bf16[64,128]{1,0:T(8,128)(2,1)S(1)}, bf16[64,128]{1,0:T(8,128)(2,1)S(1)}, u32[]{:S(2)}, u32[]{:S(2)}) collective-permute-start(bf16[64,128]{1,0:T(8,128)(2,1)S(1)} %bitcast.149), channel_id=1, source_target_pairs={{16,3},{17,2},{18,1},{19,0},{20,7},{21,6},{22,5},{23,4},{24,11},{2... | collective-permute-start | bytes 49160 | tf_op jit(solution)/shard_map/ppermute | solution.py:26
  495.3 52.2 %collective-permute-start.71 = (bf16[64,128]{1,0:T(8,128)(2,1)S(1)}, bf16[64,128]{1,0:T(8,128)(2,1)S(1)}, u32[]{:S(2)}, u32[]{:S(2)}) collective-permute-start(bf16[64,128]{1,0:T(8,128)(2,1)S(1)} %bitcast.150), channel_id=1, source_target_pairs={{16,2},{17,3},{18,0},{19,1},{20,6},{21,7},{22,4},{23,5},{24,10},{2... | collective-permute-start | bytes 49160 | tf_op jit(solution)/shard_map/ppermute | solution.py:26
  520.7 26.8 %collective-permute-start.70 = (bf16[64,128]{1,0:T(8,128)(2,1)S(1)}, bf16[64,128]{1,0:T(8,128)(2,1)S(1)}, u32[]{:S(2)}, u32[]{:S(2)}) collective-permute-start(bf16[64,128]{1,0:T(8,128)(2,1)S(1)} %bitcast.152), channel_id=1, source_target_pairs={{16,1},{17,0},{18,3},{19,2},{20,5},{21,4},{22,7},{23,6},{24,9},{25... | collective-permute-start | bytes 49160 | tf_op jit(solution)/shard_map/ppermute | solution.py:26
  534.0 14.6 %collective-permute-start.69 = (bf16[64,128]{1,0:T(8,128)(2,1)S(1)}, bf16[64,128]{1,0:T(8,128)(2,1)S(1)}, u32[]{:S(2)}, u32[]{:S(2)}) collective-permute-start(bf16[64,128]{1,0:T(8,128)(2,1)S(1)} %bitcast.151), channel_id=1, source_target_pairs={{16,0},{17,1},{18,2},{19,3},{20,4},{21,5},{22,6},{23,7},{24,8},{25... | collective-permute-start | bytes 49160 | tf_op jit(solution)/shard_map/ppermute | solution.py:26
  (14 other events, 1017.6 us)
Sparse Core Ops, SparseCore 0:
  10.4 76.1 all-gather.6
  89.1 77.0 all-gather.4

commit v2 on v1

v2 whole, which is shorter than its diff:
```python
import jax
import jax.numpy as jnp
from jax import lax
from jax.sharding import PartitionSpec as P

AXES = ("tm", "blk")
SIDE = 4
PLANE = SIDE * SIDE


def moved(p, b, along_reduce, step):
    y, x = divmod(b, SIDE)
    if (p % 2 == 0) == along_reduce:
        x ^= step
    else:
        y ^= step
    return y * SIDE + x


def send(value, partitions, shift, along_reduce, step):
    pairs = [
        (p * PLANE + b, (p + shift) * PLANE + moved(p, b, along_reduce, step))
        for p in partitions
        for b in range(PLANE)
    ]
    return lax.ppermute(value, AXES, pairs)


def swap_cores(value, count):
    pairs = [(p * PLANE + b, (p ^ 1) * PLANE + b) for p in range(count) for b in range(PLANE)]
    return lax.ppermute(value, AXES, pairs)


def turn_messages(message, turn, count):
    last = turn - 1
    period = 4 if last % 2 == 0 else 8
    senders = range(last % period, count - 1, period)
    if last % 2 == 0:
        first = swap_cores(message, count)
    else:
        first = send(message, senders, 1, True, 0)
    return [send(message, senders, 1, True, step) for step in (2, 1, 3)] + [first]


def tie(values, *others):
    return lax.optimization_barrier((values, others))[0]


def shards(interior_inverse, coupling, separator, link, source, weights):
    f32, bf16 = jnp.float32, jnp.bfloat16
    count = lax.axis_size("tm")
    everyone = range(count)
    inverse_rows, coupling_rows, separator_rows = interior_inverse[0], coupling[0], separator[0]
    link_rows, source_rows, weight_row = link[0], source[0], weights[0]
    rows, nodes = link_rows.shape
    keys = source_rows.shape[0]
    group = SIDE * rows
    p = lax.axis_index("tm")
    b = lax.axis_index("blk")
    y, x = b // SIDE, b % SIDE
    even = p % 2 == 0
    r = jnp.where(even, x, y)
    q = jnp.where(even, y, x)

    def shard_at(place_q, place_r):
        return jnp.where(even, SIDE * place_q + place_r, SIDE * place_r + place_q)

    def strips(array, shard_indices):
        return jnp.concatenate(
            [lax.dynamic_slice(array, (0, s * rows), (array.shape[0], rows)) for s in shard_indices],
            axis=1,
        )

    def output_columns(array, place_q):
        return strips(array, [shard_at(place_q, j) for j in range(SIDE)])

    def input_columns(array, place_r):
        return strips(array, [shard_at(j, place_r) for j in range(SIDE)])

    def ordered(pieces, place):
        stacked = jnp.stack(pieces)
        return jnp.stack(
            [lax.dynamic_index_in_dim(stacked, place ^ k, 0, keepdims=False) for k in range(SIDE)]
        )

    def gathered(array, along_reduce):
        return [array] + [send(array, everyone, 0, along_reduce, step) for step in (1, 2, 3)]

    high = weight_row.astype(bf16)
    rest = weight_row - high.astype(f32)
    middle = rest.astype(bf16)
    low = (rest - middle.astype(f32)).astype(bf16)
    packed = jnp.zeros((16, group), bf16)
    packed = packed.at[:3, :rows].set(jnp.stack([high, middle, low]))

    def chunk(step):
        return jnp.concatenate([input_columns(link_rows, r ^ step), packed], axis=0)

    pieces = [chunk(0)] + [send(chunk(step), everyone, 0, True, step) for step in (1, 2, 3)]
    pieces = ordered(pieces, r)
    block = pieces[:, :rows].reshape(group, group)
    weight_group = pieces[:, rows : rows + 3, :rows].astype(f32).sum(axis=1).reshape(1, group)
    own = lax.dynamic_update_slice(
        jnp.zeros((keys, group), f32), weight_row[None, :] * source_rows, (0, r * rows)
    )
    block, own, weight_group = tie((block, own, weight_group))

    turned = strips(coupling_rows, [shard_at(q ^ k, j) for k in range(SIDE) for j in range(SIDE)])
    bulk_inverse, bulk_coupling, bulk_turned = tie((inverse_rows, coupling_rows, turned), block)
    inverse_out = gathered(bulk_inverse, True)
    coupling_in = gathered(bulk_coupling, False)
    coupling_out = gathered(bulk_turned, True)

    message = own.astype(bf16)
    final = message
    for turn in range(1, count):
        parts = [part.astype(f32) for part in turn_messages(message, turn, count)]
        previous = (parts[0] + parts[1] + parts[2] + parts[3]).astype(bf16)
        if turn == 5:
            inverse_out, coupling_in = tie((inverse_out, coupling_in), message)
            inner = lax.dot_general(
                jnp.concatenate(inverse_out),
                jnp.concatenate(coupling_in),
                (((1,), (1,)), ((), ())),
                preferred_element_type=f32,
            ).astype(bf16)
            inner = strips(inner, [q ^ k for k in range(SIDE)])
            inner_all = gathered(inner, False)
            previous = tie(previous, inner)
        if turn == 9:
            coupling_out, inner_all = tie((coupling_out, inner_all), message)
            inner_rows = jnp.concatenate(
                [
                    lax.dynamic_slice(piece, ((r ^ j) * rows, 0), (rows, group))
                    for piece in inner_all
                    for j in range(SIDE)
                ]
            )
            folded = jnp.dot(
                jnp.concatenate(coupling_out), inner_rows, preferred_element_type=f32
            ).astype(bf16)
            back_rows = [folded[:rows]] + [
                send(folded[step * rows : (step + 1) * rows], everyone, 0, True, step)
                for step in (1, 2, 3)
            ]
            previous = tie(previous, folded)
        if turn == 12:
            back_rows = tie(back_rows, message)
            placed = ordered(back_rows, r).reshape(SIDE, rows, SIDE, rows)
            product_rows = jnp.where(
                even, placed.transpose(1, 2, 0, 3), placed.transpose(1, 0, 2, 3)
            ).reshape(rows, nodes)
            schur_rows = separator_rows - product_rows.astype(f32)
            columns = strips(
                schur_rows.astype(bf16),
                [shard_at(q ^ k, j) for k in range(SIDE) for j in range(SIDE)],
            )
            previous = tie(previous, schur_rows, columns)
        product = lax.dot_general(
            previous, block, (((1,), (1,)), ((), ())), preferred_element_type=f32
        )
        message = (own - weight_group * product).astype(bf16)
        final = jnp.where(p == turn, message, final)

    total = final.astype(f32)
    for step in (2, 1, 3):
        total = total + send(final, everyone, 0, True, step).astype(f32)
    rounded = total.astype(bf16)
    sweep = lax.dynamic_slice(total, (0, r * rows), (keys, rows))

    back = jnp.dot(rounded, block, preferred_element_type=f32).astype(bf16)
    following = jnp.zeros((keys, rows), f32)
    for step in (2, 1, 3, 0):
        piece = lax.dynamic_slice(back, (0, (q ^ step) * rows), (keys, rows))
        following = following + send(piece, range(1, count), -1, False, step).astype(f32)

    own_terms = jnp.zeros((keys, rows), f32)
    for step, seen in enumerate(gathered(rounded, False)):
        own_terms = own_terms + lax.dot_general(
            seen,
            columns[:, step * group : (step + 1) * group],
            (((1,), (1,)), ((), ())),
            preferred_element_type=f32,
        )
    residual = sweep / weight_row[None, :] - own_terms - following
    return schur_rows[None], sweep[None], residual[None]


def solution(mesh):
    in_specs = (
        P("tm", "blk", None),
        P("tm", "blk", None),
        P("tm", "blk", None),
        P("tm", "blk", None),
        P("tm", None, "blk"),
        P("tm", "blk"),
    )
    out_specs = (P("tm", "blk", None), P("tm", None, "blk"), P("tm", None, "blk"))
    return jax.shard_map(shards, mesh=mesh, in_specs=in_specs, out_specs=out_specs, check_vma=False)
```

time: 561 us -> 224 us (0.40)
  starting transfers between devices: 503 us -> 107 us
  waiting for transfers between devices: 16 us -> 76.7 us
  local copies, waits for them, and re-layouts: 3.88 us -> 17.8 us
  between operations: 15.2 us -> 2.15 us
    ppermute x73 -> x80, starting transfers between devices: 502 us -> 103 us  [send(): return lax.ppermute(value, AXES, pairs)]
    ppermute x73 -> x80, waiting for transfers between devices: 14.6 us -> 74.9 us  [send(): return lax.ppermute(value, AXES, pairs)]
    unnamed x10 -> x82, local copies, waits for them, and re-layouts: 0.03 us -> 13.2 us
    dot_general x5 -> x6, matrix products: 12 us -> 6.76 us  [the longest x1 2.8 us: shards(): lax.dot_general(jnp.concatenate(inverse_out), jnp.concatenate(coupling_in...]
  transfers between devices with their start and end apart: 75 -> 88, of which waited for: 7 -> 22; matrix products, arithmetic and copies ran while one was open for 4% -> 9% of each run, Pallas kernels for 0% -> 0%
where the time goes in v2:
time: 224 us; the launch traced here: 222 us
  starting transfers between devices  107 us (48%)
  waiting for transfers between devices  76.7 us (34%)
  local copies, waits for them, and re-layouts  17.8 us (8%)
  matrix products  14.4 us (6%)
  other arithmetic  4.44 us (2%)
    ppermute x80, starting transfers between devices, send(): return lax.ppermute(value, AXES, pairs)  103 us
    ppermute x80, waiting for transfers between devices, send(): return lax.ppermute(value, AXES, pairs)  74.9 us
    unnamed x82, local copies, waits for them, and re-layouts  13.2 us
    dot_general x15, matrix products, shards(): lax.dot_general(previous, block, (((1,), (1,)), ((), ())), preferred_elem...  7.44 us
  transfers between devices with their start and end apart: 88, of which 22 were waited for; matrix products, arithmetic and copies ran while one was open for 9% of the time, Pallas kernels for 0%

profile of v2, /device:TPU:224, one launch (start us, length us, event | category | flops | bytes accessed | tf_op | source)
XLA Modules:
  0.0 222.2 jit_solution(5377658585070024571)
XLA Ops:
  1.6 1.2 dynamic-slice_bitcast_fusion.15
  2.8 1.6 collective-permute-start
  4.4 2.7 %collective-permute-start.1 = (bf16[144,512]{1,0:T(8,128)(2,1)S(1)}, bf16[144,512]{1,0:T(8,128)(2,1)S(1)}, u32[]{:S(2)}, u32[]{:S(2)}) collective-permute-start(bf16[144,512]{1,0:T(8,128)(2,1)S(1)} %get-tuple-element.134), channel_id=1, source_target_pairs={{0,2},{1,3},{2,0},{3,1},{4,6},{5,7},{6,4},{7,5},{8,10},{9,11},{10,... | collective-permute-start | bytes 442376 | tf_op jit(solution)/shard_map/ppermute | solution.py:26
  23.7 3.7 %collective-permute-start.20 = (bf16[64,512]{1,0:T(8,128)(2,1)S(1)}, bf16[64,512]{1,0:T(8,128)(2,1)S(1)}, u32[]{:S(2)}, u32[]{:S(2)}) collective-permute-start(bf16[64,512]{1,0:T(8,128)(2,1)S(1)} %fusion.47), channel_id=1, source_target_pairs={{32,50},{33,51},{34,48},{35,49},{36,54},{37,55},{38,52},{39,53},{4... | collective-permute-start | bytes 196616 | tf_op jit(solution)/shard_map/ppermute | solution.py:26
  27.4 1.3 collective-permute-start.21
  28.7 2.0 collective-permute-start.22
  31.4 3.2 %collective-permute-start.10 = (bf16[128,2048]{1,0:T(8,128)(2,1)S(1)}, bf16[128,2048]{1,0:T(8,128)(2,1)S(1)}, u32[]{:S(2)}, u32[]{:S(2)}) collective-permute-start(bf16[128,2048]{1,0:T(8,128)(2,1)S(1)} %bitcast.143), channel_id=1, source_target_pairs={{0,8},{1,9},{2,10},{3,11},{4,12},{5,13},{6,14},{7,15},{8,0},{9,1},... | collective-permute-start | bytes 1572872 | tf_op jit(solution)/shard_map/ppermute | solution.py:26
  40.1 1.6 collective-permute-start.11
  42.6 3.3 %collective-permute-start.7 = (bf16[128,2048]{1,0:T(8,128)(2,1)S(1)}, bf16[128,2048]{1,0:T(8,128)(2,1)}, u32[]{:S(2)}, u32[]{:S(2)}) collective-permute-start(bf16[128,2048]{1,0:T(8,128)(2,1)S(1)} %bitcast.172), channel_id=1, source_target_pairs={{0,2},{1,3},{2,0},{3,1},{4,6},{5,7},{6,4},{7,5},{8,10},{9,11},{10,... | collective-permute-start | bytes 1572872 | tf_op jit(solution)/shard_map/ppermute | solution.py:26
  46.6 7.3 %collective-permute-done.11 = bf16[128,2048]{1,0:T(8,128)(2,1)S(1)} collective-permute-done((bf16[128,2048]{1,0:T(8,128)(2,1)S(1)}, bf16[128,2048]{1,0:T(8,128)(2,1)S(1)}, u32[]{:S(2)}, u32[]{:S(2)}) %collective-permute-start.11) | collective-permute-done | bytes 524320 | tf_op jit(solution)/shard_map/ppermute | solution.py:26
  53.9 10.5 %collective-permute-done.7 = bf16[128,2048]{1,0:T(8,128)(2,1)} collective-permute-done((bf16[128,2048]{1,0:T(8,128)(2,1)S(1)}, bf16[128,2048]{1,0:T(8,128)(2,1)}, u32[]{:S(2)}, u32[]{:S(2)}) %collective-permute-start.7) | collective-permute-done | bytes 524320 | tf_op jit(solution)/shard_map/ppermute | solution.py:26
  64.4 2.8 %fusion.26 = bf16[512,512]{0,1:T(8,128)(2,1)S(1)} fusion(bf16[128,2048]{1,0:T(8,128)(2,1)S(1)} %collective-permute-done.11, bf16[128,2048]{1,0:T(8,128)(2,1)S(1)} %collective-permute-done.10, bf16[128,2048]{1,0:T(8,128)(2,1)} %collective-permute-done.9, bf16[128,2048]{1,0:T(8,128)(2,1)S(1)} %bitcast.146, bf16[128,2048]{1,0:T(8,128)(2,1)} %collective-permute-done.8, ...), kind=kOutput, calls=%fused_computation.24 | convolution fusion | flops 1090781184 | bytes 4718592 | tf_op jit(solution)/shard_map/dot_general | solution.py:121
  67.6 1.3 collective-permute-start.35
  68.9 1.3 collective-permute-start.36
  70.2 1.3 collective-permute-start.37
  71.5 1.3 collective-permute-start.38
  72.8 11.9 %collective-permute-done.35 = bf16[64,512]{1,0:T(8,128)(2,1)S(1)} collective-permute-done((bf16[64,512]{1,0:T(8,128)(2,1)S(1)}, bf16[64,512]{1,0:T(8,128)(2,1)S(1)}, u32[]{:S(2)}, u32[]{:S(2)}) %collective-permute-start.35) | collective-permute-done | bytes 65568 | tf_op jit(solution)/shard_map/ppermute | solution.py:26
  85.5 2.9 %collective-permute-done.37 = bf16[64,512]{1,0:T(8,128)(2,1)S(1)} collective-permute-done((bf16[64,512]{1,0:T(8,128)(2,1)S(1)}, bf16[64,512]{1,0:T(8,128)(2,1)S(1)}, u32[]{:S(2)}, u32[]{:S(2)}) %collective-permute-start.37) | collective-permute-done | bytes 65568 | tf_op jit(solution)/shard_map/ppermute | solution.py:26
  89.2 1.3 collective-permute-start.39
  90.5 1.3 collective-permute-start.40
  91.8 1.3 collective-permute-start.41
  100.3 2.3 %collective-permute-start.53 = (bf16[64,512]{1,0:T(8,128)(2,1)S(1)}, bf16[64,512]{1,0:T(8,128)(2,1)S(1)}, u32[]{:S(2)}, u32[]{:S(2)}) collective-permute-start(bf16[64,512]{1,0:T(8,128)(2,1)S(1)} %fusion.53), channel_id=1, source_target_pairs={{0,16},{1,17},{2,18},{3,19},{4,20},{5,21},{6,22},{7,23},{8,24},{9,... | collective-permute-start | bytes 196616 | tf_op jit(solution)/shard_map/ppermute | solution.py:31
  102.8 1.5 collective-permute-start.4
  104.4 2.1 collective-permute-start.5
  106.5 2.8 %collective-permute-start.29 = (bf16[512,512]{0,1:T(8,128)(2,1)S(1)}, bf16[512,512]{0,1:T(8,128)(2,1)S(1)}, u32[]{:S(2)}, u32[]{:S(2)}) collective-permute-start(bf16[512,512]{0,1:T(8,128)(2,1)S(1)} %pad_maximum_fusion.2), channel_id=1, source_target_pairs={{0,8},{1,9},{2,10},{3,11},{4,12},{5,13},{6,14},{7,15},{8,0},{9,1},... | collective-permute-start | bytes 1572872 | tf_op jit(solution)/shard_map/ppermute | solution.py:26
  109.3 1.9 collective-permute-start.30
  111.3 7.5 %collective-permute-done.4 = bf16[128,2048]{1,0:T(8,128)(2,1)} collective-permute-done((bf16[128,2048]{1,0:T(8,128)(2,1)}, bf16[128,2048]{1,0:T(8,128)(2,1)}, u32[]{:S(2)}, u32[]{:S(2)}) %collective-permute-start.4) | collective-permute-done | bytes 524320 | tf_op jit(solution)/shard_map/ppermute | solution.py:26
  118.8 11.0 %collective-permute-done.5 = bf16[128,2048]{1,0:T(8,128)(2,1)} collective-permute-done((bf16[128,2048]{1,0:T(8,128)(2,1)}, bf16[128,2048]{1,0:T(8,128)(2,1)}, u32[]{:S(2)}, u32[]{:S(2)}) %collective-permute-start.5) | collective-permute-done | bytes 524320 | tf_op jit(solution)/shard_map/ppermute | solution.py:26
  130.7 2.7 %fusion.23 = bf16[512,512]{1,0:T(8,128)(2,1)S(1)} fusion(bf16[2048,512]{0,1:T(8,128)(2,1)S(1)} %dynamic-slice_dynamic-update-slice_fusion, bf16[128,2048]{1,0:T(8,128)(2,1)} %collective-permute-done.5, bf16[128,2048]{1,0:T(8,128)(2,1)} %collective-permute-done.4, bf16[128,2048]{1,0:T(8,128)(2,1)S(1)} %copy-done.24, ...), kind=kOutput, calls=%fused_computation.23 | convolution fusion | flops 1082392576 | bytes 4718592 | tf_op jit(solution)/shard_map/dot_general | solution.py:139
  135.1 1.3 collective-permute-start.56
  136.4 1.3 collective-permute-start.57
  138.0 1.2 fusion.55
  139.2 3.8 %collective-permute-start.58 = (bf16[64,512]{1,0:T(8,128)(2,1)S(1)}, bf16[64,512]{1,0:T(8,128)(2,1)S(1)}, u32[]{:S(2)}, u32[]{:S(2)}) collective-permute-start(bf16[64,512]{1,0:T(8,128)(2,1)S(1)} %fusion.55), channel_id=1, source_target_pairs={{32,50},{33,51},{34,48},{35,49},{36,54},{37,55},{38,52},{39,53},{4... | collective-permute-start | bytes 196616 | tf_op jit(solution)/shard_map/ppermute | solution.py:26
  143.0 1.3 collective-permute-start.59
  144.3 2.3 %collective-permute-start.60 = (bf16[64,512]{1,0:T(8,128)(2,1)S(1)}, bf16[64,512]{1,0:T(8,128)(2,1)S(1)}, u32[]{:S(2)}, u32[]{:S(2)}) collective-permute-start(bf16[64,512]{1,0:T(8,128)(2,1)S(1)} %fusion.55), channel_id=1, source_target_pairs={{32,51},{33,50},{34,49},{35,48},{36,55},{37,54},{38,53},{39,52},{4... | collective-permute-start | bytes 196616 | tf_op jit(solution)/shard_map/ppermute | solution.py:26
  147.7 1.8 collective-permute-start.48
  149.5 2.0 collective-permute-start.49
  152.5 1.7 collective-permute-done.48
  154.2 1.5 collective-permute-done.49
  158.1 1.3 collective-permute-start.64
  159.4 1.3 collective-permute-start.65
  161.7 1.6 copy.16
  167.0 1.2 collective-permute-done.69
  168.5 1.3 collective-permute-start.70
  169.8 1.3 collective-permute-start.71
  171.1 1.3 collective-permute-start.72
  172.4 1.3 collective-permute-start.73
  173.7 8.6 %collective-permute-done.70 = bf16[64,512]{1,0:T(8,128)(2,1)S(1)} collective-permute-done((bf16[64,512]{1,0:T(8,128)(2,1)S(1)}, bf16[64,512]{1,0:T(8,128)(2,1)S(1)}, u32[]{:S(2)}, u32[]{:S(2)}) %collective-permute-start.70) | collective-permute-done | bytes 65568 | tf_op jit(solution)/shard_map/ppermute | solution.py:26
  182.3 3.0 %collective-permute-done.72 = bf16[64,512]{1,0:T(8,128)(2,1)S(1)} collective-permute-done((bf16[64,512]{1,0:T(8,128)(2,1)S(1)}, bf16[64,512]{1,0:T(8,128)(2,1)S(1)}, u32[]{:S(2)}, u32[]{:S(2)}) %collective-permute-start.72) | collective-permute-done | bytes 65568 | tf_op jit(solution)/shard_map/ppermute | solution.py:26
  186.5 1.9 collective-permute-start.74
  188.4 1.9 collective-permute-start.75
  190.3 1.9 collective-permute-start.76
  193.3 2.6 %copy.20 = f32[1,128,2048]{2,1,0:T(8,128)} copy(f32[1,128,2048]{1,2,0:T(8,128)} %sub.84) | data formatting | bytes 2097152
  196.0 1.3 fusion.61
  198.2 2.5 %collective-permute-start.79 = (bf16[64,512]{1,0:T(8,128)(2,1)S(1)}, bf16[64,512]{1,0:T(8,128)(2,1)S(1)}, u32[]{:S(2)}, u32[]{:S(2)}) collective-permute-start(bf16[64,512]{1,0:T(8,128)(2,1)S(1)} %fusion.61), channel_id=1, source_target_pairs={{0,1},{1,0},{2,3},{3,2},{4,5},{5,4},{6,7},{7,6},{8,9},{9,8},{10,11... | collective-permute-start | bytes 196616 | tf_op jit(solution)/shard_map/ppermute | solution.py:26
  201.7 1.6 collective-permute-done.78
  203.6 2.5 %collective-permute-done.80 = bf16[64,512]{1,0:T(8,128)(2,1)S(1)} collective-permute-done((bf16[64,512]{1,0:T(8,128)(2,1)S(1)}, bf16[64,512]{1,0:T(8,128)(2,1)S(1)}, u32[]{:S(2)}, u32[]{:S(2)}) %collective-permute-start.80) | collective-permute-done | bytes 65568 | tf_op jit(solution)/shard_map/ppermute | solution.py:26
  206.3 3.2 %collective-permute-start.82 = (bf16[64,512]{1,0:T(8,128)(2,1)S(1)}, bf16[64,512]{1,0:T(8,128)(2,1)S(1)}, u32[]{:S(2)}, u32[]{:S(2)}) collective-permute-start(bf16[64,512]{1,0:T(8,128)(2,1)S(1)} %get-tuple-element.76), channel_id=1, source_target_pairs={{0,8},{1,9},{2,10},{3,11},{4,12},{5,13},{6,14},{7,15},{8,0},{9,1},... | collective-permute-start | bytes 196616 | tf_op jit(solution)/shard_map/ppermute | solution.py:26
  209.5 1.5 collective-permute-start.83
  211.2 1.9 collective-permute-start.84
  213.2 1.9 collective-permute-start.85
  215.1 1.9 collective-permute-start.86
  217.2 1.9 collective-permute-start.87
  219.5 1.9 collective-permute-done.86
  (250 shorter events, 52.6 us)
Async XLA Ops:
  2.8 13.1 %collective-permute-start = (bf16[144,512]{1,0:T(8,128)(2,1)S(1)}, bf16[144,512]{1,0:T(8,128)(2,1)S(1)}, u32[]{:S(2)}, u32[]{:S(2)}) collective-permute-start(bf16[144,512]{1,0:T(8,128)(2,1)S(1)} %get-tuple-element.133), channel_id=1, source_target_pairs={{0,1},{1,0},{2,3},{3,2},{4,5},{5,4},{6,7},{7,6},{8,9},{9,8},{10,11... | collective-permute-start | bytes 442376 | tf_op jit(solution)/shard_map/ppermute | solution.py:26
  4.4 11.5 %collective-permute-start.1 = (bf16[144,512]{1,0:T(8,128)(2,1)S(1)}, bf16[144,512]{1,0:T(8,128)(2,1)S(1)}, u32[]{:S(2)}, u32[]{:S(2)}) collective-permute-start(bf16[144,512]{1,0:T(8,128)(2,1)S(1)} %get-tuple-element.134), channel_id=1, source_target_pairs={{0,2},{1,3},{2,0},{3,1},{4,6},{5,7},{6,4},{7,5},{8,10},{9,11},{10,... | collective-permute-start | bytes 442376 | tf_op jit(solution)/shard_map/ppermute | solution.py:26
  7.1 8.8 %collective-permute-start.2 = (bf16[144,512]{1,0:T(8,128)(2,1)S(1)}, bf16[144,512]{1,0:T(8,128)(2,1)S(1)}, u32[]{:S(2)}, u32[]{:S(2)}) collective-permute-start(bf16[144,512]{1,0:T(8,128)(2,1)S(1)} %pad_maximum_fusion.5), channel_id=1, source_target_pairs={{0,3},{1,2},{2,1},{3,0},{4,7},{5,6},{6,5},{7,4},{8,11},{9,10},{10,... | collective-permute-start | bytes 442376 | tf_op jit(solution)/shard_map/ppermute | solution.py:26
  20.0 3.3 %collective-permute-start.16 = (bf16[64,512]{1,0:T(8,128)(2,1)S(1)}, bf16[64,512]{1,0:T(8,128)(2,1)S(1)}, u32[]{:S(2)}, u32[]{:S(2)}) collective-permute-start(bf16[64,512]{1,0:T(8,128)(2,1)S(1)} %fusion.46), channel_id=1, source_target_pairs={{16,40},{17,41},{18,42},{19,43},{20,44},{21,45},{22,46},{23,47},{2... | collective-permute-start | bytes 196616 | tf_op jit(solution)/shard_map/ppermute | solution.py:26
  23.7 11.0 %collective-permute-start.20 = (bf16[64,512]{1,0:T(8,128)(2,1)S(1)}, bf16[64,512]{1,0:T(8,128)(2,1)S(1)}, u32[]{:S(2)}, u32[]{:S(2)}) collective-permute-start(bf16[64,512]{1,0:T(8,128)(2,1)S(1)} %fusion.47), channel_id=1, source_target_pairs={{32,50},{33,51},{34,48},{35,49},{36,54},{37,55},{38,52},{39,53},{4... | collective-permute-start | bytes 196616 | tf_op jit(solution)/shard_map/ppermute | solution.py:26
  27.4 7.2 %collective-permute-start.21 = (bf16[64,512]{1,0:T(8,128)(2,1)S(1)}, bf16[64,512]{1,0:T(8,128)(2,1)S(1)}, u32[]{:S(2)}, u32[]{:S(2)}) collective-permute-start(bf16[64,512]{1,0:T(8,128)(2,1)S(1)} %fusion.47), channel_id=1, source_target_pairs={{32,49},{33,48},{34,51},{35,50},{36,53},{37,52},{38,55},{39,54},{4... | collective-permute-start | bytes 196616 | tf_op jit(solution)/shard_map/ppermute | solution.py:26
  28.7 5.9 %collective-permute-start.22 = (bf16[64,512]{1,0:T(8,128)(2,1)S(1)}, bf16[64,512]{1,0:T(8,128)(2,1)S(1)}, u32[]{:S(2)}, u32[]{:S(2)}) collective-permute-start(bf16[64,512]{1,0:T(8,128)(2,1)S(1)} %fusion.47), channel_id=1, source_target_pairs={{32,51},{33,50},{34,49},{35,48},{36,55},{37,54},{38,53},{39,52},{4... | collective-permute-start | bytes 196616 | tf_op jit(solution)/shard_map/ppermute | solution.py:26
  30.7 3.9 %collective-permute-start.23 = (bf16[64,512]{1,0:T(8,128)(2,1)S(1)}, bf16[64,512]{1,0:T(8,128)(2,1)S(1)}, u32[]{:S(2)}, u32[]{:S(2)}) collective-permute-start(bf16[64,512]{1,0:T(8,128)(2,1)S(1)} %fusion.47), channel_id=1, source_target_pairs={{0,16},{1,17},{2,18},{3,19},{4,20},{5,21},{6,22},{7,23},{8,24},{9,... | collective-permute-start | bytes 196616 | tf_op jit(solution)/shard_map/ppermute | solution.py:31
  31.4 15.0 %collective-permute-start.10 = (bf16[128,2048]{1,0:T(8,128)(2,1)S(1)}, bf16[128,2048]{1,0:T(8,128)(2,1)S(1)}, u32[]{:S(2)}, u32[]{:S(2)}) collective-permute-start(bf16[128,2048]{1,0:T(8,128)(2,1)S(1)} %bitcast.143), channel_id=1, source_target_pairs={{0,8},{1,9},{2,10},{3,11},{4,12},{5,13},{6,14},{7,15},{8,0},{9,1},... | collective-permute-start | bytes 1572872 | tf_op jit(solution)/shard_map/ppermute | solution.py:26
  39.3 3.3 %collective-permute-start.33 = (bf16[64,512]{1,0:T(8,128)(2,1)S(1)}, bf16[64,512]{1,0:T(8,128)(2,1)S(1)}, u32[]{:S(2)}, u32[]{:S(2)}) collective-permute-start(bf16[64,512]{1,0:T(8,128)(2,1)S(1)} %fusion.49), channel_id=1, source_target_pairs={{0,19},{1,18},{2,17},{3,16},{4,23},{5,22},{6,21},{7,20},{8,27},{9,... | collective-permute-start | bytes 196616 | tf_op jit(solution)/shard_map/ppermute | solution.py:26
  40.0 5.9 %collective-permute-start.34 = (bf16[64,512]{1,0:T(8,128)(2,1)S(1)}, bf16[64,512]{1,0:T(8,128)(2,1)S(1)}, u32[]{:S(2)}, u32[]{:S(2)}) collective-permute-start(bf16[64,512]{1,0:T(8,128)(2,1)S(1)} %fusion.49), channel_id=1, source_target_pairs={{0,16},{1,17},{2,18},{3,19},{4,20},{5,21},{6,22},{7,23},{8,24},{9,... | collective-permute-start | bytes 196616 | tf_op jit(solution)/shard_map/ppermute | solution.py:31
  40.1 13.7 %collective-permute-start.11 = (bf16[128,2048]{1,0:T(8,128)(2,1)S(1)}, bf16[128,2048]{1,0:T(8,128)(2,1)S(1)}, u32[]{:S(2)}, u32[]{:S(2)}) collective-permute-start(bf16[128,2048]{1,0:T(8,128)(2,1)S(1)} %bitcast.144), channel_id=1, source_target_pairs={{0,12},{1,13},{2,14},{3,15},{4,8},{5,9},{6,10},{7,11},{8,4},{9,5},... | collective-permute-start | bytes 1572872 | tf_op jit(solution)/shard_map/ppermute | solution.py:26
  41.7 12.2 %collective-permute-start.6 = (bf16[128,2048]{1,0:T(8,128)(2,1)S(1)}, bf16[128,2048]{1,0:T(8,128)(2,1)}, u32[]{:S(2)}, u32[]{:S(2)}) collective-permute-start(bf16[128,2048]{1,0:T(8,128)(2,1)S(1)} %bitcast.171), channel_id=1, source_target_pairs={{0,1},{1,0},{2,3},{3,2},{4,5},{5,4},{6,7},{7,6},{8,9},{9,8},{10,11... | collective-permute-start | bytes 1572872 | tf_op jit(solution)/shard_map/ppermute | solution.py:26
  42.6 21.8 %collective-permute-start.7 = (bf16[128,2048]{1,0:T(8,128)(2,1)S(1)}, bf16[128,2048]{1,0:T(8,128)(2,1)}, u32[]{:S(2)}, u32[]{:S(2)}) collective-permute-start(bf16[128,2048]{1,0:T(8,128)(2,1)S(1)} %bitcast.172), channel_id=1, source_target_pairs={{0,2},{1,3},{2,0},{3,1},{4,6},{5,7},{6,4},{7,5},{8,10},{9,11},{10,... | collective-permute-start | bytes 1572872 | tf_op jit(solution)/shard_map/ppermute | solution.py:26
  45.9 18.5 %collective-permute-start.8 = (bf16[128,2048]{1,0:T(8,128)(2,1)S(1)}, bf16[128,2048]{1,0:T(8,128)(2,1)}, u32[]{:S(2)}, u32[]{:S(2)}) collective-permute-start(bf16[128,2048]{1,0:T(8,128)(2,1)S(1)} %bitcast.173), channel_id=1, source_target_pairs={{0,3},{1,2},{2,1},{3,0},{4,7},{5,6},{6,5},{7,4},{8,11},{9,10},{10,... | collective-permute-start | bytes 1572872 | tf_op jit(solution)/shard_map/ppermute | solution.py:26
  46.4 18.0 %collective-permute-start.9 = (bf16[128,2048]{1,0:T(8,128)(2,1)S(1)}, bf16[128,2048]{1,0:T(8,128)(2,1)}, u32[]{:S(2)}, u32[]{:S(2)}) collective-permute-start(bf16[128,2048]{1,0:T(8,128)(2,1)S(1)} %bitcast.145), channel_id=1, source_target_pairs={{0,4},{1,5},{2,6},{3,7},{4,0},{5,1},{6,2},{7,3},{8,12},{9,13},{10,... | collective-permute-start | bytes 1572872 | tf_op jit(solution)/shard_map/ppermute | solution.py:26
  67.6 17.1 %collective-permute-start.35 = (bf16[64,512]{1,0:T(8,128)(2,1)S(1)}, bf16[64,512]{1,0:T(8,128)(2,1)S(1)}, u32[]{:S(2)}, u32[]{:S(2)}) collective-permute-start(bf16[64,512]{1,0:T(8,128)(2,1)S(1)} %fusion.50), channel_id=1, source_target_pairs={{80,104},{81,105},{82,106},{83,107},{84,108},{85,109},{86,110},{87... | collective-permute-start | bytes 196616 | tf_op jit(solution)/shard_map/ppermute | solution.py:26
  68.9 16.6 %collective-permute-start.36 = (bf16[64,512]{1,0:T(8,128)(2,1)S(1)}, bf16[64,512]{1,0:T(8,128)(2,1)S(1)}, u32[]{:S(2)}, u32[]{:S(2)}) collective-permute-start(bf16[64,512]{1,0:T(8,128)(2,1)S(1)} %fusion.50), channel_id=1, source_target_pairs={{80,100},{81,101},{82,102},{83,103},{84,96},{85,97},{86,98},{87,99... | collective-permute-start | bytes 196616 | tf_op jit(solution)/shard_map/ppermute | solution.py:26
  70.2 18.2 %collective-permute-start.37 = (bf16[64,512]{1,0:T(8,128)(2,1)S(1)}, bf16[64,512]{1,0:T(8,128)(2,1)S(1)}, u32[]{:S(2)}, u32[]{:S(2)}) collective-permute-start(bf16[64,512]{1,0:T(8,128)(2,1)S(1)} %fusion.50), channel_id=1, source_target_pairs={{80,108},{81,109},{82,110},{83,111},{84,104},{85,105},{86,106},{87... | collective-permute-start | bytes 196616 | tf_op jit(solution)/shard_map/ppermute | solution.py:26
  71.5 17.4 %collective-permute-start.38 = (bf16[64,512]{1,0:T(8,128)(2,1)S(1)}, bf16[64,512]{1,0:T(8,128)(2,1)S(1)}, u32[]{:S(2)}, u32[]{:S(2)}) collective-permute-start(bf16[64,512]{1,0:T(8,128)(2,1)S(1)} %fusion.50), channel_id=1, source_target_pairs={{80,96},{81,97},{82,98},{83,99},{84,100},{85,101},{86,102},{87,103... | collective-permute-start | bytes 196616 | tf_op jit(solution)/shard_map/ppermute | solution.py:26
  89.2 5.2 %collective-permute-start.39 = (bf16[64,512]{1,0:T(8,128)(2,1)S(1)}, bf16[64,512]{1,0:T(8,128)(2,1)S(1)}, u32[]{:S(2)}, u32[]{:S(2)}) collective-permute-start(bf16[64,512]{1,0:T(8,128)(2,1)S(1)} %fusion.51), channel_id=1, source_target_pairs={{32,50},{33,51},{34,48},{35,49},{36,54},{37,55},{38,52},{39,53},{4... | collective-permute-start | bytes 196616 | tf_op jit(solution)/shard_map/ppermute | solution.py:26
  90.5 3.9 %collective-permute-start.40 = (bf16[64,512]{1,0:T(8,128)(2,1)S(1)}, bf16[64,512]{1,0:T(8,128)(2,1)S(1)}, u32[]{:S(2)}, u32[]{:S(2)}) collective-permute-start(bf16[64,512]{1,0:T(8,128)(2,1)S(1)} %fusion.51), channel_id=1, source_target_pairs={{32,49},{33,48},{34,51},{35,50},{36,53},{37,52},{38,55},{39,54},{4... | collective-permute-start | bytes 196616 | tf_op jit(solution)/shard_map/ppermute | solution.py:26
  91.8 3.2 %collective-permute-start.41 = (bf16[64,512]{1,0:T(8,128)(2,1)S(1)}, bf16[64,512]{1,0:T(8,128)(2,1)S(1)}, u32[]{:S(2)}, u32[]{:S(2)}) collective-permute-start(bf16[64,512]{1,0:T(8,128)(2,1)S(1)} %fusion.51), channel_id=1, source_target_pairs={{32,51},{33,50},{34,49},{35,48},{36,55},{37,54},{38,53},{39,52},{4... | collective-permute-start | bytes 196616 | tf_op jit(solution)/shard_map/ppermute | solution.py:26
  93.4 9.5 %collective-permute-start.3 = (bf16[128,2048]{1,0:T(8,128)(2,1)}, bf16[128,2048]{1,0:T(8,128)(2,1)S(1)}, u32[]{:S(2)}, u32[]{:S(2)}) collective-permute-start(bf16[128,2048]{1,0:T(8,128)(2,1)} %constant_dynamic-update-slice_fusion), channel_id=1, source_target_pairs={{0,1},{1,0},{2,3},{3,2},{4,5},{5,4},{6,7},{7,6},{8,9},{9,8},{10,11... | collective-permute-start | bytes 1572872 | tf_op jit(solution)/shard_map/ppermute | solution.py:26
  98.3 6.1 %collective-permute-start.50 = (bf16[64,512]{1,0:T(8,128)(2,1)S(1)}, bf16[64,512]{1,0:T(8,128)(2,1)S(1)}, u32[]{:S(2)}, u32[]{:S(2)}) collective-permute-start(bf16[64,512]{1,0:T(8,128)(2,1)S(1)} %fusion.53), channel_id=1, source_target_pairs={{0,18},{1,19},{2,16},{3,17},{4,22},{5,23},{6,20},{7,21},{8,26},{9,... | collective-permute-start | bytes 196616 | tf_op jit(solution)/shard_map/ppermute | solution.py:26
  99.0 7.5 %collective-permute-start.51 = (bf16[64,512]{1,0:T(8,128)(2,1)S(1)}, bf16[64,512]{1,0:T(8,128)(2,1)S(1)}, u32[]{:S(2)}, u32[]{:S(2)}) collective-permute-start(bf16[64,512]{1,0:T(8,128)(2,1)S(1)} %fusion.53), channel_id=1, source_target_pairs={{0,17},{1,16},{2,19},{3,18},{4,21},{5,20},{6,23},{7,22},{8,25},{9,... | collective-permute-start | bytes 196616 | tf_op jit(solution)/shard_map/ppermute | solution.py:26
  99.6 6.8 %collective-permute-start.52 = (bf16[64,512]{1,0:T(8,128)(2,1)S(1)}, bf16[64,512]{1,0:T(8,128)(2,1)S(1)}, u32[]{:S(2)}, u32[]{:S(2)}) collective-permute-start(bf16[64,512]{1,0:T(8,128)(2,1)S(1)} %fusion.53), channel_id=1, source_target_pairs={{0,19},{1,18},{2,17},{3,16},{4,23},{5,22},{6,21},{7,20},{8,27},{9,... | collective-permute-start | bytes 196616 | tf_op jit(solution)/shard_map/ppermute | solution.py:26
  100.3 9.0 %collective-permute-start.53 = (bf16[64,512]{1,0:T(8,128)(2,1)S(1)}, bf16[64,512]{1,0:T(8,128)(2,1)S(1)}, u32[]{:S(2)}, u32[]{:S(2)}) collective-permute-start(bf16[64,512]{1,0:T(8,128)(2,1)S(1)} %fusion.53), channel_id=1, source_target_pairs={{0,16},{1,17},{2,18},{3,19},{4,20},{5,21},{6,22},{7,23},{8,24},{9,... | collective-permute-start | bytes 196616 | tf_op jit(solution)/shard_map/ppermute | solution.py:31
  102.8 16.0 %collective-permute-start.4 = (bf16[128,2048]{1,0:T(8,128)(2,1)}, bf16[128,2048]{1,0:T(8,128)(2,1)}, u32[]{:S(2)}, u32[]{:S(2)}) collective-permute-start(bf16[128,2048]{1,0:T(8,128)(2,1)} %constant_dynamic-update-slice_fusion), channel_id=1, source_target_pairs={{0,2},{1,3},{2,0},{3,1},{4,6},{5,7},{6,4},{7,5},{8,10},{9,11},{10,... | collective-permute-start | bytes 1572872 | tf_op jit(solution)/shard_map/ppermute | solution.py:26
  104.4 25.4 %collective-permute-start.5 = (bf16[128,2048]{1,0:T(8,128)(2,1)}, bf16[128,2048]{1,0:T(8,128)(2,1)}, u32[]{:S(2)}, u32[]{:S(2)}) collective-permute-start(bf16[128,2048]{1,0:T(8,128)(2,1)} %constant_dynamic-update-slice_fusion), channel_id=1, source_target_pairs={{0,3},{1,2},{2,1},{3,0},{4,7},{5,6},{6,5},{7,4},{8,11},{9,10},{10,... | collective-permute-start | bytes 1572872 | tf_op jit(solution)/shard_map/ppermute | solution.py:26
  106.5 23.3 %collective-permute-start.28 = (bf16[512,512]{0,1:T(8,128)(2,1)S(1)}, bf16[512,512]{0,1:T(8,128)(2,1)S(1)}, u32[]{:S(2)}, u32[]{:S(2)}) collective-permute-start(bf16[512,512]{0,1:T(8,128)(2,1)S(1)} %pad_maximum_fusion.2), channel_id=1, source_target_pairs={{0,4},{1,5},{2,6},{3,7},{4,0},{5,1},{6,2},{7,3},{8,12},{9,13},{10,... | collective-permute-start | bytes 1572872 | tf_op jit(solution)/shard_map/ppermute | solution.py:26
  106.5 23.3 %collective-permute-start.29 = (bf16[512,512]{0,1:T(8,128)(2,1)S(1)}, bf16[512,512]{0,1:T(8,128)(2,1)S(1)}, u32[]{:S(2)}, u32[]{:S(2)}) collective-permute-start(bf16[512,512]{0,1:T(8,128)(2,1)S(1)} %pad_maximum_fusion.2), channel_id=1, source_target_pairs={{0,8},{1,9},{2,10},{3,11},{4,12},{5,13},{6,14},{7,15},{8,0},{9,1},... | collective-permute-start | bytes 1572872 | tf_op jit(solution)/shard_map/ppermute | solution.py:26
  109.3 20.5 %collective-permute-start.30 = (bf16[512,512]{0,1:T(8,128)(2,1)S(1)}, bf16[512,512]{0,1:T(8,128)(2,1)S(1)}, u32[]{:S(2)}, u32[]{:S(2)}) collective-permute-start(bf16[512,512]{0,1:T(8,128)(2,1)S(1)} %pad_maximum_fusion.2), channel_id=1, source_target_pairs={{0,12},{1,13},{2,14},{3,15},{4,8},{5,9},{6,10},{7,11},{8,4},{9,5},... | collective-permute-start | bytes 1572872 | tf_op jit(solution)/shard_map/ppermute | solution.py:26
  133.8 4.2 %collective-permute-start.54 = (bf16[64,512]{1,0:T(8,128)(2,1)S(1)}, bf16[64,512]{1,0:T(8,128)(2,1)S(1)}, u32[]{:S(2)}, u32[]{:S(2)}) collective-permute-start(bf16[64,512]{1,0:T(8,128)(2,1)S(1)} %fusion.54), channel_id=1, source_target_pairs={{16,40},{17,41},{18,42},{19,43},{20,44},{21,45},{22,46},{23,47},{2... | collective-permute-start | bytes 196616 | tf_op jit(solution)/shard_map/ppermute | solution.py:26
  134.4 3.6 %collective-permute-start.55 = (bf16[64,512]{1,0:T(8,128)(2,1)S(1)}, bf16[64,512]{1,0:T(8,128)(2,1)S(1)}, u32[]{:S(2)}, u32[]{:S(2)}) collective-permute-start(bf16[64,512]{1,0:T(8,128)(2,1)S(1)} %fusion.54), channel_id=1, source_target_pairs={{16,36},{17,37},{18,38},{19,39},{20,32},{21,33},{22,34},{23,35},{2... | collective-permute-start | bytes 196616 | tf_op jit(solution)/shard_map/ppermute | solution.py:26
  139.2 8.5 %collective-permute-start.58 = (bf16[64,512]{1,0:T(8,128)(2,1)S(1)}, bf16[64,512]{1,0:T(8,128)(2,1)S(1)}, u32[]{:S(2)}, u32[]{:S(2)}) collective-permute-start(bf16[64,512]{1,0:T(8,128)(2,1)S(1)} %fusion.55), channel_id=1, source_target_pairs={{32,50},{33,51},{34,48},{35,49},{36,54},{37,55},{38,52},{39,53},{4... | collective-permute-start | bytes 196616 | tf_op jit(solution)/shard_map/ppermute | solution.py:26
  143.0 6.5 %collective-permute-start.59 = (bf16[64,512]{1,0:T(8,128)(2,1)S(1)}, bf16[64,512]{1,0:T(8,128)(2,1)S(1)}, u32[]{:S(2)}, u32[]{:S(2)}) collective-permute-start(bf16[64,512]{1,0:T(8,128)(2,1)S(1)} %fusion.55), channel_id=1, source_target_pairs={{32,49},{33,48},{34,51},{35,50},{36,53},{37,52},{38,55},{39,54},{4... | collective-permute-start | bytes 196616 | tf_op jit(solution)/shard_map/ppermute | solution.py:26
  144.3 7.2 %collective-permute-start.60 = (bf16[64,512]{1,0:T(8,128)(2,1)S(1)}, bf16[64,512]{1,0:T(8,128)(2,1)S(1)}, u32[]{:S(2)}, u32[]{:S(2)}) collective-permute-start(bf16[64,512]{1,0:T(8,128)(2,1)S(1)} %fusion.55), channel_id=1, source_target_pairs={{32,51},{33,50},{34,49},{35,48},{36,55},{37,54},{38,53},{39,52},{4... | collective-permute-start | bytes 196616 | tf_op jit(solution)/shard_map/ppermute | solution.py:26
  146.6 4.9 %collective-permute-start.61 = (bf16[64,512]{1,0:T(8,128)(2,1)S(1)}, bf16[64,512]{1,0:T(8,128)(2,1)S(1)}, u32[]{:S(2)}, u32[]{:S(2)}) collective-permute-start(bf16[64,512]{1,0:T(8,128)(2,1)S(1)} %fusion.55), channel_id=1, source_target_pairs={{0,16},{1,17},{2,18},{3,19},{4,20},{5,21},{6,22},{7,23},{8,24},{9,... | collective-permute-start | bytes 196616 | tf_op jit(solution)/shard_map/ppermute | solution.py:31
  146.8 5.7 %collective-permute-start.47 = (bf16[128,512]{1,0:T(8,128)(2,1)S(1)}, bf16[128,512]{1,0:T(8,128)(2,1)S(1)}, u32[]{:S(2)}, u32[]{:S(2)}) collective-permute-start(bf16[128,512]{1,0:T(8,128)(2,1)S(1)} %get-tuple-element.104), channel_id=1, source_target_pairs={{0,1},{1,0},{2,3},{3,2},{4,5},{5,4},{6,7},{7,6},{8,9},{9,8},{10,11... | collective-permute-start | bytes 393224 | tf_op jit(solution)/shard_map/ppermute | solution.py:26
  147.7 6.5 %collective-permute-start.48 = (bf16[128,512]{1,0:T(8,128)(2,1)S(1)}, bf16[128,512]{1,0:T(8,128)(2,1)S(1)}, u32[]{:S(2)}, u32[]{:S(2)}) collective-permute-start(bf16[128,512]{1,0:T(8,128)(2,1)S(1)} %get-tuple-element.103), channel_id=1, source_target_pairs={{0,2},{1,3},{2,0},{3,1},{4,6},{5,7},{6,4},{7,5},{8,10},{9,11},{10,... | collective-permute-start | bytes 393224 | tf_op jit(solution)/shard_map/ppermute | solution.py:26
  149.5 6.2 %collective-permute-start.49 = (bf16[128,512]{1,0:T(8,128)(2,1)S(1)}, bf16[128,512]{1,0:T(8,128)(2,1)S(1)}, u32[]{:S(2)}, u32[]{:S(2)}) collective-permute-start(bf16[128,512]{1,0:T(8,128)(2,1)S(1)} %get-tuple-element.102), channel_id=1, source_target_pairs={{0,3},{1,2},{2,1},{3,0},{4,7},{5,6},{6,5},{7,4},{8,11},{9,10},{10,... | collective-permute-start | bytes 393224 | tf_op jit(solution)/shard_map/ppermute | solution.py:26
  156.8 6.6 %collective-permute-start.62 = (bf16[64,512]{1,0:T(8,128)(2,1)}, bf16[64,512]{1,0:T(8,128)(2,1)S(1)}, u32[]{:S(2)}, u32[]{:S(2)}) collective-permute-start(bf16[64,512]{1,0:T(8,128)(2,1)} %fusion.56), channel_id=1, source_target_pairs={{48,72},{49,73},{50,74},{51,75},{52,76},{53,77},{54,78},{55,79},{5... | collective-permute-start | bytes 196616 | tf_op jit(solution)/shard_map/ppermute | solution.py:26
  157.4 6.0 %collective-permute-start.63 = (bf16[64,512]{1,0:T(8,128)(2,1)}, bf16[64,512]{1,0:T(8,128)(2,1)S(1)}, u32[]{:S(2)}, u32[]{:S(2)}) collective-permute-start(bf16[64,512]{1,0:T(8,128)(2,1)} %fusion.56), channel_id=1, source_target_pairs={{48,68},{49,69},{50,70},{51,71},{52,64},{53,65},{54,66},{55,67},{5... | collective-permute-start | bytes 196616 | tf_op jit(solution)/shard_map/ppermute | solution.py:26
  158.1 5.3 %collective-permute-start.64 = (bf16[64,512]{1,0:T(8,128)(2,1)}, bf16[64,512]{1,0:T(8,128)(2,1)}, u32[]{:S(2)}, u32[]{:S(2)}) collective-permute-start(bf16[64,512]{1,0:T(8,128)(2,1)} %fusion.56), channel_id=1, source_target_pairs={{48,76},{49,77},{50,78},{51,79},{52,72},{53,73},{54,74},{55,75},{5... | collective-permute-start | bytes 196616 | tf_op jit(solution)/shard_map/ppermute | solution.py:26
  159.4 4.0 %collective-permute-start.65 = (bf16[64,512]{1,0:T(8,128)(2,1)}, bf16[64,512]{1,0:T(8,128)(2,1)}, u32[]{:S(2)}, u32[]{:S(2)}) collective-permute-start(bf16[64,512]{1,0:T(8,128)(2,1)} %fusion.56), channel_id=1, source_target_pairs={{48,64},{49,65},{50,66},{51,67},{52,68},{53,69},{54,70},{55,71},{5... | collective-permute-start | bytes 196616 | tf_op jit(solution)/shard_map/ppermute | solution.py:26
  168.5 13.8 %collective-permute-start.70 = (bf16[64,512]{1,0:T(8,128)(2,1)S(1)}, bf16[64,512]{1,0:T(8,128)(2,1)S(1)}, u32[]{:S(2)}, u32[]{:S(2)}) collective-permute-start(bf16[64,512]{1,0:T(8,128)(2,1)S(1)} %fusion.58), channel_id=1, source_target_pairs={{80,104},{81,105},{82,106},{83,107},{84,108},{85,109},{86,110},{87... | collective-permute-start | bytes 196616 | tf_op jit(solution)/shard_map/ppermute | solution.py:26
  169.8 12.5 %collective-permute-start.71 = (bf16[64,512]{1,0:T(8,128)(2,1)S(1)}, bf16[64,512]{1,0:T(8,128)(2,1)S(1)}, u32[]{:S(2)}, u32[]{:S(2)}) collective-permute-start(bf16[64,512]{1,0:T(8,128)(2,1)S(1)} %fusion.58), channel_id=1, source_target_pairs={{80,100},{81,101},{82,102},{83,103},{84,96},{85,97},{86,98},{87,99... | collective-permute-start | bytes 196616 | tf_op jit(solution)/shard_map/ppermute | solution.py:26
  171.1 14.2 %collective-permute-start.72 = (bf16[64,512]{1,0:T(8,128)(2,1)S(1)}, bf16[64,512]{1,0:T(8,128)(2,1)S(1)}, u32[]{:S(2)}, u32[]{:S(2)}) collective-permute-start(bf16[64,512]{1,0:T(8,128)(2,1)S(1)} %fusion.58), channel_id=1, source_target_pairs={{80,108},{81,109},{82,110},{83,111},{84,104},{85,105},{86,106},{87... | collective-permute-start | bytes 196616 | tf_op jit(solution)/shard_map/ppermute | solution.py:26
  172.4 13.2 %collective-permute-start.73 = (bf16[64,512]{1,0:T(8,128)(2,1)S(1)}, bf16[64,512]{1,0:T(8,128)(2,1)S(1)}, u32[]{:S(2)}, u32[]{:S(2)}) collective-permute-start(bf16[64,512]{1,0:T(8,128)(2,1)S(1)} %fusion.58), channel_id=1, source_target_pairs={{80,96},{81,97},{82,98},{83,99},{84,100},{85,101},{86,102},{87,103... | collective-permute-start | bytes 196616 | tf_op jit(solution)/shard_map/ppermute | solution.py:26
  186.5 9.5 %collective-permute-start.74 = (bf16[64,512]{1,0:T(8,128)(2,1)}, bf16[64,512]{1,0:T(8,128)(2,1)}, u32[]{:S(2)}, u32[]{:S(2)}) collective-permute-start(bf16[64,512]{1,0:T(8,128)(2,1)} %fusion.59), channel_id=1, source_target_pairs={{32,50},{33,51},{34,48},{35,49},{36,54},{37,55},{38,52},{39,53},{4... | collective-permute-start | bytes 196616 | tf_op jit(solution)/shard_map/ppermute | solution.py:26
  188.4 7.6 %collective-permute-start.75 = (bf16[64,512]{1,0:T(8,128)(2,1)}, bf16[64,512]{1,0:T(8,128)(2,1)}, u32[]{:S(2)}, u32[]{:S(2)}) collective-permute-start(bf16[64,512]{1,0:T(8,128)(2,1)} %fusion.59), channel_id=1, source_target_pairs={{32,49},{33,48},{34,51},{35,50},{36,53},{37,52},{38,55},{39,54},{4... | collective-permute-start | bytes 196616 | tf_op jit(solution)/shard_map/ppermute | solution.py:26
  190.3 5.7 %collective-permute-start.76 = (bf16[64,512]{1,0:T(8,128)(2,1)}, bf16[64,512]{1,0:T(8,128)(2,1)}, u32[]{:S(2)}, u32[]{:S(2)}) collective-permute-start(bf16[64,512]{1,0:T(8,128)(2,1)} %fusion.59), channel_id=1, source_target_pairs={{32,51},{33,50},{34,49},{35,48},{36,55},{37,54},{38,53},{39,52},{4... | collective-permute-start | bytes 196616 | tf_op jit(solution)/shard_map/ppermute | solution.py:26
  192.2 3.8 %collective-permute-start.77 = (bf16[64,512]{1,0:T(8,128)(2,1)}, bf16[64,512]{1,0:T(8,128)(2,1)}, u32[]{:S(2)}, u32[]{:S(2)}) collective-permute-start(bf16[64,512]{1,0:T(8,128)(2,1)} %fusion.59), channel_id=1, source_target_pairs={{0,16},{1,17},{2,18},{3,19},{4,20},{5,21},{6,22},{7,23},{8,24},{9,... | collective-permute-start | bytes 196616 | tf_op jit(solution)/shard_map/ppermute | solution.py:31
  197.3 5.9 %collective-permute-start.78 = (bf16[64,512]{1,0:T(8,128)(2,1)S(1)}, bf16[64,512]{1,0:T(8,128)(2,1)S(1)}, u32[]{:S(2)}, u32[]{:S(2)}) collective-permute-start(bf16[64,512]{1,0:T(8,128)(2,1)S(1)} %fusion.61), channel_id=1, source_target_pairs={{0,2},{1,3},{2,0},{3,1},{4,6},{5,7},{6,4},{7,5},{8,10},{9,11},{10,... | collective-permute-start | bytes 196616 | tf_op jit(solution)/shard_map/ppermute | solution.py:26
  198.2 5.4 %collective-permute-start.79 = (bf16[64,512]{1,0:T(8,128)(2,1)S(1)}, bf16[64,512]{1,0:T(8,128)(2,1)S(1)}, u32[]{:S(2)}, u32[]{:S(2)}) collective-permute-start(bf16[64,512]{1,0:T(8,128)(2,1)S(1)} %fusion.61), channel_id=1, source_target_pairs={{0,1},{1,0},{2,3},{3,2},{4,5},{5,4},{6,7},{7,6},{8,9},{9,8},{10,11... | collective-permute-start | bytes 196616 | tf_op jit(solution)/shard_map/ppermute | solution.py:26
  200.7 5.5 %collective-permute-start.80 = (bf16[64,512]{1,0:T(8,128)(2,1)S(1)}, bf16[64,512]{1,0:T(8,128)(2,1)S(1)}, u32[]{:S(2)}, u32[]{:S(2)}) collective-permute-start(bf16[64,512]{1,0:T(8,128)(2,1)S(1)} %fusion.61), channel_id=1, source_target_pairs={{0,3},{1,2},{2,1},{3,0},{4,7},{5,6},{6,5},{7,4},{8,11},{9,10},{10,... | collective-permute-start | bytes 196616 | tf_op jit(solution)/shard_map/ppermute | solution.py:26
  206.2 8.9 %collective-permute-start.81 = (bf16[64,512]{1,0:T(8,128)(2,1)S(1)}, bf16[64,512]{1,0:T(8,128)(2,1)S(1)}, u32[]{:S(2)}, u32[]{:S(2)}) collective-permute-start(bf16[64,512]{1,0:T(8,128)(2,1)S(1)} %get-tuple-element.76), channel_id=1, source_target_pairs={{0,4},{1,5},{2,6},{3,7},{4,0},{5,1},{6,2},{7,3},{8,12},{9,13},{10,... | collective-permute-start | bytes 196616 | tf_op jit(solution)/shard_map/ppermute | solution.py:26
  206.3 10.9 %collective-permute-start.82 = (bf16[64,512]{1,0:T(8,128)(2,1)S(1)}, bf16[64,512]{1,0:T(8,128)(2,1)S(1)}, u32[]{:S(2)}, u32[]{:S(2)}) collective-permute-start(bf16[64,512]{1,0:T(8,128)(2,1)S(1)} %get-tuple-element.76), channel_id=1, source_target_pairs={{0,8},{1,9},{2,10},{3,11},{4,12},{5,13},{6,14},{7,15},{8,0},{9,1},... | collective-permute-start | bytes 196616 | tf_op jit(solution)/shard_map/ppermute | solution.py:26
  209.5 9.8 %collective-permute-start.83 = (bf16[64,512]{1,0:T(8,128)(2,1)S(1)}, bf16[64,512]{1,0:T(8,128)(2,1)S(1)}, u32[]{:S(2)}, u32[]{:S(2)}) collective-permute-start(bf16[64,512]{1,0:T(8,128)(2,1)S(1)} %get-tuple-element.76), channel_id=1, source_target_pairs={{0,12},{1,13},{2,14},{3,15},{4,8},{5,9},{6,10},{7,11},{8,4},{9,5},... | collective-permute-start | bytes 196616 | tf_op jit(solution)/shard_map/ppermute | solution.py:26
  211.2 8.2 %collective-permute-start.84 = (bf16[64,128]{1,0:T(8,128)(2,1)S(1)}, bf16[64,128]{1,0:T(8,128)(2,1)S(1)}, u32[]{:S(2)}, u32[]{:S(2)}) collective-permute-start(bf16[64,128]{1,0:T(8,128)(2,1)S(1)} %get-tuple-element.128), channel_id=1, source_target_pairs={{16,2},{17,3},{18,0},{19,1},{20,6},{21,7},{22,4},{23,5},{24,10},{2... | collective-permute-start | bytes 49160 | tf_op jit(solution)/shard_map/ppermute | solution.py:26
  213.2 6.3 %collective-permute-start.85 = (bf16[64,128]{1,0:T(8,128)(2,1)S(1)}, bf16[64,128]{1,0:T(8,128)(2,1)S(1)}, u32[]{:S(2)}, u32[]{:S(2)}) collective-permute-start(bf16[64,128]{1,0:T(8,128)(2,1)S(1)} %get-tuple-element.131), channel_id=1, source_target_pairs={{16,1},{17,0},{18,3},{19,2},{20,5},{21,4},{22,7},{23,6},{24,9},{25... | collective-permute-start | bytes 49160 | tf_op jit(solution)/shard_map/ppermute | solution.py:26
  215.1 6.3 %collective-permute-start.86 = (bf16[64,128]{1,0:T(8,128)(2,1)S(1)}, bf16[64,128]{1,0:T(8,128)(2,1)S(1)}, u32[]{:S(2)}, u32[]{:S(2)}) collective-permute-start(bf16[64,128]{1,0:T(8,128)(2,1)S(1)} %get-tuple-element.130), channel_id=1, source_target_pairs={{16,3},{17,2},{18,1},{19,0},{20,7},{21,6},{22,5},{23,4},{24,11},{2... | collective-permute-start | bytes 49160 | tf_op jit(solution)/shard_map/ppermute | solution.py:26
  217.2 4.2 %collective-permute-start.87 = (bf16[64,128]{1,0:T(8,128)(2,1)S(1)}, bf16[64,128]{1,0:T(8,128)(2,1)S(1)}, u32[]{:S(2)}, u32[]{:S(2)}) collective-permute-start(bf16[64,128]{1,0:T(8,128)(2,1)S(1)} %get-tuple-element.129), channel_id=1, source_target_pairs={{16,0},{17,1},{18,2},{19,3},{20,4},{21,5},{22,6},{23,7},{24,8},{25... | collective-permute-start | bytes 49160 | tf_op jit(solution)/shard_map/ppermute | solution.py:26
  (49 other events, 321.3 us)

commit v3 on v0

v3 whole, which is shorter than its diff:
```python
import jax
import jax.numpy as jnp
from jax import lax
from jax.experimental import pallas as pl
from jax.experimental.pallas import tpu as pltpu
from jax.sharding import PartitionSpec as P

AXES = ("tm", "blk")
SIDE = 4
PLANE = SIDE * SIDE
PARTITIONS = 16
f32, bf16 = jnp.float32, jnp.bfloat16


def partner(p, y):
    return y ^ 1 if p % 2 == 0 else y ^ 3


def other(p, y):
    return y ^ 3 if p % 2 == 0 else y ^ 1


def permuted(value, rule, partitions=range(PARTITIONS)):
    pairs = []
    for p in partitions:
        for b in range(PLANE):
            target, y, x = rule(p, *divmod(b, SIDE))
            pairs.append((p * PLANE + b, target * PLANE + y * SIDE + x))
    return lax.ppermute(value, AXES, pairs)


def along_x(value, step):
    return permuted(value, lambda p, y, x: (p, y, x ^ step))


def along_y(value, step):
    return permuted(value, lambda p, y, x: (p, y ^ step, x))


def turn_messages(message, last):
    if last % 2 == 0:
        far = permuted(message, lambda p, y, x: (p ^ 1, y ^ 1, x))
        near = permuted(message, lambda p, y, x: (p ^ 1, y, x))
    else:
        far = permuted(message, lambda p, y, x: (p + 1, partner(p, y), x), [last])
        near = permuted(message, lambda p, y, x: (p + 1, y, x), [last])
    return far, near


def tie(values, *others):
    return lax.optimization_barrier((values, others))[0]


def kernel_call(body, place, operands, out_shapes, flops=0):
    out_bytes = sum(s.size * s.dtype.itemsize for s in out_shapes)
    in_bytes = sum(o.size * o.dtype.itemsize for o in operands)
    whole = pl.BlockSpec(memory_space=pltpu.VMEM)
    return pl.pallas_call(
        body,
        out_shape=out_shapes,
        in_specs=[pl.BlockSpec(memory_space=pltpu.SMEM)] + [whole] * len(operands),
        out_specs=[whole] * len(out_shapes),
        compiler_params=pltpu.CompilerParams(vmem_limit_bytes=24 * 1024 * 1024),
        cost_estimate=pl.CostEstimate(
            flops=flops, bytes_accessed=in_bytes + out_bytes, transcendentals=0
        ),
    )(place, *operands)


def block_of(index, size):
    return pl.ds(pl.multiple_of(index * size, size), size)


def split_link(place, link, keep, give):
    size = keep.shape[1] // 2
    for half in range(2):
        keep[:, half * size : (half + 1) * size] = link[:, block_of(place[half], size)]
        give[:, half * size : (half + 1) * size] = link[:, block_of(place[2 + half], size)]


def assemble_link(place, *refs):
    *pieces, out = refs
    size = pieces[0].shape[0] // 2
    for step in range(SIDE):
        for half in range(2):
            out[block_of(half * SIDE + (place[0] ^ step), size), :] = pieces[step][
                half * size : (half + 1) * size, :
            ]


def inner_kernel(place, *refs):
    *pieces, out = refs
    inverse, coupling = pieces[:SIDE], pieces[SIDE:]
    size = inverse[0].shape[0]
    for j in range(SIDE):
        for k in range(SIDE):
            out[block_of(place[0] ^ j, size), block_of(place[1] ^ k, size)] = lax.dot_general(
                inverse[j][...],
                coupling[k][...],
                (((1,), (1,)), ((), ())),
                preferred_element_type=f32,
            ).astype(bf16)


def folded_kernel(place, *refs):
    pieces, outs = refs[: 2 * SIDE], refs[2 * SIDE :]
    coupling, inner = pieces[:SIDE], pieces[SIDE:]
    size = inner[0].shape[0]
    for j in range(SIDE):
        total = jnp.zeros(outs[j].shape, f32)
        for k in range(SIDE):
            total = total + jnp.dot(
                coupling[j][:, block_of(place[1] ^ k, size)],
                inner[k][...],
                preferred_element_type=f32,
            )
        outs[j][...] = total.astype(bf16)


def schur_kernel(place, *refs):
    separator, *pieces, schur, narrow = refs
    size = schur.shape[0]
    for step in range(SIDE):
        for row in range(SIDE):
            columns = block_of(row * SIDE + (place[0] ^ step), size)
            value = separator[:, columns] - pieces[step][:, row * size : (row + 1) * size].astype(f32)
            schur[:, columns] = value
            narrow[:, columns] = value.astype(bf16)


def shards(interior_inverse, coupling, separator, link, source, weights):
    inverse_rows, coupling_rows, separator_rows = interior_inverse[0], coupling[0], separator[0]
    link_rows, source_rows, weight_row = link[0], source[0], weights[0]
    rows, nodes = link_rows.shape
    keys = source_rows.shape[0]
    share = keys // SIDE
    line = SIDE * rows
    half = 2 * line
    shape = jax.ShapeDtypeStruct
    p = lax.axis_index("tm").astype(jnp.int32)
    b = lax.axis_index("blk").astype(jnp.int32)
    y, x = b >> 2, b & 3
    even = (p & 1) == 0
    pair = y >> 1
    ring = ((y + 1) >> 1) & 1
    out_place = jnp.where(even, y & 1, pair)
    in_place = jnp.where(even, pair, y & 1)
    in_low = jnp.where(even, ring, 2 * pair)
    in_high = jnp.where(even, 3 - ring, 2 * pair + 1)
    away_low = jnp.where(even, 1 - ring, 2 - 2 * pair)
    away_high = jnp.where(even, 2 + ring, 3 - 2 * pair)
    place = jnp.stack([x, y])

    def ordered(pieces):
        stacked = jnp.stack(pieces)
        return [
            lax.dynamic_index_in_dim(stacked, x ^ k, 0, keepdims=False) for k in range(SIDE)
        ]

    def spread_x(array):
        return [array] + [along_x(array, step) for step in (1, 2, 3)]

    def exchange_x(chunk):
        return [chunk(0)] + [along_x(chunk(step), step) for step in (1, 2, 3)]

    keep, give = kernel_call(
        split_link,
        jnp.stack([in_low, in_high, away_low, away_high]),
        [link_rows],
        [shape((rows, half), bf16)] * 2,
    )
    got = permuted(give, lambda p, y, x: (p, partner(p, y), x))
    started = weight_row[None, :] * source_rows

    def source_chunk(step):
        part = lax.dynamic_slice(started, ((x ^ step) * share, 0), (share, rows))
        return jnp.concatenate([part, jnp.broadcast_to(weight_row[None, :], (8, rows))], axis=0)

    line_values = jnp.concatenate(ordered(exchange_x(source_chunk)), axis=1)
    line_weights = line_values[share : share + 1]
    away_weights = permuted(line_weights, lambda p, y, x: (p, partner(p, y), x))
    two = jnp.where(
        out_place == 0, jnp.concatenate([keep, got]), jnp.concatenate([got, keep])
    )
    (block,) = kernel_call(
        assemble_link, place, spread_x(two), [shape((half, half), bf16)]
    )
    weight_half = jnp.where(
        out_place == 0,
        jnp.concatenate([line_weights, away_weights], axis=1),
        jnp.concatenate([away_weights, line_weights], axis=1),
    )
    zeros = jnp.zeros((share, line), f32)
    own = jnp.where(
        out_place == 0,
        jnp.concatenate([line_values[:share], zeros], axis=1),
        jnp.concatenate([zeros, line_values[:share]], axis=1),
    )

    coupling_in = [coupling_rows] + [along_y(coupling_rows, step) for step in (1, 2, 3)]
    inverse_out = spread_x(tie(inverse_rows, block))

    message = own.astype(bf16)
    final = message
    for turn in range(1, PARTITIONS):
        far, near = turn_messages(message, turn - 1)
        previous = (far.astype(f32) + near.astype(f32)).astype(bf16)
        if turn == 6:
            inverse_out, coupling_in = tie((inverse_out, coupling_in), message)
            (inner,) = kernel_call(
                inner_kernel,
                place,
                inverse_out + coupling_in,
                [shape((line, line), bf16)],
                flops=2 * line * line * nodes,
            )
            inner_all = [inner] + [along_y(inner, step) for step in (1, 2, 3)]
            coupling_out = spread_x(tie(coupling_rows, inner))
            previous = tie(previous, inner)
        if turn == 12:
            coupling_out, inner_all = tie((coupling_out, inner_all), message)
            folded = kernel_call(
                folded_kernel,
                place,
                coupling_out + inner_all,
                [shape((rows, line), bf16)] * SIDE,
                flops=2 * line * line * nodes,
            )
            back_rows = exchange_x(lambda step: folded[step])
            previous = tie(previous, folded)
        if turn == 14:
            back_rows = tie(back_rows, message)
            schur_rows, narrow = kernel_call(
                schur_kernel,
                place,
                [separator_rows] + back_rows,
                [shape((rows, nodes), f32), shape((rows, nodes), bf16)],
            )
            previous = tie(previous, schur_rows, narrow)
        product = lax.dot_general(
            previous, block, (((1,), (1,)), ((), ())), preferred_element_type=f32
        )
        message = (own - weight_half * product).astype(bf16)
        final = jnp.where(p == turn, message, final)

    total = final.astype(f32) + permuted(
        final, lambda p, y, x: (p, partner(p, y), x)
    ).astype(f32)
    rounded = total.astype(bf16)

    back = jnp.dot(rounded, block, preferred_element_type=f32).astype(bf16)
    mine = lax.dynamic_slice(back, (0, in_place * line), (share, line))
    theirs = lax.dynamic_slice(back, (0, (1 - in_place) * line), (share, line))
    later = range(1, PARTITIONS)
    following_line = permuted(
        theirs, lambda p, y, x: (p - 1, other(p, y), x), later
    ).astype(f32) + permuted(mine, lambda p, y, x: (p - 1, y, x), later).astype(f32)

    def own_shard(line_array):
        pieces = exchange_x(
            lambda step: lax.dynamic_slice(line_array, (0, (x ^ step) * rows), (share, rows))
        )
        return jnp.concatenate(ordered(pieces), axis=0)

    rest = permuted(rounded, lambda p, y, x: (p, other(p, y), x))
    m0, m1, r0, r1 = rounded[:, :line], rounded[:, line:], rest[:, :line], rest[:, line:]
    lines = jnp.where(
        even,
        jnp.where(
            pair == 0,
            jnp.concatenate([m0, m1, r0, r1], axis=1),
            jnp.concatenate([r0, r1, m0, m1], axis=1),
        ),
        jnp.where(
            ring == 0,
            jnp.concatenate([m0, r0, r1, m1], axis=1),
            jnp.concatenate([r0, m0, m1, r1], axis=1),
        ),
    )
    terms = lax.dot_general(
        jnp.concatenate(spread_x(lines)),
        narrow,
        (((1,), (1,)), ((), ())),
        preferred_element_type=f32,
    ).reshape(SIDE, share, rows)
    own_terms = jnp.concatenate(ordered([terms[step] for step in range(SIDE)]), axis=0)
    sweep = own_shard(lax.dynamic_slice(total, (0, out_place * line), (share, line)))
    following = own_shard(following_line)
    residual = sweep / weight_row[None, :] - own_terms - following
    return schur_rows[None], sweep[None], residual[None]


def solution(mesh):
    in_specs = (
        P("tm", "blk", None),
        P("tm", "blk", None),
        P("tm", "blk", None),
        P("tm", "blk", None),
        P("tm", None, "blk"),
        P("tm", "blk"),
    )
    out_specs = (P("tm", "blk", None), P("tm", None, "blk"), P("tm", None, "blk"))
    return jax.shard_map(shards, mesh=mesh, in_specs=in_specs, out_specs=out_specs, check_vma=False)
```

time: 680 us -> 237 us (0.35)
  the two profiles are of different devices: /device:TPU:224 before, /device:TPU:161 now
where the time goes in v3:
time: 237 us; the launch traced here: 232 us
  waiting for transfers between devices  120 us (51%)
  starting transfers between devices  87.8 us (37%)
  matrix products  10.4 us (4%)
  Pallas kernels  7.66 us (3%)
  other arithmetic  2.43 us (1%)
    ppermute x66, waiting for transfers between devices, permuted(): return lax.ppermute(value, AXES, pairs)  120 us
    ppermute x66, starting transfers between devices, permuted(): return lax.ppermute(value, AXES, pairs)  87.8 us
    dot_general x15, matrix products, shards(): lax.dot_general(previous, block, (((1,), (1,)), ((), ())), preferred_elem...  9.74 us
    pallas_call x5, Pallas kernels, kernel_call(): pl.pallas_call(body, out_shape=out_shapes, in_specs=[pl.BlockSpec(memory_...  7.66 us
  transfers between devices with their start and end apart: 66, of which 35 were waited for; matrix products, arithmetic and copies ran while one was open for 2% of the time, Pallas kernels for 0%

profile of v3, /device:TPU:161, one launch (start us, length us, event | category | flops | bytes accessed | tf_op | source)
XLA Modules:
  0.0 232.0 jit_solution(10778543693000391205)
XLA Ops:
  0.7 1.0 copy-done.3
  2.4 2.8 %collective-permute-start = (bf16[128,1024]{1,0:T(8,128)(2,1)S(1)}, bf16[128,1024]{1,0:T(8,128)(2,1)S(1)}, u32[]{:S(2)}, u32[]{:S(2)}) collective-permute-start(bf16[128,1024]{1,0:T(8,128)(2,1)S(1)} %get-tuple-element.37), channel_id=1, source_target_pairs={{0,4},{1,5},{2,6},{3,7},{4,0},{5,1},{6,2},{7,3},{8,12},{9,13},{10,... | collective-permute-start | bytes 786440 | tf_op jit(solution)/shard_map/ppermute | solution.py:29
  6.6 2.5 %collective-permute-start.12 = (f32[24,128]{1,0:T(8,128)S(1)}, f32[24,128]{1,0:T(8,128)S(1)}, u32[]{:S(2)}, u32[]{:S(2)}) collective-permute-start(f32[24,128]{1,0:T(8,128)S(1)} %get-tuple-element.112), channel_id=1, source_target_pairs={{0,3},{1,2},{2,1},{3,0},{4,7},{5,6},{6,5},{7,4},{8,11},{9,10},{10,... | collective-permute-start | bytes 36872 | tf_op jit(solution)/shard_map/ppermute | solution.py:29
  10.8 2.4 %collective-permute-done.11 = f32[24,128]{1,0:T(8,128)S(1)} collective-permute-done((f32[24,128]{1,0:T(8,128)S(1)}, f32[24,128]{1,0:T(8,128)S(1)}, u32[]{:S(2)}, u32[]{:S(2)}) %collective-permute-start.11) | collective-permute-done | bytes 12320 | tf_op jit(solution)/shard_map/ppermute | solution.py:29
  13.4 2.0 collective-permute-start.2
  15.4 1.8 collective-permute-start.3
  17.4 2.3 collective-permute-start.15
  19.8 1.3 collective-permute-done.13
  21.0 1.9 collective-permute-start.14
  23.0 2.9 %collective-permute-done.1.refs_1_ = bf16[256,1024]{1,0:T(8,128)(2,1)S(1)} collective-permute-done((bf16[256,1024]{1,0:T(8,128)(2,1)S(1)}, bf16[256,1024]{1,0:T(8,128)(2,1)S(1)}, u32[]{:S(2)}, u32[]{:S(2)}) %collective-permute-start.1) | collective-permute-done | bytes 524320 | tf_op jit(solution)/shard_map/ppermute | solution.py:29
  25.9 11.6 %collective-permute-done.2.refs_2_ = bf16[256,1024]{1,0:T(8,128)(2,1)S(1)} collective-permute-done((bf16[256,1024]{1,0:T(8,128)(2,1)S(1)}, bf16[256,1024]{1,0:T(8,128)(2,1)S(1)}, u32[]{:S(2)}, u32[]{:S(2)}) %collective-permute-start.2) | collective-permute-done | bytes 524320 | tf_op jit(solution)/shard_map/ppermute | solution.py:29
  37.4 2.1 collective-permute-done.3.refs_3_
  43.0 2.7 %collective-permute-start.19 = (bf16[16,1024]{1,0:T(8,128)(2,1)S(1)}, bf16[16,1024]{1,0:T(8,128)(2,1)S(1)}, u32[]{:S(2)}, u32[]{:S(2)}) collective-permute-start(bf16[16,1024]{1,0:T(8,128)(2,1)S(1)} %fusion.16), channel_id=1, source_target_pairs={{0,16},{1,17},{2,18},{3,19},{4,20},{5,21},{6,22},{7,23},{8,24},{9,... | collective-permute-start | bytes 98312 | tf_op jit(solution)/shard_map/ppermute | solution.py:29
  46.6 2.5 %collective-permute-done.18 = bf16[16,1024]{1,0:T(8,128)(2,1)S(1)} collective-permute-done((bf16[16,1024]{1,0:T(8,128)(2,1)S(1)}, bf16[16,1024]{1,0:T(8,128)(2,1)S(1)}, u32[]{:S(2)}, u32[]{:S(2)}) %collective-permute-start.18) | collective-permute-done | bytes 32800 | tf_op jit(solution)/shard_map/ppermute | solution.py:29
  52.3 1.4 collective-permute-start.22
  53.7 11.8 %collective-permute-done.22 = bf16[16,1024]{1,0:T(8,128)(2,1)S(1)} collective-permute-done((bf16[16,1024]{1,0:T(8,128)(2,1)S(1)}, bf16[16,1024]{1,0:T(8,128)(2,1)S(1)}, u32[]{:S(2)}, u32[]{:S(2)}) %collective-permute-start.22) | collective-permute-done | bytes 32800 | tf_op jit(solution)/shard_map/ppermute | solution.py:29
  67.5 0.8 collective-permute-start.8
  68.4 2.0 collective-permute-start.9
  70.4 2.9 %collective-permute-start.5 = (bf16[128,2048]{1,0:T(8,128)(2,1)S(1)}, bf16[128,2048]{1,0:T(8,128)(2,1)S(1)}, u32[]{:S(2)}, u32[]{:S(2)}) collective-permute-start(bf16[128,2048]{1,0:T(8,128)(2,1)S(1)} %bitcast.84), channel_id=1, source_target_pairs={{0,2},{1,3},{2,0},{3,1},{4,6},{5,7},{6,4},{7,5},{8,10},{9,11},{10,... | collective-permute-start | bytes 1572872 | tf_op jit(solution)/shard_map/ppermute | solution.py:29
  73.3 0.9 collective-permute-start.6
  74.2 8.5 %collective-permute-done.8.refs_6_ = bf16[128,2048]{1,0:T(8,128)(2,1)S(1)} collective-permute-done((bf16[128,2048]{1,0:T(8,128)(2,1)S(1)}, bf16[128,2048]{1,0:T(8,128)(2,1)S(1)}, u32[]{:S(2)}, u32[]{:S(2)}) %collective-permute-start.8) | collective-permute-done | bytes 524320 | tf_op jit(solution)/shard_map/ppermute | solution.py:29
  82.7 11.8 %collective-permute-done.9.refs_7_ = bf16[128,2048]{1,0:T(8,128)(2,1)S(1)} collective-permute-done((bf16[128,2048]{1,0:T(8,128)(2,1)S(1)}, bf16[128,2048]{1,0:T(8,128)(2,1)S(1)}, u32[]{:S(2)}, u32[]{:S(2)}) %collective-permute-start.9) | collective-permute-done | bytes 524320 | tf_op jit(solution)/shard_map/ppermute | solution.py:29
  94.5 1.4 collective-permute-done.5.refs_2_
  95.9 2.0 collective-permute-done.6.refs_3_
  97.9 2.9 %shard_map.87.refs_4_ = bf16[512,512]{1,0:T(8,128)(2,1)S(1)} custom-call(s32[2]{0:T(128)S(1)} %pad_add_fusion.place, bf16[128,2048]{1,0:T(8,128)(2,1)S(1)} %bitcast.86, bf16[128,2048]{1,0:T(8,128)(2,1)S(1)} %collective-permute-done.4.refs_1_, bf16[128,2048]{1,0:T(8,128)(2,1)S(1)} %collective-permute-done.5.refs_2_, ...), custom_call_target="tpu_custom_call" | custom-call | flops 1073741824 | bytes 4718592 | tf_op jit(solution)/shard_map/pallas_call | solution.py:58
  101.4 2.2 collective-permute-start.33
  104.5 2.5 %collective-permute-done.32 = bf16[16,1024]{1,0:T(8,128)(2,1)S(1)} collective-permute-done((bf16[16,1024]{1,0:T(8,128)(2,1)S(1)}, bf16[16,1024]{1,0:T(8,128)(2,1)S(1)}, u32[]{:S(2)}, u32[]{:S(2)}) %collective-permute-start.32) | collective-permute-done | bytes 32800 | tf_op jit(solution)/shard_map/ppermute | solution.py:29
  110.9 2.3 %collective-permute-done.36 = bf16[16,1024]{1,0:T(8,128)(2,1)S(1)} collective-permute-done((bf16[16,1024]{1,0:T(8,128)(2,1)S(1)}, bf16[16,1024]{1,0:T(8,128)(2,1)S(1)}, u32[]{:S(2)}, u32[]{:S(2)}) %collective-permute-start.36) | collective-permute-done | bytes 32800 | tf_op jit(solution)/shard_map/ppermute | solution.py:29
  116.0 12.6 %collective-permute-start.41 = (bf16[16,1024]{1,0:T(8,128)(2,1)S(1)}, bf16[16,1024]{1,0:T(8,128)(2,1)S(1)}, u32[]{:S(2)}, u32[]{:S(2)}) collective-permute-start(bf16[16,1024]{1,0:T(8,128)(2,1)S(1)} %fusion.24), channel_id=1, source_target_pairs={{0,16},{1,17},{2,18},{3,19},{4,20},{5,21},{6,22},{7,23},{8,24},{9,... | collective-permute-start | bytes 98312 | tf_op jit(solution)/shard_map/ppermute | solution.py:29
  128.6 0.9 collective-permute-done.41
  129.4 2.5 %collective-permute-done.40 = bf16[16,1024]{1,0:T(8,128)(2,1)S(1)} collective-permute-done((bf16[16,1024]{1,0:T(8,128)(2,1)S(1)}, bf16[16,1024]{1,0:T(8,128)(2,1)S(1)}, u32[]{:S(2)}, u32[]{:S(2)}) %collective-permute-start.40) | collective-permute-done | bytes 32800 | tf_op jit(solution)/shard_map/ppermute | solution.py:29
  132.6 1.3 collective-permute-start.46
  133.9 1.3 collective-permute-start.45
  135.3 1.1 collective-permute-start.26
  136.3 8.7 %collective-permute-start.27 = (bf16[512,512]{1,0:T(8,128)(2,1)S(1)}, bf16[512,512]{1,0:T(8,128)(2,1)S(1)}, u32[]{:S(2)}, u32[]{:S(2)}) collective-permute-start(bf16[512,512]{1,0:T(8,128)(2,1)S(1)} %shard_map.87.refs_4_), channel_id=1, source_target_pairs={{0,4},{1,5},{2,6},{3,7},{4,0},{5,1},{6,2},{7,3},{8,12},{9,13},{10,... | collective-permute-start | bytes 1572872 | tf_op jit(solution)/shard_map/ppermute | solution.py:29
  145.0 3.1 %collective-permute-start.28 = (bf16[512,512]{1,0:T(8,128)(2,1)S(1)}, bf16[512,512]{1,0:T(8,128)(2,1)S(1)}, u32[]{:S(2)}, u32[]{:S(2)}) collective-permute-start(bf16[512,512]{1,0:T(8,128)(2,1)S(1)} %shard_map.87.refs_4_), channel_id=1, source_target_pairs={{0,8},{1,9},{2,10},{3,11},{4,12},{5,13},{6,14},{7,15},{8,0},{9,1},... | collective-permute-start | bytes 1572872 | tf_op jit(solution)/shard_map/ppermute | solution.py:29
  148.9 0.9 collective-permute-done.25.refs_2_
  149.8 11.2 %collective-permute-done.26.refs_3_ = bf16[128,2048]{1,0:T(8,128)(2,1)S(1)} collective-permute-done((bf16[128,2048]{1,0:T(8,128)(2,1)S(1)}, bf16[128,2048]{1,0:T(8,128)(2,1)S(1)}, u32[]{:S(2)}, u32[]{:S(2)}) %collective-permute-start.26) | collective-permute-done | bytes 524320 | tf_op jit(solution)/shard_map/ppermute | solution.py:29
  161.0 10.2 %collective-permute-done.28.refs_6_ = bf16[512,512]{1,0:T(8,128)(2,1)S(1)} collective-permute-done((bf16[512,512]{1,0:T(8,128)(2,1)S(1)}, bf16[512,512]{1,0:T(8,128)(2,1)S(1)}, u32[]{:S(2)}, u32[]{:S(2)}) %collective-permute-start.28) | collective-permute-done | bytes 524320 | tf_op jit(solution)/shard_map/ppermute | solution.py:29
  171.2 3.2 %collective-permute-done.29.refs_7_ = bf16[512,512]{1,0:T(8,128)(2,1)S(1)} collective-permute-done((bf16[512,512]{1,0:T(8,128)(2,1)S(1)}, bf16[512,512]{1,0:T(8,128)(2,1)S(1)}, u32[]{:S(2)}, u32[]{:S(2)}) %collective-permute-start.29) | collective-permute-done | bytes 524320 | tf_op jit(solution)/shard_map/ppermute | solution.py:29
  174.4 1.8 shard_map.88
  177.4 0.9 collective-permute-done.48
  178.3 2.5 %collective-permute-done.47 = bf16[16,1024]{1,0:T(8,128)(2,1)S(1)} collective-permute-done((bf16[16,1024]{1,0:T(8,128)(2,1)S(1)}, bf16[16,1024]{1,0:T(8,128)(2,1)S(1)}, u32[]{:S(2)}, u32[]{:S(2)}) %collective-permute-start.47) | collective-permute-done | bytes 32800 | tf_op jit(solution)/shard_map/ppermute | solution.py:29
  182.8 1.7 collective-permute-start.42
  184.5 1.3 collective-permute-start.43
  185.8 1.2 collective-permute-start.44
  187.0 1.2 collective-permute-done.42.refs_2_
  188.2 4.0 %collective-permute-done.43.refs_3_ = bf16[128,512]{1,0:T(8,128)(2,1)S(1)} collective-permute-done((bf16[128,512]{1,0:T(8,128)(2,1)S(1)}, bf16[128,512]{1,0:T(8,128)(2,1)S(1)}, u32[]{:S(2)}, u32[]{:S(2)}) %collective-permute-start.43) | collective-permute-done | bytes 131104 | tf_op jit(solution)/shard_map/ppermute | solution.py:29
  192.3 2.5 %collective-permute-done.44.refs_4_ = bf16[128,512]{1,0:T(8,128)(2,1)S(1)} collective-permute-done((bf16[128,512]{1,0:T(8,128)(2,1)S(1)}, bf16[128,512]{1,0:T(8,128)(2,1)S(1)}, u32[]{:S(2)}, u32[]{:S(2)}) %collective-permute-start.44) | collective-permute-done | bytes 131104 | tf_op jit(solution)/shard_map/ppermute | solution.py:29
  194.8 1.7 shard_map.89
  198.0 0.9 collective-permute-done.52
  198.9 2.5 %collective-permute-done.51 = bf16[16,1024]{1,0:T(8,128)(2,1)S(1)} collective-permute-done((bf16[16,1024]{1,0:T(8,128)(2,1)S(1)}, bf16[16,1024]{1,0:T(8,128)(2,1)S(1)}, u32[]{:S(2)}, u32[]{:S(2)}) %collective-permute-start.51) | collective-permute-done | bytes 32800 | tf_op jit(solution)/shard_map/ppermute | solution.py:29
  202.6 3.4 %collective-permute-done.53 = bf16[16,1024]{1,0:T(8,128)(2,1)S(1)} collective-permute-done((bf16[16,1024]{1,0:T(8,128)(2,1)S(1)}, bf16[16,1024]{1,0:T(8,128)(2,1)S(1)}, u32[]{:S(2)}, u32[]{:S(2)}) %collective-permute-start.53) | collective-permute-done | bytes 32800 | tf_op jit(solution)/shard_map/ppermute | solution.py:29
  206.5 1.2 collective-permute-start.56
  207.7 2.1 collective-permute-start.54
  209.8 3.6 %collective-permute-start.62 = (bf16[16,512]{1,0:T(8,128)(2,1)S(1)}, bf16[16,512]{1,0:T(8,128)(2,1)S(1)}, u32[]{:S(2)}, u32[]{:S(2)}) collective-permute-start(bf16[16,512]{1,0:T(8,128)(2,1)S(1)} %get-tuple-element.88), channel_id=1, source_target_pairs={{16,0},{17,1},{18,2},{19,3},{20,4},{21,5},{22,6},{23,7},{24,8},{25... | collective-permute-start | bytes 49160 | tf_op jit(solution)/shard_map/ppermute | solution.py:29
  213.5 1.9 collective-permute-start.61
  216.1 4.6 %collective-permute-done.61 = bf16[16,512]{1,0:T(8,128)(2,1)S(1)} collective-permute-done((bf16[16,512]{1,0:T(8,128)(2,1)S(1)}, bf16[16,512]{1,0:T(8,128)(2,1)S(1)}, u32[]{:S(2)}, u32[]{:S(2)}) %collective-permute-start.61) | collective-permute-done | bytes 16416 | tf_op jit(solution)/shard_map/ppermute | solution.py:29
  220.6 1.5 collective-permute-start.65
  222.5 1.7 collective-permute-start.63
  224.2 1.3 collective-permute-start.60
  226.1 1.5 collective-permute-start.58
  227.6 1.1 collective-permute-done.60
  228.7 2.1 collective-permute-done.59
  (133 shorter events, 32.3 us)
Async XLA Ops:
  2.4 10.8 %collective-permute-start = (bf16[128,1024]{1,0:T(8,128)(2,1)S(1)}, bf16[128,1024]{1,0:T(8,128)(2,1)S(1)}, u32[]{:S(2)}, u32[]{:S(2)}) collective-permute-start(bf16[128,1024]{1,0:T(8,128)(2,1)S(1)} %get-tuple-element.37), channel_id=1, source_target_pairs={{0,4},{1,5},{2,6},{3,7},{4,0},{5,1},{6,2},{7,3},{8,12},{9,13},{10,... | collective-permute-start | bytes 786440 | tf_op jit(solution)/shard_map/ppermute | solution.py:29
  6.6 4.1 %collective-permute-start.12 = (f32[24,128]{1,0:T(8,128)S(1)}, f32[24,128]{1,0:T(8,128)S(1)}, u32[]{:S(2)}, u32[]{:S(2)}) collective-permute-start(f32[24,128]{1,0:T(8,128)S(1)} %get-tuple-element.112), channel_id=1, source_target_pairs={{0,3},{1,2},{2,1},{3,0},{4,7},{5,6},{6,5},{7,4},{8,11},{9,10},{10,... | collective-permute-start | bytes 36872 | tf_op jit(solution)/shard_map/ppermute | solution.py:29
  9.1 4.0 %collective-permute-start.11 = (f32[24,128]{1,0:T(8,128)S(1)}, f32[24,128]{1,0:T(8,128)S(1)}, u32[]{:S(2)}, u32[]{:S(2)}) collective-permute-start(f32[24,128]{1,0:T(8,128)S(1)} %get-tuple-element.111), channel_id=1, source_target_pairs={{0,2},{1,3},{2,0},{3,1},{4,6},{5,7},{6,4},{7,5},{8,10},{9,11},{10,... | collective-permute-start | bytes 36872 | tf_op jit(solution)/shard_map/ppermute | solution.py:29
  9.6 3.5 %collective-permute-start.10 = (f32[24,128]{1,0:T(8,128)S(1)}, f32[24,128]{1,0:T(8,128)S(1)}, u32[]{:S(2)}, u32[]{:S(2)}) collective-permute-start(f32[24,128]{1,0:T(8,128)S(1)} %get-tuple-element.110), channel_id=1, source_target_pairs={{0,1},{1,0},{2,3},{3,2},{4,5},{5,4},{6,7},{7,6},{8,9},{9,8},{10,11... | collective-permute-start | bytes 36872 | tf_op jit(solution)/shard_map/ppermute | solution.py:29
  13.3 12.6 %collective-permute-start.1 = (bf16[256,1024]{1,0:T(8,128)(2,1)S(1)}, bf16[256,1024]{1,0:T(8,128)(2,1)S(1)}, u32[]{:S(2)}, u32[]{:S(2)}) collective-permute-start(bf16[256,1024]{1,0:T(8,128)(2,1)S(1)} %maximum_select_fusion.refs_0_), channel_id=1, source_target_pairs={{0,1},{1,0},{2,3},{3,2},{4,5},{5,4},{6,7},{7,6},{8,9},{9,8},{10,11... | collective-permute-start | bytes 1572872 | tf_op jit(solution)/shard_map/ppermute | solution.py:29
  13.4 24.0 %collective-permute-start.2 = (bf16[256,1024]{1,0:T(8,128)(2,1)S(1)}, bf16[256,1024]{1,0:T(8,128)(2,1)S(1)}, u32[]{:S(2)}, u32[]{:S(2)}) collective-permute-start(bf16[256,1024]{1,0:T(8,128)(2,1)S(1)} %maximum_select_fusion.refs_0_), channel_id=1, source_target_pairs={{0,2},{1,3},{2,0},{3,1},{4,6},{5,7},{6,4},{7,5},{8,10},{9,11},{10,... | collective-permute-start | bytes 1572872 | tf_op jit(solution)/shard_map/ppermute | solution.py:29
  15.4 24.1 %collective-permute-start.3 = (bf16[256,1024]{1,0:T(8,128)(2,1)S(1)}, bf16[256,1024]{1,0:T(8,128)(2,1)S(1)}, u32[]{:S(2)}, u32[]{:S(2)}) collective-permute-start(bf16[256,1024]{1,0:T(8,128)(2,1)S(1)} %maximum_select_fusion.refs_0_), channel_id=1, source_target_pairs={{0,3},{1,2},{2,1},{3,0},{4,7},{5,6},{6,5},{7,4},{8,11},{9,10},{10,... | collective-permute-start | bytes 1572872 | tf_op jit(solution)/shard_map/ppermute | solution.py:29
  17.3 3.7 %collective-permute-start.13 = (f32[1,512]{1,0:T(1,128)S(1)}, f32[1,512]{1,0:T(1,128)S(1)}, u32[]{:S(2)}, u32[]{:S(2)}) collective-permute-start(f32[1,512]{1,0:T(1,128)S(1)} %pad_maximum_fusion.9), channel_id=1, source_target_pairs={{0,4},{1,5},{2,6},{3,7},{4,0},{5,1},{6,2},{7,3},{8,12},{9,13},{10,... | collective-permute-start | bytes 6152 | tf_op jit(solution)/shard_map/ppermute | solution.py:29
  17.4 22.8 %collective-permute-start.15 = (bf16[16,1024]{1,0:T(8,128)(2,1)S(1)}, bf16[16,1024]{1,0:T(8,128)(2,1)S(1)}, u32[]{:S(2)}, u32[]{:S(2)}) collective-permute-start(bf16[16,1024]{1,0:T(8,128)(2,1)S(1)} %fusion.40), channel_id=1, source_target_pairs={{0,16},{1,17},{2,18},{3,19},{4,20},{5,21},{6,22},{7,23},{8,24},{9,... | collective-permute-start | bytes 98312 | tf_op jit(solution)/shard_map/ppermute | solution.py:29
  21.0 19.2 %collective-permute-start.14 = (bf16[16,1024]{1,0:T(8,128)(2,1)S(1)}, bf16[16,1024]{1,0:T(8,128)(2,1)S(1)}, u32[]{:S(2)}, u32[]{:S(2)}) collective-permute-start(bf16[16,1024]{1,0:T(8,128)(2,1)S(1)} %fusion.40), channel_id=1, source_target_pairs={{0,20},{1,21},{2,22},{3,23},{4,16},{5,17},{6,18},{7,19},{8,28},{9,... | collective-permute-start | bytes 98312 | tf_op jit(solution)/shard_map/ppermute | solution.py:29
  40.9 1.5 collective-permute-start.17
  43.0 3.6 %collective-permute-start.19 = (bf16[16,1024]{1,0:T(8,128)(2,1)S(1)}, bf16[16,1024]{1,0:T(8,128)(2,1)S(1)}, u32[]{:S(2)}, u32[]{:S(2)}) collective-permute-start(bf16[16,1024]{1,0:T(8,128)(2,1)S(1)} %fusion.16), channel_id=1, source_target_pairs={{0,16},{1,17},{2,18},{3,19},{4,20},{5,21},{6,22},{7,23},{8,24},{9,... | collective-permute-start | bytes 98312 | tf_op jit(solution)/shard_map/ppermute | solution.py:29
  45.7 3.4 %collective-permute-start.18 = (bf16[16,1024]{1,0:T(8,128)(2,1)S(1)}, bf16[16,1024]{1,0:T(8,128)(2,1)S(1)}, u32[]{:S(2)}, u32[]{:S(2)}) collective-permute-start(bf16[16,1024]{1,0:T(8,128)(2,1)S(1)} %fusion.16), channel_id=1, source_target_pairs={{0,20},{1,21},{2,22},{3,23},{4,16},{5,17},{6,18},{7,19},{8,28},{9,... | collective-permute-start | bytes 98312 | tf_op jit(solution)/shard_map/ppermute | solution.py:29
  49.7 1.5 collective-permute-start.21
  50.4 0.9 collective-permute-start.20
  51.1 19.2 %collective-permute-start.7 = (bf16[128,2048]{1,0:T(8,128)(2,1)S(1)}, bf16[128,2048]{1,0:T(8,128)(2,1)S(1)}, u32[]{:S(2)}, u32[]{:S(2)}) collective-permute-start(bf16[128,2048]{1,0:T(8,128)(2,1)S(1)} %bitcast.74), channel_id=1, source_target_pairs={{0,4},{1,5},{2,6},{3,7},{4,0},{5,1},{6,2},{7,3},{8,12},{9,13},{10,... | collective-permute-start | bytes 1572872 | tf_op jit(solution)/shard_map/ppermute | solution.py:29
  51.9 1.8 collective-permute-start.23
  52.3 13.3 %collective-permute-start.22 = (bf16[16,1024]{1,0:T(8,128)(2,1)S(1)}, bf16[16,1024]{1,0:T(8,128)(2,1)S(1)}, u32[]{:S(2)}, u32[]{:S(2)}) collective-permute-start(bf16[16,1024]{1,0:T(8,128)(2,1)S(1)} %fusion.18), channel_id=1, source_target_pairs={{0,20},{1,21},{2,22},{3,23},{4,16},{5,17},{6,18},{7,19},{8,28},{9,... | collective-permute-start | bytes 98312 | tf_op jit(solution)/shard_map/ppermute | solution.py:29
  66.2 4.2 %collective-permute-start.31 = (bf16[16,1024]{1,0:T(8,128)(2,1)S(1)}, bf16[16,1024]{1,0:T(8,128)(2,1)S(1)}, u32[]{:S(2)}, u32[]{:S(2)}) collective-permute-start(bf16[16,1024]{1,0:T(8,128)(2,1)S(1)} %fusion.19), channel_id=1, source_target_pairs={{80,96},{81,97},{82,98},{83,99},{84,100},{85,101},{86,102},{87,103... | collective-permute-start | bytes 98312 | tf_op jit(solution)/shard_map/ppermute | solution.py:29
  66.9 6.5 %collective-permute-start.30 = (bf16[16,1024]{1,0:T(8,128)(2,1)S(1)}, bf16[16,1024]{1,0:T(8,128)(2,1)S(1)}, u32[]{:S(2)}, u32[]{:S(2)}) collective-permute-start(bf16[16,1024]{1,0:T(8,128)(2,1)S(1)} %fusion.19), channel_id=1, source_target_pairs={{80,108},{81,109},{82,110},{83,111},{84,104},{85,105},{86,106},{87... | collective-permute-start | bytes 98312 | tf_op jit(solution)/shard_map/ppermute | solution.py:29
  67.5 15.2 %collective-permute-start.8 = (bf16[128,2048]{1,0:T(8,128)(2,1)S(1)}, bf16[128,2048]{1,0:T(8,128)(2,1)S(1)}, u32[]{:S(2)}, u32[]{:S(2)}) collective-permute-start(bf16[128,2048]{1,0:T(8,128)(2,1)S(1)} %bitcast.75), channel_id=1, source_target_pairs={{0,8},{1,9},{2,10},{3,11},{4,12},{5,13},{6,14},{7,15},{8,0},{9,1},... | collective-permute-start | bytes 1572872 | tf_op jit(solution)/shard_map/ppermute | solution.py:29
  68.4 26.1 %collective-permute-start.9 = (bf16[128,2048]{1,0:T(8,128)(2,1)S(1)}, bf16[128,2048]{1,0:T(8,128)(2,1)S(1)}, u32[]{:S(2)}, u32[]{:S(2)}) collective-permute-start(bf16[128,2048]{1,0:T(8,128)(2,1)S(1)} %bitcast.76), channel_id=1, source_target_pairs={{0,12},{1,13},{2,14},{3,15},{4,8},{5,9},{6,10},{7,11},{8,4},{9,5},... | collective-permute-start | bytes 1572872 | tf_op jit(solution)/shard_map/ppermute | solution.py:29
  70.4 24.1 %collective-permute-start.4 = (bf16[128,2048]{1,0:T(8,128)(2,1)S(1)}, bf16[128,2048]{1,0:T(8,128)(2,1)S(1)}, u32[]{:S(2)}, u32[]{:S(2)}) collective-permute-start(bf16[128,2048]{1,0:T(8,128)(2,1)S(1)} %bitcast.83), channel_id=1, source_target_pairs={{0,1},{1,0},{2,3},{3,2},{4,5},{5,4},{6,7},{7,6},{8,9},{9,8},{10,11... | collective-permute-start | bytes 1572872 | tf_op jit(solution)/shard_map/ppermute | solution.py:29
  70.4 25.5 %collective-permute-start.5 = (bf16[128,2048]{1,0:T(8,128)(2,1)S(1)}, bf16[128,2048]{1,0:T(8,128)(2,1)S(1)}, u32[]{:S(2)}, u32[]{:S(2)}) collective-permute-start(bf16[128,2048]{1,0:T(8,128)(2,1)S(1)} %bitcast.84), channel_id=1, source_target_pairs={{0,2},{1,3},{2,0},{3,1},{4,6},{5,7},{6,4},{7,5},{8,10},{9,11},{10,... | collective-permute-start | bytes 1572872 | tf_op jit(solution)/shard_map/ppermute | solution.py:29
  73.3 24.6 %collective-permute-start.6 = (bf16[128,2048]{1,0:T(8,128)(2,1)S(1)}, bf16[128,2048]{1,0:T(8,128)(2,1)S(1)}, u32[]{:S(2)}, u32[]{:S(2)}) collective-permute-start(bf16[128,2048]{1,0:T(8,128)(2,1)S(1)} %bitcast.85), channel_id=1, source_target_pairs={{0,3},{1,2},{2,1},{3,0},{4,7},{5,6},{6,5},{7,4},{8,11},{9,10},{10,... | collective-permute-start | bytes 1572872 | tf_op jit(solution)/shard_map/ppermute | solution.py:29
  101.4 3.1 %collective-permute-start.33 = (bf16[16,1024]{1,0:T(8,128)(2,1)S(1)}, bf16[16,1024]{1,0:T(8,128)(2,1)S(1)}, u32[]{:S(2)}, u32[]{:S(2)}) collective-permute-start(bf16[16,1024]{1,0:T(8,128)(2,1)S(1)} %fusion.20), channel_id=1, source_target_pairs={{0,16},{1,17},{2,18},{3,19},{4,20},{5,21},{6,22},{7,23},{8,24},{9,... | collective-permute-start | bytes 98312 | tf_op jit(solution)/shard_map/ppermute | solution.py:29
  103.7 3.4 %collective-permute-start.32 = (bf16[16,1024]{1,0:T(8,128)(2,1)S(1)}, bf16[16,1024]{1,0:T(8,128)(2,1)S(1)}, u32[]{:S(2)}, u32[]{:S(2)}) collective-permute-start(bf16[16,1024]{1,0:T(8,128)(2,1)S(1)} %fusion.20), channel_id=1, source_target_pairs={{0,20},{1,21},{2,22},{3,23},{4,16},{5,17},{6,18},{7,19},{8,28},{9,... | collective-permute-start | bytes 98312 | tf_op jit(solution)/shard_map/ppermute | solution.py:29
  107.7 1.3 collective-permute-start.35
  109.7 1.2 collective-permute-start.37
  109.8 3.5 %collective-permute-start.36 = (bf16[16,1024]{1,0:T(8,128)(2,1)S(1)}, bf16[16,1024]{1,0:T(8,128)(2,1)S(1)}, u32[]{:S(2)}, u32[]{:S(2)}) collective-permute-start(bf16[16,1024]{1,0:T(8,128)(2,1)S(1)} %fusion.22), channel_id=1, source_target_pairs={{0,20},{1,21},{2,22},{3,23},{4,16},{5,17},{6,18},{7,19},{8,28},{9,... | collective-permute-start | bytes 98312 | tf_op jit(solution)/shard_map/ppermute | solution.py:29
  113.9 1.4 collective-permute-start.39
  114.6 0.8 collective-permute-start.38
  115.2 32.9 %collective-permute-start.24 = (bf16[128,2048]{1,0:T(8,128)(2,1)S(1)}, bf16[128,2048]{1,0:T(8,128)(2,1)S(1)}, u32[]{:S(2)}, u32[]{:S(2)}) collective-permute-start(bf16[128,2048]{1,0:T(8,128)(2,1)S(1)} %bitcast.78), channel_id=1, source_target_pairs={{0,1},{1,0},{2,3},{3,2},{4,5},{5,4},{6,7},{7,6},{8,9},{9,8},{10,11... | collective-permute-start | bytes 1572872 | tf_op jit(solution)/shard_map/ppermute | solution.py:29
  116.0 13.4 %collective-permute-start.41 = (bf16[16,1024]{1,0:T(8,128)(2,1)S(1)}, bf16[16,1024]{1,0:T(8,128)(2,1)S(1)}, u32[]{:S(2)}, u32[]{:S(2)}) collective-permute-start(bf16[16,1024]{1,0:T(8,128)(2,1)S(1)} %fusion.24), channel_id=1, source_target_pairs={{0,16},{1,17},{2,18},{3,19},{4,20},{5,21},{6,22},{7,23},{8,24},{9,... | collective-permute-start | bytes 98312 | tf_op jit(solution)/shard_map/ppermute | solution.py:29
  128.6 3.4 %collective-permute-start.40 = (bf16[16,1024]{1,0:T(8,128)(2,1)S(1)}, bf16[16,1024]{1,0:T(8,128)(2,1)S(1)}, u32[]{:S(2)}, u32[]{:S(2)}) collective-permute-start(bf16[16,1024]{1,0:T(8,128)(2,1)S(1)} %fusion.24), channel_id=1, source_target_pairs={{0,20},{1,21},{2,22},{3,23},{4,16},{5,17},{6,18},{7,19},{8,28},{9,... | collective-permute-start | bytes 98312 | tf_op jit(solution)/shard_map/ppermute | solution.py:29
  132.6 3.8 %collective-permute-start.46 = (bf16[16,1024]{1,0:T(8,128)(2,1)S(1)}, bf16[16,1024]{1,0:T(8,128)(2,1)S(1)}, u32[]{:S(2)}, u32[]{:S(2)}) collective-permute-start(bf16[16,1024]{1,0:T(8,128)(2,1)S(1)} %fusion.25), channel_id=1, source_target_pairs={{176,192},{177,193},{178,194},{179,195},{180,196},{181,197},{182,1... | collective-permute-start | bytes 98312 | tf_op jit(solution)/shard_map/ppermute | solution.py:29
  133.9 11.2 %collective-permute-start.45 = (bf16[16,1024]{1,0:T(8,128)(2,1)S(1)}, bf16[16,1024]{1,0:T(8,128)(2,1)S(1)}, u32[]{:S(2)}, u32[]{:S(2)}) collective-permute-start(bf16[16,1024]{1,0:T(8,128)(2,1)S(1)} %fusion.25), channel_id=1, source_target_pairs={{176,204},{177,205},{178,206},{179,207},{180,200},{181,201},{182,2... | collective-permute-start | bytes 98312 | tf_op jit(solution)/shard_map/ppermute | solution.py:29
  135.2 14.6 %collective-permute-start.25 = (bf16[128,2048]{1,0:T(8,128)(2,1)S(1)}, bf16[128,2048]{1,0:T(8,128)(2,1)S(1)}, u32[]{:S(2)}, u32[]{:S(2)}) collective-permute-start(bf16[128,2048]{1,0:T(8,128)(2,1)S(1)} %bitcast.79), channel_id=1, source_target_pairs={{0,2},{1,3},{2,0},{3,1},{4,6},{5,7},{6,4},{7,5},{8,10},{9,11},{10,... | collective-permute-start | bytes 1572872 | tf_op jit(solution)/shard_map/ppermute | solution.py:29
  135.3 25.7 %collective-permute-start.26 = (bf16[128,2048]{1,0:T(8,128)(2,1)S(1)}, bf16[128,2048]{1,0:T(8,128)(2,1)S(1)}, u32[]{:S(2)}, u32[]{:S(2)}) collective-permute-start(bf16[128,2048]{1,0:T(8,128)(2,1)S(1)} %bitcast.80), channel_id=1, source_target_pairs={{0,3},{1,2},{2,1},{3,0},{4,7},{5,6},{6,5},{7,4},{8,11},{9,10},{10,... | collective-permute-start | bytes 1572872 | tf_op jit(solution)/shard_map/ppermute | solution.py:29
  136.3 24.7 %collective-permute-start.27 = (bf16[512,512]{1,0:T(8,128)(2,1)S(1)}, bf16[512,512]{1,0:T(8,128)(2,1)S(1)}, u32[]{:S(2)}, u32[]{:S(2)}) collective-permute-start(bf16[512,512]{1,0:T(8,128)(2,1)S(1)} %shard_map.87.refs_4_), channel_id=1, source_target_pairs={{0,4},{1,5},{2,6},{3,7},{4,0},{5,1},{6,2},{7,3},{8,12},{9,13},{10,... | collective-permute-start | bytes 1572872 | tf_op jit(solution)/shard_map/ppermute | solution.py:29
  145.0 26.2 %collective-permute-start.28 = (bf16[512,512]{1,0:T(8,128)(2,1)S(1)}, bf16[512,512]{1,0:T(8,128)(2,1)S(1)}, u32[]{:S(2)}, u32[]{:S(2)}) collective-permute-start(bf16[512,512]{1,0:T(8,128)(2,1)S(1)} %shard_map.87.refs_4_), channel_id=1, source_target_pairs={{0,8},{1,9},{2,10},{3,11},{4,12},{5,13},{6,14},{7,15},{8,0},{9,1},... | collective-permute-start | bytes 1572872 | tf_op jit(solution)/shard_map/ppermute | solution.py:29
  148.2 26.3 %collective-permute-start.29 = (bf16[512,512]{1,0:T(8,128)(2,1)S(1)}, bf16[512,512]{1,0:T(8,128)(2,1)S(1)}, u32[]{:S(2)}, u32[]{:S(2)}) collective-permute-start(bf16[512,512]{1,0:T(8,128)(2,1)S(1)} %shard_map.87.refs_4_), channel_id=1, source_target_pairs={{0,12},{1,13},{2,14},{3,15},{4,8},{5,9},{6,10},{7,11},{8,4},{9,5},... | collective-permute-start | bytes 1572872 | tf_op jit(solution)/shard_map/ppermute | solution.py:29
  176.9 1.4 collective-permute-start.48
  177.4 3.4 %collective-permute-start.47 = (bf16[16,1024]{1,0:T(8,128)(2,1)S(1)}, bf16[16,1024]{1,0:T(8,128)(2,1)S(1)}, u32[]{:S(2)}, u32[]{:S(2)}) collective-permute-start(bf16[16,1024]{1,0:T(8,128)(2,1)S(1)} %fusion.26), channel_id=1, source_target_pairs={{0,20},{1,21},{2,22},{3,23},{4,16},{5,17},{6,18},{7,19},{8,28},{9,... | collective-permute-start | bytes 98312 | tf_op jit(solution)/shard_map/ppermute | solution.py:29
  181.4 5.6 %collective-permute-start.50 = (bf16[16,1024]{1,0:T(8,128)(2,1)S(1)}, bf16[16,1024]{1,0:T(8,128)(2,1)S(1)}, u32[]{:S(2)}, u32[]{:S(2)}) collective-permute-start(bf16[16,1024]{1,0:T(8,128)(2,1)S(1)} %fusion.27), channel_id=1, source_target_pairs={{208,224},{209,225},{210,226},{211,227},{212,228},{213,229},{214,2... | collective-permute-start | bytes 98312 | tf_op jit(solution)/shard_map/ppermute | solution.py:29
  182.1 4.9 %collective-permute-start.49 = (bf16[16,1024]{1,0:T(8,128)(2,1)S(1)}, bf16[16,1024]{1,0:T(8,128)(2,1)S(1)}, u32[]{:S(2)}, u32[]{:S(2)}) collective-permute-start(bf16[16,1024]{1,0:T(8,128)(2,1)S(1)} %fusion.27), channel_id=1, source_target_pairs={{208,236},{209,237},{210,238},{211,239},{212,232},{213,233},{214,2... | collective-permute-start | bytes 98312 | tf_op jit(solution)/shard_map/ppermute | solution.py:29
  182.8 5.4 %collective-permute-start.42 = (bf16[128,512]{1,0:T(8,128)(2,1)S(1)}, bf16[128,512]{1,0:T(8,128)(2,1)S(1)}, u32[]{:S(2)}, u32[]{:S(2)}) collective-permute-start(bf16[128,512]{1,0:T(8,128)(2,1)S(1)} %get-tuple-element.58), channel_id=1, source_target_pairs={{0,1},{1,0},{2,3},{3,2},{4,5},{5,4},{6,7},{7,6},{8,9},{9,8},{10,11... | collective-permute-start | bytes 393224 | tf_op jit(solution)/shard_map/ppermute | solution.py:29
  184.5 7.8 %collective-permute-start.43 = (bf16[128,512]{1,0:T(8,128)(2,1)S(1)}, bf16[128,512]{1,0:T(8,128)(2,1)S(1)}, u32[]{:S(2)}, u32[]{:S(2)}) collective-permute-start(bf16[128,512]{1,0:T(8,128)(2,1)S(1)} %get-tuple-element.59), channel_id=1, source_target_pairs={{0,2},{1,3},{2,0},{3,1},{4,6},{5,7},{6,4},{7,5},{8,10},{9,11},{10,... | collective-permute-start | bytes 393224 | tf_op jit(solution)/shard_map/ppermute | solution.py:29
  185.8 9.0 %collective-permute-start.44 = (bf16[128,512]{1,0:T(8,128)(2,1)S(1)}, bf16[128,512]{1,0:T(8,128)(2,1)S(1)}, u32[]{:S(2)}, u32[]{:S(2)}) collective-permute-start(bf16[128,512]{1,0:T(8,128)(2,1)S(1)} %get-tuple-element.60), channel_id=1, source_target_pairs={{0,3},{1,2},{2,1},{3,0},{4,7},{5,6},{6,5},{7,4},{8,11},{9,10},{10,... | collective-permute-start | bytes 393224 | tf_op jit(solution)/shard_map/ppermute | solution.py:29
  197.2 1.7 collective-permute-start.52
  198.0 3.4 %collective-permute-start.51 = (bf16[16,1024]{1,0:T(8,128)(2,1)S(1)}, bf16[16,1024]{1,0:T(8,128)(2,1)S(1)}, u32[]{:S(2)}, u32[]{:S(2)}) collective-permute-start(bf16[16,1024]{1,0:T(8,128)(2,1)S(1)} %fusion.28), channel_id=1, source_target_pairs={{0,20},{1,21},{2,22},{3,23},{4,16},{5,17},{6,18},{7,19},{8,28},{9,... | collective-permute-start | bytes 98312 | tf_op jit(solution)/shard_map/ppermute | solution.py:29
  202.0 4.0 %collective-permute-start.53 = (bf16[16,1024]{1,0:T(8,128)(2,1)S(1)}, bf16[16,1024]{1,0:T(8,128)(2,1)S(1)}, u32[]{:S(2)}, u32[]{:S(2)}) collective-permute-start(bf16[16,1024]{1,0:T(8,128)(2,1)S(1)} %fusion.30), channel_id=1, source_target_pairs={{0,4},{1,5},{2,6},{3,7},{4,0},{5,1},{6,2},{7,3},{8,12},{9,13},{10,... | collective-permute-start | bytes 98312 | tf_op jit(solution)/shard_map/ppermute | solution.py:29
  206.4 17.8 %collective-permute-start.57 = (bf16[16,1024]{1,0:T(8,128)(2,1)S(1)}, bf16[16,1024]{1,0:T(8,128)(2,1)S(1)}, u32[]{:S(2)}, u32[]{:S(2)}) collective-permute-start(bf16[16,1024]{1,0:T(8,128)(2,1)S(1)} %get-tuple-element.69), channel_id=1, source_target_pairs={{0,12},{1,13},{2,14},{3,15},{4,8},{5,9},{6,10},{7,11},{8,4},{9,5},... | collective-permute-start | bytes 98312 | tf_op jit(solution)/shard_map/ppermute | solution.py:29
  206.5 6.9 %collective-permute-start.56 = (f32[16,128]{1,0:T(8,128)S(1)}, f32[16,128]{1,0:T(8,128)S(1)}, u32[]{:S(2)}, u32[]{:S(2)}) collective-permute-start(f32[16,128]{1,0:T(8,128)S(1)} %get-tuple-element.72), channel_id=1, source_target_pairs={{0,3},{1,2},{2,1},{3,0},{4,7},{5,6},{6,5},{7,4},{8,11},{9,10},{10,... | collective-permute-start | bytes 24584 | tf_op jit(solution)/shard_map/ppermute | solution.py:29
  207.7 7.6 %collective-permute-start.55 = (f32[16,128]{1,0:T(8,128)S(1)}, f32[16,128]{1,0:T(8,128)S(1)}, u32[]{:S(2)}, u32[]{:S(2)}) collective-permute-start(f32[16,128]{1,0:T(8,128)S(1)} %get-tuple-element.73), channel_id=1, source_target_pairs={{0,2},{1,3},{2,0},{3,1},{4,6},{5,7},{6,4},{7,5},{8,10},{9,11},{10,... | collective-permute-start | bytes 24584 | tf_op jit(solution)/shard_map/ppermute | solution.py:29
  207.7 7.7 %collective-permute-start.54 = (f32[16,128]{1,0:T(8,128)S(1)}, f32[16,128]{1,0:T(8,128)S(1)}, u32[]{:S(2)}, u32[]{:S(2)}) collective-permute-start(f32[16,128]{1,0:T(8,128)S(1)} %get-tuple-element.74), channel_id=1, source_target_pairs={{0,1},{1,0},{2,3},{3,2},{4,5},{5,4},{6,7},{7,6},{8,9},{9,8},{10,11... | collective-permute-start | bytes 24584 | tf_op jit(solution)/shard_map/ppermute | solution.py:29
  209.8 6.2 %collective-permute-start.62 = (bf16[16,512]{1,0:T(8,128)(2,1)S(1)}, bf16[16,512]{1,0:T(8,128)(2,1)S(1)}, u32[]{:S(2)}, u32[]{:S(2)}) collective-permute-start(bf16[16,512]{1,0:T(8,128)(2,1)S(1)} %get-tuple-element.88), channel_id=1, source_target_pairs={{16,0},{17,1},{18,2},{19,3},{20,4},{21,5},{22,6},{23,7},{24,8},{25... | collective-permute-start | bytes 49160 | tf_op jit(solution)/shard_map/ppermute | solution.py:29
  213.5 7.2 %collective-permute-start.61 = (bf16[16,512]{1,0:T(8,128)(2,1)S(1)}, bf16[16,512]{1,0:T(8,128)(2,1)S(1)}, u32[]{:S(2)}, u32[]{:S(2)}) collective-permute-start(bf16[16,512]{1,0:T(8,128)(2,1)S(1)} %get-tuple-element.87), channel_id=1, source_target_pairs={{16,4},{17,5},{18,6},{19,7},{20,0},{21,1},{22,2},{23,3},{24,12},{2... | collective-permute-start | bytes 49160 | tf_op jit(solution)/shard_map/ppermute | solution.py:29
  220.6 5.5 %collective-permute-start.65 = (f32[16,128]{1,0:T(8,128)S(1)}, f32[16,128]{1,0:T(8,128)S(1)}, u32[]{:S(2)}, u32[]{:S(2)}) collective-permute-start(f32[16,128]{1,0:T(8,128)S(1)} %get-tuple-element.84), channel_id=1, source_target_pairs={{0,3},{1,2},{2,1},{3,0},{4,7},{5,6},{6,5},{7,4},{8,11},{9,10},{10,... | collective-permute-start | bytes 24584 | tf_op jit(solution)/shard_map/ppermute | solution.py:29
  222.1 5.5 %collective-permute-start.64 = (f32[16,128]{1,0:T(8,128)S(1)}, f32[16,128]{1,0:T(8,128)S(1)}, u32[]{:S(2)}, u32[]{:S(2)}) collective-permute-start(f32[16,128]{1,0:T(8,128)S(1)} %get-tuple-element.85), channel_id=1, source_target_pairs={{0,2},{1,3},{2,0},{3,1},{4,6},{5,7},{6,4},{7,5},{8,10},{9,11},{10,... | collective-permute-start | bytes 24584 | tf_op jit(solution)/shard_map/ppermute | solution.py:29
  222.5 5.1 %collective-permute-start.63 = (f32[16,128]{1,0:T(8,128)S(1)}, f32[16,128]{1,0:T(8,128)S(1)}, u32[]{:S(2)}, u32[]{:S(2)}) collective-permute-start(f32[16,128]{1,0:T(8,128)S(1)} %get-tuple-element.86), channel_id=1, source_target_pairs={{0,1},{1,0},{2,3},{3,2},{4,5},{5,4},{6,7},{7,6},{8,9},{9,8},{10,11... | collective-permute-start | bytes 24584 | tf_op jit(solution)/shard_map/ppermute | solution.py:29
  224.2 4.4 %collective-permute-start.60 = (bf16[16,2048]{1,0:T(8,128)(2,1)S(1)}, bf16[16,2048]{1,0:T(8,128)(2,1)S(1)}, u32[]{:S(2)}, u32[]{:S(2)}) collective-permute-start(bf16[16,2048]{1,0:T(8,128)(2,1)S(1)} %fusion.39), channel_id=1, source_target_pairs={{0,3},{1,2},{2,1},{3,0},{4,7},{5,6},{6,5},{7,4},{8,11},{9,10},{10,... | collective-permute-start | bytes 196616 | tf_op jit(solution)/shard_map/ppermute | solution.py:29
  225.5 5.2 %collective-permute-start.59 = (bf16[16,2048]{1,0:T(8,128)(2,1)S(1)}, bf16[16,2048]{1,0:T(8,128)(2,1)S(1)}, u32[]{:S(2)}, u32[]{:S(2)}) collective-permute-start(bf16[16,2048]{1,0:T(8,128)(2,1)S(1)} %fusion.39), channel_id=1, source_target_pairs={{0,2},{1,3},{2,0},{3,1},{4,6},{5,7},{6,4},{7,5},{8,10},{9,11},{10,... | collective-permute-start | bytes 196616 | tf_op jit(solution)/shard_map/ppermute | solution.py:29
  226.1 4.7 %collective-permute-start.58 = (bf16[16,2048]{1,0:T(8,128)(2,1)S(1)}, bf16[16,2048]{1,0:T(8,128)(2,1)S(1)}, u32[]{:S(2)}, u32[]{:S(2)}) collective-permute-start(bf16[16,2048]{1,0:T(8,128)(2,1)S(1)} %fusion.39), channel_id=1, source_target_pairs={{0,1},{1,0},{2,3},{3,2},{4,5},{5,4},{6,7},{7,6},{8,9},{9,8},{10,11... | collective-permute-start | bytes 196616 | tf_op jit(solution)/shard_map/ppermute | solution.py:29
  (7 other events, 75.6 us)

commit v4 on v3

--- a/solution.py
+++ b/solution.py
@@ -88,44 +88,58 @@
             ]
 
 
-def inner_kernel(place, *refs):
-    *pieces, out = refs
-    inverse, coupling = pieces[:SIDE], pieces[SIDE:]
-    size = inverse[0].shape[0]
-    for j in range(SIDE):
-        for k in range(SIDE):
-            out[block_of(place[0] ^ j, size), block_of(place[1] ^ k, size)] = lax.dot_general(
-                inverse[j][...],
-                coupling[k][...],
-                (((1,), (1,)), ((), ())),
-                preferred_element_type=f32,
-            ).astype(bf16)
-
-
-def folded_kernel(place, *refs):
-    pieces, outs = refs[: 2 * SIDE], refs[2 * SIDE :]
-    coupling, inner = pieces[:SIDE], pieces[SIDE:]
-    size = inner[0].shape[0]
-    for j in range(SIDE):
-        total = jnp.zeros(outs[j].shape, f32)
-        for k in range(SIDE):
-            total = total + jnp.dot(
-                coupling[j][:, block_of(place[1] ^ k, size)],
-                inner[k][...],
-                preferred_element_type=f32,
-            )
-        outs[j][...] = total.astype(bf16)
-
-
 def schur_kernel(place, *refs):
     separator, *pieces, schur, narrow = refs
     size = schur.shape[0]
     for step in range(SIDE):
-        for row in range(SIDE):
-            columns = block_of(row * SIDE + (place[0] ^ step), size)
-            value = separator[:, columns] - pieces[step][:, row * size : (row + 1) * size].astype(f32)
+        for k in range(SIDE):
+            columns = block_of(k * place[1] + (place[0] ^ step) * place[2], size)
+            value = separator[:, columns] - pieces[step][:, k * size : (k + 1) * size].astype(f32)
             schur[:, columns] = value
             narrow[:, columns] = value.astype(bf16)
+
+
+def finish_kernel(place, narrow, weight, *refs):
+    *pieces, sweep, residual = refs
+    rows, nodes = narrow.shape
+    share = pieces[0].shape[0]
+    iterate = jnp.concatenate([piece[:, :nodes] for piece in pieces], axis=0)
+    terms = lax.dot_general(
+        iterate, narrow[...], (((1,), (1,)), ((), ())), preferred_element_type=f32
+    )
+    for step in range(SIDE):
+        extra = [
+            pieces[step][:, nodes + k * rows : nodes + (k + 1) * rows].astype(f32) for k in range(3)
+        ]
+        value = extra[1] + extra[2]
+        target = block_of(place[0] ^ step, share)
+        sweep[target, :] = value
+        residual[target, :] = (
+            value / weight[...] - terms[step * share : (step + 1) * share] - extra[0]
+        )
+
+
+def gather_groups(along_reduce):
+    groups = []
+    for p in range(PARTITIONS):
+        for k in range(SIDE):
+            if (p % 2 == 0) == along_reduce:
+                groups.append([p * PLANE + k * SIDE + x for x in range(SIDE)])
+            else:
+                groups.append([p * PLANE + y * SIDE + k for y in range(SIDE)])
+    return groups
+
+
+def gathered(array, along_reduce):
+    return lax.all_gather(
+        array, AXES, axis=0, tiled=True, axis_index_groups=gather_groups(along_reduce)
+    )
+
+
+def along_reduce(value, step):
+    return permuted(
+        value, lambda p, y, x: (p, y, x ^ step) if p % 2 == 0 else (p, y ^ step, x)
+    )
 
 
 def shards(interior_inverse, coupling, separator, link, source, weights):
@@ -141,6 +155,7 @@
     b = lax.axis_index("blk").astype(jnp.int32)
     y, x = b >> 2, b & 3
     even = (p & 1) == 0
+    r = jnp.where(even, x, y)
     pair = y >> 1
     ring = ((y + 1) >> 1) & 1
     out_place = jnp.where(even, y & 1, pair)
@@ -151,6 +166,15 @@
     away_high = jnp.where(even, 2 + ring, 3 - 2 * pair)
     place = jnp.stack([x, y])
 
+    coupling_in = gathered(coupling_rows, False)
+    inverse_out = gathered(inverse_rows, True)
+    turned = jnp.where(
+        even,
+        coupling_rows,
+        coupling_rows.reshape(rows, SIDE, SIDE, rows).transpose(0, 2, 1, 3).reshape(rows, nodes),
+    )
+    coupling_out = gathered(turned, True)
+
     def ordered(pieces):
         stacked = jnp.stack(pieces)
         return [
@@ -170,6 +194,11 @@
         [shape((rows, half), bf16)] * 2,
     )
     got = permuted(give, lambda p, y, x: (p, partner(p, y), x))
+    two = jnp.where(
+        out_place == 0, jnp.concatenate([keep, got]), jnp.concatenate([got, keep])
+    )
+    pieces = spread_x(two)
+    source_rows, weight_row = tie((source_rows, weight_row), two)
     started = weight_row[None, :] * source_rows
 
     def source_chunk(step):
@@ -179,12 +208,7 @@
     line_values = jnp.concatenate(ordered(exchange_x(source_chunk)), axis=1)
     line_weights = line_values[share : share + 1]
     away_weights = permuted(line_weights, lambda p, y, x: (p, partner(p, y), x))
-    two = jnp.where(
-        out_place == 0, jnp.concatenate([keep, got]), jnp.concatenate([got, keep])
-    )
-    (block,) = kernel_call(
-        assemble_link, place, spread_x(two), [shape((half, half), bf16)]
-    )
+    (block,) = kernel_call(assemble_link, place, pieces, [shape((half, half), bf16)])
     weight_half = jnp.where(
         out_place == 0,
         jnp.concatenate([line_weights, away_weights], axis=1),
@@ -197,46 +221,18 @@
         jnp.concatenate([zeros, line_values[:share]], axis=1),
     )
 
-    coupling_in = [coupling_rows] + [along_y(coupling_rows, step) for step in (1, 2, 3)]
-    inverse_out = spread_x(tie(inverse_rows, block))
-
     message = own.astype(bf16)
     final = message
     for turn in range(1, PARTITIONS):
         far, near = turn_messages(message, turn - 1)
         previous = (far.astype(f32) + near.astype(f32)).astype(bf16)
-        if turn == 6:
+        if turn == 8:
             inverse_out, coupling_in = tie((inverse_out, coupling_in), message)
-            (inner,) = kernel_call(
-                inner_kernel,
-                place,
-                inverse_out + coupling_in,
-                [shape((line, line), bf16)],
-                flops=2 * line * line * nodes,
-            )
-            inner_all = [inner] + [along_y(inner, step) for step in (1, 2, 3)]
-            coupling_out = spread_x(tie(coupling_rows, inner))
+            inner = lax.dot_general(
+                inverse_out, coupling_in, (((1,), (1,)), ((), ())), preferred_element_type=f32
+            ).astype(bf16)
+            inner_all = gathered(inner, False)
             previous = tie(previous, inner)
-        if turn == 12:
-            coupling_out, inner_all = tie((coupling_out, inner_all), message)
-            folded = kernel_call(
-                folded_kernel,
-                place,
-                coupling_out + inner_all,
-                [shape((rows, line), bf16)] * SIDE,
-                flops=2 * line * line * nodes,
-            )
-            back_rows = exchange_x(lambda step: folded[step])
-            previous = tie(previous, folded)
-        if turn == 14:
-            back_rows = tie(back_rows, message)
-            schur_rows, narrow = kernel_call(
-                schur_kernel,
-                place,
-                [separator_rows] + back_rows,
-                [shape((rows, nodes), f32), shape((rows, nodes), bf16)],
-            )
-            previous = tie(previous, schur_rows, narrow)
         product = lax.dot_general(
             previous, block, (((1,), (1,)), ((), ())), preferred_element_type=f32
         )
@@ -252,15 +248,10 @@
     mine = lax.dynamic_slice(back, (0, in_place * line), (share, line))
     theirs = lax.dynamic_slice(back, (0, (1 - in_place) * line), (share, line))
     later = range(1, PARTITIONS)
-    following_line = permuted(
+    following = permuted(
         theirs, lambda p, y, x: (p - 1, other(p, y), x), later
     ).astype(f32) + permuted(mine, lambda p, y, x: (p - 1, y, x), later).astype(f32)
-
-    def own_shard(line_array):
-        pieces = exchange_x(
-            lambda step: lax.dynamic_slice(line_array, (0, (x ^ step) * rows), (share, rows))
-        )
-        return jnp.concatenate(ordered(pieces), axis=0)
+    following = following.astype(bf16)
 
     rest = permuted(rounded, lambda p, y, x: (p, other(p, y), x))
     m0, m1, r0, r1 = rounded[:, :line], rounded[:, line:], rest[:, :line], rest[:, line:]
@@ -277,16 +268,40 @@
             jnp.concatenate([r0, m0, m1, r1], axis=1),
         ),
     )
-    terms = lax.dot_general(
-        jnp.concatenate(spread_x(lines)),
-        narrow,
-        (((1,), (1,)), ((), ())),
-        preferred_element_type=f32,
-    ).reshape(SIDE, share, rows)
-    own_terms = jnp.concatenate(ordered([terms[step] for step in range(SIDE)]), axis=0)
-    sweep = own_shard(lax.dynamic_slice(total, (0, out_place * line), (share, line)))
-    following = own_shard(following_line)
-    residual = sweep / weight_row[None, :] - own_terms - following
+    sweep_line = lax.dynamic_slice(total, (0, out_place * line), (share, line))
+    sweep_high = sweep_line.astype(bf16)
+    sweep_low = (sweep_line - sweep_high.astype(f32)).astype(bf16)
+
+    def last_chunk(step):
+        start = (0, (x ^ step) * rows)
+        extra = [
+            lax.dynamic_slice(array, start, (share, rows))
+            for array in (following, sweep_high, sweep_low)
+        ]
+        return jnp.concatenate([lines] + extra, axis=1)
+
+    last = exchange_x(last_chunk)
+
+    coupling_out, inner_all = tie((coupling_out, inner_all), lines)
+    folded = jnp.dot(coupling_out, inner_all, preferred_element_type=f32).astype(bf16)
+
+    def folded_chunk(step):
+        return lax.dynamic_slice(folded, ((r ^ step) * rows, 0), (rows, line))
+
+    back_rows = [folded_chunk(0)] + [along_reduce(folded_chunk(s), s) for s in (1, 2, 3)]
+    schur_rows, narrow = kernel_call(
+        schur_kernel,
+        jnp.stack([r, jnp.where(even, SIDE, 1), jnp.where(even, 1, SIDE)]),
+        [separator_rows] + back_rows,
+        [shape((rows, nodes), f32), shape((rows, nodes), bf16)],
+    )
+    sweep, residual = kernel_call(
+        finish_kernel,
+        place,
+        [narrow, weight_row[None, :]] + last,
+        [shape((keys, rows), f32)] * 2,
+        flops=2 * keys * rows * nodes,
+    )
     return schur_rows[None], sweep[None], residual[None]
 
 

time: 237 us -> 175 us (0.74)
  the two profiles are of different devices: /device:TPU:161 before, /device:TPU:224 now
where the time goes in v4:
time: 175 us; the launch traced here: 173 us
  waiting for transfers between devices  81.4 us (47%)
  starting transfers between devices  49.4 us (28%)
  matrix products  17.9 us (10%)
  between operations  14.3 us (8%)
  Pallas kernels  4.48 us (3%)
  local copies, waits for them, and re-layouts  3.99 us (2%)
    ppermute x48, waiting for transfers between devices, permuted(): return lax.ppermute(value, AXES, pairs)  69.1 us
    ppermute x48, starting transfers between devices, permuted(): return lax.ppermute(value, AXES, pairs)  49.2 us
    all_gather x4, waiting for transfers between devices, gathered(): lax.all_gather(array, AXES, axis=0, tiled=True, axis_index_groups=gather_...  10.9 us
    dot_general x15, matrix products, shards(): lax.dot_general(previous, block, (((1,), (1,)), ((), ())), preferred_elem...  9.77 us
    pallas_call x4, Pallas kernels, kernel_call(): pl.pallas_call(body, out_shape=out_shapes, in_specs=[pl.BlockSpec(memory_...  4.48 us
    dot_general x1, matrix products, shards(): lax.dot_general(inverse_out, coupling_in, (((1,), (1,)), ((), ())), prefe...  4.3 us
  transfers between devices with their start and end apart: 52, of which 20 were waited for; matrix products, arithmetic and copies ran while one was open for 11% of the time, Pallas kernels for 2%

profile of v4, /device:TPU:224, one launch (start us, length us, event | category | flops | bytes accessed | tf_op | source)
XLA Modules:
  0.0 172.9 jit_solution(16316725945582065920)
XLA Ops:
  7.2 0.7 all-gather.11.cloned.1.call-update
  8.0 0.7 all-gather.13.cloned.1.call-update
  8.8 1.0 copy-done.1
  10.5 1.7 collective-permute-start
  12.1 4.8 %collective-permute-done = bf16[128,1024]{1,0:T(8,128)(2,1)S(1)} collective-permute-done((bf16[128,1024]{1,0:T(8,128)(2,1)S(1)}, bf16[128,1024]{1,0:T(8,128)(2,1)S(1)}, u32[]{:S(2)}, u32[]{:S(2)}) %collective-permute-start) | collective-permute-done | bytes 262176 | tf_op jit(solution)/shard_map/ppermute | solution.py:29
  17.1 1.6 collective-permute-start.1
  18.7 2.7 %collective-permute-start.2 = (f32[24,128]{1,0:T(8,128)S(1)}, f32[24,128]{1,0:T(8,128)S(1)}, u32[]{:S(2)}, u32[]{:S(2)}) collective-permute-start(f32[24,128]{1,0:T(8,128)S(1)} %get-tuple-element.69), channel_id=1, source_target_pairs={{0,2},{1,3},{2,0},{3,1},{4,6},{5,7},{6,4},{7,5},{8,10},{9,11},{10,... | collective-permute-start | bytes 36872 | tf_op jit(solution)/shard_map/ppermute | solution.py:29
  22.3 3.9 %collective-permute-start.8 = (bf16[256,1024]{1,0:T(8,128)(2,1)S(1)}, bf16[256,1024]{1,0:T(8,128)(2,1)S(1)}, u32[]{:S(2)}, u32[]{:S(2)}) collective-permute-start(bf16[256,1024]{1,0:T(8,128)(2,1)S(1)} %maximum_select_fusion.refs_0_), channel_id=1, source_target_pairs={{0,2},{1,3},{2,0},{3,1},{4,6},{5,7},{6,4},{7,5},{8,10},{9,11},{10,... | collective-permute-start | bytes 1572872 | tf_op jit(solution)/shard_map/ppermute | solution.py:29
  26.8 1.7 collective-permute-start.4
  28.6 1.9 %collective-permute-done.4 = f32[1,512]{1,0:T(1,128)S(1)} collective-permute-done((f32[1,512]{1,0:T(1,128)S(1)}, f32[1,512]{1,0:T(1,128)S(1)}, u32[]{:S(2)}, u32[]{:S(2)}) %collective-permute-start.4) | collective-permute-done | bytes 2080 | tf_op jit(solution)/shard_map/ppermute | solution.py:29
  30.5 11.9 %collective-permute-done.7.refs_1_ = bf16[256,1024]{1,0:T(8,128)(2,1)S(1)} collective-permute-done((bf16[256,1024]{1,0:T(8,128)(2,1)S(1)}, bf16[256,1024]{1,0:T(8,128)(2,1)S(1)}, u32[]{:S(2)}, u32[]{:S(2)}) %collective-permute-start.7) | collective-permute-done | bytes 524320 | tf_op jit(solution)/shard_map/ppermute | solution.py:29
  42.4 14.5 %collective-permute-done.8.refs_2_ = bf16[256,1024]{1,0:T(8,128)(2,1)S(1)} collective-permute-done((bf16[256,1024]{1,0:T(8,128)(2,1)S(1)}, bf16[256,1024]{1,0:T(8,128)(2,1)S(1)}, u32[]{:S(2)}, u32[]{:S(2)}) %collective-permute-start.8) | collective-permute-done | bytes 524320 | tf_op jit(solution)/shard_map/ppermute | solution.py:29
  57.4 0.7 shard_map.86
  58.2 0.7 fusion.15
  58.8 0.7 collective-permute-start.10
  59.5 0.7 collective-permute-start.11
  60.5 1.0 copy.9
  61.5 1.4 reshape.44
  63.0 0.7 fusion.16
  63.6 1.6 collective-permute-start.13
  65.2 0.8 bitcast_select_fusion
  66.2 1.2 collective-permute-done.12
  68.0 0.7 collective-permute-start.14
  68.7 0.7 collective-permute-start.15
  69.4 0.7 fusion.18
  70.0 1.2 collective-permute-start.17
  71.3 2.1 %collective-permute-done.16 = bf16[16,1024]{1,0:T(8,128)(2,1)S(1)} collective-permute-done((bf16[16,1024]{1,0:T(8,128)(2,1)S(1)}, bf16[16,1024]{1,0:T(8,128)(2,1)S(1)}, u32[]{:S(2)}, u32[]{:S(2)}) %collective-permute-start.16) | collective-permute-done | bytes 32800 | tf_op jit(solution)/shard_map/ppermute | solution.py:29
  74.1 0.7 collective-permute-start.18
  74.7 0.7 collective-permute-start.19
  75.4 0.7 fusion.20
  76.1 1.2 collective-permute-start.21
  77.3 2.6 %collective-permute-done.20 = bf16[16,1024]{1,0:T(8,128)(2,1)S(1)} collective-permute-done((bf16[16,1024]{1,0:T(8,128)(2,1)S(1)}, bf16[16,1024]{1,0:T(8,128)(2,1)S(1)}, u32[]{:S(2)}, u32[]{:S(2)}) %collective-permute-start.20) | collective-permute-done | bytes 32800 | tf_op jit(solution)/shard_map/ppermute | solution.py:29
  80.5 0.7 collective-permute-start.22
  81.2 0.7 collective-permute-start.23
  81.9 4.4 %all-gather.13.cloned.1.call-done = bf16[1,512,2048]{2,1,0:T(8,128)(2,1)} async-done(((bf16[1,128,2048]{2,1,0:T(8,128)(2,1)}), bf16[1,512,2048]{2,1,0:T(8,128)(2,1)}) %all-gather.13.cloned.1.call-update) | async-done | bytes 2097168 | tf_op jit(solution)/shard_map/all_gather | solution.py:134
  86.3 4.3 %convolution_convert_fusion.1 = bf16[512,512]{1,0:T(8,128)(2,1)} fusion(bf16[512,2048]{1,0:T(8,128)(2,1)} %bitcast.70, bf16[512,2048]{1,0:T(8,128)(2,1)} %bitcast.71), kind=kOutput, calls=%fused_computation.1 | convolution fusion | flops 1074003968 | bytes 4718592 | tf_op jit(solution)/shard_map/dot_general | solution.py:231
  91.8 2.8 %collective-permute-done.24 = bf16[16,1024]{1,0:T(8,128)(2,1)S(1)} collective-permute-done((bf16[16,1024]{1,0:T(8,128)(2,1)S(1)}, bf16[16,1024]{1,0:T(8,128)(2,1)S(1)}, u32[]{:S(2)}, u32[]{:S(2)}) %collective-permute-start.24) | collective-permute-done | bytes 32800 | tf_op jit(solution)/shard_map/ppermute | solution.py:29
  95.3 0.7 collective-permute-start.26
  96.0 0.7 collective-permute-start.27
  96.7 0.7 fusion.24
  98.1 2.6 %collective-permute-done.28 = bf16[16,1024]{1,0:T(8,128)(2,1)S(1)} collective-permute-done((bf16[16,1024]{1,0:T(8,128)(2,1)S(1)}, bf16[16,1024]{1,0:T(8,128)(2,1)S(1)}, u32[]{:S(2)}, u32[]{:S(2)}) %collective-permute-start.28) | collective-permute-done | bytes 32800 | tf_op jit(solution)/shard_map/ppermute | solution.py:29
  101.3 0.7 collective-permute-start.30
  102.0 0.7 collective-permute-start.31
  104.2 2.9 %collective-permute-done.32 = bf16[16,1024]{1,0:T(8,128)(2,1)S(1)} collective-permute-done((bf16[16,1024]{1,0:T(8,128)(2,1)S(1)}, bf16[16,1024]{1,0:T(8,128)(2,1)S(1)}, u32[]{:S(2)}, u32[]{:S(2)}) %collective-permute-start.32) | collective-permute-done | bytes 32800 | tf_op jit(solution)/shard_map/ppermute | solution.py:29
  107.7 1.3 collective-permute-start.34
  109.0 1.3 collective-permute-start.35
  110.3 13.4 %collective-permute-done.34 = bf16[16,1024]{1,0:T(8,128)(2,1)S(1)} collective-permute-done((bf16[16,1024]{1,0:T(8,128)(2,1)S(1)}, bf16[16,1024]{1,0:T(8,128)(2,1)S(1)}, u32[]{:S(2)}, u32[]{:S(2)}) %collective-permute-start.34) | collective-permute-done | bytes 32800 | tf_op jit(solution)/shard_map/ppermute | solution.py:29
  124.4 2.3 %collective-permute-start.37 = (bf16[16,1024]{1,0:T(8,128)(2,1)S(1)}, bf16[16,1024]{1,0:T(8,128)(2,1)S(1)}, u32[]{:S(2)}, u32[]{:S(2)}) collective-permute-start(bf16[16,1024]{1,0:T(8,128)(2,1)S(1)} %fusion.28), channel_id=1, source_target_pairs={{0,16},{1,17},{2,18},{3,19},{4,20},{5,21},{6,22},{7,23},{8,24},{9,... | collective-permute-start | bytes 98312 | tf_op jit(solution)/shard_map/ppermute | solution.py:29
  126.6 1.1 collective-permute-done.36
  127.7 0.7 fusion.30
  128.4 2.1 %collective-permute-start.38 = (bf16[16,1024]{1,0:T(8,128)(2,1)S(1)}, bf16[16,1024]{1,0:T(8,128)(2,1)S(1)}, u32[]{:S(2)}, u32[]{:S(2)}) collective-permute-start(bf16[16,1024]{1,0:T(8,128)(2,1)S(1)} %fusion.30), channel_id=1, source_target_pairs={{0,4},{1,5},{2,6},{3,7},{4,0},{5,1},{6,2},{7,3},{8,12},{9,13},{10,... | collective-permute-start | bytes 98312 | tf_op jit(solution)/shard_map/ppermute | solution.py:29
  130.5 1.9 %collective-permute-done.38 = bf16[16,1024]{1,0:T(8,128)(2,1)S(1)} collective-permute-done((bf16[16,1024]{1,0:T(8,128)(2,1)S(1)}, bf16[16,1024]{1,0:T(8,128)(2,1)S(1)}, u32[]{:S(2)}, u32[]{:S(2)}) %collective-permute-start.38) | collective-permute-done | bytes 32800 | tf_op jit(solution)/shard_map/ppermute | solution.py:29
  132.4 1.8 %collective-permute-start.39 = (bf16[16,1024]{1,0:T(8,128)(2,1)S(1)}, bf16[16,1024]{1,0:T(8,128)(2,1)S(1)}, u32[]{:S(2)}, u32[]{:S(2)}) collective-permute-start(bf16[16,1024]{1,0:T(8,128)(2,1)S(1)} %get-tuple-element.40), channel_id=1, source_target_pairs={{0,12},{1,13},{2,14},{3,15},{4,8},{5,9},{6,10},{7,11},{8,4},{9,5},... | collective-permute-start | bytes 98312 | tf_op jit(solution)/shard_map/ppermute | solution.py:29
  134.6 1.9 %collective-permute-start.43 = (bf16[16,512]{1,0:T(8,128)(2,1)S(1)}, bf16[16,512]{1,0:T(8,128)(2,1)S(1)}, u32[]{:S(2)}, u32[]{:S(2)}) collective-permute-start(bf16[16,512]{1,0:T(8,128)(2,1)S(1)} %get-tuple-element.45), channel_id=1, source_target_pairs={{16,4},{17,5},{18,6},{19,7},{20,0},{21,1},{22,2},{23,3},{24,12},{2... | collective-permute-start | bytes 49160 | tf_op jit(solution)/shard_map/ppermute | solution.py:29
  136.6 1.9 %collective-permute-start.44 = (bf16[16,512]{1,0:T(8,128)(2,1)S(1)}, bf16[16,512]{1,0:T(8,128)(2,1)S(1)}, u32[]{:S(2)}, u32[]{:S(2)}) collective-permute-start(bf16[16,512]{1,0:T(8,128)(2,1)S(1)} %get-tuple-element.46), channel_id=1, source_target_pairs={{16,0},{17,1},{18,2},{19,3},{20,4},{21,5},{22,6},{23,7},{24,8},{25... | collective-permute-start | bytes 49160 | tf_op jit(solution)/shard_map/ppermute | solution.py:29
  138.6 1.2 collective-permute-done.43
  140.0 6.4 %all-gather.9.cloned.1.call-done = bf16[2048,512]{1,0:T(8,128)(2,1)} async-done(((bf16[512,512]{1,0:T(8,128)(2,1)}), bf16[2048,512]{1,0:T(8,128)(2,1)}) %all-gather.9.cloned.1.call-update) | async-done | bytes 2097168 | tf_op jit(solution)/shard_map/all_gather | solution.py:134
  146.5 3.5 %convolution_convert_fusion = bf16[512,512]{1,0:T(8,128)(2,1)S(1)} fusion(bf16[512,2048]{1,0:T(8,128)(2,1)} %all-gather.7.cloned.1.call-done, bf16[2048,512]{1,0:T(8,128)(2,1)} %all-gather.9.cloned.1.call-done), kind=kOutput, calls=%fused_computation | convolution fusion | flops 1074003968 | bytes 4718592 | tf_op jit(solution)/shard_map/dot_general | solution.py:286
  150.0 1.7 collective-permute-start.40
  151.7 2.7 %collective-permute-start.41 = (bf16[128,512]{1,0:T(8,128)(2,1)S(1)}, bf16[128,512]{1,0:T(8,128)(2,1)S(1)}, u32[]{:S(2)}, u32[]{:S(2)}) collective-permute-start(bf16[128,512]{1,0:T(8,128)(2,1)S(1)} %get-tuple-element.32), channel_id=1, source_target_pairs={{0,2},{1,3},{2,0},{3,1},{4,6},{5,7},{6,4},{7,5},{8,10},{9,11},{10,... | collective-permute-start | bytes 393224 | tf_op jit(solution)/shard_map/ppermute | solution.py:29
  155.3 3.9 %collective-permute-start.46 = (bf16[16,2432]{1,0:T(8,128)(2,1)S(1)}, bf16[16,2432]{1,0:T(8,128)(2,1)S(1)}, u32[]{:S(2)}, u32[]{:S(2)}) collective-permute-start(bf16[16,2432]{1,0:T(8,128)(2,1)S(1)} %get-tuple-element.37), channel_id=1, source_target_pairs={{0,2},{1,3},{2,0},{3,1},{4,6},{5,7},{6,4},{7,5},{8,10},{9,11},{10,... | collective-permute-start | bytes 233480 | tf_op jit(solution)/shard_map/ppermute | solution.py:29
  160.3 2.8 %collective-permute-done.42.refs_4_ = bf16[128,512]{1,0:T(8,128)(2,1)S(1)} collective-permute-done((bf16[128,512]{1,0:T(8,128)(2,1)S(1)}, bf16[128,512]{1,0:T(8,128)(2,1)S(1)}, u32[]{:S(2)}, u32[]{:S(2)}) %collective-permute-start.42) | collective-permute-done | bytes 131104 | tf_op jit(solution)/shard_map/ppermute | solution.py:29
  163.1 1.8 %shard_map.87 = (f32[128,2048]{1,0:T(8,128)}, bf16[128,2048]{1,0:T(8,128)(2,1)S(1)}) custom-call(s32[3]{0:T(128)S(1)} %pad_add_fusion.place, f32[128,2048]{1,0:T(8,128)S(1)} %bitcast.59, bf16[128,512]{1,0:T(8,128)(2,1)S(1)} %get-tuple-element.34.refs_1_, bf16[128,512]{1,0:T(8,128)(2,1)S(1)} %collective-permute-done.40.refs_2_, ...), custom_call_target="tpu_custom_call" | custom-call | bytes 3145728 | tf_op jit(solution)/shard_map/pallas_call | solution.py:58
  164.9 1.5 shard_map.88
  (107 shorter events, 14.2 us)
Async XLA Ops:
  7.2 9.9 %copy-start.4 = (f32[1,64,128]{2,1,0:T(8,128)S(1)}, f32[1,64,128]{2,1,0:T(8,128)}, u32[]{:S(2)}) copy-start(f32[1,64,128]{2,1,0:T(8,128)} %param.10) | copy-start | bytes 98308
  7.2 9.9 %copy-start.2 = (f32[1,128]{1,0:T(1,128)S(1)}, f32[1,128]{1,0:T(1,128)}, u32[]{:S(2)}) copy-start(f32[1,128]{1,0:T(1,128)} %param.11) | copy-start | bytes 1540
  7.2 74.7 %all-gather.11.cloned.1.call-start = ((), (), s32[]{:S(2)}) async-start(), calls=%async_computation.2 | async-start | bytes 2621440 | tf_op jit(solution)/shard_map/all_gather | solution.py:134
  7.9 78.4 %all-gather.13.cloned.1.call-start = ((), (), s32[]{:S(2)}) async-start(), calls=%async_computation.3 | async-start | bytes 2621440 | tf_op jit(solution)/shard_map/all_gather | solution.py:134
  8.7 131.3 %all-gather.7.cloned.1.call-start = ((), (), s32[]{:S(2)}) async-start(), calls=%async_computation | async-start | bytes 2621440 | tf_op jit(solution)/shard_map/all_gather | solution.py:134
  8.8 1.0 copy-start.1
  10.5 6.5 %collective-permute-start = (bf16[128,1024]{1,0:T(8,128)(2,1)S(1)}, bf16[128,1024]{1,0:T(8,128)(2,1)S(1)}, u32[]{:S(2)}, u32[]{:S(2)}) collective-permute-start(bf16[128,1024]{1,0:T(8,128)(2,1)S(1)} %get-tuple-element.17), channel_id=1, source_target_pairs={{0,4},{1,5},{2,6},{3,7},{4,0},{5,1},{6,2},{7,3},{8,12},{9,13},{10,... | collective-permute-start | bytes 786440 | tf_op jit(solution)/shard_map/ppermute | solution.py:29
  17.1 9.1 %collective-permute-start.1 = (f32[24,128]{1,0:T(8,128)S(1)}, f32[24,128]{1,0:T(8,128)S(1)}, u32[]{:S(2)}, u32[]{:S(2)}) collective-permute-start(f32[24,128]{1,0:T(8,128)S(1)} %get-tuple-element.68), channel_id=1, source_target_pairs={{0,1},{1,0},{2,3},{3,2},{4,5},{5,4},{6,7},{7,6},{8,9},{9,8},{10,11... | collective-permute-start | bytes 36872 | tf_op jit(solution)/shard_map/ppermute | solution.py:29
  18.7 8.0 %collective-permute-start.2 = (f32[24,128]{1,0:T(8,128)S(1)}, f32[24,128]{1,0:T(8,128)S(1)}, u32[]{:S(2)}, u32[]{:S(2)}) collective-permute-start(f32[24,128]{1,0:T(8,128)S(1)} %get-tuple-element.69), channel_id=1, source_target_pairs={{0,2},{1,3},{2,0},{3,1},{4,6},{5,7},{6,4},{7,5},{8,10},{9,11},{10,... | collective-permute-start | bytes 36872 | tf_op jit(solution)/shard_map/ppermute | solution.py:29
  21.4 5.3 %collective-permute-start.3 = (f32[24,128]{1,0:T(8,128)S(1)}, f32[24,128]{1,0:T(8,128)S(1)}, u32[]{:S(2)}, u32[]{:S(2)}) collective-permute-start(f32[24,128]{1,0:T(8,128)S(1)} %get-tuple-element.70), channel_id=1, source_target_pairs={{0,3},{1,2},{2,1},{3,0},{4,7},{5,6},{6,5},{7,4},{8,11},{9,10},{10,... | collective-permute-start | bytes 36872 | tf_op jit(solution)/shard_map/ppermute | solution.py:29
  22.0 20.4 %collective-permute-start.7 = (bf16[256,1024]{1,0:T(8,128)(2,1)S(1)}, bf16[256,1024]{1,0:T(8,128)(2,1)S(1)}, u32[]{:S(2)}, u32[]{:S(2)}) collective-permute-start(bf16[256,1024]{1,0:T(8,128)(2,1)S(1)} %maximum_select_fusion.refs_0_), channel_id=1, source_target_pairs={{0,1},{1,0},{2,3},{3,2},{4,5},{5,4},{6,7},{7,6},{8,9},{9,8},{10,11... | collective-permute-start | bytes 1572872 | tf_op jit(solution)/shard_map/ppermute | solution.py:29
  22.3 34.6 %collective-permute-start.8 = (bf16[256,1024]{1,0:T(8,128)(2,1)S(1)}, bf16[256,1024]{1,0:T(8,128)(2,1)S(1)}, u32[]{:S(2)}, u32[]{:S(2)}) collective-permute-start(bf16[256,1024]{1,0:T(8,128)(2,1)S(1)} %maximum_select_fusion.refs_0_), channel_id=1, source_target_pairs={{0,2},{1,3},{2,0},{3,1},{4,6},{5,7},{6,4},{7,5},{8,10},{9,11},{10,... | collective-permute-start | bytes 1572872 | tf_op jit(solution)/shard_map/ppermute | solution.py:29
  26.2 31.2 %collective-permute-start.9 = (bf16[256,1024]{1,0:T(8,128)(2,1)S(1)}, bf16[256,1024]{1,0:T(8,128)(2,1)S(1)}, u32[]{:S(2)}, u32[]{:S(2)}) collective-permute-start(bf16[256,1024]{1,0:T(8,128)(2,1)S(1)} %maximum_select_fusion.refs_0_), channel_id=1, source_target_pairs={{0,3},{1,2},{2,1},{3,0},{4,7},{5,6},{6,5},{7,4},{8,11},{9,10},{10,... | collective-permute-start | bytes 1572872 | tf_op jit(solution)/shard_map/ppermute | solution.py:29
  26.8 3.7 %collective-permute-start.4 = (f32[1,512]{1,0:T(1,128)S(1)}, f32[1,512]{1,0:T(1,128)S(1)}, u32[]{:S(2)}, u32[]{:S(2)}) collective-permute-start(f32[1,512]{1,0:T(1,128)S(1)} %pad_maximum_fusion.10), channel_id=1, source_target_pairs={{0,4},{1,5},{2,6},{3,7},{4,0},{5,1},{6,2},{7,3},{8,12},{9,13},{10,... | collective-permute-start | bytes 6152 | tf_op jit(solution)/shard_map/ppermute | solution.py:29
  28.5 29.7 %collective-permute-start.5 = (bf16[16,1024]{1,0:T(8,128)(2,1)S(1)}, bf16[16,1024]{1,0:T(8,128)(2,1)S(1)}, u32[]{:S(2)}, u32[]{:S(2)}) collective-permute-start(bf16[16,1024]{1,0:T(8,128)(2,1)S(1)} %fusion.32), channel_id=1, source_target_pairs={{0,20},{1,21},{2,22},{3,23},{4,16},{5,17},{6,18},{7,19},{8,28},{9,... | collective-permute-start | bytes 98312 | tf_op jit(solution)/shard_map/ppermute | solution.py:29
  30.4 27.7 %collective-permute-start.6 = (bf16[16,1024]{1,0:T(8,128)(2,1)S(1)}, bf16[16,1024]{1,0:T(8,128)(2,1)S(1)}, u32[]{:S(2)}, u32[]{:S(2)}) collective-permute-start(bf16[16,1024]{1,0:T(8,128)(2,1)S(1)} %fusion.32), channel_id=1, source_target_pairs={{0,16},{1,17},{2,18},{3,19},{4,20},{5,21},{6,22},{7,23},{8,24},{9,... | collective-permute-start | bytes 98312 | tf_op jit(solution)/shard_map/ppermute | solution.py:29
  58.1 2.0 %copy-start.3 = (bf16[1,128,2048]{2,1,0:T(8,128)(2,1)S(1)}, bf16[1,128,2048]{2,1,0:T(8,128)(2,1)}, u32[]{:S(2)}) copy-start(bf16[1,128,2048]{2,1,0:T(8,128)(2,1)} %param.7) | copy-start | bytes 1572868
  58.8 4.2 %collective-permute-start.10 = (bf16[16,1024]{1,0:T(8,128)(2,1)S(1)}, bf16[16,1024]{1,0:T(8,128)(2,1)S(1)}, u32[]{:S(2)}, u32[]{:S(2)}) collective-permute-start(bf16[16,1024]{1,0:T(8,128)(2,1)S(1)} %fusion.15), channel_id=1, source_target_pairs={{16,44},{17,45},{18,46},{19,47},{20,40},{21,41},{22,42},{23,43},{2... | collective-permute-start | bytes 98312 | tf_op jit(solution)/shard_map/ppermute | solution.py:29
  59.5 3.5 %collective-permute-start.11 = (bf16[16,1024]{1,0:T(8,128)(2,1)S(1)}, bf16[16,1024]{1,0:T(8,128)(2,1)S(1)}, u32[]{:S(2)}, u32[]{:S(2)}) collective-permute-start(bf16[16,1024]{1,0:T(8,128)(2,1)S(1)} %fusion.15), channel_id=1, source_target_pairs={{16,32},{17,33},{18,34},{19,35},{20,36},{21,37},{22,38},{23,39},{2... | collective-permute-start | bytes 98312 | tf_op jit(solution)/shard_map/ppermute | solution.py:29
  63.6 3.7 %collective-permute-start.12 = (bf16[16,1024]{1,0:T(8,128)(2,1)S(1)}, bf16[16,1024]{1,0:T(8,128)(2,1)S(1)}, u32[]{:S(2)}, u32[]{:S(2)}) collective-permute-start(bf16[16,1024]{1,0:T(8,128)(2,1)S(1)} %fusion.16), channel_id=1, source_target_pairs={{0,20},{1,21},{2,22},{3,23},{4,16},{5,17},{6,18},{7,19},{8,28},{9,... | collective-permute-start | bytes 98312 | tf_op jit(solution)/shard_map/ppermute | solution.py:29
  63.6 3.7 %collective-permute-start.13 = (bf16[16,1024]{1,0:T(8,128)(2,1)S(1)}, bf16[16,1024]{1,0:T(8,128)(2,1)S(1)}, u32[]{:S(2)}, u32[]{:S(2)}) collective-permute-start(bf16[16,1024]{1,0:T(8,128)(2,1)S(1)} %fusion.16), channel_id=1, source_target_pairs={{0,16},{1,17},{2,18},{3,19},{4,20},{5,21},{6,22},{7,23},{8,24},{9,... | collective-permute-start | bytes 98312 | tf_op jit(solution)/shard_map/ppermute | solution.py:29
  66.1 80.4 %all-gather.9.cloned.1.call-start = ((), (), s32[]{:S(2)}) async-start(), calls=%async_computation.1 | async-start | bytes 2621440 | tf_op jit(solution)/shard_map/all_gather | solution.py:134
  68.0 1.3 collective-permute-start.14
  68.7 0.7 collective-permute-start.15
  70.0 3.4 %collective-permute-start.16 = (bf16[16,1024]{1,0:T(8,128)(2,1)S(1)}, bf16[16,1024]{1,0:T(8,128)(2,1)S(1)}, u32[]{:S(2)}, u32[]{:S(2)}) collective-permute-start(bf16[16,1024]{1,0:T(8,128)(2,1)S(1)} %fusion.18), channel_id=1, source_target_pairs={{0,20},{1,21},{2,22},{3,23},{4,16},{5,17},{6,18},{7,19},{8,28},{9,... | collective-permute-start | bytes 98312 | tf_op jit(solution)/shard_map/ppermute | solution.py:29
  70.0 3.4 %collective-permute-start.17 = (bf16[16,1024]{1,0:T(8,128)(2,1)S(1)}, bf16[16,1024]{1,0:T(8,128)(2,1)S(1)}, u32[]{:S(2)}, u32[]{:S(2)}) collective-permute-start(bf16[16,1024]{1,0:T(8,128)(2,1)S(1)} %fusion.18), channel_id=1, source_target_pairs={{0,16},{1,17},{2,18},{3,19},{4,20},{5,21},{6,22},{7,23},{8,24},{9,... | collective-permute-start | bytes 98312 | tf_op jit(solution)/shard_map/ppermute | solution.py:29
  74.1 1.3 collective-permute-start.18
  74.7 0.7 collective-permute-start.19
  76.1 3.8 %collective-permute-start.20 = (bf16[16,1024]{1,0:T(8,128)(2,1)S(1)}, bf16[16,1024]{1,0:T(8,128)(2,1)S(1)}, u32[]{:S(2)}, u32[]{:S(2)}) collective-permute-start(bf16[16,1024]{1,0:T(8,128)(2,1)S(1)} %fusion.20), channel_id=1, source_target_pairs={{0,20},{1,21},{2,22},{3,23},{4,16},{5,17},{6,18},{7,19},{8,28},{9,... | collective-permute-start | bytes 98312 | tf_op jit(solution)/shard_map/ppermute | solution.py:29
  76.1 3.8 %collective-permute-start.21 = (bf16[16,1024]{1,0:T(8,128)(2,1)S(1)}, bf16[16,1024]{1,0:T(8,128)(2,1)S(1)}, u32[]{:S(2)}, u32[]{:S(2)}) collective-permute-start(bf16[16,1024]{1,0:T(8,128)(2,1)S(1)} %fusion.20), channel_id=1, source_target_pairs={{0,16},{1,17},{2,18},{3,19},{4,20},{5,21},{6,22},{7,23},{8,24},{9,... | collective-permute-start | bytes 98312 | tf_op jit(solution)/shard_map/ppermute | solution.py:29
  80.5 1.3 collective-permute-start.22
  81.2 0.7 collective-permute-start.23
  91.3 3.4 %collective-permute-start.24 = (bf16[16,1024]{1,0:T(8,128)(2,1)S(1)}, bf16[16,1024]{1,0:T(8,128)(2,1)S(1)}, u32[]{:S(2)}, u32[]{:S(2)}) collective-permute-start(bf16[16,1024]{1,0:T(8,128)(2,1)S(1)} %fusion.22), channel_id=1, source_target_pairs={{0,20},{1,21},{2,22},{3,23},{4,16},{5,17},{6,18},{7,19},{8,28},{9,... | collective-permute-start | bytes 98312 | tf_op jit(solution)/shard_map/ppermute | solution.py:29
  91.3 3.4 %collective-permute-start.25 = (bf16[16,1024]{1,0:T(8,128)(2,1)S(1)}, bf16[16,1024]{1,0:T(8,128)(2,1)S(1)}, u32[]{:S(2)}, u32[]{:S(2)}) collective-permute-start(bf16[16,1024]{1,0:T(8,128)(2,1)S(1)} %fusion.22), channel_id=1, source_target_pairs={{0,16},{1,17},{2,18},{3,19},{4,20},{5,21},{6,22},{7,23},{8,24},{9,... | collective-permute-start | bytes 98312 | tf_op jit(solution)/shard_map/ppermute | solution.py:29
  95.3 1.3 collective-permute-start.26
  96.0 0.7 collective-permute-start.27
  97.3 3.4 %collective-permute-start.28 = (bf16[16,1024]{1,0:T(8,128)(2,1)S(1)}, bf16[16,1024]{1,0:T(8,128)(2,1)S(1)}, u32[]{:S(2)}, u32[]{:S(2)}) collective-permute-start(bf16[16,1024]{1,0:T(8,128)(2,1)S(1)} %fusion.24), channel_id=1, source_target_pairs={{0,20},{1,21},{2,22},{3,23},{4,16},{5,17},{6,18},{7,19},{8,28},{9,... | collective-permute-start | bytes 98312 | tf_op jit(solution)/shard_map/ppermute | solution.py:29
  97.7 3.0 %collective-permute-start.29 = (bf16[16,1024]{1,0:T(8,128)(2,1)S(1)}, bf16[16,1024]{1,0:T(8,128)(2,1)S(1)}, u32[]{:S(2)}, u32[]{:S(2)}) collective-permute-start(bf16[16,1024]{1,0:T(8,128)(2,1)S(1)} %fusion.24), channel_id=1, source_target_pairs={{0,16},{1,17},{2,18},{3,19},{4,20},{5,21},{6,22},{7,23},{8,24},{9,... | collective-permute-start | bytes 98312 | tf_op jit(solution)/shard_map/ppermute | solution.py:29
  101.3 1.4 collective-permute-start.30
  102.0 0.7 collective-permute-start.31
  103.4 3.7 %collective-permute-start.32 = (bf16[16,1024]{1,0:T(8,128)(2,1)S(1)}, bf16[16,1024]{1,0:T(8,128)(2,1)S(1)}, u32[]{:S(2)}, u32[]{:S(2)}) collective-permute-start(bf16[16,1024]{1,0:T(8,128)(2,1)S(1)} %fusion.26), channel_id=1, source_target_pairs={{0,20},{1,21},{2,22},{3,23},{4,16},{5,17},{6,18},{7,19},{8,28},{9,... | collective-permute-start | bytes 98312 | tf_op jit(solution)/shard_map/ppermute | solution.py:29
  103.8 3.3 %collective-permute-start.33 = (bf16[16,1024]{1,0:T(8,128)(2,1)S(1)}, bf16[16,1024]{1,0:T(8,128)(2,1)S(1)}, u32[]{:S(2)}, u32[]{:S(2)}) collective-permute-start(bf16[16,1024]{1,0:T(8,128)(2,1)S(1)} %fusion.26), channel_id=1, source_target_pairs={{0,16},{1,17},{2,18},{3,19},{4,20},{5,21},{6,22},{7,23},{8,24},{9,... | collective-permute-start | bytes 98312 | tf_op jit(solution)/shard_map/ppermute | solution.py:29
  107.7 16.0 %collective-permute-start.34 = (bf16[16,1024]{1,0:T(8,128)(2,1)S(1)}, bf16[16,1024]{1,0:T(8,128)(2,1)S(1)}, u32[]{:S(2)}, u32[]{:S(2)}) collective-permute-start(bf16[16,1024]{1,0:T(8,128)(2,1)S(1)} %fusion.27), channel_id=1, source_target_pairs={{208,236},{209,237},{210,238},{211,239},{212,232},{213,233},{214,2... | collective-permute-start | bytes 98312 | tf_op jit(solution)/shard_map/ppermute | solution.py:29
  109.0 14.7 %collective-permute-start.35 = (bf16[16,1024]{1,0:T(8,128)(2,1)S(1)}, bf16[16,1024]{1,0:T(8,128)(2,1)S(1)}, u32[]{:S(2)}, u32[]{:S(2)}) collective-permute-start(bf16[16,1024]{1,0:T(8,128)(2,1)S(1)} %fusion.27), channel_id=1, source_target_pairs={{208,224},{209,225},{210,226},{211,227},{212,228},{213,229},{214,2... | collective-permute-start | bytes 98312 | tf_op jit(solution)/shard_map/ppermute | solution.py:29
  124.3 3.4 %collective-permute-start.36 = (bf16[16,1024]{1,0:T(8,128)(2,1)S(1)}, bf16[16,1024]{1,0:T(8,128)(2,1)S(1)}, u32[]{:S(2)}, u32[]{:S(2)}) collective-permute-start(bf16[16,1024]{1,0:T(8,128)(2,1)S(1)} %fusion.28), channel_id=1, source_target_pairs={{0,20},{1,21},{2,22},{3,23},{4,16},{5,17},{6,18},{7,19},{8,28},{9,... | collective-permute-start | bytes 98312 | tf_op jit(solution)/shard_map/ppermute | solution.py:29
  124.4 3.4 %collective-permute-start.37 = (bf16[16,1024]{1,0:T(8,128)(2,1)S(1)}, bf16[16,1024]{1,0:T(8,128)(2,1)S(1)}, u32[]{:S(2)}, u32[]{:S(2)}) collective-permute-start(bf16[16,1024]{1,0:T(8,128)(2,1)S(1)} %fusion.28), channel_id=1, source_target_pairs={{0,16},{1,17},{2,18},{3,19},{4,20},{5,21},{6,22},{7,23},{8,24},{9,... | collective-permute-start | bytes 98312 | tf_op jit(solution)/shard_map/ppermute | solution.py:29
  128.4 4.0 %collective-permute-start.38 = (bf16[16,1024]{1,0:T(8,128)(2,1)S(1)}, bf16[16,1024]{1,0:T(8,128)(2,1)S(1)}, u32[]{:S(2)}, u32[]{:S(2)}) collective-permute-start(bf16[16,1024]{1,0:T(8,128)(2,1)S(1)} %fusion.30), channel_id=1, source_target_pairs={{0,4},{1,5},{2,6},{3,7},{4,0},{5,1},{6,2},{7,3},{8,12},{9,13},{10,... | collective-permute-start | bytes 98312 | tf_op jit(solution)/shard_map/ppermute | solution.py:29
  132.4 7.5 %collective-permute-start.39 = (bf16[16,1024]{1,0:T(8,128)(2,1)S(1)}, bf16[16,1024]{1,0:T(8,128)(2,1)S(1)}, u32[]{:S(2)}, u32[]{:S(2)}) collective-permute-start(bf16[16,1024]{1,0:T(8,128)(2,1)S(1)} %get-tuple-element.40), channel_id=1, source_target_pairs={{0,12},{1,13},{2,14},{3,15},{4,8},{5,9},{6,10},{7,11},{8,4},{9,5},... | collective-permute-start | bytes 98312 | tf_op jit(solution)/shard_map/ppermute | solution.py:29
  134.6 5.1 %collective-permute-start.43 = (bf16[16,512]{1,0:T(8,128)(2,1)S(1)}, bf16[16,512]{1,0:T(8,128)(2,1)S(1)}, u32[]{:S(2)}, u32[]{:S(2)}) collective-permute-start(bf16[16,512]{1,0:T(8,128)(2,1)S(1)} %get-tuple-element.45), channel_id=1, source_target_pairs={{16,4},{17,5},{18,6},{19,7},{20,0},{21,1},{22,2},{23,3},{24,12},{2... | collective-permute-start | bytes 49160 | tf_op jit(solution)/shard_map/ppermute | solution.py:29
  136.6 3.4 %collective-permute-start.44 = (bf16[16,512]{1,0:T(8,128)(2,1)S(1)}, bf16[16,512]{1,0:T(8,128)(2,1)S(1)}, u32[]{:S(2)}, u32[]{:S(2)}) collective-permute-start(bf16[16,512]{1,0:T(8,128)(2,1)S(1)} %get-tuple-element.46), channel_id=1, source_target_pairs={{16,0},{17,1},{18,2},{19,3},{20,4},{21,5},{22,6},{23,7},{24,8},{25... | collective-permute-start | bytes 49160 | tf_op jit(solution)/shard_map/ppermute | solution.py:29
  149.9 13.2 %copy-start = (f32[1,128,2048]{2,1,0:T(8,128)S(1)}, f32[1,128,2048]{2,1,0:T(8,128)}, u32[]{:S(2)}) copy-start(f32[1,128,2048]{2,1,0:T(8,128)} %param.8) | copy-start | bytes 3145732
  150.0 9.2 %collective-permute-start.40 = (bf16[128,512]{1,0:T(8,128)(2,1)S(1)}, bf16[128,512]{1,0:T(8,128)(2,1)S(1)}, u32[]{:S(2)}, u32[]{:S(2)}) collective-permute-start(bf16[128,512]{1,0:T(8,128)(2,1)S(1)} %get-tuple-element.33), channel_id=1, source_target_pairs={{0,1},{1,0},{2,3},{3,2},{4,5},{5,4},{6,7},{7,6},{8,9},{9,8},{10,11... | collective-permute-start | bytes 393224 | tf_op jit(solution)/shard_map/ppermute | solution.py:29
  151.7 8.6 %collective-permute-start.41 = (bf16[128,512]{1,0:T(8,128)(2,1)S(1)}, bf16[128,512]{1,0:T(8,128)(2,1)S(1)}, u32[]{:S(2)}, u32[]{:S(2)}) collective-permute-start(bf16[128,512]{1,0:T(8,128)(2,1)S(1)} %get-tuple-element.32), channel_id=1, source_target_pairs={{0,2},{1,3},{2,0},{3,1},{4,6},{5,7},{6,4},{7,5},{8,10},{9,11},{10,... | collective-permute-start | bytes 393224 | tf_op jit(solution)/shard_map/ppermute | solution.py:29
  154.4 8.7 %collective-permute-start.42 = (bf16[128,512]{1,0:T(8,128)(2,1)S(1)}, bf16[128,512]{1,0:T(8,128)(2,1)S(1)}, u32[]{:S(2)}, u32[]{:S(2)}) collective-permute-start(bf16[128,512]{1,0:T(8,128)(2,1)S(1)} %get-tuple-element.31), channel_id=1, source_target_pairs={{0,3},{1,2},{2,1},{3,0},{4,7},{5,6},{6,5},{7,4},{8,11},{9,10},{10,... | collective-permute-start | bytes 393224 | tf_op jit(solution)/shard_map/ppermute | solution.py:29
  154.8 10.1 %collective-permute-start.45 = (bf16[16,2432]{1,0:T(8,128)(2,1)S(1)}, bf16[16,2432]{1,0:T(8,128)(2,1)S(1)}, u32[]{:S(2)}, u32[]{:S(2)}) collective-permute-start(bf16[16,2432]{1,0:T(8,128)(2,1)S(1)} %get-tuple-element.36), channel_id=1, source_target_pairs={{0,1},{1,0},{2,3},{3,2},{4,5},{5,4},{6,7},{7,6},{8,9},{9,8},{10,11... | collective-permute-start | bytes 233480 | tf_op jit(solution)/shard_map/ppermute | solution.py:29
  155.3 9.6 %collective-permute-start.46 = (bf16[16,2432]{1,0:T(8,128)(2,1)S(1)}, bf16[16,2432]{1,0:T(8,128)(2,1)S(1)}, u32[]{:S(2)}, u32[]{:S(2)}) collective-permute-start(bf16[16,2432]{1,0:T(8,128)(2,1)S(1)} %get-tuple-element.37), channel_id=1, source_target_pairs={{0,2},{1,3},{2,0},{3,1},{4,6},{5,7},{6,4},{7,5},{8,10},{9,11},{10,... | collective-permute-start | bytes 233480 | tf_op jit(solution)/shard_map/ppermute | solution.py:29
  159.2 5.7 %collective-permute-start.47 = (bf16[16,2432]{1,0:T(8,128)(2,1)S(1)}, bf16[16,2432]{1,0:T(8,128)(2,1)S(1)}, u32[]{:S(2)}, u32[]{:S(2)}) collective-permute-start(bf16[16,2432]{1,0:T(8,128)(2,1)S(1)} %get-tuple-element.35), channel_id=1, source_target_pairs={{0,3},{1,2},{2,1},{3,0},{4,7},{5,6},{6,5},{7,4},{8,11},{9,10},{10,... | collective-permute-start | bytes 233480 | tf_op jit(solution)/shard_map/ppermute | solution.py:29
Sparse Core Ops, SparseCore 0:
  9.8 48.2 all-gather.10
  59.9 26.3 all-gather.12
  88.7 27.7 all-gather.6
  118.2 28.1 all-gather.8

commit v5 on v4

--- a/solution.py
+++ b/solution.py
@@ -51,7 +51,7 @@
     return lax.optimization_barrier((values, others))[0]
 
 
-def kernel_call(body, place, operands, out_shapes, flops=0):
+def kernel_call(body, place, operands, out_shapes, flops=0, scratch=()):
     out_bytes = sum(s.size * s.dtype.itemsize for s in out_shapes)
     in_bytes = sum(o.size * o.dtype.itemsize for o in operands)
     whole = pl.BlockSpec(memory_space=pltpu.VMEM)
@@ -60,6 +60,7 @@
         out_shape=out_shapes,
         in_specs=[pl.BlockSpec(memory_space=pltpu.SMEM)] + [whole] * len(operands),
         out_specs=[whole] * len(out_shapes),
+        scratch_shapes=scratch,
         compiler_params=pltpu.CompilerParams(vmem_limit_bytes=24 * 1024 * 1024),
         cost_estimate=pl.CostEstimate(
             flops=flops, bytes_accessed=in_bytes + out_bytes, transcendentals=0
@@ -119,26 +120,54 @@
         )
 
 
-def gather_groups(along_reduce):
+def inner_kernel(place, first, second, out):
+    def multiply(left, right):
+        out[...] = lax.dot_general(
+            left[...], right[...], (((1,), (1,)), ((), ())), preferred_element_type=f32
+        ).astype(bf16)
+
+    pl.when(place[0] == 1)(lambda: multiply(second, first))
+    pl.when(place[0] == 0)(lambda: multiply(first, second))
+
+
+def folded_kernel(place, coupling, *refs):
+    early, late, inner, outs, turned = refs[:3], refs[3:6], refs[6], refs[7:11], refs[11]
+    size = coupling.shape[0]
+    for j, step in enumerate((0, 1, 3, 2)):
+        for k in range(SIDE * SIDE):
+            columns = block_of((k // SIDE) * place[0] + (k % SIDE) * place[1], size)
+            if step == 0:
+                value = coupling[:, columns]
+            else:
+                value = early[j - 1][:, columns] + late[j - 1][:, columns]
+            turned[:, k * size : (k + 1) * size] = value
+        outs[step][...] = jnp.dot(
+            turned[...], inner[...], preferred_element_type=f32
+        ).astype(bf16)
+
+
+def over_axis(array, axis):
+    if axis == "x":
+        groups = [[k * SIDE + i for i in range(SIDE)] for k in range(SIDE)]
+    else:
+        groups = [[i * SIDE + k for i in range(SIDE)] for k in range(SIDE)]
+    return lax.all_gather(array, "blk", axis=0, tiled=True, axis_index_groups=groups)
+
+
+def over_other(array):
     groups = []
     for p in range(PARTITIONS):
         for k in range(SIDE):
-            if (p % 2 == 0) == along_reduce:
-                groups.append([p * PLANE + k * SIDE + x for x in range(SIDE)])
+            if p % 2 == 0:
+                groups.append([p * PLANE + i * SIDE + k for i in range(SIDE)])
             else:
-                groups.append([p * PLANE + y * SIDE + k for y in range(SIDE)])
-    return groups
-
-
-def gathered(array, along_reduce):
-    return lax.all_gather(
-        array, AXES, axis=0, tiled=True, axis_index_groups=gather_groups(along_reduce)
-    )
-
-
-def along_reduce(value, step):
+                groups.append([p * PLANE + k * SIDE + i for i in range(SIDE)])
+    return lax.all_gather(array, AXES, axis=0, tiled=True, axis_index_groups=groups)
+
+
+def along_reduce(value, step, partitions=range(PARTITIONS)):
     return permuted(
-        value, lambda p, y, x: (p, y, x ^ step) if p % 2 == 0 else (p, y ^ step, x)
+        value, lambda p, y, x: (p, y, x ^ step) if p % 2 == 0 else (p, y ^ step, x), partitions
     )
 
 
@@ -166,14 +195,9 @@
     away_high = jnp.where(even, 2 + ring, 3 - 2 * pair)
     place = jnp.stack([x, y])
 
-    coupling_in = gathered(coupling_rows, False)
-    inverse_out = gathered(inverse_rows, True)
-    turned = jnp.where(
-        even,
-        coupling_rows,
-        coupling_rows.reshape(rows, SIDE, SIDE, rows).transpose(0, 2, 1, 3).reshape(rows, nodes),
-    )
-    coupling_out = gathered(turned, True)
+    first = over_axis(jnp.where(even, coupling_rows, inverse_rows), "y")
+    second = over_axis(jnp.where(even, inverse_rows, coupling_rows), "x")
+    early, late = range(PARTITIONS // 2, PARTITIONS), range(PARTITIONS // 2)
 
     def ordered(pieces):
         stacked = jnp.stack(pieces)
@@ -197,7 +221,11 @@
     two = jnp.where(
         out_place == 0, jnp.concatenate([keep, got]), jnp.concatenate([got, keep])
     )
-    pieces = spread_x(two)
+    pieces = [two] + [
+        permuted(two, lambda p, y, x: (p, y, x ^ step), range(1, PARTITIONS)) for step in (1, 2, 3)
+    ]
+    early_rows = tie(coupling_rows, two)
+    early_pieces = [along_reduce(early_rows, 1, early), along_reduce(early_rows, 3, early)]
     source_rows, weight_row = tie((source_rows, weight_row), two)
     started = weight_row[None, :] * source_rows
 
@@ -226,12 +254,27 @@
     for turn in range(1, PARTITIONS):
         far, near = turn_messages(message, turn - 1)
         previous = (far.astype(f32) + near.astype(f32)).astype(bf16)
-        if turn == 8:
-            inverse_out, coupling_in = tie((inverse_out, coupling_in), message)
-            inner = lax.dot_general(
-                inverse_out, coupling_in, (((1,), (1,)), ((), ())), preferred_element_type=f32
-            ).astype(bf16)
-            inner_all = gathered(inner, False)
+        if turn == 3:
+            early_pieces.append(along_reduce(early_pieces[0], 3, early))
+            previous = tie(previous, early_pieces[:2])
+        if turn == 7:
+            previous = tie(previous, early_pieces[2])
+        if turn == 9:
+            late_rows = tie(coupling_rows, message)
+            late_pieces = [along_reduce(late_rows, 1, late), along_reduce(late_rows, 3, late)]
+        if turn == 12:
+            late_pieces.append(along_reduce(late_pieces[0], 3, late))
+            previous = tie(previous, late_pieces[:2])
+        if turn == 10:
+            first, second = tie((first, second), message)
+            (inner,) = kernel_call(
+                inner_kernel,
+                jnp.stack([even.astype(jnp.int32)]),
+                [first, second],
+                [shape((line, line), bf16)],
+                flops=2 * line * line * nodes,
+            )
+            inner_all = over_other(inner)
             previous = tie(previous, inner)
         product = lax.dot_general(
             previous, block, (((1,), (1,)), ((), ())), preferred_element_type=f32
@@ -282,16 +325,20 @@
 
     last = exchange_x(last_chunk)
 
-    coupling_out, inner_all = tie((coupling_out, inner_all), lines)
-    folded = jnp.dot(coupling_out, inner_all, preferred_element_type=f32).astype(bf16)
-
-    def folded_chunk(step):
-        return lax.dynamic_slice(folded, ((r ^ step) * rows, 0), (rows, line))
-
-    back_rows = [folded_chunk(0)] + [along_reduce(folded_chunk(s), s) for s in (1, 2, 3)]
+    inner_all = tie(inner_all, rounded)
+    strides = [jnp.where(even, SIDE, 1), jnp.where(even, 1, SIDE)]
+    folded = kernel_call(
+        folded_kernel,
+        jnp.stack(strides),
+        [coupling_rows] + early_pieces + late_pieces + [inner_all],
+        [shape((rows, line), bf16)] * SIDE,
+        flops=2 * line * line * nodes,
+        scratch=[pltpu.VMEM((rows, nodes), bf16)],
+    )
+    back_rows = [folded[0]] + [along_reduce(folded[step], step) for step in (1, 2, 3)]
     schur_rows, narrow = kernel_call(
         schur_kernel,
-        jnp.stack([r, jnp.where(even, SIDE, 1), jnp.where(even, 1, SIDE)]),
+        jnp.stack([r] + strides),
         [separator_rows] + back_rows,
         [shape((rows, nodes), f32), shape((rows, nodes), bf16)],
     )

time: 175 us -> 193 us (1.10)
  starting transfers between devices: 49.4 us -> 68 us
  waiting for transfers between devices: 81.4 us -> 73.8 us
  Pallas kernels: 4.48 us -> 10.2 us
  matrix products: 17.9 us -> 12.2 us
  other arithmetic: 1.36 us -> 5.22 us
  local copies, waits for them, and re-layouts: 3.99 us -> 6.98 us
    ppermute x48 -> x54, starting transfers between devices: 49.2 us -> 67.8 us  [permuted(): return lax.ppermute(value, AXES, pairs)]
    all_gather x4 -> x3, waiting for transfers between devices: 10.9 us -> 0.06 us  [the longest x2 0.04 us: over_axis(): lax.all_gather(array, 'blk', axis=0, tiled=True, axis_index_groups=groups)]
    dot_general x2 -> x0, matrix products: 7.76 us -> none  [the longest x1 4.3 us: shards(): lax.dot_general(inverse_out, coupling_in, (((1,), (1,)), ((), ())), prefe...]
    unnamed x10 -> x28, local copies, waits for them, and re-layouts: 1.06 us -> 6.88 us
    pallas_call x4 -> x6, Pallas kernels: 4.48 us -> 10.2 us  [kernel_call(): pl.pallas_call(body, out_shape=out_shapes, in_specs=[pl.BlockSpec(memory_...]
    ppermute x48 -> x54, waiting for transfers between devices: 69.1 us -> 73.7 us  [permuted(): return lax.ppermute(value, AXES, pairs)]
    dot_general x15, matrix products: 9.77 us -> 11.8 us  [shards(): lax.dot_general(previous, block, (((1,), (1,)), ((), ())), preferred_elem...]
  transfers between devices with their start and end apart: 52 -> 57, of which waited for: 20 -> 20; matrix products, arithmetic and copies ran while one was open for 11% -> 8% of each run, Pallas kernels for 2% -> 2%
where the time goes in v5:
time: 193 us; the launch traced here: 191 us
  waiting for transfers between devices  73.8 us (38%)
  starting transfers between devices  68 us (35%)
  between operations  14.4 us (7%)
  matrix products  12.2 us (6%)
  Pallas kernels  10.2 us (5%)
  local copies, waits for them, and re-layouts  6.98 us (4%)
  other arithmetic  5.22 us (3%)
    ppermute x54, waiting for transfers between devices, permuted(): return lax.ppermute(value, AXES, pairs)  73.7 us
    ppermute x54, starting transfers between devices, permuted(): return lax.ppermute(value, AXES, pairs)  67.8 us
    dot_general x15, matrix products, shards(): lax.dot_general(previous, block, (((1,), (1,)), ((), ())), preferred_elem...  11.8 us
    pallas_call x6, Pallas kernels, kernel_call(): pl.pallas_call(body, out_shape=out_shapes, in_specs=[pl.BlockSpec(memory_...  10.2 us
    unnamed x28, local copies, waits for them, and re-layouts  6.88 us
  transfers between devices with their start and end apart: 57, of which 20 were waited for; matrix products, arithmetic and copies ran while one was open for 8% of the time, Pallas kernels for 2%

profile of v5, /device:TPU:224, one launch (start us, length us, event | category | flops | bytes accessed | tf_op | source)
XLA Modules:
  0.0 190.8 jit_solution(5835341421006065538)
XLA Ops:
  7.3 2.3 %bitcast_select_fusion = (bf16[128,2048]{1,0:T(8,128)(2,1)}, bf16[128,2048]{1,0:T(8,128)(2,1)}) fusion(bf16[1,128,2048]{2,1,0:T(8,128)(2,1)} %param.6, pred[]{:T(512)S(6)} %eq.59, bf16[1,128,2048]{2,1,0:T(8,128)(2,1)} %param.7), kind=kLoop, calls=%fused_computation.48 | loop fusion | flops 524288 | bytes 2097153 | tf_op jit(solution)/shard_map/jit(_where)/select_n | solution.py:199
  10.3 1.7 collective-permute-start
  12.0 4.8 %collective-permute-done = bf16[128,1024]{1,0:T(8,128)(2,1)S(1)} collective-permute-done((bf16[128,1024]{1,0:T(8,128)(2,1)S(1)}, bf16[128,1024]{1,0:T(8,128)(2,1)S(1)}, u32[]{:S(2)}, u32[]{:S(2)}) %collective-permute-start) | collective-permute-done | bytes 262176 | tf_op jit(solution)/shard_map/ppermute | solution.py:29
  17.0 1.6 collective-permute-start.4
  18.6 2.7 %collective-permute-start.5 = (f32[24,128]{1,0:T(8,128)S(1)}, f32[24,128]{1,0:T(8,128)S(1)}, u32[]{:S(2)}, u32[]{:S(2)}) collective-permute-start(f32[24,128]{1,0:T(8,128)S(1)} %get-tuple-element.83), channel_id=1, source_target_pairs={{0,2},{1,3},{2,0},{3,1},{4,6},{5,7},{6,4},{7,5},{8,10},{9,11},{10,... | collective-permute-start | bytes 36872 | tf_op jit(solution)/shard_map/ppermute | solution.py:29
  21.9 2.2 %collective-permute-start.10 = (bf16[256,1024]{1,0:T(8,128)(2,1)S(1)}, bf16[256,1024]{1,0:T(8,128)(2,1)S(1)}, u32[]{:S(2)}, u32[]{:S(2)}) collective-permute-start(bf16[256,1024]{1,0:T(8,128)(2,1)S(1)} %maximum_select_fusion.refs_0_), channel_id=1, source_target_pairs={{16,17},{17,16},{18,19},{19,18},{20,21},{21,20},{22,23},{23,22},{2... | collective-permute-start | bytes 1572872 | tf_op jit(solution)/shard_map/ppermute | solution.py:29
  24.1 5.8 %collective-permute-start.11 = (bf16[256,1024]{1,0:T(8,128)(2,1)S(1)}, bf16[256,1024]{1,0:T(8,128)(2,1)S(1)}, u32[]{:S(2)}, u32[]{:S(2)}) collective-permute-start(bf16[256,1024]{1,0:T(8,128)(2,1)S(1)} %maximum_select_fusion.refs_0_), channel_id=1, source_target_pairs={{16,18},{17,19},{18,16},{19,17},{20,22},{21,23},{22,20},{23,21},{2... | collective-permute-start | bytes 1572872 | tf_op jit(solution)/shard_map/ppermute | solution.py:29
  29.9 2.4 %collective-permute-start.12 = (bf16[256,1024]{1,0:T(8,128)(2,1)S(1)}, bf16[256,1024]{1,0:T(8,128)(2,1)S(1)}, u32[]{:S(2)}, u32[]{:S(2)}) collective-permute-start(bf16[256,1024]{1,0:T(8,128)(2,1)S(1)} %maximum_select_fusion.refs_0_), channel_id=1, source_target_pairs={{16,19},{17,18},{18,17},{19,16},{20,23},{21,22},{22,21},{23,20},{2... | collective-permute-start | bytes 1572872 | tf_op jit(solution)/shard_map/ppermute | solution.py:29
  32.4 1.7 collective-permute-start.7
  34.2 1.9 collective-permute-done.7
  36.1 2.5 %collective-permute-done.10.refs_1_ = bf16[256,1024]{1,0:T(8,128)(2,1)S(1)} collective-permute-done((bf16[256,1024]{1,0:T(8,128)(2,1)S(1)}, bf16[256,1024]{1,0:T(8,128)(2,1)S(1)}, u32[]{:S(2)}, u32[]{:S(2)}) %collective-permute-start.10) | collective-permute-done | bytes 524320 | tf_op jit(solution)/shard_map/ppermute | solution.py:29
  38.6 11.6 %collective-permute-done.11.refs_2_ = bf16[256,1024]{1,0:T(8,128)(2,1)S(1)} collective-permute-done((bf16[256,1024]{1,0:T(8,128)(2,1)S(1)}, bf16[256,1024]{1,0:T(8,128)(2,1)S(1)}, u32[]{:S(2)}, u32[]{:S(2)}) %collective-permute-start.11) | collective-permute-done | bytes 524320 | tf_op jit(solution)/shard_map/ppermute | solution.py:29
  50.3 6.4 %collective-permute-done.12.refs_3_ = bf16[256,1024]{1,0:T(8,128)(2,1)S(1)} collective-permute-done((bf16[256,1024]{1,0:T(8,128)(2,1)S(1)}, bf16[256,1024]{1,0:T(8,128)(2,1)S(1)}, u32[]{:S(2)}, u32[]{:S(2)}) %collective-permute-start.12) | collective-permute-done | bytes 524320 | tf_op jit(solution)/shard_map/ppermute | solution.py:29
  56.7 0.7 shard_map.86
  59.5 1.9 %collective-permute-start.1 = (bf16[128,2048]{1,0:T(8,128)(2,1)S(1)}, bf16[128,2048]{1,0:T(8,128)(2,1)S(1)}, u32[]{:S(2)}, u32[]{:S(2)}) collective-permute-start(bf16[128,2048]{1,0:T(8,128)(2,1)S(1)} %bitcast.60), channel_id=1, source_target_pairs={{128,129},{129,128},{130,131},{131,130},{132,133},{133,132},{134,1... | collective-permute-start | bytes 1572872 | tf_op jit(solution)/shard_map/ppermute | solution.py:29
  61.4 2.4 %collective-permute-start.2 = (bf16[128,2048]{1,0:T(8,128)(2,1)S(1)}, bf16[128,2048]{1,0:T(8,128)(2,1)S(1)}, u32[]{:S(2)}, u32[]{:S(2)}) collective-permute-start(bf16[128,2048]{1,0:T(8,128)(2,1)S(1)} %bitcast.61), channel_id=1, source_target_pairs={{128,131},{129,130},{130,129},{131,128},{132,135},{133,134},{134,1... | collective-permute-start | bytes 1572872 | tf_op jit(solution)/shard_map/ppermute | solution.py:29
  65.2 2.9 %collective-permute-done.15 = bf16[16,1024]{1,0:T(8,128)(2,1)S(1)} collective-permute-done((bf16[16,1024]{1,0:T(8,128)(2,1)S(1)}, bf16[16,1024]{1,0:T(8,128)(2,1)S(1)}, u32[]{:S(2)}, u32[]{:S(2)}) %collective-permute-start.15) | collective-permute-done | bytes 32800 | tf_op jit(solution)/shard_map/ppermute | solution.py:29
  68.1 2.4 %collective-permute-done.1.refs_0_ = bf16[128,2048]{1,0:T(8,128)(2,1)S(1)} collective-permute-done((bf16[128,2048]{1,0:T(8,128)(2,1)S(1)}, bf16[128,2048]{1,0:T(8,128)(2,1)S(1)}, u32[]{:S(2)}, u32[]{:S(2)}) %collective-permute-start.1) | collective-permute-done | bytes 524320 | tf_op jit(solution)/shard_map/ppermute | solution.py:29
  70.5 3.6 %collective-permute-done.2.refs_1_ = bf16[128,2048]{1,0:T(8,128)(2,1)S(1)} collective-permute-done((bf16[128,2048]{1,0:T(8,128)(2,1)S(1)}, bf16[128,2048]{1,0:T(8,128)(2,1)S(1)}, u32[]{:S(2)}, u32[]{:S(2)}) %collective-permute-start.2) | collective-permute-done | bytes 524320 | tf_op jit(solution)/shard_map/ppermute | solution.py:29
  77.1 3.0 %collective-permute-done.19 = bf16[16,1024]{1,0:T(8,128)(2,1)S(1)} collective-permute-done((bf16[16,1024]{1,0:T(8,128)(2,1)S(1)}, bf16[16,1024]{1,0:T(8,128)(2,1)S(1)}, u32[]{:S(2)}, u32[]{:S(2)}) %collective-permute-start.19) | collective-permute-done | bytes 32800 | tf_op jit(solution)/shard_map/ppermute | solution.py:29
  82.2 2.0 %collective-permute-start.3 = (bf16[128,2048]{1,0:T(8,128)(2,1)S(1)}, bf16[128,2048]{1,0:T(8,128)(2,1)S(1)}, u32[]{:S(2)}, u32[]{:S(2)}) collective-permute-start(bf16[128,2048]{1,0:T(8,128)(2,1)S(1)} %collective-permute-done.1.refs_0_), channel_id=1, source_target_pairs={{128,131},{129,130},{130,129},{131,128},{132,135},{133,134},{134,1... | collective-permute-start | bytes 1572872 | tf_op jit(solution)/shard_map/ppermute | solution.py:29
  84.8 2.8 %collective-permute-start.23 = (bf16[16,1024]{1,0:T(8,128)(2,1)S(1)}, bf16[16,1024]{1,0:T(8,128)(2,1)S(1)}, u32[]{:S(2)}, u32[]{:S(2)}) collective-permute-start(bf16[16,1024]{1,0:T(8,128)(2,1)S(1)} %fusion.20), channel_id=1, source_target_pairs={{0,20},{1,21},{2,22},{3,23},{4,16},{5,17},{6,18},{7,19},{8,28},{9,... | collective-permute-start | bytes 98312 | tf_op jit(solution)/shard_map/ppermute | solution.py:29
  87.6 1.7 collective-permute-done.23
  89.3 6.8 %collective-permute-done.3.refs_2_ = bf16[128,2048]{1,0:T(8,128)(2,1)S(1)} collective-permute-done((bf16[128,2048]{1,0:T(8,128)(2,1)S(1)}, bf16[128,2048]{1,0:T(8,128)(2,1)S(1)}, u32[]{:S(2)}, u32[]{:S(2)}) %collective-permute-start.3) | collective-permute-done | bytes 524320 | tf_op jit(solution)/shard_map/ppermute | solution.py:29
  98.9 1.3 collective-permute-start.31
  100.2 2.1 %collective-permute-done.30 = bf16[16,1024]{1,0:T(8,128)(2,1)S(1)} collective-permute-done((bf16[16,1024]{1,0:T(8,128)(2,1)S(1)}, bf16[16,1024]{1,0:T(8,128)(2,1)S(1)}, u32[]{:S(2)}, u32[]{:S(2)}) %collective-permute-start.30) | collective-permute-done | bytes 32800 | tf_op jit(solution)/shard_map/ppermute | solution.py:29
  103.6 1.3 collective-permute-start.33
  104.9 0.8 add_convert_fusion.5
  105.8 1.6 copy-done.2
  107.4 1.6 copy-done.3
  108.9 2.1 %shard_map.87 = bf16[512,512]{1,0:T(8,128)(2,1)} custom-call(s32[1]{0:T(128)} %bitcast.24.place, bf16[512,2048]{1,0:T(8,128)(2,1)S(1)} %copy-done.2, bf16[512,2048]{1,0:T(8,128)(2,1)S(1)} %copy-done.3), custom_call_target="tpu_custom_call" | custom-call | flops 1073741824 | bytes 4718592 | tf_op jit(solution)/shard_map/pallas_call | solution.py:58
  111.7 1.2 collective-permute-start.35
  112.9 1.5 collective-permute-start.27
  114.4 1.4 collective-permute-start.28
  116.5 1.3 collective-permute-start.36
  117.8 1.3 collective-permute-start.37
  119.1 0.8 add_convert_fusion.3
  121.6 2.5 %collective-permute-done.38 = bf16[16,1024]{1,0:T(8,128)(2,1)S(1)} collective-permute-done((bf16[16,1024]{1,0:T(8,128)(2,1)S(1)}, bf16[16,1024]{1,0:T(8,128)(2,1)S(1)}, u32[]{:S(2)}, u32[]{:S(2)}) %collective-permute-start.38) | collective-permute-done | bytes 32800 | tf_op jit(solution)/shard_map/ppermute | solution.py:29
  124.7 1.3 collective-permute-start.40
  126.0 1.3 collective-permute-start.41
  127.3 14.9 %collective-permute-done.40 = bf16[16,1024]{1,0:T(8,128)(2,1)S(1)} collective-permute-done((bf16[16,1024]{1,0:T(8,128)(2,1)S(1)}, bf16[16,1024]{1,0:T(8,128)(2,1)S(1)}, u32[]{:S(2)}, u32[]{:S(2)}) %collective-permute-start.40) | collective-permute-done | bytes 32800 | tf_op jit(solution)/shard_map/ppermute | solution.py:29
  142.7 1.3 fusion.28
  144.0 2.1 %collective-permute-start.43 = (bf16[16,1024]{1,0:T(8,128)(2,1)}, bf16[16,1024]{1,0:T(8,128)(2,1)}, u32[]{:S(2)}, u32[]{:S(2)}) collective-permute-start(bf16[16,1024]{1,0:T(8,128)(2,1)} %fusion.28), channel_id=1, source_target_pairs={{0,16},{1,17},{2,18},{3,19},{4,20},{5,21},{6,22},{7,23},{8,24},{9,... | collective-permute-start | bytes 98312 | tf_op jit(solution)/shard_map/ppermute | solution.py:29
  146.1 2.0 %collective-permute-done.42 = bf16[16,1024]{1,0:T(8,128)(2,1)} collective-permute-done((bf16[16,1024]{1,0:T(8,128)(2,1)}, bf16[16,1024]{1,0:T(8,128)(2,1)}, u32[]{:S(2)}, u32[]{:S(2)}) %collective-permute-start.42) | collective-permute-done | bytes 32800 | tf_op jit(solution)/shard_map/ppermute | solution.py:29
  148.1 2.1 %fusion.30 = bf16[16,1024]{1,0:T(8,128)(2,1)} fusion(bf16[1024,1024]{1,0:T(8,128)(2,1)S(1)} %shard_map.86, f32[16,512]{1,0:T(8,128)S(1)} %slice.31, bf16[16,1024]{1,0:T(8,128)(2,1)} %collective-permute-done.43, bf16[16,1024]{1,0:T(8,128)(2,1)} %collective-permute-done.42, bf16[16,1024]{1,0:T(8,128)(2,1)} %fusion.28, bf16[16,1024]{1,0:T(8,128)(2,1)} %copy-done.12, ...), kind=kOutput, calls=%fused_computation.46 | convolution fusion | flops 33947648 | bytes 2691088 | tf_op jit(solution)/shard_map/dot_general | solution.py:279
  150.2 1.7 collective-permute-start.44
  151.9 1.5 collective-permute-start.29
  153.4 1.2 collective-permute-done.44
  154.6 0.8 convert_add_fusion
  155.4 1.1 collective-permute-start.48
  156.9 2.3 %collective-permute-start.49 = (bf16[16,512]{1,0:T(8,128)(2,1)S(1)}, bf16[16,512]{1,0:T(8,128)(2,1)S(1)}, u32[]{:S(2)}, u32[]{:S(2)}) collective-permute-start(bf16[16,512]{1,0:T(8,128)(2,1)S(1)} %get-tuple-element.63), channel_id=1, source_target_pairs={{16,4},{17,5},{18,6},{19,7},{20,0},{21,1},{22,2},{23,3},{24,12},{2... | collective-permute-start | bytes 49160 | tf_op jit(solution)/shard_map/ppermute | solution.py:29
  159.2 1.9 %collective-permute-start.50 = (bf16[16,512]{1,0:T(8,128)(2,1)S(1)}, bf16[16,512]{1,0:T(8,128)(2,1)S(1)}, u32[]{:S(2)}, u32[]{:S(2)}) collective-permute-start(bf16[16,512]{1,0:T(8,128)(2,1)S(1)} %get-tuple-element.64), channel_id=1, source_target_pairs={{16,0},{17,1},{18,2},{19,3},{20,4},{21,5},{22,6},{23,7},{24,8},{25... | collective-permute-start | bytes 49160 | tf_op jit(solution)/shard_map/ppermute | solution.py:29
  161.2 0.8 collective-permute-done.49
  162.7 1.6 copy-done
  164.3 1.0 copy-done.6
  165.4 1.0 copy-done.8
  166.4 3.5 %shard_map.88 = (bf16[128,512]{1,0:T(8,128)(2,1)S(1)}, bf16[128,512]{1,0:T(8,128)(2,1)S(1)}, bf16[128,512]{1,0:T(8,128)(2,1)S(1)}, bf16[128,512]{1,0:T(8,128)(2,1)S(1)}) custom-call(s32[2]{0:T(128)S(1)} %pad_add_fusion.1.place, bf16[128,2048]{1,0:T(8,128)(2,1)S(1)} %bitcast.64, bf16[128,2048]{1,0:T(8,128)(2,1)S(1)} %collective-permute-done.1.refs_0_, ...), custom_call_target="tpu_custom_call" | custom-call | flops 1073741824 | bytes 6291456 | tf_op jit(solution)/shard_map/pallas_call | solution.py:58
  170.6 1.8 collective-permute-start.46
  172.3 2.4 %collective-permute-start.47 = (bf16[128,512]{1,0:T(8,128)(2,1)S(1)}, bf16[128,512]{1,0:T(8,128)(2,1)S(1)}, u32[]{:S(2)}, u32[]{:S(2)}) collective-permute-start(bf16[128,512]{1,0:T(8,128)(2,1)S(1)} %get-tuple-element.40), channel_id=1, source_target_pairs={{0,3},{1,2},{2,1},{3,0},{4,7},{5,6},{6,5},{7,4},{8,11},{9,10},{10,... | collective-permute-start | bytes 393224 | tf_op jit(solution)/shard_map/ppermute | solution.py:29
  174.9 2.3 %collective-permute-start.52 = (bf16[16,2432]{1,0:T(8,128)(2,1)S(1)}, bf16[16,2432]{1,0:T(8,128)(2,1)S(1)}, u32[]{:S(2)}, u32[]{:S(2)}) collective-permute-start(bf16[16,2432]{1,0:T(8,128)(2,1)S(1)} %get-tuple-element.51), channel_id=1, source_target_pairs={{0,2},{1,3},{2,0},{3,1},{4,6},{5,7},{6,4},{7,5},{8,10},{9,11},{10,... | collective-permute-start | bytes 233480 | tf_op jit(solution)/shard_map/ppermute | solution.py:29
  177.2 2.4 %collective-permute-start.53 = (bf16[16,2432]{1,0:T(8,128)(2,1)S(1)}, bf16[16,2432]{1,0:T(8,128)(2,1)S(1)}, u32[]{:S(2)}, u32[]{:S(2)}) collective-permute-start(bf16[16,2432]{1,0:T(8,128)(2,1)S(1)} %get-tuple-element.49), channel_id=1, source_target_pairs={{0,3},{1,2},{2,1},{3,0},{4,7},{5,6},{6,5},{7,4},{8,11},{9,10},{10,... | collective-permute-start | bytes 233480 | tf_op jit(solution)/shard_map/ppermute | solution.py:29
  179.7 1.8 shard_map.89
  181.5 1.3 collective-permute-done.53.refs_3_
  182.8 1.5 shard_map.90
  (134 shorter events, 21.0 us)
Async XLA Ops:
  7.2 98.5 %all-gather.4.cloned.1.call-start = ((), (), s32[]{:S(2)}) async-start(), calls=%async_computation | async-start | bytes 2621440 | tf_op jit(solution)/shard_map/all_gather | solution.py:154
  7.2 9.7 %copy-start.10 = (f32[1,128]{1,0:T(1,128)S(1)}, f32[1,128]{1,0:T(1,128)}, u32[]{:S(2)}) copy-start(f32[1,128]{1,0:T(1,128)} %param.11) | copy-start | bytes 1540
  7.2 9.7 %copy-start.13 = (f32[1,64,128]{2,1,0:T(8,128)S(1)}, f32[1,64,128]{2,1,0:T(8,128)}, u32[]{:S(2)}) copy-start(f32[1,64,128]{2,1,0:T(8,128)} %param.10) | copy-start | bytes 98308
  9.6 96.2 %all-gather.6.cloned.1.call-start = ((), (), s32[]{:S(2)}) async-start(), calls=%async_computation.1 | async-start | bytes 2621440 | tf_op jit(solution)/shard_map/all_gather | solution.py:154
  10.3 6.5 %collective-permute-start = (bf16[128,1024]{1,0:T(8,128)(2,1)S(1)}, bf16[128,1024]{1,0:T(8,128)(2,1)S(1)}, u32[]{:S(2)}, u32[]{:S(2)}) collective-permute-start(bf16[128,1024]{1,0:T(8,128)(2,1)S(1)} %get-tuple-element.25), channel_id=1, source_target_pairs={{0,4},{1,5},{2,6},{3,7},{4,0},{5,1},{6,2},{7,3},{8,12},{9,13},{10,... | collective-permute-start | bytes 786440 | tf_op jit(solution)/shard_map/ppermute | solution.py:29
  17.0 12.9 %collective-permute-start.4 = (f32[24,128]{1,0:T(8,128)S(1)}, f32[24,128]{1,0:T(8,128)S(1)}, u32[]{:S(2)}, u32[]{:S(2)}) collective-permute-start(f32[24,128]{1,0:T(8,128)S(1)} %get-tuple-element.82), channel_id=1, source_target_pairs={{0,1},{1,0},{2,3},{3,2},{4,5},{5,4},{6,7},{7,6},{8,9},{9,8},{10,11... | collective-permute-start | bytes 36872 | tf_op jit(solution)/shard_map/ppermute | solution.py:29
  18.6 13.7 %collective-permute-start.5 = (f32[24,128]{1,0:T(8,128)S(1)}, f32[24,128]{1,0:T(8,128)S(1)}, u32[]{:S(2)}, u32[]{:S(2)}) collective-permute-start(f32[24,128]{1,0:T(8,128)S(1)} %get-tuple-element.83), channel_id=1, source_target_pairs={{0,2},{1,3},{2,0},{3,1},{4,6},{5,7},{6,4},{7,5},{8,10},{9,11},{10,... | collective-permute-start | bytes 36872 | tf_op jit(solution)/shard_map/ppermute | solution.py:29
  21.3 11.0 %collective-permute-start.6 = (f32[24,128]{1,0:T(8,128)S(1)}, f32[24,128]{1,0:T(8,128)S(1)}, u32[]{:S(2)}, u32[]{:S(2)}) collective-permute-start(f32[24,128]{1,0:T(8,128)S(1)} %get-tuple-element.84), channel_id=1, source_target_pairs={{0,3},{1,2},{2,1},{3,0},{4,7},{5,6},{6,5},{7,4},{8,11},{9,10},{10,... | collective-permute-start | bytes 36872 | tf_op jit(solution)/shard_map/ppermute | solution.py:29
  21.9 16.7 %collective-permute-start.10 = (bf16[256,1024]{1,0:T(8,128)(2,1)S(1)}, bf16[256,1024]{1,0:T(8,128)(2,1)S(1)}, u32[]{:S(2)}, u32[]{:S(2)}) collective-permute-start(bf16[256,1024]{1,0:T(8,128)(2,1)S(1)} %maximum_select_fusion.refs_0_), channel_id=1, source_target_pairs={{16,17},{17,16},{18,19},{19,18},{20,21},{21,20},{22,23},{23,22},{2... | collective-permute-start | bytes 1572872 | tf_op jit(solution)/shard_map/ppermute | solution.py:29
  24.1 26.2 %collective-permute-start.11 = (bf16[256,1024]{1,0:T(8,128)(2,1)S(1)}, bf16[256,1024]{1,0:T(8,128)(2,1)S(1)}, u32[]{:S(2)}, u32[]{:S(2)}) collective-permute-start(bf16[256,1024]{1,0:T(8,128)(2,1)S(1)} %maximum_select_fusion.refs_0_), channel_id=1, source_target_pairs={{16,18},{17,19},{18,16},{19,17},{20,22},{21,23},{22,20},{23,21},{2... | collective-permute-start | bytes 1572872 | tf_op jit(solution)/shard_map/ppermute | solution.py:29
  29.9 26.7 %collective-permute-start.12 = (bf16[256,1024]{1,0:T(8,128)(2,1)S(1)}, bf16[256,1024]{1,0:T(8,128)(2,1)S(1)}, u32[]{:S(2)}, u32[]{:S(2)}) collective-permute-start(bf16[256,1024]{1,0:T(8,128)(2,1)S(1)} %maximum_select_fusion.refs_0_), channel_id=1, source_target_pairs={{16,19},{17,18},{18,17},{19,16},{20,23},{21,22},{22,21},{23,20},{2... | collective-permute-start | bytes 1572872 | tf_op jit(solution)/shard_map/ppermute | solution.py:29
  32.4 3.7 %collective-permute-start.7 = (f32[1,512]{1,0:T(1,128)S(1)}, f32[1,512]{1,0:T(1,128)S(1)}, u32[]{:S(2)}, u32[]{:S(2)}) collective-permute-start(f32[1,512]{1,0:T(1,128)S(1)} %pad_maximum_fusion.10), channel_id=1, source_target_pairs={{0,4},{1,5},{2,6},{3,7},{4,0},{5,1},{6,2},{7,3},{8,12},{9,13},{10,... | collective-permute-start | bytes 6152 | tf_op jit(solution)/shard_map/ppermute | solution.py:29
  34.1 23.3 %collective-permute-start.8 = (bf16[16,1024]{1,0:T(8,128)(2,1)S(1)}, bf16[16,1024]{1,0:T(8,128)(2,1)S(1)}, u32[]{:S(2)}, u32[]{:S(2)}) collective-permute-start(bf16[16,1024]{1,0:T(8,128)(2,1)S(1)} %fusion.32), channel_id=1, source_target_pairs={{0,20},{1,21},{2,22},{3,23},{4,16},{5,17},{6,18},{7,19},{8,28},{9,... | collective-permute-start | bytes 98312 | tf_op jit(solution)/shard_map/ppermute | solution.py:29
  36.1 21.3 %collective-permute-start.9 = (bf16[16,1024]{1,0:T(8,128)(2,1)S(1)}, bf16[16,1024]{1,0:T(8,128)(2,1)S(1)}, u32[]{:S(2)}, u32[]{:S(2)}) collective-permute-start(bf16[16,1024]{1,0:T(8,128)(2,1)S(1)} %fusion.32), channel_id=1, source_target_pairs={{0,16},{1,17},{2,18},{3,19},{4,20},{5,21},{6,22},{7,23},{8,24},{9,... | collective-permute-start | bytes 98312 | tf_op jit(solution)/shard_map/ppermute | solution.py:29
  58.0 5.8 %collective-permute-start.13 = (bf16[16,1024]{1,0:T(8,128)(2,1)S(1)}, bf16[16,1024]{1,0:T(8,128)(2,1)S(1)}, u32[]{:S(2)}, u32[]{:S(2)}) collective-permute-start(bf16[16,1024]{1,0:T(8,128)(2,1)S(1)} %fusion.15), channel_id=1, source_target_pairs={{16,44},{17,45},{18,46},{19,47},{20,40},{21,41},{22,42},{23,43},{2... | collective-permute-start | bytes 98312 | tf_op jit(solution)/shard_map/ppermute | solution.py:29
  58.7 5.1 %collective-permute-start.14 = (bf16[16,1024]{1,0:T(8,128)(2,1)S(1)}, bf16[16,1024]{1,0:T(8,128)(2,1)S(1)}, u32[]{:S(2)}, u32[]{:S(2)}) collective-permute-start(bf16[16,1024]{1,0:T(8,128)(2,1)S(1)} %fusion.15), channel_id=1, source_target_pairs={{16,32},{17,33},{18,34},{19,35},{20,36},{21,37},{22,38},{23,39},{2... | collective-permute-start | bytes 98312 | tf_op jit(solution)/shard_map/ppermute | solution.py:29
  59.4 103.3 %all-gather.8.cloned.1.call-start = ((), (), s32[]{:S(2)}) async-start(), calls=%async_computation.2 | async-start | bytes 2621440 | tf_op jit(solution)/shard_map/all_gather | solution.py:165
  59.5 11.1 %collective-permute-start.1 = (bf16[128,2048]{1,0:T(8,128)(2,1)S(1)}, bf16[128,2048]{1,0:T(8,128)(2,1)S(1)}, u32[]{:S(2)}, u32[]{:S(2)}) collective-permute-start(bf16[128,2048]{1,0:T(8,128)(2,1)S(1)} %bitcast.60), channel_id=1, source_target_pairs={{128,129},{129,128},{130,131},{131,130},{132,133},{133,132},{134,1... | collective-permute-start | bytes 1572872 | tf_op jit(solution)/shard_map/ppermute | solution.py:29
  61.4 12.7 %collective-permute-start.2 = (bf16[128,2048]{1,0:T(8,128)(2,1)S(1)}, bf16[128,2048]{1,0:T(8,128)(2,1)S(1)}, u32[]{:S(2)}, u32[]{:S(2)}) collective-permute-start(bf16[128,2048]{1,0:T(8,128)(2,1)S(1)} %bitcast.61), channel_id=1, source_target_pairs={{128,131},{129,130},{130,129},{131,128},{132,135},{133,134},{134,1... | collective-permute-start | bytes 1572872 | tf_op jit(solution)/shard_map/ppermute | solution.py:29
  64.5 3.7 %collective-permute-start.15 = (bf16[16,1024]{1,0:T(8,128)(2,1)S(1)}, bf16[16,1024]{1,0:T(8,128)(2,1)S(1)}, u32[]{:S(2)}, u32[]{:S(2)}) collective-permute-start(bf16[16,1024]{1,0:T(8,128)(2,1)S(1)} %fusion.16), channel_id=1, source_target_pairs={{0,20},{1,21},{2,22},{3,23},{4,16},{5,17},{6,18},{7,19},{8,28},{9,... | collective-permute-start | bytes 98312 | tf_op jit(solution)/shard_map/ppermute | solution.py:29
  65.0 3.1 %collective-permute-start.16 = (bf16[16,1024]{1,0:T(8,128)(2,1)S(1)}, bf16[16,1024]{1,0:T(8,128)(2,1)S(1)}, u32[]{:S(2)}, u32[]{:S(2)}) collective-permute-start(bf16[16,1024]{1,0:T(8,128)(2,1)S(1)} %fusion.16), channel_id=1, source_target_pairs={{0,16},{1,17},{2,18},{3,19},{4,20},{5,21},{6,22},{7,23},{8,24},{9,... | collective-permute-start | bytes 98312 | tf_op jit(solution)/shard_map/ppermute | solution.py:29
  74.1 2.7 %copy-start.5 = (bf16[128,2048]{1,0:T(8,128)(2,1)}, bf16[128,2048]{1,0:T(8,128)(2,1)S(1)}, u32[]{:S(2)}) copy-start(bf16[128,2048]{1,0:T(8,128)(2,1)S(1)} %collective-permute-done.2.refs_1_) | copy-start | bytes 1572868
  74.7 1.3 collective-permute-start.17
  75.4 0.7 collective-permute-start.18
  76.8 3.4 %collective-permute-start.19 = (bf16[16,1024]{1,0:T(8,128)(2,1)S(1)}, bf16[16,1024]{1,0:T(8,128)(2,1)S(1)}, u32[]{:S(2)}, u32[]{:S(2)}) collective-permute-start(bf16[16,1024]{1,0:T(8,128)(2,1)S(1)} %fusion.18), channel_id=1, source_target_pairs={{0,20},{1,21},{2,22},{3,23},{4,16},{5,17},{6,18},{7,19},{8,28},{9,... | collective-permute-start | bytes 98312 | tf_op jit(solution)/shard_map/ppermute | solution.py:29
  76.8 3.3 %collective-permute-start.20 = (bf16[16,1024]{1,0:T(8,128)(2,1)S(1)}, bf16[16,1024]{1,0:T(8,128)(2,1)S(1)}, u32[]{:S(2)}, u32[]{:S(2)}) collective-permute-start(bf16[16,1024]{1,0:T(8,128)(2,1)S(1)} %fusion.18), channel_id=1, source_target_pairs={{0,16},{1,17},{2,18},{3,19},{4,20},{5,21},{6,22},{7,23},{8,24},{9,... | collective-permute-start | bytes 98312 | tf_op jit(solution)/shard_map/ppermute | solution.py:29
  80.8 3.3 %collective-permute-start.21 = (bf16[16,1024]{1,0:T(8,128)(2,1)S(1)}, bf16[16,1024]{1,0:T(8,128)(2,1)S(1)}, u32[]{:S(2)}, u32[]{:S(2)}) collective-permute-start(bf16[16,1024]{1,0:T(8,128)(2,1)S(1)} %fusion.19), channel_id=1, source_target_pairs={{80,108},{81,109},{82,110},{83,111},{84,104},{85,105},{86,106},{87... | collective-permute-start | bytes 98312 | tf_op jit(solution)/shard_map/ppermute | solution.py:29
  81.5 2.7 %collective-permute-start.22 = (bf16[16,1024]{1,0:T(8,128)(2,1)S(1)}, bf16[16,1024]{1,0:T(8,128)(2,1)S(1)}, u32[]{:S(2)}, u32[]{:S(2)}) collective-permute-start(bf16[16,1024]{1,0:T(8,128)(2,1)S(1)} %fusion.19), channel_id=1, source_target_pairs={{80,96},{81,97},{82,98},{83,99},{84,100},{85,101},{86,102},{87,103... | collective-permute-start | bytes 98312 | tf_op jit(solution)/shard_map/ppermute | solution.py:29
  82.2 14.0 %collective-permute-start.3 = (bf16[128,2048]{1,0:T(8,128)(2,1)S(1)}, bf16[128,2048]{1,0:T(8,128)(2,1)S(1)}, u32[]{:S(2)}, u32[]{:S(2)}) collective-permute-start(bf16[128,2048]{1,0:T(8,128)(2,1)S(1)} %collective-permute-done.1.refs_0_), channel_id=1, source_target_pairs={{128,131},{129,130},{130,129},{131,128},{132,135},{133,134},{134,1... | collective-permute-start | bytes 1572872 | tf_op jit(solution)/shard_map/ppermute | solution.py:29
  84.8 4.5 %collective-permute-start.23 = (bf16[16,1024]{1,0:T(8,128)(2,1)S(1)}, bf16[16,1024]{1,0:T(8,128)(2,1)S(1)}, u32[]{:S(2)}, u32[]{:S(2)}) collective-permute-start(bf16[16,1024]{1,0:T(8,128)(2,1)S(1)} %fusion.20), channel_id=1, source_target_pairs={{0,20},{1,21},{2,22},{3,23},{4,16},{5,17},{6,18},{7,19},{8,28},{9,... | collective-permute-start | bytes 98312 | tf_op jit(solution)/shard_map/ppermute | solution.py:29
  87.6 1.7 collective-permute-start.24
  96.2 2.7 %copy-start.7 = (bf16[128,2048]{1,0:T(8,128)(2,1)}, bf16[128,2048]{1,0:T(8,128)(2,1)S(1)}, u32[]{:S(2)}) copy-start(bf16[128,2048]{1,0:T(8,128)(2,1)S(1)} %collective-permute-done.3.refs_2_) | copy-start | bytes 1572868
  96.8 1.3 collective-permute-start.25
  97.5 0.7 collective-permute-start.26
  98.8 3.5 %collective-permute-start.30 = (bf16[16,1024]{1,0:T(8,128)(2,1)S(1)}, bf16[16,1024]{1,0:T(8,128)(2,1)S(1)}, u32[]{:S(2)}, u32[]{:S(2)}) collective-permute-start(bf16[16,1024]{1,0:T(8,128)(2,1)S(1)} %fusion.22), channel_id=1, source_target_pairs={{0,20},{1,21},{2,22},{3,23},{4,16},{5,17},{6,18},{7,19},{8,28},{9,... | collective-permute-start | bytes 98312 | tf_op jit(solution)/shard_map/ppermute | solution.py:29
  98.9 3.4 %collective-permute-start.31 = (bf16[16,1024]{1,0:T(8,128)(2,1)S(1)}, bf16[16,1024]{1,0:T(8,128)(2,1)S(1)}, u32[]{:S(2)}, u32[]{:S(2)}) collective-permute-start(bf16[16,1024]{1,0:T(8,128)(2,1)S(1)} %fusion.22), channel_id=1, source_target_pairs={{0,16},{1,17},{2,18},{3,19},{4,20},{5,21},{6,22},{7,23},{8,24},{9,... | collective-permute-start | bytes 98312 | tf_op jit(solution)/shard_map/ppermute | solution.py:29
  103.0 2.0 %collective-permute-start.32 = (bf16[16,1024]{1,0:T(8,128)(2,1)S(1)}, bf16[16,1024]{1,0:T(8,128)(2,1)S(1)}, u32[]{:S(2)}, u32[]{:S(2)}) collective-permute-start(bf16[16,1024]{1,0:T(8,128)(2,1)S(1)} %fusion.23), channel_id=1, source_target_pairs={{144,172},{145,173},{146,174},{147,175},{148,168},{149,169},{150,1... | collective-permute-start | bytes 98312 | tf_op jit(solution)/shard_map/ppermute | solution.py:29
  103.6 1.3 collective-permute-start.33
  111.7 4.1 %collective-permute-start.34 = (bf16[16,1024]{1,0:T(8,128)(2,1)S(1)}, bf16[16,1024]{1,0:T(8,128)(2,1)S(1)}, u32[]{:S(2)}, u32[]{:S(2)}) collective-permute-start(bf16[16,1024]{1,0:T(8,128)(2,1)S(1)} %fusion.24), channel_id=1, source_target_pairs={{0,20},{1,21},{2,22},{3,23},{4,16},{5,17},{6,18},{7,19},{8,28},{9,... | collective-permute-start | bytes 98312 | tf_op jit(solution)/shard_map/ppermute | solution.py:29
  111.7 4.1 %collective-permute-start.35 = (bf16[16,1024]{1,0:T(8,128)(2,1)S(1)}, bf16[16,1024]{1,0:T(8,128)(2,1)S(1)}, u32[]{:S(2)}, u32[]{:S(2)}) collective-permute-start(bf16[16,1024]{1,0:T(8,128)(2,1)S(1)} %fusion.24), channel_id=1, source_target_pairs={{0,16},{1,17},{2,18},{3,19},{4,20},{5,21},{6,22},{7,23},{8,24},{9,... | collective-permute-start | bytes 98312 | tf_op jit(solution)/shard_map/ppermute | solution.py:29
  112.9 6.9 %collective-permute-start.27 = (bf16[128,2048]{1,0:T(8,128)(2,1)S(1)}, bf16[128,2048]{1,0:T(8,128)(2,1)}, u32[]{:S(2)}, u32[]{:S(2)}) collective-permute-start(bf16[128,2048]{1,0:T(8,128)(2,1)S(1)} %bitcast.62), channel_id=1, source_target_pairs={{0,1},{1,0},{2,3},{3,2},{4,5},{5,4},{6,7},{7,6},{8,9},{9,8},{10,11... | collective-permute-start | bytes 1572872 | tf_op jit(solution)/shard_map/ppermute | solution.py:29
  114.4 5.5 %collective-permute-start.28 = (bf16[128,2048]{1,0:T(8,128)(2,1)S(1)}, bf16[128,2048]{1,0:T(8,128)(2,1)}, u32[]{:S(2)}, u32[]{:S(2)}) collective-permute-start(bf16[128,2048]{1,0:T(8,128)(2,1)S(1)} %bitcast.63), channel_id=1, source_target_pairs={{0,3},{1,2},{2,1},{3,0},{4,7},{5,6},{6,5},{7,4},{8,11},{9,10},{10,... | collective-permute-start | bytes 1572872 | tf_op jit(solution)/shard_map/ppermute | solution.py:29
  116.5 2.6 %collective-permute-start.36 = (bf16[16,1024]{1,0:T(8,128)(2,1)S(1)}, bf16[16,1024]{1,0:T(8,128)(2,1)}, u32[]{:S(2)}, u32[]{:S(2)}) collective-permute-start(bf16[16,1024]{1,0:T(8,128)(2,1)S(1)} %fusion.25), channel_id=1, source_target_pairs={{176,204},{177,205},{178,206},{179,207},{180,200},{181,201},{182,2... | collective-permute-start | bytes 98312 | tf_op jit(solution)/shard_map/ppermute | solution.py:29
  117.8 1.3 collective-permute-start.37
  120.5 23.4 %copy-start.11 = (bf16[16,1024]{1,0:T(8,128)(2,1)}, bf16[16,1024]{1,0:T(8,128)(2,1)S(1)}, u32[]{:S(2)}) copy-start(bf16[16,1024]{1,0:T(8,128)(2,1)S(1)} %fusion.26) | copy-start | bytes 98308
  120.5 3.5 %collective-permute-start.38 = (bf16[16,1024]{1,0:T(8,128)(2,1)S(1)}, bf16[16,1024]{1,0:T(8,128)(2,1)S(1)}, u32[]{:S(2)}, u32[]{:S(2)}) collective-permute-start(bf16[16,1024]{1,0:T(8,128)(2,1)S(1)} %fusion.26), channel_id=1, source_target_pairs={{0,20},{1,21},{2,22},{3,23},{4,16},{5,17},{6,18},{7,19},{8,28},{9,... | collective-permute-start | bytes 98312 | tf_op jit(solution)/shard_map/ppermute | solution.py:29
  121.1 3.0 %collective-permute-start.39 = (bf16[16,1024]{1,0:T(8,128)(2,1)S(1)}, bf16[16,1024]{1,0:T(8,128)(2,1)S(1)}, u32[]{:S(2)}, u32[]{:S(2)}) collective-permute-start(bf16[16,1024]{1,0:T(8,128)(2,1)S(1)} %fusion.26), channel_id=1, source_target_pairs={{0,16},{1,17},{2,18},{3,19},{4,20},{5,21},{6,22},{7,23},{8,24},{9,... | collective-permute-start | bytes 98312 | tf_op jit(solution)/shard_map/ppermute | solution.py:29
  124.7 19.3 %copy-start.12 = (bf16[16,1024]{1,0:T(8,128)(2,1)}, bf16[16,1024]{1,0:T(8,128)(2,1)S(1)}, u32[]{:S(2)}) copy-start(bf16[16,1024]{1,0:T(8,128)(2,1)S(1)} %fusion.27) | copy-start | bytes 98308
  124.7 17.5 %collective-permute-start.40 = (bf16[16,1024]{1,0:T(8,128)(2,1)S(1)}, bf16[16,1024]{1,0:T(8,128)(2,1)S(1)}, u32[]{:S(2)}, u32[]{:S(2)}) collective-permute-start(bf16[16,1024]{1,0:T(8,128)(2,1)S(1)} %fusion.27), channel_id=1, source_target_pairs={{208,236},{209,237},{210,238},{211,239},{212,232},{213,233},{214,2... | collective-permute-start | bytes 98312 | tf_op jit(solution)/shard_map/ppermute | solution.py:29
  126.0 16.7 %collective-permute-start.41 = (bf16[16,1024]{1,0:T(8,128)(2,1)S(1)}, bf16[16,1024]{1,0:T(8,128)(2,1)S(1)}, u32[]{:S(2)}, u32[]{:S(2)}) collective-permute-start(bf16[16,1024]{1,0:T(8,128)(2,1)S(1)} %fusion.27), channel_id=1, source_target_pairs={{208,224},{209,225},{210,226},{211,227},{212,228},{213,229},{214,2... | collective-permute-start | bytes 98312 | tf_op jit(solution)/shard_map/ppermute | solution.py:29
  144.0 4.1 %collective-permute-start.42 = (bf16[16,1024]{1,0:T(8,128)(2,1)}, bf16[16,1024]{1,0:T(8,128)(2,1)}, u32[]{:S(2)}, u32[]{:S(2)}) collective-permute-start(bf16[16,1024]{1,0:T(8,128)(2,1)} %fusion.28), channel_id=1, source_target_pairs={{0,20},{1,21},{2,22},{3,23},{4,16},{5,17},{6,18},{7,19},{8,28},{9,... | collective-permute-start | bytes 98312 | tf_op jit(solution)/shard_map/ppermute | solution.py:29
  144.0 4.1 %collective-permute-start.43 = (bf16[16,1024]{1,0:T(8,128)(2,1)}, bf16[16,1024]{1,0:T(8,128)(2,1)}, u32[]{:S(2)}, u32[]{:S(2)}) collective-permute-start(bf16[16,1024]{1,0:T(8,128)(2,1)} %fusion.28), channel_id=1, source_target_pairs={{0,16},{1,17},{2,18},{3,19},{4,20},{5,21},{6,22},{7,23},{8,24},{9,... | collective-permute-start | bytes 98312 | tf_op jit(solution)/shard_map/ppermute | solution.py:29
  150.2 4.5 %collective-permute-start.44 = (bf16[16,1024]{1,0:T(8,128)(2,1)}, bf16[16,1024]{1,0:T(8,128)(2,1)S(1)}, u32[]{:S(2)}, u32[]{:S(2)}) collective-permute-start(bf16[16,1024]{1,0:T(8,128)(2,1)} %fusion.30), channel_id=1, source_target_pairs={{0,4},{1,5},{2,6},{3,7},{4,0},{5,1},{6,2},{7,3},{8,12},{9,13},{10,... | collective-permute-start | bytes 98312 | tf_op jit(solution)/shard_map/ppermute | solution.py:29
  151.9 10.8 %collective-permute-start.29 = (bf16[128,2048]{1,0:T(8,128)(2,1)}, bf16[128,2048]{1,0:T(8,128)(2,1)}, u32[]{:S(2)}, u32[]{:S(2)}) collective-permute-start(bf16[128,2048]{1,0:T(8,128)(2,1)} %collective-permute-done.27.refs_3_), channel_id=1, source_target_pairs={{0,3},{1,2},{2,1},{3,0},{4,7},{5,6},{6,5},{7,4},{8,11},{9,10},{10,... | collective-permute-start | bytes 1572872 | tf_op jit(solution)/shard_map/ppermute | solution.py:29
  155.4 7.2 %collective-permute-start.48 = (bf16[16,1024]{1,0:T(8,128)(2,1)S(1)}, bf16[16,1024]{1,0:T(8,128)(2,1)S(1)}, u32[]{:S(2)}, u32[]{:S(2)}) collective-permute-start(bf16[16,1024]{1,0:T(8,128)(2,1)S(1)} %get-tuple-element.54), channel_id=1, source_target_pairs={{0,12},{1,13},{2,14},{3,15},{4,8},{5,9},{6,10},{7,11},{8,4},{9,5},... | collective-permute-start | bytes 98312 | tf_op jit(solution)/shard_map/ppermute | solution.py:29
  156.9 5.1 %collective-permute-start.49 = (bf16[16,512]{1,0:T(8,128)(2,1)S(1)}, bf16[16,512]{1,0:T(8,128)(2,1)S(1)}, u32[]{:S(2)}, u32[]{:S(2)}) collective-permute-start(bf16[16,512]{1,0:T(8,128)(2,1)S(1)} %get-tuple-element.63), channel_id=1, source_target_pairs={{16,4},{17,5},{18,6},{19,7},{20,0},{21,1},{22,2},{23,3},{24,12},{2... | collective-permute-start | bytes 49160 | tf_op jit(solution)/shard_map/ppermute | solution.py:29
  159.2 3.4 %collective-permute-start.50 = (bf16[16,512]{1,0:T(8,128)(2,1)S(1)}, bf16[16,512]{1,0:T(8,128)(2,1)S(1)}, u32[]{:S(2)}, u32[]{:S(2)}) collective-permute-start(bf16[16,512]{1,0:T(8,128)(2,1)S(1)} %get-tuple-element.64), channel_id=1, source_target_pairs={{16,0},{17,1},{18,2},{19,3},{20,4},{21,5},{22,6},{23,7},{24,8},{25... | collective-permute-start | bytes 49160 | tf_op jit(solution)/shard_map/ppermute | solution.py:29
  166.4 13.2 %copy-start.4 = (f32[1,128,2048]{2,1,0:T(8,128)S(1)}, f32[1,128,2048]{2,1,0:T(8,128)}, u32[]{:S(2)}) copy-start(f32[1,128,2048]{2,1,0:T(8,128)} %param.8) | copy-start | bytes 3145732
  170.0 7.2 %collective-permute-start.45 = (bf16[128,512]{1,0:T(8,128)(2,1)S(1)}, bf16[128,512]{1,0:T(8,128)(2,1)S(1)}, u32[]{:S(2)}, u32[]{:S(2)}) collective-permute-start(bf16[128,512]{1,0:T(8,128)(2,1)S(1)} %get-tuple-element.38), channel_id=1, source_target_pairs={{0,1},{1,0},{2,3},{3,2},{4,5},{5,4},{6,7},{7,6},{8,9},{9,8},{10,11... | collective-permute-start | bytes 393224 | tf_op jit(solution)/shard_map/ppermute | solution.py:29
  170.6 9.1 %collective-permute-start.46 = (bf16[128,512]{1,0:T(8,128)(2,1)S(1)}, bf16[128,512]{1,0:T(8,128)(2,1)S(1)}, u32[]{:S(2)}, u32[]{:S(2)}) collective-permute-start(bf16[128,512]{1,0:T(8,128)(2,1)S(1)} %get-tuple-element.39), channel_id=1, source_target_pairs={{0,2},{1,3},{2,0},{3,1},{4,6},{5,7},{6,4},{7,5},{8,10},{9,11},{10,... | collective-permute-start | bytes 393224 | tf_op jit(solution)/shard_map/ppermute | solution.py:29
  172.3 7.3 %collective-permute-start.47 = (bf16[128,512]{1,0:T(8,128)(2,1)S(1)}, bf16[128,512]{1,0:T(8,128)(2,1)S(1)}, u32[]{:S(2)}, u32[]{:S(2)}) collective-permute-start(bf16[128,512]{1,0:T(8,128)(2,1)S(1)} %get-tuple-element.40), channel_id=1, source_target_pairs={{0,3},{1,2},{2,1},{3,0},{4,7},{5,6},{6,5},{7,4},{8,11},{9,10},{10,... | collective-permute-start | bytes 393224 | tf_op jit(solution)/shard_map/ppermute | solution.py:29
  174.8 6.7 %collective-permute-start.51 = (bf16[16,2432]{1,0:T(8,128)(2,1)S(1)}, bf16[16,2432]{1,0:T(8,128)(2,1)S(1)}, u32[]{:S(2)}, u32[]{:S(2)}) collective-permute-start(bf16[16,2432]{1,0:T(8,128)(2,1)S(1)} %get-tuple-element.50), channel_id=1, source_target_pairs={{0,1},{1,0},{2,3},{3,2},{4,5},{5,4},{6,7},{7,6},{8,9},{9,8},{10,11... | collective-permute-start | bytes 233480 | tf_op jit(solution)/shard_map/ppermute | solution.py:29
  174.9 6.6 %collective-permute-start.52 = (bf16[16,2432]{1,0:T(8,128)(2,1)S(1)}, bf16[16,2432]{1,0:T(8,128)(2,1)S(1)}, u32[]{:S(2)}, u32[]{:S(2)}) collective-permute-start(bf16[16,2432]{1,0:T(8,128)(2,1)S(1)} %get-tuple-element.51), channel_id=1, source_target_pairs={{0,2},{1,3},{2,0},{3,1},{4,6},{5,7},{6,4},{7,5},{8,10},{9,11},{10,... | collective-permute-start | bytes 233480 | tf_op jit(solution)/shard_map/ppermute | solution.py:29
  177.2 5.6 %collective-permute-start.53 = (bf16[16,2432]{1,0:T(8,128)(2,1)S(1)}, bf16[16,2432]{1,0:T(8,128)(2,1)S(1)}, u32[]{:S(2)}, u32[]{:S(2)}) collective-permute-start(bf16[16,2432]{1,0:T(8,128)(2,1)S(1)} %get-tuple-element.49), channel_id=1, source_target_pairs={{0,3},{1,2},{2,1},{3,0},{4,7},{5,6},{6,5},{7,4},{8,11},{9,10},{10,... | collective-permute-start | bytes 233480 | tf_op jit(solution)/shard_map/ppermute | solution.py:29
  (7 other events, 11.5 us)
Sparse Core Ops, SparseCore 0:
  9.8 33.8 all-gather.3
  59.5 32.2 all-gather.5
  119.2 36.0 all-gather.7

commit v6 on v4

--- a/solution.py
+++ b/solution.py
@@ -119,21 +119,45 @@
         )
 
 
-def gather_groups(along_reduce):
+def inner_kernel(place, second, right, *refs):
+    *left, out = refs
+    size, cut = left[0].shape
+
+    def dot(a, b):
+        return lax.dot_general(a, b, (((1,), (1,)), ((), ())), preferred_element_type=f32)
+
+    for step in range(SIDE):
+        target = block_of(place[1] ^ step, size)
+
+        def by_rows(step=step, target=target):
+            value = dot(left[step][...], second[:, :cut]) + dot(right[target, :], second[:, cut:])
+            out[target, :] = value.astype(bf16)
+
+        def by_columns(step=step, target=target):
+            value = dot(second[:, :cut], left[step][...]) + dot(second[:, cut:], right[target, :])
+            out[:, target] = value.astype(bf16)
+
+        pl.when(place[0] == 1)(by_columns)
+        pl.when(place[0] == 0)(by_rows)
+
+
+def over_axis(array, axis):
+    if axis == "x":
+        groups = [[k * SIDE + i for i in range(SIDE)] for k in range(SIDE)]
+    else:
+        groups = [[i * SIDE + k for i in range(SIDE)] for k in range(SIDE)]
+    return lax.all_gather(array, "blk", axis=0, tiled=True, axis_index_groups=groups)
+
+
+def over_parity(array, reduce_axis):
     groups = []
     for p in range(PARTITIONS):
         for k in range(SIDE):
-            if (p % 2 == 0) == along_reduce:
-                groups.append([p * PLANE + k * SIDE + x for x in range(SIDE)])
+            if (p % 2 == 0) == reduce_axis:
+                groups.append([p * PLANE + k * SIDE + i for i in range(SIDE)])
             else:
-                groups.append([p * PLANE + y * SIDE + k for y in range(SIDE)])
-    return groups
-
-
-def gathered(array, along_reduce):
-    return lax.all_gather(
-        array, AXES, axis=0, tiled=True, axis_index_groups=gather_groups(along_reduce)
-    )
+                groups.append([p * PLANE + i * SIDE + k for i in range(SIDE)])
+    return lax.all_gather(array, AXES, axis=0, tiled=True, axis_index_groups=groups)
 
 
 def along_reduce(value, step):
@@ -166,14 +190,9 @@
     away_high = jnp.where(even, 2 + ring, 3 - 2 * pair)
     place = jnp.stack([x, y])
 
-    coupling_in = gathered(coupling_rows, False)
-    inverse_out = gathered(inverse_rows, True)
-    turned = jnp.where(
-        even,
-        coupling_rows,
-        coupling_rows.reshape(rows, SIDE, SIDE, rows).transpose(0, 2, 1, 3).reshape(rows, nodes),
-    )
-    coupling_out = gathered(turned, True)
+    first = jnp.where(even, coupling_rows, inverse_rows)
+    second = jnp.where(even, inverse_rows, coupling_rows)
+    first_right = over_axis(first[:, nodes // 2 :], "y")
 
     def ordered(pieces):
         stacked = jnp.stack(pieces)
@@ -198,6 +217,16 @@
         out_place == 0, jnp.concatenate([keep, got]), jnp.concatenate([got, keep])
     )
     pieces = spread_x(two)
+    left, second, coupling_rows = tie((first[:, : nodes // 2], second, coupling_rows), two)
+    second = over_axis(second, "x")
+    first_left = [left] + [along_y(left, step) for step in (1, 2, 3)]
+    turned = jnp.where(
+        even,
+        coupling_rows,
+        coupling_rows.reshape(rows, SIDE, SIDE, rows).transpose(0, 2, 1, 3).reshape(rows, nodes),
+    )
+    coupling_out = over_parity(turned, True)
+    pieces = tie(pieces, first_left, turned)
     source_rows, weight_row = tie((source_rows, weight_row), two)
     started = weight_row[None, :] * source_rows
 
@@ -226,12 +255,16 @@
     for turn in range(1, PARTITIONS):
         far, near = turn_messages(message, turn - 1)
         previous = (far.astype(f32) + near.astype(f32)).astype(bf16)
-        if turn == 8:
-            inverse_out, coupling_in = tie((inverse_out, coupling_in), message)
-            inner = lax.dot_general(
-                inverse_out, coupling_in, (((1,), (1,)), ((), ())), preferred_element_type=f32
-            ).astype(bf16)
-            inner_all = gathered(inner, False)
+        if turn == 12:
+            second, first_right = tie((second, first_right), message)
+            (inner,) = kernel_call(
+                inner_kernel,
+                jnp.stack([even.astype(jnp.int32), y]),
+                [second, first_right] + first_left,
+                [shape((line, line), bf16)],
+                flops=2 * line * line * nodes,
+            )
+            inner_all = over_parity(inner, False)
             previous = tie(previous, inner)
         product = lax.dot_general(
             previous, block, (((1,), (1,)), ((), ())), preferred_element_type=f32
@@ -282,7 +315,7 @@
 
     last = exchange_x(last_chunk)
 
-    coupling_out, inner_all = tie((coupling_out, inner_all), lines)
+    coupling_out, inner_all = tie((coupling_out, inner_all), rounded)
     folded = jnp.dot(coupling_out, inner_all, preferred_element_type=f32).astype(bf16)
 
     def folded_chunk(step):

time: 175 us -> 181 us (1.034)
  waiting for transfers between devices: 81.4 us -> 69.5 us
  local copies, waits for them, and re-layouts: 3.99 us -> 13.2 us
  Pallas kernels: 4.48 us -> 8.96 us
  starting transfers between devices: 49.4 us -> 52.7 us
  other arithmetic: 1.36 us -> 4.34 us
  matrix products: 17.9 us -> 15.1 us
    unnamed x10 -> x34, local copies, waits for them, and re-layouts: 1.06 us -> 8.7 us
    ppermute x48 -> x51, waiting for transfers between devices: 69.1 us -> 63.2 us  [permuted(): return lax.ppermute(value, AXES, pairs)]
    all_gather x4, waiting for transfers between devices: 10.9 us -> 6.18 us  [the longest x2 6.18 us: over_parity(): lax.all_gather(array, AXES, axis=0, tiled=True, axis_index_groups=groups)]
    pallas_call x4 -> x5, Pallas kernels: 4.48 us -> 8.96 us  [kernel_call(): pl.pallas_call(body, out_shape=out_shapes, in_specs=[pl.BlockSpec(memory_...]
    dot_general x1 -> x0, matrix products: 4.3 us -> none  [shards(): lax.dot_general(inverse_out, coupling_in, (((1,), (1,)), ((), ())), prefe...]
    ppermute x48 -> x51, starting transfers between devices: 49.2 us -> 52.5 us  [permuted(): return lax.ppermute(value, AXES, pairs)]
    reshape x1 -> x3, local copies, waits for them, and re-layouts: 1.42 us -> 3.59 us  [shards(): coupling_rows.reshape(rows, SIDE, SIDE, rows).transpose(0, 2, 1, 3)]
    select_n x0 -> x1, other arithmetic: none -> 2.14 us  [shards(): second = jnp.where(even, inverse_rows, coupling_rows)]
  transfers between devices with their start and end apart: 52 -> 55, of which waited for: 20 -> 22; matrix products, arithmetic and copies ran while one was open for 11% -> 10% of each run, Pallas kernels for 2% -> 4%
where the time goes in v6:
time: 181 us; the launch traced here: 178 us
  waiting for transfers between devices  69.5 us (38%)
  starting transfers between devices  52.7 us (29%)
  matrix products  15.1 us (8%)
  between operations  14.4 us (8%)
  local copies, waits for them, and re-layouts  13.2 us (7%)
  Pallas kernels  8.96 us (5%)
  other arithmetic  4.34 us (2%)
    ppermute x51, waiting for transfers between devices, permuted(): return lax.ppermute(value, AXES, pairs)  63.2 us
    ppermute x51, starting transfers between devices, permuted(): return lax.ppermute(value, AXES, pairs)  52.5 us
    dot_general x15, matrix products, shards(): lax.dot_general(previous, block, (((1,), (1,)), ((), ())), preferred_elem...  11.3 us
    pallas_call x5, Pallas kernels, kernel_call(): pl.pallas_call(body, out_shape=out_shapes, in_specs=[pl.BlockSpec(memory_...  8.96 us
    unnamed x34, local copies, waits for them, and re-layouts  8.7 us
    all_gather x2, waiting for transfers between devices, over_parity(): lax.all_gather(array, AXES, axis=0, tiled=True, axis_index_groups=groups)  6.18 us
  transfers between devices with their start and end apart: 55, of which 22 were waited for; matrix products, arithmetic and copies ran while one was open for 10% of the time, Pallas kernels for 4%

profile of v6, /device:TPU:224, one launch (start us, length us, event | category | flops | bytes accessed | tf_op | source)
XLA Modules:
  0.0 178.1 jit_solution(9694236564459029453)
XLA Ops:
  7.2 2.1 %bitcast_select_fusion = (bf16[128,2048]{1,0:T(8,128)(2,1)}, bf16[128,2048]{1,0:T(8,128)(2,1)S(1)}) fusion(bf16[1,128,2048]{2,1,0:T(8,128)(2,1)} %param.6, pred[]{:T(512)S(6)} %eq.59, bf16[1,128,2048]{2,1,0:T(8,128)(2,1)} %param.7), kind=kLoop, calls=%fused_computation.49 | loop fusion | flops 524288 | bytes 2097153 | tf_op jit(solution)/shard_map/jit(_where)/select_n | solution.py:194
  9.4 0.7 fusion.35
  10.9 1.7 collective-permute-start
  12.5 4.8 %collective-permute-done = bf16[128,1024]{1,0:T(8,128)(2,1)S(1)} collective-permute-done((bf16[128,1024]{1,0:T(8,128)(2,1)S(1)}, bf16[128,1024]{1,0:T(8,128)(2,1)S(1)}, u32[]{:S(2)}, u32[]{:S(2)}) %collective-permute-start) | collective-permute-done | bytes 262176 | tf_op jit(solution)/shard_map/ppermute | solution.py:29
  17.7 1.6 collective-permute-start.1
  19.2 2.7 %collective-permute-start.2 = (f32[24,128]{1,0:T(8,128)S(1)}, f32[24,128]{1,0:T(8,128)S(1)}, u32[]{:S(2)}, u32[]{:S(2)}) collective-permute-start(f32[24,128]{1,0:T(8,128)S(1)} %get-tuple-element.87), channel_id=1, source_target_pairs={{0,2},{1,3},{2,0},{3,1},{4,6},{5,7},{6,4},{7,5},{8,10},{9,11},{10,... | collective-permute-start | bytes 36872 | tf_op jit(solution)/shard_map/ppermute | solution.py:29
  22.5 1.6 collective-permute-start.10
  24.4 2.4 %collective-permute-done.3 = f32[24,128]{1,0:T(8,128)S(1)} collective-permute-done((f32[24,128]{1,0:T(8,128)S(1)}, f32[24,128]{1,0:T(8,128)S(1)}, u32[]{:S(2)}, u32[]{:S(2)}) %collective-permute-start.3) | collective-permute-done | bytes 12320 | tf_op jit(solution)/shard_map/ppermute | solution.py:29
  26.9 1.7 collective-permute-start.4
  28.6 2.9 %collective-permute-start.11 = (bf16[128,1024]{1,0:T(8,128)(2,1)S(1)}, bf16[128,1024]{1,0:T(8,128)(2,1)S(1)}, u32[]{:S(2)}, u32[]{:S(2)}) collective-permute-start(bf16[128,1024]{1,0:T(8,128)(2,1)S(1)} %get-tuple-element.29.refs_0_), channel_id=1, source_target_pairs={{0,8},{1,9},{2,10},{3,11},{4,12},{5,13},{6,14},{7,15},{8,0},{9,1},... | collective-permute-start | bytes 786440 | tf_op jit(solution)/shard_map/ppermute | solution.py:29
  31.8 1.2 reshape.47
  33.0 1.3 copy.11
  34.2 1.2 reshape.48
  35.4 1.6 collective-permute-done.4
  36.9 1.6 collective-permute-start.8
  39.3 1.5 collective-permute-start.9
  40.8 0.9 broadcast_select_fusion
  41.7 4.6 %collective-permute-done.11.refs_2_ = bf16[128,1024]{1,0:T(8,128)(2,1)S(1)} collective-permute-done((bf16[128,1024]{1,0:T(8,128)(2,1)S(1)}, bf16[128,1024]{1,0:T(8,128)(2,1)S(1)}, u32[]{:S(2)}, u32[]{:S(2)}) %collective-permute-start.11) | collective-permute-done | bytes 262176 | tf_op jit(solution)/shard_map/ppermute | solution.py:29
  47.0 0.8 collective-permute-done.12.refs_3_
  48.5 6.6 %collective-permute-done.8.refs_2_ = bf16[256,1024]{1,0:T(8,128)(2,1)S(1)} collective-permute-done((bf16[256,1024]{1,0:T(8,128)(2,1)S(1)}, bf16[256,1024]{1,0:T(8,128)(2,1)S(1)}, u32[]{:S(2)}, u32[]{:S(2)}) %collective-permute-start.8) | collective-permute-done | bytes 524320 | tf_op jit(solution)/shard_map/ppermute | solution.py:29
  55.1 0.8 copy-done.3
  55.9 6.0 %collective-permute-done.9.refs_3_ = bf16[256,1024]{1,0:T(8,128)(2,1)S(1)} collective-permute-done((bf16[256,1024]{1,0:T(8,128)(2,1)S(1)}, bf16[256,1024]{1,0:T(8,128)(2,1)S(1)}, u32[]{:S(2)}, u32[]{:S(2)}) %collective-permute-start.9) | collective-permute-done | bytes 524320 | tf_op jit(solution)/shard_map/ppermute | solution.py:29
  62.0 0.8 copy-done.5
  62.8 1.0 copy-done.4
  63.8 1.0 copy-done.6
  68.3 1.2 collective-permute-start.16
  69.5 2.1 %collective-permute-done.15 = bf16[16,1024]{1,0:T(8,128)(2,1)S(1)} collective-permute-done((bf16[16,1024]{1,0:T(8,128)(2,1)S(1)}, bf16[16,1024]{1,0:T(8,128)(2,1)S(1)}, u32[]{:S(2)}, u32[]{:S(2)}) %collective-permute-start.15) | collective-permute-done | bytes 32800 | tf_op jit(solution)/shard_map/ppermute | solution.py:29
  73.0 0.8 collective-permute-start.18
  74.9 0.8 collective-permute-start.20
  75.7 2.4 %collective-permute-done.19 = bf16[16,1024]{1,0:T(8,128)(2,1)S(1)} collective-permute-done((bf16[16,1024]{1,0:T(8,128)(2,1)S(1)}, bf16[16,1024]{1,0:T(8,128)(2,1)S(1)}, u32[]{:S(2)}, u32[]{:S(2)}) %collective-permute-start.19) | collective-permute-done | bytes 32800 | tf_op jit(solution)/shard_map/ppermute | solution.py:29
  82.0 2.2 %collective-permute-done.23 = bf16[16,1024]{1,0:T(8,128)(2,1)S(1)} collective-permute-done((bf16[16,1024]{1,0:T(8,128)(2,1)S(1)}, bf16[16,1024]{1,0:T(8,128)(2,1)S(1)}, u32[]{:S(2)}, u32[]{:S(2)}) %collective-permute-start.23) | collective-permute-done | bytes 32800 | tf_op jit(solution)/shard_map/ppermute | solution.py:29
  86.8 0.9 collective-permute-start.27
  88.1 2.1 %collective-permute-done.27 = bf16[16,1024]{1,0:T(8,128)(2,1)S(1)} collective-permute-done((bf16[16,1024]{1,0:T(8,128)(2,1)S(1)}, bf16[16,1024]{1,0:T(8,128)(2,1)S(1)}, u32[]{:S(2)}, u32[]{:S(2)}) %collective-permute-start.27) | collective-permute-done | bytes 32800 | tf_op jit(solution)/shard_map/ppermute | solution.py:29
  90.8 1.3 collective-permute-start.29
  92.1 1.3 collective-permute-start.30
  93.4 1.5 fusion.24
  94.9 0.9 collective-permute-start.31
  96.3 2.0 %collective-permute-done.31 = bf16[16,1024]{1,0:T(8,128)(2,1)S(1)} collective-permute-done((bf16[16,1024]{1,0:T(8,128)(2,1)S(1)}, bf16[16,1024]{1,0:T(8,128)(2,1)S(1)}, u32[]{:S(2)}, u32[]{:S(2)}) %collective-permute-start.31) | collective-permute-done | bytes 32800 | tf_op jit(solution)/shard_map/ppermute | solution.py:29
  98.2 1.3 fusion.25
  99.5 1.3 collective-permute-start.33
  100.8 1.3 collective-permute-start.34
  102.1 1.6 copy-done
  103.7 1.2 copy-done.1
  105.0 4.5 %shard_map.87 = bf16[512,512]{1,0:T(8,128)(2,1)} custom-call(s32[2]{0:T(128)S(1)} %pad_add_fusion.2.place, bf16[512,2048]{1,0:T(8,128)(2,1)S(1)} %copy-done, bf16[512,1024]{1,0:T(8,128)(2,1)S(1)} %copy-done.1, bf16[128,1024]{1,0:T(8,128)(2,1)S(1)} %get-tuple-element.29.refs_0_, bf16[128,1024]{1,0:T(8,128)(2,1)S(1)} %copy-done.9, ...), custom_call_target="tpu_custom_call" | custom-call | flops 1073741824 | bytes 4718592 | tf_op jit(solution)/shard_map/pallas_call | solution.py:58
  109.5 0.8 add_convert_fusion.3
  110.9 1.8 collective-permute-start.35
  112.7 1.6 collective-permute-done.35
  115.0 1.3 collective-permute-start.37
  116.3 1.3 collective-permute-start.38
  117.6 11.5 %collective-permute-done.37 = bf16[16,1024]{1,0:T(8,128)(2,1)S(1)} collective-permute-done((bf16[16,1024]{1,0:T(8,128)(2,1)S(1)}, bf16[16,1024]{1,0:T(8,128)(2,1)S(1)}, u32[]{:S(2)}, u32[]{:S(2)}) %collective-permute-start.37) | collective-permute-done | bytes 32800 | tf_op jit(solution)/shard_map/ppermute | solution.py:29
  129.9 3.2 %collective-permute-done.39 = bf16[16,1024]{1,0:T(8,128)(2,1)S(1)} collective-permute-done((bf16[16,1024]{1,0:T(8,128)(2,1)S(1)}, bf16[16,1024]{1,0:T(8,128)(2,1)S(1)}, u32[]{:S(2)}, u32[]{:S(2)}) %collective-permute-start.39) | collective-permute-done | bytes 32800 | tf_op jit(solution)/shard_map/ppermute | solution.py:29
  133.9 3.8 %collective-permute-done.41 = bf16[16,1024]{1,0:T(8,128)(2,1)S(1)} collective-permute-done((bf16[16,1024]{1,0:T(8,128)(2,1)S(1)}, bf16[16,1024]{1,0:T(8,128)(2,1)S(1)}, u32[]{:S(2)}, u32[]{:S(2)}) %collective-permute-start.41) | collective-permute-done | bytes 32800 | tf_op jit(solution)/shard_map/ppermute | solution.py:29
  137.7 1.9 %collective-permute-start.45 = (bf16[16,1024]{1,0:T(8,128)(2,1)S(1)}, bf16[16,1024]{1,0:T(8,128)(2,1)S(1)}, u32[]{:S(2)}, u32[]{:S(2)}) collective-permute-start(bf16[16,1024]{1,0:T(8,128)(2,1)S(1)} %get-tuple-element.58), channel_id=1, source_target_pairs={{0,12},{1,13},{2,14},{3,15},{4,8},{5,9},{6,10},{7,11},{8,4},{9,5},... | collective-permute-start | bytes 98312 | tf_op jit(solution)/shard_map/ppermute | solution.py:29
  140.1 1.9 %collective-permute-start.46 = (bf16[16,512]{1,0:T(8,128)(2,1)S(1)}, bf16[16,512]{1,0:T(8,128)(2,1)S(1)}, u32[]{:S(2)}, u32[]{:S(2)}) collective-permute-start(bf16[16,512]{1,0:T(8,128)(2,1)S(1)} %get-tuple-element.67), channel_id=1, source_target_pairs={{16,4},{17,5},{18,6},{19,7},{20,0},{21,1},{22,2},{23,3},{24,12},{2... | collective-permute-start | bytes 49160 | tf_op jit(solution)/shard_map/ppermute | solution.py:29
  142.0 1.9 %collective-permute-start.47 = (bf16[16,512]{1,0:T(8,128)(2,1)S(1)}, bf16[16,512]{1,0:T(8,128)(2,1)S(1)}, u32[]{:S(2)}, u32[]{:S(2)}) collective-permute-start(bf16[16,512]{1,0:T(8,128)(2,1)S(1)} %get-tuple-element.68), channel_id=1, source_target_pairs={{16,0},{17,1},{18,2},{19,3},{20,4},{21,5},{22,6},{23,7},{24,8},{25... | collective-permute-start | bytes 49160 | tf_op jit(solution)/shard_map/ppermute | solution.py:29
  144.0 1.2 collective-permute-done.46
  145.4 6.2 %all-gather.11.cloned.1.call-done = bf16[2048,512]{1,0:T(8,128)(2,1)} async-done(((bf16[512,512]{1,0:T(8,128)(2,1)}), bf16[2048,512]{1,0:T(8,128)(2,1)}) %all-gather.11.cloned.1.call-update) | async-done | bytes 2097168 | tf_op jit(solution)/shard_map/all_gather | solution.py:160
  151.6 3.5 %convolution_convert_fusion = bf16[512,512]{1,0:T(8,128)(2,1)S(1)} fusion(bf16[512,2048]{1,0:T(8,128)(2,1)} %all-gather.5.cloned.1.call-done, bf16[2048,512]{1,0:T(8,128)(2,1)} %all-gather.11.cloned.1.call-done), kind=kOutput, calls=%fused_computation | convolution fusion | flops 1074003968 | bytes 4718592 | tf_op jit(solution)/shard_map/dot_general | solution.py:319
  155.1 1.8 %collective-permute-start.42 = (bf16[128,512]{1,0:T(8,128)(2,1)S(1)}, bf16[128,512]{1,0:T(8,128)(2,1)S(1)}, u32[]{:S(2)}, u32[]{:S(2)}) collective-permute-start(bf16[128,512]{1,0:T(8,128)(2,1)S(1)} %get-tuple-element.49), channel_id=1, source_target_pairs={{0,1},{1,0},{2,3},{3,2},{4,5},{5,4},{6,7},{7,6},{8,9},{9,8},{10,11... | collective-permute-start | bytes 393224 | tf_op jit(solution)/shard_map/ppermute | solution.py:29
  156.9 2.4 %collective-permute-start.43 = (bf16[128,512]{1,0:T(8,128)(2,1)S(1)}, bf16[128,512]{1,0:T(8,128)(2,1)S(1)}, u32[]{:S(2)}, u32[]{:S(2)}) collective-permute-start(bf16[128,512]{1,0:T(8,128)(2,1)S(1)} %get-tuple-element.48), channel_id=1, source_target_pairs={{0,2},{1,3},{2,0},{3,1},{4,6},{5,7},{6,4},{7,5},{8,10},{9,11},{10,... | collective-permute-start | bytes 393224 | tf_op jit(solution)/shard_map/ppermute | solution.py:29
  160.5 3.6 %collective-permute-start.49 = (bf16[16,2432]{1,0:T(8,128)(2,1)S(1)}, bf16[16,2432]{1,0:T(8,128)(2,1)S(1)}, u32[]{:S(2)}, u32[]{:S(2)}) collective-permute-start(bf16[16,2432]{1,0:T(8,128)(2,1)S(1)} %get-tuple-element.55), channel_id=1, source_target_pairs={{0,2},{1,3},{2,0},{3,1},{4,6},{5,7},{6,4},{7,5},{8,10},{9,11},{10,... | collective-permute-start | bytes 233480 | tf_op jit(solution)/shard_map/ppermute | solution.py:29
  165.4 3.0 %collective-permute-done.44.refs_4_ = bf16[128,512]{1,0:T(8,128)(2,1)S(1)} collective-permute-done((bf16[128,512]{1,0:T(8,128)(2,1)S(1)}, bf16[128,512]{1,0:T(8,128)(2,1)S(1)}, u32[]{:S(2)}, u32[]{:S(2)}) %collective-permute-start.44) | collective-permute-done | bytes 131104 | tf_op jit(solution)/shard_map/ppermute | solution.py:29
  168.4 1.8 shard_map.88
  170.1 1.5 shard_map.89
  (140 shorter events, 24.1 us)
Async XLA Ops:
  7.2 3.1 %copy-start.7 = (bf16[1,128,2048]{2,1,0:T(8,128)(2,1)S(1)}, bf16[1,128,2048]{2,1,0:T(8,128)(2,1)}, u32[]{:S(2)}) copy-start(bf16[1,128,2048]{2,1,0:T(8,128)(2,1)} %param.9) | copy-start | bytes 1572868
  7.2 94.9 %all-gather.9.cloned.1.call-start = ((), (), s32[]{:S(2)}) async-start(), calls=%async_computation.2 | async-start | bytes 1310720 | tf_op jit(solution)/shard_map/all_gather | solution.py:149
  9.4 8.2 %copy-start.14 = (f32[1,128]{1,0:T(1,128)S(1)}, f32[1,128]{1,0:T(1,128)}, u32[]{:S(2)}) copy-start(f32[1,128]{1,0:T(1,128)} %param.11) | copy-start | bytes 1540
  9.4 8.2 %copy-start.16 = (f32[1,64,128]{2,1,0:T(8,128)S(1)}, f32[1,64,128]{2,1,0:T(8,128)}, u32[]{:S(2)}) copy-start(f32[1,64,128]{2,1,0:T(8,128)} %param.10) | copy-start | bytes 98308
  9.4 22.4 %copy-start.15 = (bf16[1,128,2048]{2,1,0:T(8,128)(2,1)S(1)}, bf16[1,128,2048]{2,1,0:T(8,128)(2,1)}, u32[]{:S(2)}) copy-start(bf16[1,128,2048]{2,1,0:T(8,128)(2,1)} %param.7) | copy-start | bytes 1572868
  10.1 91.9 %all-gather.7.cloned.1.call-start = ((), (), s32[]{:S(2)}) async-start(), calls=%async_computation.1 | async-start | bytes 2621440 | tf_op jit(solution)/shard_map/all_gather | solution.py:149
  10.9 6.5 %collective-permute-start = (bf16[128,1024]{1,0:T(8,128)(2,1)S(1)}, bf16[128,1024]{1,0:T(8,128)(2,1)S(1)}, u32[]{:S(2)}, u32[]{:S(2)}) collective-permute-start(bf16[128,1024]{1,0:T(8,128)(2,1)S(1)} %get-tuple-element.24), channel_id=1, source_target_pairs={{0,4},{1,5},{2,6},{3,7},{4,0},{5,1},{6,2},{7,3},{8,12},{9,13},{10,... | collective-permute-start | bytes 786440 | tf_op jit(solution)/shard_map/ppermute | solution.py:29
  17.5 127.9 %all-gather.5.cloned.1.call-start = ((), (), s32[]{:S(2)}) async-start(), calls=%async_computation | async-start | bytes 2621440 | tf_op jit(solution)/shard_map/all_gather | solution.py:160
  17.7 6.4 %collective-permute-start.1 = (f32[24,128]{1,0:T(8,128)S(1)}, f32[24,128]{1,0:T(8,128)S(1)}, u32[]{:S(2)}, u32[]{:S(2)}) collective-permute-start(f32[24,128]{1,0:T(8,128)S(1)} %get-tuple-element.86), channel_id=1, source_target_pairs={{0,1},{1,0},{2,3},{3,2},{4,5},{5,4},{6,7},{7,6},{8,9},{9,8},{10,11... | collective-permute-start | bytes 36872 | tf_op jit(solution)/shard_map/ppermute | solution.py:29
  19.2 5.2 %collective-permute-start.2 = (f32[24,128]{1,0:T(8,128)S(1)}, f32[24,128]{1,0:T(8,128)S(1)}, u32[]{:S(2)}, u32[]{:S(2)}) collective-permute-start(f32[24,128]{1,0:T(8,128)S(1)} %get-tuple-element.87), channel_id=1, source_target_pairs={{0,2},{1,3},{2,0},{3,1},{4,6},{5,7},{6,4},{7,5},{8,10},{9,11},{10,... | collective-permute-start | bytes 36872 | tf_op jit(solution)/shard_map/ppermute | solution.py:29
  22.0 4.9 %collective-permute-start.3 = (f32[24,128]{1,0:T(8,128)S(1)}, f32[24,128]{1,0:T(8,128)S(1)}, u32[]{:S(2)}, u32[]{:S(2)}) collective-permute-start(f32[24,128]{1,0:T(8,128)S(1)} %get-tuple-element.88), channel_id=1, source_target_pairs={{0,3},{1,2},{2,1},{3,0},{4,7},{5,6},{6,5},{7,4},{8,11},{9,10},{10,... | collective-permute-start | bytes 36872 | tf_op jit(solution)/shard_map/ppermute | solution.py:29
  22.5 16.1 %collective-permute-start.10 = (bf16[128,1024]{1,0:T(8,128)(2,1)S(1)}, bf16[128,1024]{1,0:T(8,128)(2,1)S(1)}, u32[]{:S(2)}, u32[]{:S(2)}) collective-permute-start(bf16[128,1024]{1,0:T(8,128)(2,1)S(1)} %get-tuple-element.29.refs_0_), channel_id=1, source_target_pairs={{0,4},{1,5},{2,6},{3,7},{4,0},{5,1},{6,2},{7,3},{8,12},{9,13},{10,... | collective-permute-start | bytes 786440 | tf_op jit(solution)/shard_map/ppermute | solution.py:29
  26.9 10.0 %collective-permute-start.4 = (f32[1,512]{1,0:T(1,128)S(1)}, f32[1,512]{1,0:T(1,128)S(1)}, u32[]{:S(2)}, u32[]{:S(2)}) collective-permute-start(f32[1,512]{1,0:T(1,128)S(1)} %pad_maximum_fusion.10), channel_id=1, source_target_pairs={{0,4},{1,5},{2,6},{3,7},{4,0},{5,1},{6,2},{7,3},{8,12},{9,13},{10,... | collective-permute-start | bytes 6152 | tf_op jit(solution)/shard_map/ppermute | solution.py:29
  28.6 17.6 %collective-permute-start.11 = (bf16[128,1024]{1,0:T(8,128)(2,1)S(1)}, bf16[128,1024]{1,0:T(8,128)(2,1)S(1)}, u32[]{:S(2)}, u32[]{:S(2)}) collective-permute-start(bf16[128,1024]{1,0:T(8,128)(2,1)S(1)} %get-tuple-element.29.refs_0_), channel_id=1, source_target_pairs={{0,8},{1,9},{2,10},{3,11},{4,12},{5,13},{6,14},{7,15},{8,0},{9,1},... | collective-permute-start | bytes 786440 | tf_op jit(solution)/shard_map/ppermute | solution.py:29
  31.6 16.2 %collective-permute-start.12 = (bf16[128,1024]{1,0:T(8,128)(2,1)S(1)}, bf16[128,1024]{1,0:T(8,128)(2,1)S(1)}, u32[]{:S(2)}, u32[]{:S(2)}) collective-permute-start(bf16[128,1024]{1,0:T(8,128)(2,1)S(1)} %get-tuple-element.29.refs_0_), channel_id=1, source_target_pairs={{0,12},{1,13},{2,14},{3,15},{4,8},{5,9},{6,10},{7,11},{8,4},{9,5},... | collective-permute-start | bytes 786440 | tf_op jit(solution)/shard_map/ppermute | solution.py:29
  31.8 16.7 %collective-permute-start.7 = (bf16[256,1024]{1,0:T(8,128)(2,1)S(1)}, bf16[256,1024]{1,0:T(8,128)(2,1)S(1)}, u32[]{:S(2)}, u32[]{:S(2)}) collective-permute-start(bf16[256,1024]{1,0:T(8,128)(2,1)S(1)} %maximum_select_fusion.refs_0_), channel_id=1, source_target_pairs={{0,1},{1,0},{2,3},{3,2},{4,5},{5,4},{6,7},{7,6},{8,9},{9,8},{10,11... | collective-permute-start | bytes 1572872 | tf_op jit(solution)/shard_map/ppermute | solution.py:29
  36.9 18.2 %collective-permute-start.8 = (bf16[256,1024]{1,0:T(8,128)(2,1)S(1)}, bf16[256,1024]{1,0:T(8,128)(2,1)S(1)}, u32[]{:S(2)}, u32[]{:S(2)}) collective-permute-start(bf16[256,1024]{1,0:T(8,128)(2,1)S(1)} %maximum_select_fusion.refs_0_), channel_id=1, source_target_pairs={{0,2},{1,3},{2,0},{3,1},{4,6},{5,7},{6,4},{7,5},{8,10},{9,11},{10,... | collective-permute-start | bytes 1572872 | tf_op jit(solution)/shard_map/ppermute | solution.py:29
  39.3 22.7 %collective-permute-start.9 = (bf16[256,1024]{1,0:T(8,128)(2,1)S(1)}, bf16[256,1024]{1,0:T(8,128)(2,1)S(1)}, u32[]{:S(2)}, u32[]{:S(2)}) collective-permute-start(bf16[256,1024]{1,0:T(8,128)(2,1)S(1)} %maximum_select_fusion.refs_0_), channel_id=1, source_target_pairs={{0,3},{1,2},{2,1},{3,0},{4,7},{5,6},{6,5},{7,4},{8,11},{9,10},{10,... | collective-permute-start | bytes 1572872 | tf_op jit(solution)/shard_map/ppermute | solution.py:29
  47.0 18.5 %collective-permute-start.5 = (bf16[16,1024]{1,0:T(8,128)(2,1)S(1)}, bf16[16,1024]{1,0:T(8,128)(2,1)S(1)}, u32[]{:S(2)}, u32[]{:S(2)}) collective-permute-start(bf16[16,1024]{1,0:T(8,128)(2,1)S(1)} %fusion.32), channel_id=1, source_target_pairs={{0,20},{1,21},{2,22},{3,23},{4,16},{5,17},{6,18},{7,19},{8,28},{9,... | collective-permute-start | bytes 98312 | tf_op jit(solution)/shard_map/ppermute | solution.py:29
  48.5 17.1 %collective-permute-start.6 = (bf16[16,1024]{1,0:T(8,128)(2,1)S(1)}, bf16[16,1024]{1,0:T(8,128)(2,1)S(1)}, u32[]{:S(2)}, u32[]{:S(2)}) collective-permute-start(bf16[16,1024]{1,0:T(8,128)(2,1)S(1)} %fusion.32), channel_id=1, source_target_pairs={{0,16},{1,17},{2,18},{3,19},{4,20},{5,21},{6,22},{7,23},{8,24},{9,... | collective-permute-start | bytes 98312 | tf_op jit(solution)/shard_map/ppermute | solution.py:29
  66.2 1.4 collective-permute-start.13
  66.9 0.8 collective-permute-start.14
  67.6 84.0 %all-gather.11.cloned.1.call-start = ((), (), s32[]{:S(2)}) async-start(), calls=%async_computation.3 | async-start | bytes 2621440 | tf_op jit(solution)/shard_map/all_gather | solution.py:160
  68.3 3.4 %collective-permute-start.15 = (bf16[16,1024]{1,0:T(8,128)(2,1)S(1)}, bf16[16,1024]{1,0:T(8,128)(2,1)S(1)}, u32[]{:S(2)}, u32[]{:S(2)}) collective-permute-start(bf16[16,1024]{1,0:T(8,128)(2,1)S(1)} %fusion.16), channel_id=1, source_target_pairs={{0,20},{1,21},{2,22},{3,23},{4,16},{5,17},{6,18},{7,19},{8,28},{9,... | collective-permute-start | bytes 98312 | tf_op jit(solution)/shard_map/ppermute | solution.py:29
  68.3 3.4 %collective-permute-start.16 = (bf16[16,1024]{1,0:T(8,128)(2,1)S(1)}, bf16[16,1024]{1,0:T(8,128)(2,1)S(1)}, u32[]{:S(2)}, u32[]{:S(2)}) collective-permute-start(bf16[16,1024]{1,0:T(8,128)(2,1)S(1)} %fusion.16), channel_id=1, source_target_pairs={{0,16},{1,17},{2,18},{3,19},{4,20},{5,21},{6,22},{7,23},{8,24},{9,... | collective-permute-start | bytes 98312 | tf_op jit(solution)/shard_map/ppermute | solution.py:29
  72.3 1.5 collective-permute-start.17
  73.0 0.9 collective-permute-start.18
  74.5 3.6 %collective-permute-start.19 = (bf16[16,1024]{1,0:T(8,128)(2,1)S(1)}, bf16[16,1024]{1,0:T(8,128)(2,1)S(1)}, u32[]{:S(2)}, u32[]{:S(2)}) collective-permute-start(bf16[16,1024]{1,0:T(8,128)(2,1)S(1)} %fusion.18), channel_id=1, source_target_pairs={{0,20},{1,21},{2,22},{3,23},{4,16},{5,17},{6,18},{7,19},{8,28},{9,... | collective-permute-start | bytes 98312 | tf_op jit(solution)/shard_map/ppermute | solution.py:29
  74.9 3.2 %collective-permute-start.20 = (bf16[16,1024]{1,0:T(8,128)(2,1)S(1)}, bf16[16,1024]{1,0:T(8,128)(2,1)S(1)}, u32[]{:S(2)}, u32[]{:S(2)}) collective-permute-start(bf16[16,1024]{1,0:T(8,128)(2,1)S(1)} %fusion.18), channel_id=1, source_target_pairs={{0,16},{1,17},{2,18},{3,19},{4,20},{5,21},{6,22},{7,23},{8,24},{9,... | collective-permute-start | bytes 98312 | tf_op jit(solution)/shard_map/ppermute | solution.py:29
  78.8 1.3 collective-permute-start.21
  79.5 0.7 collective-permute-start.22
  80.8 3.4 %collective-permute-start.23 = (bf16[16,1024]{1,0:T(8,128)(2,1)S(1)}, bf16[16,1024]{1,0:T(8,128)(2,1)S(1)}, u32[]{:S(2)}, u32[]{:S(2)}) collective-permute-start(bf16[16,1024]{1,0:T(8,128)(2,1)S(1)} %fusion.20), channel_id=1, source_target_pairs={{0,20},{1,21},{2,22},{3,23},{4,16},{5,17},{6,18},{7,19},{8,28},{9,... | collective-permute-start | bytes 98312 | tf_op jit(solution)/shard_map/ppermute | solution.py:29
  81.5 2.6 %collective-permute-start.24 = (bf16[16,1024]{1,0:T(8,128)(2,1)S(1)}, bf16[16,1024]{1,0:T(8,128)(2,1)S(1)}, u32[]{:S(2)}, u32[]{:S(2)}) collective-permute-start(bf16[16,1024]{1,0:T(8,128)(2,1)S(1)} %fusion.20), channel_id=1, source_target_pairs={{0,16},{1,17},{2,18},{3,19},{4,20},{5,21},{6,22},{7,23},{8,24},{9,... | collective-permute-start | bytes 98312 | tf_op jit(solution)/shard_map/ppermute | solution.py:29
  84.8 1.3 collective-permute-start.25
  85.5 0.7 collective-permute-start.26
  86.8 3.4 %collective-permute-start.27 = (bf16[16,1024]{1,0:T(8,128)(2,1)S(1)}, bf16[16,1024]{1,0:T(8,128)(2,1)S(1)}, u32[]{:S(2)}, u32[]{:S(2)}) collective-permute-start(bf16[16,1024]{1,0:T(8,128)(2,1)S(1)} %fusion.22), channel_id=1, source_target_pairs={{0,20},{1,21},{2,22},{3,23},{4,16},{5,17},{6,18},{7,19},{8,28},{9,... | collective-permute-start | bytes 98312 | tf_op jit(solution)/shard_map/ppermute | solution.py:29
  87.7 2.5 %collective-permute-start.28 = (bf16[16,1024]{1,0:T(8,128)(2,1)S(1)}, bf16[16,1024]{1,0:T(8,128)(2,1)S(1)}, u32[]{:S(2)}, u32[]{:S(2)}) collective-permute-start(bf16[16,1024]{1,0:T(8,128)(2,1)S(1)} %fusion.22), channel_id=1, source_target_pairs={{0,16},{1,17},{2,18},{3,19},{4,20},{5,21},{6,22},{7,23},{8,24},{9,... | collective-permute-start | bytes 98312 | tf_op jit(solution)/shard_map/ppermute | solution.py:29
  90.8 2.6 %collective-permute-start.29 = (bf16[16,1024]{1,0:T(8,128)(2,1)S(1)}, bf16[16,1024]{1,0:T(8,128)(2,1)}, u32[]{:S(2)}, u32[]{:S(2)}) collective-permute-start(bf16[16,1024]{1,0:T(8,128)(2,1)S(1)} %fusion.23), channel_id=1, source_target_pairs={{144,172},{145,173},{146,174},{147,175},{148,168},{149,169},{150,1... | collective-permute-start | bytes 98312 | tf_op jit(solution)/shard_map/ppermute | solution.py:29
  92.1 1.3 collective-permute-start.30
  93.4 8.7 %copy-start.9 = (bf16[128,1024]{1,0:T(8,128)(2,1)S(1)}, bf16[128,1024]{1,0:T(8,128)(2,1)}, u32[]{:S(2)}) copy-start(bf16[128,1024]{1,0:T(8,128)(2,1)} %copy-done.8) | copy-start | bytes 786436
  93.4 8.7 %copy-start.11 = (bf16[128,1024]{1,0:T(8,128)(2,1)S(1)}, bf16[128,1024]{1,0:T(8,128)(2,1)}, u32[]{:S(2)}) copy-start(bf16[128,1024]{1,0:T(8,128)(2,1)} %copy-done.10) | copy-start | bytes 786436
  93.4 8.7 %copy-start.13 = (bf16[128,1024]{1,0:T(8,128)(2,1)S(1)}, bf16[128,1024]{1,0:T(8,128)(2,1)}, u32[]{:S(2)}) copy-start(bf16[128,1024]{1,0:T(8,128)(2,1)} %copy-done.12) | copy-start | bytes 786436
  94.9 3.3 %collective-permute-start.31 = (bf16[16,1024]{1,0:T(8,128)(2,1)S(1)}, bf16[16,1024]{1,0:T(8,128)(2,1)S(1)}, u32[]{:S(2)}, u32[]{:S(2)}) collective-permute-start(bf16[16,1024]{1,0:T(8,128)(2,1)S(1)} %fusion.24), channel_id=1, source_target_pairs={{0,20},{1,21},{2,22},{3,23},{4,16},{5,17},{6,18},{7,19},{8,28},{9,... | collective-permute-start | bytes 98312 | tf_op jit(solution)/shard_map/ppermute | solution.py:29
  95.8 2.5 %collective-permute-start.32 = (bf16[16,1024]{1,0:T(8,128)(2,1)S(1)}, bf16[16,1024]{1,0:T(8,128)(2,1)S(1)}, u32[]{:S(2)}, u32[]{:S(2)}) collective-permute-start(bf16[16,1024]{1,0:T(8,128)(2,1)S(1)} %fusion.24), channel_id=1, source_target_pairs={{0,16},{1,17},{2,18},{3,19},{4,20},{5,21},{6,22},{7,23},{8,24},{9,... | collective-permute-start | bytes 98312 | tf_op jit(solution)/shard_map/ppermute | solution.py:29
  99.5 9.9 %collective-permute-start.33 = (bf16[16,1024]{1,0:T(8,128)(2,1)}, bf16[16,1024]{1,0:T(8,128)(2,1)}, u32[]{:S(2)}, u32[]{:S(2)}) collective-permute-start(bf16[16,1024]{1,0:T(8,128)(2,1)} %fusion.25), channel_id=1, source_target_pairs={{176,204},{177,205},{178,206},{179,207},{180,200},{181,201},{182,2... | collective-permute-start | bytes 98312 | tf_op jit(solution)/shard_map/ppermute | solution.py:29
  100.8 8.7 %collective-permute-start.34 = (bf16[16,1024]{1,0:T(8,128)(2,1)}, bf16[16,1024]{1,0:T(8,128)(2,1)}, u32[]{:S(2)}, u32[]{:S(2)}) collective-permute-start(bf16[16,1024]{1,0:T(8,128)(2,1)} %fusion.25), channel_id=1, source_target_pairs={{176,192},{177,193},{178,194},{179,195},{180,196},{181,197},{182,1... | collective-permute-start | bytes 98312 | tf_op jit(solution)/shard_map/ppermute | solution.py:29
  102.1 1.6 copy-start
  110.9 3.4 %collective-permute-start.35 = (bf16[16,1024]{1,0:T(8,128)(2,1)S(1)}, bf16[16,1024]{1,0:T(8,128)(2,1)S(1)}, u32[]{:S(2)}, u32[]{:S(2)}) collective-permute-start(bf16[16,1024]{1,0:T(8,128)(2,1)S(1)} %fusion.26), channel_id=1, source_target_pairs={{0,20},{1,21},{2,22},{3,23},{4,16},{5,17},{6,18},{7,19},{8,28},{9,... | collective-permute-start | bytes 98312 | tf_op jit(solution)/shard_map/ppermute | solution.py:29
  112.7 1.6 collective-permute-start.36
  115.0 14.1 %collective-permute-start.37 = (bf16[16,1024]{1,0:T(8,128)(2,1)S(1)}, bf16[16,1024]{1,0:T(8,128)(2,1)S(1)}, u32[]{:S(2)}, u32[]{:S(2)}) collective-permute-start(bf16[16,1024]{1,0:T(8,128)(2,1)S(1)} %fusion.27), channel_id=1, source_target_pairs={{208,236},{209,237},{210,238},{211,239},{212,232},{213,233},{214,2... | collective-permute-start | bytes 98312 | tf_op jit(solution)/shard_map/ppermute | solution.py:29
  116.3 12.8 %collective-permute-start.38 = (bf16[16,1024]{1,0:T(8,128)(2,1)S(1)}, bf16[16,1024]{1,0:T(8,128)(2,1)S(1)}, u32[]{:S(2)}, u32[]{:S(2)}) collective-permute-start(bf16[16,1024]{1,0:T(8,128)(2,1)S(1)} %fusion.27), channel_id=1, source_target_pairs={{208,224},{209,225},{210,226},{211,227},{212,228},{213,229},{214,2... | collective-permute-start | bytes 98312 | tf_op jit(solution)/shard_map/ppermute | solution.py:29
  129.7 3.4 %collective-permute-start.39 = (bf16[16,1024]{1,0:T(8,128)(2,1)S(1)}, bf16[16,1024]{1,0:T(8,128)(2,1)S(1)}, u32[]{:S(2)}, u32[]{:S(2)}) collective-permute-start(bf16[16,1024]{1,0:T(8,128)(2,1)S(1)} %fusion.28), channel_id=1, source_target_pairs={{0,20},{1,21},{2,22},{3,23},{4,16},{5,17},{6,18},{7,19},{8,28},{9,... | collective-permute-start | bytes 98312 | tf_op jit(solution)/shard_map/ppermute | solution.py:29
  129.7 3.4 %collective-permute-start.40 = (bf16[16,1024]{1,0:T(8,128)(2,1)S(1)}, bf16[16,1024]{1,0:T(8,128)(2,1)S(1)}, u32[]{:S(2)}, u32[]{:S(2)}) collective-permute-start(bf16[16,1024]{1,0:T(8,128)(2,1)S(1)} %fusion.28), channel_id=1, source_target_pairs={{0,16},{1,17},{2,18},{3,19},{4,20},{5,21},{6,22},{7,23},{8,24},{9,... | collective-permute-start | bytes 98312 | tf_op jit(solution)/shard_map/ppermute | solution.py:29
  133.8 3.9 %collective-permute-start.41 = (bf16[16,1024]{1,0:T(8,128)(2,1)S(1)}, bf16[16,1024]{1,0:T(8,128)(2,1)S(1)}, u32[]{:S(2)}, u32[]{:S(2)}) collective-permute-start(bf16[16,1024]{1,0:T(8,128)(2,1)S(1)} %fusion.30), channel_id=1, source_target_pairs={{0,4},{1,5},{2,6},{3,7},{4,0},{5,1},{6,2},{7,3},{8,12},{9,13},{10,... | collective-permute-start | bytes 98312 | tf_op jit(solution)/shard_map/ppermute | solution.py:29
  137.7 7.6 %collective-permute-start.45 = (bf16[16,1024]{1,0:T(8,128)(2,1)S(1)}, bf16[16,1024]{1,0:T(8,128)(2,1)S(1)}, u32[]{:S(2)}, u32[]{:S(2)}) collective-permute-start(bf16[16,1024]{1,0:T(8,128)(2,1)S(1)} %get-tuple-element.58), channel_id=1, source_target_pairs={{0,12},{1,13},{2,14},{3,15},{4,8},{5,9},{6,10},{7,11},{8,4},{9,5},... | collective-permute-start | bytes 98312 | tf_op jit(solution)/shard_map/ppermute | solution.py:29
  140.1 5.1 %collective-permute-start.46 = (bf16[16,512]{1,0:T(8,128)(2,1)S(1)}, bf16[16,512]{1,0:T(8,128)(2,1)S(1)}, u32[]{:S(2)}, u32[]{:S(2)}) collective-permute-start(bf16[16,512]{1,0:T(8,128)(2,1)S(1)} %get-tuple-element.67), channel_id=1, source_target_pairs={{16,4},{17,5},{18,6},{19,7},{20,0},{21,1},{22,2},{23,3},{24,12},{2... | collective-permute-start | bytes 49160 | tf_op jit(solution)/shard_map/ppermute | solution.py:29
  142.0 3.4 %collective-permute-start.47 = (bf16[16,512]{1,0:T(8,128)(2,1)S(1)}, bf16[16,512]{1,0:T(8,128)(2,1)S(1)}, u32[]{:S(2)}, u32[]{:S(2)}) collective-permute-start(bf16[16,512]{1,0:T(8,128)(2,1)S(1)} %get-tuple-element.68), channel_id=1, source_target_pairs={{16,0},{17,1},{18,2},{19,3},{20,4},{21,5},{22,6},{23,7},{24,8},{25... | collective-permute-start | bytes 49160 | tf_op jit(solution)/shard_map/ppermute | solution.py:29
  155.1 13.3 %copy-start.2 = (f32[1,128,2048]{2,1,0:T(8,128)S(1)}, f32[1,128,2048]{2,1,0:T(8,128)}, u32[]{:S(2)}) copy-start(f32[1,128,2048]{2,1,0:T(8,128)} %param.8) | copy-start | bytes 3145732
  155.1 9.0 %collective-permute-start.42 = (bf16[128,512]{1,0:T(8,128)(2,1)S(1)}, bf16[128,512]{1,0:T(8,128)(2,1)S(1)}, u32[]{:S(2)}, u32[]{:S(2)}) collective-permute-start(bf16[128,512]{1,0:T(8,128)(2,1)S(1)} %get-tuple-element.49), channel_id=1, source_target_pairs={{0,1},{1,0},{2,3},{3,2},{4,5},{5,4},{6,7},{7,6},{8,9},{9,8},{10,11... | collective-permute-start | bytes 393224 | tf_op jit(solution)/shard_map/ppermute | solution.py:29
  156.9 8.5 %collective-permute-start.43 = (bf16[128,512]{1,0:T(8,128)(2,1)S(1)}, bf16[128,512]{1,0:T(8,128)(2,1)S(1)}, u32[]{:S(2)}, u32[]{:S(2)}) collective-permute-start(bf16[128,512]{1,0:T(8,128)(2,1)S(1)} %get-tuple-element.48), channel_id=1, source_target_pairs={{0,2},{1,3},{2,0},{3,1},{4,6},{5,7},{6,4},{7,5},{8,10},{9,11},{10,... | collective-permute-start | bytes 393224 | tf_op jit(solution)/shard_map/ppermute | solution.py:29
  159.3 9.1 %collective-permute-start.44 = (bf16[128,512]{1,0:T(8,128)(2,1)S(1)}, bf16[128,512]{1,0:T(8,128)(2,1)S(1)}, u32[]{:S(2)}, u32[]{:S(2)}) collective-permute-start(bf16[128,512]{1,0:T(8,128)(2,1)S(1)} %get-tuple-element.47), channel_id=1, source_target_pairs={{0,3},{1,2},{2,1},{3,0},{4,7},{5,6},{6,5},{7,4},{8,11},{9,10},{10,... | collective-permute-start | bytes 393224 | tf_op jit(solution)/shard_map/ppermute | solution.py:29
  160.0 10.2 %collective-permute-start.48 = (bf16[16,2432]{1,0:T(8,128)(2,1)S(1)}, bf16[16,2432]{1,0:T(8,128)(2,1)S(1)}, u32[]{:S(2)}, u32[]{:S(2)}) collective-permute-start(bf16[16,2432]{1,0:T(8,128)(2,1)S(1)} %get-tuple-element.54), channel_id=1, source_target_pairs={{0,1},{1,0},{2,3},{3,2},{4,5},{5,4},{6,7},{7,6},{8,9},{9,8},{10,11... | collective-permute-start | bytes 233480 | tf_op jit(solution)/shard_map/ppermute | solution.py:29
  160.5 9.6 %collective-permute-start.49 = (bf16[16,2432]{1,0:T(8,128)(2,1)S(1)}, bf16[16,2432]{1,0:T(8,128)(2,1)S(1)}, u32[]{:S(2)}, u32[]{:S(2)}) collective-permute-start(bf16[16,2432]{1,0:T(8,128)(2,1)S(1)} %get-tuple-element.55), channel_id=1, source_target_pairs={{0,2},{1,3},{2,0},{3,1},{4,6},{5,7},{6,4},{7,5},{8,10},{9,11},{10,... | collective-permute-start | bytes 233480 | tf_op jit(solution)/shard_map/ppermute | solution.py:29
  164.1 6.0 %collective-permute-start.50 = (bf16[16,2432]{1,0:T(8,128)(2,1)S(1)}, bf16[16,2432]{1,0:T(8,128)(2,1)S(1)}, u32[]{:S(2)}, u32[]{:S(2)}) collective-permute-start(bf16[16,2432]{1,0:T(8,128)(2,1)S(1)} %get-tuple-element.53), channel_id=1, source_target_pairs={{0,3},{1,2},{2,1},{3,0},{4,7},{5,6},{6,5},{7,4},{8,11},{9,10},{10,... | collective-permute-start | bytes 233480 | tf_op jit(solution)/shard_map/ppermute | solution.py:29
  (8 other events, 7.0 us)
Sparse Core Ops, SparseCore 0:
  10.3 36.4 all-gather.8
  48.6 32.6 all-gather.6
  83.6 27.5 all-gather.4
  112.8 38.7 all-gather.10

commit v7 on v4

--- a/solution.py
+++ b/solution.py
@@ -51,15 +51,16 @@
     return lax.optimization_barrier((values, others))[0]
 
 
-def kernel_call(body, place, operands, out_shapes, flops=0):
+def kernel_call(body, place, operands, out_shapes, flops=0, space=pltpu.VMEM, scratch=()):
     out_bytes = sum(s.size * s.dtype.itemsize for s in out_shapes)
     in_bytes = sum(o.size * o.dtype.itemsize for o in operands)
-    whole = pl.BlockSpec(memory_space=pltpu.VMEM)
+    whole = pl.BlockSpec(memory_space=space)
     return pl.pallas_call(
         body,
         out_shape=out_shapes,
         in_specs=[pl.BlockSpec(memory_space=pltpu.SMEM)] + [whole] * len(operands),
         out_specs=[whole] * len(out_shapes),
+        scratch_shapes=scratch,
         compiler_params=pltpu.CompilerParams(vmem_limit_bytes=24 * 1024 * 1024),
         cost_estimate=pl.CostEstimate(
             flops=flops, bytes_accessed=in_bytes + out_bytes, transcendentals=0
@@ -71,21 +72,43 @@
     return pl.ds(pl.multiple_of(index * size, size), size)
 
 
-def split_link(place, link, keep, give):
-    size = keep.shape[1] // 2
+def split_link(place, link, weight, keep, give):
+    rows, size = keep.shape[0], keep.shape[1] // 2
     for half in range(2):
         keep[:, half * size : (half + 1) * size] = link[:, block_of(place[half], size)]
-        give[:, half * size : (half + 1) * size] = link[:, block_of(place[2 + half], size)]
+        give[:rows, half * size : (half + 1) * size] = link[:, block_of(place[2 + half], size)]
+    high = weight[...].astype(bf16)
+    rest = weight[...] - high.astype(f32)
+    middle = rest.astype(bf16)
+    low = (rest - middle.astype(f32)).astype(bf16)
+    width = weight.shape[1]
+    row = lax.broadcasted_iota(jnp.int32, (16, width), 0)
+    parts = jnp.where(
+        row == 0,
+        high.astype(f32),
+        jnp.where(row == 1, middle.astype(f32), jnp.where(row == 2, low.astype(f32), 0.0)),
+    )
+    give[rows:, :] = jnp.zeros((16, 2 * size), bf16)
+    give[rows:, :width] = parts.astype(bf16)
 
 
 def assemble_link(place, *refs):
-    *pieces, out = refs
+    pieces, out, sems = refs[:SIDE], refs[SIDE], refs[SIDE + 1]
     size = pieces[0].shape[0] // 2
+    copies = []
     for step in range(SIDE):
         for half in range(2):
-            out[block_of(half * SIDE + (place[0] ^ step), size), :] = pieces[step][
-                half * size : (half + 1) * size, :
-            ]
+            copies.append(
+                pltpu.make_async_copy(
+                    pieces[step].at[half * size : (half + 1) * size, :],
+                    out.at[block_of(half * SIDE + (place[0] ^ step), size), :],
+                    sems.at[2 * step + half],
+                )
+            )
+    for copy in copies:
+        copy.start()
+    for copy in copies:
+        copy.wait()
 
 
 def schur_kernel(place, *refs):
@@ -167,13 +190,6 @@
     place = jnp.stack([x, y])
 
     coupling_in = gathered(coupling_rows, False)
-    inverse_out = gathered(inverse_rows, True)
-    turned = jnp.where(
-        even,
-        coupling_rows,
-        coupling_rows.reshape(rows, SIDE, SIDE, rows).transpose(0, 2, 1, 3).reshape(rows, nodes),
-    )
-    coupling_out = gathered(turned, True)
 
     def ordered(pieces):
         stacked = jnp.stack(pieces)
@@ -190,25 +206,45 @@
     keep, give = kernel_call(
         split_link,
         jnp.stack([in_low, in_high, away_low, away_high]),
-        [link_rows],
-        [shape((rows, half), bf16)] * 2,
+        [link_rows, weight_row[None, :]],
+        [shape((rows, half), bf16), shape((rows + 16, half), bf16)],
     )
     got = permuted(give, lambda p, y, x: (p, partner(p, y), x))
+    away_weight = got[rows : rows + 3, :rows].astype(f32).sum(axis=0, keepdims=True)
+    got = got[:rows]
     two = jnp.where(
         out_place == 0, jnp.concatenate([keep, got]), jnp.concatenate([got, keep])
     )
     pieces = spread_x(two)
-    source_rows, weight_row = tie((source_rows, weight_row), two)
+    source_rows, away_weight, coupling_late = tie(
+        (source_rows, away_weight, coupling_rows), pieces[1]
+    )
     started = weight_row[None, :] * source_rows
+    both_weights = jnp.concatenate(
+        [weight_row[None, :], away_weight, jnp.zeros((6, rows), f32)], axis=0
+    )
 
     def source_chunk(step):
         part = lax.dynamic_slice(started, ((x ^ step) * share, 0), (share, rows))
-        return jnp.concatenate([part, jnp.broadcast_to(weight_row[None, :], (8, rows))], axis=0)
+        return jnp.concatenate([part, both_weights], axis=0)
 
     line_values = jnp.concatenate(ordered(exchange_x(source_chunk)), axis=1)
-    line_weights = line_values[share : share + 1]
-    away_weights = permuted(line_weights, lambda p, y, x: (p, partner(p, y), x))
-    (block,) = kernel_call(assemble_link, place, pieces, [shape((half, half), bf16)])
+    line_weights, away_weights = line_values[share : share + 1], line_values[share + 1 : share + 2]
+    turned = jnp.where(
+        even,
+        coupling_late,
+        coupling_late.reshape(rows, SIDE, SIDE, rows).transpose(0, 2, 1, 3).reshape(rows, nodes),
+    )
+    outer = gathered(jnp.concatenate([inverse_rows, turned]), True).reshape(SIDE, 2, rows, nodes)
+    pieces = tie(pieces, line_values, turned)
+    (block,) = kernel_call(
+        assemble_link,
+        place,
+        pieces,
+        [shape((half, half), bf16)],
+        space=pl.ANY,
+        scratch=[pltpu.SemaphoreType.DMA((2 * SIDE,))],
+    )
     weight_half = jnp.where(
         out_place == 0,
         jnp.concatenate([line_weights, away_weights], axis=1),
@@ -226,10 +262,13 @@
     for turn in range(1, PARTITIONS):
         far, near = turn_messages(message, turn - 1)
         previous = (far.astype(f32) + near.astype(f32)).astype(bf16)
-        if turn == 8:
-            inverse_out, coupling_in = tie((inverse_out, coupling_in), message)
+        if turn == 10:
+            outer, coupling_in = tie((outer, coupling_in), message)
             inner = lax.dot_general(
-                inverse_out, coupling_in, (((1,), (1,)), ((), ())), preferred_element_type=f32
+                outer[:, 0].reshape(line, nodes),
+                coupling_in,
+                (((1,), (1,)), ((), ())),
+                preferred_element_type=f32,
             ).astype(bf16)
             inner_all = gathered(inner, False)
             previous = tie(previous, inner)
@@ -282,8 +321,10 @@
 
     last = exchange_x(last_chunk)
 
-    coupling_out, inner_all = tie((coupling_out, inner_all), lines)
-    folded = jnp.dot(coupling_out, inner_all, preferred_element_type=f32).astype(bf16)
+    inner_all = tie(inner_all, rounded)
+    folded = jnp.dot(
+        outer[:, 1].reshape(line, nodes), inner_all, preferred_element_type=f32
+    ).astype(bf16)
 
     def folded_chunk(step):
         return lax.dynamic_slice(folded, ((r ^ step) * rows, 0), (rows, line))

time: 175 us -> 193 us (1.10)
  waiting for transfers between devices: 81.4 us -> 105 us
  starting transfers between devices: 49.4 us -> 43.5 us
  local copies, waits for them, and re-layouts: 3.99 us -> 7.59 us
  matrix products: 17.9 us -> 15.7 us
    ppermute x48 -> x47, waiting for transfers between devices: 69.1 us -> 104 us  [permuted(): return lax.ppermute(value, AXES, pairs)]
    all_gather x4 -> x3, waiting for transfers between devices: 10.9 us -> 0.06 us  [gathered(): lax.all_gather(array, AXES, axis=0, tiled=True, axis_index_groups=gather_...]
    ppermute x48 -> x47, starting transfers between devices: 49.2 us -> 43.4 us  [permuted(): return lax.ppermute(value, AXES, pairs)]
    slice x0 -> x3, local copies, waits for them, and re-layouts: none -> 4.34 us  [the longest x1 4.32 us: shards(): outer[:, 0].reshape(line, nodes)]
    dot_general x2, matrix products: 7.76 us -> 5.54 us  [the longest x1 3.47 us: shards(): jnp.dot(outer[:, 1].reshape(line, nodes), inner_all, preferred_element_ty...]
  transfers between devices with their start and end apart: 52 -> 50, of which waited for: 20 -> 24; matrix products, arithmetic and copies ran while one was open for 11% -> 6% of each run, Pallas kernels for 2% -> 2%
where the time goes in v7:
time: 193 us
  waiting for transfers between devices  105 us (54%)
  starting transfers between devices  43.5 us (23%)
  matrix products  15.7 us (8%)
  between operations  14.4 us (7%)
  local copies, waits for them, and re-layouts  7.59 us (4%)
  Pallas kernels  4.6 us (2%)
    ppermute x47, waiting for transfers between devices, permuted(): return lax.ppermute(value, AXES, pairs)  104 us
    ppermute x47, starting transfers between devices, permuted(): return lax.ppermute(value, AXES, pairs)  43.4 us
    dot_general x15, matrix products, shards(): lax.dot_general(previous, block, (((1,), (1,)), ((), ())), preferred_elem...  9.73 us
    pallas_call x4, Pallas kernels, kernel_call(): pl.pallas_call(body, out_shape=out_shapes, in_specs=[pl.BlockSpec(memory_...  4.6 us
    slice x1, local copies, waits for them, and re-layouts, shards(): outer[:, 0].reshape(line, nodes)  4.32 us
  transfers between devices with their start and end apart: 50, of which 24 were waited for; matrix products, arithmetic and copies ran while one was open for 6% of the time, Pallas kernels for 2%

profile of v7, /device:TPU:224, one launch (start us, length us, event | category | flops | bytes accessed | tf_op | source)
XLA Modules:
  0.0 192.6 jit_solution(9945108408103125906)
XLA Ops:
  7.2 0.7 all-gather.9.cloned.1.call-update
  8.1 1.0 copy-done.1
  9.1 0.7 copy-done.2
  10.3 1.7 collective-permute-start
  12.0 5.1 %collective-permute-done = bf16[144,1024]{1,0:T(8,128)(2,1)S(1)} collective-permute-done((bf16[144,1024]{1,0:T(8,128)(2,1)S(1)}, bf16[144,1024]{1,0:T(8,128)(2,1)S(1)}, u32[]{:S(2)}, u32[]{:S(2)}) %collective-permute-start) | collective-permute-done | bytes 294944 | tf_op jit(solution)/shard_map/ppermute | solution.py:29
  17.3 1.6 collective-permute-start.1
  18.9 15.6 %collective-permute-done.1.refs_1_ = bf16[256,1024]{1,0:T(8,128)(2,1)S(1)} collective-permute-done((bf16[256,1024]{1,0:T(8,128)(2,1)S(1)}, bf16[256,1024]{1,0:T(8,128)(2,1)S(1)}, u32[]{:S(2)}, u32[]{:S(2)}) %collective-permute-start.1) | collective-permute-done | bytes 524320 | tf_op jit(solution)/shard_map/ppermute | solution.py:29
  35.9 1.0 pad_maximum_fusion
  37.2 3.3 %collective-permute-start.4 = (f32[24,128]{1,0:T(8,128)S(1)}, f32[24,128]{1,0:T(8,128)S(1)}, u32[]{:S(2)}, u32[]{:S(2)}) collective-permute-start(f32[24,128]{1,0:T(8,128)S(1)} %get-tuple-element.82), channel_id=1, source_target_pairs={{0,3},{1,2},{2,1},{3,0},{4,7},{5,6},{6,5},{7,4},{8,11},{9,10},{10,... | collective-permute-start | bytes 36872 | tf_op jit(solution)/shard_map/ppermute | solution.py:29
  40.5 0.9 collective-permute-start.3
  41.6 3.1 %collective-permute-start.7 = (bf16[256,1024]{1,0:T(8,128)(2,1)S(1)}, bf16[256,1024]{1,0:T(8,128)(2,1)S(1)}, u32[]{:S(2)}, u32[]{:S(2)}) collective-permute-start(bf16[256,1024]{1,0:T(8,128)(2,1)S(1)} %maximum_select_fusion.refs_0_), channel_id=1, source_target_pairs={{0,2},{1,3},{2,0},{3,1},{4,6},{5,7},{6,4},{7,5},{8,10},{9,11},{10,... | collective-permute-start | bytes 1572872 | tf_op jit(solution)/shard_map/ppermute | solution.py:29
  44.7 1.6 collective-permute-start.8
  46.4 0.8 collective-permute-start.5
  47.3 7.7 %collective-permute-done.7.refs_2_ = bf16[256,1024]{1,0:T(8,128)(2,1)S(1)} collective-permute-done((bf16[256,1024]{1,0:T(8,128)(2,1)S(1)}, bf16[256,1024]{1,0:T(8,128)(2,1)S(1)}, u32[]{:S(2)}, u32[]{:S(2)}) %collective-permute-start.7) | collective-permute-done | bytes 524320 | tf_op jit(solution)/shard_map/ppermute | solution.py:29
  54.9 11.0 %collective-permute-done.8.refs_3_ = bf16[256,1024]{1,0:T(8,128)(2,1)S(1)} collective-permute-done((bf16[256,1024]{1,0:T(8,128)(2,1)S(1)}, bf16[256,1024]{1,0:T(8,128)(2,1)S(1)}, u32[]{:S(2)}, u32[]{:S(2)}) %collective-permute-start.8) | collective-permute-done | bytes 524320 | tf_op jit(solution)/shard_map/ppermute | solution.py:29
  66.0 0.8 shard_map.86
  66.8 0.7 fusion.15
  67.4 0.7 collective-permute-start.10
  68.1 0.7 collective-permute-start.9
  68.8 0.7 fusion.16
  69.5 1.1 collective-permute-done.12
  70.6 2.6 %collective-permute-done.11 = bf16[16,1024]{1,0:T(8,128)(2,1)S(1)} collective-permute-done((bf16[16,1024]{1,0:T(8,128)(2,1)S(1)}, bf16[16,1024]{1,0:T(8,128)(2,1)S(1)}, u32[]{:S(2)}, u32[]{:S(2)}) %collective-permute-start.11) | collective-permute-done | bytes 32800 | tf_op jit(solution)/shard_map/ppermute | solution.py:29
  73.9 0.7 collective-permute-start.14
  74.6 0.7 collective-permute-start.13
  75.9 0.8 collective-permute-start.16
  76.7 0.9 collective-permute-done.16
  77.6 3.0 %collective-permute-done.15 = bf16[16,1024]{1,0:T(8,128)(2,1)S(1)} collective-permute-done((bf16[16,1024]{1,0:T(8,128)(2,1)S(1)}, bf16[16,1024]{1,0:T(8,128)(2,1)S(1)}, u32[]{:S(2)}, u32[]{:S(2)}) %collective-permute-start.15) | collective-permute-done | bytes 32800 | tf_op jit(solution)/shard_map/ppermute | solution.py:29
  81.3 0.7 collective-permute-start.18
  82.0 0.8 collective-permute-start.17
  84.0 0.9 collective-permute-done.20
  84.8 2.6 %collective-permute-done.19 = bf16[16,1024]{1,0:T(8,128)(2,1)S(1)} collective-permute-done((bf16[16,1024]{1,0:T(8,128)(2,1)S(1)}, bf16[16,1024]{1,0:T(8,128)(2,1)S(1)}, u32[]{:S(2)}, u32[]{:S(2)}) %collective-permute-start.19) | collective-permute-done | bytes 32800 | tf_op jit(solution)/shard_map/ppermute | solution.py:29
  88.0 0.7 collective-permute-start.22
  88.7 0.7 collective-permute-start.21
  90.3 0.9 collective-permute-done.24
  91.3 2.3 %collective-permute-done.23 = bf16[16,1024]{1,0:T(8,128)(2,1)S(1)} collective-permute-done((bf16[16,1024]{1,0:T(8,128)(2,1)S(1)}, bf16[16,1024]{1,0:T(8,128)(2,1)S(1)}, u32[]{:S(2)}, u32[]{:S(2)}) %collective-permute-start.23) | collective-permute-done | bytes 32800 | tf_op jit(solution)/shard_map/ppermute | solution.py:29
  94.2 0.7 collective-permute-start.26
  94.9 0.7 collective-permute-start.25
  95.7 4.3 %fusion.39 = (bf16[4,1,128,2048]{3,2,1,0:T(8,128)(2,1)S(1)}, bf16[4,1,128,2048]{3,2,1,0:T(8,128)(2,1)}) fusion(bf16[4,2,128,2048]{3,2,1,0:T(8,128)(2,1)} %bitcast.68), kind=kLoop, calls=%fused_computation.129 | loop fusion | bytes 8388608 | tf_op jit(solution)/shard_map/slice | solution.py:268
  100.0 2.1 %convolution_convert_fusion.1 = bf16[512,512]{1,0:T(8,128)(2,1)} fusion(bf16[512,2048]{1,0:T(8,128)(2,1)S(1)} %bitcast.71, bf16[512,2048]{1,0:T(8,128)(2,1)S(1)} %bitcast.80), kind=kOutput, calls=%fused_computation.1 | convolution fusion | flops 1074003968 | bytes 4718592 | tf_op jit(solution)/shard_map/dot_general | solution.py:267
  103.1 0.9 collective-permute-done.28
  103.9 2.5 %collective-permute-done.27 = bf16[16,1024]{1,0:T(8,128)(2,1)S(1)} collective-permute-done((bf16[16,1024]{1,0:T(8,128)(2,1)S(1)}, bf16[16,1024]{1,0:T(8,128)(2,1)S(1)}, u32[]{:S(2)}, u32[]{:S(2)}) %collective-permute-start.27) | collective-permute-done | bytes 32800 | tf_op jit(solution)/shard_map/ppermute | solution.py:29
  107.1 0.7 collective-permute-start.30
  107.8 0.7 collective-permute-start.29
  109.4 1.0 collective-permute-done.32
  110.3 2.3 %collective-permute-done.31 = bf16[16,1024]{1,0:T(8,128)(2,1)S(1)} collective-permute-done((bf16[16,1024]{1,0:T(8,128)(2,1)S(1)}, bf16[16,1024]{1,0:T(8,128)(2,1)S(1)}, u32[]{:S(2)}, u32[]{:S(2)}) %collective-permute-start.31) | collective-permute-done | bytes 32800 | tf_op jit(solution)/shard_map/ppermute | solution.py:29
  113.3 1.3 collective-permute-start.34
  114.6 1.3 collective-permute-start.33
  115.9 28.8 %collective-permute-done.34 = bf16[16,1024]{1,0:T(8,128)(2,1)S(1)} collective-permute-done((bf16[16,1024]{1,0:T(8,128)(2,1)S(1)}, bf16[16,1024]{1,0:T(8,128)(2,1)S(1)}, u32[]{:S(2)}, u32[]{:S(2)}) %collective-permute-start.34) | collective-permute-done | bytes 32800 | tf_op jit(solution)/shard_map/ppermute | solution.py:29
  144.7 1.3 collective-permute-done.33
  147.0 0.9 collective-permute-done.36
  147.8 2.4 %collective-permute-done.35 = bf16[16,1024]{1,0:T(8,128)(2,1)S(1)} collective-permute-done((bf16[16,1024]{1,0:T(8,128)(2,1)S(1)}, bf16[16,1024]{1,0:T(8,128)(2,1)S(1)}, u32[]{:S(2)}, u32[]{:S(2)}) %collective-permute-start.35) | collective-permute-done | bytes 32800 | tf_op jit(solution)/shard_map/ppermute | solution.py:29
  150.3 0.7 fusion.30
  151.1 4.0 %collective-permute-done.37 = bf16[16,1024]{1,0:T(8,128)(2,1)S(1)} collective-permute-done((bf16[16,1024]{1,0:T(8,128)(2,1)S(1)}, bf16[16,1024]{1,0:T(8,128)(2,1)S(1)}, u32[]{:S(2)}, u32[]{:S(2)}) %collective-permute-start.37) | collective-permute-done | bytes 32800 | tf_op jit(solution)/shard_map/ppermute | solution.py:29
  155.1 3.4 %collective-permute-start.41 = (bf16[16,1024]{1,0:T(8,128)(2,1)S(1)}, bf16[16,1024]{1,0:T(8,128)(2,1)S(1)}, u32[]{:S(2)}, u32[]{:S(2)}) collective-permute-start(bf16[16,1024]{1,0:T(8,128)(2,1)S(1)} %get-tuple-element.50), channel_id=1, source_target_pairs={{0,12},{1,13},{2,14},{3,15},{4,8},{5,9},{6,10},{7,11},{8,4},{9,5},... | collective-permute-start | bytes 98312 | tf_op jit(solution)/shard_map/ppermute | solution.py:29
  158.9 1.9 collective-permute-start.43
  160.8 1.9 collective-permute-start.42
  162.8 3.1 %collective-permute-done.42 = bf16[16,512]{1,0:T(8,128)(2,1)S(1)} collective-permute-done((bf16[16,512]{1,0:T(8,128)(2,1)S(1)}, bf16[16,512]{1,0:T(8,128)(2,1)S(1)}, u32[]{:S(2)}, u32[]{:S(2)}) %collective-permute-start.42) | collective-permute-done | bytes 16416 | tf_op jit(solution)/shard_map/ppermute | solution.py:29
  166.0 3.5 %convolution_convert_fusion = bf16[512,512]{1,0:T(8,128)(2,1)S(1)} fusion(bf16[512,2048]{1,0:T(8,128)(2,1)} %bitcast.70, bf16[2048,512]{1,0:T(8,128)(2,1)} %all-gather.7.cloned.1.call-done), kind=kOutput, calls=%fused_computation | convolution fusion | flops 1074003968 | bytes 4718592 | tf_op jit(solution)/shard_map/dot_general | solution.py:325
  169.5 1.8 collective-permute-start.38
  171.3 2.4 %collective-permute-start.39 = (bf16[128,512]{1,0:T(8,128)(2,1)S(1)}, bf16[128,512]{1,0:T(8,128)(2,1)S(1)}, u32[]{:S(2)}, u32[]{:S(2)}) collective-permute-start(bf16[128,512]{1,0:T(8,128)(2,1)S(1)} %get-tuple-element.42), channel_id=1, source_target_pairs={{0,2},{1,3},{2,0},{3,1},{4,6},{5,7},{6,4},{7,5},{8,10},{9,11},{10,... | collective-permute-start | bytes 393224 | tf_op jit(solution)/shard_map/ppermute | solution.py:29
  175.0 3.6 %collective-permute-start.45 = (bf16[16,2432]{1,0:T(8,128)(2,1)S(1)}, bf16[16,2432]{1,0:T(8,128)(2,1)S(1)}, u32[]{:S(2)}, u32[]{:S(2)}) collective-permute-start(bf16[16,2432]{1,0:T(8,128)(2,1)S(1)} %get-tuple-element.47), channel_id=1, source_target_pairs={{0,2},{1,3},{2,0},{3,1},{4,6},{5,7},{6,4},{7,5},{8,10},{9,11},{10,... | collective-permute-start | bytes 233480 | tf_op jit(solution)/shard_map/ppermute | solution.py:29
  179.8 3.0 %collective-permute-done.40.refs_4_ = bf16[128,512]{1,0:T(8,128)(2,1)S(1)} collective-permute-done((bf16[128,512]{1,0:T(8,128)(2,1)S(1)}, bf16[128,512]{1,0:T(8,128)(2,1)S(1)}, u32[]{:S(2)}, u32[]{:S(2)}) %collective-permute-start.40) | collective-permute-done | bytes 131104 | tf_op jit(solution)/shard_map/ppermute | solution.py:29
  182.9 1.8 shard_map.87
  184.6 1.5 shard_map.88
  (113 shorter events, 15.7 us)
Async XLA Ops:
  7.2 27.3 %copy-start.4 = (bf16[1,128,2048]{2,1,0:T(8,128)(2,1)S(1)}, bf16[1,128,2048]{2,1,0:T(8,128)(2,1)}, u32[]{:S(2)}) copy-start(bf16[1,128,2048]{2,1,0:T(8,128)(2,1)} %param.7) | copy-start | bytes 1572868
  7.2 88.4 %all-gather.9.cloned.1.call-start = ((), (), s32[]{:S(2)}) async-start(), calls=%async_computation.2 | async-start | bytes 2621440 | tf_op jit(solution)/shard_map/all_gather | solution.py:157
  7.9 87.7 %all-gather.5.cloned.1.call-start = ((), (), s32[]{:S(2)}) async-start(), calls=%async_computation | async-start | bytes 5242880 | tf_op jit(solution)/shard_map/all_gather | solution.py:157
  8.1 1.0 copy-start.1
  9.1 0.7 copy-start.2
  10.3 6.8 %collective-permute-start = (bf16[144,1024]{1,0:T(8,128)(2,1)S(1)}, bf16[144,1024]{1,0:T(8,128)(2,1)S(1)}, u32[]{:S(2)}, u32[]{:S(2)}) collective-permute-start(bf16[144,1024]{1,0:T(8,128)(2,1)S(1)} %get-tuple-element.20), channel_id=1, source_target_pairs={{0,4},{1,5},{2,6},{3,7},{4,0},{5,1},{6,2},{7,3},{8,12},{9,13},{10,... | collective-permute-start | bytes 884744 | tf_op jit(solution)/shard_map/ppermute | solution.py:29
  17.3 17.2 %collective-permute-start.1 = (bf16[256,1024]{1,0:T(8,128)(2,1)S(1)}, bf16[256,1024]{1,0:T(8,128)(2,1)S(1)}, u32[]{:S(2)}, u32[]{:S(2)}) collective-permute-start(bf16[256,1024]{1,0:T(8,128)(2,1)S(1)} %maximum_select_fusion.refs_0_), channel_id=1, source_target_pairs={{0,1},{1,0},{2,3},{3,2},{4,5},{5,4},{6,7},{7,6},{8,9},{9,8},{10,11... | collective-permute-start | bytes 1572872 | tf_op jit(solution)/shard_map/ppermute | solution.py:29
  34.9 1.0 copy-start.5
  35.5 1.6 copy-start.3
  35.5 1.6 copy-start.6
  37.0 129.0 %all-gather.7.cloned.1.call-start = ((), (), s32[]{:S(2)}) async-start(), calls=%async_computation.1 | async-start | bytes 2621440 | tf_op jit(solution)/shard_map/all_gather | solution.py:157
  37.2 9.0 %collective-permute-start.4 = (f32[24,128]{1,0:T(8,128)S(1)}, f32[24,128]{1,0:T(8,128)S(1)}, u32[]{:S(2)}, u32[]{:S(2)}) collective-permute-start(f32[24,128]{1,0:T(8,128)S(1)} %get-tuple-element.82), channel_id=1, source_target_pairs={{0,3},{1,2},{2,1},{3,0},{4,7},{5,6},{6,5},{7,4},{8,11},{9,10},{10,... | collective-permute-start | bytes 36872 | tf_op jit(solution)/shard_map/ppermute | solution.py:29
  40.5 5.7 %collective-permute-start.3 = (f32[24,128]{1,0:T(8,128)S(1)}, f32[24,128]{1,0:T(8,128)S(1)}, u32[]{:S(2)}, u32[]{:S(2)}) collective-permute-start(f32[24,128]{1,0:T(8,128)S(1)} %get-tuple-element.81), channel_id=1, source_target_pairs={{0,2},{1,3},{2,0},{3,1},{4,6},{5,7},{6,4},{7,5},{8,10},{9,11},{10,... | collective-permute-start | bytes 36872 | tf_op jit(solution)/shard_map/ppermute | solution.py:29
  41.5 4.8 %collective-permute-start.2 = (f32[24,128]{1,0:T(8,128)S(1)}, f32[24,128]{1,0:T(8,128)S(1)}, u32[]{:S(2)}, u32[]{:S(2)}) collective-permute-start(f32[24,128]{1,0:T(8,128)S(1)} %get-tuple-element.80), channel_id=1, source_target_pairs={{0,1},{1,0},{2,3},{3,2},{4,5},{5,4},{6,7},{7,6},{8,9},{9,8},{10,11... | collective-permute-start | bytes 36872 | tf_op jit(solution)/shard_map/ppermute | solution.py:29
  41.6 13.3 %collective-permute-start.7 = (bf16[256,1024]{1,0:T(8,128)(2,1)S(1)}, bf16[256,1024]{1,0:T(8,128)(2,1)S(1)}, u32[]{:S(2)}, u32[]{:S(2)}) collective-permute-start(bf16[256,1024]{1,0:T(8,128)(2,1)S(1)} %maximum_select_fusion.refs_0_), channel_id=1, source_target_pairs={{0,2},{1,3},{2,0},{3,1},{4,6},{5,7},{6,4},{7,5},{8,10},{9,11},{10,... | collective-permute-start | bytes 1572872 | tf_op jit(solution)/shard_map/ppermute | solution.py:29
  44.7 21.3 %collective-permute-start.8 = (bf16[256,1024]{1,0:T(8,128)(2,1)S(1)}, bf16[256,1024]{1,0:T(8,128)(2,1)S(1)}, u32[]{:S(2)}, u32[]{:S(2)}) collective-permute-start(bf16[256,1024]{1,0:T(8,128)(2,1)S(1)} %maximum_select_fusion.refs_0_), channel_id=1, source_target_pairs={{0,3},{1,2},{2,1},{3,0},{4,7},{5,6},{6,5},{7,4},{8,11},{9,10},{10,... | collective-permute-start | bytes 1572872 | tf_op jit(solution)/shard_map/ppermute | solution.py:29
  46.3 20.4 %collective-permute-start.6 = (bf16[16,1024]{1,0:T(8,128)(2,1)S(1)}, bf16[16,1024]{1,0:T(8,128)(2,1)S(1)}, u32[]{:S(2)}, u32[]{:S(2)}) collective-permute-start(bf16[16,1024]{1,0:T(8,128)(2,1)S(1)} %fusion.32), channel_id=1, source_target_pairs={{0,16},{1,17},{2,18},{3,19},{4,20},{5,21},{6,22},{7,23},{8,24},{9,... | collective-permute-start | bytes 98312 | tf_op jit(solution)/shard_map/ppermute | solution.py:29
  46.4 20.3 %collective-permute-start.5 = (bf16[16,1024]{1,0:T(8,128)(2,1)S(1)}, bf16[16,1024]{1,0:T(8,128)(2,1)S(1)}, u32[]{:S(2)}, u32[]{:S(2)}) collective-permute-start(bf16[16,1024]{1,0:T(8,128)(2,1)S(1)} %fusion.32), channel_id=1, source_target_pairs={{0,20},{1,21},{2,22},{3,23},{4,16},{5,17},{6,18},{7,19},{8,28},{9,... | collective-permute-start | bytes 98312 | tf_op jit(solution)/shard_map/ppermute | solution.py:29
  67.4 1.3 collective-permute-start.10
  68.1 0.7 collective-permute-start.9
  69.4 1.2 collective-permute-start.12
  69.4 3.8 %collective-permute-start.11 = (bf16[16,1024]{1,0:T(8,128)(2,1)S(1)}, bf16[16,1024]{1,0:T(8,128)(2,1)S(1)}, u32[]{:S(2)}, u32[]{:S(2)}) collective-permute-start(bf16[16,1024]{1,0:T(8,128)(2,1)S(1)} %fusion.16), channel_id=1, source_target_pairs={{0,20},{1,21},{2,22},{3,23},{4,16},{5,17},{6,18},{7,19},{8,28},{9,... | collective-permute-start | bytes 98312 | tf_op jit(solution)/shard_map/ppermute | solution.py:29
  73.9 1.3 collective-permute-start.14
  74.6 0.7 collective-permute-start.13
  75.9 1.7 collective-permute-start.16
  76.7 3.9 %collective-permute-start.15 = (bf16[16,1024]{1,0:T(8,128)(2,1)S(1)}, bf16[16,1024]{1,0:T(8,128)(2,1)S(1)}, u32[]{:S(2)}, u32[]{:S(2)}) collective-permute-start(bf16[16,1024]{1,0:T(8,128)(2,1)S(1)} %fusion.18), channel_id=1, source_target_pairs={{0,20},{1,21},{2,22},{3,23},{4,16},{5,17},{6,18},{7,19},{8,28},{9,... | collective-permute-start | bytes 98312 | tf_op jit(solution)/shard_map/ppermute | solution.py:29
  81.3 1.5 collective-permute-start.18
  82.0 0.9 collective-permute-start.17
  83.5 1.3 collective-permute-start.20
  84.0 3.4 %collective-permute-start.19 = (bf16[16,1024]{1,0:T(8,128)(2,1)S(1)}, bf16[16,1024]{1,0:T(8,128)(2,1)S(1)}, u32[]{:S(2)}, u32[]{:S(2)}) collective-permute-start(bf16[16,1024]{1,0:T(8,128)(2,1)S(1)} %fusion.20), channel_id=1, source_target_pairs={{0,20},{1,21},{2,22},{3,23},{4,16},{5,17},{6,18},{7,19},{8,28},{9,... | collective-permute-start | bytes 98312 | tf_op jit(solution)/shard_map/ppermute | solution.py:29
  88.0 1.3 collective-permute-start.22
  88.7 0.7 collective-permute-start.21
  90.1 1.2 collective-permute-start.24
  90.2 3.4 %collective-permute-start.23 = (bf16[16,1024]{1,0:T(8,128)(2,1)S(1)}, bf16[16,1024]{1,0:T(8,128)(2,1)S(1)}, u32[]{:S(2)}, u32[]{:S(2)}) collective-permute-start(bf16[16,1024]{1,0:T(8,128)(2,1)S(1)} %fusion.22), channel_id=1, source_target_pairs={{0,20},{1,21},{2,22},{3,23},{4,16},{5,17},{6,18},{7,19},{8,28},{9,... | collective-permute-start | bytes 98312 | tf_op jit(solution)/shard_map/ppermute | solution.py:29
  94.2 1.3 collective-permute-start.26
  94.9 0.7 collective-permute-start.25
  95.6 4.3 %copy-start.7 = (bf16[1,512,2048]{2,1,0:T(8,128)(2,1)S(1)}, bf16[1,512,2048]{2,1,0:T(8,128)(2,1)}, u32[]{:S(2)}) copy-start(bf16[1,512,2048]{2,1,0:T(8,128)(2,1)} %all-gather.9.cloned.1.call-done) | copy-start | bytes 6291460
  102.7 1.2 collective-permute-start.28
  103.1 3.4 %collective-permute-start.27 = (bf16[16,1024]{1,0:T(8,128)(2,1)S(1)}, bf16[16,1024]{1,0:T(8,128)(2,1)S(1)}, u32[]{:S(2)}, u32[]{:S(2)}) collective-permute-start(bf16[16,1024]{1,0:T(8,128)(2,1)S(1)} %fusion.24), channel_id=1, source_target_pairs={{0,20},{1,21},{2,22},{3,23},{4,16},{5,17},{6,18},{7,19},{8,28},{9,... | collective-permute-start | bytes 98312 | tf_op jit(solution)/shard_map/ppermute | solution.py:29
  107.1 1.4 collective-permute-start.30
  107.8 0.7 collective-permute-start.29
  109.1 1.2 collective-permute-start.32
  109.3 3.4 %collective-permute-start.31 = (bf16[16,1024]{1,0:T(8,128)(2,1)S(1)}, bf16[16,1024]{1,0:T(8,128)(2,1)S(1)}, u32[]{:S(2)}, u32[]{:S(2)}) collective-permute-start(bf16[16,1024]{1,0:T(8,128)(2,1)S(1)} %fusion.26), channel_id=1, source_target_pairs={{0,20},{1,21},{2,22},{3,23},{4,16},{5,17},{6,18},{7,19},{8,28},{9,... | collective-permute-start | bytes 98312 | tf_op jit(solution)/shard_map/ppermute | solution.py:29
  113.3 31.4 %collective-permute-start.34 = (bf16[16,1024]{1,0:T(8,128)(2,1)S(1)}, bf16[16,1024]{1,0:T(8,128)(2,1)S(1)}, u32[]{:S(2)}, u32[]{:S(2)}) collective-permute-start(bf16[16,1024]{1,0:T(8,128)(2,1)S(1)} %fusion.27), channel_id=1, source_target_pairs={{208,224},{209,225},{210,226},{211,227},{212,228},{213,229},{214,2... | collective-permute-start | bytes 98312 | tf_op jit(solution)/shard_map/ppermute | solution.py:29
  114.6 31.4 %collective-permute-start.33 = (bf16[16,1024]{1,0:T(8,128)(2,1)S(1)}, bf16[16,1024]{1,0:T(8,128)(2,1)S(1)}, u32[]{:S(2)}, u32[]{:S(2)}) collective-permute-start(bf16[16,1024]{1,0:T(8,128)(2,1)S(1)} %fusion.27), channel_id=1, source_target_pairs={{208,236},{209,237},{210,238},{211,239},{212,232},{213,233},{214,2... | collective-permute-start | bytes 98312 | tf_op jit(solution)/shard_map/ppermute | solution.py:29
  146.6 1.2 collective-permute-start.36
  146.6 3.7 %collective-permute-start.35 = (bf16[16,1024]{1,0:T(8,128)(2,1)S(1)}, bf16[16,1024]{1,0:T(8,128)(2,1)S(1)}, u32[]{:S(2)}, u32[]{:S(2)}) collective-permute-start(bf16[16,1024]{1,0:T(8,128)(2,1)S(1)} %fusion.28), channel_id=1, source_target_pairs={{0,20},{1,21},{2,22},{3,23},{4,16},{5,17},{6,18},{7,19},{8,28},{9,... | collective-permute-start | bytes 98312 | tf_op jit(solution)/shard_map/ppermute | solution.py:29
  150.9 4.1 %collective-permute-start.37 = (bf16[16,1024]{1,0:T(8,128)(2,1)S(1)}, bf16[16,1024]{1,0:T(8,128)(2,1)S(1)}, u32[]{:S(2)}, u32[]{:S(2)}) collective-permute-start(bf16[16,1024]{1,0:T(8,128)(2,1)S(1)} %fusion.30), channel_id=1, source_target_pairs={{0,4},{1,5},{2,6},{3,7},{4,0},{5,1},{6,2},{7,3},{8,12},{9,13},{10,... | collective-permute-start | bytes 98312 | tf_op jit(solution)/shard_map/ppermute | solution.py:29
  155.1 10.8 %collective-permute-start.41 = (bf16[16,1024]{1,0:T(8,128)(2,1)S(1)}, bf16[16,1024]{1,0:T(8,128)(2,1)S(1)}, u32[]{:S(2)}, u32[]{:S(2)}) collective-permute-start(bf16[16,1024]{1,0:T(8,128)(2,1)S(1)} %get-tuple-element.50), channel_id=1, source_target_pairs={{0,12},{1,13},{2,14},{3,15},{4,8},{5,9},{6,10},{7,11},{8,4},{9,5},... | collective-permute-start | bytes 98312 | tf_op jit(solution)/shard_map/ppermute | solution.py:29
  158.9 3.9 %collective-permute-start.43 = (bf16[16,512]{1,0:T(8,128)(2,1)S(1)}, bf16[16,512]{1,0:T(8,128)(2,1)S(1)}, u32[]{:S(2)}, u32[]{:S(2)}) collective-permute-start(bf16[16,512]{1,0:T(8,128)(2,1)S(1)} %get-tuple-element.62), channel_id=1, source_target_pairs={{16,0},{17,1},{18,2},{19,3},{20,4},{21,5},{22,6},{23,7},{24,8},{25... | collective-permute-start | bytes 49160 | tf_op jit(solution)/shard_map/ppermute | solution.py:29
  160.8 5.1 %collective-permute-start.42 = (bf16[16,512]{1,0:T(8,128)(2,1)S(1)}, bf16[16,512]{1,0:T(8,128)(2,1)S(1)}, u32[]{:S(2)}, u32[]{:S(2)}) collective-permute-start(bf16[16,512]{1,0:T(8,128)(2,1)S(1)} %get-tuple-element.61), channel_id=1, source_target_pairs={{16,4},{17,5},{18,6},{19,7},{20,0},{21,1},{22,2},{23,3},{24,12},{2... | collective-permute-start | bytes 49160 | tf_op jit(solution)/shard_map/ppermute | solution.py:29
  169.4 13.4 %copy-start = (f32[1,128,2048]{2,1,0:T(8,128)S(1)}, f32[1,128,2048]{2,1,0:T(8,128)}, u32[]{:S(2)}) copy-start(f32[1,128,2048]{2,1,0:T(8,128)} %param.8) | copy-start | bytes 3145732
  169.5 9.1 %collective-permute-start.38 = (bf16[128,512]{1,0:T(8,128)(2,1)S(1)}, bf16[128,512]{1,0:T(8,128)(2,1)S(1)}, u32[]{:S(2)}, u32[]{:S(2)}) collective-permute-start(bf16[128,512]{1,0:T(8,128)(2,1)S(1)} %get-tuple-element.43), channel_id=1, source_target_pairs={{0,1},{1,0},{2,3},{3,2},{4,5},{5,4},{6,7},{7,6},{8,9},{9,8},{10,11... | collective-permute-start | bytes 393224 | tf_op jit(solution)/shard_map/ppermute | solution.py:29
  171.3 8.5 %collective-permute-start.39 = (bf16[128,512]{1,0:T(8,128)(2,1)S(1)}, bf16[128,512]{1,0:T(8,128)(2,1)S(1)}, u32[]{:S(2)}, u32[]{:S(2)}) collective-permute-start(bf16[128,512]{1,0:T(8,128)(2,1)S(1)} %get-tuple-element.42), channel_id=1, source_target_pairs={{0,2},{1,3},{2,0},{3,1},{4,6},{5,7},{6,4},{7,5},{8,10},{9,11},{10,... | collective-permute-start | bytes 393224 | tf_op jit(solution)/shard_map/ppermute | solution.py:29
  173.8 9.1 %collective-permute-start.40 = (bf16[128,512]{1,0:T(8,128)(2,1)S(1)}, bf16[128,512]{1,0:T(8,128)(2,1)S(1)}, u32[]{:S(2)}, u32[]{:S(2)}) collective-permute-start(bf16[128,512]{1,0:T(8,128)(2,1)S(1)} %get-tuple-element.41), channel_id=1, source_target_pairs={{0,3},{1,2},{2,1},{3,0},{4,7},{5,6},{6,5},{7,4},{8,11},{9,10},{10,... | collective-permute-start | bytes 393224 | tf_op jit(solution)/shard_map/ppermute | solution.py:29
  174.3 10.3 %collective-permute-start.44 = (bf16[16,2432]{1,0:T(8,128)(2,1)S(1)}, bf16[16,2432]{1,0:T(8,128)(2,1)S(1)}, u32[]{:S(2)}, u32[]{:S(2)}) collective-permute-start(bf16[16,2432]{1,0:T(8,128)(2,1)S(1)} %get-tuple-element.46), channel_id=1, source_target_pairs={{0,1},{1,0},{2,3},{3,2},{4,5},{5,4},{6,7},{7,6},{8,9},{9,8},{10,11... | collective-permute-start | bytes 233480 | tf_op jit(solution)/shard_map/ppermute | solution.py:29
  175.0 9.7 %collective-permute-start.45 = (bf16[16,2432]{1,0:T(8,128)(2,1)S(1)}, bf16[16,2432]{1,0:T(8,128)(2,1)S(1)}, u32[]{:S(2)}, u32[]{:S(2)}) collective-permute-start(bf16[16,2432]{1,0:T(8,128)(2,1)S(1)} %get-tuple-element.47), channel_id=1, source_target_pairs={{0,2},{1,3},{2,0},{3,1},{4,6},{5,7},{6,4},{7,5},{8,10},{9,11},{10,... | collective-permute-start | bytes 233480 | tf_op jit(solution)/shard_map/ppermute | solution.py:29
  178.6 6.0 %collective-permute-start.46 = (bf16[16,2432]{1,0:T(8,128)(2,1)S(1)}, bf16[16,2432]{1,0:T(8,128)(2,1)S(1)}, u32[]{:S(2)}, u32[]{:S(2)}) collective-permute-start(bf16[16,2432]{1,0:T(8,128)(2,1)S(1)} %get-tuple-element.45), channel_id=1, source_target_pairs={{0,3},{1,2},{2,1},{3,0},{4,7},{5,6},{6,5},{7,4},{8,11},{9,10},{10,... | collective-permute-start | bytes 233480 | tf_op jit(solution)/shard_map/ppermute | solution.py:29
Sparse Core Ops, SparseCore 0:
  9.8 27.9 all-gather.8
  40.1 43.3 all-gather.4
  108.6 49.8 all-gather.6

commit v8 on v4

--- a/solution.py
+++ b/solution.py
@@ -167,13 +167,12 @@
     place = jnp.stack([x, y])
 
     coupling_in = gathered(coupling_rows, False)
-    inverse_out = gathered(inverse_rows, True)
     turned = jnp.where(
         even,
         coupling_rows,
         coupling_rows.reshape(rows, SIDE, SIDE, rows).transpose(0, 2, 1, 3).reshape(rows, nodes),
     )
-    coupling_out = gathered(turned, True)
+    outer = gathered(jnp.concatenate([inverse_rows, turned], axis=1), True)
 
     def ordered(pieces):
         stacked = jnp.stack(pieces)
@@ -194,11 +193,6 @@
         [shape((rows, half), bf16)] * 2,
     )
     got = permuted(give, lambda p, y, x: (p, partner(p, y), x))
-    two = jnp.where(
-        out_place == 0, jnp.concatenate([keep, got]), jnp.concatenate([got, keep])
-    )
-    pieces = spread_x(two)
-    source_rows, weight_row = tie((source_rows, weight_row), two)
     started = weight_row[None, :] * source_rows
 
     def source_chunk(step):
@@ -206,7 +200,12 @@
         return jnp.concatenate([part, jnp.broadcast_to(weight_row[None, :], (8, rows))], axis=0)
 
     line_values = jnp.concatenate(ordered(exchange_x(source_chunk)), axis=1)
+    keep, got, line_values = tie((keep, got, line_values), turned)
     line_weights = line_values[share : share + 1]
+    two = jnp.where(
+        out_place == 0, jnp.concatenate([keep, got]), jnp.concatenate([got, keep])
+    )
+    pieces = spread_x(two)
     away_weights = permuted(line_weights, lambda p, y, x: (p, partner(p, y), x))
     (block,) = kernel_call(assemble_link, place, pieces, [shape((half, half), bf16)])
     weight_half = jnp.where(
@@ -226,10 +225,10 @@
     for turn in range(1, PARTITIONS):
         far, near = turn_messages(message, turn - 1)
         previous = (far.astype(f32) + near.astype(f32)).astype(bf16)
-        if turn == 8:
-            inverse_out, coupling_in = tie((inverse_out, coupling_in), message)
+        if turn == 10:
+            outer, coupling_in = tie((outer, coupling_in), message)
             inner = lax.dot_general(
-                inverse_out, coupling_in, (((1,), (1,)), ((), ())), preferred_element_type=f32
+                outer[:, :nodes], coupling_in, (((1,), (1,)), ((), ())), preferred_element_type=f32
             ).astype(bf16)
             inner_all = gathered(inner, False)
             previous = tie(previous, inner)
@@ -282,8 +281,8 @@
 
     last = exchange_x(last_chunk)
 
-    coupling_out, inner_all = tie((coupling_out, inner_all), lines)
-    folded = jnp.dot(coupling_out, inner_all, preferred_element_type=f32).astype(bf16)
+    inner_all = tie(inner_all, rounded)
+    folded = jnp.dot(outer[:, nodes:], inner_all, preferred_element_type=f32).astype(bf16)
 
     def folded_chunk(step):
         return lax.dynamic_slice(folded, ((r ^ step) * rows, 0), (rows, line))

time: 175 us -> 167 us (0.954)
  waiting for transfers between devices: 81.4 us -> 78.2 us
  starting transfers between devices: 49.4 us -> 46.9 us
    all_gather x4 -> x3, waiting for transfers between devices: 10.9 us -> 7.31 us  [gathered(): lax.all_gather(array, AXES, axis=0, tiled=True, axis_index_groups=gather_...]
    ppermute x48, starting transfers between devices: 49.2 us -> 46.7 us  [permuted(): return lax.ppermute(value, AXES, pairs)]
  transfers between devices with their start and end apart: 52 -> 51, of which waited for: 20 -> 20; matrix products, arithmetic and copies ran while one was open for 11% -> 8% of each run, Pallas kernels for 2% -> 2%
where the time goes in v8:
time: 167 us; the launch traced here: 166 us
  waiting for transfers between devices  78.2 us (47%)
  starting transfers between devices  46.9 us (28%)
  matrix products  17.9 us (11%)
  between operations  14.5 us (9%)
  Pallas kernels  4.49 us (3%)
  local copies, waits for them, and re-layouts  2.46 us (1%)
    ppermute x48, waiting for transfers between devices, permuted(): return lax.ppermute(value, AXES, pairs)  70.2 us
    ppermute x48, starting transfers between devices, permuted(): return lax.ppermute(value, AXES, pairs)  46.7 us
    dot_general x15, matrix products, shards(): lax.dot_general(previous, block, (((1,), (1,)), ((), ())), preferred_elem...  9.76 us
    all_gather x3, waiting for transfers between devices, gathered(): lax.all_gather(array, AXES, axis=0, tiled=True, axis_index_groups=gather_...  7.31 us
    pallas_call x4, Pallas kernels, kernel_call(): pl.pallas_call(body, out_shape=out_shapes, in_specs=[pl.BlockSpec(memory_...  4.49 us
    dot_general x1, matrix products, shards(): lax.dot_general(outer[:, :nodes], coupling_in, (((1,), (1,)), ((), ())),...  4.3 us
    dot_general x1, matrix products, shards(): jnp.dot(outer[:, nodes:], inner_all, preferred_element_type=f32)  3.47 us
  transfers between devices with their start and end apart: 51, of which 20 were waited for; matrix products, arithmetic and copies ran while one was open for 8% of the time, Pallas kernels for 2%

profile of v8, /device:TPU:224, one launch (start us, length us, event | category | flops | bytes accessed | tf_op | source)
XLA Modules:
  0.0 166.0 jit_solution(11960257125133359636)
XLA Ops:
  7.2 0.7 all-gather.9.cloned.1.call-update
  8.0 1.4 reshape_squeeze.3
  10.4 1.1 pad_maximum_fusion
  11.6 1.6 collective-permute-start.1
  13.2 2.7 %collective-permute-start.2 = (f32[24,128]{1,0:T(8,128)S(1)}, f32[24,128]{1,0:T(8,128)S(1)}, u32[]{:S(2)}, u32[]{:S(2)}) collective-permute-start(f32[24,128]{1,0:T(8,128)S(1)} %get-tuple-element.69), channel_id=1, source_target_pairs={{0,2},{1,3},{2,0},{3,1},{4,6},{5,7},{6,4},{7,5},{8,10},{9,11},{10,... | collective-permute-start | bytes 36872 | tf_op jit(solution)/shard_map/ppermute | solution.py:29
  17.1 1.7 %collective-permute-start = (bf16[128,1024]{1,0:T(8,128)(2,1)S(1)}, bf16[128,1024]{1,0:T(8,128)(2,1)S(1)}, u32[]{:S(2)}, u32[]{:S(2)}) collective-permute-start(bf16[128,1024]{1,0:T(8,128)(2,1)S(1)} %get-tuple-element.17), channel_id=1, source_target_pairs={{0,4},{1,5},{2,6},{3,7},{4,0},{5,1},{6,2},{7,3},{8,12},{9,13},{10,... | collective-permute-start | bytes 786440 | tf_op jit(solution)/shard_map/ppermute | solution.py:29
  18.8 2.1 %collective-permute-done.3 = f32[24,128]{1,0:T(8,128)S(1)} collective-permute-done((f32[24,128]{1,0:T(8,128)S(1)}, f32[24,128]{1,0:T(8,128)S(1)}, u32[]{:S(2)}, u32[]{:S(2)}) %collective-permute-start.3) | collective-permute-done | bytes 12320 | tf_op jit(solution)/shard_map/ppermute | solution.py:29
  20.9 2.7 %collective-permute-done = bf16[128,1024]{1,0:T(8,128)(2,1)S(1)} collective-permute-done((bf16[128,1024]{1,0:T(8,128)(2,1)S(1)}, bf16[128,1024]{1,0:T(8,128)(2,1)S(1)}, u32[]{:S(2)}, u32[]{:S(2)}) %collective-permute-start) | collective-permute-done | bytes 262176 | tf_op jit(solution)/shard_map/ppermute | solution.py:29
  24.1 3.9 %collective-permute-start.8 = (bf16[256,1024]{1,0:T(8,128)(2,1)S(1)}, bf16[256,1024]{1,0:T(8,128)(2,1)S(1)}, u32[]{:S(2)}, u32[]{:S(2)}) collective-permute-start(bf16[256,1024]{1,0:T(8,128)(2,1)S(1)} %maximum_select_fusion.refs_0_), channel_id=1, source_target_pairs={{0,2},{1,3},{2,0},{3,1},{4,6},{5,7},{6,4},{7,5},{8,10},{9,11},{10,... | collective-permute-start | bytes 1572872 | tf_op jit(solution)/shard_map/ppermute | solution.py:29
  28.6 1.6 collective-permute-start.4
  30.2 2.0 %collective-permute-done.4 = f32[1,512]{1,0:T(1,128)S(1)} collective-permute-done((f32[1,512]{1,0:T(1,128)S(1)}, f32[1,512]{1,0:T(1,128)S(1)}, u32[]{:S(2)}, u32[]{:S(2)}) %collective-permute-start.4) | collective-permute-done | bytes 2080 | tf_op jit(solution)/shard_map/ppermute | solution.py:29
  32.2 12.0 %collective-permute-done.7.refs_1_ = bf16[256,1024]{1,0:T(8,128)(2,1)S(1)} collective-permute-done((bf16[256,1024]{1,0:T(8,128)(2,1)S(1)}, bf16[256,1024]{1,0:T(8,128)(2,1)S(1)}, u32[]{:S(2)}, u32[]{:S(2)}) %collective-permute-start.7) | collective-permute-done | bytes 524320 | tf_op jit(solution)/shard_map/ppermute | solution.py:29
  44.2 13.5 %collective-permute-done.8.refs_2_ = bf16[256,1024]{1,0:T(8,128)(2,1)S(1)} collective-permute-done((bf16[256,1024]{1,0:T(8,128)(2,1)S(1)}, bf16[256,1024]{1,0:T(8,128)(2,1)S(1)}, u32[]{:S(2)}, u32[]{:S(2)}) %collective-permute-start.8) | collective-permute-done | bytes 524320 | tf_op jit(solution)/shard_map/ppermute | solution.py:29
  57.8 0.7 shard_map.86
  58.5 0.7 fusion.25
  59.1 0.7 collective-permute-start.10
  59.8 0.7 collective-permute-start.11
  60.5 0.7 fusion.26
  61.1 1.4 collective-permute-start.13
  62.6 2.1 %collective-permute-done.12 = bf16[16,1024]{1,0:T(8,128)(2,1)S(1)} collective-permute-done((bf16[16,1024]{1,0:T(8,128)(2,1)S(1)}, bf16[16,1024]{1,0:T(8,128)(2,1)S(1)}, u32[]{:S(2)}, u32[]{:S(2)}) %collective-permute-start.12) | collective-permute-done | bytes 32800 | tf_op jit(solution)/shard_map/ppermute | solution.py:29
  64.7 0.7 fusion.27
  65.4 0.7 collective-permute-start.14
  66.0 0.7 collective-permute-start.15
  66.7 0.7 fusion.28
  67.4 1.2 collective-permute-start.17
  68.6 2.3 %collective-permute-done.16 = bf16[16,1024]{1,0:T(8,128)(2,1)S(1)} collective-permute-done((bf16[16,1024]{1,0:T(8,128)(2,1)S(1)}, bf16[16,1024]{1,0:T(8,128)(2,1)S(1)}, u32[]{:S(2)}, u32[]{:S(2)}) %collective-permute-start.16) | collective-permute-done | bytes 32800 | tf_op jit(solution)/shard_map/ppermute | solution.py:29
  70.9 0.7 fusion.29
  71.6 0.7 collective-permute-start.18
  72.3 0.7 collective-permute-start.19
  72.9 0.7 fusion.30
  73.6 1.0 collective-permute-start.21
  74.6 2.9 %collective-permute-done.20 = bf16[16,1024]{1,0:T(8,128)(2,1)S(1)} collective-permute-done((bf16[16,1024]{1,0:T(8,128)(2,1)S(1)}, bf16[16,1024]{1,0:T(8,128)(2,1)S(1)}, u32[]{:S(2)}, u32[]{:S(2)}) %collective-permute-start.20) | collective-permute-done | bytes 32800 | tf_op jit(solution)/shard_map/ppermute | solution.py:29
  78.1 0.7 collective-permute-start.22
  78.8 0.7 collective-permute-start.23
  79.5 0.7 fusion.32
  81.2 2.7 %collective-permute-done.24 = bf16[16,1024]{1,0:T(8,128)(2,1)S(1)} collective-permute-done((bf16[16,1024]{1,0:T(8,128)(2,1)S(1)}, bf16[16,1024]{1,0:T(8,128)(2,1)S(1)}, u32[]{:S(2)}, u32[]{:S(2)}) %collective-permute-start.24) | collective-permute-done | bytes 32800 | tf_op jit(solution)/shard_map/ppermute | solution.py:29
  84.5 0.7 collective-permute-start.26
  85.2 0.7 collective-permute-start.27
  85.9 7.3 %all-gather.5.cloned.1.call-done = bf16[512,4096]{1,0:T(8,128)(2,1)} async-done(((bf16[128,4096]{1,0:T(8,128)(2,1)}), bf16[512,4096]{1,0:T(8,128)(2,1)}) %all-gather.5.cloned.1.call-update) | async-done | bytes 4194320 | tf_op jit(solution)/shard_map/all_gather | solution.py:134
  93.2 4.3 %fusion.7 = bf16[512,512]{1,0:T(8,128)(2,1)} fusion(bf16[512,2048]{1,0:T(8,128)(2,1)} %bitcast.68, bf16[512,4096]{1,0:T(8,128)(2,1)} %all-gather.5.cloned.1.call-done), kind=kOutput, calls=%fused_computation.5 | convolution fusion | flops 1074003968 | bytes 4718592 | tf_op jit(solution)/shard_map/dot_general | solution.py:230
  98.2 1.5 collective-permute-start.29
  99.7 1.9 %collective-permute-done.28 = bf16[16,1024]{1,0:T(8,128)(2,1)S(1)} collective-permute-done((bf16[16,1024]{1,0:T(8,128)(2,1)S(1)}, bf16[16,1024]{1,0:T(8,128)(2,1)S(1)}, u32[]{:S(2)}, u32[]{:S(2)}) %collective-permute-start.28) | collective-permute-done | bytes 32800 | tf_op jit(solution)/shard_map/ppermute | solution.py:29
  102.2 0.7 collective-permute-start.30
  102.9 0.7 collective-permute-start.31
  104.3 1.5 collective-permute-start.33
  105.7 1.9 %collective-permute-done.32 = bf16[16,1024]{1,0:T(8,128)(2,1)S(1)} collective-permute-done((bf16[16,1024]{1,0:T(8,128)(2,1)S(1)}, bf16[16,1024]{1,0:T(8,128)(2,1)S(1)}, u32[]{:S(2)}, u32[]{:S(2)}) %collective-permute-start.32) | collective-permute-done | bytes 32800 | tf_op jit(solution)/shard_map/ppermute | solution.py:29
  108.3 1.3 collective-permute-start.34
  109.6 1.3 collective-permute-start.35
  110.9 14.5 %collective-permute-done.34 = bf16[16,1024]{1,0:T(8,128)(2,1)S(1)} collective-permute-done((bf16[16,1024]{1,0:T(8,128)(2,1)S(1)}, bf16[16,1024]{1,0:T(8,128)(2,1)S(1)}, u32[]{:S(2)}, u32[]{:S(2)}) %collective-permute-start.34) | collective-permute-done | bytes 32800 | tf_op jit(solution)/shard_map/ppermute | solution.py:29
  126.8 3.2 %collective-permute-done.36 = bf16[16,1024]{1,0:T(8,128)(2,1)S(1)} collective-permute-done((bf16[16,1024]{1,0:T(8,128)(2,1)S(1)}, bf16[16,1024]{1,0:T(8,128)(2,1)S(1)}, u32[]{:S(2)}, u32[]{:S(2)}) %collective-permute-start.36) | collective-permute-done | bytes 32800 | tf_op jit(solution)/shard_map/ppermute | solution.py:29
  129.9 0.7 fusion.40
  130.7 3.9 %collective-permute-done.38 = bf16[16,1024]{1,0:T(8,128)(2,1)S(1)} collective-permute-done((bf16[16,1024]{1,0:T(8,128)(2,1)S(1)}, bf16[16,1024]{1,0:T(8,128)(2,1)S(1)}, u32[]{:S(2)}, u32[]{:S(2)}) %collective-permute-start.38) | collective-permute-done | bytes 32800 | tf_op jit(solution)/shard_map/ppermute | solution.py:29
  134.6 1.9 %collective-permute-start.42 = (bf16[16,1024]{1,0:T(8,128)(2,1)S(1)}, bf16[16,1024]{1,0:T(8,128)(2,1)S(1)}, u32[]{:S(2)}, u32[]{:S(2)}) collective-permute-start(bf16[16,1024]{1,0:T(8,128)(2,1)S(1)} %get-tuple-element.40), channel_id=1, source_target_pairs={{0,12},{1,13},{2,14},{3,15},{4,8},{5,9},{6,10},{7,11},{8,4},{9,5},... | collective-permute-start | bytes 98312 | tf_op jit(solution)/shard_map/ppermute | solution.py:29
  136.8 1.9 %collective-permute-start.43 = (bf16[16,512]{1,0:T(8,128)(2,1)S(1)}, bf16[16,512]{1,0:T(8,128)(2,1)S(1)}, u32[]{:S(2)}, u32[]{:S(2)}) collective-permute-start(bf16[16,512]{1,0:T(8,128)(2,1)S(1)} %get-tuple-element.49), channel_id=1, source_target_pairs={{16,4},{17,5},{18,6},{19,7},{20,0},{21,1},{22,2},{23,3},{24,12},{2... | collective-permute-start | bytes 49160 | tf_op jit(solution)/shard_map/ppermute | solution.py:29
  138.7 1.9 %collective-permute-start.44 = (bf16[16,512]{1,0:T(8,128)(2,1)S(1)}, bf16[16,512]{1,0:T(8,128)(2,1)S(1)}, u32[]{:S(2)}, u32[]{:S(2)}) collective-permute-start(bf16[16,512]{1,0:T(8,128)(2,1)S(1)} %get-tuple-element.50), channel_id=1, source_target_pairs={{16,0},{17,1},{18,2},{19,3},{20,4},{21,5},{22,6},{23,7},{24,8},{25... | collective-permute-start | bytes 49160 | tf_op jit(solution)/shard_map/ppermute | solution.py:29
  140.7 1.1 collective-permute-done.43
  142.2 3.5 %fusion.4 = bf16[512,512]{1,0:T(8,128)(2,1)S(1)} fusion(bf16[2048,512]{1,0:T(8,128)(2,1)} %all-gather.7.cloned.1.call-done, bf16[512,4096]{1,0:T(8,128)(2,1)} %all-gather.5.cloned.1.call-done), kind=kOutput, calls=%fused_computation.4 | convolution fusion | flops 1074003968 | bytes 4718592 | tf_op jit(solution)/shard_map/dot_general | solution.py:285
  145.8 1.7 %collective-permute-start.40 = (bf16[128,512]{1,0:T(8,128)(2,1)S(1)}, bf16[128,512]{1,0:T(8,128)(2,1)S(1)}, u32[]{:S(2)}, u32[]{:S(2)}) collective-permute-start(bf16[128,512]{1,0:T(8,128)(2,1)S(1)} %get-tuple-element.32), channel_id=1, source_target_pairs={{0,2},{1,3},{2,0},{3,1},{4,6},{5,7},{6,4},{7,5},{8,10},{9,11},{10,... | collective-permute-start | bytes 393224 | tf_op jit(solution)/shard_map/ppermute | solution.py:29
  147.6 2.9 %collective-permute-start.41 = (bf16[128,512]{1,0:T(8,128)(2,1)S(1)}, bf16[128,512]{1,0:T(8,128)(2,1)S(1)}, u32[]{:S(2)}, u32[]{:S(2)}) collective-permute-start(bf16[128,512]{1,0:T(8,128)(2,1)S(1)} %get-tuple-element.31), channel_id=1, source_target_pairs={{0,3},{1,2},{2,1},{3,0},{4,7},{5,6},{6,5},{7,4},{8,11},{9,10},{10,... | collective-permute-start | bytes 393224 | tf_op jit(solution)/shard_map/ppermute | solution.py:29
  150.6 1.7 %collective-permute-start.46 = (bf16[16,2432]{1,0:T(8,128)(2,1)S(1)}, bf16[16,2432]{1,0:T(8,128)(2,1)S(1)}, u32[]{:S(2)}, u32[]{:S(2)}) collective-permute-start(bf16[16,2432]{1,0:T(8,128)(2,1)S(1)} %get-tuple-element.37), channel_id=1, source_target_pairs={{0,2},{1,3},{2,0},{3,1},{4,6},{5,7},{6,4},{7,5},{8,10},{9,11},{10,... | collective-permute-start | bytes 233480 | tf_op jit(solution)/shard_map/ppermute | solution.py:29
  152.4 2.9 %collective-permute-start.47 = (bf16[16,2432]{1,0:T(8,128)(2,1)S(1)}, bf16[16,2432]{1,0:T(8,128)(2,1)S(1)}, u32[]{:S(2)}, u32[]{:S(2)}) collective-permute-start(bf16[16,2432]{1,0:T(8,128)(2,1)S(1)} %get-tuple-element.35), channel_id=1, source_target_pairs={{0,3},{1,2},{2,1},{3,0},{4,7},{5,6},{6,5},{7,4},{8,11},{9,10},{10,... | collective-permute-start | bytes 233480 | tf_op jit(solution)/shard_map/ppermute | solution.py:29
  155.4 1.8 %shard_map.87 = (f32[128,2048]{1,0:T(8,128)}, bf16[128,2048]{1,0:T(8,128)(2,1)S(1)}) custom-call(s32[3]{0:T(128)S(1)} %pad_add_fusion.place, f32[128,2048]{1,0:T(8,128)S(1)} %bitcast.57, bf16[128,512]{1,0:T(8,128)(2,1)S(1)} %get-tuple-element.34.refs_1_, bf16[128,512]{1,0:T(8,128)(2,1)S(1)} %collective-permute-done.39.refs_2_, ...), custom_call_target="tpu_custom_call" | custom-call | bytes 3145728 | tf_op jit(solution)/shard_map/pallas_call | solution.py:58
  157.2 0.8 collective-permute-done.47.refs_3_
  158.0 1.5 shard_map.88
  (107 shorter events, 11.1 us)
Async XLA Ops:
  7.2 2.8 %copy-start.3 = (bf16[1,128,2048]{2,1,0:T(8,128)(2,1)S(1)}, bf16[1,128,2048]{2,1,0:T(8,128)(2,1)}, u32[]{:S(2)}) copy-start(bf16[1,128,2048]{2,1,0:T(8,128)(2,1)} %param.7) | copy-start | bytes 1572868
  7.2 78.7 %all-gather.9.cloned.1.call-start = ((), (), s32[]{:S(2)}) async-start(), calls=%async_computation.2 | async-start | bytes 2621440 | tf_op jit(solution)/shard_map/all_gather | solution.py:134
  7.9 85.3 %all-gather.5.cloned.1.call-start = ((), (), s32[]{:S(2)}) async-start(), calls=%async_computation | async-start | bytes 5242880 | tf_op jit(solution)/shard_map/all_gather | solution.py:134
  9.4 1.0 copy-start.4
  10.0 1.6 copy-start.2
  10.0 1.6 copy-start.5
  10.1 6.4 %copy-start.1 = (bf16[1,128,2048]{2,1,0:T(8,128)(2,1)S(1)}, bf16[1,128,2048]{2,1,0:T(8,128)(2,1)}, u32[]{:S(2)}) copy-start(bf16[1,128,2048]{2,1,0:T(8,128)(2,1)} %param.9) | copy-start | bytes 1572868
  11.5 130.7 %all-gather.7.cloned.1.call-start = ((), (), s32[]{:S(2)}) async-start(), calls=%async_computation.1 | async-start | bytes 2621440 | tf_op jit(solution)/shard_map/all_gather | solution.py:134
  11.6 7.1 %collective-permute-start.1 = (f32[24,128]{1,0:T(8,128)S(1)}, f32[24,128]{1,0:T(8,128)S(1)}, u32[]{:S(2)}, u32[]{:S(2)}) collective-permute-start(f32[24,128]{1,0:T(8,128)S(1)} %get-tuple-element.68), channel_id=1, source_target_pairs={{0,1},{1,0},{2,3},{3,2},{4,5},{5,4},{6,7},{7,6},{8,9},{9,8},{10,11... | collective-permute-start | bytes 36872 | tf_op jit(solution)/shard_map/ppermute | solution.py:29
  13.2 5.5 %collective-permute-start.2 = (f32[24,128]{1,0:T(8,128)S(1)}, f32[24,128]{1,0:T(8,128)S(1)}, u32[]{:S(2)}, u32[]{:S(2)}) collective-permute-start(f32[24,128]{1,0:T(8,128)S(1)} %get-tuple-element.69), channel_id=1, source_target_pairs={{0,2},{1,3},{2,0},{3,1},{4,6},{5,7},{6,4},{7,5},{8,10},{9,11},{10,... | collective-permute-start | bytes 36872 | tf_op jit(solution)/shard_map/ppermute | solution.py:29
  16.0 4.9 %collective-permute-start.3 = (f32[24,128]{1,0:T(8,128)S(1)}, f32[24,128]{1,0:T(8,128)S(1)}, u32[]{:S(2)}, u32[]{:S(2)}) collective-permute-start(f32[24,128]{1,0:T(8,128)S(1)} %get-tuple-element.70), channel_id=1, source_target_pairs={{0,3},{1,2},{2,1},{3,0},{4,7},{5,6},{6,5},{7,4},{8,11},{9,10},{10,... | collective-permute-start | bytes 36872 | tf_op jit(solution)/shard_map/ppermute | solution.py:29
  17.1 6.5 %collective-permute-start = (bf16[128,1024]{1,0:T(8,128)(2,1)S(1)}, bf16[128,1024]{1,0:T(8,128)(2,1)S(1)}, u32[]{:S(2)}, u32[]{:S(2)}) collective-permute-start(bf16[128,1024]{1,0:T(8,128)(2,1)S(1)} %get-tuple-element.17), channel_id=1, source_target_pairs={{0,4},{1,5},{2,6},{3,7},{4,0},{5,1},{6,2},{7,3},{8,12},{9,13},{10,... | collective-permute-start | bytes 786440 | tf_op jit(solution)/shard_map/ppermute | solution.py:29
  23.7 20.5 %collective-permute-start.7 = (bf16[256,1024]{1,0:T(8,128)(2,1)S(1)}, bf16[256,1024]{1,0:T(8,128)(2,1)S(1)}, u32[]{:S(2)}, u32[]{:S(2)}) collective-permute-start(bf16[256,1024]{1,0:T(8,128)(2,1)S(1)} %maximum_select_fusion.refs_0_), channel_id=1, source_target_pairs={{0,1},{1,0},{2,3},{3,2},{4,5},{5,4},{6,7},{7,6},{8,9},{9,8},{10,11... | collective-permute-start | bytes 1572872 | tf_op jit(solution)/shard_map/ppermute | solution.py:29
  24.1 33.6 %collective-permute-start.8 = (bf16[256,1024]{1,0:T(8,128)(2,1)S(1)}, bf16[256,1024]{1,0:T(8,128)(2,1)S(1)}, u32[]{:S(2)}, u32[]{:S(2)}) collective-permute-start(bf16[256,1024]{1,0:T(8,128)(2,1)S(1)} %maximum_select_fusion.refs_0_), channel_id=1, source_target_pairs={{0,2},{1,3},{2,0},{3,1},{4,6},{5,7},{6,4},{7,5},{8,10},{9,11},{10,... | collective-permute-start | bytes 1572872 | tf_op jit(solution)/shard_map/ppermute | solution.py:29
  28.0 29.8 %collective-permute-start.9 = (bf16[256,1024]{1,0:T(8,128)(2,1)S(1)}, bf16[256,1024]{1,0:T(8,128)(2,1)S(1)}, u32[]{:S(2)}, u32[]{:S(2)}) collective-permute-start(bf16[256,1024]{1,0:T(8,128)(2,1)S(1)} %maximum_select_fusion.refs_0_), channel_id=1, source_target_pairs={{0,3},{1,2},{2,1},{3,0},{4,7},{5,6},{6,5},{7,4},{8,11},{9,10},{10,... | collective-permute-start | bytes 1572872 | tf_op jit(solution)/shard_map/ppermute | solution.py:29
  28.6 3.6 %collective-permute-start.4 = (f32[1,512]{1,0:T(1,128)S(1)}, f32[1,512]{1,0:T(1,128)S(1)}, u32[]{:S(2)}, u32[]{:S(2)}) collective-permute-start(f32[1,512]{1,0:T(1,128)S(1)} %slice.32), channel_id=1, source_target_pairs={{0,4},{1,5},{2,6},{3,7},{4,0},{5,1},{6,2},{7,3},{8,12},{9,13},{10,... | collective-permute-start | bytes 6152 | tf_op jit(solution)/shard_map/ppermute | solution.py:29
  30.2 28.3 %collective-permute-start.5 = (bf16[16,1024]{1,0:T(8,128)(2,1)S(1)}, bf16[16,1024]{1,0:T(8,128)(2,1)S(1)}, u32[]{:S(2)}, u32[]{:S(2)}) collective-permute-start(bf16[16,1024]{1,0:T(8,128)(2,1)S(1)} %fusion.42), channel_id=1, source_target_pairs={{0,20},{1,21},{2,22},{3,23},{4,16},{5,17},{6,18},{7,19},{8,28},{9,... | collective-permute-start | bytes 98312 | tf_op jit(solution)/shard_map/ppermute | solution.py:29
  32.2 26.3 %collective-permute-start.6 = (bf16[16,1024]{1,0:T(8,128)(2,1)S(1)}, bf16[16,1024]{1,0:T(8,128)(2,1)S(1)}, u32[]{:S(2)}, u32[]{:S(2)}) collective-permute-start(bf16[16,1024]{1,0:T(8,128)(2,1)S(1)} %fusion.42), channel_id=1, source_target_pairs={{0,16},{1,17},{2,18},{3,19},{4,20},{5,21},{6,22},{7,23},{8,24},{9,... | collective-permute-start | bytes 98312 | tf_op jit(solution)/shard_map/ppermute | solution.py:29
  59.1 1.3 collective-permute-start.10
  59.8 0.7 collective-permute-start.11
  61.1 3.6 %collective-permute-start.12 = (bf16[16,1024]{1,0:T(8,128)(2,1)S(1)}, bf16[16,1024]{1,0:T(8,128)(2,1)S(1)}, u32[]{:S(2)}, u32[]{:S(2)}) collective-permute-start(bf16[16,1024]{1,0:T(8,128)(2,1)S(1)} %fusion.26), channel_id=1, source_target_pairs={{0,20},{1,21},{2,22},{3,23},{4,16},{5,17},{6,18},{7,19},{8,28},{9,... | collective-permute-start | bytes 98312 | tf_op jit(solution)/shard_map/ppermute | solution.py:29
  61.1 3.6 %collective-permute-start.13 = (bf16[16,1024]{1,0:T(8,128)(2,1)S(1)}, bf16[16,1024]{1,0:T(8,128)(2,1)S(1)}, u32[]{:S(2)}, u32[]{:S(2)}) collective-permute-start(bf16[16,1024]{1,0:T(8,128)(2,1)S(1)} %fusion.26), channel_id=1, source_target_pairs={{0,16},{1,17},{2,18},{3,19},{4,20},{5,21},{6,22},{7,23},{8,24},{9,... | collective-permute-start | bytes 98312 | tf_op jit(solution)/shard_map/ppermute | solution.py:29
  65.4 1.3 collective-permute-start.14
  66.0 0.7 collective-permute-start.15
  67.4 3.5 %collective-permute-start.16 = (bf16[16,1024]{1,0:T(8,128)(2,1)S(1)}, bf16[16,1024]{1,0:T(8,128)(2,1)S(1)}, u32[]{:S(2)}, u32[]{:S(2)}) collective-permute-start(bf16[16,1024]{1,0:T(8,128)(2,1)S(1)} %fusion.28), channel_id=1, source_target_pairs={{0,20},{1,21},{2,22},{3,23},{4,16},{5,17},{6,18},{7,19},{8,28},{9,... | collective-permute-start | bytes 98312 | tf_op jit(solution)/shard_map/ppermute | solution.py:29
  67.4 3.5 %collective-permute-start.17 = (bf16[16,1024]{1,0:T(8,128)(2,1)S(1)}, bf16[16,1024]{1,0:T(8,128)(2,1)S(1)}, u32[]{:S(2)}, u32[]{:S(2)}) collective-permute-start(bf16[16,1024]{1,0:T(8,128)(2,1)S(1)} %fusion.28), channel_id=1, source_target_pairs={{0,16},{1,17},{2,18},{3,19},{4,20},{5,21},{6,22},{7,23},{8,24},{9,... | collective-permute-start | bytes 98312 | tf_op jit(solution)/shard_map/ppermute | solution.py:29
  71.6 1.3 collective-permute-start.18
  72.3 0.7 collective-permute-start.19
  73.6 3.9 %collective-permute-start.20 = (bf16[16,1024]{1,0:T(8,128)(2,1)S(1)}, bf16[16,1024]{1,0:T(8,128)(2,1)S(1)}, u32[]{:S(2)}, u32[]{:S(2)}) collective-permute-start(bf16[16,1024]{1,0:T(8,128)(2,1)S(1)} %fusion.30), channel_id=1, source_target_pairs={{0,20},{1,21},{2,22},{3,23},{4,16},{5,17},{6,18},{7,19},{8,28},{9,... | collective-permute-start | bytes 98312 | tf_op jit(solution)/shard_map/ppermute | solution.py:29
  73.6 3.9 %collective-permute-start.21 = (bf16[16,1024]{1,0:T(8,128)(2,1)S(1)}, bf16[16,1024]{1,0:T(8,128)(2,1)S(1)}, u32[]{:S(2)}, u32[]{:S(2)}) collective-permute-start(bf16[16,1024]{1,0:T(8,128)(2,1)S(1)} %fusion.30), channel_id=1, source_target_pairs={{0,16},{1,17},{2,18},{3,19},{4,20},{5,21},{6,22},{7,23},{8,24},{9,... | collective-permute-start | bytes 98312 | tf_op jit(solution)/shard_map/ppermute | solution.py:29
  78.1 1.3 collective-permute-start.22
  78.8 0.7 collective-permute-start.23
  80.2 3.7 %collective-permute-start.24 = (bf16[16,1024]{1,0:T(8,128)(2,1)S(1)}, bf16[16,1024]{1,0:T(8,128)(2,1)S(1)}, u32[]{:S(2)}, u32[]{:S(2)}) collective-permute-start(bf16[16,1024]{1,0:T(8,128)(2,1)S(1)} %fusion.32), channel_id=1, source_target_pairs={{0,20},{1,21},{2,22},{3,23},{4,16},{5,17},{6,18},{7,19},{8,28},{9,... | collective-permute-start | bytes 98312 | tf_op jit(solution)/shard_map/ppermute | solution.py:29
  80.5 3.3 %collective-permute-start.25 = (bf16[16,1024]{1,0:T(8,128)(2,1)S(1)}, bf16[16,1024]{1,0:T(8,128)(2,1)S(1)}, u32[]{:S(2)}, u32[]{:S(2)}) collective-permute-start(bf16[16,1024]{1,0:T(8,128)(2,1)S(1)} %fusion.32), channel_id=1, source_target_pairs={{0,16},{1,17},{2,18},{3,19},{4,20},{5,21},{6,22},{7,23},{8,24},{9,... | collective-permute-start | bytes 98312 | tf_op jit(solution)/shard_map/ppermute | solution.py:29
  84.5 1.3 collective-permute-start.26
  85.2 0.7 collective-permute-start.27
  98.1 3.4 %collective-permute-start.28 = (bf16[16,1024]{1,0:T(8,128)(2,1)S(1)}, bf16[16,1024]{1,0:T(8,128)(2,1)S(1)}, u32[]{:S(2)}, u32[]{:S(2)}) collective-permute-start(bf16[16,1024]{1,0:T(8,128)(2,1)S(1)} %fusion.34), channel_id=1, source_target_pairs={{0,20},{1,21},{2,22},{3,23},{4,16},{5,17},{6,18},{7,19},{8,28},{9,... | collective-permute-start | bytes 98312 | tf_op jit(solution)/shard_map/ppermute | solution.py:29
  98.2 3.3 %collective-permute-start.29 = (bf16[16,1024]{1,0:T(8,128)(2,1)S(1)}, bf16[16,1024]{1,0:T(8,128)(2,1)S(1)}, u32[]{:S(2)}, u32[]{:S(2)}) collective-permute-start(bf16[16,1024]{1,0:T(8,128)(2,1)S(1)} %fusion.34), channel_id=1, source_target_pairs={{0,16},{1,17},{2,18},{3,19},{4,20},{5,21},{6,22},{7,23},{8,24},{9,... | collective-permute-start | bytes 98312 | tf_op jit(solution)/shard_map/ppermute | solution.py:29
  102.2 1.4 collective-permute-start.30
  102.9 0.7 collective-permute-start.31
  104.2 3.4 %collective-permute-start.32 = (bf16[16,1024]{1,0:T(8,128)(2,1)S(1)}, bf16[16,1024]{1,0:T(8,128)(2,1)S(1)}, u32[]{:S(2)}, u32[]{:S(2)}) collective-permute-start(bf16[16,1024]{1,0:T(8,128)(2,1)S(1)} %fusion.36), channel_id=1, source_target_pairs={{0,20},{1,21},{2,22},{3,23},{4,16},{5,17},{6,18},{7,19},{8,28},{9,... | collective-permute-start | bytes 98312 | tf_op jit(solution)/shard_map/ppermute | solution.py:29
  104.3 3.4 %collective-permute-start.33 = (bf16[16,1024]{1,0:T(8,128)(2,1)S(1)}, bf16[16,1024]{1,0:T(8,128)(2,1)S(1)}, u32[]{:S(2)}, u32[]{:S(2)}) collective-permute-start(bf16[16,1024]{1,0:T(8,128)(2,1)S(1)} %fusion.36), channel_id=1, source_target_pairs={{0,16},{1,17},{2,18},{3,19},{4,20},{5,21},{6,22},{7,23},{8,24},{9,... | collective-permute-start | bytes 98312 | tf_op jit(solution)/shard_map/ppermute | solution.py:29
  108.3 17.1 %collective-permute-start.34 = (bf16[16,1024]{1,0:T(8,128)(2,1)S(1)}, bf16[16,1024]{1,0:T(8,128)(2,1)S(1)}, u32[]{:S(2)}, u32[]{:S(2)}) collective-permute-start(bf16[16,1024]{1,0:T(8,128)(2,1)S(1)} %fusion.37), channel_id=1, source_target_pairs={{208,236},{209,237},{210,238},{211,239},{212,232},{213,233},{214,2... | collective-permute-start | bytes 98312 | tf_op jit(solution)/shard_map/ppermute | solution.py:29
  109.6 16.2 %collective-permute-start.35 = (bf16[16,1024]{1,0:T(8,128)(2,1)S(1)}, bf16[16,1024]{1,0:T(8,128)(2,1)S(1)}, u32[]{:S(2)}, u32[]{:S(2)}) collective-permute-start(bf16[16,1024]{1,0:T(8,128)(2,1)S(1)} %fusion.37), channel_id=1, source_target_pairs={{208,224},{209,225},{210,226},{211,227},{212,228},{213,229},{214,2... | collective-permute-start | bytes 98312 | tf_op jit(solution)/shard_map/ppermute | solution.py:29
  126.4 3.5 %collective-permute-start.36 = (bf16[16,1024]{1,0:T(8,128)(2,1)S(1)}, bf16[16,1024]{1,0:T(8,128)(2,1)S(1)}, u32[]{:S(2)}, u32[]{:S(2)}) collective-permute-start(bf16[16,1024]{1,0:T(8,128)(2,1)S(1)} %fusion.38), channel_id=1, source_target_pairs={{0,20},{1,21},{2,22},{3,23},{4,16},{5,17},{6,18},{7,19},{8,28},{9,... | collective-permute-start | bytes 98312 | tf_op jit(solution)/shard_map/ppermute | solution.py:29
  126.4 3.5 %collective-permute-start.37 = (bf16[16,1024]{1,0:T(8,128)(2,1)S(1)}, bf16[16,1024]{1,0:T(8,128)(2,1)S(1)}, u32[]{:S(2)}, u32[]{:S(2)}) collective-permute-start(bf16[16,1024]{1,0:T(8,128)(2,1)S(1)} %fusion.38), channel_id=1, source_target_pairs={{0,16},{1,17},{2,18},{3,19},{4,20},{5,21},{6,22},{7,23},{8,24},{9,... | collective-permute-start | bytes 98312 | tf_op jit(solution)/shard_map/ppermute | solution.py:29
  130.6 3.9 %collective-permute-start.38 = (bf16[16,1024]{1,0:T(8,128)(2,1)S(1)}, bf16[16,1024]{1,0:T(8,128)(2,1)S(1)}, u32[]{:S(2)}, u32[]{:S(2)}) collective-permute-start(bf16[16,1024]{1,0:T(8,128)(2,1)S(1)} %fusion.40), channel_id=1, source_target_pairs={{0,4},{1,5},{2,6},{3,7},{4,0},{5,1},{6,2},{7,3},{8,12},{9,13},{10,... | collective-permute-start | bytes 98312 | tf_op jit(solution)/shard_map/ppermute | solution.py:29
  134.6 7.6 %collective-permute-start.42 = (bf16[16,1024]{1,0:T(8,128)(2,1)S(1)}, bf16[16,1024]{1,0:T(8,128)(2,1)S(1)}, u32[]{:S(2)}, u32[]{:S(2)}) collective-permute-start(bf16[16,1024]{1,0:T(8,128)(2,1)S(1)} %get-tuple-element.40), channel_id=1, source_target_pairs={{0,12},{1,13},{2,14},{3,15},{4,8},{5,9},{6,10},{7,11},{8,4},{9,5},... | collective-permute-start | bytes 98312 | tf_op jit(solution)/shard_map/ppermute | solution.py:29
  136.8 5.1 %collective-permute-start.43 = (bf16[16,512]{1,0:T(8,128)(2,1)S(1)}, bf16[16,512]{1,0:T(8,128)(2,1)S(1)}, u32[]{:S(2)}, u32[]{:S(2)}) collective-permute-start(bf16[16,512]{1,0:T(8,128)(2,1)S(1)} %get-tuple-element.49), channel_id=1, source_target_pairs={{16,4},{17,5},{18,6},{19,7},{20,0},{21,1},{22,2},{23,3},{24,12},{2... | collective-permute-start | bytes 49160 | tf_op jit(solution)/shard_map/ppermute | solution.py:29
  138.7 3.4 %collective-permute-start.44 = (bf16[16,512]{1,0:T(8,128)(2,1)S(1)}, bf16[16,512]{1,0:T(8,128)(2,1)S(1)}, u32[]{:S(2)}, u32[]{:S(2)}) collective-permute-start(bf16[16,512]{1,0:T(8,128)(2,1)S(1)} %get-tuple-element.50), channel_id=1, source_target_pairs={{16,0},{17,1},{18,2},{19,3},{20,4},{21,5},{22,6},{23,7},{24,8},{25... | collective-permute-start | bytes 49160 | tf_op jit(solution)/shard_map/ppermute | solution.py:29
  145.7 9.8 %copy-start = (f32[1,128,2048]{2,1,0:T(8,128)S(1)}, f32[1,128,2048]{2,1,0:T(8,128)}, u32[]{:S(2)}) copy-start(f32[1,128,2048]{2,1,0:T(8,128)} %param.8) | copy-start | bytes 3145732
  145.7 6.7 %collective-permute-start.39 = (bf16[128,512]{1,0:T(8,128)(2,1)S(1)}, bf16[128,512]{1,0:T(8,128)(2,1)S(1)}, u32[]{:S(2)}, u32[]{:S(2)}) collective-permute-start(bf16[128,512]{1,0:T(8,128)(2,1)S(1)} %get-tuple-element.33), channel_id=1, source_target_pairs={{0,1},{1,0},{2,3},{3,2},{4,5},{5,4},{6,7},{7,6},{8,9},{9,8},{10,11... | collective-permute-start | bytes 393224 | tf_op jit(solution)/shard_map/ppermute | solution.py:29
  145.8 9.6 %collective-permute-start.40 = (bf16[128,512]{1,0:T(8,128)(2,1)S(1)}, bf16[128,512]{1,0:T(8,128)(2,1)S(1)}, u32[]{:S(2)}, u32[]{:S(2)}) collective-permute-start(bf16[128,512]{1,0:T(8,128)(2,1)S(1)} %get-tuple-element.32), channel_id=1, source_target_pairs={{0,2},{1,3},{2,0},{3,1},{4,6},{5,7},{6,4},{7,5},{8,10},{9,11},{10,... | collective-permute-start | bytes 393224 | tf_op jit(solution)/shard_map/ppermute | solution.py:29
  147.6 7.8 %collective-permute-start.41 = (bf16[128,512]{1,0:T(8,128)(2,1)S(1)}, bf16[128,512]{1,0:T(8,128)(2,1)S(1)}, u32[]{:S(2)}, u32[]{:S(2)}) collective-permute-start(bf16[128,512]{1,0:T(8,128)(2,1)S(1)} %get-tuple-element.31), channel_id=1, source_target_pairs={{0,3},{1,2},{2,1},{3,0},{4,7},{5,6},{6,5},{7,4},{8,11},{9,10},{10,... | collective-permute-start | bytes 393224 | tf_op jit(solution)/shard_map/ppermute | solution.py:29
  150.5 6.6 %collective-permute-start.45 = (bf16[16,2432]{1,0:T(8,128)(2,1)S(1)}, bf16[16,2432]{1,0:T(8,128)(2,1)S(1)}, u32[]{:S(2)}, u32[]{:S(2)}) collective-permute-start(bf16[16,2432]{1,0:T(8,128)(2,1)S(1)} %get-tuple-element.36), channel_id=1, source_target_pairs={{0,1},{1,0},{2,3},{3,2},{4,5},{5,4},{6,7},{7,6},{8,9},{9,8},{10,11... | collective-permute-start | bytes 233480 | tf_op jit(solution)/shard_map/ppermute | solution.py:29
  150.6 6.5 %collective-permute-start.46 = (bf16[16,2432]{1,0:T(8,128)(2,1)S(1)}, bf16[16,2432]{1,0:T(8,128)(2,1)S(1)}, u32[]{:S(2)}, u32[]{:S(2)}) collective-permute-start(bf16[16,2432]{1,0:T(8,128)(2,1)S(1)} %get-tuple-element.37), channel_id=1, source_target_pairs={{0,2},{1,3},{2,0},{3,1},{4,6},{5,7},{6,4},{7,5},{8,10},{9,11},{10,... | collective-permute-start | bytes 233480 | tf_op jit(solution)/shard_map/ppermute | solution.py:29
  152.4 5.6 %collective-permute-start.47 = (bf16[16,2432]{1,0:T(8,128)(2,1)S(1)}, bf16[16,2432]{1,0:T(8,128)(2,1)S(1)}, u32[]{:S(2)}, u32[]{:S(2)}) collective-permute-start(bf16[16,2432]{1,0:T(8,128)(2,1)S(1)} %get-tuple-element.35), channel_id=1, source_target_pairs={{0,3},{1,2},{2,1},{3,0},{4,7},{5,6},{6,5},{7,4},{8,11},{9,10},{10,... | collective-permute-start | bytes 233480 | tf_op jit(solution)/shard_map/ppermute | solution.py:29
Sparse Core Ops, SparseCore 0:
  9.8 28.0 all-gather.8
  40.3 52.8 all-gather.4
  103.7 34.9 all-gather.6

commit v9 on v8

--- a/solution.py
+++ b/solution.py
@@ -88,15 +88,24 @@
             ]
 
 
+def outer_kernel(place, inverse, coupling, out):
+    nodes = inverse.shape[1]
+    size = nodes // PLANE
+    out[:, :nodes] = inverse[...]
+    for k in range(PLANE):
+        source = (k % SIDE) * SIDE + k // SIDE
+        out[:, nodes + k * size : nodes + (k + 1) * size] = coupling[
+            :, source * size : (source + 1) * size
+        ]
+
+
 def schur_kernel(place, *refs):
     separator, *pieces, schur, narrow = refs
-    size = schur.shape[0]
     for step in range(SIDE):
-        for k in range(SIDE):
-            columns = block_of(k * place[1] + (place[0] ^ step) * place[2], size)
-            value = separator[:, columns] - pieces[step][:, k * size : (k + 1) * size].astype(f32)
-            schur[:, columns] = value
-            narrow[:, columns] = value.astype(bf16)
+        columns = block_of(place[1] ^ step, pieces[step].shape[1])
+        value = separator[:, columns] - pieces[step][...].astype(f32)
+        schur[:, columns] = value
+        narrow[:, columns] = value.astype(bf16)
 
 
 def finish_kernel(place, narrow, weight, *refs):
@@ -119,27 +128,12 @@
         )
 
 
-def gather_groups(along_reduce):
-    groups = []
-    for p in range(PARTITIONS):
-        for k in range(SIDE):
-            if (p % 2 == 0) == along_reduce:
-                groups.append([p * PLANE + k * SIDE + x for x in range(SIDE)])
-            else:
-                groups.append([p * PLANE + y * SIDE + k for y in range(SIDE)])
-    return groups
-
-
-def gathered(array, along_reduce):
-    return lax.all_gather(
-        array, AXES, axis=0, tiled=True, axis_index_groups=gather_groups(along_reduce)
-    )
-
-
-def along_reduce(value, step):
-    return permuted(
-        value, lambda p, y, x: (p, y, x ^ step) if p % 2 == 0 else (p, y ^ step, x)
-    )
+def over_axis(array, axis):
+    if axis == "x":
+        groups = [[k * SIDE + i for i in range(SIDE)] for k in range(SIDE)]
+    else:
+        groups = [[i * SIDE + k for i in range(SIDE)] for k in range(SIDE)]
+    return lax.all_gather(array, "blk", axis=0, tiled=True, axis_index_groups=groups)
 
 
 def shards(interior_inverse, coupling, separator, link, source, weights):
@@ -155,7 +149,6 @@
     b = lax.axis_index("blk").astype(jnp.int32)
     y, x = b >> 2, b & 3
     even = (p & 1) == 0
-    r = jnp.where(even, x, y)
     pair = y >> 1
     ring = ((y + 1) >> 1) & 1
     out_place = jnp.where(even, y & 1, pair)
@@ -166,13 +159,11 @@
     away_high = jnp.where(even, 2 + ring, 3 - 2 * pair)
     place = jnp.stack([x, y])
 
-    coupling_in = gathered(coupling_rows, False)
-    turned = jnp.where(
-        even,
-        coupling_rows,
-        coupling_rows.reshape(rows, SIDE, SIDE, rows).transpose(0, 2, 1, 3).reshape(rows, nodes),
-    )
-    outer = gathered(jnp.concatenate([inverse_rows, turned], axis=1), True)
+    (outer,) = kernel_call(
+        outer_kernel, place, [inverse_rows, coupling_rows], [shape((rows, 2 * nodes), bf16)]
+    )
+    link_rows = tie(link_rows, outer)
+    outer = over_axis(outer, "y")
 
     def ordered(pieces):
         stacked = jnp.stack(pieces)
@@ -200,12 +191,13 @@
         return jnp.concatenate([part, jnp.broadcast_to(weight_row[None, :], (8, rows))], axis=0)
 
     line_values = jnp.concatenate(ordered(exchange_x(source_chunk)), axis=1)
-    keep, got, line_values = tie((keep, got, line_values), turned)
+    keep, got, line_values = tie((keep, got, line_values))
     line_weights = line_values[share : share + 1]
     two = jnp.where(
         out_place == 0, jnp.concatenate([keep, got]), jnp.concatenate([got, keep])
     )
     pieces = spread_x(two)
+    coupling_in = over_axis(tie(coupling_rows, pieces[1]), "x")
     away_weights = permuted(line_weights, lambda p, y, x: (p, partner(p, y), x))
     (block,) = kernel_call(assemble_link, place, pieces, [shape((half, half), bf16)])
     weight_half = jnp.where(
@@ -230,7 +222,7 @@
             inner = lax.dot_general(
                 outer[:, :nodes], coupling_in, (((1,), (1,)), ((), ())), preferred_element_type=f32
             ).astype(bf16)
-            inner_all = gathered(inner, False)
+            inner_all = over_axis(inner, "x")
             previous = tie(previous, inner)
         product = lax.dot_general(
             previous, block, (((1,), (1,)), ((), ())), preferred_element_type=f32
@@ -285,12 +277,12 @@
     folded = jnp.dot(outer[:, nodes:], inner_all, preferred_element_type=f32).astype(bf16)
 
     def folded_chunk(step):
-        return lax.dynamic_slice(folded, ((r ^ step) * rows, 0), (rows, line))
-
-    back_rows = [folded_chunk(0)] + [along_reduce(folded_chunk(s), s) for s in (1, 2, 3)]
+        return lax.dynamic_slice(folded, ((y ^ step) * rows, 0), (rows, line))
+
+    back_rows = [folded_chunk(0)] + [along_y(folded_chunk(step), step) for step in (1, 2, 3)]
     schur_rows, narrow = kernel_call(
         schur_kernel,
-        jnp.stack([r, jnp.where(even, SIDE, 1), jnp.where(even, 1, SIDE)]),
+        place,
         [separator_rows] + back_rows,
         [shape((rows, nodes), f32), shape((rows, nodes), bf16)],
     )

time: 167 us -> 209 us (1.25); the launches traced: 166 us -> 206 us
  waiting for transfers between devices: 78.2 us -> 119 us
  starting transfers between devices: 46.9 us -> 44.4 us
    all_gather x3, waiting for transfers between devices: 7.31 us -> 37.7 us  [over_axis(): lax.all_gather(array, 'blk', axis=0, tiled=True, axis_index_groups=groups)]
    ppermute x48, waiting for transfers between devices: 70.2 us -> 80.5 us  [permuted(): return lax.ppermute(value, AXES, pairs)]
    ppermute x48, starting transfers between devices: 46.7 us -> 44.3 us  [permuted(): return lax.ppermute(value, AXES, pairs)]
    pallas_call x4 -> x5, Pallas kernels: 4.49 us -> 6 us  [kernel_call(): pl.pallas_call(body, out_shape=out_shapes, in_specs=[pl.BlockSpec(memory_...]
  transfers between devices with their start and end apart: 51 -> 51, of which waited for: 20 -> 21; matrix products, arithmetic and copies ran while one was open for 8% -> 4% of each run, Pallas kernels for 2% -> 2%
where the time goes in v9:
time: 209 us; the launch traced here: 206 us
  waiting for transfers between devices  119 us (57%)
  starting transfers between devices  44.4 us (21%)
  matrix products  17.9 us (9%)
  between operations  14.3 us (7%)
  Pallas kernels  6 us (3%)
  local copies, waits for them, and re-layouts  2.88 us (1%)
    ppermute x48, waiting for transfers between devices, permuted(): return lax.ppermute(value, AXES, pairs)  80.5 us
    ppermute x48, starting transfers between devices, permuted(): return lax.ppermute(value, AXES, pairs)  44.3 us
    all_gather x3, waiting for transfers between devices, over_axis(): lax.all_gather(array, 'blk', axis=0, tiled=True, axis_index_groups=groups)  37.7 us
    dot_general x15, matrix products, shards(): lax.dot_general(previous, block, (((1,), (1,)), ((), ())), preferred_elem...  9.76 us
    pallas_call x5, Pallas kernels, kernel_call(): pl.pallas_call(body, out_shape=out_shapes, in_specs=[pl.BlockSpec(memory_...  6 us
    dot_general x1, matrix products, shards(): lax.dot_general(outer[:, :nodes], coupling_in, (((1,), (1,)), ((), ())),...  4.3 us
  transfers between devices with their start and end apart: 51, of which 21 were waited for; matrix products, arithmetic and copies ran while one was open for 4% of the time, Pallas kernels for 2%

profile of v9, /device:TPU:224, one launch (start us, length us, event | category | flops | bytes accessed | tf_op | source)
XLA Modules:
  0.0 205.6 jit_solution(4950967155143773743)
XLA Ops:
  7.2 0.8 bitcast_multiply_fusion
  8.0 0.7 broadcast_in_dim.8
  8.7 1.5 collective-permute-start.1
  10.2 2.7 %collective-permute-start.2 = (f32[24,128]{1,0:T(8,128)S(1)}, f32[24,128]{1,0:T(8,128)S(1)}, u32[]{:S(2)}, u32[]{:S(2)}) collective-permute-start(f32[24,128]{1,0:T(8,128)S(1)} %get-tuple-element.73), channel_id=1, source_target_pairs={{0,2},{1,3},{2,0},{3,1},{4,6},{5,7},{6,4},{7,5},{8,10},{9,11},{10,... | collective-permute-start | bytes 36872 | tf_op jit(solution)/shard_map/ppermute | solution.py:29
  13.5 1.0 copy-done
  14.6 1.0 copy-done.2
  15.6 1.6 shard_map.85
  17.9 1.7 collective-permute-start
  19.6 4.7 %collective-permute-done = bf16[128,1024]{1,0:T(8,128)(2,1)S(1)} collective-permute-done((bf16[128,1024]{1,0:T(8,128)(2,1)S(1)}, bf16[128,1024]{1,0:T(8,128)(2,1)S(1)}, u32[]{:S(2)}, u32[]{:S(2)}) %collective-permute-start) | collective-permute-done | bytes 262176 | tf_op jit(solution)/shard_map/ppermute | solution.py:29
  24.8 12.7 %collective-permute-done.4.refs_1_ = bf16[256,1024]{1,0:T(8,128)(2,1)S(1)} collective-permute-done((bf16[256,1024]{1,0:T(8,128)(2,1)S(1)}, bf16[256,1024]{1,0:T(8,128)(2,1)S(1)}, u32[]{:S(2)}, u32[]{:S(2)}) %collective-permute-start.4) | collective-permute-done | bytes 524320 | tf_op jit(solution)/shard_map/ppermute | solution.py:29
  37.6 0.7 all-gather.4.cloned.1.call-update
  38.3 2.6 %collective-permute-start.8 = (bf16[256,1024]{1,0:T(8,128)(2,1)S(1)}, bf16[256,1024]{1,0:T(8,128)(2,1)S(1)}, u32[]{:S(2)}, u32[]{:S(2)}) collective-permute-start(bf16[256,1024]{1,0:T(8,128)(2,1)S(1)} %maximum_select_fusion.refs_0_), channel_id=1, source_target_pairs={{0,2},{1,3},{2,0},{3,1},{4,6},{5,7},{6,4},{7,5},{8,10},{9,11},{10,... | collective-permute-start | bytes 1572872 | tf_op jit(solution)/shard_map/ppermute | solution.py:29
  42.0 1.5 collective-permute-start.7
  43.5 1.4 collective-permute-done.5
  44.9 7.1 %collective-permute-done.8.refs_2_ = bf16[256,1024]{1,0:T(8,128)(2,1)S(1)} collective-permute-done((bf16[256,1024]{1,0:T(8,128)(2,1)S(1)}, bf16[256,1024]{1,0:T(8,128)(2,1)S(1)}, u32[]{:S(2)}, u32[]{:S(2)}) %collective-permute-start.8) | collective-permute-done | bytes 524320 | tf_op jit(solution)/shard_map/ppermute | solution.py:29
  52.0 21.2 %collective-permute-done.9.refs_3_ = bf16[256,1024]{1,0:T(8,128)(2,1)S(1)} collective-permute-done((bf16[256,1024]{1,0:T(8,128)(2,1)S(1)}, bf16[256,1024]{1,0:T(8,128)(2,1)S(1)}, u32[]{:S(2)}, u32[]{:S(2)}) %collective-permute-start.9) | collective-permute-done | bytes 524320 | tf_op jit(solution)/shard_map/ppermute | solution.py:29
  73.3 0.7 shard_map.87
  74.6 0.7 collective-permute-start.10
  75.3 0.7 collective-permute-start.11
  76.0 0.7 fusion.26
  76.7 3.2 %collective-permute-done.12 = bf16[16,1024]{1,0:T(8,128)(2,1)S(1)} collective-permute-done((bf16[16,1024]{1,0:T(8,128)(2,1)S(1)}, bf16[16,1024]{1,0:T(8,128)(2,1)S(1)}, u32[]{:S(2)}, u32[]{:S(2)}) %collective-permute-start.12) | collective-permute-done | bytes 32800 | tf_op jit(solution)/shard_map/ppermute | solution.py:29
  80.6 0.7 collective-permute-start.14
  81.3 0.7 collective-permute-start.15
  82.0 0.7 fusion.28
  82.8 3.4 %collective-permute-done.16 = bf16[16,1024]{1,0:T(8,128)(2,1)S(1)} collective-permute-done((bf16[16,1024]{1,0:T(8,128)(2,1)S(1)}, bf16[16,1024]{1,0:T(8,128)(2,1)S(1)}, u32[]{:S(2)}, u32[]{:S(2)}) %collective-permute-start.16) | collective-permute-done | bytes 32800 | tf_op jit(solution)/shard_map/ppermute | solution.py:29
  86.8 0.7 collective-permute-start.18
  87.5 0.7 collective-permute-start.19
  88.2 0.7 fusion.30
  89.1 3.5 %collective-permute-done.20 = bf16[16,1024]{1,0:T(8,128)(2,1)S(1)} collective-permute-done((bf16[16,1024]{1,0:T(8,128)(2,1)S(1)}, bf16[16,1024]{1,0:T(8,128)(2,1)S(1)}, u32[]{:S(2)}, u32[]{:S(2)}) %collective-permute-start.20) | collective-permute-done | bytes 32800 | tf_op jit(solution)/shard_map/ppermute | solution.py:29
  93.2 0.7 collective-permute-start.22
  93.9 0.7 collective-permute-start.23
  94.6 0.7 fusion.32
  95.5 3.2 %collective-permute-done.24 = bf16[16,1024]{1,0:T(8,128)(2,1)S(1)} collective-permute-done((bf16[16,1024]{1,0:T(8,128)(2,1)S(1)}, bf16[16,1024]{1,0:T(8,128)(2,1)S(1)}, u32[]{:S(2)}, u32[]{:S(2)}) %collective-permute-start.24) | collective-permute-done | bytes 32800 | tf_op jit(solution)/shard_map/ppermute | solution.py:29
  99.3 0.7 collective-permute-start.26
  100.0 0.7 collective-permute-start.27
  100.7 32.6 %all-gather.4.cloned.1.call-done = bf16[512,4096]{1,0:T(8,128)(2,1)} async-done(((bf16[128,4096]{1,0:T(8,128)(2,1)}), bf16[512,4096]{1,0:T(8,128)(2,1)}) %all-gather.4.cloned.1.call-update) | async-done | bytes 4194320 | tf_op jit(solution)/shard_map/all_gather | solution.py:136
  133.3 4.3 %fusion.7 = bf16[512,512]{1,0:T(8,128)(2,1)} fusion(bf16[512,2048]{1,0:T(8,128)(2,1)} %all-gather.6.cloned.1.call-done, bf16[512,4096]{1,0:T(8,128)(2,1)} %all-gather.4.cloned.1.call-done), kind=kOutput, calls=%fused_computation.5 | convolution fusion | flops 1074003968 | bytes 4718592 | tf_op jit(solution)/shard_map/dot_general | solution.py:222
  138.5 0.7 collective-permute-start.29
  139.2 2.7 %collective-permute-done.28 = bf16[16,1024]{1,0:T(8,128)(2,1)S(1)} collective-permute-done((bf16[16,1024]{1,0:T(8,128)(2,1)S(1)}, bf16[16,1024]{1,0:T(8,128)(2,1)S(1)}, u32[]{:S(2)}, u32[]{:S(2)}) %collective-permute-start.28) | collective-permute-done | bytes 32800 | tf_op jit(solution)/shard_map/ppermute | solution.py:29
  142.6 0.7 collective-permute-start.30
  143.3 0.7 collective-permute-start.31
  145.6 2.4 %collective-permute-done.32 = bf16[16,1024]{1,0:T(8,128)(2,1)S(1)} collective-permute-done((bf16[16,1024]{1,0:T(8,128)(2,1)S(1)}, bf16[16,1024]{1,0:T(8,128)(2,1)S(1)}, u32[]{:S(2)}, u32[]{:S(2)}) %collective-permute-start.32) | collective-permute-done | bytes 32800 | tf_op jit(solution)/shard_map/ppermute | solution.py:29
  148.7 1.3 collective-permute-start.34
  150.0 1.3 collective-permute-start.35
  151.3 7.1 %collective-permute-done.34 = bf16[16,1024]{1,0:T(8,128)(2,1)S(1)} collective-permute-done((bf16[16,1024]{1,0:T(8,128)(2,1)S(1)}, bf16[16,1024]{1,0:T(8,128)(2,1)S(1)}, u32[]{:S(2)}, u32[]{:S(2)}) %collective-permute-start.34) | collective-permute-done | bytes 32800 | tf_op jit(solution)/shard_map/ppermute | solution.py:29
  159.4 2.1 %collective-permute-start.37 = (bf16[16,1024]{1,0:T(8,128)(2,1)S(1)}, bf16[16,1024]{1,0:T(8,128)(2,1)S(1)}, u32[]{:S(2)}, u32[]{:S(2)}) collective-permute-start(bf16[16,1024]{1,0:T(8,128)(2,1)S(1)} %fusion.38), channel_id=1, source_target_pairs={{0,16},{1,17},{2,18},{3,19},{4,20},{5,21},{6,22},{7,23},{8,24},{9,... | collective-permute-start | bytes 98312 | tf_op jit(solution)/shard_map/ppermute | solution.py:29
  161.5 1.2 collective-permute-done.36
  162.8 0.7 fusion.40
  163.4 2.0 collective-permute-start.38
  165.4 1.9 collective-permute-done.38
  167.4 1.8 collective-permute-start.42
  169.5 1.9 collective-permute-start.43
  171.4 1.9 collective-permute-start.44
  173.4 1.1 collective-permute-done.43
  174.8 5.1 %all-gather.8.cloned.1.call-done = bf16[2048,512]{1,0:T(8,128)(2,1)} async-done(((bf16[512,512]{1,0:T(8,128)(2,1)}), bf16[2048,512]{1,0:T(8,128)(2,1)}) %all-gather.8.cloned.1.call-update) | async-done | bytes 2097168 | tf_op jit(solution)/shard_map/all_gather | solution.py:136
  179.9 3.5 %fusion.4 = bf16[512,512]{1,0:T(8,128)(2,1)S(1)} fusion(bf16[2048,512]{1,0:T(8,128)(2,1)} %all-gather.8.cloned.1.call-done, bf16[512,4096]{1,0:T(8,128)(2,1)} %all-gather.4.cloned.1.call-done), kind=kOutput, calls=%fused_computation.4 | convolution fusion | flops 1074003968 | bytes 4718592 | tf_op jit(solution)/shard_map/dot_general | solution.py:277
  183.5 1.6 collective-permute-start.39
  185.0 2.7 %collective-permute-start.40 = (bf16[128,512]{1,0:T(8,128)(2,1)S(1)}, bf16[128,512]{1,0:T(8,128)(2,1)S(1)}, u32[]{:S(2)}, u32[]{:S(2)}) collective-permute-start(bf16[128,512]{1,0:T(8,128)(2,1)S(1)} %get-tuple-element.36), channel_id=1, source_target_pairs={{0,8},{1,9},{2,10},{3,11},{4,12},{5,13},{6,14},{7,15},{8,0},{9,1},... | collective-permute-start | bytes 393224 | tf_op jit(solution)/shard_map/ppermute | solution.py:29
  188.9 1.8 collective-permute-start.46
  190.7 2.4 %collective-permute-start.47 = (bf16[16,2432]{1,0:T(8,128)(2,1)S(1)}, bf16[16,2432]{1,0:T(8,128)(2,1)S(1)}, u32[]{:S(2)}, u32[]{:S(2)}) collective-permute-start(bf16[16,2432]{1,0:T(8,128)(2,1)S(1)} %get-tuple-element.39), channel_id=1, source_target_pairs={{0,3},{1,2},{2,1},{3,0},{4,7},{5,6},{6,5},{7,4},{8,11},{9,10},{10,... | collective-permute-start | bytes 233480 | tf_op jit(solution)/shard_map/ppermute | solution.py:29
  193.1 0.8 collective-permute-done.40.refs_3_
  193.9 2.1 %collective-permute-done.41.refs_4_ = bf16[128,512]{1,0:T(8,128)(2,1)S(1)} collective-permute-done((bf16[128,512]{1,0:T(8,128)(2,1)S(1)}, bf16[128,512]{1,0:T(8,128)(2,1)S(1)}, u32[]{:S(2)}, u32[]{:S(2)}) %collective-permute-start.41) | collective-permute-done | bytes 131104 | tf_op jit(solution)/shard_map/ppermute | solution.py:29
  195.9 1.6 shard_map.88
  197.6 1.5 shard_map.89
  (100 shorter events, 13.8 us)
Async XLA Ops:
  7.2 93.6 %all-gather.6.cloned.1.call-start = ((), (), s32[]{:S(2)}) async-start(), calls=%async_computation.1 | async-start | bytes 2621440 | tf_op jit(solution)/shard_map/all_gather | solution.py:136
  8.7 10.8 %collective-permute-start.1 = (f32[24,128]{1,0:T(8,128)S(1)}, f32[24,128]{1,0:T(8,128)S(1)}, u32[]{:S(2)}, u32[]{:S(2)}) collective-permute-start(f32[24,128]{1,0:T(8,128)S(1)} %get-tuple-element.72), channel_id=1, source_target_pairs={{0,1},{1,0},{2,3},{3,2},{4,5},{5,4},{6,7},{7,6},{8,9},{9,8},{10,11... | collective-permute-start | bytes 36872 | tf_op jit(solution)/shard_map/ppermute | solution.py:29
  10.2 9.4 %collective-permute-start.2 = (f32[24,128]{1,0:T(8,128)S(1)}, f32[24,128]{1,0:T(8,128)S(1)}, u32[]{:S(2)}, u32[]{:S(2)}) collective-permute-start(f32[24,128]{1,0:T(8,128)S(1)} %get-tuple-element.73), channel_id=1, source_target_pairs={{0,2},{1,3},{2,0},{3,1},{4,6},{5,7},{6,4},{7,5},{8,10},{9,11},{10,... | collective-permute-start | bytes 36872 | tf_op jit(solution)/shard_map/ppermute | solution.py:29
  12.9 6.6 %collective-permute-start.3 = (f32[24,128]{1,0:T(8,128)S(1)}, f32[24,128]{1,0:T(8,128)S(1)}, u32[]{:S(2)}, u32[]{:S(2)}) collective-permute-start(f32[24,128]{1,0:T(8,128)S(1)} %get-tuple-element.74), channel_id=1, source_target_pairs={{0,3},{1,2},{2,1},{3,0},{4,7},{5,6},{6,5},{7,4},{8,11},{9,10},{10,... | collective-permute-start | bytes 36872 | tf_op jit(solution)/shard_map/ppermute | solution.py:29
  13.5 1.0 copy-start
  14.6 1.0 copy-start.2
  15.6 1.6 copy-start.3
  17.9 6.5 %collective-permute-start = (bf16[128,1024]{1,0:T(8,128)(2,1)S(1)}, bf16[128,1024]{1,0:T(8,128)(2,1)S(1)}, u32[]{:S(2)}, u32[]{:S(2)}) collective-permute-start(bf16[128,1024]{1,0:T(8,128)(2,1)S(1)} %get-tuple-element.20), channel_id=1, source_target_pairs={{0,4},{1,5},{2,6},{3,7},{4,0},{5,1},{6,2},{7,3},{8,12},{9,13},{10,... | collective-permute-start | bytes 786440 | tf_op jit(solution)/shard_map/ppermute | solution.py:29
  24.4 13.0 %collective-permute-start.4 = (bf16[256,1024]{1,0:T(8,128)(2,1)S(1)}, bf16[256,1024]{1,0:T(8,128)(2,1)S(1)}, u32[]{:S(2)}, u32[]{:S(2)}) collective-permute-start(bf16[256,1024]{1,0:T(8,128)(2,1)S(1)} %maximum_select_fusion.refs_0_), channel_id=1, source_target_pairs={{0,1},{1,0},{2,3},{3,2},{4,5},{5,4},{6,7},{7,6},{8,9},{9,8},{10,11... | collective-permute-start | bytes 1572872 | tf_op jit(solution)/shard_map/ppermute | solution.py:29
  37.5 95.8 %all-gather.4.cloned.1.call-start = ((), (), s32[]{:S(2)}) async-start(), calls=%async_computation | async-start | bytes 5242880 | tf_op jit(solution)/shard_map/all_gather | solution.py:136
  38.3 141.7 %all-gather.8.cloned.1.call-start = ((), (), s32[]{:S(2)}) async-start(), calls=%async_computation.2 | async-start | bytes 2621440 | tf_op jit(solution)/shard_map/all_gather | solution.py:136
  38.3 13.7 %collective-permute-start.8 = (bf16[256,1024]{1,0:T(8,128)(2,1)S(1)}, bf16[256,1024]{1,0:T(8,128)(2,1)S(1)}, u32[]{:S(2)}, u32[]{:S(2)}) collective-permute-start(bf16[256,1024]{1,0:T(8,128)(2,1)S(1)} %maximum_select_fusion.refs_0_), channel_id=1, source_target_pairs={{0,2},{1,3},{2,0},{3,1},{4,6},{5,7},{6,4},{7,5},{8,10},{9,11},{10,... | collective-permute-start | bytes 1572872 | tf_op jit(solution)/shard_map/ppermute | solution.py:29
  40.9 32.4 %collective-permute-start.9 = (bf16[256,1024]{1,0:T(8,128)(2,1)S(1)}, bf16[256,1024]{1,0:T(8,128)(2,1)S(1)}, u32[]{:S(2)}, u32[]{:S(2)}) collective-permute-start(bf16[256,1024]{1,0:T(8,128)(2,1)S(1)} %maximum_select_fusion.refs_0_), channel_id=1, source_target_pairs={{0,3},{1,2},{2,1},{3,0},{4,7},{5,6},{6,5},{7,4},{8,11},{9,10},{10,... | collective-permute-start | bytes 1572872 | tf_op jit(solution)/shard_map/ppermute | solution.py:29
  41.4 3.6 %collective-permute-start.5 = (f32[1,512]{1,0:T(1,128)S(1)}, f32[1,512]{1,0:T(1,128)S(1)}, u32[]{:S(2)}, u32[]{:S(2)}) collective-permute-start(f32[1,512]{1,0:T(1,128)S(1)} %slice.32), channel_id=1, source_target_pairs={{0,4},{1,5},{2,6},{3,7},{4,0},{5,1},{6,2},{7,3},{8,12},{9,13},{10,... | collective-permute-start | bytes 6152 | tf_op jit(solution)/shard_map/ppermute | solution.py:29
  42.0 32.0 %collective-permute-start.6 = (bf16[16,1024]{1,0:T(8,128)(2,1)S(1)}, bf16[16,1024]{1,0:T(8,128)(2,1)S(1)}, u32[]{:S(2)}, u32[]{:S(2)}) collective-permute-start(bf16[16,1024]{1,0:T(8,128)(2,1)S(1)} %fusion.42), channel_id=1, source_target_pairs={{0,20},{1,21},{2,22},{3,23},{4,16},{5,17},{6,18},{7,19},{8,28},{9,... | collective-permute-start | bytes 98312 | tf_op jit(solution)/shard_map/ppermute | solution.py:29
  42.0 32.0 %collective-permute-start.7 = (bf16[16,1024]{1,0:T(8,128)(2,1)S(1)}, bf16[16,1024]{1,0:T(8,128)(2,1)S(1)}, u32[]{:S(2)}, u32[]{:S(2)}) collective-permute-start(bf16[16,1024]{1,0:T(8,128)(2,1)S(1)} %fusion.42), channel_id=1, source_target_pairs={{0,16},{1,17},{2,18},{3,19},{4,20},{5,21},{6,22},{7,23},{8,24},{9,... | collective-permute-start | bytes 98312 | tf_op jit(solution)/shard_map/ppermute | solution.py:29
  74.6 1.3 collective-permute-start.10
  75.3 0.7 collective-permute-start.11
  76.6 3.3 %collective-permute-start.12 = (bf16[16,1024]{1,0:T(8,128)(2,1)S(1)}, bf16[16,1024]{1,0:T(8,128)(2,1)S(1)}, u32[]{:S(2)}, u32[]{:S(2)}) collective-permute-start(bf16[16,1024]{1,0:T(8,128)(2,1)S(1)} %fusion.26), channel_id=1, source_target_pairs={{0,20},{1,21},{2,22},{3,23},{4,16},{5,17},{6,18},{7,19},{8,28},{9,... | collective-permute-start | bytes 98312 | tf_op jit(solution)/shard_map/ppermute | solution.py:29
  76.6 3.3 %collective-permute-start.13 = (bf16[16,1024]{1,0:T(8,128)(2,1)S(1)}, bf16[16,1024]{1,0:T(8,128)(2,1)S(1)}, u32[]{:S(2)}, u32[]{:S(2)}) collective-permute-start(bf16[16,1024]{1,0:T(8,128)(2,1)S(1)} %fusion.26), channel_id=1, source_target_pairs={{0,16},{1,17},{2,18},{3,19},{4,20},{5,21},{6,22},{7,23},{8,24},{9,... | collective-permute-start | bytes 98312 | tf_op jit(solution)/shard_map/ppermute | solution.py:29
  80.6 1.3 collective-permute-start.14
  81.3 0.7 collective-permute-start.15
  82.6 3.5 %collective-permute-start.16 = (bf16[16,1024]{1,0:T(8,128)(2,1)S(1)}, bf16[16,1024]{1,0:T(8,128)(2,1)S(1)}, u32[]{:S(2)}, u32[]{:S(2)}) collective-permute-start(bf16[16,1024]{1,0:T(8,128)(2,1)S(1)} %fusion.28), channel_id=1, source_target_pairs={{0,20},{1,21},{2,22},{3,23},{4,16},{5,17},{6,18},{7,19},{8,28},{9,... | collective-permute-start | bytes 98312 | tf_op jit(solution)/shard_map/ppermute | solution.py:29
  82.6 3.5 %collective-permute-start.17 = (bf16[16,1024]{1,0:T(8,128)(2,1)S(1)}, bf16[16,1024]{1,0:T(8,128)(2,1)S(1)}, u32[]{:S(2)}, u32[]{:S(2)}) collective-permute-start(bf16[16,1024]{1,0:T(8,128)(2,1)S(1)} %fusion.28), channel_id=1, source_target_pairs={{0,16},{1,17},{2,18},{3,19},{4,20},{5,21},{6,22},{7,23},{8,24},{9,... | collective-permute-start | bytes 98312 | tf_op jit(solution)/shard_map/ppermute | solution.py:29
  86.8 1.3 collective-permute-start.18
  87.5 0.7 collective-permute-start.19
  88.8 3.7 %collective-permute-start.20 = (bf16[16,1024]{1,0:T(8,128)(2,1)S(1)}, bf16[16,1024]{1,0:T(8,128)(2,1)S(1)}, u32[]{:S(2)}, u32[]{:S(2)}) collective-permute-start(bf16[16,1024]{1,0:T(8,128)(2,1)S(1)} %fusion.30), channel_id=1, source_target_pairs={{0,20},{1,21},{2,22},{3,23},{4,16},{5,17},{6,18},{7,19},{8,28},{9,... | collective-permute-start | bytes 98312 | tf_op jit(solution)/shard_map/ppermute | solution.py:29
  89.0 3.6 %collective-permute-start.21 = (bf16[16,1024]{1,0:T(8,128)(2,1)S(1)}, bf16[16,1024]{1,0:T(8,128)(2,1)S(1)}, u32[]{:S(2)}, u32[]{:S(2)}) collective-permute-start(bf16[16,1024]{1,0:T(8,128)(2,1)S(1)} %fusion.30), channel_id=1, source_target_pairs={{0,16},{1,17},{2,18},{3,19},{4,20},{5,21},{6,22},{7,23},{8,24},{9,... | collective-permute-start | bytes 98312 | tf_op jit(solution)/shard_map/ppermute | solution.py:29
  93.2 1.3 collective-permute-start.22
  93.9 0.7 collective-permute-start.23
  95.2 3.4 %collective-permute-start.24 = (bf16[16,1024]{1,0:T(8,128)(2,1)S(1)}, bf16[16,1024]{1,0:T(8,128)(2,1)S(1)}, u32[]{:S(2)}, u32[]{:S(2)}) collective-permute-start(bf16[16,1024]{1,0:T(8,128)(2,1)S(1)} %fusion.32), channel_id=1, source_target_pairs={{0,20},{1,21},{2,22},{3,23},{4,16},{5,17},{6,18},{7,19},{8,28},{9,... | collective-permute-start | bytes 98312 | tf_op jit(solution)/shard_map/ppermute | solution.py:29
  95.2 3.4 %collective-permute-start.25 = (bf16[16,1024]{1,0:T(8,128)(2,1)S(1)}, bf16[16,1024]{1,0:T(8,128)(2,1)S(1)}, u32[]{:S(2)}, u32[]{:S(2)}) collective-permute-start(bf16[16,1024]{1,0:T(8,128)(2,1)S(1)} %fusion.32), channel_id=1, source_target_pairs={{0,16},{1,17},{2,18},{3,19},{4,20},{5,21},{6,22},{7,23},{8,24},{9,... | collective-permute-start | bytes 98312 | tf_op jit(solution)/shard_map/ppermute | solution.py:29
  99.3 1.3 collective-permute-start.26
  100.0 0.7 collective-permute-start.27
  138.3 3.7 %collective-permute-start.28 = (bf16[16,1024]{1,0:T(8,128)(2,1)S(1)}, bf16[16,1024]{1,0:T(8,128)(2,1)S(1)}, u32[]{:S(2)}, u32[]{:S(2)}) collective-permute-start(bf16[16,1024]{1,0:T(8,128)(2,1)S(1)} %fusion.34), channel_id=1, source_target_pairs={{0,20},{1,21},{2,22},{3,23},{4,16},{5,17},{6,18},{7,19},{8,28},{9,... | collective-permute-start | bytes 98312 | tf_op jit(solution)/shard_map/ppermute | solution.py:29
  138.5 3.4 %collective-permute-start.29 = (bf16[16,1024]{1,0:T(8,128)(2,1)S(1)}, bf16[16,1024]{1,0:T(8,128)(2,1)S(1)}, u32[]{:S(2)}, u32[]{:S(2)}) collective-permute-start(bf16[16,1024]{1,0:T(8,128)(2,1)S(1)} %fusion.34), channel_id=1, source_target_pairs={{0,16},{1,17},{2,18},{3,19},{4,20},{5,21},{6,22},{7,23},{8,24},{9,... | collective-permute-start | bytes 98312 | tf_op jit(solution)/shard_map/ppermute | solution.py:29
  142.6 1.4 collective-permute-start.30
  143.3 0.7 collective-permute-start.31
  144.6 3.4 %collective-permute-start.32 = (bf16[16,1024]{1,0:T(8,128)(2,1)S(1)}, bf16[16,1024]{1,0:T(8,128)(2,1)S(1)}, u32[]{:S(2)}, u32[]{:S(2)}) collective-permute-start(bf16[16,1024]{1,0:T(8,128)(2,1)S(1)} %fusion.36), channel_id=1, source_target_pairs={{0,20},{1,21},{2,22},{3,23},{4,16},{5,17},{6,18},{7,19},{8,28},{9,... | collective-permute-start | bytes 98312 | tf_op jit(solution)/shard_map/ppermute | solution.py:29
  145.2 2.8 %collective-permute-start.33 = (bf16[16,1024]{1,0:T(8,128)(2,1)S(1)}, bf16[16,1024]{1,0:T(8,128)(2,1)S(1)}, u32[]{:S(2)}, u32[]{:S(2)}) collective-permute-start(bf16[16,1024]{1,0:T(8,128)(2,1)S(1)} %fusion.36), channel_id=1, source_target_pairs={{0,16},{1,17},{2,18},{3,19},{4,20},{5,21},{6,22},{7,23},{8,24},{9,... | collective-permute-start | bytes 98312 | tf_op jit(solution)/shard_map/ppermute | solution.py:29
  148.7 9.7 %collective-permute-start.34 = (bf16[16,1024]{1,0:T(8,128)(2,1)S(1)}, bf16[16,1024]{1,0:T(8,128)(2,1)S(1)}, u32[]{:S(2)}, u32[]{:S(2)}) collective-permute-start(bf16[16,1024]{1,0:T(8,128)(2,1)S(1)} %fusion.37), channel_id=1, source_target_pairs={{208,236},{209,237},{210,238},{211,239},{212,232},{213,233},{214,2... | collective-permute-start | bytes 98312 | tf_op jit(solution)/shard_map/ppermute | solution.py:29
  150.0 8.8 %collective-permute-start.35 = (bf16[16,1024]{1,0:T(8,128)(2,1)S(1)}, bf16[16,1024]{1,0:T(8,128)(2,1)S(1)}, u32[]{:S(2)}, u32[]{:S(2)}) collective-permute-start(bf16[16,1024]{1,0:T(8,128)(2,1)S(1)} %fusion.37), channel_id=1, source_target_pairs={{208,224},{209,225},{210,226},{211,227},{212,228},{213,229},{214,2... | collective-permute-start | bytes 98312 | tf_op jit(solution)/shard_map/ppermute | solution.py:29
  159.4 3.3 %collective-permute-start.36 = (bf16[16,1024]{1,0:T(8,128)(2,1)S(1)}, bf16[16,1024]{1,0:T(8,128)(2,1)S(1)}, u32[]{:S(2)}, u32[]{:S(2)}) collective-permute-start(bf16[16,1024]{1,0:T(8,128)(2,1)S(1)} %fusion.38), channel_id=1, source_target_pairs={{0,20},{1,21},{2,22},{3,23},{4,16},{5,17},{6,18},{7,19},{8,28},{9,... | collective-permute-start | bytes 98312 | tf_op jit(solution)/shard_map/ppermute | solution.py:29
  159.4 3.3 %collective-permute-start.37 = (bf16[16,1024]{1,0:T(8,128)(2,1)S(1)}, bf16[16,1024]{1,0:T(8,128)(2,1)S(1)}, u32[]{:S(2)}, u32[]{:S(2)}) collective-permute-start(bf16[16,1024]{1,0:T(8,128)(2,1)S(1)} %fusion.38), channel_id=1, source_target_pairs={{0,16},{1,17},{2,18},{3,19},{4,20},{5,21},{6,22},{7,23},{8,24},{9,... | collective-permute-start | bytes 98312 | tf_op jit(solution)/shard_map/ppermute | solution.py:29
  163.4 3.9 %collective-permute-start.38 = (bf16[16,1024]{1,0:T(8,128)(2,1)S(1)}, bf16[16,1024]{1,0:T(8,128)(2,1)S(1)}, u32[]{:S(2)}, u32[]{:S(2)}) collective-permute-start(bf16[16,1024]{1,0:T(8,128)(2,1)S(1)} %fusion.40), channel_id=1, source_target_pairs={{0,4},{1,5},{2,6},{3,7},{4,0},{5,1},{6,2},{7,3},{8,12},{9,13},{10,... | collective-permute-start | bytes 98312 | tf_op jit(solution)/shard_map/ppermute | solution.py:29
  167.4 7.4 %collective-permute-start.42 = (bf16[16,1024]{1,0:T(8,128)(2,1)S(1)}, bf16[16,1024]{1,0:T(8,128)(2,1)S(1)}, u32[]{:S(2)}, u32[]{:S(2)}) collective-permute-start(bf16[16,1024]{1,0:T(8,128)(2,1)S(1)} %get-tuple-element.44), channel_id=1, source_target_pairs={{0,12},{1,13},{2,14},{3,15},{4,8},{5,9},{6,10},{7,11},{8,4},{9,5},... | collective-permute-start | bytes 98312 | tf_op jit(solution)/shard_map/ppermute | solution.py:29
  169.5 5.1 %collective-permute-start.43 = (bf16[16,512]{1,0:T(8,128)(2,1)S(1)}, bf16[16,512]{1,0:T(8,128)(2,1)S(1)}, u32[]{:S(2)}, u32[]{:S(2)}) collective-permute-start(bf16[16,512]{1,0:T(8,128)(2,1)S(1)} %get-tuple-element.53), channel_id=1, source_target_pairs={{16,4},{17,5},{18,6},{19,7},{20,0},{21,1},{22,2},{23,3},{24,12},{2... | collective-permute-start | bytes 49160 | tf_op jit(solution)/shard_map/ppermute | solution.py:29
  171.4 3.4 %collective-permute-start.44 = (bf16[16,512]{1,0:T(8,128)(2,1)S(1)}, bf16[16,512]{1,0:T(8,128)(2,1)S(1)}, u32[]{:S(2)}, u32[]{:S(2)}) collective-permute-start(bf16[16,512]{1,0:T(8,128)(2,1)S(1)} %get-tuple-element.54), channel_id=1, source_target_pairs={{16,0},{17,1},{18,2},{19,3},{20,4},{21,5},{22,6},{23,7},{24,8},{25... | collective-permute-start | bytes 49160 | tf_op jit(solution)/shard_map/ppermute | solution.py:29
  183.4 12.6 %copy-start.1 = (f32[1,128,2048]{2,1,0:T(8,128)S(1)}, f32[1,128,2048]{2,1,0:T(8,128)}, u32[]{:S(2)}) copy-start(f32[1,128,2048]{2,1,0:T(8,128)} %param.8) | copy-start | bytes 3145732
  183.4 14.2 %copy-start.4 = (f32[1,128]{1,0:T(1,128)S(1)}, f32[1,128]{1,0:T(1,128)}, u32[]{:S(2)}) copy-start(f32[1,128]{1,0:T(1,128)} %weight.1) | copy-start | bytes 1540
  183.5 7.2 %collective-permute-start.39 = (bf16[128,512]{1,0:T(8,128)(2,1)S(1)}, bf16[128,512]{1,0:T(8,128)(2,1)S(1)}, u32[]{:S(2)}, u32[]{:S(2)}) collective-permute-start(bf16[128,512]{1,0:T(8,128)(2,1)S(1)} %get-tuple-element.37), channel_id=1, source_target_pairs={{0,4},{1,5},{2,6},{3,7},{4,0},{5,1},{6,2},{7,3},{8,12},{9,13},{10,... | collective-permute-start | bytes 393224 | tf_op jit(solution)/shard_map/ppermute | solution.py:29
  185.0 8.8 %collective-permute-start.40 = (bf16[128,512]{1,0:T(8,128)(2,1)S(1)}, bf16[128,512]{1,0:T(8,128)(2,1)S(1)}, u32[]{:S(2)}, u32[]{:S(2)}) collective-permute-start(bf16[128,512]{1,0:T(8,128)(2,1)S(1)} %get-tuple-element.36), channel_id=1, source_target_pairs={{0,8},{1,9},{2,10},{3,11},{4,12},{5,13},{6,14},{7,15},{8,0},{9,1},... | collective-permute-start | bytes 393224 | tf_op jit(solution)/shard_map/ppermute | solution.py:29
  187.8 8.2 %collective-permute-start.41 = (bf16[128,512]{1,0:T(8,128)(2,1)S(1)}, bf16[128,512]{1,0:T(8,128)(2,1)S(1)}, u32[]{:S(2)}, u32[]{:S(2)}) collective-permute-start(bf16[128,512]{1,0:T(8,128)(2,1)S(1)} %get-tuple-element.35), channel_id=1, source_target_pairs={{0,12},{1,13},{2,14},{3,15},{4,8},{5,9},{6,10},{7,11},{8,4},{9,5},... | collective-permute-start | bytes 393224 | tf_op jit(solution)/shard_map/ppermute | solution.py:29
  188.3 9.3 %collective-permute-start.45 = (bf16[16,2432]{1,0:T(8,128)(2,1)S(1)}, bf16[16,2432]{1,0:T(8,128)(2,1)S(1)}, u32[]{:S(2)}, u32[]{:S(2)}) collective-permute-start(bf16[16,2432]{1,0:T(8,128)(2,1)S(1)} %get-tuple-element.40), channel_id=1, source_target_pairs={{0,1},{1,0},{2,3},{3,2},{4,5},{5,4},{6,7},{7,6},{8,9},{9,8},{10,11... | collective-permute-start | bytes 233480 | tf_op jit(solution)/shard_map/ppermute | solution.py:29
  188.9 8.7 %collective-permute-start.46 = (bf16[16,2432]{1,0:T(8,128)(2,1)S(1)}, bf16[16,2432]{1,0:T(8,128)(2,1)S(1)}, u32[]{:S(2)}, u32[]{:S(2)}) collective-permute-start(bf16[16,2432]{1,0:T(8,128)(2,1)S(1)} %get-tuple-element.41), channel_id=1, source_target_pairs={{0,2},{1,3},{2,0},{3,1},{4,6},{5,7},{6,4},{7,5},{8,10},{9,11},{10,... | collective-permute-start | bytes 233480 | tf_op jit(solution)/shard_map/ppermute | solution.py:29
  190.7 6.9 %collective-permute-start.47 = (bf16[16,2432]{1,0:T(8,128)(2,1)S(1)}, bf16[16,2432]{1,0:T(8,128)(2,1)S(1)}, u32[]{:S(2)}, u32[]{:S(2)}) collective-permute-start(bf16[16,2432]{1,0:T(8,128)(2,1)S(1)} %get-tuple-element.39), channel_id=1, source_target_pairs={{0,3},{1,2},{2,1},{3,0},{4,7},{5,6},{6,5},{7,4},{8,11},{9,10},{10,... | collective-permute-start | bytes 233480 | tf_op jit(solution)/shard_map/ppermute | solution.py:29
Sparse Core Ops, SparseCore 0:
  37.6 42.7 all-gather.5
  82.8 50.4 all-gather.3
  144.1 35.7 all-gather.7

commit v10 on v9

--- a/solution.py
+++ b/solution.py
@@ -88,24 +88,15 @@
             ]
 
 
-def outer_kernel(place, inverse, coupling, out):
-    nodes = inverse.shape[1]
-    size = nodes // PLANE
-    out[:, :nodes] = inverse[...]
-    for k in range(PLANE):
-        source = (k % SIDE) * SIDE + k // SIDE
-        out[:, nodes + k * size : nodes + (k + 1) * size] = coupling[
-            :, source * size : (source + 1) * size
-        ]
-
-
 def schur_kernel(place, *refs):
     separator, *pieces, schur, narrow = refs
+    size = schur.shape[0]
     for step in range(SIDE):
-        columns = block_of(place[1] ^ step, pieces[step].shape[1])
-        value = separator[:, columns] - pieces[step][...].astype(f32)
-        schur[:, columns] = value
-        narrow[:, columns] = value.astype(bf16)
+        for k in range(SIDE):
+            columns = block_of(k * SIDE + (place[0] ^ step), size)
+            value = separator[:, columns] - pieces[step][:, k * size : (k + 1) * size].astype(f32)
+            schur[:, columns] = value
+            narrow[:, columns] = value.astype(bf16)
 
 
 def finish_kernel(place, narrow, weight, *refs):
@@ -159,11 +150,8 @@
     away_high = jnp.where(even, 2 + ring, 3 - 2 * pair)
     place = jnp.stack([x, y])
 
-    (outer,) = kernel_call(
-        outer_kernel, place, [inverse_rows, coupling_rows], [shape((rows, 2 * nodes), bf16)]
-    )
-    link_rows = tie(link_rows, outer)
-    outer = over_axis(outer, "y")
+    coupling_in = over_axis(coupling_rows, "y")
+    outer = over_axis(jnp.concatenate([inverse_rows, coupling_rows], axis=1), "x")
 
     def ordered(pieces):
         stacked = jnp.stack(pieces)
@@ -197,7 +185,6 @@
         out_place == 0, jnp.concatenate([keep, got]), jnp.concatenate([got, keep])
     )
     pieces = spread_x(two)
-    coupling_in = over_axis(tie(coupling_rows, pieces[1]), "x")
     away_weights = permuted(line_weights, lambda p, y, x: (p, partner(p, y), x))
     (block,) = kernel_call(assemble_link, place, pieces, [shape((half, half), bf16)])
     weight_half = jnp.where(
@@ -222,7 +209,7 @@
             inner = lax.dot_general(
                 outer[:, :nodes], coupling_in, (((1,), (1,)), ((), ())), preferred_element_type=f32
             ).astype(bf16)
-            inner_all = over_axis(inner, "x")
+            inner_all = over_axis(inner, "y")
             previous = tie(previous, inner)
         product = lax.dot_general(
             previous, block, (((1,), (1,)), ((), ())), preferred_element_type=f32
@@ -277,9 +264,9 @@
     folded = jnp.dot(outer[:, nodes:], inner_all, preferred_element_type=f32).astype(bf16)
 
     def folded_chunk(step):
-        return lax.dynamic_slice(folded, ((y ^ step) * rows, 0), (rows, line))
-
-    back_rows = [folded_chunk(0)] + [along_y(folded_chunk(step), step) for step in (1, 2, 3)]
+        return lax.dynamic_slice(folded, ((x ^ step) * rows, 0), (rows, line))
+
+    back_rows = exchange_x(folded_chunk)
     schur_rows, narrow = kernel_call(
         schur_kernel,
         place,

time: 209 us -> 175 us (0.84)
  waiting for transfers between devices: 119 us -> 83.6 us
  starting transfers between devices: 44.4 us -> 49.6 us
  local copies, waits for them, and re-layouts: 2.88 us -> 0.15 us
    ppermute x48, waiting for transfers between devices: 80.5 us -> 61.4 us  [permuted(): return lax.ppermute(value, AXES, pairs)]
    all_gather x3, waiting for transfers between devices: 37.7 us -> 21.5 us  [over_axis(): lax.all_gather(array, 'blk', axis=0, tiled=True, axis_index_groups=groups)]
    ppermute x48, starting transfers between devices: 44.3 us -> 49.5 us  [permuted(): return lax.ppermute(value, AXES, pairs)]
    concatenate x0 -> x1, other arithmetic: none -> 2.26 us  [shards(): jnp.concatenate([inverse_rows, coupling_rows], axis=1)]
    pallas_call x5 -> x4, Pallas kernels: 6 us -> 4.48 us  [kernel_call(): pl.pallas_call(body, out_shape=out_shapes, in_specs=[pl.BlockSpec(memory_...]
  transfers between devices with their start and end apart: 51 -> 51, of which waited for: 21 -> 21; matrix products, arithmetic and copies ran while one was open for 4% -> 7% of each run, Pallas kernels for 2% -> 2%
where the time goes in v10:
time: 175 us; the launch traced here: 173 us
  waiting for transfers between devices  83.6 us (48%)
  starting transfers between devices  49.6 us (28%)
  matrix products  17.9 us (10%)
  between operations  14.3 us (8%)
  Pallas kernels  4.48 us (3%)
  other arithmetic  2.68 us (2%)
    ppermute x48, waiting for transfers between devices, permuted(): return lax.ppermute(value, AXES, pairs)  61.4 us
    ppermute x48, starting transfers between devices, permuted(): return lax.ppermute(value, AXES, pairs)  49.5 us
    all_gather x3, waiting for transfers between devices, over_axis(): lax.all_gather(array, 'blk', axis=0, tiled=True, axis_index_groups=groups)  21.5 us
    dot_general x15, matrix products, shards(): lax.dot_general(previous, block, (((1,), (1,)), ((), ())), preferred_elem...  9.76 us
    pallas_call x4, Pallas kernels, kernel_call(): pl.pallas_call(body, out_shape=out_shapes, in_specs=[pl.BlockSpec(memory_...  4.48 us
    dot_general x1, matrix products, shards(): lax.dot_general(outer[:, :nodes], coupling_in, (((1,), (1,)), ((), ())),...  4.3 us
  transfers between devices with their start and end apart: 51, of which 21 were waited for; matrix products, arithmetic and copies ran while one was open for 7% of the time, Pallas kernels for 2%

profile of v10, /device:TPU:224, one launch (start us, length us, event | category | flops | bytes accessed | tf_op | source)
XLA Modules:
  0.0 172.7 jit_solution(7073022143163021496)
XLA Ops:
  7.2 0.7 all-gather.9.cloned.1.call-update
  8.0 2.3 %pad_maximum_fusion = bf16[128,4096]{1,0:T(8,128)(2,1)} fusion(bf16[128,2048]{1,0:T(8,128)(2,1)} %bitcast.56, bf16[128,2048]{1,0:T(8,128)(2,1)} %bitcast.57), kind=kLoop, calls=%fused_computation.53 | loop fusion | flops 2097152 | bytes 2097152 | tf_op jit(solution)/shard_map/concatenate | solution.py:154
  10.4 1.6 collective-permute-start.1
  12.0 2.7 %collective-permute-start.2 = (f32[24,128]{1,0:T(8,128)S(1)}, f32[24,128]{1,0:T(8,128)S(1)}, u32[]{:S(2)}, u32[]{:S(2)}) collective-permute-start(f32[24,128]{1,0:T(8,128)S(1)} %get-tuple-element.69), channel_id=1, source_target_pairs={{0,2},{1,3},{2,0},{3,1},{4,6},{5,7},{6,4},{7,5},{8,10},{9,11},{10,... | collective-permute-start | bytes 36872 | tf_op jit(solution)/shard_map/ppermute | solution.py:29
  15.9 1.7 collective-permute-start
  17.6 2.1 %collective-permute-done.3 = f32[24,128]{1,0:T(8,128)S(1)} collective-permute-done((f32[24,128]{1,0:T(8,128)S(1)}, f32[24,128]{1,0:T(8,128)S(1)}, u32[]{:S(2)}, u32[]{:S(2)}) %collective-permute-start.3) | collective-permute-done | bytes 12320 | tf_op jit(solution)/shard_map/ppermute | solution.py:29
  19.7 2.7 %collective-permute-done = bf16[128,1024]{1,0:T(8,128)(2,1)S(1)} collective-permute-done((bf16[128,1024]{1,0:T(8,128)(2,1)S(1)}, bf16[128,1024]{1,0:T(8,128)(2,1)S(1)}, u32[]{:S(2)}, u32[]{:S(2)}) %collective-permute-start) | collective-permute-done | bytes 262176 | tf_op jit(solution)/shard_map/ppermute | solution.py:29
  22.8 3.9 %collective-permute-start.8 = (bf16[256,1024]{1,0:T(8,128)(2,1)S(1)}, bf16[256,1024]{1,0:T(8,128)(2,1)S(1)}, u32[]{:S(2)}, u32[]{:S(2)}) collective-permute-start(bf16[256,1024]{1,0:T(8,128)(2,1)S(1)} %maximum_select_fusion.refs_0_), channel_id=1, source_target_pairs={{0,2},{1,3},{2,0},{3,1},{4,6},{5,7},{6,4},{7,5},{8,10},{9,11},{10,... | collective-permute-start | bytes 1572872 | tf_op jit(solution)/shard_map/ppermute | solution.py:29
  27.3 1.6 collective-permute-start.4
  29.0 2.0 %collective-permute-done.4 = f32[1,512]{1,0:T(1,128)S(1)} collective-permute-done((f32[1,512]{1,0:T(1,128)S(1)}, f32[1,512]{1,0:T(1,128)S(1)}, u32[]{:S(2)}, u32[]{:S(2)}) %collective-permute-start.4) | collective-permute-done | bytes 2080 | tf_op jit(solution)/shard_map/ppermute | solution.py:29
  31.0 6.4 %collective-permute-done.7.refs_1_ = bf16[256,1024]{1,0:T(8,128)(2,1)S(1)} collective-permute-done((bf16[256,1024]{1,0:T(8,128)(2,1)S(1)}, bf16[256,1024]{1,0:T(8,128)(2,1)S(1)}, u32[]{:S(2)}, u32[]{:S(2)}) %collective-permute-start.7) | collective-permute-done | bytes 524320 | tf_op jit(solution)/shard_map/ppermute | solution.py:29
  37.4 11.6 %collective-permute-done.8.refs_2_ = bf16[256,1024]{1,0:T(8,128)(2,1)S(1)} collective-permute-done((bf16[256,1024]{1,0:T(8,128)(2,1)S(1)}, bf16[256,1024]{1,0:T(8,128)(2,1)S(1)}, u32[]{:S(2)}, u32[]{:S(2)}) %collective-permute-start.8) | collective-permute-done | bytes 524320 | tf_op jit(solution)/shard_map/ppermute | solution.py:29
  49.0 2.6 %collective-permute-done.9.refs_3_ = bf16[256,1024]{1,0:T(8,128)(2,1)S(1)} collective-permute-done((bf16[256,1024]{1,0:T(8,128)(2,1)S(1)}, bf16[256,1024]{1,0:T(8,128)(2,1)S(1)}, u32[]{:S(2)}, u32[]{:S(2)}) %collective-permute-start.9) | collective-permute-done | bytes 524320 | tf_op jit(solution)/shard_map/ppermute | solution.py:29
  51.6 0.7 shard_map.86
  53.0 0.7 collective-permute-start.10
  53.7 0.7 collective-permute-start.11
  54.3 0.7 fusion.26
  55.0 0.7 collective-permute-start.13
  55.7 2.6 %collective-permute-done.12 = bf16[16,1024]{1,0:T(8,128)(2,1)S(1)} collective-permute-done((bf16[16,1024]{1,0:T(8,128)(2,1)S(1)}, bf16[16,1024]{1,0:T(8,128)(2,1)S(1)}, u32[]{:S(2)}, u32[]{:S(2)}) %collective-permute-start.12) | collective-permute-done | bytes 32800 | tf_op jit(solution)/shard_map/ppermute | solution.py:29
  59.0 0.7 collective-permute-start.14
  59.7 0.7 collective-permute-start.15
  60.4 0.7 fusion.28
  62.1 2.3 %collective-permute-done.16 = bf16[16,1024]{1,0:T(8,128)(2,1)S(1)} collective-permute-done((bf16[16,1024]{1,0:T(8,128)(2,1)S(1)}, bf16[16,1024]{1,0:T(8,128)(2,1)S(1)}, u32[]{:S(2)}, u32[]{:S(2)}) %collective-permute-start.16) | collective-permute-done | bytes 32800 | tf_op jit(solution)/shard_map/ppermute | solution.py:29
  65.0 0.7 collective-permute-start.18
  65.7 0.7 collective-permute-start.19
  67.0 1.3 collective-permute-start.20
  68.3 2.4 %collective-permute-done.20 = bf16[16,1024]{1,0:T(8,128)(2,1)S(1)} collective-permute-done((bf16[16,1024]{1,0:T(8,128)(2,1)S(1)}, bf16[16,1024]{1,0:T(8,128)(2,1)S(1)}, u32[]{:S(2)}, u32[]{:S(2)}) %collective-permute-start.20) | collective-permute-done | bytes 32800 | tf_op jit(solution)/shard_map/ppermute | solution.py:29
  71.4 0.7 collective-permute-start.22
  72.1 0.7 collective-permute-start.23
  73.5 1.3 collective-permute-start.24
  74.7 2.1 %collective-permute-done.24 = bf16[16,1024]{1,0:T(8,128)(2,1)S(1)} collective-permute-done((bf16[16,1024]{1,0:T(8,128)(2,1)S(1)}, bf16[16,1024]{1,0:T(8,128)(2,1)S(1)}, u32[]{:S(2)}, u32[]{:S(2)}) %collective-permute-start.24) | collective-permute-done | bytes 32800 | tf_op jit(solution)/shard_map/ppermute | solution.py:29
  77.5 0.7 collective-permute-start.26
  78.2 0.7 collective-permute-start.27
  78.9 18.7 %all-gather.5.cloned.1.call-done = bf16[512,4096]{1,0:T(8,128)(2,1)} async-done(((bf16[128,4096]{1,0:T(8,128)(2,1)}), bf16[512,4096]{1,0:T(8,128)(2,1)}) %all-gather.5.cloned.1.call-update) | async-done | bytes 4194320 | tf_op jit(solution)/shard_map/all_gather | solution.py:127
  97.7 4.3 %fusion.7 = bf16[512,512]{1,0:T(8,128)(2,1)} fusion(bf16[512,2048]{1,0:T(8,128)(2,1)} %bitcast.63, bf16[512,4096]{1,0:T(8,128)(2,1)} %all-gather.5.cloned.1.call-done), kind=kOutput, calls=%fused_computation.5 | convolution fusion | flops 1074003968 | bytes 4718592 | tf_op jit(solution)/shard_map/dot_general | solution.py:209
  102.6 0.9 collective-permute-start.28
  103.6 0.7 collective-permute-start.29
  104.2 2.1 %collective-permute-done.28 = bf16[16,1024]{1,0:T(8,128)(2,1)S(1)} collective-permute-done((bf16[16,1024]{1,0:T(8,128)(2,1)S(1)}, bf16[16,1024]{1,0:T(8,128)(2,1)S(1)}, u32[]{:S(2)}, u32[]{:S(2)}) %collective-permute-start.28) | collective-permute-done | bytes 32800 | tf_op jit(solution)/shard_map/ppermute | solution.py:29
  106.9 0.7 collective-permute-start.30
  107.6 0.7 collective-permute-start.31
  109.0 1.2 collective-permute-start.32
  110.6 1.8 %collective-permute-done.32 = bf16[16,1024]{1,0:T(8,128)(2,1)S(1)} collective-permute-done((bf16[16,1024]{1,0:T(8,128)(2,1)S(1)}, bf16[16,1024]{1,0:T(8,128)(2,1)S(1)}, u32[]{:S(2)}, u32[]{:S(2)}) %collective-permute-start.32) | collective-permute-done | bytes 32800 | tf_op jit(solution)/shard_map/ppermute | solution.py:29
  113.0 1.3 collective-permute-start.34
  114.3 1.3 collective-permute-start.35
  115.6 7.8 %collective-permute-done.34 = bf16[16,1024]{1,0:T(8,128)(2,1)S(1)} collective-permute-done((bf16[16,1024]{1,0:T(8,128)(2,1)S(1)}, bf16[16,1024]{1,0:T(8,128)(2,1)S(1)}, u32[]{:S(2)}, u32[]{:S(2)}) %collective-permute-start.34) | collective-permute-done | bytes 32800 | tf_op jit(solution)/shard_map/ppermute | solution.py:29
  123.4 0.7 collective-permute-done.35
  124.7 1.9 %collective-permute-start.37 = (bf16[16,1024]{1,0:T(8,128)(2,1)S(1)}, bf16[16,1024]{1,0:T(8,128)(2,1)S(1)}, u32[]{:S(2)}, u32[]{:S(2)}) collective-permute-start(bf16[16,1024]{1,0:T(8,128)(2,1)S(1)} %fusion.38), channel_id=1, source_target_pairs={{0,16},{1,17},{2,18},{3,19},{4,20},{5,21},{6,22},{7,23},{8,24},{9,... | collective-permute-start | bytes 98312 | tf_op jit(solution)/shard_map/ppermute | solution.py:29
  126.7 2.3 %collective-permute-done.36 = bf16[16,1024]{1,0:T(8,128)(2,1)S(1)} collective-permute-done((bf16[16,1024]{1,0:T(8,128)(2,1)S(1)}, bf16[16,1024]{1,0:T(8,128)(2,1)S(1)}, u32[]{:S(2)}, u32[]{:S(2)}) %collective-permute-start.36) | collective-permute-done | bytes 32800 | tf_op jit(solution)/shard_map/ppermute | solution.py:29
  129.0 0.7 fusion.40
  129.7 1.6 collective-permute-start.38
  131.2 3.0 %collective-permute-done.38 = bf16[16,1024]{1,0:T(8,128)(2,1)S(1)} collective-permute-done((bf16[16,1024]{1,0:T(8,128)(2,1)S(1)}, bf16[16,1024]{1,0:T(8,128)(2,1)S(1)}, u32[]{:S(2)}, u32[]{:S(2)}) %collective-permute-start.38) | collective-permute-done | bytes 32800 | tf_op jit(solution)/shard_map/ppermute | solution.py:29
  134.3 1.6 collective-permute-start.42
  136.2 1.9 %collective-permute-start.43 = (bf16[16,512]{1,0:T(8,128)(2,1)S(1)}, bf16[16,512]{1,0:T(8,128)(2,1)S(1)}, u32[]{:S(2)}, u32[]{:S(2)}) collective-permute-start(bf16[16,512]{1,0:T(8,128)(2,1)S(1)} %get-tuple-element.49), channel_id=1, source_target_pairs={{16,4},{17,5},{18,6},{19,7},{20,0},{21,1},{22,2},{23,3},{24,12},{2... | collective-permute-start | bytes 49160 | tf_op jit(solution)/shard_map/ppermute | solution.py:29
  138.2 1.9 %collective-permute-start.44 = (bf16[16,512]{1,0:T(8,128)(2,1)S(1)}, bf16[16,512]{1,0:T(8,128)(2,1)S(1)}, u32[]{:S(2)}, u32[]{:S(2)}) collective-permute-start(bf16[16,512]{1,0:T(8,128)(2,1)S(1)} %get-tuple-element.50), channel_id=1, source_target_pairs={{16,0},{17,1},{18,2},{19,3},{20,4},{21,5},{22,6},{23,7},{24,8},{25... | collective-permute-start | bytes 49160 | tf_op jit(solution)/shard_map/ppermute | solution.py:29
  140.1 1.5 collective-permute-done.43
  141.7 2.8 %all-gather.7.cloned.1.call-done = bf16[2048,512]{1,0:T(8,128)(2,1)} async-done(((bf16[512,512]{1,0:T(8,128)(2,1)}), bf16[2048,512]{1,0:T(8,128)(2,1)}) %all-gather.7.cloned.1.call-update) | async-done | bytes 2097168 | tf_op jit(solution)/shard_map/all_gather | solution.py:127
  144.5 3.5 %fusion.4 = bf16[512,512]{1,0:T(8,128)(2,1)S(1)} fusion(bf16[2048,512]{1,0:T(8,128)(2,1)} %all-gather.7.cloned.1.call-done, bf16[512,4096]{1,0:T(8,128)(2,1)} %all-gather.5.cloned.1.call-done), kind=kOutput, calls=%fused_computation.4 | convolution fusion | flops 1074003968 | bytes 4718592 | tf_op jit(solution)/shard_map/dot_general | solution.py:264
  148.0 1.6 collective-permute-start.39
  149.6 2.7 %collective-permute-start.40 = (bf16[128,512]{1,0:T(8,128)(2,1)S(1)}, bf16[128,512]{1,0:T(8,128)(2,1)S(1)}, u32[]{:S(2)}, u32[]{:S(2)}) collective-permute-start(bf16[128,512]{1,0:T(8,128)(2,1)S(1)} %get-tuple-element.32), channel_id=1, source_target_pairs={{0,2},{1,3},{2,0},{3,1},{4,6},{5,7},{6,4},{7,5},{8,10},{9,11},{10,... | collective-permute-start | bytes 393224 | tf_op jit(solution)/shard_map/ppermute | solution.py:29
  153.2 3.9 %collective-permute-start.46 = (bf16[16,2432]{1,0:T(8,128)(2,1)S(1)}, bf16[16,2432]{1,0:T(8,128)(2,1)S(1)}, u32[]{:S(2)}, u32[]{:S(2)}) collective-permute-start(bf16[16,2432]{1,0:T(8,128)(2,1)S(1)} %get-tuple-element.37), channel_id=1, source_target_pairs={{0,2},{1,3},{2,0},{3,1},{4,6},{5,7},{6,4},{7,5},{8,10},{9,11},{10,... | collective-permute-start | bytes 233480 | tf_op jit(solution)/shard_map/ppermute | solution.py:29
  157.6 1.9 %collective-permute-done.40.refs_3_ = bf16[128,512]{1,0:T(8,128)(2,1)S(1)} collective-permute-done((bf16[128,512]{1,0:T(8,128)(2,1)S(1)}, bf16[128,512]{1,0:T(8,128)(2,1)S(1)}, u32[]{:S(2)}, u32[]{:S(2)}) %collective-permute-start.40) | collective-permute-done | bytes 131104 | tf_op jit(solution)/shard_map/ppermute | solution.py:29
  159.5 3.4 %collective-permute-done.41.refs_4_ = bf16[128,512]{1,0:T(8,128)(2,1)S(1)} collective-permute-done((bf16[128,512]{1,0:T(8,128)(2,1)S(1)}, bf16[128,512]{1,0:T(8,128)(2,1)S(1)}, u32[]{:S(2)}, u32[]{:S(2)}) %collective-permute-start.41) | collective-permute-done | bytes 131104 | tf_op jit(solution)/shard_map/ppermute | solution.py:29
  162.9 1.7 %shard_map.87 = (f32[128,2048]{1,0:T(8,128)}, bf16[128,2048]{1,0:T(8,128)(2,1)S(1)}) custom-call(s32[2]{0:T(128)S(1)} %pad_add_fusion.place, f32[128,2048]{1,0:T(8,128)S(1)} %bitcast.52, bf16[128,512]{1,0:T(8,128)(2,1)S(1)} %get-tuple-element.34.refs_1_, bf16[128,512]{1,0:T(8,128)(2,1)S(1)} %collective-permute-done.39.refs_2_, ...), custom_call_target="tpu_custom_call" | custom-call | bytes 3145728 | tf_op jit(solution)/shard_map/pallas_call | solution.py:58
  164.7 1.5 shard_map.88
  (98 shorter events, 13.8 us)
Async XLA Ops:
  7.2 3.2 %copy-start.2 = (f32[1,128]{1,0:T(1,128)S(1)}, f32[1,128]{1,0:T(1,128)}, u32[]{:S(2)}) copy-start(f32[1,128]{1,0:T(1,128)} %weight.1) | copy-start | bytes 1540
  7.2 3.2 %copy-start.3 = (f32[1,64,128]{2,1,0:T(8,128)S(1)}, f32[1,64,128]{2,1,0:T(8,128)}, u32[]{:S(2)}) copy-start(f32[1,64,128]{2,1,0:T(8,128)} %param.10) | copy-start | bytes 98308
  7.2 8.1 %copy-start.1 = (bf16[1,128,2048]{2,1,0:T(8,128)(2,1)S(1)}, bf16[1,128,2048]{2,1,0:T(8,128)(2,1)}, u32[]{:S(2)}) copy-start(bf16[1,128,2048]{2,1,0:T(8,128)(2,1)} %param.9) | copy-start | bytes 1572868
  7.2 71.7 %all-gather.9.cloned.1.call-start = ((), (), s32[]{:S(2)}) async-start(), calls=%async_computation.2 | async-start | bytes 2621440 | tf_op jit(solution)/shard_map/all_gather | solution.py:127
  7.9 89.7 %all-gather.5.cloned.1.call-start = ((), (), s32[]{:S(2)}) async-start(), calls=%async_computation | async-start | bytes 5242880 | tf_op jit(solution)/shard_map/all_gather | solution.py:127
  10.3 134.2 %all-gather.7.cloned.1.call-start = ((), (), s32[]{:S(2)}) async-start(), calls=%async_computation.1 | async-start | bytes 2621440 | tf_op jit(solution)/shard_map/all_gather | solution.py:127
  10.4 7.1 %collective-permute-start.1 = (f32[24,128]{1,0:T(8,128)S(1)}, f32[24,128]{1,0:T(8,128)S(1)}, u32[]{:S(2)}, u32[]{:S(2)}) collective-permute-start(f32[24,128]{1,0:T(8,128)S(1)} %get-tuple-element.68), channel_id=1, source_target_pairs={{0,1},{1,0},{2,3},{3,2},{4,5},{5,4},{6,7},{7,6},{8,9},{9,8},{10,11... | collective-permute-start | bytes 36872 | tf_op jit(solution)/shard_map/ppermute | solution.py:29
  12.0 5.5 %collective-permute-start.2 = (f32[24,128]{1,0:T(8,128)S(1)}, f32[24,128]{1,0:T(8,128)S(1)}, u32[]{:S(2)}, u32[]{:S(2)}) collective-permute-start(f32[24,128]{1,0:T(8,128)S(1)} %get-tuple-element.69), channel_id=1, source_target_pairs={{0,2},{1,3},{2,0},{3,1},{4,6},{5,7},{6,4},{7,5},{8,10},{9,11},{10,... | collective-permute-start | bytes 36872 | tf_op jit(solution)/shard_map/ppermute | solution.py:29
  14.7 4.9 %collective-permute-start.3 = (f32[24,128]{1,0:T(8,128)S(1)}, f32[24,128]{1,0:T(8,128)S(1)}, u32[]{:S(2)}, u32[]{:S(2)}) collective-permute-start(f32[24,128]{1,0:T(8,128)S(1)} %get-tuple-element.70), channel_id=1, source_target_pairs={{0,3},{1,2},{2,1},{3,0},{4,7},{5,6},{6,5},{7,4},{8,11},{9,10},{10,... | collective-permute-start | bytes 36872 | tf_op jit(solution)/shard_map/ppermute | solution.py:29
  15.9 6.5 %collective-permute-start = (bf16[128,1024]{1,0:T(8,128)(2,1)S(1)}, bf16[128,1024]{1,0:T(8,128)(2,1)S(1)}, u32[]{:S(2)}, u32[]{:S(2)}) collective-permute-start(bf16[128,1024]{1,0:T(8,128)(2,1)S(1)} %get-tuple-element.17), channel_id=1, source_target_pairs={{0,4},{1,5},{2,6},{3,7},{4,0},{5,1},{6,2},{7,3},{8,12},{9,13},{10,... | collective-permute-start | bytes 786440 | tf_op jit(solution)/shard_map/ppermute | solution.py:29
  22.5 14.9 %collective-permute-start.7 = (bf16[256,1024]{1,0:T(8,128)(2,1)S(1)}, bf16[256,1024]{1,0:T(8,128)(2,1)S(1)}, u32[]{:S(2)}, u32[]{:S(2)}) collective-permute-start(bf16[256,1024]{1,0:T(8,128)(2,1)S(1)} %maximum_select_fusion.refs_0_), channel_id=1, source_target_pairs={{0,1},{1,0},{2,3},{3,2},{4,5},{5,4},{6,7},{7,6},{8,9},{9,8},{10,11... | collective-permute-start | bytes 1572872 | tf_op jit(solution)/shard_map/ppermute | solution.py:29
  22.8 26.2 %collective-permute-start.8 = (bf16[256,1024]{1,0:T(8,128)(2,1)S(1)}, bf16[256,1024]{1,0:T(8,128)(2,1)S(1)}, u32[]{:S(2)}, u32[]{:S(2)}) collective-permute-start(bf16[256,1024]{1,0:T(8,128)(2,1)S(1)} %maximum_select_fusion.refs_0_), channel_id=1, source_target_pairs={{0,2},{1,3},{2,0},{3,1},{4,6},{5,7},{6,4},{7,5},{8,10},{9,11},{10,... | collective-permute-start | bytes 1572872 | tf_op jit(solution)/shard_map/ppermute | solution.py:29
  26.8 24.8 %collective-permute-start.9 = (bf16[256,1024]{1,0:T(8,128)(2,1)S(1)}, bf16[256,1024]{1,0:T(8,128)(2,1)S(1)}, u32[]{:S(2)}, u32[]{:S(2)}) collective-permute-start(bf16[256,1024]{1,0:T(8,128)(2,1)S(1)} %maximum_select_fusion.refs_0_), channel_id=1, source_target_pairs={{0,3},{1,2},{2,1},{3,0},{4,7},{5,6},{6,5},{7,4},{8,11},{9,10},{10,... | collective-permute-start | bytes 1572872 | tf_op jit(solution)/shard_map/ppermute | solution.py:29
  27.3 3.6 %collective-permute-start.4 = (f32[1,512]{1,0:T(1,128)S(1)}, f32[1,512]{1,0:T(1,128)S(1)}, u32[]{:S(2)}, u32[]{:S(2)}) collective-permute-start(f32[1,512]{1,0:T(1,128)S(1)} %slice.32), channel_id=1, source_target_pairs={{0,4},{1,5},{2,6},{3,7},{4,0},{5,1},{6,2},{7,3},{8,12},{9,13},{10,... | collective-permute-start | bytes 6152 | tf_op jit(solution)/shard_map/ppermute | solution.py:29
  29.0 23.3 %collective-permute-start.5 = (bf16[16,1024]{1,0:T(8,128)(2,1)S(1)}, bf16[16,1024]{1,0:T(8,128)(2,1)S(1)}, u32[]{:S(2)}, u32[]{:S(2)}) collective-permute-start(bf16[16,1024]{1,0:T(8,128)(2,1)S(1)} %fusion.42), channel_id=1, source_target_pairs={{0,20},{1,21},{2,22},{3,23},{4,16},{5,17},{6,18},{7,19},{8,28},{9,... | collective-permute-start | bytes 98312 | tf_op jit(solution)/shard_map/ppermute | solution.py:29
  31.0 21.3 %collective-permute-start.6 = (bf16[16,1024]{1,0:T(8,128)(2,1)S(1)}, bf16[16,1024]{1,0:T(8,128)(2,1)S(1)}, u32[]{:S(2)}, u32[]{:S(2)}) collective-permute-start(bf16[16,1024]{1,0:T(8,128)(2,1)S(1)} %fusion.42), channel_id=1, source_target_pairs={{0,16},{1,17},{2,18},{3,19},{4,20},{5,21},{6,22},{7,23},{8,24},{9,... | collective-permute-start | bytes 98312 | tf_op jit(solution)/shard_map/ppermute | solution.py:29
  53.0 1.3 collective-permute-start.10
  53.7 0.7 collective-permute-start.11
  55.0 3.4 %collective-permute-start.12 = (bf16[16,1024]{1,0:T(8,128)(2,1)S(1)}, bf16[16,1024]{1,0:T(8,128)(2,1)S(1)}, u32[]{:S(2)}, u32[]{:S(2)}) collective-permute-start(bf16[16,1024]{1,0:T(8,128)(2,1)S(1)} %fusion.26), channel_id=1, source_target_pairs={{0,20},{1,21},{2,22},{3,23},{4,16},{5,17},{6,18},{7,19},{8,28},{9,... | collective-permute-start | bytes 98312 | tf_op jit(solution)/shard_map/ppermute | solution.py:29
  55.0 3.4 %collective-permute-start.13 = (bf16[16,1024]{1,0:T(8,128)(2,1)S(1)}, bf16[16,1024]{1,0:T(8,128)(2,1)S(1)}, u32[]{:S(2)}, u32[]{:S(2)}) collective-permute-start(bf16[16,1024]{1,0:T(8,128)(2,1)S(1)} %fusion.26), channel_id=1, source_target_pairs={{0,16},{1,17},{2,18},{3,19},{4,20},{5,21},{6,22},{7,23},{8,24},{9,... | collective-permute-start | bytes 98312 | tf_op jit(solution)/shard_map/ppermute | solution.py:29
  59.0 1.3 collective-permute-start.14
  59.7 0.7 collective-permute-start.15
  61.0 3.3 %collective-permute-start.16 = (bf16[16,1024]{1,0:T(8,128)(2,1)S(1)}, bf16[16,1024]{1,0:T(8,128)(2,1)S(1)}, u32[]{:S(2)}, u32[]{:S(2)}) collective-permute-start(bf16[16,1024]{1,0:T(8,128)(2,1)S(1)} %fusion.28), channel_id=1, source_target_pairs={{0,20},{1,21},{2,22},{3,23},{4,16},{5,17},{6,18},{7,19},{8,28},{9,... | collective-permute-start | bytes 98312 | tf_op jit(solution)/shard_map/ppermute | solution.py:29
  61.7 2.7 %collective-permute-start.17 = (bf16[16,1024]{1,0:T(8,128)(2,1)S(1)}, bf16[16,1024]{1,0:T(8,128)(2,1)S(1)}, u32[]{:S(2)}, u32[]{:S(2)}) collective-permute-start(bf16[16,1024]{1,0:T(8,128)(2,1)S(1)} %fusion.28), channel_id=1, source_target_pairs={{0,16},{1,17},{2,18},{3,19},{4,20},{5,21},{6,22},{7,23},{8,24},{9,... | collective-permute-start | bytes 98312 | tf_op jit(solution)/shard_map/ppermute | solution.py:29
  65.0 1.3 collective-permute-start.18
  65.7 0.7 collective-permute-start.19
  67.0 3.7 %collective-permute-start.20 = (bf16[16,1024]{1,0:T(8,128)(2,1)S(1)}, bf16[16,1024]{1,0:T(8,128)(2,1)S(1)}, u32[]{:S(2)}, u32[]{:S(2)}) collective-permute-start(bf16[16,1024]{1,0:T(8,128)(2,1)S(1)} %fusion.30), channel_id=1, source_target_pairs={{0,20},{1,21},{2,22},{3,23},{4,16},{5,17},{6,18},{7,19},{8,28},{9,... | collective-permute-start | bytes 98312 | tf_op jit(solution)/shard_map/ppermute | solution.py:29
  68.3 2.5 %collective-permute-start.21 = (bf16[16,1024]{1,0:T(8,128)(2,1)S(1)}, bf16[16,1024]{1,0:T(8,128)(2,1)S(1)}, u32[]{:S(2)}, u32[]{:S(2)}) collective-permute-start(bf16[16,1024]{1,0:T(8,128)(2,1)S(1)} %fusion.30), channel_id=1, source_target_pairs={{0,16},{1,17},{2,18},{3,19},{4,20},{5,21},{6,22},{7,23},{8,24},{9,... | collective-permute-start | bytes 98312 | tf_op jit(solution)/shard_map/ppermute | solution.py:29
  71.4 1.3 collective-permute-start.22
  72.1 0.7 collective-permute-start.23
  73.5 3.4 %collective-permute-start.24 = (bf16[16,1024]{1,0:T(8,128)(2,1)S(1)}, bf16[16,1024]{1,0:T(8,128)(2,1)S(1)}, u32[]{:S(2)}, u32[]{:S(2)}) collective-permute-start(bf16[16,1024]{1,0:T(8,128)(2,1)S(1)} %fusion.32), channel_id=1, source_target_pairs={{0,20},{1,21},{2,22},{3,23},{4,16},{5,17},{6,18},{7,19},{8,28},{9,... | collective-permute-start | bytes 98312 | tf_op jit(solution)/shard_map/ppermute | solution.py:29
  74.7 2.1 %collective-permute-start.25 = (bf16[16,1024]{1,0:T(8,128)(2,1)S(1)}, bf16[16,1024]{1,0:T(8,128)(2,1)S(1)}, u32[]{:S(2)}, u32[]{:S(2)}) collective-permute-start(bf16[16,1024]{1,0:T(8,128)(2,1)S(1)} %fusion.32), channel_id=1, source_target_pairs={{0,16},{1,17},{2,18},{3,19},{4,20},{5,21},{6,22},{7,23},{8,24},{9,... | collective-permute-start | bytes 98312 | tf_op jit(solution)/shard_map/ppermute | solution.py:29
  77.5 1.3 collective-permute-start.26
  78.2 0.7 collective-permute-start.27
  102.6 3.7 %collective-permute-start.28 = (bf16[16,1024]{1,0:T(8,128)(2,1)S(1)}, bf16[16,1024]{1,0:T(8,128)(2,1)S(1)}, u32[]{:S(2)}, u32[]{:S(2)}) collective-permute-start(bf16[16,1024]{1,0:T(8,128)(2,1)S(1)} %fusion.34), channel_id=1, source_target_pairs={{0,20},{1,21},{2,22},{3,23},{4,16},{5,17},{6,18},{7,19},{8,28},{9,... | collective-permute-start | bytes 98312 | tf_op jit(solution)/shard_map/ppermute | solution.py:29
  103.6 2.7 %collective-permute-start.29 = (bf16[16,1024]{1,0:T(8,128)(2,1)S(1)}, bf16[16,1024]{1,0:T(8,128)(2,1)S(1)}, u32[]{:S(2)}, u32[]{:S(2)}) collective-permute-start(bf16[16,1024]{1,0:T(8,128)(2,1)S(1)} %fusion.34), channel_id=1, source_target_pairs={{0,16},{1,17},{2,18},{3,19},{4,20},{5,21},{6,22},{7,23},{8,24},{9,... | collective-permute-start | bytes 98312 | tf_op jit(solution)/shard_map/ppermute | solution.py:29
  106.9 1.4 collective-permute-start.30
  107.6 0.7 collective-permute-start.31
  109.0 3.4 %collective-permute-start.32 = (bf16[16,1024]{1,0:T(8,128)(2,1)S(1)}, bf16[16,1024]{1,0:T(8,128)(2,1)S(1)}, u32[]{:S(2)}, u32[]{:S(2)}) collective-permute-start(bf16[16,1024]{1,0:T(8,128)(2,1)S(1)} %fusion.36), channel_id=1, source_target_pairs={{0,20},{1,21},{2,22},{3,23},{4,16},{5,17},{6,18},{7,19},{8,28},{9,... | collective-permute-start | bytes 98312 | tf_op jit(solution)/shard_map/ppermute | solution.py:29
  110.2 2.2 %collective-permute-start.33 = (bf16[16,1024]{1,0:T(8,128)(2,1)S(1)}, bf16[16,1024]{1,0:T(8,128)(2,1)S(1)}, u32[]{:S(2)}, u32[]{:S(2)}) collective-permute-start(bf16[16,1024]{1,0:T(8,128)(2,1)S(1)} %fusion.36), channel_id=1, source_target_pairs={{0,16},{1,17},{2,18},{3,19},{4,20},{5,21},{6,22},{7,23},{8,24},{9,... | collective-permute-start | bytes 98312 | tf_op jit(solution)/shard_map/ppermute | solution.py:29
  113.0 10.4 %collective-permute-start.34 = (bf16[16,1024]{1,0:T(8,128)(2,1)S(1)}, bf16[16,1024]{1,0:T(8,128)(2,1)S(1)}, u32[]{:S(2)}, u32[]{:S(2)}) collective-permute-start(bf16[16,1024]{1,0:T(8,128)(2,1)S(1)} %fusion.37), channel_id=1, source_target_pairs={{208,236},{209,237},{210,238},{211,239},{212,232},{213,233},{214,2... | collective-permute-start | bytes 98312 | tf_op jit(solution)/shard_map/ppermute | solution.py:29
  114.3 9.8 %collective-permute-start.35 = (bf16[16,1024]{1,0:T(8,128)(2,1)S(1)}, bf16[16,1024]{1,0:T(8,128)(2,1)S(1)}, u32[]{:S(2)}, u32[]{:S(2)}) collective-permute-start(bf16[16,1024]{1,0:T(8,128)(2,1)S(1)} %fusion.37), channel_id=1, source_target_pairs={{208,224},{209,225},{210,226},{211,227},{212,228},{213,229},{214,2... | collective-permute-start | bytes 98312 | tf_op jit(solution)/shard_map/ppermute | solution.py:29
  124.7 4.2 %collective-permute-start.36 = (bf16[16,1024]{1,0:T(8,128)(2,1)S(1)}, bf16[16,1024]{1,0:T(8,128)(2,1)S(1)}, u32[]{:S(2)}, u32[]{:S(2)}) collective-permute-start(bf16[16,1024]{1,0:T(8,128)(2,1)S(1)} %fusion.38), channel_id=1, source_target_pairs={{0,20},{1,21},{2,22},{3,23},{4,16},{5,17},{6,18},{7,19},{8,28},{9,... | collective-permute-start | bytes 98312 | tf_op jit(solution)/shard_map/ppermute | solution.py:29
  124.7 4.2 %collective-permute-start.37 = (bf16[16,1024]{1,0:T(8,128)(2,1)S(1)}, bf16[16,1024]{1,0:T(8,128)(2,1)S(1)}, u32[]{:S(2)}, u32[]{:S(2)}) collective-permute-start(bf16[16,1024]{1,0:T(8,128)(2,1)S(1)} %fusion.38), channel_id=1, source_target_pairs={{0,16},{1,17},{2,18},{3,19},{4,20},{5,21},{6,22},{7,23},{8,24},{9,... | collective-permute-start | bytes 98312 | tf_op jit(solution)/shard_map/ppermute | solution.py:29
  129.7 4.6 %collective-permute-start.38 = (bf16[16,1024]{1,0:T(8,128)(2,1)S(1)}, bf16[16,1024]{1,0:T(8,128)(2,1)S(1)}, u32[]{:S(2)}, u32[]{:S(2)}) collective-permute-start(bf16[16,1024]{1,0:T(8,128)(2,1)S(1)} %fusion.40), channel_id=1, source_target_pairs={{0,4},{1,5},{2,6},{3,7},{4,0},{5,1},{6,2},{7,3},{8,12},{9,13},{10,... | collective-permute-start | bytes 98312 | tf_op jit(solution)/shard_map/ppermute | solution.py:29
  134.3 7.4 %collective-permute-start.42 = (bf16[16,1024]{1,0:T(8,128)(2,1)S(1)}, bf16[16,1024]{1,0:T(8,128)(2,1)S(1)}, u32[]{:S(2)}, u32[]{:S(2)}) collective-permute-start(bf16[16,1024]{1,0:T(8,128)(2,1)S(1)} %get-tuple-element.40), channel_id=1, source_target_pairs={{0,12},{1,13},{2,14},{3,15},{4,8},{5,9},{6,10},{7,11},{8,4},{9,5},... | collective-permute-start | bytes 98312 | tf_op jit(solution)/shard_map/ppermute | solution.py:29
  136.2 5.4 %collective-permute-start.43 = (bf16[16,512]{1,0:T(8,128)(2,1)S(1)}, bf16[16,512]{1,0:T(8,128)(2,1)S(1)}, u32[]{:S(2)}, u32[]{:S(2)}) collective-permute-start(bf16[16,512]{1,0:T(8,128)(2,1)S(1)} %get-tuple-element.49), channel_id=1, source_target_pairs={{16,4},{17,5},{18,6},{19,7},{20,0},{21,1},{22,2},{23,3},{24,12},{2... | collective-permute-start | bytes 49160 | tf_op jit(solution)/shard_map/ppermute | solution.py:29
  138.2 3.5 %collective-permute-start.44 = (bf16[16,512]{1,0:T(8,128)(2,1)S(1)}, bf16[16,512]{1,0:T(8,128)(2,1)S(1)}, u32[]{:S(2)}, u32[]{:S(2)}) collective-permute-start(bf16[16,512]{1,0:T(8,128)(2,1)S(1)} %get-tuple-element.50), channel_id=1, source_target_pairs={{16,0},{17,1},{18,2},{19,3},{20,4},{21,5},{22,6},{23,7},{24,8},{25... | collective-permute-start | bytes 49160 | tf_op jit(solution)/shard_map/ppermute | solution.py:29
  147.9 15.0 %copy-start = (f32[1,128,2048]{2,1,0:T(8,128)S(1)}, f32[1,128,2048]{2,1,0:T(8,128)}, u32[]{:S(2)}) copy-start(f32[1,128,2048]{2,1,0:T(8,128)} %param.8) | copy-start | bytes 3145732
  148.0 9.1 %collective-permute-start.39 = (bf16[128,512]{1,0:T(8,128)(2,1)S(1)}, bf16[128,512]{1,0:T(8,128)(2,1)S(1)}, u32[]{:S(2)}, u32[]{:S(2)}) collective-permute-start(bf16[128,512]{1,0:T(8,128)(2,1)S(1)} %get-tuple-element.33), channel_id=1, source_target_pairs={{0,1},{1,0},{2,3},{3,2},{4,5},{5,4},{6,7},{7,6},{8,9},{9,8},{10,11... | collective-permute-start | bytes 393224 | tf_op jit(solution)/shard_map/ppermute | solution.py:29
  149.6 9.9 %collective-permute-start.40 = (bf16[128,512]{1,0:T(8,128)(2,1)S(1)}, bf16[128,512]{1,0:T(8,128)(2,1)S(1)}, u32[]{:S(2)}, u32[]{:S(2)}) collective-permute-start(bf16[128,512]{1,0:T(8,128)(2,1)S(1)} %get-tuple-element.32), channel_id=1, source_target_pairs={{0,2},{1,3},{2,0},{3,1},{4,6},{5,7},{6,4},{7,5},{8,10},{9,11},{10,... | collective-permute-start | bytes 393224 | tf_op jit(solution)/shard_map/ppermute | solution.py:29
  152.2 10.7 %collective-permute-start.41 = (bf16[128,512]{1,0:T(8,128)(2,1)S(1)}, bf16[128,512]{1,0:T(8,128)(2,1)S(1)}, u32[]{:S(2)}, u32[]{:S(2)}) collective-permute-start(bf16[128,512]{1,0:T(8,128)(2,1)S(1)} %get-tuple-element.31), channel_id=1, source_target_pairs={{0,3},{1,2},{2,1},{3,0},{4,7},{5,6},{6,5},{7,4},{8,11},{9,10},{10,... | collective-permute-start | bytes 393224 | tf_op jit(solution)/shard_map/ppermute | solution.py:29
  152.8 11.8 %collective-permute-start.45 = (bf16[16,2432]{1,0:T(8,128)(2,1)S(1)}, bf16[16,2432]{1,0:T(8,128)(2,1)S(1)}, u32[]{:S(2)}, u32[]{:S(2)}) collective-permute-start(bf16[16,2432]{1,0:T(8,128)(2,1)S(1)} %get-tuple-element.36), channel_id=1, source_target_pairs={{0,1},{1,0},{2,3},{3,2},{4,5},{5,4},{6,7},{7,6},{8,9},{9,8},{10,11... | collective-permute-start | bytes 233480 | tf_op jit(solution)/shard_map/ppermute | solution.py:29
  153.2 11.5 %collective-permute-start.46 = (bf16[16,2432]{1,0:T(8,128)(2,1)S(1)}, bf16[16,2432]{1,0:T(8,128)(2,1)S(1)}, u32[]{:S(2)}, u32[]{:S(2)}) collective-permute-start(bf16[16,2432]{1,0:T(8,128)(2,1)S(1)} %get-tuple-element.37), channel_id=1, source_target_pairs={{0,2},{1,3},{2,0},{3,1},{4,6},{5,7},{6,4},{7,5},{8,10},{9,11},{10,... | collective-permute-start | bytes 233480 | tf_op jit(solution)/shard_map/ppermute | solution.py:29
  157.1 7.6 %collective-permute-start.47 = (bf16[16,2432]{1,0:T(8,128)(2,1)S(1)}, bf16[16,2432]{1,0:T(8,128)(2,1)S(1)}, u32[]{:S(2)}, u32[]{:S(2)}) collective-permute-start(bf16[16,2432]{1,0:T(8,128)(2,1)S(1)} %get-tuple-element.35), channel_id=1, source_target_pairs={{0,3},{1,2},{2,1},{3,0},{4,7},{5,6},{6,5},{7,4},{8,11},{9,10},{10,... | collective-permute-start | bytes 233480 | tf_op jit(solution)/shard_map/ppermute | solution.py:29
Sparse Core Ops, SparseCore 0:
  9.8 33.8 all-gather.8
  46.1 51.5 all-gather.4
  108.4 35.9 all-gather.6

commit v11 on v10

--- a/solution.py
+++ b/solution.py
@@ -88,12 +88,22 @@
             ]
 
 
+def inner_kernel(place, first, second, out):
+    def multiply(left, right):
+        out[...] = lax.dot_general(
+            left[...], right[...], (((1,), (1,)), ((), ())), preferred_element_type=f32
+        ).astype(bf16)
+
+    pl.when(place[0] == 1)(lambda: multiply(second, first))
+    pl.when(place[0] == 0)(lambda: multiply(first, second))
+
+
 def schur_kernel(place, *refs):
     separator, *pieces, schur, narrow = refs
     size = schur.shape[0]
     for step in range(SIDE):
         for k in range(SIDE):
-            columns = block_of(k * SIDE + (place[0] ^ step), size)
+            columns = block_of(k * place[1] + (place[0] ^ step) * place[2], size)
             value = separator[:, columns] - pieces[step][:, k * size : (k + 1) * size].astype(f32)
             schur[:, columns] = value
             narrow[:, columns] = value.astype(bf16)
@@ -125,6 +135,23 @@
     else:
         groups = [[i * SIDE + k for i in range(SIDE)] for k in range(SIDE)]
     return lax.all_gather(array, "blk", axis=0, tiled=True, axis_index_groups=groups)
+
+
+def over_other(array):
+    groups = []
+    for p in range(PARTITIONS):
+        for k in range(SIDE):
+            if p % 2 == 0:
+                groups.append([p * PLANE + i * SIDE + k for i in range(SIDE)])
+            else:
+                groups.append([p * PLANE + k * SIDE + i for i in range(SIDE)])
+    return lax.all_gather(array, AXES, axis=0, tiled=True, axis_index_groups=groups)
+
+
+def along_reduce(value, step):
+    return permuted(
+        value, lambda p, y, x: (p, y, x ^ step) if p % 2 == 0 else (p, y ^ step, x)
+    )
 
 
 def shards(interior_inverse, coupling, separator, link, source, weights):
@@ -140,6 +167,7 @@
     b = lax.axis_index("blk").astype(jnp.int32)
     y, x = b >> 2, b & 3
     even = (p & 1) == 0
+    r = jnp.where(even, x, y)
     pair = y >> 1
     ring = ((y + 1) >> 1) & 1
     out_place = jnp.where(even, y & 1, pair)
@@ -150,8 +178,8 @@
     away_high = jnp.where(even, 2 + ring, 3 - 2 * pair)
     place = jnp.stack([x, y])
 
-    coupling_in = over_axis(coupling_rows, "y")
-    outer = over_axis(jnp.concatenate([inverse_rows, coupling_rows], axis=1), "x")
+    first = over_axis(jnp.where(even, coupling_rows, inverse_rows), "y")
+    second = over_axis(jnp.where(even, inverse_rows, coupling_rows), "x")
 
     def ordered(pieces):
         stacked = jnp.stack(pieces)
@@ -185,6 +213,12 @@
         out_place == 0, jnp.concatenate([keep, got]), jnp.concatenate([got, keep])
     )
     pieces = spread_x(two)
+    coupling_late = tie(coupling_rows, two)
+    turned = jnp.where(
+        even,
+        coupling_late,
+        coupling_late.reshape(rows, SIDE, SIDE, rows).transpose(0, 2, 1, 3).reshape(rows, nodes),
+    )
     away_weights = permuted(line_weights, lambda p, y, x: (p, partner(p, y), x))
     (block,) = kernel_call(assemble_link, place, pieces, [shape((half, half), bf16)])
     weight_half = jnp.where(
@@ -199,18 +233,31 @@
         jnp.concatenate([zeros, line_values[:share]], axis=1),
     )
 
+    own = tie(own, turned)
+
     message = own.astype(bf16)
     final = message
     for turn in range(1, PARTITIONS):
         far, near = turn_messages(message, turn - 1)
         previous = (far.astype(f32) + near.astype(f32)).astype(bf16)
-        if turn == 10:
-            outer, coupling_in = tie((outer, coupling_in), message)
-            inner = lax.dot_general(
-                outer[:, :nodes], coupling_in, (((1,), (1,)), ((), ())), preferred_element_type=f32
-            ).astype(bf16)
-            inner_all = over_axis(inner, "y")
+        if turn == 8:
+            first, second = tie((first, second), message)
+            (inner,) = kernel_call(
+                inner_kernel,
+                jnp.stack([even.astype(jnp.int32)]),
+                [first, second],
+                [shape((line, line), bf16)],
+                flops=2 * line * line * nodes,
+            )
+            inner_all = over_other(inner)
             previous = tie(previous, inner)
+        if turn == 12:
+            turned = tie(turned, message)
+            coupling_out = [turned] + [along_reduce(turned, step) for step in (1, 2, 3)]
+        if turn == 14:
+            previous = tie(previous, coupling_out)
+        if turn == 15:
+            previous = tie(previous, inner_all)
         product = lax.dot_general(
             previous, block, (((1,), (1,)), ((), ())), preferred_element_type=f32
         )
@@ -220,7 +267,13 @@
     total = final.astype(f32) + permuted(
         final, lambda p, y, x: (p, partner(p, y), x)
     ).astype(f32)
-    rounded = total.astype(bf16)
+    folded = jnp.dot(
+        jnp.concatenate(coupling_out), inner_all, preferred_element_type=f32
+    ).astype(bf16)
+    back_rows = [folded[:rows]] + [
+        along_reduce(folded[step * rows : (step + 1) * rows], step) for step in (1, 2, 3)
+    ]
+    rounded = tie(total.astype(bf16), folded)
 
     back = jnp.dot(rounded, block, preferred_element_type=f32).astype(bf16)
     mine = lax.dynamic_slice(back, (0, in_place * line), (share, line))
@@ -258,18 +311,12 @@
         ]
         return jnp.concatenate([lines] + extra, axis=1)
 
+    lines = tie(lines, back_rows)
     last = exchange_x(last_chunk)
 
-    inner_all = tie(inner_all, rounded)
-    folded = jnp.dot(outer[:, nodes:], inner_all, preferred_element_type=f32).astype(bf16)
-
-    def folded_chunk(step):
-        return lax.dynamic_slice(folded, ((x ^ step) * rows, 0), (rows, line))
-
-    back_rows = exchange_x(folded_chunk)
     schur_rows, narrow = kernel_call(
         schur_kernel,
-        place,
+        jnp.stack([r, jnp.where(even, SIDE, 1), jnp.where(even, 1, SIDE)]),
         [separator_rows] + back_rows,
         [shape((rows, nodes), f32), shape((rows, nodes), bf16)],
     )

time: 175 us -> 178 us (1.017)
  waiting for transfers between devices: 83.6 us -> 66 us
  starting transfers between devices: 49.6 us -> 62.8 us
  local copies, waits for them, and re-layouts: 0.15 us -> 10.8 us
  matrix products: 17.9 us -> 12.6 us
  Pallas kernels: 4.48 us -> 6.56 us
    all_gather x3 -> x2, waiting for transfers between devices: 21.5 us -> 6.77 us  [over_axis(): lax.all_gather(array, 'blk', axis=0, tiled=True, axis_index_groups=groups)]
    ppermute x48 -> x51, starting transfers between devices: 49.5 us -> 62.7 us  [permuted(): return lax.ppermute(value, AXES, pairs)]
    unnamed x8 -> x34, local copies, waits for them, and re-layouts: 0.02 us -> 7.9 us
    dot_general x2 -> x1, matrix products: 7.76 us -> 2.45 us  [shards(): jnp.dot(jnp.concatenate(coupling_out), inner_all, preferred_element_type=...]
    select_n x0 -> x3, other arithmetic: none -> 3.21 us  [the longest x1 2.31 us: shards(): second = over_axis(jnp.where(even, inverse_rows, coupling_rows), 'x')]
    reshape x0 -> x3, local copies, waits for them, and re-layouts: none -> 2.81 us  [shards(): coupling_late.reshape(rows, SIDE, SIDE, rows).transpose(0, 2, 1, 3)]
    concatenate x1 -> x0, other arithmetic: 2.26 us -> none  [shards(): jnp.concatenate([inverse_rows, coupling_rows], axis=1)]
    ppermute x48 -> x51, waiting for transfers between devices: 61.4 us -> 59.2 us  [permuted(): return lax.ppermute(value, AXES, pairs)]
  transfers between devices with their start and end apart: 51 -> 54, of which waited for: 21 -> 18; matrix products, arithmetic and copies ran while one was open for 7% -> 9% of each run, Pallas kernels for 2% -> 2%
where the time goes in v11:
time: 178 us; the launch traced here: 177 us
  waiting for transfers between devices  66 us (37%)
  starting transfers between devices  62.8 us (35%)
  between operations  14.4 us (8%)
  matrix products  12.6 us (7%)
  local copies, waits for them, and re-layouts  10.8 us (6%)
  Pallas kernels  6.56 us (4%)
  other arithmetic  3.73 us (2%)
    ppermute x51, starting transfers between devices, permuted(): return lax.ppermute(value, AXES, pairs)  62.7 us
    ppermute x51, waiting for transfers between devices, permuted(): return lax.ppermute(value, AXES, pairs)  59.2 us
    dot_general x15, matrix products, shards(): lax.dot_general(previous, block, (((1,), (1,)), ((), ())), preferred_elem...  9.8 us
    unnamed x34, local copies, waits for them, and re-layouts  7.9 us
    all_gather x2, waiting for transfers between devices, over_axis(): lax.all_gather(array, 'blk', axis=0, tiled=True, axis_index_groups=groups)  6.77 us
    pallas_call x5, Pallas kernels, kernel_call(): pl.pallas_call(body, out_shape=out_shapes, in_specs=[pl.BlockSpec(memory_...  6.56 us
  transfers between devices with their start and end apart: 54, of which 18 were waited for; matrix products, arithmetic and copies ran while one was open for 9% of the time, Pallas kernels for 2%

profile of v11, /device:TPU:224, one launch (start us, length us, event | category | flops | bytes accessed | tf_op | source)
XLA Modules:
  0.0 177.0 jit_solution(10054109018428148022)
XLA Ops:
  7.2 2.3 %bitcast_select_fusion = (bf16[128,2048]{1,0:T(8,128)(2,1)}, bf16[128,2048]{1,0:T(8,128)(2,1)}) fusion(bf16[1,128,2048]{2,1,0:T(8,128)(2,1)} %param.6, pred[]{:T(512)S(6)} %eq.59, bf16[1,128,2048]{2,1,0:T(8,128)(2,1)} %param.7), kind=kLoop, calls=%fused_computation.57 | loop fusion | flops 524288 | bytes 2097153 | tf_op jit(solution)/shard_map/jit(_where)/select_n | solution.py:182
  9.7 1.6 collective-permute-start.1
  11.3 2.7 %collective-permute-start.2 = (f32[24,128]{1,0:T(8,128)S(1)}, f32[24,128]{1,0:T(8,128)S(1)}, u32[]{:S(2)}, u32[]{:S(2)}) collective-permute-start(f32[24,128]{1,0:T(8,128)S(1)} %get-tuple-element.83), channel_id=1, source_target_pairs={{0,2},{1,3},{2,0},{3,1},{4,6},{5,7},{6,4},{7,5},{8,10},{9,11},{10,... | collective-permute-start | bytes 36872 | tf_op jit(solution)/shard_map/ppermute | solution.py:29
  15.2 1.7 collective-permute-start
  17.0 1.9 %collective-permute-done.3 = f32[24,128]{1,0:T(8,128)S(1)} collective-permute-done((f32[24,128]{1,0:T(8,128)S(1)}, f32[24,128]{1,0:T(8,128)S(1)}, u32[]{:S(2)}, u32[]{:S(2)}) %collective-permute-start.3) | collective-permute-done | bytes 12320 | tf_op jit(solution)/shard_map/ppermute | solution.py:29
  19.0 2.7 %collective-permute-done = bf16[128,1024]{1,0:T(8,128)(2,1)S(1)} collective-permute-done((bf16[128,1024]{1,0:T(8,128)(2,1)S(1)}, bf16[128,1024]{1,0:T(8,128)(2,1)S(1)}, u32[]{:S(2)}, u32[]{:S(2)}) %collective-permute-start) | collective-permute-done | bytes 262176 | tf_op jit(solution)/shard_map/ppermute | solution.py:29
  22.2 3.9 %collective-permute-start.8 = (bf16[256,1024]{1,0:T(8,128)(2,1)S(1)}, bf16[256,1024]{1,0:T(8,128)(2,1)S(1)}, u32[]{:S(2)}, u32[]{:S(2)}) collective-permute-start(bf16[256,1024]{1,0:T(8,128)(2,1)S(1)} %maximum_select_fusion.refs_0_), channel_id=1, source_target_pairs={{0,2},{1,3},{2,0},{3,1},{4,6},{5,7},{6,4},{7,5},{8,10},{9,11},{10,... | collective-permute-start | bytes 1572872 | tf_op jit(solution)/shard_map/ppermute | solution.py:29
  27.0 1.0 copy.11
  28.0 1.4 reshape.47
  29.4 1.7 collective-permute-start.4
  31.1 0.9 broadcast_select_fusion
  32.1 1.0 collective-permute-done.4
  33.1 3.6 %collective-permute-done.7.refs_1_ = bf16[256,1024]{1,0:T(8,128)(2,1)S(1)} collective-permute-done((bf16[256,1024]{1,0:T(8,128)(2,1)S(1)}, bf16[256,1024]{1,0:T(8,128)(2,1)S(1)}, u32[]{:S(2)}, u32[]{:S(2)}) %collective-permute-start.7) | collective-permute-done | bytes 524320 | tf_op jit(solution)/shard_map/ppermute | solution.py:29
  36.8 11.6 %collective-permute-done.8.refs_2_ = bf16[256,1024]{1,0:T(8,128)(2,1)S(1)} collective-permute-done((bf16[256,1024]{1,0:T(8,128)(2,1)S(1)}, bf16[256,1024]{1,0:T(8,128)(2,1)S(1)}, u32[]{:S(2)}, u32[]{:S(2)}) %collective-permute-start.8) | collective-permute-done | bytes 524320 | tf_op jit(solution)/shard_map/ppermute | solution.py:29
  48.4 0.8 copy-done.3
  49.2 1.8 collective-permute-done.9.refs_3_
  51.0 0.8 copy-done.5
  51.8 1.0 copy-done.4
  52.8 1.0 copy-done.6
  53.8 0.7 shard_map.86
  55.2 0.7 collective-permute-start.10
  55.9 0.7 collective-permute-start.11
  56.6 0.7 fusion.27
  57.2 0.7 collective-permute-start.13
  57.9 2.6 %collective-permute-done.12 = bf16[16,1024]{1,0:T(8,128)(2,1)S(1)} collective-permute-done((bf16[16,1024]{1,0:T(8,128)(2,1)S(1)}, bf16[16,1024]{1,0:T(8,128)(2,1)S(1)}, u32[]{:S(2)}, u32[]{:S(2)}) %collective-permute-start.12) | collective-permute-done | bytes 32800 | tf_op jit(solution)/shard_map/ppermute | solution.py:29
  61.2 0.7 collective-permute-start.14
  61.9 0.7 collective-permute-start.15
  64.3 2.3 %collective-permute-done.16 = bf16[16,1024]{1,0:T(8,128)(2,1)S(1)} collective-permute-done((bf16[16,1024]{1,0:T(8,128)(2,1)S(1)}, bf16[16,1024]{1,0:T(8,128)(2,1)S(1)}, u32[]{:S(2)}, u32[]{:S(2)}) %collective-permute-start.16) | collective-permute-done | bytes 32800 | tf_op jit(solution)/shard_map/ppermute | solution.py:29
  67.2 0.7 collective-permute-start.18
  69.3 1.1 collective-permute-start.20
  70.4 2.4 %collective-permute-done.20 = bf16[16,1024]{1,0:T(8,128)(2,1)S(1)} collective-permute-done((bf16[16,1024]{1,0:T(8,128)(2,1)S(1)}, bf16[16,1024]{1,0:T(8,128)(2,1)S(1)}, u32[]{:S(2)}, u32[]{:S(2)}) %collective-permute-start.20) | collective-permute-done | bytes 32800 | tf_op jit(solution)/shard_map/ppermute | solution.py:29
  73.5 6.8 %all-gather.6.cloned.1.call-done.second = bf16[512,2048]{1,0:T(8,128)(2,1)} async-done(((bf16[128,2048]{1,0:T(8,128)(2,1)}), bf16[512,2048]{1,0:T(8,128)(2,1)}) %all-gather.6.cloned.1.call-update) | async-done | bytes 2097168 | tf_op jit(solution)/shard_map/all_gather | solution.py:137
  80.3 1.6 copy-done
  81.8 1.6 copy-done.1
  83.4 2.1 %shard_map.87 = bf16[512,512]{1,0:T(8,128)(2,1)} custom-call(s32[1]{0:T(128)} %bitcast.25.place, bf16[512,2048]{1,0:T(8,128)(2,1)S(1)} %copy-done, bf16[512,2048]{1,0:T(8,128)(2,1)S(1)} %copy-done.1), custom_call_target="tpu_custom_call" | custom-call | flops 1073741824 | bytes 4718592 | tf_op jit(solution)/shard_map/pallas_call | solution.py:58
  85.5 0.7 collective-permute-start.22
  86.2 0.7 collective-permute-start.23
  87.6 0.9 collective-permute-start.24
  88.5 0.7 collective-permute-start.25
  89.2 2.0 %collective-permute-done.24 = bf16[16,1024]{1,0:T(8,128)(2,1)S(1)} collective-permute-done((bf16[16,1024]{1,0:T(8,128)(2,1)S(1)}, bf16[16,1024]{1,0:T(8,128)(2,1)S(1)}, u32[]{:S(2)}, u32[]{:S(2)}) %collective-permute-start.24) | collective-permute-done | bytes 32800 | tf_op jit(solution)/shard_map/ppermute | solution.py:29
  91.9 0.7 collective-permute-start.26
  93.9 1.3 collective-permute-start.28
  95.6 1.8 collective-permute-done.28
  98.0 0.7 collective-permute-start.36
  100.0 1.2 collective-permute-start.38
  102.2 1.8 %collective-permute-start.31 = (bf16[128,2048]{1,0:T(8,128)(2,1)S(1)}, bf16[128,2048]{1,0:T(8,128)(2,1)S(1)}, u32[]{:S(2)}, u32[]{:S(2)}) collective-permute-start(bf16[128,2048]{1,0:T(8,128)(2,1)S(1)} %copy-done.10), channel_id=1, source_target_pairs={{0,2},{1,3},{2,0},{3,1},{4,6},{5,7},{6,4},{7,5},{8,10},{9,11},{10,... | collective-permute-start | bytes 1572872 | tf_op jit(solution)/shard_map/ppermute | solution.py:29
  103.9 2.4 %collective-permute-start.32 = (bf16[128,2048]{1,0:T(8,128)(2,1)S(1)}, bf16[128,2048]{1,0:T(8,128)(2,1)S(1)}, u32[]{:S(2)}, u32[]{:S(2)}) collective-permute-start(bf16[128,2048]{1,0:T(8,128)(2,1)S(1)} %copy-done.10), channel_id=1, source_target_pairs={{0,3},{1,2},{2,1},{3,0},{4,7},{5,6},{6,5},{7,4},{8,11},{9,10},{10,... | collective-permute-start | bytes 1572872 | tf_op jit(solution)/shard_map/ppermute | solution.py:29
  107.0 1.3 collective-permute-start.40
  108.3 1.3 collective-permute-start.41
  109.6 15.4 %collective-permute-done.40 = bf16[16,1024]{1,0:T(8,128)(2,1)S(1)} collective-permute-done((bf16[16,1024]{1,0:T(8,128)(2,1)S(1)}, bf16[16,1024]{1,0:T(8,128)(2,1)S(1)}, u32[]{:S(2)}, u32[]{:S(2)}) %collective-permute-start.40) | collective-permute-done | bytes 32800 | tf_op jit(solution)/shard_map/ppermute | solution.py:29
  126.8 2.9 %collective-permute-done.42 = bf16[16,1024]{1,0:T(8,128)(2,1)S(1)} collective-permute-done((bf16[16,1024]{1,0:T(8,128)(2,1)S(1)}, bf16[16,1024]{1,0:T(8,128)(2,1)S(1)}, u32[]{:S(2)}, u32[]{:S(2)}) %collective-permute-start.42) | collective-permute-done | bytes 32800 | tf_op jit(solution)/shard_map/ppermute | solution.py:29
  129.7 0.7 fusion.41
  131.4 2.5 %fusion.8 = bf16[512,512]{1,0:T(8,128)(2,1)S(1)} fusion(bf16[2048,512]{1,0:T(8,128)(2,1)S(1)} %copy-done.12, bf16[128,2048]{1,0:T(8,128)(2,1)} %copy-done.16, bf16[128,2048]{1,0:T(8,128)(2,1)} %copy-done.15, bf16[128,2048]{1,0:T(8,128)(2,1)S(1)} %copy-done.14, bf16[128,2048]{1,0:T(8,128)(2,1)S(1)} %copy-done.10), kind=kOutput, calls=%fused_computation.8 | convolution fusion | flops 1082392576 | bytes 4718592 | tf_op jit(solution)/shard_map/dot_general | solution.py:270
  134.5 1.8 collective-permute-start.34
  136.3 2.4 %collective-permute-start.35 = (bf16[128,512]{1,0:T(8,128)(2,1)S(1)}, bf16[128,512]{1,0:T(8,128)(2,1)S(1)}, u32[]{:S(2)}, u32[]{:S(2)}) collective-permute-start(bf16[128,512]{1,0:T(8,128)(2,1)S(1)} %get-tuple-element.45), channel_id=1, source_target_pairs={{0,3},{1,2},{2,1},{3,0},{4,7},{5,6},{6,5},{7,4},{8,11},{9,10},{10,... | collective-permute-start | bytes 393224 | tf_op jit(solution)/shard_map/ppermute | solution.py:29
  139.1 11.9 %collective-permute-start.46 = (bf16[16,512]{1,0:T(8,128)(2,1)S(1)}, bf16[16,512]{1,0:T(8,128)(2,1)S(1)}, u32[]{:S(2)}, u32[]{:S(2)}) collective-permute-start(bf16[16,512]{1,0:T(8,128)(2,1)S(1)} %get-tuple-element.63), channel_id=1, source_target_pairs={{16,4},{17,5},{18,6},{19,7},{20,0},{21,1},{22,2},{23,3},{24,12},{2... | collective-permute-start | bytes 49160 | tf_op jit(solution)/shard_map/ppermute | solution.py:29
  151.0 3.1 %collective-permute-start.47 = (bf16[16,512]{1,0:T(8,128)(2,1)S(1)}, bf16[16,512]{1,0:T(8,128)(2,1)S(1)}, u32[]{:S(2)}, u32[]{:S(2)}) collective-permute-start(bf16[16,512]{1,0:T(8,128)(2,1)S(1)} %get-tuple-element.64), channel_id=1, source_target_pairs={{16,0},{17,1},{18,2},{19,3},{20,4},{21,5},{22,6},{23,7},{24,8},{25... | collective-permute-start | bytes 49160 | tf_op jit(solution)/shard_map/ppermute | solution.py:29
  154.2 1.6 collective-permute-start.45
  155.8 3.6 %collective-permute-done.45 = bf16[16,1024]{1,0:T(8,128)(2,1)S(1)} collective-permute-done((bf16[16,1024]{1,0:T(8,128)(2,1)S(1)}, bf16[16,1024]{1,0:T(8,128)(2,1)S(1)}, u32[]{:S(2)}, u32[]{:S(2)}) %collective-permute-start.45) | collective-permute-done | bytes 32800 | tf_op jit(solution)/shard_map/ppermute | solution.py:29
  159.6 3.8 %collective-permute-start.49 = (bf16[16,2432]{1,0:T(8,128)(2,1)S(1)}, bf16[16,2432]{1,0:T(8,128)(2,1)S(1)}, u32[]{:S(2)}, u32[]{:S(2)}) collective-permute-start(bf16[16,2432]{1,0:T(8,128)(2,1)S(1)} %get-tuple-element.51), channel_id=1, source_target_pairs={{0,2},{1,3},{2,0},{3,1},{4,6},{5,7},{6,4},{7,5},{8,10},{9,11},{10,... | collective-permute-start | bytes 233480 | tf_op jit(solution)/shard_map/ppermute | solution.py:29
  163.4 0.8 collective-permute-start.50
  164.3 1.8 shard_map.88
  166.6 2.4 %collective-permute-done.50.refs_3_ = bf16[16,2432]{1,0:T(8,128)(2,1)S(1)} collective-permute-done((bf16[16,2432]{1,0:T(8,128)(2,1)S(1)}, bf16[16,2432]{1,0:T(8,128)(2,1)S(1)}, u32[]{:S(2)}, u32[]{:S(2)}) %collective-permute-start.50) | collective-permute-done | bytes 77856 | tf_op jit(solution)/shard_map/ppermute | solution.py:29
  169.0 1.5 shard_map.89
  (138 shorter events, 19.8 us)
Async XLA Ops:
  7.2 2.5 %copy-start.8 = (f32[1,128]{1,0:T(1,128)S(1)}, f32[1,128]{1,0:T(1,128)}, u32[]{:S(2)}) copy-start(f32[1,128]{1,0:T(1,128)} %weight.1) | copy-start | bytes 1540
  7.2 2.5 %copy-start.11 = (f32[1,64,128]{2,1,0:T(8,128)S(1)}, f32[1,64,128]{2,1,0:T(8,128)}, u32[]{:S(2)}) copy-start(f32[1,64,128]{2,1,0:T(8,128)} %param.10) | copy-start | bytes 98308
  7.2 7.4 %copy-start.7 = (bf16[1,128,2048]{2,1,0:T(8,128)(2,1)S(1)}, bf16[1,128,2048]{2,1,0:T(8,128)(2,1)}, u32[]{:S(2)}) copy-start(bf16[1,128,2048]{2,1,0:T(8,128)(2,1)} %param.9) | copy-start | bytes 1572868
  7.2 66.3 %all-gather.4.cloned.1.call-start = ((), (), s32[]{:S(2)}) async-start(), calls=%async_computation | async-start | bytes 2621440 | tf_op jit(solution)/shard_map/all_gather | solution.py:137
  9.6 17.0 %copy-start.9 = (bf16[1,128,2048]{2,1,0:T(8,128)(2,1)S(1)}, bf16[1,128,2048]{2,1,0:T(8,128)(2,1)}, u32[]{:S(2)}) copy-start(bf16[1,128,2048]{2,1,0:T(8,128)(2,1)} %param.7) | copy-start | bytes 1572868
  9.6 70.7 %all-gather.6.cloned.1.call-start = ((), (), s32[]{:S(2)}) async-start(), calls=%async_computation.1 | async-start | bytes 2621440 | tf_op jit(solution)/shard_map/all_gather | solution.py:137
  9.7 7.3 %collective-permute-start.1 = (f32[24,128]{1,0:T(8,128)S(1)}, f32[24,128]{1,0:T(8,128)S(1)}, u32[]{:S(2)}, u32[]{:S(2)}) collective-permute-start(f32[24,128]{1,0:T(8,128)S(1)} %get-tuple-element.82), channel_id=1, source_target_pairs={{0,1},{1,0},{2,3},{3,2},{4,5},{5,4},{6,7},{7,6},{8,9},{9,8},{10,11... | collective-permute-start | bytes 36872 | tf_op jit(solution)/shard_map/ppermute | solution.py:29
  11.3 5.7 %collective-permute-start.2 = (f32[24,128]{1,0:T(8,128)S(1)}, f32[24,128]{1,0:T(8,128)S(1)}, u32[]{:S(2)}, u32[]{:S(2)}) collective-permute-start(f32[24,128]{1,0:T(8,128)S(1)} %get-tuple-element.83), channel_id=1, source_target_pairs={{0,2},{1,3},{2,0},{3,1},{4,6},{5,7},{6,4},{7,5},{8,10},{9,11},{10,... | collective-permute-start | bytes 36872 | tf_op jit(solution)/shard_map/ppermute | solution.py:29
  14.1 4.9 %collective-permute-start.3 = (f32[24,128]{1,0:T(8,128)S(1)}, f32[24,128]{1,0:T(8,128)S(1)}, u32[]{:S(2)}, u32[]{:S(2)}) collective-permute-start(f32[24,128]{1,0:T(8,128)S(1)} %get-tuple-element.84), channel_id=1, source_target_pairs={{0,3},{1,2},{2,1},{3,0},{4,7},{5,6},{6,5},{7,4},{8,11},{9,10},{10,... | collective-permute-start | bytes 36872 | tf_op jit(solution)/shard_map/ppermute | solution.py:29
  15.2 6.5 %collective-permute-start = (bf16[128,1024]{1,0:T(8,128)(2,1)S(1)}, bf16[128,1024]{1,0:T(8,128)(2,1)S(1)}, u32[]{:S(2)}, u32[]{:S(2)}) collective-permute-start(bf16[128,1024]{1,0:T(8,128)(2,1)S(1)} %get-tuple-element.23), channel_id=1, source_target_pairs={{0,4},{1,5},{2,6},{3,7},{4,0},{5,1},{6,2},{7,3},{8,12},{9,13},{10,... | collective-permute-start | bytes 786440 | tf_op jit(solution)/shard_map/ppermute | solution.py:29
  16.9 112.8 %all-gather.8.cloned.1.call-start = ((), (), s32[]{:S(2)}) async-start(), calls=%async_computation.2 | async-start | bytes 2621440 | tf_op jit(solution)/shard_map/all_gather | solution.py:148
  21.8 14.9 %collective-permute-start.7 = (bf16[256,1024]{1,0:T(8,128)(2,1)S(1)}, bf16[256,1024]{1,0:T(8,128)(2,1)S(1)}, u32[]{:S(2)}, u32[]{:S(2)}) collective-permute-start(bf16[256,1024]{1,0:T(8,128)(2,1)S(1)} %maximum_select_fusion.refs_0_), channel_id=1, source_target_pairs={{0,1},{1,0},{2,3},{3,2},{4,5},{5,4},{6,7},{7,6},{8,9},{9,8},{10,11... | collective-permute-start | bytes 1572872 | tf_op jit(solution)/shard_map/ppermute | solution.py:29
  22.2 26.2 %collective-permute-start.8 = (bf16[256,1024]{1,0:T(8,128)(2,1)S(1)}, bf16[256,1024]{1,0:T(8,128)(2,1)S(1)}, u32[]{:S(2)}, u32[]{:S(2)}) collective-permute-start(bf16[256,1024]{1,0:T(8,128)(2,1)S(1)} %maximum_select_fusion.refs_0_), channel_id=1, source_target_pairs={{0,2},{1,3},{2,0},{3,1},{4,6},{5,7},{6,4},{7,5},{8,10},{9,11},{10,... | collective-permute-start | bytes 1572872 | tf_op jit(solution)/shard_map/ppermute | solution.py:29
  26.1 24.8 %collective-permute-start.9 = (bf16[256,1024]{1,0:T(8,128)(2,1)S(1)}, bf16[256,1024]{1,0:T(8,128)(2,1)S(1)}, u32[]{:S(2)}, u32[]{:S(2)}) collective-permute-start(bf16[256,1024]{1,0:T(8,128)(2,1)S(1)} %maximum_select_fusion.refs_0_), channel_id=1, source_target_pairs={{0,3},{1,2},{2,1},{3,0},{4,7},{5,6},{6,5},{7,4},{8,11},{9,10},{10,... | collective-permute-start | bytes 1572872 | tf_op jit(solution)/shard_map/ppermute | solution.py:29
  29.4 3.7 %collective-permute-start.4 = (f32[1,512]{1,0:T(1,128)S(1)}, f32[1,512]{1,0:T(1,128)S(1)}, u32[]{:S(2)}, u32[]{:S(2)}) collective-permute-start(f32[1,512]{1,0:T(1,128)S(1)} %slice.38), channel_id=1, source_target_pairs={{0,4},{1,5},{2,6},{3,7},{4,0},{5,1},{6,2},{7,3},{8,12},{9,13},{10,... | collective-permute-start | bytes 6152 | tf_op jit(solution)/shard_map/ppermute | solution.py:29
  32.0 22.5 %collective-permute-start.5 = (bf16[16,1024]{1,0:T(8,128)(2,1)S(1)}, bf16[16,1024]{1,0:T(8,128)(2,1)S(1)}, u32[]{:S(2)}, u32[]{:S(2)}) collective-permute-start(bf16[16,1024]{1,0:T(8,128)(2,1)S(1)} %convert_element_type.217), channel_id=1, source_target_pairs={{0,20},{1,21},{2,22},{3,23},{4,16},{5,17},{6,18},{7,19},{8,28},{9,... | collective-permute-start | bytes 98312 | tf_op jit(solution)/shard_map/ppermute | solution.py:29
  33.1 21.4 %collective-permute-start.6 = (bf16[16,1024]{1,0:T(8,128)(2,1)S(1)}, bf16[16,1024]{1,0:T(8,128)(2,1)S(1)}, u32[]{:S(2)}, u32[]{:S(2)}) collective-permute-start(bf16[16,1024]{1,0:T(8,128)(2,1)S(1)} %convert_element_type.217), channel_id=1, source_target_pairs={{0,16},{1,17},{2,18},{3,19},{4,20},{5,21},{6,22},{7,23},{8,24},{9,... | collective-permute-start | bytes 98312 | tf_op jit(solution)/shard_map/ppermute | solution.py:29
  55.2 1.3 collective-permute-start.10
  55.9 0.7 collective-permute-start.11
  57.2 3.3 %collective-permute-start.12 = (bf16[16,1024]{1,0:T(8,128)(2,1)S(1)}, bf16[16,1024]{1,0:T(8,128)(2,1)S(1)}, u32[]{:S(2)}, u32[]{:S(2)}) collective-permute-start(bf16[16,1024]{1,0:T(8,128)(2,1)S(1)} %fusion.27), channel_id=1, source_target_pairs={{0,20},{1,21},{2,22},{3,23},{4,16},{5,17},{6,18},{7,19},{8,28},{9,... | collective-permute-start | bytes 98312 | tf_op jit(solution)/shard_map/ppermute | solution.py:29
  57.2 3.3 %collective-permute-start.13 = (bf16[16,1024]{1,0:T(8,128)(2,1)S(1)}, bf16[16,1024]{1,0:T(8,128)(2,1)S(1)}, u32[]{:S(2)}, u32[]{:S(2)}) collective-permute-start(bf16[16,1024]{1,0:T(8,128)(2,1)S(1)} %fusion.27), channel_id=1, source_target_pairs={{0,16},{1,17},{2,18},{3,19},{4,20},{5,21},{6,22},{7,23},{8,24},{9,... | collective-permute-start | bytes 98312 | tf_op jit(solution)/shard_map/ppermute | solution.py:29
  61.2 1.3 collective-permute-start.14
  61.9 0.7 collective-permute-start.15
  63.2 3.3 %collective-permute-start.16 = (bf16[16,1024]{1,0:T(8,128)(2,1)S(1)}, bf16[16,1024]{1,0:T(8,128)(2,1)S(1)}, u32[]{:S(2)}, u32[]{:S(2)}) collective-permute-start(bf16[16,1024]{1,0:T(8,128)(2,1)S(1)} %fusion.29), channel_id=1, source_target_pairs={{0,20},{1,21},{2,22},{3,23},{4,16},{5,17},{6,18},{7,19},{8,28},{9,... | collective-permute-start | bytes 98312 | tf_op jit(solution)/shard_map/ppermute | solution.py:29
  63.9 2.7 %collective-permute-start.17 = (bf16[16,1024]{1,0:T(8,128)(2,1)S(1)}, bf16[16,1024]{1,0:T(8,128)(2,1)S(1)}, u32[]{:S(2)}, u32[]{:S(2)}) collective-permute-start(bf16[16,1024]{1,0:T(8,128)(2,1)S(1)} %fusion.29), channel_id=1, source_target_pairs={{0,16},{1,17},{2,18},{3,19},{4,20},{5,21},{6,22},{7,23},{8,24},{9,... | collective-permute-start | bytes 98312 | tf_op jit(solution)/shard_map/ppermute | solution.py:29
  67.2 1.3 collective-permute-start.18
  67.9 0.7 collective-permute-start.19
  69.3 3.6 %collective-permute-start.20 = (bf16[16,1024]{1,0:T(8,128)(2,1)S(1)}, bf16[16,1024]{1,0:T(8,128)(2,1)S(1)}, u32[]{:S(2)}, u32[]{:S(2)}) collective-permute-start(bf16[16,1024]{1,0:T(8,128)(2,1)S(1)} %fusion.31), channel_id=1, source_target_pairs={{0,20},{1,21},{2,22},{3,23},{4,16},{5,17},{6,18},{7,19},{8,28},{9,... | collective-permute-start | bytes 98312 | tf_op jit(solution)/shard_map/ppermute | solution.py:29
  70.4 2.5 %collective-permute-start.21 = (bf16[16,1024]{1,0:T(8,128)(2,1)S(1)}, bf16[16,1024]{1,0:T(8,128)(2,1)S(1)}, u32[]{:S(2)}, u32[]{:S(2)}) collective-permute-start(bf16[16,1024]{1,0:T(8,128)(2,1)S(1)} %fusion.31), channel_id=1, source_target_pairs={{0,16},{1,17},{2,18},{3,19},{4,20},{5,21},{6,22},{7,23},{8,24},{9,... | collective-permute-start | bytes 98312 | tf_op jit(solution)/shard_map/ppermute | solution.py:29
  80.2 1.6 copy-start
  81.8 1.6 copy-start.1
  85.5 1.3 collective-permute-start.22
  86.2 0.7 collective-permute-start.23
  87.6 3.7 %collective-permute-start.24 = (bf16[16,1024]{1,0:T(8,128)(2,1)S(1)}, bf16[16,1024]{1,0:T(8,128)(2,1)S(1)}, u32[]{:S(2)}, u32[]{:S(2)}) collective-permute-start(bf16[16,1024]{1,0:T(8,128)(2,1)S(1)} %fusion.33), channel_id=1, source_target_pairs={{0,20},{1,21},{2,22},{3,23},{4,16},{5,17},{6,18},{7,19},{8,28},{9,... | collective-permute-start | bytes 98312 | tf_op jit(solution)/shard_map/ppermute | solution.py:29
  88.5 2.7 %collective-permute-start.25 = (bf16[16,1024]{1,0:T(8,128)(2,1)S(1)}, bf16[16,1024]{1,0:T(8,128)(2,1)S(1)}, u32[]{:S(2)}, u32[]{:S(2)}) collective-permute-start(bf16[16,1024]{1,0:T(8,128)(2,1)S(1)} %fusion.33), channel_id=1, source_target_pairs={{0,16},{1,17},{2,18},{3,19},{4,20},{5,21},{6,22},{7,23},{8,24},{9,... | collective-permute-start | bytes 98312 | tf_op jit(solution)/shard_map/ppermute | solution.py:29
  91.9 1.3 collective-permute-start.26
  92.6 0.7 collective-permute-start.27
  93.9 7.7 %copy-start.10 = (bf16[128,2048]{1,0:T(8,128)(2,1)S(1)}, bf16[128,2048]{1,0:T(8,128)(2,1)}, u32[]{:S(2)}) copy-start(bf16[128,2048]{1,0:T(8,128)(2,1)} %broadcast_select_fusion) | copy-start | bytes 1572868
  93.9 3.4 %collective-permute-start.28 = (bf16[16,1024]{1,0:T(8,128)(2,1)S(1)}, bf16[16,1024]{1,0:T(8,128)(2,1)S(1)}, u32[]{:S(2)}, u32[]{:S(2)}) collective-permute-start(bf16[16,1024]{1,0:T(8,128)(2,1)S(1)} %fusion.35), channel_id=1, source_target_pairs={{0,20},{1,21},{2,22},{3,23},{4,16},{5,17},{6,18},{7,19},{8,28},{9,... | collective-permute-start | bytes 98312 | tf_op jit(solution)/shard_map/ppermute | solution.py:29
  95.2 2.2 %collective-permute-start.29 = (bf16[16,1024]{1,0:T(8,128)(2,1)S(1)}, bf16[16,1024]{1,0:T(8,128)(2,1)S(1)}, u32[]{:S(2)}, u32[]{:S(2)}) collective-permute-start(bf16[16,1024]{1,0:T(8,128)(2,1)S(1)} %fusion.35), channel_id=1, source_target_pairs={{0,16},{1,17},{2,18},{3,19},{4,20},{5,21},{6,22},{7,23},{8,24},{9,... | collective-permute-start | bytes 98312 | tf_op jit(solution)/shard_map/ppermute | solution.py:29
  98.0 1.3 collective-permute-start.36
  98.6 0.7 collective-permute-start.37
  100.0 6.3 %collective-permute-start.38 = (bf16[16,1024]{1,0:T(8,128)(2,1)S(1)}, bf16[16,1024]{1,0:T(8,128)(2,1)S(1)}, u32[]{:S(2)}, u32[]{:S(2)}) collective-permute-start(bf16[16,1024]{1,0:T(8,128)(2,1)S(1)} %fusion.37), channel_id=1, source_target_pairs={{0,20},{1,21},{2,22},{3,23},{4,16},{5,17},{6,18},{7,19},{8,28},{9,... | collective-permute-start | bytes 98312 | tf_op jit(solution)/shard_map/ppermute | solution.py:29
  101.2 5.1 %collective-permute-start.39 = (bf16[16,1024]{1,0:T(8,128)(2,1)S(1)}, bf16[16,1024]{1,0:T(8,128)(2,1)S(1)}, u32[]{:S(2)}, u32[]{:S(2)}) collective-permute-start(bf16[16,1024]{1,0:T(8,128)(2,1)S(1)} %fusion.37), channel_id=1, source_target_pairs={{0,16},{1,17},{2,18},{3,19},{4,20},{5,21},{6,22},{7,23},{8,24},{9,... | collective-permute-start | bytes 98312 | tf_op jit(solution)/shard_map/ppermute | solution.py:29
  101.6 23.9 %collective-permute-start.30 = (bf16[128,2048]{1,0:T(8,128)(2,1)S(1)}, bf16[128,2048]{1,0:T(8,128)(2,1)S(1)}, u32[]{:S(2)}, u32[]{:S(2)}) collective-permute-start(bf16[128,2048]{1,0:T(8,128)(2,1)S(1)} %copy-done.10), channel_id=1, source_target_pairs={{0,1},{1,0},{2,3},{3,2},{4,5},{5,4},{6,7},{7,6},{8,9},{9,8},{10,11... | collective-permute-start | bytes 1572872 | tf_op jit(solution)/shard_map/ppermute | solution.py:29
  102.2 23.4 %collective-permute-start.31 = (bf16[128,2048]{1,0:T(8,128)(2,1)S(1)}, bf16[128,2048]{1,0:T(8,128)(2,1)S(1)}, u32[]{:S(2)}, u32[]{:S(2)}) collective-permute-start(bf16[128,2048]{1,0:T(8,128)(2,1)S(1)} %copy-done.10), channel_id=1, source_target_pairs={{0,2},{1,3},{2,0},{3,1},{4,6},{5,7},{6,4},{7,5},{8,10},{9,11},{10,... | collective-permute-start | bytes 1572872 | tf_op jit(solution)/shard_map/ppermute | solution.py:29
  103.9 21.6 %collective-permute-start.32 = (bf16[128,2048]{1,0:T(8,128)(2,1)S(1)}, bf16[128,2048]{1,0:T(8,128)(2,1)S(1)}, u32[]{:S(2)}, u32[]{:S(2)}) collective-permute-start(bf16[128,2048]{1,0:T(8,128)(2,1)S(1)} %copy-done.10), channel_id=1, source_target_pairs={{0,3},{1,2},{2,1},{3,0},{4,7},{5,6},{6,5},{7,4},{8,11},{9,10},{10,... | collective-permute-start | bytes 1572872 | tf_op jit(solution)/shard_map/ppermute | solution.py:29
  107.0 18.0 %collective-permute-start.40 = (bf16[16,1024]{1,0:T(8,128)(2,1)S(1)}, bf16[16,1024]{1,0:T(8,128)(2,1)S(1)}, u32[]{:S(2)}, u32[]{:S(2)}) collective-permute-start(bf16[16,1024]{1,0:T(8,128)(2,1)S(1)} %fusion.38), channel_id=1, source_target_pairs={{208,236},{209,237},{210,238},{211,239},{212,232},{213,233},{214,2... | collective-permute-start | bytes 98312 | tf_op jit(solution)/shard_map/ppermute | solution.py:29
  108.3 17.2 %collective-permute-start.41 = (bf16[16,1024]{1,0:T(8,128)(2,1)S(1)}, bf16[16,1024]{1,0:T(8,128)(2,1)S(1)}, u32[]{:S(2)}, u32[]{:S(2)}) collective-permute-start(bf16[16,1024]{1,0:T(8,128)(2,1)S(1)} %fusion.38), channel_id=1, source_target_pairs={{208,224},{209,225},{210,226},{211,227},{212,228},{213,229},{214,2... | collective-permute-start | bytes 98312 | tf_op jit(solution)/shard_map/ppermute | solution.py:29
  126.3 3.3 %collective-permute-start.42 = (bf16[16,1024]{1,0:T(8,128)(2,1)S(1)}, bf16[16,1024]{1,0:T(8,128)(2,1)S(1)}, u32[]{:S(2)}, u32[]{:S(2)}) collective-permute-start(bf16[16,1024]{1,0:T(8,128)(2,1)S(1)} %fusion.39), channel_id=1, source_target_pairs={{0,20},{1,21},{2,22},{3,23},{4,16},{5,17},{6,18},{7,19},{8,28},{9,... | collective-permute-start | bytes 98312 | tf_op jit(solution)/shard_map/ppermute | solution.py:29
  126.7 3.0 %collective-permute-start.43 = (bf16[16,1024]{1,0:T(8,128)(2,1)S(1)}, bf16[16,1024]{1,0:T(8,128)(2,1)S(1)}, u32[]{:S(2)}, u32[]{:S(2)}) collective-permute-start(bf16[16,1024]{1,0:T(8,128)(2,1)S(1)} %fusion.39), channel_id=1, source_target_pairs={{0,16},{1,17},{2,18},{3,19},{4,20},{5,21},{6,22},{7,23},{8,24},{9,... | collective-permute-start | bytes 98312 | tf_op jit(solution)/shard_map/ppermute | solution.py:29
  129.7 1.6 copy-start.12
  129.7 1.7 copy-start.14
  130.4 8.3 %collective-permute-start.44 = (bf16[16,1024]{1,0:T(8,128)(2,1)S(1)}, bf16[16,1024]{1,0:T(8,128)(2,1)S(1)}, u32[]{:S(2)}, u32[]{:S(2)}) collective-permute-start(bf16[16,1024]{1,0:T(8,128)(2,1)S(1)} %fusion.41), channel_id=1, source_target_pairs={{0,4},{1,5},{2,6},{3,7},{4,0},{5,1},{6,2},{7,3},{8,12},{9,13},{10,... | collective-permute-start | bytes 98312 | tf_op jit(solution)/shard_map/ppermute | solution.py:29
  133.9 30.5 %copy-start.2 = (f32[1,128,2048]{2,1,0:T(8,128)S(1)}, f32[1,128,2048]{2,1,0:T(8,128)}, u32[]{:S(2)}) copy-start(f32[1,128,2048]{2,1,0:T(8,128)} %param.8) | copy-start | bytes 3145732
  133.9 25.5 %collective-permute-start.33 = (bf16[128,512]{1,0:T(8,128)(2,1)S(1)}, bf16[128,512]{1,0:T(8,128)(2,1)S(1)}, u32[]{:S(2)}, u32[]{:S(2)}) collective-permute-start(bf16[128,512]{1,0:T(8,128)(2,1)S(1)} %get-tuple-element.47), channel_id=1, source_target_pairs={{0,1},{1,0},{2,3},{3,2},{4,5},{5,4},{6,7},{7,6},{8,9},{9,8},{10,11... | collective-permute-start | bytes 393224 | tf_op jit(solution)/shard_map/ppermute | solution.py:29
  134.5 24.9 %collective-permute-start.34 = (bf16[128,512]{1,0:T(8,128)(2,1)S(1)}, bf16[128,512]{1,0:T(8,128)(2,1)S(1)}, u32[]{:S(2)}, u32[]{:S(2)}) collective-permute-start(bf16[128,512]{1,0:T(8,128)(2,1)S(1)} %get-tuple-element.46), channel_id=1, source_target_pairs={{0,2},{1,3},{2,0},{3,1},{4,6},{5,7},{6,4},{7,5},{8,10},{9,11},{10,... | collective-permute-start | bytes 393224 | tf_op jit(solution)/shard_map/ppermute | solution.py:29
  136.3 23.1 %collective-permute-start.35 = (bf16[128,512]{1,0:T(8,128)(2,1)S(1)}, bf16[128,512]{1,0:T(8,128)(2,1)S(1)}, u32[]{:S(2)}, u32[]{:S(2)}) collective-permute-start(bf16[128,512]{1,0:T(8,128)(2,1)S(1)} %get-tuple-element.45), channel_id=1, source_target_pairs={{0,3},{1,2},{2,1},{3,0},{4,7},{5,6},{6,5},{7,4},{8,11},{9,10},{10,... | collective-permute-start | bytes 393224 | tf_op jit(solution)/shard_map/ppermute | solution.py:29
  139.1 15.0 %collective-permute-start.46 = (bf16[16,512]{1,0:T(8,128)(2,1)S(1)}, bf16[16,512]{1,0:T(8,128)(2,1)S(1)}, u32[]{:S(2)}, u32[]{:S(2)}) collective-permute-start(bf16[16,512]{1,0:T(8,128)(2,1)S(1)} %get-tuple-element.63), channel_id=1, source_target_pairs={{16,4},{17,5},{18,6},{19,7},{20,0},{21,1},{22,2},{23,3},{24,12},{2... | collective-permute-start | bytes 49160 | tf_op jit(solution)/shard_map/ppermute | solution.py:29
  151.0 4.7 %collective-permute-start.47 = (bf16[16,512]{1,0:T(8,128)(2,1)S(1)}, bf16[16,512]{1,0:T(8,128)(2,1)S(1)}, u32[]{:S(2)}, u32[]{:S(2)}) collective-permute-start(bf16[16,512]{1,0:T(8,128)(2,1)S(1)} %get-tuple-element.64), channel_id=1, source_target_pairs={{16,0},{17,1},{18,2},{19,3},{20,4},{21,5},{22,6},{23,7},{24,8},{25... | collective-permute-start | bytes 49160 | tf_op jit(solution)/shard_map/ppermute | solution.py:29
  154.2 5.2 %collective-permute-start.45 = (bf16[16,1024]{1,0:T(8,128)(2,1)S(1)}, bf16[16,1024]{1,0:T(8,128)(2,1)S(1)}, u32[]{:S(2)}, u32[]{:S(2)}) collective-permute-start(bf16[16,1024]{1,0:T(8,128)(2,1)S(1)} %get-tuple-element.37), channel_id=1, source_target_pairs={{0,12},{1,13},{2,14},{3,15},{4,8},{5,9},{6,10},{7,11},{8,4},{9,5},... | collective-permute-start | bytes 98312 | tf_op jit(solution)/shard_map/ppermute | solution.py:29
  159.5 6.6 %collective-permute-start.48 = (bf16[16,2432]{1,0:T(8,128)(2,1)S(1)}, bf16[16,2432]{1,0:T(8,128)(2,1)S(1)}, u32[]{:S(2)}, u32[]{:S(2)}) collective-permute-start(bf16[16,2432]{1,0:T(8,128)(2,1)S(1)} %get-tuple-element.50), channel_id=1, source_target_pairs={{0,1},{1,0},{2,3},{3,2},{4,5},{5,4},{6,7},{7,6},{8,9},{9,8},{10,11... | collective-permute-start | bytes 233480 | tf_op jit(solution)/shard_map/ppermute | solution.py:29
  159.6 7.0 %collective-permute-start.49 = (bf16[16,2432]{1,0:T(8,128)(2,1)S(1)}, bf16[16,2432]{1,0:T(8,128)(2,1)S(1)}, u32[]{:S(2)}, u32[]{:S(2)}) collective-permute-start(bf16[16,2432]{1,0:T(8,128)(2,1)S(1)} %get-tuple-element.51), channel_id=1, source_target_pairs={{0,2},{1,3},{2,0},{3,1},{4,6},{5,7},{6,4},{7,5},{8,10},{9,11},{10,... | collective-permute-start | bytes 233480 | tf_op jit(solution)/shard_map/ppermute | solution.py:29
  163.4 5.6 %collective-permute-start.50 = (bf16[16,2432]{1,0:T(8,128)(2,1)S(1)}, bf16[16,2432]{1,0:T(8,128)(2,1)S(1)}, u32[]{:S(2)}, u32[]{:S(2)}) collective-permute-start(bf16[16,2432]{1,0:T(8,128)(2,1)S(1)} %get-tuple-element.49), channel_id=1, source_target_pairs={{0,3},{1,2},{2,1},{3,0},{4,7},{5,6},{6,5},{7,4},{8,11},{9,10},{10,... | collective-permute-start | bytes 233480 | tf_op jit(solution)/shard_map/ppermute | solution.py:29
  (7 other events, 6.6 us)
Sparse Core Ops, SparseCore 0:
  9.8 33.8 all-gather.3
  46.1 34.0 all-gather.5
  85.7 31.3 all-gather.7

commit v12 on v11

--- a/solution.py
+++ b/solution.py
@@ -51,15 +51,17 @@
     return lax.optimization_barrier((values, others))[0]
 
 
-def kernel_call(body, place, operands, out_shapes, flops=0):
+def kernel_call(body, place, operands, out_shapes, flops=0, space=pltpu.VMEM, scratch=()):
     out_bytes = sum(s.size * s.dtype.itemsize for s in out_shapes)
     in_bytes = sum(o.size * o.dtype.itemsize for o in operands)
     whole = pl.BlockSpec(memory_space=pltpu.VMEM)
     return pl.pallas_call(
         body,
         out_shape=out_shapes,
-        in_specs=[pl.BlockSpec(memory_space=pltpu.SMEM)] + [whole] * len(operands),
+        in_specs=[pl.BlockSpec(memory_space=pltpu.SMEM)]
+        + [pl.BlockSpec(memory_space=space)] * len(operands),
         out_specs=[whole] * len(out_shapes),
+        scratch_shapes=scratch,
         compiler_params=pltpu.CompilerParams(vmem_limit_bytes=24 * 1024 * 1024),
         cost_estimate=pl.CostEstimate(
             flops=flops, bytes_accessed=in_bytes + out_bytes, transcendentals=0
@@ -79,13 +81,22 @@
 
 
 def assemble_link(place, *refs):
-    *pieces, out = refs
+    pieces, out, sems = refs[:SIDE], refs[SIDE], refs[SIDE + 1]
     size = pieces[0].shape[0] // 2
+    copies = []
     for step in range(SIDE):
         for half in range(2):
-            out[block_of(half * SIDE + (place[0] ^ step), size), :] = pieces[step][
-                half * size : (half + 1) * size, :
-            ]
+            copies.append(
+                pltpu.make_async_copy(
+                    pieces[step].at[half * size : (half + 1) * size, :],
+                    out.at[block_of(half * SIDE + (place[0] ^ step), size), :],
+                    sems.at[2 * step + half],
+                )
+            )
+    for copy in copies:
+        copy.start()
+    for copy in copies:
+        copy.wait()
 
 
 def inner_kernel(place, first, second, out):
@@ -220,7 +231,14 @@
         coupling_late.reshape(rows, SIDE, SIDE, rows).transpose(0, 2, 1, 3).reshape(rows, nodes),
     )
     away_weights = permuted(line_weights, lambda p, y, x: (p, partner(p, y), x))
-    (block,) = kernel_call(assemble_link, place, pieces, [shape((half, half), bf16)])
+    (block,) = kernel_call(
+        assemble_link,
+        place,
+        pieces,
+        [shape((half, half), bf16)],
+        space=pltpu.HBM,
+        scratch=[pltpu.SemaphoreType.DMA((2 * SIDE,))],
+    )
     weight_half = jnp.where(
         out_place == 0,
         jnp.concatenate([line_weights, away_weights], axis=1),
@@ -250,14 +268,14 @@
                 flops=2 * line * line * nodes,
             )
             inner_all = over_other(inner)
-            previous = tie(previous, inner)
-        if turn == 12:
+            own = tie(own, inner)
+        if turn == 10:
             turned = tie(turned, message)
             coupling_out = [turned] + [along_reduce(turned, step) for step in (1, 2, 3)]
-        if turn == 14:
-            previous = tie(previous, coupling_out)
+        if turn == 12:
+            own = tie(own, coupling_out)
         if turn == 15:
-            previous = tie(previous, inner_all)
+            own = tie(own, inner_all)
         product = lax.dot_general(
             previous, block, (((1,), (1,)), ((), ())), preferred_element_type=f32
         )

time: 178 us -> 174 us (0.978)
  starting transfers between devices: 62.8 us -> 55.5 us
  waiting for transfers between devices: 66 us -> 68.6 us
    ppermute x51, starting transfers between devices: 62.7 us -> 55.4 us  [permuted(): return lax.ppermute(value, AXES, pairs)]
    ppermute x51, waiting for transfers between devices: 59.2 us -> 61.9 us  [permuted(): return lax.ppermute(value, AXES, pairs)]
  transfers between devices with their start and end apart: 54 -> 54, of which waited for: 18 -> 20; matrix products, arithmetic and copies ran while one was open for 9% -> 9% of each run, Pallas kernels for 2% -> 2%
where the time goes in v12:
time: 174 us; the launch traced here: 171 us
  waiting for transfers between devices  68.6 us (39%)
  starting transfers between devices  55.5 us (32%)
  between operations  14.4 us (8%)
  matrix products  12.6 us (7%)
  local copies, waits for them, and re-layouts  9.88 us (6%)
  Pallas kernels  6.67 us (4%)
  other arithmetic  3.7 us (2%)
    ppermute x51, waiting for transfers between devices, permuted(): return lax.ppermute(value, AXES, pairs)  61.9 us
    ppermute x51, starting transfers between devices, permuted(): return lax.ppermute(value, AXES, pairs)  55.4 us
    dot_general x15, matrix products, shards(): lax.dot_general(previous, block, (((1,), (1,)), ((), ())), preferred_elem...  9.77 us
    unnamed x34, local copies, waits for them, and re-layouts  6.94 us
    all_gather x2, waiting for transfers between devices, over_axis(): lax.all_gather(array, 'blk', axis=0, tiled=True, axis_index_groups=groups)  6.68 us
    pallas_call x5, Pallas kernels, kernel_call(): pl.pallas_call(body, out_shape=out_shapes, in_specs=[pl.BlockSpec(memory_...  6.67 us
  transfers between devices with their start and end apart: 54, of which 20 were waited for; matrix products, arithmetic and copies ran while one was open for 9% of the time, Pallas kernels for 2%

profile of v12, /device:TPU:224, one launch (start us, length us, event | category | flops | bytes accessed | tf_op | source)
XLA Modules:
  0.0 171.3 jit_solution(8107258048004405410)
XLA Ops:
  7.2 2.3 %bitcast_select_fusion = (bf16[128,2048]{1,0:T(8,128)(2,1)}, bf16[128,2048]{1,0:T(8,128)(2,1)}) fusion(bf16[1,128,2048]{2,1,0:T(8,128)(2,1)} %param.6, pred[]{:T(512)S(6)} %eq.59, bf16[1,128,2048]{2,1,0:T(8,128)(2,1)} %param.7), kind=kLoop, calls=%fused_computation.57 | loop fusion | flops 524288 | bytes 2097153 | tf_op jit(solution)/shard_map/jit(_where)/select_n | solution.py:193
  9.7 1.6 collective-permute-start.1
  11.3 2.7 %collective-permute-start.2 = (f32[24,128]{1,0:T(8,128)S(1)}, f32[24,128]{1,0:T(8,128)S(1)}, u32[]{:S(2)}, u32[]{:S(2)}) collective-permute-start(f32[24,128]{1,0:T(8,128)S(1)} %get-tuple-element.83), channel_id=1, source_target_pairs={{0,2},{1,3},{2,0},{3,1},{4,6},{5,7},{6,4},{7,5},{8,10},{9,11},{10,... | collective-permute-start | bytes 36872 | tf_op jit(solution)/shard_map/ppermute | solution.py:29
  15.2 1.7 collective-permute-start
  17.0 1.9 %collective-permute-done.3 = f32[24,128]{1,0:T(8,128)S(1)} collective-permute-done((f32[24,128]{1,0:T(8,128)S(1)}, f32[24,128]{1,0:T(8,128)S(1)}, u32[]{:S(2)}, u32[]{:S(2)}) %collective-permute-start.3) | collective-permute-done | bytes 12320 | tf_op jit(solution)/shard_map/ppermute | solution.py:29
  19.0 2.7 %collective-permute-done = bf16[128,1024]{1,0:T(8,128)(2,1)S(1)} collective-permute-done((bf16[128,1024]{1,0:T(8,128)(2,1)S(1)}, bf16[128,1024]{1,0:T(8,128)(2,1)S(1)}, u32[]{:S(2)}, u32[]{:S(2)}) %collective-permute-start) | collective-permute-done | bytes 262176 | tf_op jit(solution)/shard_map/ppermute | solution.py:29
  22.2 3.9 %collective-permute-start.8 = (bf16[256,1024]{1,0:T(8,128)(2,1)S(1)}, bf16[256,1024]{1,0:T(8,128)(2,1)S(1)}, u32[]{:S(2)}, u32[]{:S(2)}) collective-permute-start(bf16[256,1024]{1,0:T(8,128)(2,1)S(1)} %maximum_select_fusion.refs_0_), channel_id=1, source_target_pairs={{0,2},{1,3},{2,0},{3,1},{4,6},{5,7},{6,4},{7,5},{8,10},{9,11},{10,... | collective-permute-start | bytes 1572872 | tf_op jit(solution)/shard_map/ppermute | solution.py:29
  27.0 1.0 copy.11
  28.0 1.4 reshape.47
  29.4 1.7 collective-permute-start.4
  31.1 0.9 broadcast_select_fusion
  32.1 1.0 collective-permute-done.4
  33.1 3.6 %collective-permute-done.7.refs_1_ = bf16[256,1024]{1,0:T(8,128)(2,1)S(1)} collective-permute-done((bf16[256,1024]{1,0:T(8,128)(2,1)S(1)}, bf16[256,1024]{1,0:T(8,128)(2,1)S(1)}, u32[]{:S(2)}, u32[]{:S(2)}) %collective-permute-start.7) | collective-permute-done | bytes 524320 | tf_op jit(solution)/shard_map/ppermute | solution.py:29
  36.8 11.6 %collective-permute-done.8.refs_2_ = bf16[256,1024]{1,0:T(8,128)(2,1)S(1)} collective-permute-done((bf16[256,1024]{1,0:T(8,128)(2,1)S(1)}, bf16[256,1024]{1,0:T(8,128)(2,1)S(1)}, u32[]{:S(2)}, u32[]{:S(2)}) %collective-permute-start.8) | collective-permute-done | bytes 524320 | tf_op jit(solution)/shard_map/ppermute | solution.py:29
  48.4 0.8 copy-done.3
  49.2 1.8 %collective-permute-done.9.refs_3_ = bf16[256,1024]{1,0:T(8,128)(2,1)S(1)} collective-permute-done((bf16[256,1024]{1,0:T(8,128)(2,1)S(1)}, bf16[256,1024]{1,0:T(8,128)(2,1)S(1)}, u32[]{:S(2)}, u32[]{:S(2)}) %collective-permute-start.9) | collective-permute-done | bytes 524320 | tf_op jit(solution)/shard_map/ppermute | solution.py:29
  51.0 0.8 copy-done.5
  51.8 1.0 copy-done.4
  52.8 1.0 copy-done.6
  53.8 0.8 shard_map.86
  55.3 0.7 collective-permute-start.10
  57.3 0.7 collective-permute-start.13
  58.0 2.6 %collective-permute-done.12 = bf16[16,1024]{1,0:T(8,128)(2,1)S(1)} collective-permute-done((bf16[16,1024]{1,0:T(8,128)(2,1)S(1)}, bf16[16,1024]{1,0:T(8,128)(2,1)S(1)}, u32[]{:S(2)}, u32[]{:S(2)}) %collective-permute-start.12) | collective-permute-done | bytes 32800 | tf_op jit(solution)/shard_map/ppermute | solution.py:29
  61.3 0.7 collective-permute-start.14
  64.4 2.3 %collective-permute-done.16 = bf16[16,1024]{1,0:T(8,128)(2,1)S(1)} collective-permute-done((bf16[16,1024]{1,0:T(8,128)(2,1)S(1)}, bf16[16,1024]{1,0:T(8,128)(2,1)S(1)}, u32[]{:S(2)}, u32[]{:S(2)}) %collective-permute-start.16) | collective-permute-done | bytes 32800 | tf_op jit(solution)/shard_map/ppermute | solution.py:29
  67.3 0.7 collective-permute-start.18
  69.3 1.1 collective-permute-start.20
  70.5 2.4 %collective-permute-done.20 = bf16[16,1024]{1,0:T(8,128)(2,1)S(1)} collective-permute-done((bf16[16,1024]{1,0:T(8,128)(2,1)S(1)}, bf16[16,1024]{1,0:T(8,128)(2,1)S(1)}, u32[]{:S(2)}, u32[]{:S(2)}) %collective-permute-start.20) | collective-permute-done | bytes 32800 | tf_op jit(solution)/shard_map/ppermute | solution.py:29
  73.6 6.7 %all-gather.6.cloned.1.call-done.second = bf16[512,2048]{1,0:T(8,128)(2,1)} async-done(((bf16[128,2048]{1,0:T(8,128)(2,1)}), bf16[512,2048]{1,0:T(8,128)(2,1)}) %all-gather.6.cloned.1.call-update) | async-done | bytes 2097168 | tf_op jit(solution)/shard_map/all_gather | solution.py:148
  80.3 1.6 copy-done
  81.8 1.6 copy-done.1
  83.4 2.1 %shard_map.87 = bf16[512,512]{1,0:T(8,128)(2,1)} custom-call(s32[1]{0:T(128)} %bitcast.21.place, bf16[512,2048]{1,0:T(8,128)(2,1)S(1)} %copy-done, bf16[512,2048]{1,0:T(8,128)(2,1)S(1)} %copy-done.1), custom_call_target="tpu_custom_call" | custom-call | flops 1073741824 | bytes 4718592 | tf_op jit(solution)/shard_map/pallas_call | solution.py:58
  85.5 0.8 collective-permute-start.22
  87.7 0.9 collective-permute-start.24
  88.6 0.7 collective-permute-start.25
  89.3 2.0 %collective-permute-done.24 = bf16[16,1024]{1,0:T(8,128)(2,1)S(1)} collective-permute-done((bf16[16,1024]{1,0:T(8,128)(2,1)S(1)}, bf16[16,1024]{1,0:T(8,128)(2,1)S(1)}, u32[]{:S(2)}, u32[]{:S(2)}) %collective-permute-start.24) | collective-permute-done | bytes 32800 | tf_op jit(solution)/shard_map/ppermute | solution.py:29
  92.0 0.7 collective-permute-start.32
  94.0 1.8 %collective-permute-start.27 = (bf16[128,2048]{1,0:T(8,128)(2,1)S(1)}, bf16[128,2048]{1,0:T(8,128)(2,1)S(1)}, u32[]{:S(2)}, u32[]{:S(2)}) collective-permute-start(bf16[128,2048]{1,0:T(8,128)(2,1)S(1)} %copy-done.10), channel_id=1, source_target_pairs={{0,2},{1,3},{2,0},{3,1},{4,6},{5,7},{6,4},{7,5},{8,10},{9,11},{10,... | collective-permute-start | bytes 1572872 | tf_op jit(solution)/shard_map/ppermute | solution.py:29
  95.8 2.4 %collective-permute-start.28 = (bf16[128,2048]{1,0:T(8,128)(2,1)S(1)}, bf16[128,2048]{1,0:T(8,128)(2,1)S(1)}, u32[]{:S(2)}, u32[]{:S(2)}) collective-permute-start(bf16[128,2048]{1,0:T(8,128)(2,1)S(1)} %copy-done.10), channel_id=1, source_target_pairs={{0,3},{1,2},{2,1},{3,0},{4,7},{5,6},{6,5},{7,4},{8,11},{9,10},{10,... | collective-permute-start | bytes 1572872 | tf_op jit(solution)/shard_map/ppermute | solution.py:29
  98.8 1.6 collective-permute-start.35
  100.4 12.6 %collective-permute-done.34 = bf16[16,1024]{1,0:T(8,128)(2,1)S(1)} collective-permute-done((bf16[16,1024]{1,0:T(8,128)(2,1)S(1)}, bf16[16,1024]{1,0:T(8,128)(2,1)S(1)}, u32[]{:S(2)}, u32[]{:S(2)}) %collective-permute-start.34) | collective-permute-done | bytes 32800 | tf_op jit(solution)/shard_map/ppermute | solution.py:29
  113.7 0.7 collective-permute-start.36
  115.1 0.9 collective-permute-done.28
  115.9 0.7 fusion.37
  116.6 1.7 collective-permute-start.39
  118.3 1.7 collective-permute-done.38
  120.6 1.3 collective-permute-start.40
  121.9 1.3 collective-permute-start.41
  123.2 7.6 %collective-permute-done.40 = bf16[16,1024]{1,0:T(8,128)(2,1)S(1)} collective-permute-done((bf16[16,1024]{1,0:T(8,128)(2,1)S(1)}, bf16[16,1024]{1,0:T(8,128)(2,1)S(1)}, u32[]{:S(2)}, u32[]{:S(2)}) %collective-permute-start.40) | collective-permute-done | bytes 32800 | tf_op jit(solution)/shard_map/ppermute | solution.py:29
  132.0 2.2 %collective-permute-start.43 = (bf16[16,1024]{1,0:T(8,128)(2,1)S(1)}, bf16[16,1024]{1,0:T(8,128)(2,1)S(1)}, u32[]{:S(2)}, u32[]{:S(2)}) collective-permute-start(bf16[16,1024]{1,0:T(8,128)(2,1)S(1)} %fusion.39), channel_id=1, source_target_pairs={{0,16},{1,17},{2,18},{3,19},{4,20},{5,21},{6,22},{7,23},{8,24},{9,... | collective-permute-start | bytes 98312 | tf_op jit(solution)/shard_map/ppermute | solution.py:29
  134.2 1.1 collective-permute-done.42
  136.0 2.1 %collective-permute-start.44 = (bf16[16,1024]{1,0:T(8,128)(2,1)S(1)}, bf16[16,1024]{1,0:T(8,128)(2,1)S(1)}, u32[]{:S(2)}, u32[]{:S(2)}) collective-permute-start(bf16[16,1024]{1,0:T(8,128)(2,1)S(1)} %fusion.41), channel_id=1, source_target_pairs={{0,4},{1,5},{2,6},{3,7},{4,0},{5,1},{6,2},{7,3},{8,12},{9,13},{10,... | collective-permute-start | bytes 98312 | tf_op jit(solution)/shard_map/ppermute | solution.py:29
  138.1 2.5 %fusion.8 = bf16[512,512]{1,0:T(8,128)(2,1)S(1)} fusion(bf16[2048,512]{1,0:T(8,128)(2,1)S(1)} %copy-done.12, bf16[128,2048]{1,0:T(8,128)(2,1)} %copy-done.16, bf16[128,2048]{1,0:T(8,128)(2,1)} %copy-done.15, bf16[128,2048]{1,0:T(8,128)(2,1)S(1)} %copy-done.14, bf16[128,2048]{1,0:T(8,128)(2,1)S(1)} %copy-done.10), kind=kOutput, calls=%fused_computation.8 | convolution fusion | flops 1082392576 | bytes 4718592 | tf_op jit(solution)/shard_map/dot_general | solution.py:288
  140.7 1.5 collective-permute-start.30
  142.2 3.2 %collective-permute-start.31 = (bf16[128,512]{1,0:T(8,128)(2,1)S(1)}, bf16[128,512]{1,0:T(8,128)(2,1)S(1)}, u32[]{:S(2)}, u32[]{:S(2)}) collective-permute-start(bf16[128,512]{1,0:T(8,128)(2,1)S(1)} %get-tuple-element.45), channel_id=1, source_target_pairs={{0,3},{1,2},{2,1},{3,0},{4,7},{5,6},{6,5},{7,4},{8,11},{9,10},{10,... | collective-permute-start | bytes 393224 | tf_op jit(solution)/shard_map/ppermute | solution.py:29
  145.8 1.9 %collective-permute-start.46 = (bf16[16,512]{1,0:T(8,128)(2,1)S(1)}, bf16[16,512]{1,0:T(8,128)(2,1)S(1)}, u32[]{:S(2)}, u32[]{:S(2)}) collective-permute-start(bf16[16,512]{1,0:T(8,128)(2,1)S(1)} %get-tuple-element.63), channel_id=1, source_target_pairs={{16,4},{17,5},{18,6},{19,7},{20,0},{21,1},{22,2},{23,3},{24,12},{2... | collective-permute-start | bytes 49160 | tf_op jit(solution)/shard_map/ppermute | solution.py:29
  147.8 1.9 %collective-permute-start.47 = (bf16[16,512]{1,0:T(8,128)(2,1)S(1)}, bf16[16,512]{1,0:T(8,128)(2,1)S(1)}, u32[]{:S(2)}, u32[]{:S(2)}) collective-permute-start(bf16[16,512]{1,0:T(8,128)(2,1)S(1)} %get-tuple-element.64), channel_id=1, source_target_pairs={{16,0},{17,1},{18,2},{19,3},{20,4},{21,5},{22,6},{23,7},{24,8},{25... | collective-permute-start | bytes 49160 | tf_op jit(solution)/shard_map/ppermute | solution.py:29
  149.7 1.1 collective-permute-done.46
  150.9 1.4 collective-permute-start.45
  152.3 3.7 %collective-permute-done.45 = bf16[16,1024]{1,0:T(8,128)(2,1)S(1)} collective-permute-done((bf16[16,1024]{1,0:T(8,128)(2,1)S(1)}, bf16[16,1024]{1,0:T(8,128)(2,1)S(1)}, u32[]{:S(2)}, u32[]{:S(2)}) %collective-permute-start.45) | collective-permute-done | bytes 32800 | tf_op jit(solution)/shard_map/ppermute | solution.py:29
  156.2 1.5 collective-permute-start.49
  157.7 3.2 %collective-permute-start.50 = (bf16[16,2432]{1,0:T(8,128)(2,1)S(1)}, bf16[16,2432]{1,0:T(8,128)(2,1)S(1)}, u32[]{:S(2)}, u32[]{:S(2)}) collective-permute-start(bf16[16,2432]{1,0:T(8,128)(2,1)S(1)} %get-tuple-element.49), channel_id=1, source_target_pairs={{0,3},{1,2},{2,1},{3,0},{4,7},{5,6},{6,5},{7,4},{8,11},{9,10},{10,... | collective-permute-start | bytes 233480 | tf_op jit(solution)/shard_map/ppermute | solution.py:29
  161.0 1.8 %shard_map.88 = (f32[128,2048]{1,0:T(8,128)}, bf16[128,2048]{1,0:T(8,128)(2,1)S(1)}) custom-call(s32[3]{0:T(128)S(1)} %pad_add_fusion.place, f32[128,2048]{1,0:T(8,128)S(1)} %bitcast.60, bf16[128,512]{1,0:T(8,128)(2,1)S(1)} %get-tuple-element.48.refs_1_, bf16[128,512]{1,0:T(8,128)(2,1)S(1)} %collective-permute-done.29.refs_2_, ...), custom_call_target="tpu_custom_call" | custom-call | bytes 3145728 | tf_op jit(solution)/shard_map/pallas_call | solution.py:58
  163.3 1.5 shard_map.89
  (135 shorter events, 19.7 us)
Async XLA Ops:
  7.2 2.5 %copy-start.8 = (f32[1,128]{1,0:T(1,128)S(1)}, f32[1,128]{1,0:T(1,128)}, u32[]{:S(2)}) copy-start(f32[1,128]{1,0:T(1,128)} %weight.1) | copy-start | bytes 1540
  7.2 7.4 %copy-start.7 = (bf16[1,128,2048]{2,1,0:T(8,128)(2,1)S(1)}, bf16[1,128,2048]{2,1,0:T(8,128)(2,1)}, u32[]{:S(2)}) copy-start(bf16[1,128,2048]{2,1,0:T(8,128)(2,1)} %param.9) | copy-start | bytes 1572868
  7.2 66.4 %all-gather.4.cloned.1.call-start = ((), (), s32[]{:S(2)}) async-start(), calls=%async_computation | async-start | bytes 2621440 | tf_op jit(solution)/shard_map/all_gather | solution.py:148
  9.6 17.0 %copy-start.9 = (bf16[1,128,2048]{2,1,0:T(8,128)(2,1)S(1)}, bf16[1,128,2048]{2,1,0:T(8,128)(2,1)}, u32[]{:S(2)}) copy-start(bf16[1,128,2048]{2,1,0:T(8,128)(2,1)} %param.7) | copy-start | bytes 1572868
  9.6 70.7 %all-gather.6.cloned.1.call-start = ((), (), s32[]{:S(2)}) async-start(), calls=%async_computation.1 | async-start | bytes 2621440 | tf_op jit(solution)/shard_map/all_gather | solution.py:148
  9.7 7.3 %collective-permute-start.1 = (f32[24,128]{1,0:T(8,128)S(1)}, f32[24,128]{1,0:T(8,128)S(1)}, u32[]{:S(2)}, u32[]{:S(2)}) collective-permute-start(f32[24,128]{1,0:T(8,128)S(1)} %get-tuple-element.82), channel_id=1, source_target_pairs={{0,1},{1,0},{2,3},{3,2},{4,5},{5,4},{6,7},{7,6},{8,9},{9,8},{10,11... | collective-permute-start | bytes 36872 | tf_op jit(solution)/shard_map/ppermute | solution.py:29
  11.3 5.7 %collective-permute-start.2 = (f32[24,128]{1,0:T(8,128)S(1)}, f32[24,128]{1,0:T(8,128)S(1)}, u32[]{:S(2)}, u32[]{:S(2)}) collective-permute-start(f32[24,128]{1,0:T(8,128)S(1)} %get-tuple-element.83), channel_id=1, source_target_pairs={{0,2},{1,3},{2,0},{3,1},{4,6},{5,7},{6,4},{7,5},{8,10},{9,11},{10,... | collective-permute-start | bytes 36872 | tf_op jit(solution)/shard_map/ppermute | solution.py:29
  14.1 4.9 %collective-permute-start.3 = (f32[24,128]{1,0:T(8,128)S(1)}, f32[24,128]{1,0:T(8,128)S(1)}, u32[]{:S(2)}, u32[]{:S(2)}) collective-permute-start(f32[24,128]{1,0:T(8,128)S(1)} %get-tuple-element.84), channel_id=1, source_target_pairs={{0,3},{1,2},{2,1},{3,0},{4,7},{5,6},{6,5},{7,4},{8,11},{9,10},{10,... | collective-permute-start | bytes 36872 | tf_op jit(solution)/shard_map/ppermute | solution.py:29
  15.2 6.5 %collective-permute-start = (bf16[128,1024]{1,0:T(8,128)(2,1)S(1)}, bf16[128,1024]{1,0:T(8,128)(2,1)S(1)}, u32[]{:S(2)}, u32[]{:S(2)}) collective-permute-start(bf16[128,1024]{1,0:T(8,128)(2,1)S(1)} %get-tuple-element.23), channel_id=1, source_target_pairs={{0,4},{1,5},{2,6},{3,7},{4,0},{5,1},{6,2},{7,3},{8,12},{9,13},{10,... | collective-permute-start | bytes 786440 | tf_op jit(solution)/shard_map/ppermute | solution.py:29
  16.9 117.3 %all-gather.8.cloned.1.call-start = ((), (), s32[]{:S(2)}) async-start(), calls=%async_computation.2 | async-start | bytes 2621440 | tf_op jit(solution)/shard_map/all_gather | solution.py:159
  21.8 14.9 %collective-permute-start.7 = (bf16[256,1024]{1,0:T(8,128)(2,1)S(1)}, bf16[256,1024]{1,0:T(8,128)(2,1)S(1)}, u32[]{:S(2)}, u32[]{:S(2)}) collective-permute-start(bf16[256,1024]{1,0:T(8,128)(2,1)S(1)} %maximum_select_fusion.refs_0_), channel_id=1, source_target_pairs={{0,1},{1,0},{2,3},{3,2},{4,5},{5,4},{6,7},{7,6},{8,9},{9,8},{10,11... | collective-permute-start | bytes 1572872 | tf_op jit(solution)/shard_map/ppermute | solution.py:29
  22.2 26.2 %collective-permute-start.8 = (bf16[256,1024]{1,0:T(8,128)(2,1)S(1)}, bf16[256,1024]{1,0:T(8,128)(2,1)S(1)}, u32[]{:S(2)}, u32[]{:S(2)}) collective-permute-start(bf16[256,1024]{1,0:T(8,128)(2,1)S(1)} %maximum_select_fusion.refs_0_), channel_id=1, source_target_pairs={{0,2},{1,3},{2,0},{3,1},{4,6},{5,7},{6,4},{7,5},{8,10},{9,11},{10,... | collective-permute-start | bytes 1572872 | tf_op jit(solution)/shard_map/ppermute | solution.py:29
  26.1 24.8 %collective-permute-start.9 = (bf16[256,1024]{1,0:T(8,128)(2,1)S(1)}, bf16[256,1024]{1,0:T(8,128)(2,1)S(1)}, u32[]{:S(2)}, u32[]{:S(2)}) collective-permute-start(bf16[256,1024]{1,0:T(8,128)(2,1)S(1)} %maximum_select_fusion.refs_0_), channel_id=1, source_target_pairs={{0,3},{1,2},{2,1},{3,0},{4,7},{5,6},{6,5},{7,4},{8,11},{9,10},{10,... | collective-permute-start | bytes 1572872 | tf_op jit(solution)/shard_map/ppermute | solution.py:29
  29.4 3.7 %collective-permute-start.4 = (f32[1,512]{1,0:T(1,128)S(1)}, f32[1,512]{1,0:T(1,128)S(1)}, u32[]{:S(2)}, u32[]{:S(2)}) collective-permute-start(f32[1,512]{1,0:T(1,128)S(1)} %slice.38), channel_id=1, source_target_pairs={{0,4},{1,5},{2,6},{3,7},{4,0},{5,1},{6,2},{7,3},{8,12},{9,13},{10,... | collective-permute-start | bytes 6152 | tf_op jit(solution)/shard_map/ppermute | solution.py:29
  32.0 22.6 %collective-permute-start.5 = (bf16[16,1024]{1,0:T(8,128)(2,1)S(1)}, bf16[16,1024]{1,0:T(8,128)(2,1)S(1)}, u32[]{:S(2)}, u32[]{:S(2)}) collective-permute-start(bf16[16,1024]{1,0:T(8,128)(2,1)S(1)} %convert_element_type.217), channel_id=1, source_target_pairs={{0,20},{1,21},{2,22},{3,23},{4,16},{5,17},{6,18},{7,19},{8,28},{9,... | collective-permute-start | bytes 98312 | tf_op jit(solution)/shard_map/ppermute | solution.py:29
  33.1 21.5 %collective-permute-start.6 = (bf16[16,1024]{1,0:T(8,128)(2,1)S(1)}, bf16[16,1024]{1,0:T(8,128)(2,1)S(1)}, u32[]{:S(2)}, u32[]{:S(2)}) collective-permute-start(bf16[16,1024]{1,0:T(8,128)(2,1)S(1)} %convert_element_type.217), channel_id=1, source_target_pairs={{0,16},{1,17},{2,18},{3,19},{4,20},{5,21},{6,22},{7,23},{8,24},{9,... | collective-permute-start | bytes 98312 | tf_op jit(solution)/shard_map/ppermute | solution.py:29
  55.3 1.3 collective-permute-start.10
  56.0 0.7 collective-permute-start.11
  57.3 3.3 %collective-permute-start.12 = (bf16[16,1024]{1,0:T(8,128)(2,1)S(1)}, bf16[16,1024]{1,0:T(8,128)(2,1)S(1)}, u32[]{:S(2)}, u32[]{:S(2)}) collective-permute-start(bf16[16,1024]{1,0:T(8,128)(2,1)S(1)} %fusion.27), channel_id=1, source_target_pairs={{0,20},{1,21},{2,22},{3,23},{4,16},{5,17},{6,18},{7,19},{8,28},{9,... | collective-permute-start | bytes 98312 | tf_op jit(solution)/shard_map/ppermute | solution.py:29
  57.3 3.3 %collective-permute-start.13 = (bf16[16,1024]{1,0:T(8,128)(2,1)S(1)}, bf16[16,1024]{1,0:T(8,128)(2,1)S(1)}, u32[]{:S(2)}, u32[]{:S(2)}) collective-permute-start(bf16[16,1024]{1,0:T(8,128)(2,1)S(1)} %fusion.27), channel_id=1, source_target_pairs={{0,16},{1,17},{2,18},{3,19},{4,20},{5,21},{6,22},{7,23},{8,24},{9,... | collective-permute-start | bytes 98312 | tf_op jit(solution)/shard_map/ppermute | solution.py:29
  61.3 1.3 collective-permute-start.14
  62.0 0.7 collective-permute-start.15
  63.3 3.3 %collective-permute-start.16 = (bf16[16,1024]{1,0:T(8,128)(2,1)S(1)}, bf16[16,1024]{1,0:T(8,128)(2,1)S(1)}, u32[]{:S(2)}, u32[]{:S(2)}) collective-permute-start(bf16[16,1024]{1,0:T(8,128)(2,1)S(1)} %fusion.29), channel_id=1, source_target_pairs={{0,20},{1,21},{2,22},{3,23},{4,16},{5,17},{6,18},{7,19},{8,28},{9,... | collective-permute-start | bytes 98312 | tf_op jit(solution)/shard_map/ppermute | solution.py:29
  63.9 2.7 %collective-permute-start.17 = (bf16[16,1024]{1,0:T(8,128)(2,1)S(1)}, bf16[16,1024]{1,0:T(8,128)(2,1)S(1)}, u32[]{:S(2)}, u32[]{:S(2)}) collective-permute-start(bf16[16,1024]{1,0:T(8,128)(2,1)S(1)} %fusion.29), channel_id=1, source_target_pairs={{0,16},{1,17},{2,18},{3,19},{4,20},{5,21},{6,22},{7,23},{8,24},{9,... | collective-permute-start | bytes 98312 | tf_op jit(solution)/shard_map/ppermute | solution.py:29
  67.3 1.3 collective-permute-start.18
  68.0 0.7 collective-permute-start.19
  69.3 3.6 %collective-permute-start.20 = (bf16[16,1024]{1,0:T(8,128)(2,1)S(1)}, bf16[16,1024]{1,0:T(8,128)(2,1)S(1)}, u32[]{:S(2)}, u32[]{:S(2)}) collective-permute-start(bf16[16,1024]{1,0:T(8,128)(2,1)S(1)} %fusion.31), channel_id=1, source_target_pairs={{0,20},{1,21},{2,22},{3,23},{4,16},{5,17},{6,18},{7,19},{8,28},{9,... | collective-permute-start | bytes 98312 | tf_op jit(solution)/shard_map/ppermute | solution.py:29
  70.4 2.5 %collective-permute-start.21 = (bf16[16,1024]{1,0:T(8,128)(2,1)S(1)}, bf16[16,1024]{1,0:T(8,128)(2,1)S(1)}, u32[]{:S(2)}, u32[]{:S(2)}) collective-permute-start(bf16[16,1024]{1,0:T(8,128)(2,1)S(1)} %fusion.31), channel_id=1, source_target_pairs={{0,16},{1,17},{2,18},{3,19},{4,20},{5,21},{6,22},{7,23},{8,24},{9,... | collective-permute-start | bytes 98312 | tf_op jit(solution)/shard_map/ppermute | solution.py:29
  85.5 7.8 %copy-start.10 = (bf16[128,2048]{1,0:T(8,128)(2,1)S(1)}, bf16[128,2048]{1,0:T(8,128)(2,1)}, u32[]{:S(2)}) copy-start(bf16[128,2048]{1,0:T(8,128)(2,1)} %broadcast_select_fusion) | copy-start | bytes 1572868
  85.5 1.5 collective-permute-start.22
  86.3 0.7 collective-permute-start.23
  87.7 3.7 %collective-permute-start.24 = (bf16[16,1024]{1,0:T(8,128)(2,1)S(1)}, bf16[16,1024]{1,0:T(8,128)(2,1)S(1)}, u32[]{:S(2)}, u32[]{:S(2)}) collective-permute-start(bf16[16,1024]{1,0:T(8,128)(2,1)S(1)} %fusion.33), channel_id=1, source_target_pairs={{0,20},{1,21},{2,22},{3,23},{4,16},{5,17},{6,18},{7,19},{8,28},{9,... | collective-permute-start | bytes 98312 | tf_op jit(solution)/shard_map/ppermute | solution.py:29
  88.6 2.7 %collective-permute-start.25 = (bf16[16,1024]{1,0:T(8,128)(2,1)S(1)}, bf16[16,1024]{1,0:T(8,128)(2,1)S(1)}, u32[]{:S(2)}, u32[]{:S(2)}) collective-permute-start(bf16[16,1024]{1,0:T(8,128)(2,1)S(1)} %fusion.33), channel_id=1, source_target_pairs={{0,16},{1,17},{2,18},{3,19},{4,20},{5,21},{6,22},{7,23},{8,24},{9,... | collective-permute-start | bytes 98312 | tf_op jit(solution)/shard_map/ppermute | solution.py:29
  92.0 6.1 %collective-permute-start.32 = (bf16[16,1024]{1,0:T(8,128)(2,1)S(1)}, bf16[16,1024]{1,0:T(8,128)(2,1)S(1)}, u32[]{:S(2)}, u32[]{:S(2)}) collective-permute-start(bf16[16,1024]{1,0:T(8,128)(2,1)S(1)} %fusion.34), channel_id=1, source_target_pairs={{144,172},{145,173},{146,174},{147,175},{148,168},{149,169},{150,1... | collective-permute-start | bytes 98312 | tf_op jit(solution)/shard_map/ppermute | solution.py:29
  92.7 5.5 %collective-permute-start.33 = (bf16[16,1024]{1,0:T(8,128)(2,1)S(1)}, bf16[16,1024]{1,0:T(8,128)(2,1)S(1)}, u32[]{:S(2)}, u32[]{:S(2)}) collective-permute-start(bf16[16,1024]{1,0:T(8,128)(2,1)S(1)} %fusion.34), channel_id=1, source_target_pairs={{144,160},{145,161},{146,162},{147,163},{148,164},{149,165},{150,1... | collective-permute-start | bytes 98312 | tf_op jit(solution)/shard_map/ppermute | solution.py:29
  93.4 21.7 %collective-permute-start.26 = (bf16[128,2048]{1,0:T(8,128)(2,1)S(1)}, bf16[128,2048]{1,0:T(8,128)(2,1)S(1)}, u32[]{:S(2)}, u32[]{:S(2)}) collective-permute-start(bf16[128,2048]{1,0:T(8,128)(2,1)S(1)} %copy-done.10), channel_id=1, source_target_pairs={{0,1},{1,0},{2,3},{3,2},{4,5},{5,4},{6,7},{7,6},{8,9},{9,8},{10,11... | collective-permute-start | bytes 1572872 | tf_op jit(solution)/shard_map/ppermute | solution.py:29
  94.0 21.0 %collective-permute-start.27 = (bf16[128,2048]{1,0:T(8,128)(2,1)S(1)}, bf16[128,2048]{1,0:T(8,128)(2,1)S(1)}, u32[]{:S(2)}, u32[]{:S(2)}) collective-permute-start(bf16[128,2048]{1,0:T(8,128)(2,1)S(1)} %copy-done.10), channel_id=1, source_target_pairs={{0,2},{1,3},{2,0},{3,1},{4,6},{5,7},{6,4},{7,5},{8,10},{9,11},{10,... | collective-permute-start | bytes 1572872 | tf_op jit(solution)/shard_map/ppermute | solution.py:29
  95.8 20.2 %collective-permute-start.28 = (bf16[128,2048]{1,0:T(8,128)(2,1)S(1)}, bf16[128,2048]{1,0:T(8,128)(2,1)S(1)}, u32[]{:S(2)}, u32[]{:S(2)}) collective-permute-start(bf16[128,2048]{1,0:T(8,128)(2,1)S(1)} %copy-done.10), channel_id=1, source_target_pairs={{0,3},{1,2},{2,1},{3,0},{4,7},{5,6},{6,5},{7,4},{8,11},{9,10},{10,... | collective-permute-start | bytes 1572872 | tf_op jit(solution)/shard_map/ppermute | solution.py:29
  98.8 14.2 %collective-permute-start.34 = (bf16[16,1024]{1,0:T(8,128)(2,1)S(1)}, bf16[16,1024]{1,0:T(8,128)(2,1)S(1)}, u32[]{:S(2)}, u32[]{:S(2)}) collective-permute-start(bf16[16,1024]{1,0:T(8,128)(2,1)S(1)} %fusion.35), channel_id=1, source_target_pairs={{0,20},{1,21},{2,22},{3,23},{4,16},{5,17},{6,18},{7,19},{8,28},{9,... | collective-permute-start | bytes 98312 | tf_op jit(solution)/shard_map/ppermute | solution.py:29
  98.8 14.2 %collective-permute-start.35 = (bf16[16,1024]{1,0:T(8,128)(2,1)S(1)}, bf16[16,1024]{1,0:T(8,128)(2,1)S(1)}, u32[]{:S(2)}, u32[]{:S(2)}) collective-permute-start(bf16[16,1024]{1,0:T(8,128)(2,1)S(1)} %fusion.35), channel_id=1, source_target_pairs={{0,16},{1,17},{2,18},{3,19},{4,20},{5,21},{6,22},{7,23},{8,24},{9,... | collective-permute-start | bytes 98312 | tf_op jit(solution)/shard_map/ppermute | solution.py:29
  113.7 2.3 %collective-permute-start.36 = (bf16[16,1024]{1,0:T(8,128)(2,1)S(1)}, bf16[16,1024]{1,0:T(8,128)(2,1)S(1)}, u32[]{:S(2)}, u32[]{:S(2)}) collective-permute-start(bf16[16,1024]{1,0:T(8,128)(2,1)S(1)} %fusion.36), channel_id=1, source_target_pairs={{176,204},{177,205},{178,206},{179,207},{180,200},{181,201},{182,2... | collective-permute-start | bytes 98312 | tf_op jit(solution)/shard_map/ppermute | solution.py:29
  114.3 1.6 collective-permute-start.37
  115.0 5.6 %copy-start.13 = (bf16[128,2048]{1,0:T(8,128)(2,1)}, bf16[128,2048]{1,0:T(8,128)(2,1)S(1)}, u32[]{:S(2)}) copy-start(bf16[128,2048]{1,0:T(8,128)(2,1)S(1)} %collective-permute-done.26) | copy-start | bytes 1572868
  115.0 5.6 %copy-start.15 = (bf16[128,2048]{1,0:T(8,128)(2,1)}, bf16[128,2048]{1,0:T(8,128)(2,1)S(1)}, u32[]{:S(2)}) copy-start(bf16[128,2048]{1,0:T(8,128)(2,1)S(1)} %collective-permute-done.27) | copy-start | bytes 1572868
  115.9 4.7 %copy-start.16 = (bf16[128,2048]{1,0:T(8,128)(2,1)}, bf16[128,2048]{1,0:T(8,128)(2,1)S(1)}, u32[]{:S(2)}) copy-start(bf16[128,2048]{1,0:T(8,128)(2,1)S(1)} %collective-permute-done.28) | copy-start | bytes 1572868
  116.6 3.3 %collective-permute-start.38 = (bf16[16,1024]{1,0:T(8,128)(2,1)S(1)}, bf16[16,1024]{1,0:T(8,128)(2,1)S(1)}, u32[]{:S(2)}, u32[]{:S(2)}) collective-permute-start(bf16[16,1024]{1,0:T(8,128)(2,1)S(1)} %fusion.37), channel_id=1, source_target_pairs={{0,20},{1,21},{2,22},{3,23},{4,16},{5,17},{6,18},{7,19},{8,28},{9,... | collective-permute-start | bytes 98312 | tf_op jit(solution)/shard_map/ppermute | solution.py:29
  116.6 3.3 %collective-permute-start.39 = (bf16[16,1024]{1,0:T(8,128)(2,1)S(1)}, bf16[16,1024]{1,0:T(8,128)(2,1)S(1)}, u32[]{:S(2)}, u32[]{:S(2)}) collective-permute-start(bf16[16,1024]{1,0:T(8,128)(2,1)S(1)} %fusion.37), channel_id=1, source_target_pairs={{0,16},{1,17},{2,18},{3,19},{4,20},{5,21},{6,22},{7,23},{8,24},{9,... | collective-permute-start | bytes 98312 | tf_op jit(solution)/shard_map/ppermute | solution.py:29
  120.6 10.2 %collective-permute-start.40 = (bf16[16,1024]{1,0:T(8,128)(2,1)S(1)}, bf16[16,1024]{1,0:T(8,128)(2,1)S(1)}, u32[]{:S(2)}, u32[]{:S(2)}) collective-permute-start(bf16[16,1024]{1,0:T(8,128)(2,1)S(1)} %fusion.38), channel_id=1, source_target_pairs={{208,236},{209,237},{210,238},{211,239},{212,232},{213,233},{214,2... | collective-permute-start | bytes 98312 | tf_op jit(solution)/shard_map/ppermute | solution.py:29
  121.9 9.4 %collective-permute-start.41 = (bf16[16,1024]{1,0:T(8,128)(2,1)S(1)}, bf16[16,1024]{1,0:T(8,128)(2,1)S(1)}, u32[]{:S(2)}, u32[]{:S(2)}) collective-permute-start(bf16[16,1024]{1,0:T(8,128)(2,1)S(1)} %fusion.38), channel_id=1, source_target_pairs={{208,224},{209,225},{210,226},{211,227},{212,228},{213,229},{214,2... | collective-permute-start | bytes 98312 | tf_op jit(solution)/shard_map/ppermute | solution.py:29
  132.0 3.4 %collective-permute-start.42 = (bf16[16,1024]{1,0:T(8,128)(2,1)S(1)}, bf16[16,1024]{1,0:T(8,128)(2,1)S(1)}, u32[]{:S(2)}, u32[]{:S(2)}) collective-permute-start(bf16[16,1024]{1,0:T(8,128)(2,1)S(1)} %fusion.39), channel_id=1, source_target_pairs={{0,20},{1,21},{2,22},{3,23},{4,16},{5,17},{6,18},{7,19},{8,28},{9,... | collective-permute-start | bytes 98312 | tf_op jit(solution)/shard_map/ppermute | solution.py:29
  132.0 3.4 %collective-permute-start.43 = (bf16[16,1024]{1,0:T(8,128)(2,1)S(1)}, bf16[16,1024]{1,0:T(8,128)(2,1)S(1)}, u32[]{:S(2)}, u32[]{:S(2)}) collective-permute-start(bf16[16,1024]{1,0:T(8,128)(2,1)S(1)} %fusion.39), channel_id=1, source_target_pairs={{0,16},{1,17},{2,18},{3,19},{4,20},{5,21},{6,22},{7,23},{8,24},{9,... | collective-permute-start | bytes 98312 | tf_op jit(solution)/shard_map/ppermute | solution.py:29
  134.2 3.9 %copy-start.12 = (bf16[2048,512]{1,0:T(8,128)(2,1)S(1)}, bf16[2048,512]{1,0:T(8,128)(2,1)}, u32[]{:S(2)}) copy-start(bf16[2048,512]{1,0:T(8,128)(2,1)} %all-gather.8.cloned.1.call-done) | copy-start | bytes 6291460
  134.2 3.9 %copy-start.14 = (bf16[128,2048]{1,0:T(8,128)(2,1)S(1)}, bf16[128,2048]{1,0:T(8,128)(2,1)}, u32[]{:S(2)}) copy-start(bf16[128,2048]{1,0:T(8,128)(2,1)} %copy-done.13) | copy-start | bytes 1572868
  136.0 9.4 %collective-permute-start.44 = (bf16[16,1024]{1,0:T(8,128)(2,1)S(1)}, bf16[16,1024]{1,0:T(8,128)(2,1)S(1)}, u32[]{:S(2)}, u32[]{:S(2)}) collective-permute-start(bf16[16,1024]{1,0:T(8,128)(2,1)S(1)} %fusion.41), channel_id=1, source_target_pairs={{0,4},{1,5},{2,6},{3,7},{4,0},{5,1},{6,2},{7,3},{8,12},{9,13},{10,... | collective-permute-start | bytes 98312 | tf_op jit(solution)/shard_map/ppermute | solution.py:29
  140.6 20.4 %copy-start.2 = (f32[1,128,2048]{2,1,0:T(8,128)S(1)}, f32[1,128,2048]{2,1,0:T(8,128)}, u32[]{:S(2)}) copy-start(f32[1,128,2048]{2,1,0:T(8,128)} %param.8) | copy-start | bytes 3145732
  140.6 15.4 %collective-permute-start.29 = (bf16[128,512]{1,0:T(8,128)(2,1)S(1)}, bf16[128,512]{1,0:T(8,128)(2,1)S(1)}, u32[]{:S(2)}, u32[]{:S(2)}) collective-permute-start(bf16[128,512]{1,0:T(8,128)(2,1)S(1)} %get-tuple-element.47), channel_id=1, source_target_pairs={{0,1},{1,0},{2,3},{3,2},{4,5},{5,4},{6,7},{7,6},{8,9},{9,8},{10,11... | collective-permute-start | bytes 393224 | tf_op jit(solution)/shard_map/ppermute | solution.py:29
  140.7 15.3 %collective-permute-start.30 = (bf16[128,512]{1,0:T(8,128)(2,1)S(1)}, bf16[128,512]{1,0:T(8,128)(2,1)S(1)}, u32[]{:S(2)}, u32[]{:S(2)}) collective-permute-start(bf16[128,512]{1,0:T(8,128)(2,1)S(1)} %get-tuple-element.46), channel_id=1, source_target_pairs={{0,2},{1,3},{2,0},{3,1},{4,6},{5,7},{6,4},{7,5},{8,10},{9,11},{10,... | collective-permute-start | bytes 393224 | tf_op jit(solution)/shard_map/ppermute | solution.py:29
  142.2 13.9 %collective-permute-start.31 = (bf16[128,512]{1,0:T(8,128)(2,1)S(1)}, bf16[128,512]{1,0:T(8,128)(2,1)S(1)}, u32[]{:S(2)}, u32[]{:S(2)}) collective-permute-start(bf16[128,512]{1,0:T(8,128)(2,1)S(1)} %get-tuple-element.45), channel_id=1, source_target_pairs={{0,3},{1,2},{2,1},{3,0},{4,7},{5,6},{6,5},{7,4},{8,11},{9,10},{10,... | collective-permute-start | bytes 393224 | tf_op jit(solution)/shard_map/ppermute | solution.py:29
  145.8 5.1 %collective-permute-start.46 = (bf16[16,512]{1,0:T(8,128)(2,1)S(1)}, bf16[16,512]{1,0:T(8,128)(2,1)S(1)}, u32[]{:S(2)}, u32[]{:S(2)}) collective-permute-start(bf16[16,512]{1,0:T(8,128)(2,1)S(1)} %get-tuple-element.63), channel_id=1, source_target_pairs={{16,4},{17,5},{18,6},{19,7},{20,0},{21,1},{22,2},{23,3},{24,12},{2... | collective-permute-start | bytes 49160 | tf_op jit(solution)/shard_map/ppermute | solution.py:29
  147.8 4.5 %collective-permute-start.47 = (bf16[16,512]{1,0:T(8,128)(2,1)S(1)}, bf16[16,512]{1,0:T(8,128)(2,1)S(1)}, u32[]{:S(2)}, u32[]{:S(2)}) collective-permute-start(bf16[16,512]{1,0:T(8,128)(2,1)S(1)} %get-tuple-element.64), channel_id=1, source_target_pairs={{16,0},{17,1},{18,2},{19,3},{20,4},{21,5},{22,6},{23,7},{24,8},{25... | collective-permute-start | bytes 49160 | tf_op jit(solution)/shard_map/ppermute | solution.py:29
  150.9 5.1 %collective-permute-start.45 = (bf16[16,1024]{1,0:T(8,128)(2,1)S(1)}, bf16[16,1024]{1,0:T(8,128)(2,1)S(1)}, u32[]{:S(2)}, u32[]{:S(2)}) collective-permute-start(bf16[16,1024]{1,0:T(8,128)(2,1)S(1)} %get-tuple-element.37), channel_id=1, source_target_pairs={{0,12},{1,13},{2,14},{3,15},{4,8},{5,9},{6,10},{7,11},{8,4},{9,5},... | collective-permute-start | bytes 98312 | tf_op jit(solution)/shard_map/ppermute | solution.py:29
  156.1 6.6 %collective-permute-start.48 = (bf16[16,2432]{1,0:T(8,128)(2,1)S(1)}, bf16[16,2432]{1,0:T(8,128)(2,1)S(1)}, u32[]{:S(2)}, u32[]{:S(2)}) collective-permute-start(bf16[16,2432]{1,0:T(8,128)(2,1)S(1)} %get-tuple-element.50), channel_id=1, source_target_pairs={{0,1},{1,0},{2,3},{3,2},{4,5},{5,4},{6,7},{7,6},{8,9},{9,8},{10,11... | collective-permute-start | bytes 233480 | tf_op jit(solution)/shard_map/ppermute | solution.py:29
  156.2 6.5 %collective-permute-start.49 = (bf16[16,2432]{1,0:T(8,128)(2,1)S(1)}, bf16[16,2432]{1,0:T(8,128)(2,1)S(1)}, u32[]{:S(2)}, u32[]{:S(2)}) collective-permute-start(bf16[16,2432]{1,0:T(8,128)(2,1)S(1)} %get-tuple-element.51), channel_id=1, source_target_pairs={{0,2},{1,3},{2,0},{3,1},{4,6},{5,7},{6,4},{7,5},{8,10},{9,11},{10,... | collective-permute-start | bytes 233480 | tf_op jit(solution)/shard_map/ppermute | solution.py:29
  157.7 5.6 %collective-permute-start.50 = (bf16[16,2432]{1,0:T(8,128)(2,1)S(1)}, bf16[16,2432]{1,0:T(8,128)(2,1)S(1)}, u32[]{:S(2)}, u32[]{:S(2)}) collective-permute-start(bf16[16,2432]{1,0:T(8,128)(2,1)S(1)} %get-tuple-element.49), channel_id=1, source_target_pairs={{0,3},{1,2},{2,1},{3,0},{4,7},{5,6},{6,5},{7,4},{8,11},{9,10},{10,... | collective-permute-start | bytes 233480 | tf_op jit(solution)/shard_map/ppermute | solution.py:29
  (7 other events, 9.4 us)
Sparse Core Ops, SparseCore 0:
  9.8 33.8 all-gather.3
  46.1 34.0 all-gather.5
  85.7 35.4 all-gather.7

commit v13 on v12

--- a/solution.py
+++ b/solution.py
@@ -99,11 +99,25 @@
         copy.wait()
 
 
-def inner_kernel(place, first, second, out):
-    def multiply(left, right):
-        out[...] = lax.dot_general(
-            left[...], right[...], (((1,), (1,)), ((), ())), preferred_element_type=f32
-        ).astype(bf16)
+def inner_kernel(place, first, second, out, left, right, sems):
+    size = left.shape[0] // SIDE
+
+    def multiply(rows_from, whole):
+        copies = [pltpu.make_async_copy(whole, right, sems.at[SIDE])]
+        for k in range(SIDE):
+            rows = slice(k * size, (k + 1) * size)
+            copies.append(
+                pltpu.make_async_copy(rows_from.at[rows, :], left.at[rows, :], sems.at[k])
+            )
+        for copy in copies:
+            copy.start()
+        copies[0].wait()
+        for k in range(SIDE):
+            copies[k + 1].wait()
+            rows = slice(k * size, (k + 1) * size)
+            out[rows, :] = lax.dot_general(
+                left[rows, :], right[...], (((1,), (1,)), ((), ())), preferred_element_type=f32
+            ).astype(bf16)
 
     pl.when(place[0] == 1)(lambda: multiply(second, first))
     pl.when(place[0] == 0)(lambda: multiply(first, second))
@@ -236,7 +250,7 @@
         place,
         pieces,
         [shape((half, half), bf16)],
-        space=pltpu.HBM,
+        space=pl.ANY,
         scratch=[pltpu.SemaphoreType.DMA((2 * SIDE,))],
     )
     weight_half = jnp.where(
@@ -251,7 +265,8 @@
         jnp.concatenate([zeros, line_values[:share]], axis=1),
     )
 
-    own = tie(own, turned)
+    coupling_out = [turned] + [along_reduce(turned, step) for step in (1, 2, 3)]
+    own = tie(own, coupling_out)
 
     message = own.astype(bf16)
     final = message
@@ -266,14 +281,15 @@
                 [first, second],
                 [shape((line, line), bf16)],
                 flops=2 * line * line * nodes,
+                space=pltpu.HBM,
+                scratch=[
+                    pltpu.VMEM((line, nodes), bf16),
+                    pltpu.VMEM((line, nodes), bf16),
+                    pltpu.SemaphoreType.DMA((SIDE + 1,)),
+                ],
             )
             inner_all = over_other(inner)
             own = tie(own, inner)
-        if turn == 10:
-            turned = tie(turned, message)
-            coupling_out = [turned] + [along_reduce(turned, step) for step in (1, 2, 3)]
-        if turn == 12:
-            own = tie(own, coupling_out)
         if turn == 15:
             own = tie(own, inner_all)
         product = lax.dot_general(
@@ -288,12 +304,15 @@
     folded = jnp.dot(
         jnp.concatenate(coupling_out), inner_all, preferred_element_type=f32
     ).astype(bf16)
+    rounded = total.astype(bf16)
+
+    rest = permuted(rounded, lambda p, y, x: (p, other(p, y), x))
+
+    back = jnp.dot(rounded, block, preferred_element_type=f32).astype(bf16)
+    folded, back = tie((folded, back))
     back_rows = [folded[:rows]] + [
         along_reduce(folded[step * rows : (step + 1) * rows], step) for step in (1, 2, 3)
     ]
-    rounded = tie(total.astype(bf16), folded)
-
-    back = jnp.dot(rounded, block, preferred_element_type=f32).astype(bf16)
     mine = lax.dynamic_slice(back, (0, in_place * line), (share, line))
     theirs = lax.dynamic_slice(back, (0, (1 - in_place) * line), (share, line))
     later = range(1, PARTITIONS)
@@ -302,7 +321,6 @@
     ).astype(f32) + permuted(mine, lambda p, y, x: (p - 1, y, x), later).astype(f32)
     following = following.astype(bf16)
 
-    rest = permuted(rounded, lambda p, y, x: (p, other(p, y), x))
     m0, m1, r0, r1 = rounded[:, :line], rounded[:, line:], rest[:, :line], rest[:, line:]
     lines = jnp.where(
         even,

time: 174 us -> 179 us (1.029); the launches traced: 171 us -> 178 us
  starting transfers between devices: 55.5 us -> 71.2 us
  local copies, waits for them, and re-layouts: 9.88 us -> 4.31 us
  waiting for transfers between devices: 68.6 us -> 64.1 us
  Pallas kernels: 6.67 us -> 9.04 us
    ppermute x51, starting transfers between devices: 55.4 us -> 71.1 us  [permuted(): return lax.ppermute(value, AXES, pairs)]
    all_gather x2, waiting for transfers between devices: 6.68 us -> 1.76 us  [over_axis(): lax.all_gather(array, 'blk', axis=0, tiled=True, axis_index_groups=groups)]
    unnamed x34 -> x24, local copies, waits for them, and re-layouts: 6.94 us -> 3.22 us
    pallas_call x5, Pallas kernels: 6.67 us -> 9.04 us  [kernel_call(): pl.pallas_call(body, out_shape=out_shapes, in_specs=[pl.BlockSpec(memory_...]
    reshape x3, local copies, waits for them, and re-layouts: 2.81 us -> 0.96 us  [shards(): coupling_late.reshape(rows, SIDE, SIDE, rows).transpose(0, 2, 1, 3)]
  transfers between devices with their start and end apart: 54 -> 54, of which waited for: 20 -> 19; matrix products, arithmetic and copies ran while one was open for 9% -> 8% of each run, Pallas kernels for 2% -> 2%
where the time goes in v13:
time: 179 us; the launch traced here: 178 us
  starting transfers between devices  71.2 us (40%)
  waiting for transfers between devices  64.1 us (36%)
  between operations  14.4 us (8%)
  matrix products  12.6 us (7%)
  Pallas kernels  9.04 us (5%)
  local copies, waits for them, and re-layouts  4.31 us (2%)
  other arithmetic  2.87 us (2%)
    ppermute x51, starting transfers between devices, permuted(): return lax.ppermute(value, AXES, pairs)  71.1 us
    ppermute x51, waiting for transfers between devices, permuted(): return lax.ppermute(value, AXES, pairs)  62.3 us
    dot_general x15, matrix products, shards(): lax.dot_general(previous, block, (((1,), (1,)), ((), ())), preferred_elem...  9.76 us
    pallas_call x5, Pallas kernels, kernel_call(): pl.pallas_call(body, out_shape=out_shapes, in_specs=[pl.BlockSpec(memory_...  9.04 us
  transfers between devices with their start and end apart: 54, of which 19 were waited for; matrix products, arithmetic and copies ran while one was open for 8% of the time, Pallas kernels for 2%

profile of v13, /device:TPU:224, one launch (start us, length us, event | category | flops | bytes accessed | tf_op | source)
XLA Modules:
  0.0 178.5 jit_solution(11204266617393789958)
XLA Ops:
  7.3 2.3 %bitcast_select_fusion = (bf16[128,2048]{1,0:T(8,128)(2,1)}, bf16[128,2048]{1,0:T(8,128)(2,1)}) fusion(bf16[1,128,2048]{2,1,0:T(8,128)(2,1)} %param.6, pred[]{:T(512)S(6)} %eq.59, bf16[1,128,2048]{2,1,0:T(8,128)(2,1)} %param.7), kind=kLoop, calls=%fused_computation.57 | loop fusion | flops 524288 | bytes 2097153 | tf_op jit(solution)/shard_map/jit(_where)/select_n | solution.py:207
  9.8 1.6 collective-permute-start.1
  11.3 2.7 %collective-permute-start.2 = (f32[24,128]{1,0:T(8,128)S(1)}, f32[24,128]{1,0:T(8,128)S(1)}, u32[]{:S(2)}, u32[]{:S(2)}) collective-permute-start(f32[24,128]{1,0:T(8,128)S(1)} %get-tuple-element.81), channel_id=1, source_target_pairs={{0,2},{1,3},{2,0},{3,1},{4,6},{5,7},{6,4},{7,5},{8,10},{9,11},{10,... | collective-permute-start | bytes 36872 | tf_op jit(solution)/shard_map/ppermute | solution.py:29
  15.2 1.7 collective-permute-start
  16.9 2.1 %collective-permute-done.3 = f32[24,128]{1,0:T(8,128)S(1)} collective-permute-done((f32[24,128]{1,0:T(8,128)S(1)}, f32[24,128]{1,0:T(8,128)S(1)}, u32[]{:S(2)}, u32[]{:S(2)}) %collective-permute-start.3) | collective-permute-done | bytes 12320 | tf_op jit(solution)/shard_map/ppermute | solution.py:29
  19.0 2.7 %collective-permute-done = bf16[128,1024]{1,0:T(8,128)(2,1)S(1)} collective-permute-done((bf16[128,1024]{1,0:T(8,128)(2,1)S(1)}, bf16[128,1024]{1,0:T(8,128)(2,1)S(1)}, u32[]{:S(2)}, u32[]{:S(2)}) %collective-permute-start) | collective-permute-done | bytes 262176 | tf_op jit(solution)/shard_map/ppermute | solution.py:29
  23.3 4.0 %collective-permute-start.5 = (bf16[128,2048]{1,0:T(8,128)(2,1)S(1)}, bf16[128,2048]{1,0:T(8,128)(2,1)S(1)}, u32[]{:S(2)}, u32[]{:S(2)}) collective-permute-start(bf16[128,2048]{1,0:T(8,128)(2,1)S(1)} %broadcast_select_fusion), channel_id=1, source_target_pairs={{0,2},{1,3},{2,0},{3,1},{4,6},{5,7},{6,4},{7,5},{8,10},{9,11},{10,... | collective-permute-start | bytes 1572872 | tf_op jit(solution)/shard_map/ppermute | solution.py:29
  27.8 4.2 %collective-permute-start.11 = (bf16[256,1024]{1,0:T(8,128)(2,1)S(1)}, bf16[256,1024]{1,0:T(8,128)(2,1)S(1)}, u32[]{:S(2)}, u32[]{:S(2)}) collective-permute-start(bf16[256,1024]{1,0:T(8,128)(2,1)S(1)} %maximum_select_fusion.refs_0_), channel_id=1, source_target_pairs={{0,2},{1,3},{2,0},{3,1},{4,6},{5,7},{6,4},{7,5},{8,10},{9,11},{10,... | collective-permute-start | bytes 1572872 | tf_op jit(solution)/shard_map/ppermute | solution.py:29
  32.0 3.5 %collective-permute-done.4 = bf16[128,2048]{1,0:T(8,128)(2,1)S(1)} collective-permute-done((bf16[128,2048]{1,0:T(8,128)(2,1)S(1)}, bf16[128,2048]{1,0:T(8,128)(2,1)S(1)}, u32[]{:S(2)}, u32[]{:S(2)}) %collective-permute-start.4) | collective-permute-done | bytes 524320 | tf_op jit(solution)/shard_map/ppermute | solution.py:29
  35.5 2.8 %collective-permute-start.12 = (bf16[256,1024]{1,0:T(8,128)(2,1)S(1)}, bf16[256,1024]{1,0:T(8,128)(2,1)S(1)}, u32[]{:S(2)}, u32[]{:S(2)}) collective-permute-start(bf16[256,1024]{1,0:T(8,128)(2,1)S(1)} %maximum_select_fusion.refs_0_), channel_id=1, source_target_pairs={{0,3},{1,2},{2,1},{3,0},{4,7},{5,6},{6,5},{7,4},{8,11},{9,10},{10,... | collective-permute-start | bytes 1572872 | tf_op jit(solution)/shard_map/ppermute | solution.py:29
  38.4 10.7 %collective-permute-done.5 = bf16[128,2048]{1,0:T(8,128)(2,1)S(1)} collective-permute-done((bf16[128,2048]{1,0:T(8,128)(2,1)S(1)}, bf16[128,2048]{1,0:T(8,128)(2,1)S(1)}, u32[]{:S(2)}, u32[]{:S(2)}) %collective-permute-start.5) | collective-permute-done | bytes 524320 | tf_op jit(solution)/shard_map/ppermute | solution.py:29
  49.1 3.2 %collective-permute-start.7 = (f32[1,512]{1,0:T(1,128)S(1)}, f32[1,512]{1,0:T(1,128)S(1)}, u32[]{:S(2)}, u32[]{:S(2)}) collective-permute-start(f32[1,512]{1,0:T(1,128)S(1)} %slice.38), channel_id=1, source_target_pairs={{0,4},{1,5},{2,6},{3,7},{4,0},{5,1},{6,2},{7,3},{8,12},{9,13},{10,... | collective-permute-start | bytes 6152 | tf_op jit(solution)/shard_map/ppermute | solution.py:29
  52.3 2.4 %collective-permute-start.8 = (bf16[16,1024]{1,0:T(8,128)(2,1)S(1)}, bf16[16,1024]{1,0:T(8,128)(2,1)S(1)}, u32[]{:S(2)}, u32[]{:S(2)}) collective-permute-start(bf16[16,1024]{1,0:T(8,128)(2,1)S(1)} %convert_element_type.217), channel_id=1, source_target_pairs={{0,20},{1,21},{2,22},{3,23},{4,16},{5,17},{6,18},{7,19},{8,28},{9,... | collective-permute-start | bytes 98312 | tf_op jit(solution)/shard_map/ppermute | solution.py:29
  54.7 3.9 %collective-permute-start.9 = (bf16[16,1024]{1,0:T(8,128)(2,1)S(1)}, bf16[16,1024]{1,0:T(8,128)(2,1)S(1)}, u32[]{:S(2)}, u32[]{:S(2)}) collective-permute-start(bf16[16,1024]{1,0:T(8,128)(2,1)S(1)} %convert_element_type.217), channel_id=1, source_target_pairs={{0,16},{1,17},{2,18},{3,19},{4,20},{5,21},{6,22},{7,23},{8,24},{9,... | collective-permute-start | bytes 98312 | tf_op jit(solution)/shard_map/ppermute | solution.py:29
  58.6 4.0 %collective-permute-done.11.refs_2_ = bf16[256,1024]{1,0:T(8,128)(2,1)S(1)} collective-permute-done((bf16[256,1024]{1,0:T(8,128)(2,1)S(1)}, bf16[256,1024]{1,0:T(8,128)(2,1)S(1)}, u32[]{:S(2)}, u32[]{:S(2)}) %collective-permute-start.11) | collective-permute-done | bytes 524320 | tf_op jit(solution)/shard_map/ppermute | solution.py:29
  62.6 3.4 %collective-permute-done.12.refs_3_ = bf16[256,1024]{1,0:T(8,128)(2,1)S(1)} collective-permute-done((bf16[256,1024]{1,0:T(8,128)(2,1)S(1)}, bf16[256,1024]{1,0:T(8,128)(2,1)S(1)}, u32[]{:S(2)}, u32[]{:S(2)}) %collective-permute-start.12) | collective-permute-done | bytes 524320 | tf_op jit(solution)/shard_map/ppermute | solution.py:29
  66.0 0.8 shard_map.86
  67.4 0.7 collective-permute-start.13
  68.1 0.7 collective-permute-start.14
  69.5 3.3 %collective-permute-start.15 = (bf16[16,1024]{1,0:T(8,128)(2,1)S(1)}, bf16[16,1024]{1,0:T(8,128)(2,1)S(1)}, u32[]{:S(2)}, u32[]{:S(2)}) collective-permute-start(bf16[16,1024]{1,0:T(8,128)(2,1)S(1)} %fusion.27), channel_id=1, source_target_pairs={{0,20},{1,21},{2,22},{3,23},{4,16},{5,17},{6,18},{7,19},{8,28},{9,... | collective-permute-start | bytes 98312 | tf_op jit(solution)/shard_map/ppermute | solution.py:29
  73.1 1.2 collective-permute-done.15
  75.0 0.7 collective-permute-start.17
  75.7 0.8 collective-permute-start.18
  77.2 2.2 %collective-permute-start.19 = (bf16[16,1024]{1,0:T(8,128)(2,1)S(1)}, bf16[16,1024]{1,0:T(8,128)(2,1)S(1)}, u32[]{:S(2)}, u32[]{:S(2)}) collective-permute-start(bf16[16,1024]{1,0:T(8,128)(2,1)S(1)} %fusion.29), channel_id=1, source_target_pairs={{0,20},{1,21},{2,22},{3,23},{4,16},{5,17},{6,18},{7,19},{8,28},{9,... | collective-permute-start | bytes 98312 | tf_op jit(solution)/shard_map/ppermute | solution.py:29
  79.4 1.6 collective-permute-done.19
  81.6 0.7 collective-permute-start.21
  82.3 0.7 collective-permute-start.22
  83.6 2.1 %collective-permute-start.23 = (bf16[16,1024]{1,0:T(8,128)(2,1)S(1)}, bf16[16,1024]{1,0:T(8,128)(2,1)S(1)}, u32[]{:S(2)}, u32[]{:S(2)}) collective-permute-start(bf16[16,1024]{1,0:T(8,128)(2,1)S(1)} %fusion.31), channel_id=1, source_target_pairs={{0,20},{1,21},{2,22},{3,23},{4,16},{5,17},{6,18},{7,19},{8,28},{9,... | collective-permute-start | bytes 98312 | tf_op jit(solution)/shard_map/ppermute | solution.py:29
  85.8 1.6 collective-permute-done.23
  88.0 1.8 all-gather.6.cloned.1.call-done.second
  89.8 1.6 copy-done
  91.4 1.6 copy-done.1
  93.0 4.4 %shard_map.87 = bf16[512,512]{1,0:T(8,128)(2,1)} custom-call(s32[1]{0:T(128)} %bitcast.21.place, bf16[512,2048]{1,0:T(8,128)(2,1)S(1)} %copy-done, bf16[512,2048]{1,0:T(8,128)(2,1)S(1)} %copy-done.1), custom_call_target="tpu_custom_call" | custom-call | flops 1073741824 | bytes 4718592 | tf_op jit(solution)/shard_map/pallas_call | solution.py:58
  97.5 0.7 collective-permute-start.25
  98.1 0.7 collective-permute-start.26
  99.5 0.9 collective-permute-start.27
  100.4 0.7 collective-permute-start.28
  101.1 2.1 %collective-permute-done.27 = bf16[16,1024]{1,0:T(8,128)(2,1)S(1)} collective-permute-done((bf16[16,1024]{1,0:T(8,128)(2,1)S(1)}, bf16[16,1024]{1,0:T(8,128)(2,1)S(1)}, u32[]{:S(2)}, u32[]{:S(2)}) %collective-permute-start.27) | collective-permute-done | bytes 32800 | tf_op jit(solution)/shard_map/ppermute | solution.py:29
  103.8 0.7 collective-permute-start.29
  104.5 0.7 collective-permute-start.30
  105.8 1.2 collective-permute-start.31
  107.5 1.8 collective-permute-done.31
  109.9 0.7 collective-permute-start.33
  111.9 1.2 collective-permute-start.35
  113.5 1.8 collective-permute-done.35
  115.9 1.3 collective-permute-start.37
  117.2 1.3 collective-permute-start.38
  118.5 16.9 %collective-permute-done.37 = bf16[16,1024]{1,0:T(8,128)(2,1)S(1)} collective-permute-done((bf16[16,1024]{1,0:T(8,128)(2,1)S(1)}, bf16[16,1024]{1,0:T(8,128)(2,1)S(1)}, u32[]{:S(2)}, u32[]{:S(2)}) %collective-permute-start.37) | collective-permute-done | bytes 32800 | tf_op jit(solution)/shard_map/ppermute | solution.py:29
  136.5 2.4 %collective-permute-start.40 = (bf16[16,1024]{1,0:T(8,128)(2,1)S(1)}, bf16[16,1024]{1,0:T(8,128)(2,1)S(1)}, u32[]{:S(2)}, u32[]{:S(2)}) collective-permute-start(bf16[16,1024]{1,0:T(8,128)(2,1)S(1)} %fusion.39), channel_id=1, source_target_pairs={{0,16},{1,17},{2,18},{3,19},{4,20},{5,21},{6,22},{7,23},{8,24},{9,... | collective-permute-start | bytes 98312 | tf_op jit(solution)/shard_map/ppermute | solution.py:29
  138.9 0.9 collective-permute-done.39
  140.5 2.3 %collective-permute-start.41 = (bf16[16,1024]{1,0:T(8,128)(2,1)S(1)}, bf16[16,1024]{1,0:T(8,128)(2,1)S(1)}, u32[]{:S(2)}, u32[]{:S(2)}) collective-permute-start(bf16[16,1024]{1,0:T(8,128)(2,1)S(1)} %fusion.41), channel_id=1, source_target_pairs={{0,4},{1,5},{2,6},{3,7},{4,0},{5,1},{6,2},{7,3},{8,12},{9,13},{10,... | collective-permute-start | bytes 98312 | tf_op jit(solution)/shard_map/ppermute | solution.py:29
  142.8 2.4 %fusion.8 = bf16[512,512]{1,0:T(8,128)(2,1)S(1)} fusion(bf16[2048,512]{1,0:T(8,128)(2,1)S(1)} %copy-done.7, bf16[128,2048]{1,0:T(8,128)(2,1)} %copy-done.11, bf16[128,2048]{1,0:T(8,128)(2,1)} %copy-done.10, bf16[128,2048]{1,0:T(8,128)(2,1)S(1)} %copy-done.9, bf16[128,2048]{1,0:T(8,128)(2,1)S(1)} %broadcast_select_fusion), kind=kOutput, calls=%fused_computation.8 | convolution fusion | flops 1082392576 | bytes 4718592 | tf_op jit(solution)/shard_map/dot_general | solution.py:304
  145.3 1.6 collective-permute-start.45
  147.4 3.2 %collective-permute-start.43 = (bf16[128,512]{1,0:T(8,128)(2,1)S(1)}, bf16[128,512]{1,0:T(8,128)(2,1)S(1)}, u32[]{:S(2)}, u32[]{:S(2)}) collective-permute-start(bf16[128,512]{1,0:T(8,128)(2,1)S(1)} %get-tuple-element.44), channel_id=1, source_target_pairs={{0,2},{1,3},{2,0},{3,1},{4,6},{5,7},{6,4},{7,5},{8,10},{9,11},{10,... | collective-permute-start | bytes 393224 | tf_op jit(solution)/shard_map/ppermute | solution.py:29
  150.6 1.9 %collective-permute-start.46 = (bf16[16,512]{1,0:T(8,128)(2,1)S(1)}, bf16[16,512]{1,0:T(8,128)(2,1)S(1)}, u32[]{:S(2)}, u32[]{:S(2)}) collective-permute-start(bf16[16,512]{1,0:T(8,128)(2,1)S(1)} %get-tuple-element.61), channel_id=1, source_target_pairs={{16,4},{17,5},{18,6},{19,7},{20,0},{21,1},{22,2},{23,3},{24,12},{2... | collective-permute-start | bytes 49160 | tf_op jit(solution)/shard_map/ppermute | solution.py:29
  152.5 1.9 %collective-permute-start.47 = (bf16[16,512]{1,0:T(8,128)(2,1)S(1)}, bf16[16,512]{1,0:T(8,128)(2,1)S(1)}, u32[]{:S(2)}, u32[]{:S(2)}) collective-permute-start(bf16[16,512]{1,0:T(8,128)(2,1)S(1)} %get-tuple-element.62), channel_id=1, source_target_pairs={{16,0},{17,1},{18,2},{19,3},{20,4},{21,5},{22,6},{23,7},{24,8},{25... | collective-permute-start | bytes 49160 | tf_op jit(solution)/shard_map/ppermute | solution.py:29
  154.5 1.1 collective-permute-done.46
  155.7 1.5 collective-permute-start.44
  157.3 4.6 %collective-permute-done.44.refs_4_ = bf16[128,512]{1,0:T(8,128)(2,1)S(1)} collective-permute-done((bf16[128,512]{1,0:T(8,128)(2,1)S(1)}, bf16[128,512]{1,0:T(8,128)(2,1)S(1)}, u32[]{:S(2)}, u32[]{:S(2)}) %collective-permute-start.44) | collective-permute-done | bytes 131104 | tf_op jit(solution)/shard_map/ppermute | solution.py:29
  162.0 2.9 %collective-permute-start.49 = (bf16[16,2432]{1,0:T(8,128)(2,1)S(1)}, bf16[16,2432]{1,0:T(8,128)(2,1)S(1)}, u32[]{:S(2)}, u32[]{:S(2)}) collective-permute-start(bf16[16,2432]{1,0:T(8,128)(2,1)S(1)} %get-tuple-element.49), channel_id=1, source_target_pairs={{0,2},{1,3},{2,0},{3,1},{4,6},{5,7},{6,4},{7,5},{8,10},{9,11},{10,... | collective-permute-start | bytes 233480 | tf_op jit(solution)/shard_map/ppermute | solution.py:29
  164.9 1.8 collective-permute-start.50
  166.7 1.8 shard_map.88
  168.5 2.0 %collective-permute-done.50.refs_3_ = bf16[16,2432]{1,0:T(8,128)(2,1)S(1)} collective-permute-done((bf16[16,2432]{1,0:T(8,128)(2,1)S(1)}, bf16[16,2432]{1,0:T(8,128)(2,1)S(1)}, u32[]{:S(2)}, u32[]{:S(2)}) %collective-permute-start.50) | collective-permute-done | bytes 77856 | tf_op jit(solution)/shard_map/ppermute | solution.py:29
  170.5 1.5 shard_map.89
  (125 shorter events, 16.4 us)
Async XLA Ops:
  7.2 2.5 %copy-start.4 = (f32[1,128]{1,0:T(1,128)S(1)}, f32[1,128]{1,0:T(1,128)}, u32[]{:S(2)}) copy-start(f32[1,128]{1,0:T(1,128)} %weight.1) | copy-start | bytes 1540
  7.2 2.5 %copy-start.6 = (f32[1,64,128]{2,1,0:T(8,128)S(1)}, f32[1,64,128]{2,1,0:T(8,128)}, u32[]{:S(2)}) copy-start(f32[1,64,128]{2,1,0:T(8,128)} %param.10) | copy-start | bytes 98308
  7.2 7.4 %copy-start.3 = (bf16[1,128,2048]{2,1,0:T(8,128)(2,1)S(1)}, bf16[1,128,2048]{2,1,0:T(8,128)(2,1)}, u32[]{:S(2)}) copy-start(bf16[1,128,2048]{2,1,0:T(8,128)(2,1)} %param.9) | copy-start | bytes 1572868
  7.2 80.8 %all-gather.4.cloned.1.call-start = ((), (), s32[]{:S(2)}) async-start(), calls=%async_computation | async-start | bytes 2621440 | tf_op jit(solution)/shard_map/all_gather | solution.py:162
  7.3 14.6 %copy-start.5 = (bf16[1,128,2048]{2,1,0:T(8,128)(2,1)S(1)}, bf16[1,128,2048]{2,1,0:T(8,128)(2,1)}, u32[]{:S(2)}) copy-start(bf16[1,128,2048]{2,1,0:T(8,128)(2,1)} %param.7) | copy-start | bytes 1572868
  9.6 80.2 %all-gather.6.cloned.1.call-start = ((), (), s32[]{:S(2)}) async-start(), calls=%async_computation.1 | async-start | bytes 2621440 | tf_op jit(solution)/shard_map/all_gather | solution.py:162
  9.8 7.1 %collective-permute-start.1 = (f32[24,128]{1,0:T(8,128)S(1)}, f32[24,128]{1,0:T(8,128)S(1)}, u32[]{:S(2)}, u32[]{:S(2)}) collective-permute-start(f32[24,128]{1,0:T(8,128)S(1)} %get-tuple-element.80), channel_id=1, source_target_pairs={{0,1},{1,0},{2,3},{3,2},{4,5},{5,4},{6,7},{7,6},{8,9},{9,8},{10,11... | collective-permute-start | bytes 36872 | tf_op jit(solution)/shard_map/ppermute | solution.py:29
  11.3 5.5 %collective-permute-start.2 = (f32[24,128]{1,0:T(8,128)S(1)}, f32[24,128]{1,0:T(8,128)S(1)}, u32[]{:S(2)}, u32[]{:S(2)}) collective-permute-start(f32[24,128]{1,0:T(8,128)S(1)} %get-tuple-element.81), channel_id=1, source_target_pairs={{0,2},{1,3},{2,0},{3,1},{4,6},{5,7},{6,4},{7,5},{8,10},{9,11},{10,... | collective-permute-start | bytes 36872 | tf_op jit(solution)/shard_map/ppermute | solution.py:29
  14.1 4.9 %collective-permute-start.3 = (f32[24,128]{1,0:T(8,128)S(1)}, f32[24,128]{1,0:T(8,128)S(1)}, u32[]{:S(2)}, u32[]{:S(2)}) collective-permute-start(f32[24,128]{1,0:T(8,128)S(1)} %get-tuple-element.82), channel_id=1, source_target_pairs={{0,3},{1,2},{2,1},{3,0},{4,7},{5,6},{6,5},{7,4},{8,11},{9,10},{10,... | collective-permute-start | bytes 36872 | tf_op jit(solution)/shard_map/ppermute | solution.py:29
  15.2 6.5 %collective-permute-start = (bf16[128,1024]{1,0:T(8,128)(2,1)S(1)}, bf16[128,1024]{1,0:T(8,128)(2,1)S(1)}, u32[]{:S(2)}, u32[]{:S(2)}) collective-permute-start(bf16[128,1024]{1,0:T(8,128)(2,1)S(1)} %get-tuple-element.22), channel_id=1, source_target_pairs={{0,4},{1,5},{2,6},{3,7},{4,0},{5,1},{6,2},{7,3},{8,12},{9,13},{10,... | collective-permute-start | bytes 786440 | tf_op jit(solution)/shard_map/ppermute | solution.py:29
  22.9 12.6 %collective-permute-start.4 = (bf16[128,2048]{1,0:T(8,128)(2,1)S(1)}, bf16[128,2048]{1,0:T(8,128)(2,1)S(1)}, u32[]{:S(2)}, u32[]{:S(2)}) collective-permute-start(bf16[128,2048]{1,0:T(8,128)(2,1)S(1)} %broadcast_select_fusion), channel_id=1, source_target_pairs={{0,1},{1,0},{2,3},{3,2},{4,5},{5,4},{6,7},{7,6},{8,9},{9,8},{10,11... | collective-permute-start | bytes 1572872 | tf_op jit(solution)/shard_map/ppermute | solution.py:29
  23.3 115.7 %all-gather.8.cloned.1.call-start = ((), (), s32[]{:S(2)}) async-start(), calls=%async_computation.2 | async-start | bytes 2621440 | tf_op jit(solution)/shard_map/all_gather | solution.py:173
  23.3 25.7 %collective-permute-start.5 = (bf16[128,2048]{1,0:T(8,128)(2,1)S(1)}, bf16[128,2048]{1,0:T(8,128)(2,1)S(1)}, u32[]{:S(2)}, u32[]{:S(2)}) collective-permute-start(bf16[128,2048]{1,0:T(8,128)(2,1)S(1)} %broadcast_select_fusion), channel_id=1, source_target_pairs={{0,2},{1,3},{2,0},{3,1},{4,6},{5,7},{6,4},{7,5},{8,10},{9,11},{10,... | collective-permute-start | bytes 1572872 | tf_op jit(solution)/shard_map/ppermute | solution.py:29
  27.3 24.9 %collective-permute-start.6 = (bf16[128,2048]{1,0:T(8,128)(2,1)S(1)}, bf16[128,2048]{1,0:T(8,128)(2,1)S(1)}, u32[]{:S(2)}, u32[]{:S(2)}) collective-permute-start(bf16[128,2048]{1,0:T(8,128)(2,1)S(1)} %broadcast_select_fusion), channel_id=1, source_target_pairs={{0,3},{1,2},{2,1},{3,0},{4,7},{5,6},{6,5},{7,4},{8,11},{9,10},{10,... | collective-permute-start | bytes 1572872 | tf_op jit(solution)/shard_map/ppermute | solution.py:29
  27.8 30.8 %collective-permute-start.10 = (bf16[256,1024]{1,0:T(8,128)(2,1)S(1)}, bf16[256,1024]{1,0:T(8,128)(2,1)S(1)}, u32[]{:S(2)}, u32[]{:S(2)}) collective-permute-start(bf16[256,1024]{1,0:T(8,128)(2,1)S(1)} %maximum_select_fusion.refs_0_), channel_id=1, source_target_pairs={{0,1},{1,0},{2,3},{3,2},{4,5},{5,4},{6,7},{7,6},{8,9},{9,8},{10,11... | collective-permute-start | bytes 1572872 | tf_op jit(solution)/shard_map/ppermute | solution.py:29
  27.8 34.8 %collective-permute-start.11 = (bf16[256,1024]{1,0:T(8,128)(2,1)S(1)}, bf16[256,1024]{1,0:T(8,128)(2,1)S(1)}, u32[]{:S(2)}, u32[]{:S(2)}) collective-permute-start(bf16[256,1024]{1,0:T(8,128)(2,1)S(1)} %maximum_select_fusion.refs_0_), channel_id=1, source_target_pairs={{0,2},{1,3},{2,0},{3,1},{4,6},{5,7},{6,4},{7,5},{8,10},{9,11},{10,... | collective-permute-start | bytes 1572872 | tf_op jit(solution)/shard_map/ppermute | solution.py:29
  35.5 27.1 %copy-start.8 = (bf16[128,2048]{1,0:T(8,128)(2,1)}, bf16[128,2048]{1,0:T(8,128)(2,1)S(1)}, u32[]{:S(2)}) copy-start(bf16[128,2048]{1,0:T(8,128)(2,1)S(1)} %collective-permute-done.4) | copy-start | bytes 1572868
  35.5 30.5 %collective-permute-start.12 = (bf16[256,1024]{1,0:T(8,128)(2,1)S(1)}, bf16[256,1024]{1,0:T(8,128)(2,1)S(1)}, u32[]{:S(2)}, u32[]{:S(2)}) collective-permute-start(bf16[256,1024]{1,0:T(8,128)(2,1)S(1)} %maximum_select_fusion.refs_0_), channel_id=1, source_target_pairs={{0,3},{1,2},{2,1},{3,0},{4,7},{5,6},{6,5},{7,4},{8,11},{9,10},{10,... | collective-permute-start | bytes 1572872 | tf_op jit(solution)/shard_map/ppermute | solution.py:29
  49.1 13.5 %copy-start.10 = (bf16[128,2048]{1,0:T(8,128)(2,1)}, bf16[128,2048]{1,0:T(8,128)(2,1)S(1)}, u32[]{:S(2)}) copy-start(bf16[128,2048]{1,0:T(8,128)(2,1)S(1)} %collective-permute-done.5) | copy-start | bytes 1572868
  49.1 5.7 %collective-permute-start.7 = (f32[1,512]{1,0:T(1,128)S(1)}, f32[1,512]{1,0:T(1,128)S(1)}, u32[]{:S(2)}, u32[]{:S(2)}) collective-permute-start(f32[1,512]{1,0:T(1,128)S(1)} %slice.38), channel_id=1, source_target_pairs={{0,4},{1,5},{2,6},{3,7},{4,0},{5,1},{6,2},{7,3},{8,12},{9,13},{10,... | collective-permute-start | bytes 6152 | tf_op jit(solution)/shard_map/ppermute | solution.py:29
  52.3 10.3 %copy-start.11 = (bf16[128,2048]{1,0:T(8,128)(2,1)}, bf16[128,2048]{1,0:T(8,128)(2,1)S(1)}, u32[]{:S(2)}) copy-start(bf16[128,2048]{1,0:T(8,128)(2,1)S(1)} %collective-permute-done.6) | copy-start | bytes 1572868
  52.3 14.5 %collective-permute-start.8 = (bf16[16,1024]{1,0:T(8,128)(2,1)S(1)}, bf16[16,1024]{1,0:T(8,128)(2,1)S(1)}, u32[]{:S(2)}, u32[]{:S(2)}) collective-permute-start(bf16[16,1024]{1,0:T(8,128)(2,1)S(1)} %convert_element_type.217), channel_id=1, source_target_pairs={{0,20},{1,21},{2,22},{3,23},{4,16},{5,17},{6,18},{7,19},{8,28},{9,... | collective-permute-start | bytes 98312 | tf_op jit(solution)/shard_map/ppermute | solution.py:29
  54.7 12.1 %collective-permute-start.9 = (bf16[16,1024]{1,0:T(8,128)(2,1)S(1)}, bf16[16,1024]{1,0:T(8,128)(2,1)S(1)}, u32[]{:S(2)}, u32[]{:S(2)}) collective-permute-start(bf16[16,1024]{1,0:T(8,128)(2,1)S(1)} %convert_element_type.217), channel_id=1, source_target_pairs={{0,16},{1,17},{2,18},{3,19},{4,20},{5,21},{6,22},{7,23},{8,24},{9,... | collective-permute-start | bytes 98312 | tf_op jit(solution)/shard_map/ppermute | solution.py:29
  67.4 1.3 collective-permute-start.13
  68.1 0.7 collective-permute-start.14
  69.5 4.9 %collective-permute-start.15 = (bf16[16,1024]{1,0:T(8,128)(2,1)S(1)}, bf16[16,1024]{1,0:T(8,128)(2,1)S(1)}, u32[]{:S(2)}, u32[]{:S(2)}) collective-permute-start(bf16[16,1024]{1,0:T(8,128)(2,1)S(1)} %fusion.27), channel_id=1, source_target_pairs={{0,20},{1,21},{2,22},{3,23},{4,16},{5,17},{6,18},{7,19},{8,28},{9,... | collective-permute-start | bytes 98312 | tf_op jit(solution)/shard_map/ppermute | solution.py:29
  72.7 1.6 collective-permute-start.16
  75.0 1.5 collective-permute-start.17
  75.7 0.9 collective-permute-start.18
  77.2 3.8 %collective-permute-start.19 = (bf16[16,1024]{1,0:T(8,128)(2,1)S(1)}, bf16[16,1024]{1,0:T(8,128)(2,1)S(1)}, u32[]{:S(2)}, u32[]{:S(2)}) collective-permute-start(bf16[16,1024]{1,0:T(8,128)(2,1)S(1)} %fusion.29), channel_id=1, source_target_pairs={{0,20},{1,21},{2,22},{3,23},{4,16},{5,17},{6,18},{7,19},{8,28},{9,... | collective-permute-start | bytes 98312 | tf_op jit(solution)/shard_map/ppermute | solution.py:29
  79.4 1.6 collective-permute-start.20
  81.6 1.3 collective-permute-start.21
  82.3 0.7 collective-permute-start.22
  83.6 3.7 %collective-permute-start.23 = (bf16[16,1024]{1,0:T(8,128)(2,1)S(1)}, bf16[16,1024]{1,0:T(8,128)(2,1)S(1)}, u32[]{:S(2)}, u32[]{:S(2)}) collective-permute-start(bf16[16,1024]{1,0:T(8,128)(2,1)S(1)} %fusion.31), channel_id=1, source_target_pairs={{0,20},{1,21},{2,22},{3,23},{4,16},{5,17},{6,18},{7,19},{8,28},{9,... | collective-permute-start | bytes 98312 | tf_op jit(solution)/shard_map/ppermute | solution.py:29
  85.8 1.6 collective-permute-start.24
  97.5 1.3 collective-permute-start.25
  98.1 0.7 collective-permute-start.26
  99.5 3.7 %collective-permute-start.27 = (bf16[16,1024]{1,0:T(8,128)(2,1)S(1)}, bf16[16,1024]{1,0:T(8,128)(2,1)S(1)}, u32[]{:S(2)}, u32[]{:S(2)}) collective-permute-start(bf16[16,1024]{1,0:T(8,128)(2,1)S(1)} %fusion.33), channel_id=1, source_target_pairs={{0,20},{1,21},{2,22},{3,23},{4,16},{5,17},{6,18},{7,19},{8,28},{9,... | collective-permute-start | bytes 98312 | tf_op jit(solution)/shard_map/ppermute | solution.py:29
  100.4 2.7 %collective-permute-start.28 = (bf16[16,1024]{1,0:T(8,128)(2,1)S(1)}, bf16[16,1024]{1,0:T(8,128)(2,1)S(1)}, u32[]{:S(2)}, u32[]{:S(2)}) collective-permute-start(bf16[16,1024]{1,0:T(8,128)(2,1)S(1)} %fusion.33), channel_id=1, source_target_pairs={{0,16},{1,17},{2,18},{3,19},{4,20},{5,21},{6,22},{7,23},{8,24},{9,... | collective-permute-start | bytes 98312 | tf_op jit(solution)/shard_map/ppermute | solution.py:29
  103.8 1.3 collective-permute-start.29
  104.5 0.7 collective-permute-start.30
  105.8 3.4 %collective-permute-start.31 = (bf16[16,1024]{1,0:T(8,128)(2,1)S(1)}, bf16[16,1024]{1,0:T(8,128)(2,1)S(1)}, u32[]{:S(2)}, u32[]{:S(2)}) collective-permute-start(bf16[16,1024]{1,0:T(8,128)(2,1)S(1)} %fusion.35), channel_id=1, source_target_pairs={{0,20},{1,21},{2,22},{3,23},{4,16},{5,17},{6,18},{7,19},{8,28},{9,... | collective-permute-start | bytes 98312 | tf_op jit(solution)/shard_map/ppermute | solution.py:29
  107.1 2.2 %collective-permute-start.32 = (bf16[16,1024]{1,0:T(8,128)(2,1)S(1)}, bf16[16,1024]{1,0:T(8,128)(2,1)S(1)}, u32[]{:S(2)}, u32[]{:S(2)}) collective-permute-start(bf16[16,1024]{1,0:T(8,128)(2,1)S(1)} %fusion.35), channel_id=1, source_target_pairs={{0,16},{1,17},{2,18},{3,19},{4,20},{5,21},{6,22},{7,23},{8,24},{9,... | collective-permute-start | bytes 98312 | tf_op jit(solution)/shard_map/ppermute | solution.py:29
  109.9 1.3 collective-permute-start.33
  110.6 0.7 collective-permute-start.34
  111.9 3.4 %collective-permute-start.35 = (bf16[16,1024]{1,0:T(8,128)(2,1)S(1)}, bf16[16,1024]{1,0:T(8,128)(2,1)S(1)}, u32[]{:S(2)}, u32[]{:S(2)}) collective-permute-start(bf16[16,1024]{1,0:T(8,128)(2,1)S(1)} %fusion.37), channel_id=1, source_target_pairs={{0,20},{1,21},{2,22},{3,23},{4,16},{5,17},{6,18},{7,19},{8,28},{9,... | collective-permute-start | bytes 98312 | tf_op jit(solution)/shard_map/ppermute | solution.py:29
  113.1 2.2 %collective-permute-start.36 = (bf16[16,1024]{1,0:T(8,128)(2,1)S(1)}, bf16[16,1024]{1,0:T(8,128)(2,1)S(1)}, u32[]{:S(2)}, u32[]{:S(2)}) collective-permute-start(bf16[16,1024]{1,0:T(8,128)(2,1)S(1)} %fusion.37), channel_id=1, source_target_pairs={{0,16},{1,17},{2,18},{3,19},{4,20},{5,21},{6,22},{7,23},{8,24},{9,... | collective-permute-start | bytes 98312 | tf_op jit(solution)/shard_map/ppermute | solution.py:29
  115.9 19.5 %collective-permute-start.37 = (bf16[16,1024]{1,0:T(8,128)(2,1)S(1)}, bf16[16,1024]{1,0:T(8,128)(2,1)S(1)}, u32[]{:S(2)}, u32[]{:S(2)}) collective-permute-start(bf16[16,1024]{1,0:T(8,128)(2,1)S(1)} %fusion.38), channel_id=1, source_target_pairs={{208,236},{209,237},{210,238},{211,239},{212,232},{213,233},{214,2... | collective-permute-start | bytes 98312 | tf_op jit(solution)/shard_map/ppermute | solution.py:29
  117.2 18.6 %collective-permute-start.38 = (bf16[16,1024]{1,0:T(8,128)(2,1)S(1)}, bf16[16,1024]{1,0:T(8,128)(2,1)S(1)}, u32[]{:S(2)}, u32[]{:S(2)}) collective-permute-start(bf16[16,1024]{1,0:T(8,128)(2,1)S(1)} %fusion.38), channel_id=1, source_target_pairs={{208,224},{209,225},{210,226},{211,227},{212,228},{213,229},{214,2... | collective-permute-start | bytes 98312 | tf_op jit(solution)/shard_map/ppermute | solution.py:29
  136.5 3.4 %collective-permute-start.39 = (bf16[16,1024]{1,0:T(8,128)(2,1)S(1)}, bf16[16,1024]{1,0:T(8,128)(2,1)S(1)}, u32[]{:S(2)}, u32[]{:S(2)}) collective-permute-start(bf16[16,1024]{1,0:T(8,128)(2,1)S(1)} %fusion.39), channel_id=1, source_target_pairs={{0,20},{1,21},{2,22},{3,23},{4,16},{5,17},{6,18},{7,19},{8,28},{9,... | collective-permute-start | bytes 98312 | tf_op jit(solution)/shard_map/ppermute | solution.py:29
  136.5 3.4 %collective-permute-start.40 = (bf16[16,1024]{1,0:T(8,128)(2,1)S(1)}, bf16[16,1024]{1,0:T(8,128)(2,1)S(1)}, u32[]{:S(2)}, u32[]{:S(2)}) collective-permute-start(bf16[16,1024]{1,0:T(8,128)(2,1)S(1)} %fusion.39), channel_id=1, source_target_pairs={{0,16},{1,17},{2,18},{3,19},{4,20},{5,21},{6,22},{7,23},{8,24},{9,... | collective-permute-start | bytes 98312 | tf_op jit(solution)/shard_map/ppermute | solution.py:29
  138.9 3.9 %copy-start.7 = (bf16[2048,512]{1,0:T(8,128)(2,1)S(1)}, bf16[2048,512]{1,0:T(8,128)(2,1)}, u32[]{:S(2)}) copy-start(bf16[2048,512]{1,0:T(8,128)(2,1)} %all-gather.8.cloned.1.call-done) | copy-start | bytes 6291460
  138.9 3.9 %copy-start.9 = (bf16[128,2048]{1,0:T(8,128)(2,1)S(1)}, bf16[128,2048]{1,0:T(8,128)(2,1)}, u32[]{:S(2)}) copy-start(bf16[128,2048]{1,0:T(8,128)(2,1)} %copy-done.8) | copy-start | bytes 1572868
  140.5 4.8 %collective-permute-start.41 = (bf16[16,1024]{1,0:T(8,128)(2,1)S(1)}, bf16[16,1024]{1,0:T(8,128)(2,1)S(1)}, u32[]{:S(2)}, u32[]{:S(2)}) collective-permute-start(bf16[16,1024]{1,0:T(8,128)(2,1)S(1)} %fusion.41), channel_id=1, source_target_pairs={{0,4},{1,5},{2,6},{3,7},{4,0},{5,1},{6,2},{7,3},{8,12},{9,13},{10,... | collective-permute-start | bytes 98312 | tf_op jit(solution)/shard_map/ppermute | solution.py:29
  145.3 11.9 %collective-permute-start.45 = (bf16[16,1024]{1,0:T(8,128)(2,1)S(1)}, bf16[16,1024]{1,0:T(8,128)(2,1)S(1)}, u32[]{:S(2)}, u32[]{:S(2)}) collective-permute-start(bf16[16,1024]{1,0:T(8,128)(2,1)S(1)} %get-tuple-element.52), channel_id=1, source_target_pairs={{0,12},{1,13},{2,14},{3,15},{4,8},{5,9},{6,10},{7,11},{8,4},{9,5},... | collective-permute-start | bytes 98312 | tf_op jit(solution)/shard_map/ppermute | solution.py:29
  146.9 19.9 %copy-start.2 = (f32[1,128,2048]{2,1,0:T(8,128)S(1)}, f32[1,128,2048]{2,1,0:T(8,128)}, u32[]{:S(2)}) copy-start(f32[1,128,2048]{2,1,0:T(8,128)} %param.8) | copy-start | bytes 3145732
  147.3 9.9 %collective-permute-start.42 = (bf16[128,512]{1,0:T(8,128)(2,1)S(1)}, bf16[128,512]{1,0:T(8,128)(2,1)S(1)}, u32[]{:S(2)}, u32[]{:S(2)}) collective-permute-start(bf16[128,512]{1,0:T(8,128)(2,1)S(1)} %get-tuple-element.45), channel_id=1, source_target_pairs={{0,1},{1,0},{2,3},{3,2},{4,5},{5,4},{6,7},{7,6},{8,9},{9,8},{10,11... | collective-permute-start | bytes 393224 | tf_op jit(solution)/shard_map/ppermute | solution.py:29
  147.4 9.9 %collective-permute-start.43 = (bf16[128,512]{1,0:T(8,128)(2,1)S(1)}, bf16[128,512]{1,0:T(8,128)(2,1)S(1)}, u32[]{:S(2)}, u32[]{:S(2)}) collective-permute-start(bf16[128,512]{1,0:T(8,128)(2,1)S(1)} %get-tuple-element.44), channel_id=1, source_target_pairs={{0,2},{1,3},{2,0},{3,1},{4,6},{5,7},{6,4},{7,5},{8,10},{9,11},{10,... | collective-permute-start | bytes 393224 | tf_op jit(solution)/shard_map/ppermute | solution.py:29
  150.6 5.0 %collective-permute-start.46 = (bf16[16,512]{1,0:T(8,128)(2,1)S(1)}, bf16[16,512]{1,0:T(8,128)(2,1)S(1)}, u32[]{:S(2)}, u32[]{:S(2)}) collective-permute-start(bf16[16,512]{1,0:T(8,128)(2,1)S(1)} %get-tuple-element.61), channel_id=1, source_target_pairs={{16,4},{17,5},{18,6},{19,7},{20,0},{21,1},{22,2},{23,3},{24,12},{2... | collective-permute-start | bytes 49160 | tf_op jit(solution)/shard_map/ppermute | solution.py:29
  152.5 4.6 %collective-permute-start.47 = (bf16[16,512]{1,0:T(8,128)(2,1)S(1)}, bf16[16,512]{1,0:T(8,128)(2,1)S(1)}, u32[]{:S(2)}, u32[]{:S(2)}) collective-permute-start(bf16[16,512]{1,0:T(8,128)(2,1)S(1)} %get-tuple-element.62), channel_id=1, source_target_pairs={{16,0},{17,1},{18,2},{19,3},{20,4},{21,5},{22,6},{23,7},{24,8},{25... | collective-permute-start | bytes 49160 | tf_op jit(solution)/shard_map/ppermute | solution.py:29
  155.7 6.2 %collective-permute-start.44 = (bf16[128,512]{1,0:T(8,128)(2,1)S(1)}, bf16[128,512]{1,0:T(8,128)(2,1)S(1)}, u32[]{:S(2)}, u32[]{:S(2)}) collective-permute-start(bf16[128,512]{1,0:T(8,128)(2,1)S(1)} %get-tuple-element.43), channel_id=1, source_target_pairs={{0,3},{1,2},{2,1},{3,0},{4,7},{5,6},{6,5},{7,4},{8,11},{9,10},{10,... | collective-permute-start | bytes 393224 | tf_op jit(solution)/shard_map/ppermute | solution.py:29
  161.9 6.6 %collective-permute-start.48 = (bf16[16,2432]{1,0:T(8,128)(2,1)S(1)}, bf16[16,2432]{1,0:T(8,128)(2,1)S(1)}, u32[]{:S(2)}, u32[]{:S(2)}) collective-permute-start(bf16[16,2432]{1,0:T(8,128)(2,1)S(1)} %get-tuple-element.48), channel_id=1, source_target_pairs={{0,1},{1,0},{2,3},{3,2},{4,5},{5,4},{6,7},{7,6},{8,9},{9,8},{10,11... | collective-permute-start | bytes 233480 | tf_op jit(solution)/shard_map/ppermute | solution.py:29
  162.0 6.5 %collective-permute-start.49 = (bf16[16,2432]{1,0:T(8,128)(2,1)S(1)}, bf16[16,2432]{1,0:T(8,128)(2,1)S(1)}, u32[]{:S(2)}, u32[]{:S(2)}) collective-permute-start(bf16[16,2432]{1,0:T(8,128)(2,1)S(1)} %get-tuple-element.49), channel_id=1, source_target_pairs={{0,2},{1,3},{2,0},{3,1},{4,6},{5,7},{6,4},{7,5},{8,10},{9,11},{10,... | collective-permute-start | bytes 233480 | tf_op jit(solution)/shard_map/ppermute | solution.py:29
  164.9 5.6 %collective-permute-start.50 = (bf16[16,2432]{1,0:T(8,128)(2,1)S(1)}, bf16[16,2432]{1,0:T(8,128)(2,1)S(1)}, u32[]{:S(2)}, u32[]{:S(2)}) collective-permute-start(bf16[16,2432]{1,0:T(8,128)(2,1)S(1)} %get-tuple-element.47), channel_id=1, source_target_pairs={{0,3},{1,2},{2,1},{3,0},{4,7},{5,6},{6,5},{7,4},{8,11},{9,10},{10,... | collective-permute-start | bytes 233480 | tf_op jit(solution)/shard_map/ppermute | solution.py:29
  (2 other events, 3.2 us)
Sparse Core Ops, SparseCore 0:
  9.8 42.0 all-gather.3
  54.3 35.4 all-gather.5
  97.6 30.9 all-gather.7

commit v14 on v8

--- a/solution.py
+++ b/solution.py
@@ -80,12 +80,11 @@
 
 def assemble_link(place, *refs):
     *pieces, out = refs
-    size = pieces[0].shape[0] // 2
+    size = pieces[0].shape[0]
     for step in range(SIDE):
         for half in range(2):
-            out[block_of(half * SIDE + (place[0] ^ step), size), :] = pieces[step][
-                half * size : (half + 1) * size, :
-            ]
+            target = block_of(half * SIDE + (place[0] ^ step), size)
+            out[target, :] = pieces[2 * step + half][...]
 
 
 def schur_kernel(place, *refs):
@@ -205,7 +204,17 @@
     two = jnp.where(
         out_place == 0, jnp.concatenate([keep, got]), jnp.concatenate([got, keep])
     )
-    pieces = spread_x(two)
+    left, right = along_x(two, 1), along_x(two, 3)
+    pieces = [
+        two[:rows],
+        two[rows:],
+        left[:rows],
+        left[rows:],
+        along_x(left[:rows], 3),
+        along_x(right[rows:], 1),
+        right[:rows],
+        right[rows:],
+    ]
     away_weights = permuted(line_weights, lambda p, y, x: (p, partner(p, y), x))
     (block,) = kernel_call(assemble_link, place, pieces, [shape((half, half), bf16)])
     weight_half = jnp.where(
@@ -243,17 +252,19 @@
     ).astype(f32)
     rounded = total.astype(bf16)
 
-    back = jnp.dot(rounded, block, preferred_element_type=f32).astype(bf16)
+    back = jnp.dot(rounded, block, preferred_element_type=f32)
     mine = lax.dynamic_slice(back, (0, in_place * line), (share, line))
-    theirs = lax.dynamic_slice(back, (0, (1 - in_place) * line), (share, line))
-    later = range(1, PARTITIONS)
+    theirs = lax.dynamic_slice(back, (0, (1 - in_place) * line), (share, line)).astype(bf16)
+    rest = permuted(
+        jnp.concatenate([rounded, theirs], axis=1), lambda p, y, x: (p, other(p, y), x)
+    )
     following = permuted(
-        theirs, lambda p, y, x: (p - 1, other(p, y), x), later
-    ).astype(f32) + permuted(mine, lambda p, y, x: (p - 1, y, x), later).astype(f32)
-    following = following.astype(bf16)
-
-    rest = permuted(rounded, lambda p, y, x: (p, other(p, y), x))
-    m0, m1, r0, r1 = rounded[:, :line], rounded[:, line:], rest[:, :line], rest[:, line:]
+        (mine + rest[:, half:].astype(f32)).astype(bf16),
+        lambda p, y, x: (p - 1, y, x),
+        range(1, PARTITIONS),
+    )
+
+    m0, m1, r0, r1 = rounded[:, :line], rounded[:, line:], rest[:, :line], rest[:, line:half]
     lines = jnp.where(
         even,
         jnp.where(
@@ -267,6 +278,10 @@
             jnp.concatenate([r0, m0, m1, r1], axis=1),
         ),
     )
+    inner_all = tie(inner_all, rounded)
+    folded = jnp.dot(outer[:, nodes:], inner_all, preferred_element_type=f32).astype(bf16)
+
+    lines = tie(lines, folded)
     sweep_line = lax.dynamic_slice(total, (0, out_place * line), (share, line))
     sweep_high = sweep_line.astype(bf16)
     sweep_low = (sweep_line - sweep_high.astype(f32)).astype(bf16)
@@ -280,9 +295,6 @@
         return jnp.concatenate([lines] + extra, axis=1)
 
     last = exchange_x(last_chunk)
-
-    inner_all = tie(inner_all, rounded)
-    folded = jnp.dot(outer[:, nodes:], inner_all, preferred_element_type=f32).astype(bf16)
 
     def folded_chunk(step):
         return lax.dynamic_slice(folded, ((r ^ step) * rows, 0), (rows, line))

time: 167 us -> 164 us (0.982)
  waiting for transfers between devices: 78.2 us -> 71.1 us
  starting transfers between devices: 46.9 us -> 51.3 us
    all_gather x3, waiting for transfers between devices: 7.31 us -> 2.78 us  [gathered(): lax.all_gather(array, AXES, axis=0, tiled=True, axis_index_groups=gather_...]
    ppermute x48, starting transfers between devices: 46.7 us -> 51.2 us  [permuted(): return lax.ppermute(value, AXES, pairs)]
    ppermute x48, waiting for transfers between devices: 70.2 us -> 67.6 us  [permuted(): return lax.ppermute(value, AXES, pairs)]
  transfers between devices with their start and end apart: 51 -> 51, of which waited for: 20 -> 22; matrix products, arithmetic and copies ran while one was open for 8% -> 8% of each run, Pallas kernels for 2% -> 2%
where the time goes in v14:
time: 164 us; the launch traced here: 163 us
  waiting for transfers between devices  71.1 us (43%)
  starting transfers between devices  51.3 us (31%)
  matrix products  17.9 us (11%)
  between operations  14.4 us (9%)
  Pallas kernels  4.49 us (3%)
  local copies, waits for them, and re-layouts  2.57 us (2%)
    ppermute x48, waiting for transfers between devices, permuted(): return lax.ppermute(value, AXES, pairs)  67.6 us
    ppermute x48, starting transfers between devices, permuted(): return lax.ppermute(value, AXES, pairs)  51.2 us
    dot_general x15, matrix products, shards(): lax.dot_general(previous, block, (((1,), (1,)), ((), ())), preferred_elem...  9.76 us
    pallas_call x4, Pallas kernels, kernel_call(): pl.pallas_call(body, out_shape=out_shapes, in_specs=[pl.BlockSpec(memory_...  4.49 us
    dot_general x1, matrix products, shards(): lax.dot_general(outer[:, :nodes], coupling_in, (((1,), (1,)), ((), ())),...  4.29 us
    dot_general x1, matrix products, shards(): jnp.dot(outer[:, nodes:], inner_all, preferred_element_type=f32)  3.46 us
  transfers between devices with their start and end apart: 51, of which 22 were waited for; matrix products, arithmetic and copies ran while one was open for 8% of the time, Pallas kernels for 2%

profile of v14, /device:TPU:224, one launch (start us, length us, event | category | flops | bytes accessed | tf_op | source)
XLA Modules:
  0.0 163.3 jit_solution(12682387053491649857)
XLA Ops:
  7.2 0.7 all-gather.9.cloned.1.call-update
  8.0 1.4 reshape_squeeze.3
  10.4 1.1 pad_maximum_fusion
  11.6 1.6 collective-permute-start.1
  13.2 2.7 %collective-permute-start.2 = (f32[24,128]{1,0:T(8,128)S(1)}, f32[24,128]{1,0:T(8,128)S(1)}, u32[]{:S(2)}, u32[]{:S(2)}) collective-permute-start(f32[24,128]{1,0:T(8,128)S(1)} %get-tuple-element.75), channel_id=1, source_target_pairs={{0,2},{1,3},{2,0},{3,1},{4,6},{5,7},{6,4},{7,5},{8,10},{9,11},{10,... | collective-permute-start | bytes 36872 | tf_op jit(solution)/shard_map/ppermute | solution.py:29
  17.1 1.7 %collective-permute-start = (bf16[128,1024]{1,0:T(8,128)(2,1)S(1)}, bf16[128,1024]{1,0:T(8,128)(2,1)S(1)}, u32[]{:S(2)}, u32[]{:S(2)}) collective-permute-start(bf16[128,1024]{1,0:T(8,128)(2,1)S(1)} %get-tuple-element.18), channel_id=1, source_target_pairs={{0,4},{1,5},{2,6},{3,7},{4,0},{5,1},{6,2},{7,3},{8,12},{9,13},{10,... | collective-permute-start | bytes 786440 | tf_op jit(solution)/shard_map/ppermute | solution.py:29
  18.8 2.1 %collective-permute-done.3 = f32[24,128]{1,0:T(8,128)S(1)} collective-permute-done((f32[24,128]{1,0:T(8,128)S(1)}, f32[24,128]{1,0:T(8,128)S(1)}, u32[]{:S(2)}, u32[]{:S(2)}) %collective-permute-start.3) | collective-permute-done | bytes 12320 | tf_op jit(solution)/shard_map/ppermute | solution.py:29
  20.9 2.7 %collective-permute-done = bf16[128,1024]{1,0:T(8,128)(2,1)S(1)} collective-permute-done((bf16[128,1024]{1,0:T(8,128)(2,1)S(1)}, bf16[128,1024]{1,0:T(8,128)(2,1)S(1)}, u32[]{:S(2)}, u32[]{:S(2)}) %collective-permute-start) | collective-permute-done | bytes 262176 | tf_op jit(solution)/shard_map/ppermute | solution.py:29
  23.7 2.8 %collective-permute-start.9 = (bf16[256,1024]{1,0:T(8,128)(2,1)S(1)}, bf16[256,1024]{1,0:T(8,128)(2,1)S(1)}, u32[]{:S(2)}, u32[]{:S(2)}) collective-permute-start(bf16[256,1024]{1,0:T(8,128)(2,1)S(1)} %maximum_select_fusion), channel_id=1, source_target_pairs={{0,3},{1,2},{2,1},{3,0},{4,7},{5,6},{6,5},{7,4},{8,11},{9,10},{10,... | collective-permute-start | bytes 1572872 | tf_op jit(solution)/shard_map/ppermute | solution.py:29
  26.6 17.8 %collective-permute-done.9 = bf16[256,1024]{1,0:T(8,128)(2,1)S(1)} collective-permute-done((bf16[256,1024]{1,0:T(8,128)(2,1)S(1)}, bf16[256,1024]{1,0:T(8,128)(2,1)S(1)}, u32[]{:S(2)}, u32[]{:S(2)}) %collective-permute-start.9) | collective-permute-done | bytes 524320 | tf_op jit(solution)/shard_map/ppermute | solution.py:29
  45.1 1.4 collective-permute-start.8
  46.5 1.7 %collective-permute-start.4 = (f32[1,512]{1,0:T(1,128)S(1)}, f32[1,512]{1,0:T(1,128)S(1)}, u32[]{:S(2)}, u32[]{:S(2)}) collective-permute-start(f32[1,512]{1,0:T(1,128)S(1)} %slice.57), channel_id=1, source_target_pairs={{0,4},{1,5},{2,6},{3,7},{4,0},{5,1},{6,2},{7,3},{8,12},{9,13},{10,... | collective-permute-start | bytes 6152 | tf_op jit(solution)/shard_map/ppermute | solution.py:29
  48.8 1.4 collective-permute-done.4
  50.9 1.9 %collective-permute-done.8.refs_4_ = bf16[128,1024]{1,0:T(8,128)(2,1)S(1)} collective-permute-done((bf16[128,1024]{1,0:T(8,128)(2,1)S(1)}, bf16[128,1024]{1,0:T(8,128)(2,1)S(1)}, u32[]{:S(2)}, u32[]{:S(2)}) %collective-permute-start.8) | collective-permute-done | bytes 262176 | tf_op jit(solution)/shard_map/ppermute | solution.py:29
  52.8 0.7 shard_map.86
  54.1 0.7 collective-permute-start.11
  54.8 0.7 collective-permute-start.12
  55.5 0.7 fusion.26
  56.1 2.6 %collective-permute-start.14 = (bf16[16,1024]{1,0:T(8,128)(2,1)S(1)}, bf16[16,1024]{1,0:T(8,128)(2,1)S(1)}, u32[]{:S(2)}, u32[]{:S(2)}) collective-permute-start(bf16[16,1024]{1,0:T(8,128)(2,1)S(1)} %fusion.26), channel_id=1, source_target_pairs={{0,16},{1,17},{2,18},{3,19},{4,20},{5,21},{6,22},{7,23},{8,24},{9,... | collective-permute-start | bytes 98312 | tf_op jit(solution)/shard_map/ppermute | solution.py:29
  58.8 0.7 collective-permute-done.13
  60.3 0.7 collective-permute-start.15
  60.9 0.7 collective-permute-start.16
  61.6 0.7 fusion.28
  62.4 2.4 %collective-permute-start.18 = (bf16[16,1024]{1,0:T(8,128)(2,1)S(1)}, bf16[16,1024]{1,0:T(8,128)(2,1)S(1)}, u32[]{:S(2)}, u32[]{:S(2)}) collective-permute-start(bf16[16,1024]{1,0:T(8,128)(2,1)S(1)} %fusion.28), channel_id=1, source_target_pairs={{0,16},{1,17},{2,18},{3,19},{4,20},{5,21},{6,22},{7,23},{8,24},{9,... | collective-permute-start | bytes 98312 | tf_op jit(solution)/shard_map/ppermute | solution.py:29
  64.8 1.0 collective-permute-done.17
  66.5 0.7 collective-permute-start.19
  67.1 0.7 collective-permute-start.20
  67.8 0.7 fusion.30
  68.6 2.5 %collective-permute-start.22 = (bf16[16,1024]{1,0:T(8,128)(2,1)S(1)}, bf16[16,1024]{1,0:T(8,128)(2,1)S(1)}, u32[]{:S(2)}, u32[]{:S(2)}) collective-permute-start(bf16[16,1024]{1,0:T(8,128)(2,1)S(1)} %fusion.30), channel_id=1, source_target_pairs={{0,16},{1,17},{2,18},{3,19},{4,20},{5,21},{6,22},{7,23},{8,24},{9,... | collective-permute-start | bytes 98312 | tf_op jit(solution)/shard_map/ppermute | solution.py:29
  71.1 1.0 collective-permute-done.21
  72.8 0.7 collective-permute-start.23
  73.5 0.7 collective-permute-start.24
  74.2 0.7 fusion.32
  75.4 2.1 %collective-permute-start.26 = (bf16[16,1024]{1,0:T(8,128)(2,1)S(1)}, bf16[16,1024]{1,0:T(8,128)(2,1)S(1)}, u32[]{:S(2)}, u32[]{:S(2)}) collective-permute-start(bf16[16,1024]{1,0:T(8,128)(2,1)S(1)} %fusion.32), channel_id=1, source_target_pairs={{0,16},{1,17},{2,18},{3,19},{4,20},{5,21},{6,22},{7,23},{8,24},{9,... | collective-permute-start | bytes 98312 | tf_op jit(solution)/shard_map/ppermute | solution.py:29
  77.5 1.0 collective-permute-done.25
  79.2 0.7 collective-permute-start.27
  79.8 0.7 collective-permute-start.28
  80.6 2.8 %all-gather.5.cloned.1.call-done = bf16[512,4096]{1,0:T(8,128)(2,1)} async-done(((bf16[128,4096]{1,0:T(8,128)(2,1)}), bf16[512,4096]{1,0:T(8,128)(2,1)}) %all-gather.5.cloned.1.call-update) | async-done | bytes 4194320 | tf_op jit(solution)/shard_map/all_gather | solution.py:133
  83.4 4.3 %fusion.7 = bf16[512,512]{1,0:T(8,128)(2,1)} fusion(bf16[512,2048]{1,0:T(8,128)(2,1)} %bitcast.68, bf16[512,4096]{1,0:T(8,128)(2,1)} %all-gather.5.cloned.1.call-done), kind=kOutput, calls=%fused_computation.5 | convolution fusion | flops 1074003968 | bytes 4718592 | tf_op jit(solution)/shard_map/dot_general | solution.py:239
  88.3 0.7 collective-permute-start.29
  89.0 0.9 collective-permute-start.30
  89.9 1.7 %collective-permute-done.29 = bf16[16,1024]{1,0:T(8,128)(2,1)S(1)} collective-permute-done((bf16[16,1024]{1,0:T(8,128)(2,1)S(1)}, bf16[16,1024]{1,0:T(8,128)(2,1)S(1)}, u32[]{:S(2)}, u32[]{:S(2)}) %collective-permute-start.29) | collective-permute-done | bytes 32800 | tf_op jit(solution)/shard_map/ppermute | solution.py:29
  92.3 0.7 collective-permute-start.31
  93.0 0.7 collective-permute-start.32
  94.3 1.1 collective-permute-start.33
  96.1 1.6 collective-permute-done.33
  98.3 1.3 collective-permute-start.35
  99.6 1.3 collective-permute-start.36
  100.9 19.9 %collective-permute-done.35 = bf16[16,1024]{1,0:T(8,128)(2,1)S(1)} collective-permute-done((bf16[16,1024]{1,0:T(8,128)(2,1)S(1)}, bf16[16,1024]{1,0:T(8,128)(2,1)S(1)}, u32[]{:S(2)}, u32[]{:S(2)}) %collective-permute-start.35) | collective-permute-done | bytes 32800 | tf_op jit(solution)/shard_map/ppermute | solution.py:29
  122.0 3.3 %collective-permute-done.37 = bf16[16,1024]{1,0:T(8,128)(2,1)S(1)} collective-permute-done((bf16[16,1024]{1,0:T(8,128)(2,1)S(1)}, bf16[16,1024]{1,0:T(8,128)(2,1)S(1)}, u32[]{:S(2)}, u32[]{:S(2)}) %collective-permute-start.37) | collective-permute-done | bytes 32800 | tf_op jit(solution)/shard_map/ppermute | solution.py:29
  125.3 0.7 fusion.40
  126.1 3.8 %collective-permute-done.39 = bf16[16,1024]{1,0:T(8,128)(2,1)S(1)} collective-permute-done((bf16[16,1024]{1,0:T(8,128)(2,1)S(1)}, bf16[16,1024]{1,0:T(8,128)(2,1)S(1)}, u32[]{:S(2)}, u32[]{:S(2)}) %collective-permute-start.39) | collective-permute-done | bytes 32800 | tf_op jit(solution)/shard_map/ppermute | solution.py:29
  130.3 2.0 %collective-permute-start.43 = (bf16[16,1536]{1,0:T(8,128)(2,1)S(1)}, bf16[16,1536]{1,0:T(8,128)(2,1)S(1)}, u32[]{:S(2)}, u32[]{:S(2)}) collective-permute-start(bf16[16,1536]{1,0:T(8,128)(2,1)S(1)} %pad_maximum_fusion.7), channel_id=1, source_target_pairs={{0,12},{1,13},{2,14},{3,15},{4,8},{5,9},{6,10},{7,11},{8,4},{9,5},... | collective-permute-start | bytes 147464 | tf_op jit(solution)/shard_map/ppermute | solution.py:29
  132.4 3.3 %collective-permute-done.43 = bf16[16,1536]{1,0:T(8,128)(2,1)S(1)} collective-permute-done((bf16[16,1536]{1,0:T(8,128)(2,1)S(1)}, bf16[16,1536]{1,0:T(8,128)(2,1)S(1)}, u32[]{:S(2)}, u32[]{:S(2)}) %collective-permute-start.43) | collective-permute-done | bytes 49184 | tf_op jit(solution)/shard_map/ppermute | solution.py:29
  135.7 1.9 %collective-permute-start.44 = (bf16[16,512]{1,0:T(8,128)(2,1)S(1)}, bf16[16,512]{1,0:T(8,128)(2,1)S(1)}, u32[]{:S(2)}, u32[]{:S(2)}) collective-permute-start(bf16[16,512]{1,0:T(8,128)(2,1)S(1)} %add_convert_fusion.29), channel_id=1, source_target_pairs={{16,0},{17,1},{18,2},{19,3},{20,4},{21,5},{22,6},{23,7},{24,8},{25... | collective-permute-start | bytes 49160 | tf_op jit(solution)/shard_map/ppermute | solution.py:29
  137.7 1.4 collective-permute-done.44
  139.0 3.5 %fusion.4 = bf16[512,512]{1,0:T(8,128)(2,1)S(1)} fusion(bf16[2048,512]{1,0:T(8,128)(2,1)} %all-gather.7.cloned.1.call-done, bf16[512,4096]{1,0:T(8,128)(2,1)} %all-gather.5.cloned.1.call-done), kind=kOutput, calls=%fused_computation.4 | convolution fusion | flops 1074003968 | bytes 4718592 | tf_op jit(solution)/shard_map/dot_general | solution.py:282
  142.7 2.2 %collective-permute-start.41 = (bf16[128,512]{1,0:T(8,128)(2,1)S(1)}, bf16[128,512]{1,0:T(8,128)(2,1)S(1)}, u32[]{:S(2)}, u32[]{:S(2)}) collective-permute-start(bf16[128,512]{1,0:T(8,128)(2,1)S(1)} %get-tuple-element.34), channel_id=1, source_target_pairs={{0,2},{1,3},{2,0},{3,1},{4,6},{5,7},{6,4},{7,5},{8,10},{9,11},{10,... | collective-permute-start | bytes 393224 | tf_op jit(solution)/shard_map/ppermute | solution.py:29
  144.9 2.4 %collective-permute-start.42 = (bf16[128,512]{1,0:T(8,128)(2,1)S(1)}, bf16[128,512]{1,0:T(8,128)(2,1)S(1)}, u32[]{:S(2)}, u32[]{:S(2)}) collective-permute-start(bf16[128,512]{1,0:T(8,128)(2,1)S(1)} %get-tuple-element.33), channel_id=1, source_target_pairs={{0,3},{1,2},{2,1},{3,0},{4,7},{5,6},{6,5},{7,4},{8,11},{9,10},{10,... | collective-permute-start | bytes 393224 | tf_op jit(solution)/shard_map/ppermute | solution.py:29
  147.5 2.2 %collective-permute-start.46 = (bf16[16,2432]{1,0:T(8,128)(2,1)S(1)}, bf16[16,2432]{1,0:T(8,128)(2,1)S(1)}, u32[]{:S(2)}, u32[]{:S(2)}) collective-permute-start(bf16[16,2432]{1,0:T(8,128)(2,1)S(1)} %get-tuple-element.45), channel_id=1, source_target_pairs={{0,2},{1,3},{2,0},{3,1},{4,6},{5,7},{6,4},{7,5},{8,10},{9,11},{10,... | collective-permute-start | bytes 233480 | tf_op jit(solution)/shard_map/ppermute | solution.py:29
  149.7 2.4 %collective-permute-start.47 = (bf16[16,2432]{1,0:T(8,128)(2,1)S(1)}, bf16[16,2432]{1,0:T(8,128)(2,1)S(1)}, u32[]{:S(2)}, u32[]{:S(2)}) collective-permute-start(bf16[16,2432]{1,0:T(8,128)(2,1)S(1)} %get-tuple-element.43), channel_id=1, source_target_pairs={{0,3},{1,2},{2,1},{3,0},{4,7},{5,6},{6,5},{7,4},{8,11},{9,10},{10,... | collective-permute-start | bytes 233480 | tf_op jit(solution)/shard_map/ppermute | solution.py:29
  152.3 1.8 %shard_map.87 = (f32[128,2048]{1,0:T(8,128)}, bf16[128,2048]{1,0:T(8,128)(2,1)S(1)}) custom-call(s32[3]{0:T(128)S(1)} %pad_add_fusion.place, f32[128,2048]{1,0:T(8,128)S(1)} %bitcast.57, bf16[128,512]{1,0:T(8,128)(2,1)S(1)} %get-tuple-element.36.refs_1_, bf16[128,512]{1,0:T(8,128)(2,1)S(1)} %collective-permute-done.40.refs_2_, ...), custom_call_target="tpu_custom_call" | custom-call | bytes 3145728 | tf_op jit(solution)/shard_map/pallas_call | solution.py:58
  154.0 1.3 collective-permute-done.47.refs_3_
  155.3 1.5 shard_map.88
  (112 shorter events, 13.8 us)
Async XLA Ops:
  7.2 2.8 %copy-start.3 = (bf16[1,128,2048]{2,1,0:T(8,128)(2,1)S(1)}, bf16[1,128,2048]{2,1,0:T(8,128)(2,1)}, u32[]{:S(2)}) copy-start(bf16[1,128,2048]{2,1,0:T(8,128)(2,1)} %param.7) | copy-start | bytes 1572868
  7.2 73.4 %all-gather.9.cloned.1.call-start = ((), (), s32[]{:S(2)}) async-start(), calls=%async_computation.2 | async-start | bytes 2621440 | tf_op jit(solution)/shard_map/all_gather | solution.py:133
  7.9 75.4 %all-gather.5.cloned.1.call-start = ((), (), s32[]{:S(2)}) async-start(), calls=%async_computation | async-start | bytes 5242880 | tf_op jit(solution)/shard_map/all_gather | solution.py:133
  9.4 1.0 copy-start.4
  10.0 1.6 copy-start.2
  10.0 1.6 copy-start.5
  10.1 6.4 %copy-start.1 = (bf16[1,128,2048]{2,1,0:T(8,128)(2,1)S(1)}, bf16[1,128,2048]{2,1,0:T(8,128)(2,1)}, u32[]{:S(2)}) copy-start(bf16[1,128,2048]{2,1,0:T(8,128)(2,1)} %param.9) | copy-start | bytes 1572868
  11.5 127.6 %all-gather.7.cloned.1.call-start = ((), (), s32[]{:S(2)}) async-start(), calls=%async_computation.1 | async-start | bytes 2621440 | tf_op jit(solution)/shard_map/all_gather | solution.py:133
  11.6 7.1 %collective-permute-start.1 = (f32[24,128]{1,0:T(8,128)S(1)}, f32[24,128]{1,0:T(8,128)S(1)}, u32[]{:S(2)}, u32[]{:S(2)}) collective-permute-start(f32[24,128]{1,0:T(8,128)S(1)} %get-tuple-element.74), channel_id=1, source_target_pairs={{0,1},{1,0},{2,3},{3,2},{4,5},{5,4},{6,7},{7,6},{8,9},{9,8},{10,11... | collective-permute-start | bytes 36872 | tf_op jit(solution)/shard_map/ppermute | solution.py:29
  13.2 5.5 %collective-permute-start.2 = (f32[24,128]{1,0:T(8,128)S(1)}, f32[24,128]{1,0:T(8,128)S(1)}, u32[]{:S(2)}, u32[]{:S(2)}) collective-permute-start(f32[24,128]{1,0:T(8,128)S(1)} %get-tuple-element.75), channel_id=1, source_target_pairs={{0,2},{1,3},{2,0},{3,1},{4,6},{5,7},{6,4},{7,5},{8,10},{9,11},{10,... | collective-permute-start | bytes 36872 | tf_op jit(solution)/shard_map/ppermute | solution.py:29
  16.0 4.9 %collective-permute-start.3 = (f32[24,128]{1,0:T(8,128)S(1)}, f32[24,128]{1,0:T(8,128)S(1)}, u32[]{:S(2)}, u32[]{:S(2)}) collective-permute-start(f32[24,128]{1,0:T(8,128)S(1)} %get-tuple-element.76), channel_id=1, source_target_pairs={{0,3},{1,2},{2,1},{3,0},{4,7},{5,6},{6,5},{7,4},{8,11},{9,10},{10,... | collective-permute-start | bytes 36872 | tf_op jit(solution)/shard_map/ppermute | solution.py:29
  17.1 6.5 %collective-permute-start = (bf16[128,1024]{1,0:T(8,128)(2,1)S(1)}, bf16[128,1024]{1,0:T(8,128)(2,1)S(1)}, u32[]{:S(2)}, u32[]{:S(2)}) collective-permute-start(bf16[128,1024]{1,0:T(8,128)(2,1)S(1)} %get-tuple-element.18), channel_id=1, source_target_pairs={{0,4},{1,5},{2,6},{3,7},{4,0},{5,1},{6,2},{7,3},{8,12},{9,13},{10,... | collective-permute-start | bytes 786440 | tf_op jit(solution)/shard_map/ppermute | solution.py:29
  23.7 20.7 %collective-permute-start.9 = (bf16[256,1024]{1,0:T(8,128)(2,1)S(1)}, bf16[256,1024]{1,0:T(8,128)(2,1)S(1)}, u32[]{:S(2)}, u32[]{:S(2)}) collective-permute-start(bf16[256,1024]{1,0:T(8,128)(2,1)S(1)} %maximum_select_fusion), channel_id=1, source_target_pairs={{0,3},{1,2},{2,1},{3,0},{4,7},{5,6},{6,5},{7,4},{8,11},{9,10},{10,... | collective-permute-start | bytes 1572872 | tf_op jit(solution)/shard_map/ppermute | solution.py:29
  26.5 18.5 %collective-permute-start.7 = (bf16[256,1024]{1,0:T(8,128)(2,1)S(1)}, bf16[256,1024]{1,0:T(8,128)(2,1)S(1)}, u32[]{:S(2)}, u32[]{:S(2)}) collective-permute-start(bf16[256,1024]{1,0:T(8,128)(2,1)S(1)} %maximum_select_fusion), channel_id=1, source_target_pairs={{0,1},{1,0},{2,3},{3,2},{4,5},{5,4},{6,7},{7,6},{8,9},{9,8},{10,11... | collective-permute-start | bytes 1572872 | tf_op jit(solution)/shard_map/ppermute | solution.py:29
  44.4 6.5 %collective-permute-start.10 = (bf16[128,1024]{1,0:T(8,128)(2,1)S(1)}, bf16[128,1024]{1,0:T(8,128)(2,1)S(1)}, u32[]{:S(2)}, u32[]{:S(2)}) collective-permute-start(bf16[128,1024]{1,0:T(8,128)(2,1)S(1)} %get-tuple-element.38.refs_7_), channel_id=1, source_target_pairs={{0,1},{1,0},{2,3},{3,2},{4,5},{5,4},{6,7},{7,6},{8,9},{9,8},{10,11... | collective-permute-start | bytes 786440 | tf_op jit(solution)/shard_map/ppermute | solution.py:29
  45.1 7.7 %collective-permute-start.8 = (bf16[128,1024]{1,0:T(8,128)(2,1)S(1)}, bf16[128,1024]{1,0:T(8,128)(2,1)S(1)}, u32[]{:S(2)}, u32[]{:S(2)}) collective-permute-start(bf16[128,1024]{1,0:T(8,128)(2,1)S(1)} %get-tuple-element.40.refs_2_), channel_id=1, source_target_pairs={{0,3},{1,2},{2,1},{3,0},{4,7},{5,6},{6,5},{7,4},{8,11},{9,10},{10,... | collective-permute-start | bytes 786440 | tf_op jit(solution)/shard_map/ppermute | solution.py:29
  46.5 3.7 %collective-permute-start.4 = (f32[1,512]{1,0:T(1,128)S(1)}, f32[1,512]{1,0:T(1,128)S(1)}, u32[]{:S(2)}, u32[]{:S(2)}) collective-permute-start(f32[1,512]{1,0:T(1,128)S(1)} %slice.57), channel_id=1, source_target_pairs={{0,4},{1,5},{2,6},{3,7},{4,0},{5,1},{6,2},{7,3},{8,12},{9,13},{10,... | collective-permute-start | bytes 6152 | tf_op jit(solution)/shard_map/ppermute | solution.py:29
  48.3 5.2 %collective-permute-start.5 = (bf16[16,1024]{1,0:T(8,128)(2,1)S(1)}, bf16[16,1024]{1,0:T(8,128)(2,1)S(1)}, u32[]{:S(2)}, u32[]{:S(2)}) collective-permute-start(bf16[16,1024]{1,0:T(8,128)(2,1)S(1)} %fusion.42), channel_id=1, source_target_pairs={{0,20},{1,21},{2,22},{3,23},{4,16},{5,17},{6,18},{7,19},{8,28},{9,... | collective-permute-start | bytes 98312 | tf_op jit(solution)/shard_map/ppermute | solution.py:29
  48.3 5.2 %collective-permute-start.6 = (bf16[16,1024]{1,0:T(8,128)(2,1)S(1)}, bf16[16,1024]{1,0:T(8,128)(2,1)S(1)}, u32[]{:S(2)}, u32[]{:S(2)}) collective-permute-start(bf16[16,1024]{1,0:T(8,128)(2,1)S(1)} %fusion.42), channel_id=1, source_target_pairs={{0,16},{1,17},{2,18},{3,19},{4,20},{5,21},{6,22},{7,23},{8,24},{9,... | collective-permute-start | bytes 98312 | tf_op jit(solution)/shard_map/ppermute | solution.py:29
  54.1 1.3 collective-permute-start.11
  54.8 0.7 collective-permute-start.12
  56.1 3.4 %collective-permute-start.13 = (bf16[16,1024]{1,0:T(8,128)(2,1)S(1)}, bf16[16,1024]{1,0:T(8,128)(2,1)S(1)}, u32[]{:S(2)}, u32[]{:S(2)}) collective-permute-start(bf16[16,1024]{1,0:T(8,128)(2,1)S(1)} %fusion.26), channel_id=1, source_target_pairs={{0,20},{1,21},{2,22},{3,23},{4,16},{5,17},{6,18},{7,19},{8,28},{9,... | collective-permute-start | bytes 98312 | tf_op jit(solution)/shard_map/ppermute | solution.py:29
  56.1 3.5 %collective-permute-start.14 = (bf16[16,1024]{1,0:T(8,128)(2,1)S(1)}, bf16[16,1024]{1,0:T(8,128)(2,1)S(1)}, u32[]{:S(2)}, u32[]{:S(2)}) collective-permute-start(bf16[16,1024]{1,0:T(8,128)(2,1)S(1)} %fusion.26), channel_id=1, source_target_pairs={{0,16},{1,17},{2,18},{3,19},{4,20},{5,21},{6,22},{7,23},{8,24},{9,... | collective-permute-start | bytes 98312 | tf_op jit(solution)/shard_map/ppermute | solution.py:29
  60.3 1.3 collective-permute-start.15
  60.9 0.7 collective-permute-start.16
  62.3 3.5 %collective-permute-start.17 = (bf16[16,1024]{1,0:T(8,128)(2,1)S(1)}, bf16[16,1024]{1,0:T(8,128)(2,1)S(1)}, u32[]{:S(2)}, u32[]{:S(2)}) collective-permute-start(bf16[16,1024]{1,0:T(8,128)(2,1)S(1)} %fusion.28), channel_id=1, source_target_pairs={{0,20},{1,21},{2,22},{3,23},{4,16},{5,17},{6,18},{7,19},{8,28},{9,... | collective-permute-start | bytes 98312 | tf_op jit(solution)/shard_map/ppermute | solution.py:29
  62.4 3.5 %collective-permute-start.18 = (bf16[16,1024]{1,0:T(8,128)(2,1)S(1)}, bf16[16,1024]{1,0:T(8,128)(2,1)S(1)}, u32[]{:S(2)}, u32[]{:S(2)}) collective-permute-start(bf16[16,1024]{1,0:T(8,128)(2,1)S(1)} %fusion.28), channel_id=1, source_target_pairs={{0,16},{1,17},{2,18},{3,19},{4,20},{5,21},{6,22},{7,23},{8,24},{9,... | collective-permute-start | bytes 98312 | tf_op jit(solution)/shard_map/ppermute | solution.py:29
  66.5 1.3 collective-permute-start.19
  67.1 0.7 collective-permute-start.20
  68.5 3.7 %collective-permute-start.21 = (bf16[16,1024]{1,0:T(8,128)(2,1)S(1)}, bf16[16,1024]{1,0:T(8,128)(2,1)S(1)}, u32[]{:S(2)}, u32[]{:S(2)}) collective-permute-start(bf16[16,1024]{1,0:T(8,128)(2,1)S(1)} %fusion.30), channel_id=1, source_target_pairs={{0,20},{1,21},{2,22},{3,23},{4,16},{5,17},{6,18},{7,19},{8,28},{9,... | collective-permute-start | bytes 98312 | tf_op jit(solution)/shard_map/ppermute | solution.py:29
  68.6 3.6 %collective-permute-start.22 = (bf16[16,1024]{1,0:T(8,128)(2,1)S(1)}, bf16[16,1024]{1,0:T(8,128)(2,1)S(1)}, u32[]{:S(2)}, u32[]{:S(2)}) collective-permute-start(bf16[16,1024]{1,0:T(8,128)(2,1)S(1)} %fusion.30), channel_id=1, source_target_pairs={{0,16},{1,17},{2,18},{3,19},{4,20},{5,21},{6,22},{7,23},{8,24},{9,... | collective-permute-start | bytes 98312 | tf_op jit(solution)/shard_map/ppermute | solution.py:29
  72.8 1.3 collective-permute-start.23
  73.5 0.7 collective-permute-start.24
  74.8 3.7 %collective-permute-start.25 = (bf16[16,1024]{1,0:T(8,128)(2,1)S(1)}, bf16[16,1024]{1,0:T(8,128)(2,1)S(1)}, u32[]{:S(2)}, u32[]{:S(2)}) collective-permute-start(bf16[16,1024]{1,0:T(8,128)(2,1)S(1)} %fusion.32), channel_id=1, source_target_pairs={{0,20},{1,21},{2,22},{3,23},{4,16},{5,17},{6,18},{7,19},{8,28},{9,... | collective-permute-start | bytes 98312 | tf_op jit(solution)/shard_map/ppermute | solution.py:29
  75.4 3.2 %collective-permute-start.26 = (bf16[16,1024]{1,0:T(8,128)(2,1)S(1)}, bf16[16,1024]{1,0:T(8,128)(2,1)S(1)}, u32[]{:S(2)}, u32[]{:S(2)}) collective-permute-start(bf16[16,1024]{1,0:T(8,128)(2,1)S(1)} %fusion.32), channel_id=1, source_target_pairs={{0,16},{1,17},{2,18},{3,19},{4,20},{5,21},{6,22},{7,23},{8,24},{9,... | collective-permute-start | bytes 98312 | tf_op jit(solution)/shard_map/ppermute | solution.py:29
  79.2 1.3 collective-permute-start.27
  79.8 0.7 collective-permute-start.28
  88.3 3.4 %collective-permute-start.29 = (bf16[16,1024]{1,0:T(8,128)(2,1)S(1)}, bf16[16,1024]{1,0:T(8,128)(2,1)S(1)}, u32[]{:S(2)}, u32[]{:S(2)}) collective-permute-start(bf16[16,1024]{1,0:T(8,128)(2,1)S(1)} %fusion.34), channel_id=1, source_target_pairs={{0,20},{1,21},{2,22},{3,23},{4,16},{5,17},{6,18},{7,19},{8,28},{9,... | collective-permute-start | bytes 98312 | tf_op jit(solution)/shard_map/ppermute | solution.py:29
  89.0 2.6 %collective-permute-start.30 = (bf16[16,1024]{1,0:T(8,128)(2,1)S(1)}, bf16[16,1024]{1,0:T(8,128)(2,1)S(1)}, u32[]{:S(2)}, u32[]{:S(2)}) collective-permute-start(bf16[16,1024]{1,0:T(8,128)(2,1)S(1)} %fusion.34), channel_id=1, source_target_pairs={{0,16},{1,17},{2,18},{3,19},{4,20},{5,21},{6,22},{7,23},{8,24},{9,... | collective-permute-start | bytes 98312 | tf_op jit(solution)/shard_map/ppermute | solution.py:29
  92.3 1.4 collective-permute-start.31
  93.0 0.7 collective-permute-start.32
  94.3 3.3 %collective-permute-start.33 = (bf16[16,1024]{1,0:T(8,128)(2,1)S(1)}, bf16[16,1024]{1,0:T(8,128)(2,1)S(1)}, u32[]{:S(2)}, u32[]{:S(2)}) collective-permute-start(bf16[16,1024]{1,0:T(8,128)(2,1)S(1)} %fusion.36), channel_id=1, source_target_pairs={{0,20},{1,21},{2,22},{3,23},{4,16},{5,17},{6,18},{7,19},{8,28},{9,... | collective-permute-start | bytes 98312 | tf_op jit(solution)/shard_map/ppermute | solution.py:29
  95.5 2.2 %collective-permute-start.34 = (bf16[16,1024]{1,0:T(8,128)(2,1)S(1)}, bf16[16,1024]{1,0:T(8,128)(2,1)S(1)}, u32[]{:S(2)}, u32[]{:S(2)}) collective-permute-start(bf16[16,1024]{1,0:T(8,128)(2,1)S(1)} %fusion.36), channel_id=1, source_target_pairs={{0,16},{1,17},{2,18},{3,19},{4,20},{5,21},{6,22},{7,23},{8,24},{9,... | collective-permute-start | bytes 98312 | tf_op jit(solution)/shard_map/ppermute | solution.py:29
  98.3 22.5 %collective-permute-start.35 = (bf16[16,1024]{1,0:T(8,128)(2,1)S(1)}, bf16[16,1024]{1,0:T(8,128)(2,1)S(1)}, u32[]{:S(2)}, u32[]{:S(2)}) collective-permute-start(bf16[16,1024]{1,0:T(8,128)(2,1)S(1)} %fusion.37), channel_id=1, source_target_pairs={{208,236},{209,237},{210,238},{211,239},{212,232},{213,233},{214,2... | collective-permute-start | bytes 98312 | tf_op jit(solution)/shard_map/ppermute | solution.py:29
  99.6 21.3 %collective-permute-start.36 = (bf16[16,1024]{1,0:T(8,128)(2,1)S(1)}, bf16[16,1024]{1,0:T(8,128)(2,1)S(1)}, u32[]{:S(2)}, u32[]{:S(2)}) collective-permute-start(bf16[16,1024]{1,0:T(8,128)(2,1)S(1)} %fusion.37), channel_id=1, source_target_pairs={{208,224},{209,225},{210,226},{211,227},{212,228},{213,229},{214,2... | collective-permute-start | bytes 98312 | tf_op jit(solution)/shard_map/ppermute | solution.py:29
  121.6 3.7 %collective-permute-start.37 = (bf16[16,1024]{1,0:T(8,128)(2,1)S(1)}, bf16[16,1024]{1,0:T(8,128)(2,1)S(1)}, u32[]{:S(2)}, u32[]{:S(2)}) collective-permute-start(bf16[16,1024]{1,0:T(8,128)(2,1)S(1)} %fusion.38), channel_id=1, source_target_pairs={{0,20},{1,21},{2,22},{3,23},{4,16},{5,17},{6,18},{7,19},{8,28},{9,... | collective-permute-start | bytes 98312 | tf_op jit(solution)/shard_map/ppermute | solution.py:29
  121.6 3.7 %collective-permute-start.38 = (bf16[16,1024]{1,0:T(8,128)(2,1)S(1)}, bf16[16,1024]{1,0:T(8,128)(2,1)S(1)}, u32[]{:S(2)}, u32[]{:S(2)}) collective-permute-start(bf16[16,1024]{1,0:T(8,128)(2,1)S(1)} %fusion.38), channel_id=1, source_target_pairs={{0,16},{1,17},{2,18},{3,19},{4,20},{5,21},{6,22},{7,23},{8,24},{9,... | collective-permute-start | bytes 98312 | tf_op jit(solution)/shard_map/ppermute | solution.py:29
  126.0 3.9 %collective-permute-start.39 = (bf16[16,1024]{1,0:T(8,128)(2,1)S(1)}, bf16[16,1024]{1,0:T(8,128)(2,1)S(1)}, u32[]{:S(2)}, u32[]{:S(2)}) collective-permute-start(bf16[16,1024]{1,0:T(8,128)(2,1)S(1)} %fusion.40), channel_id=1, source_target_pairs={{0,4},{1,5},{2,6},{3,7},{4,0},{5,1},{6,2},{7,3},{8,12},{9,13},{10,... | collective-permute-start | bytes 98312 | tf_op jit(solution)/shard_map/ppermute | solution.py:29
  130.3 5.4 %collective-permute-start.43 = (bf16[16,1536]{1,0:T(8,128)(2,1)S(1)}, bf16[16,1536]{1,0:T(8,128)(2,1)S(1)}, u32[]{:S(2)}, u32[]{:S(2)}) collective-permute-start(bf16[16,1536]{1,0:T(8,128)(2,1)S(1)} %pad_maximum_fusion.7), channel_id=1, source_target_pairs={{0,12},{1,13},{2,14},{3,15},{4,8},{5,9},{6,10},{7,11},{8,4},{9,5},... | collective-permute-start | bytes 147464 | tf_op jit(solution)/shard_map/ppermute | solution.py:29
  135.7 3.3 %collective-permute-start.44 = (bf16[16,512]{1,0:T(8,128)(2,1)S(1)}, bf16[16,512]{1,0:T(8,128)(2,1)S(1)}, u32[]{:S(2)}, u32[]{:S(2)}) collective-permute-start(bf16[16,512]{1,0:T(8,128)(2,1)S(1)} %add_convert_fusion.29), channel_id=1, source_target_pairs={{16,0},{17,1},{18,2},{19,3},{20,4},{21,5},{22,6},{23,7},{24,8},{25... | collective-permute-start | bytes 49160 | tf_op jit(solution)/shard_map/ppermute | solution.py:29
  142.5 9.8 %copy-start = (f32[1,128,2048]{2,1,0:T(8,128)S(1)}, f32[1,128,2048]{2,1,0:T(8,128)}, u32[]{:S(2)}) copy-start(f32[1,128,2048]{2,1,0:T(8,128)} %param.8) | copy-start | bytes 3145732
  142.6 7.2 %collective-permute-start.40 = (bf16[128,512]{1,0:T(8,128)(2,1)S(1)}, bf16[128,512]{1,0:T(8,128)(2,1)S(1)}, u32[]{:S(2)}, u32[]{:S(2)}) collective-permute-start(bf16[128,512]{1,0:T(8,128)(2,1)S(1)} %get-tuple-element.35), channel_id=1, source_target_pairs={{0,1},{1,0},{2,3},{3,2},{4,5},{5,4},{6,7},{7,6},{8,9},{9,8},{10,11... | collective-permute-start | bytes 393224 | tf_op jit(solution)/shard_map/ppermute | solution.py:29
  142.7 9.6 %collective-permute-start.41 = (bf16[128,512]{1,0:T(8,128)(2,1)S(1)}, bf16[128,512]{1,0:T(8,128)(2,1)S(1)}, u32[]{:S(2)}, u32[]{:S(2)}) collective-permute-start(bf16[128,512]{1,0:T(8,128)(2,1)S(1)} %get-tuple-element.34), channel_id=1, source_target_pairs={{0,2},{1,3},{2,0},{3,1},{4,6},{5,7},{6,4},{7,5},{8,10},{9,11},{10,... | collective-permute-start | bytes 393224 | tf_op jit(solution)/shard_map/ppermute | solution.py:29
  144.9 7.3 %collective-permute-start.42 = (bf16[128,512]{1,0:T(8,128)(2,1)S(1)}, bf16[128,512]{1,0:T(8,128)(2,1)S(1)}, u32[]{:S(2)}, u32[]{:S(2)}) collective-permute-start(bf16[128,512]{1,0:T(8,128)(2,1)S(1)} %get-tuple-element.33), channel_id=1, source_target_pairs={{0,3},{1,2},{2,1},{3,0},{4,7},{5,6},{6,5},{7,4},{8,11},{9,10},{10,... | collective-permute-start | bytes 393224 | tf_op jit(solution)/shard_map/ppermute | solution.py:29
  147.4 6.6 %collective-permute-start.45 = (bf16[16,2432]{1,0:T(8,128)(2,1)S(1)}, bf16[16,2432]{1,0:T(8,128)(2,1)S(1)}, u32[]{:S(2)}, u32[]{:S(2)}) collective-permute-start(bf16[16,2432]{1,0:T(8,128)(2,1)S(1)} %get-tuple-element.44), channel_id=1, source_target_pairs={{0,1},{1,0},{2,3},{3,2},{4,5},{5,4},{6,7},{7,6},{8,9},{9,8},{10,11... | collective-permute-start | bytes 233480 | tf_op jit(solution)/shard_map/ppermute | solution.py:29
  147.5 6.5 %collective-permute-start.46 = (bf16[16,2432]{1,0:T(8,128)(2,1)S(1)}, bf16[16,2432]{1,0:T(8,128)(2,1)S(1)}, u32[]{:S(2)}, u32[]{:S(2)}) collective-permute-start(bf16[16,2432]{1,0:T(8,128)(2,1)S(1)} %get-tuple-element.45), channel_id=1, source_target_pairs={{0,2},{1,3},{2,0},{3,1},{4,6},{5,7},{6,4},{7,5},{8,10},{9,11},{10,... | collective-permute-start | bytes 233480 | tf_op jit(solution)/shard_map/ppermute | solution.py:29
  149.7 5.6 %collective-permute-start.47 = (bf16[16,2432]{1,0:T(8,128)(2,1)S(1)}, bf16[16,2432]{1,0:T(8,128)(2,1)S(1)}, u32[]{:S(2)}, u32[]{:S(2)}) collective-permute-start(bf16[16,2432]{1,0:T(8,128)(2,1)S(1)} %get-tuple-element.43), channel_id=1, source_target_pairs={{0,3},{1,2},{2,1},{3,0},{4,7},{5,6},{6,5},{7,4},{8,11},{9,10},{10,... | collective-permute-start | bytes 233480 | tf_op jit(solution)/shard_map/ppermute | solution.py:29
Sparse Core Ops, SparseCore 0:
  9.8 27.9 all-gather.8
  40.1 43.1 all-gather.4
  93.8 40.5 all-gather.6

commit v15 on v14

--- a/solution.py
+++ b/solution.py
@@ -166,12 +166,6 @@
     place = jnp.stack([x, y])
 
     coupling_in = gathered(coupling_rows, False)
-    turned = jnp.where(
-        even,
-        coupling_rows,
-        coupling_rows.reshape(rows, SIDE, SIDE, rows).transpose(0, 2, 1, 3).reshape(rows, nodes),
-    )
-    outer = gathered(jnp.concatenate([inverse_rows, turned], axis=1), True)
 
     def ordered(pieces):
         stacked = jnp.stack(pieces)
@@ -199,11 +193,18 @@
         return jnp.concatenate([part, jnp.broadcast_to(weight_row[None, :], (8, rows))], axis=0)
 
     line_values = jnp.concatenate(ordered(exchange_x(source_chunk)), axis=1)
-    keep, got, line_values = tie((keep, got, line_values), turned)
+    keep, got, line_values = tie((keep, got, line_values))
     line_weights = line_values[share : share + 1]
     two = jnp.where(
         out_place == 0, jnp.concatenate([keep, got]), jnp.concatenate([got, keep])
     )
+    coupling_late = tie(coupling_rows, two)
+    turned = jnp.where(
+        even,
+        coupling_late,
+        coupling_late.reshape(rows, SIDE, SIDE, rows).transpose(0, 2, 1, 3).reshape(rows, nodes),
+    )
+    outer = gathered(jnp.concatenate([inverse_rows, turned], axis=1), True)
     left, right = along_x(two, 1), along_x(two, 3)
     pieces = [
         two[:rows],
@@ -229,6 +230,8 @@
         jnp.concatenate([zeros, line_values[:share]], axis=1),
     )
 
+    own = tie(own, turned)
+
     message = own.astype(bf16)
     final = message
     for turn in range(1, PARTITIONS):
@@ -240,7 +243,7 @@
                 outer[:, :nodes], coupling_in, (((1,), (1,)), ((), ())), preferred_element_type=f32
             ).astype(bf16)
             inner_all = gathered(inner, False)
-            previous = tie(previous, inner)
+            own = tie(own, inner)
         product = lax.dot_general(
             previous, block, (((1,), (1,)), ((), ())), preferred_element_type=f32
         )

time: 164 us -> 162 us (0.988); the launches traced: 163 us -> 159 us
  waiting for transfers between devices: 71.1 us -> 67.6 us
  starting transfers between devices: 51.3 us -> 49.5 us
    ppermute x48, waiting for transfers between devices: 67.6 us -> 64.7 us  [permuted(): return lax.ppermute(value, AXES, pairs)]
    ppermute x48, starting transfers between devices: 51.2 us -> 49.3 us  [permuted(): return lax.ppermute(value, AXES, pairs)]
  transfers between devices with their start and end apart: 51 -> 51, of which waited for: 22 -> 20; matrix products, arithmetic and copies ran while one was open for 8% -> 11% of each run, Pallas kernels for 2% -> 2%
where the time goes in v15:
time: 162 us; the launch traced here: 159 us
  waiting for transfers between devices  67.6 us (42%)
  starting transfers between devices  49.5 us (31%)
  matrix products  17.9 us (11%)
  between operations  14.3 us (9%)
  Pallas kernels  4.48 us (3%)
  local copies, waits for them, and re-layouts  3.26 us (2%)
  other arithmetic  2.38 us (1%)
    ppermute x48, waiting for transfers between devices, permuted(): return lax.ppermute(value, AXES, pairs)  64.7 us
    ppermute x48, starting transfers between devices, permuted(): return lax.ppermute(value, AXES, pairs)  49.3 us
    dot_general x15, matrix products, shards(): lax.dot_general(previous, block, (((1,), (1,)), ((), ())), preferred_elem...  9.75 us
    pallas_call x4, Pallas kernels, kernel_call(): pl.pallas_call(body, out_shape=out_shapes, in_specs=[pl.BlockSpec(memory_...  4.48 us
    dot_general x1, matrix products, shards(): lax.dot_general(outer[:, :nodes], coupling_in, (((1,), (1,)), ((), ())),...  4.3 us
    dot_general x1, matrix products, shards(): jnp.dot(outer[:, nodes:], inner_all, preferred_element_type=f32)  3.47 us
  transfers between devices with their start and end apart: 51, of which 20 were waited for; matrix products, arithmetic and copies ran while one was open for 11% of the time, Pallas kernels for 2%

profile of v15, /device:TPU:224, one launch (start us, length us, event | category | flops | bytes accessed | tf_op | source)
XLA Modules:
  0.0 159.3 jit_solution(6834951974809877254)
XLA Ops:
  7.2 0.7 all-gather.9.cloned.1.call-update
  8.0 0.8 bitcast_multiply_fusion
  9.4 1.5 collective-permute-start.1
  10.9 2.7 %collective-permute-start.2 = (f32[24,128]{1,0:T(8,128)S(1)}, f32[24,128]{1,0:T(8,128)S(1)}, u32[]{:S(2)}, u32[]{:S(2)}) collective-permute-start(f32[24,128]{1,0:T(8,128)S(1)} %get-tuple-element.79), channel_id=1, source_target_pairs={{0,2},{1,3},{2,0},{3,1},{4,6},{5,7},{6,4},{7,5},{8,10},{9,11},{10,... | collective-permute-start | bytes 36872 | tf_op jit(solution)/shard_map/ppermute | solution.py:29
  14.2 1.0 copy-done.1
  15.8 1.7 %collective-permute-start = (bf16[128,1024]{1,0:T(8,128)(2,1)S(1)}, bf16[128,1024]{1,0:T(8,128)(2,1)S(1)}, u32[]{:S(2)}, u32[]{:S(2)}) collective-permute-start(bf16[128,1024]{1,0:T(8,128)(2,1)S(1)} %get-tuple-element.20), channel_id=1, source_target_pairs={{0,4},{1,5},{2,6},{3,7},{4,0},{5,1},{6,2},{7,3},{8,12},{9,13},{10,... | collective-permute-start | bytes 786440 | tf_op jit(solution)/shard_map/ppermute | solution.py:29
  17.5 1.0 collective-permute-done.3
  18.6 3.7 %collective-permute-done = bf16[128,1024]{1,0:T(8,128)(2,1)S(1)} collective-permute-done((bf16[128,1024]{1,0:T(8,128)(2,1)S(1)}, bf16[128,1024]{1,0:T(8,128)(2,1)S(1)}, u32[]{:S(2)}, u32[]{:S(2)}) %collective-permute-start) | collective-permute-done | bytes 262176 | tf_op jit(solution)/shard_map/ppermute | solution.py:29
  23.9 1.1 pad_maximum_fusion
  25.0 2.9 %collective-permute-start.9 = (bf16[256,1024]{1,0:T(8,128)(2,1)S(1)}, bf16[256,1024]{1,0:T(8,128)(2,1)S(1)}, u32[]{:S(2)}, u32[]{:S(2)}) collective-permute-start(bf16[256,1024]{1,0:T(8,128)(2,1)S(1)} %maximum_select_fusion), channel_id=1, source_target_pairs={{0,3},{1,2},{2,1},{3,0},{4,7},{5,6},{6,5},{7,4},{8,11},{9,10},{10,... | collective-permute-start | bytes 1572872 | tf_op jit(solution)/shard_map/ppermute | solution.py:29
  27.9 17.9 %collective-permute-done.9 = bf16[256,1024]{1,0:T(8,128)(2,1)S(1)} collective-permute-done((bf16[256,1024]{1,0:T(8,128)(2,1)S(1)}, bf16[256,1024]{1,0:T(8,128)(2,1)S(1)}, u32[]{:S(2)}, u32[]{:S(2)}) %collective-permute-start.9) | collective-permute-done | bytes 524320 | tf_op jit(solution)/shard_map/ppermute | solution.py:29
  46.2 1.7 %collective-permute-start.8 = (bf16[128,1024]{1,0:T(8,128)(2,1)S(1)}, bf16[128,1024]{1,0:T(8,128)(2,1)S(1)}, u32[]{:S(2)}, u32[]{:S(2)}) collective-permute-start(bf16[128,1024]{1,0:T(8,128)(2,1)S(1)} %get-tuple-element.44.refs_2_), channel_id=1, source_target_pairs={{0,3},{1,2},{2,1},{3,0},{4,7},{5,6},{6,5},{7,4},{8,11},{9,10},{10,... | collective-permute-start | bytes 786440 | tf_op jit(solution)/shard_map/ppermute | solution.py:29
  48.0 1.1 collective-permute-start.4
  49.2 1.1 collective-permute-start.6
  50.3 1.3 collective-permute-done.4
  51.7 0.7 collective-permute-done.10.refs_5_
  52.4 1.5 collective-permute-done.8.refs_4_
  53.9 0.7 shard_map.86
  55.2 0.7 collective-permute-start.11
  55.9 0.7 collective-permute-start.12
  57.2 0.9 collective-permute-start.14
  58.2 2.4 %collective-permute-done.13 = bf16[16,1024]{1,0:T(8,128)(2,1)S(1)} collective-permute-done((bf16[16,1024]{1,0:T(8,128)(2,1)S(1)}, bf16[16,1024]{1,0:T(8,128)(2,1)S(1)}, u32[]{:S(2)}, u32[]{:S(2)}) %collective-permute-start.13) | collective-permute-done | bytes 32800 | tf_op jit(solution)/shard_map/ppermute | solution.py:29
  61.3 0.7 collective-permute-start.15
  61.9 0.7 collective-permute-start.16
  64.3 2.6 %collective-permute-done.17 = bf16[16,1024]{1,0:T(8,128)(2,1)S(1)} collective-permute-done((bf16[16,1024]{1,0:T(8,128)(2,1)S(1)}, bf16[16,1024]{1,0:T(8,128)(2,1)S(1)}, u32[]{:S(2)}, u32[]{:S(2)}) %collective-permute-start.17) | collective-permute-done | bytes 32800 | tf_op jit(solution)/shard_map/ppermute | solution.py:29
  67.5 0.7 collective-permute-start.19
  68.2 0.7 collective-permute-start.20
  69.5 1.2 collective-permute-start.21
  71.0 2.5 %collective-permute-done.21 = bf16[16,1024]{1,0:T(8,128)(2,1)S(1)} collective-permute-done((bf16[16,1024]{1,0:T(8,128)(2,1)S(1)}, bf16[16,1024]{1,0:T(8,128)(2,1)S(1)}, u32[]{:S(2)}, u32[]{:S(2)}) %collective-permute-start.21) | collective-permute-done | bytes 32800 | tf_op jit(solution)/shard_map/ppermute | solution.py:29
  74.1 0.7 collective-permute-start.23
  74.8 0.7 collective-permute-start.24
  76.1 1.5 collective-permute-start.25
  77.6 2.2 %collective-permute-done.25 = bf16[16,1024]{1,0:T(8,128)(2,1)S(1)} collective-permute-done((bf16[16,1024]{1,0:T(8,128)(2,1)S(1)}, bf16[16,1024]{1,0:T(8,128)(2,1)S(1)}, u32[]{:S(2)}, u32[]{:S(2)}) %collective-permute-start.25) | collective-permute-done | bytes 32800 | tf_op jit(solution)/shard_map/ppermute | solution.py:29
  80.5 0.7 collective-permute-start.27
  81.2 0.7 collective-permute-start.28
  81.9 2.1 %all-gather.5.cloned.1.call-done = bf16[512,4096]{1,0:T(8,128)(2,1)} async-done(((bf16[128,4096]{1,0:T(8,128)(2,1)}), bf16[512,4096]{1,0:T(8,128)(2,1)}) %all-gather.5.cloned.1.call-update) | async-done | bytes 4194320 | tf_op jit(solution)/shard_map/all_gather | solution.py:133
  84.0 4.3 %fusion.7 = bf16[512,512]{1,0:T(8,128)(2,1)} fusion(bf16[512,2048]{1,0:T(8,128)(2,1)} %bitcast.70, bf16[512,4096]{1,0:T(8,128)(2,1)} %all-gather.5.cloned.1.call-done), kind=kOutput, calls=%fused_computation.5 | convolution fusion | flops 1074003968 | bytes 4718592 | tf_op jit(solution)/shard_map/dot_general | solution.py:242
  88.9 0.7 collective-permute-start.29
  89.7 0.9 collective-permute-start.30
  90.6 1.7 %collective-permute-done.29 = bf16[16,1024]{1,0:T(8,128)(2,1)S(1)} collective-permute-done((bf16[16,1024]{1,0:T(8,128)(2,1)S(1)}, bf16[16,1024]{1,0:T(8,128)(2,1)S(1)}, u32[]{:S(2)}, u32[]{:S(2)}) %collective-permute-start.29) | collective-permute-done | bytes 32800 | tf_op jit(solution)/shard_map/ppermute | solution.py:29
  93.0 0.7 collective-permute-start.31
  93.6 0.7 collective-permute-start.32
  95.0 1.1 collective-permute-start.33
  96.7 1.6 %collective-permute-done.33 = bf16[16,1024]{1,0:T(8,128)(2,1)S(1)} collective-permute-done((bf16[16,1024]{1,0:T(8,128)(2,1)S(1)}, bf16[16,1024]{1,0:T(8,128)(2,1)S(1)}, u32[]{:S(2)}, u32[]{:S(2)}) %collective-permute-start.33) | collective-permute-done | bytes 32800 | tf_op jit(solution)/shard_map/ppermute | solution.py:29
  99.0 1.3 collective-permute-start.35
  100.3 1.3 collective-permute-start.36
  101.6 14.8 %collective-permute-done.35 = bf16[16,1024]{1,0:T(8,128)(2,1)S(1)} collective-permute-done((bf16[16,1024]{1,0:T(8,128)(2,1)S(1)}, bf16[16,1024]{1,0:T(8,128)(2,1)S(1)}, u32[]{:S(2)}, u32[]{:S(2)}) %collective-permute-start.35) | collective-permute-done | bytes 32800 | tf_op jit(solution)/shard_map/ppermute | solution.py:29
  117.1 2.1 %collective-permute-start.38 = (bf16[16,1024]{1,0:T(8,128)(2,1)S(1)}, bf16[16,1024]{1,0:T(8,128)(2,1)S(1)}, u32[]{:S(2)}, u32[]{:S(2)}) collective-permute-start(bf16[16,1024]{1,0:T(8,128)(2,1)S(1)} %fusion.38), channel_id=1, source_target_pairs={{0,16},{1,17},{2,18},{3,19},{4,20},{5,21},{6,22},{7,23},{8,24},{9,... | collective-permute-start | bytes 98312 | tf_op jit(solution)/shard_map/ppermute | solution.py:29
  119.1 1.3 collective-permute-done.37
  120.4 0.7 fusion.40
  121.1 2.2 %collective-permute-start.39 = (bf16[16,1024]{1,0:T(8,128)(2,1)S(1)}, bf16[16,1024]{1,0:T(8,128)(2,1)S(1)}, u32[]{:S(2)}, u32[]{:S(2)}) collective-permute-start(bf16[16,1024]{1,0:T(8,128)(2,1)S(1)} %fusion.40), channel_id=1, source_target_pairs={{0,4},{1,5},{2,6},{3,7},{4,0},{5,1},{6,2},{7,3},{8,12},{9,13},{10,... | collective-permute-start | bytes 98312 | tf_op jit(solution)/shard_map/ppermute | solution.py:29
  123.3 2.2 %collective-permute-done.39 = bf16[16,1024]{1,0:T(8,128)(2,1)S(1)} collective-permute-done((bf16[16,1024]{1,0:T(8,128)(2,1)S(1)}, bf16[16,1024]{1,0:T(8,128)(2,1)S(1)}, u32[]{:S(2)}, u32[]{:S(2)}) %collective-permute-start.39) | collective-permute-done | bytes 32800 | tf_op jit(solution)/shard_map/ppermute | solution.py:29
  126.0 1.4 collective-permute-start.43
  127.4 4.2 %collective-permute-done.43 = bf16[16,1536]{1,0:T(8,128)(2,1)S(1)} collective-permute-done((bf16[16,1536]{1,0:T(8,128)(2,1)S(1)}, bf16[16,1536]{1,0:T(8,128)(2,1)S(1)}, u32[]{:S(2)}, u32[]{:S(2)}) %collective-permute-start.43) | collective-permute-done | bytes 49184 | tf_op jit(solution)/shard_map/ppermute | solution.py:29
  131.7 1.9 %collective-permute-start.44 = (bf16[16,512]{1,0:T(8,128)(2,1)S(1)}, bf16[16,512]{1,0:T(8,128)(2,1)S(1)}, u32[]{:S(2)}, u32[]{:S(2)}) collective-permute-start(bf16[16,512]{1,0:T(8,128)(2,1)S(1)} %add_convert_fusion.30), channel_id=1, source_target_pairs={{16,0},{17,1},{18,2},{19,3},{20,4},{21,5},{22,6},{23,7},{24,8},{25... | collective-permute-start | bytes 49160 | tf_op jit(solution)/shard_map/ppermute | solution.py:29
  133.7 1.4 collective-permute-done.44
  135.0 3.5 %fusion.4 = bf16[512,512]{1,0:T(8,128)(2,1)S(1)} fusion(bf16[2048,512]{1,0:T(8,128)(2,1)} %all-gather.7.cloned.1.call-done, bf16[512,4096]{1,0:T(8,128)(2,1)} %all-gather.5.cloned.1.call-done), kind=kOutput, calls=%fused_computation.4 | convolution fusion | flops 1074003968 | bytes 4718592 | tf_op jit(solution)/shard_map/dot_general | solution.py:285
  138.7 2.2 %collective-permute-start.41 = (bf16[128,512]{1,0:T(8,128)(2,1)S(1)}, bf16[128,512]{1,0:T(8,128)(2,1)S(1)}, u32[]{:S(2)}, u32[]{:S(2)}) collective-permute-start(bf16[128,512]{1,0:T(8,128)(2,1)S(1)} %get-tuple-element.38), channel_id=1, source_target_pairs={{0,2},{1,3},{2,0},{3,1},{4,6},{5,7},{6,4},{7,5},{8,10},{9,11},{10,... | collective-permute-start | bytes 393224 | tf_op jit(solution)/shard_map/ppermute | solution.py:29
  140.9 2.5 %collective-permute-start.42 = (bf16[128,512]{1,0:T(8,128)(2,1)S(1)}, bf16[128,512]{1,0:T(8,128)(2,1)S(1)}, u32[]{:S(2)}, u32[]{:S(2)}) collective-permute-start(bf16[128,512]{1,0:T(8,128)(2,1)S(1)} %get-tuple-element.37), channel_id=1, source_target_pairs={{0,3},{1,2},{2,1},{3,0},{4,7},{5,6},{6,5},{7,4},{8,11},{9,10},{10,... | collective-permute-start | bytes 393224 | tf_op jit(solution)/shard_map/ppermute | solution.py:29
  143.5 2.2 %collective-permute-start.46 = (bf16[16,2432]{1,0:T(8,128)(2,1)S(1)}, bf16[16,2432]{1,0:T(8,128)(2,1)S(1)}, u32[]{:S(2)}, u32[]{:S(2)}) collective-permute-start(bf16[16,2432]{1,0:T(8,128)(2,1)S(1)} %get-tuple-element.49), channel_id=1, source_target_pairs={{0,2},{1,3},{2,0},{3,1},{4,6},{5,7},{6,4},{7,5},{8,10},{9,11},{10,... | collective-permute-start | bytes 233480 | tf_op jit(solution)/shard_map/ppermute | solution.py:29
  145.7 2.5 %collective-permute-start.47 = (bf16[16,2432]{1,0:T(8,128)(2,1)S(1)}, bf16[16,2432]{1,0:T(8,128)(2,1)S(1)}, u32[]{:S(2)}, u32[]{:S(2)}) collective-permute-start(bf16[16,2432]{1,0:T(8,128)(2,1)S(1)} %get-tuple-element.47), channel_id=1, source_target_pairs={{0,3},{1,2},{2,1},{3,0},{4,7},{5,6},{6,5},{7,4},{8,11},{9,10},{10,... | collective-permute-start | bytes 233480 | tf_op jit(solution)/shard_map/ppermute | solution.py:29
  148.3 1.8 %shard_map.87 = (f32[128,2048]{1,0:T(8,128)}, bf16[128,2048]{1,0:T(8,128)(2,1)S(1)}) custom-call(s32[3]{0:T(128)S(1)} %pad_add_fusion.place, f32[128,2048]{1,0:T(8,128)S(1)} %bitcast.57, bf16[128,512]{1,0:T(8,128)(2,1)S(1)} %get-tuple-element.40.refs_1_, bf16[128,512]{1,0:T(8,128)(2,1)S(1)} %collective-permute-done.40.refs_2_, ...), custom_call_target="tpu_custom_call" | custom-call | bytes 3145728 | tf_op jit(solution)/shard_map/pallas_call | solution.py:58
  150.1 1.3 collective-permute-done.47.refs_3_
  151.3 1.5 shard_map.88
  (110 shorter events, 16.1 us)
Async XLA Ops:
  7.2 15.3 %copy-start.3 = (bf16[1,128,2048]{2,1,0:T(8,128)(2,1)S(1)}, bf16[1,128,2048]{2,1,0:T(8,128)(2,1)}, u32[]{:S(2)}) copy-start(bf16[1,128,2048]{2,1,0:T(8,128)(2,1)} %param.7) | copy-start | bytes 1572868
  7.2 74.7 %all-gather.9.cloned.1.call-start = ((), (), s32[]{:S(2)}) async-start(), calls=%async_computation.2 | async-start | bytes 2621440 | tf_op jit(solution)/shard_map/all_gather | solution.py:133
  7.9 76.1 %all-gather.5.cloned.1.call-start = ((), (), s32[]{:S(2)}) async-start(), calls=%async_computation | async-start | bytes 5242880 | tf_op jit(solution)/shard_map/all_gather | solution.py:133
  9.4 8.1 %collective-permute-start.1 = (f32[24,128]{1,0:T(8,128)S(1)}, f32[24,128]{1,0:T(8,128)S(1)}, u32[]{:S(2)}, u32[]{:S(2)}) collective-permute-start(f32[24,128]{1,0:T(8,128)S(1)} %get-tuple-element.78), channel_id=1, source_target_pairs={{0,1},{1,0},{2,3},{3,2},{4,5},{5,4},{6,7},{7,6},{8,9},{9,8},{10,11... | collective-permute-start | bytes 36872 | tf_op jit(solution)/shard_map/ppermute | solution.py:29
  10.9 6.6 %collective-permute-start.2 = (f32[24,128]{1,0:T(8,128)S(1)}, f32[24,128]{1,0:T(8,128)S(1)}, u32[]{:S(2)}, u32[]{:S(2)}) collective-permute-start(f32[24,128]{1,0:T(8,128)S(1)} %get-tuple-element.79), channel_id=1, source_target_pairs={{0,2},{1,3},{2,0},{3,1},{4,6},{5,7},{6,4},{7,5},{8,10},{9,11},{10,... | collective-permute-start | bytes 36872 | tf_op jit(solution)/shard_map/ppermute | solution.py:29
  13.6 4.9 %collective-permute-start.3 = (f32[24,128]{1,0:T(8,128)S(1)}, f32[24,128]{1,0:T(8,128)S(1)}, u32[]{:S(2)}, u32[]{:S(2)}) collective-permute-start(f32[24,128]{1,0:T(8,128)S(1)} %get-tuple-element.80), channel_id=1, source_target_pairs={{0,3},{1,2},{2,1},{3,0},{4,7},{5,6},{6,5},{7,4},{8,11},{9,10},{10,... | collective-permute-start | bytes 36872 | tf_op jit(solution)/shard_map/ppermute | solution.py:29
  14.2 1.0 copy-start.1
  15.8 6.5 %collective-permute-start = (bf16[128,1024]{1,0:T(8,128)(2,1)S(1)}, bf16[128,1024]{1,0:T(8,128)(2,1)S(1)}, u32[]{:S(2)}, u32[]{:S(2)}) collective-permute-start(bf16[128,1024]{1,0:T(8,128)(2,1)S(1)} %get-tuple-element.20), channel_id=1, source_target_pairs={{0,4},{1,5},{2,6},{3,7},{4,0},{5,1},{6,2},{7,3},{8,12},{9,13},{10,... | collective-permute-start | bytes 786440 | tf_op jit(solution)/shard_map/ppermute | solution.py:29
  22.8 1.0 copy-start.4
  24.9 110.1 %all-gather.7.cloned.1.call-start = ((), (), s32[]{:S(2)}) async-start(), calls=%async_computation.1 | async-start | bytes 2621440 | tf_op jit(solution)/shard_map/all_gather | solution.py:133
  25.0 20.8 %collective-permute-start.9 = (bf16[256,1024]{1,0:T(8,128)(2,1)S(1)}, bf16[256,1024]{1,0:T(8,128)(2,1)S(1)}, u32[]{:S(2)}, u32[]{:S(2)}) collective-permute-start(bf16[256,1024]{1,0:T(8,128)(2,1)S(1)} %maximum_select_fusion), channel_id=1, source_target_pairs={{0,3},{1,2},{2,1},{3,0},{4,7},{5,6},{6,5},{7,4},{8,11},{9,10},{10,... | collective-permute-start | bytes 1572872 | tf_op jit(solution)/shard_map/ppermute | solution.py:29
  27.8 18.3 %collective-permute-start.7 = (bf16[256,1024]{1,0:T(8,128)(2,1)S(1)}, bf16[256,1024]{1,0:T(8,128)(2,1)S(1)}, u32[]{:S(2)}, u32[]{:S(2)}) collective-permute-start(bf16[256,1024]{1,0:T(8,128)(2,1)S(1)} %maximum_select_fusion), channel_id=1, source_target_pairs={{0,1},{1,0},{2,3},{3,2},{4,5},{5,4},{6,7},{7,6},{8,9},{9,8},{10,11... | collective-permute-start | bytes 1572872 | tf_op jit(solution)/shard_map/ppermute | solution.py:29
  45.8 6.6 %collective-permute-start.10 = (bf16[128,1024]{1,0:T(8,128)(2,1)S(1)}, bf16[128,1024]{1,0:T(8,128)(2,1)S(1)}, u32[]{:S(2)}, u32[]{:S(2)}) collective-permute-start(bf16[128,1024]{1,0:T(8,128)(2,1)S(1)} %get-tuple-element.42.refs_7_), channel_id=1, source_target_pairs={{0,1},{1,0},{2,3},{3,2},{4,5},{5,4},{6,7},{7,6},{8,9},{9,8},{10,11... | collective-permute-start | bytes 786440 | tf_op jit(solution)/shard_map/ppermute | solution.py:29
  46.2 7.7 %collective-permute-start.8 = (bf16[128,1024]{1,0:T(8,128)(2,1)S(1)}, bf16[128,1024]{1,0:T(8,128)(2,1)S(1)}, u32[]{:S(2)}, u32[]{:S(2)}) collective-permute-start(bf16[128,1024]{1,0:T(8,128)(2,1)S(1)} %get-tuple-element.44.refs_2_), channel_id=1, source_target_pairs={{0,3},{1,2},{2,1},{3,0},{4,7},{5,6},{6,5},{7,4},{8,11},{9,10},{10,... | collective-permute-start | bytes 786440 | tf_op jit(solution)/shard_map/ppermute | solution.py:29
  48.0 3.7 %collective-permute-start.4 = (f32[1,512]{1,0:T(1,128)S(1)}, f32[1,512]{1,0:T(1,128)S(1)}, u32[]{:S(2)}, u32[]{:S(2)}) collective-permute-start(f32[1,512]{1,0:T(1,128)S(1)} %slice.57), channel_id=1, source_target_pairs={{0,4},{1,5},{2,6},{3,7},{4,0},{5,1},{6,2},{7,3},{8,12},{9,13},{10,... | collective-permute-start | bytes 6152 | tf_op jit(solution)/shard_map/ppermute | solution.py:29
  49.1 5.4 %collective-permute-start.5 = (bf16[16,1024]{1,0:T(8,128)(2,1)S(1)}, bf16[16,1024]{1,0:T(8,128)(2,1)S(1)}, u32[]{:S(2)}, u32[]{:S(2)}) collective-permute-start(bf16[16,1024]{1,0:T(8,128)(2,1)S(1)} %convert_element_type.216), channel_id=1, source_target_pairs={{0,20},{1,21},{2,22},{3,23},{4,16},{5,17},{6,18},{7,19},{8,28},{9,... | collective-permute-start | bytes 98312 | tf_op jit(solution)/shard_map/ppermute | solution.py:29
  49.2 5.3 %collective-permute-start.6 = (bf16[16,1024]{1,0:T(8,128)(2,1)S(1)}, bf16[16,1024]{1,0:T(8,128)(2,1)S(1)}, u32[]{:S(2)}, u32[]{:S(2)}) collective-permute-start(bf16[16,1024]{1,0:T(8,128)(2,1)S(1)} %convert_element_type.216), channel_id=1, source_target_pairs={{0,16},{1,17},{2,18},{3,19},{4,20},{5,21},{6,22},{7,23},{8,24},{9,... | collective-permute-start | bytes 98312 | tf_op jit(solution)/shard_map/ppermute | solution.py:29
  55.2 1.3 collective-permute-start.11
  55.9 0.7 collective-permute-start.12
  57.2 3.4 %collective-permute-start.13 = (bf16[16,1024]{1,0:T(8,128)(2,1)S(1)}, bf16[16,1024]{1,0:T(8,128)(2,1)S(1)}, u32[]{:S(2)}, u32[]{:S(2)}) collective-permute-start(bf16[16,1024]{1,0:T(8,128)(2,1)S(1)} %fusion.26), channel_id=1, source_target_pairs={{0,20},{1,21},{2,22},{3,23},{4,16},{5,17},{6,18},{7,19},{8,28},{9,... | collective-permute-start | bytes 98312 | tf_op jit(solution)/shard_map/ppermute | solution.py:29
  57.2 3.4 %collective-permute-start.14 = (bf16[16,1024]{1,0:T(8,128)(2,1)S(1)}, bf16[16,1024]{1,0:T(8,128)(2,1)S(1)}, u32[]{:S(2)}, u32[]{:S(2)}) collective-permute-start(bf16[16,1024]{1,0:T(8,128)(2,1)S(1)} %fusion.26), channel_id=1, source_target_pairs={{0,16},{1,17},{2,18},{3,19},{4,20},{5,21},{6,22},{7,23},{8,24},{9,... | collective-permute-start | bytes 98312 | tf_op jit(solution)/shard_map/ppermute | solution.py:29
  61.3 1.3 collective-permute-start.15
  61.9 0.7 collective-permute-start.16
  63.3 3.6 %collective-permute-start.17 = (bf16[16,1024]{1,0:T(8,128)(2,1)S(1)}, bf16[16,1024]{1,0:T(8,128)(2,1)S(1)}, u32[]{:S(2)}, u32[]{:S(2)}) collective-permute-start(bf16[16,1024]{1,0:T(8,128)(2,1)S(1)} %fusion.28), channel_id=1, source_target_pairs={{0,20},{1,21},{2,22},{3,23},{4,16},{5,17},{6,18},{7,19},{8,28},{9,... | collective-permute-start | bytes 98312 | tf_op jit(solution)/shard_map/ppermute | solution.py:29
  63.7 3.2 %collective-permute-start.18 = (bf16[16,1024]{1,0:T(8,128)(2,1)S(1)}, bf16[16,1024]{1,0:T(8,128)(2,1)S(1)}, u32[]{:S(2)}, u32[]{:S(2)}) collective-permute-start(bf16[16,1024]{1,0:T(8,128)(2,1)S(1)} %fusion.28), channel_id=1, source_target_pairs={{0,16},{1,17},{2,18},{3,19},{4,20},{5,21},{6,22},{7,23},{8,24},{9,... | collective-permute-start | bytes 98312 | tf_op jit(solution)/shard_map/ppermute | solution.py:29
  67.5 1.3 collective-permute-start.19
  68.2 0.7 collective-permute-start.20
  69.5 3.9 %collective-permute-start.21 = (bf16[16,1024]{1,0:T(8,128)(2,1)S(1)}, bf16[16,1024]{1,0:T(8,128)(2,1)S(1)}, u32[]{:S(2)}, u32[]{:S(2)}) collective-permute-start(bf16[16,1024]{1,0:T(8,128)(2,1)S(1)} %fusion.30), channel_id=1, source_target_pairs={{0,20},{1,21},{2,22},{3,23},{4,16},{5,17},{6,18},{7,19},{8,28},{9,... | collective-permute-start | bytes 98312 | tf_op jit(solution)/shard_map/ppermute | solution.py:29
  70.7 2.7 %collective-permute-start.22 = (bf16[16,1024]{1,0:T(8,128)(2,1)S(1)}, bf16[16,1024]{1,0:T(8,128)(2,1)S(1)}, u32[]{:S(2)}, u32[]{:S(2)}) collective-permute-start(bf16[16,1024]{1,0:T(8,128)(2,1)S(1)} %fusion.30), channel_id=1, source_target_pairs={{0,16},{1,17},{2,18},{3,19},{4,20},{5,21},{6,22},{7,23},{8,24},{9,... | collective-permute-start | bytes 98312 | tf_op jit(solution)/shard_map/ppermute | solution.py:29
  74.1 1.3 collective-permute-start.23
  74.8 0.7 collective-permute-start.24
  76.1 3.7 %collective-permute-start.25 = (bf16[16,1024]{1,0:T(8,128)(2,1)S(1)}, bf16[16,1024]{1,0:T(8,128)(2,1)S(1)}, u32[]{:S(2)}, u32[]{:S(2)}) collective-permute-start(bf16[16,1024]{1,0:T(8,128)(2,1)S(1)} %fusion.32), channel_id=1, source_target_pairs={{0,20},{1,21},{2,22},{3,23},{4,16},{5,17},{6,18},{7,19},{8,28},{9,... | collective-permute-start | bytes 98312 | tf_op jit(solution)/shard_map/ppermute | solution.py:29
  77.6 2.3 %collective-permute-start.26 = (bf16[16,1024]{1,0:T(8,128)(2,1)S(1)}, bf16[16,1024]{1,0:T(8,128)(2,1)S(1)}, u32[]{:S(2)}, u32[]{:S(2)}) collective-permute-start(bf16[16,1024]{1,0:T(8,128)(2,1)S(1)} %fusion.32), channel_id=1, source_target_pairs={{0,16},{1,17},{2,18},{3,19},{4,20},{5,21},{6,22},{7,23},{8,24},{9,... | collective-permute-start | bytes 98312 | tf_op jit(solution)/shard_map/ppermute | solution.py:29
  80.5 7.8 %collective-permute-start.27 = (bf16[16,1024]{1,0:T(8,128)(2,1)S(1)}, bf16[16,1024]{1,0:T(8,128)(2,1)S(1)}, u32[]{:S(2)}, u32[]{:S(2)}) collective-permute-start(bf16[16,1024]{1,0:T(8,128)(2,1)S(1)} %fusion.33), channel_id=1, source_target_pairs={{144,172},{145,173},{146,174},{147,175},{148,168},{149,169},{150,1... | collective-permute-start | bytes 98312 | tf_op jit(solution)/shard_map/ppermute | solution.py:29
  81.2 7.1 %collective-permute-start.28 = (bf16[16,1024]{1,0:T(8,128)(2,1)S(1)}, bf16[16,1024]{1,0:T(8,128)(2,1)S(1)}, u32[]{:S(2)}, u32[]{:S(2)}) collective-permute-start(bf16[16,1024]{1,0:T(8,128)(2,1)S(1)} %fusion.33), channel_id=1, source_target_pairs={{144,160},{145,161},{146,162},{147,163},{148,164},{149,165},{150,1... | collective-permute-start | bytes 98312 | tf_op jit(solution)/shard_map/ppermute | solution.py:29
  88.9 3.4 %collective-permute-start.29 = (bf16[16,1024]{1,0:T(8,128)(2,1)S(1)}, bf16[16,1024]{1,0:T(8,128)(2,1)S(1)}, u32[]{:S(2)}, u32[]{:S(2)}) collective-permute-start(bf16[16,1024]{1,0:T(8,128)(2,1)S(1)} %fusion.34), channel_id=1, source_target_pairs={{0,20},{1,21},{2,22},{3,23},{4,16},{5,17},{6,18},{7,19},{8,28},{9,... | collective-permute-start | bytes 98312 | tf_op jit(solution)/shard_map/ppermute | solution.py:29
  89.7 2.6 %collective-permute-start.30 = (bf16[16,1024]{1,0:T(8,128)(2,1)S(1)}, bf16[16,1024]{1,0:T(8,128)(2,1)S(1)}, u32[]{:S(2)}, u32[]{:S(2)}) collective-permute-start(bf16[16,1024]{1,0:T(8,128)(2,1)S(1)} %fusion.34), channel_id=1, source_target_pairs={{0,16},{1,17},{2,18},{3,19},{4,20},{5,21},{6,22},{7,23},{8,24},{9,... | collective-permute-start | bytes 98312 | tf_op jit(solution)/shard_map/ppermute | solution.py:29
  93.0 1.4 collective-permute-start.31
  93.6 0.7 collective-permute-start.32
  95.0 3.3 %collective-permute-start.33 = (bf16[16,1024]{1,0:T(8,128)(2,1)S(1)}, bf16[16,1024]{1,0:T(8,128)(2,1)S(1)}, u32[]{:S(2)}, u32[]{:S(2)}) collective-permute-start(bf16[16,1024]{1,0:T(8,128)(2,1)S(1)} %fusion.36), channel_id=1, source_target_pairs={{0,20},{1,21},{2,22},{3,23},{4,16},{5,17},{6,18},{7,19},{8,28},{9,... | collective-permute-start | bytes 98312 | tf_op jit(solution)/shard_map/ppermute | solution.py:29
  96.1 2.2 %collective-permute-start.34 = (bf16[16,1024]{1,0:T(8,128)(2,1)S(1)}, bf16[16,1024]{1,0:T(8,128)(2,1)S(1)}, u32[]{:S(2)}, u32[]{:S(2)}) collective-permute-start(bf16[16,1024]{1,0:T(8,128)(2,1)S(1)} %fusion.36), channel_id=1, source_target_pairs={{0,16},{1,17},{2,18},{3,19},{4,20},{5,21},{6,22},{7,23},{8,24},{9,... | collective-permute-start | bytes 98312 | tf_op jit(solution)/shard_map/ppermute | solution.py:29
  99.0 17.4 %collective-permute-start.35 = (bf16[16,1024]{1,0:T(8,128)(2,1)S(1)}, bf16[16,1024]{1,0:T(8,128)(2,1)S(1)}, u32[]{:S(2)}, u32[]{:S(2)}) collective-permute-start(bf16[16,1024]{1,0:T(8,128)(2,1)S(1)} %fusion.37), channel_id=1, source_target_pairs={{208,236},{209,237},{210,238},{211,239},{212,232},{213,233},{214,2... | collective-permute-start | bytes 98312 | tf_op jit(solution)/shard_map/ppermute | solution.py:29
  100.3 16.1 %collective-permute-start.36 = (bf16[16,1024]{1,0:T(8,128)(2,1)S(1)}, bf16[16,1024]{1,0:T(8,128)(2,1)S(1)}, u32[]{:S(2)}, u32[]{:S(2)}) collective-permute-start(bf16[16,1024]{1,0:T(8,128)(2,1)S(1)} %fusion.37), channel_id=1, source_target_pairs={{208,224},{209,225},{210,226},{211,227},{212,228},{213,229},{214,2... | collective-permute-start | bytes 98312 | tf_op jit(solution)/shard_map/ppermute | solution.py:29
  117.1 3.3 %collective-permute-start.37 = (bf16[16,1024]{1,0:T(8,128)(2,1)S(1)}, bf16[16,1024]{1,0:T(8,128)(2,1)S(1)}, u32[]{:S(2)}, u32[]{:S(2)}) collective-permute-start(bf16[16,1024]{1,0:T(8,128)(2,1)S(1)} %fusion.38), channel_id=1, source_target_pairs={{0,20},{1,21},{2,22},{3,23},{4,16},{5,17},{6,18},{7,19},{8,28},{9,... | collective-permute-start | bytes 98312 | tf_op jit(solution)/shard_map/ppermute | solution.py:29
  117.1 3.3 %collective-permute-start.38 = (bf16[16,1024]{1,0:T(8,128)(2,1)S(1)}, bf16[16,1024]{1,0:T(8,128)(2,1)S(1)}, u32[]{:S(2)}, u32[]{:S(2)}) collective-permute-start(bf16[16,1024]{1,0:T(8,128)(2,1)S(1)} %fusion.38), channel_id=1, source_target_pairs={{0,16},{1,17},{2,18},{3,19},{4,20},{5,21},{6,22},{7,23},{8,24},{9,... | collective-permute-start | bytes 98312 | tf_op jit(solution)/shard_map/ppermute | solution.py:29
  121.1 4.5 %collective-permute-start.39 = (bf16[16,1024]{1,0:T(8,128)(2,1)S(1)}, bf16[16,1024]{1,0:T(8,128)(2,1)S(1)}, u32[]{:S(2)}, u32[]{:S(2)}) collective-permute-start(bf16[16,1024]{1,0:T(8,128)(2,1)S(1)} %fusion.40), channel_id=1, source_target_pairs={{0,4},{1,5},{2,6},{3,7},{4,0},{5,1},{6,2},{7,3},{8,12},{9,13},{10,... | collective-permute-start | bytes 98312 | tf_op jit(solution)/shard_map/ppermute | solution.py:29
  126.0 5.7 %collective-permute-start.43 = (bf16[16,1536]{1,0:T(8,128)(2,1)S(1)}, bf16[16,1536]{1,0:T(8,128)(2,1)S(1)}, u32[]{:S(2)}, u32[]{:S(2)}) collective-permute-start(bf16[16,1536]{1,0:T(8,128)(2,1)S(1)} %pad_maximum_fusion.7), channel_id=1, source_target_pairs={{0,12},{1,13},{2,14},{3,15},{4,8},{5,9},{6,10},{7,11},{8,4},{9,5},... | collective-permute-start | bytes 147464 | tf_op jit(solution)/shard_map/ppermute | solution.py:29
  131.7 3.3 %collective-permute-start.44 = (bf16[16,512]{1,0:T(8,128)(2,1)S(1)}, bf16[16,512]{1,0:T(8,128)(2,1)S(1)}, u32[]{:S(2)}, u32[]{:S(2)}) collective-permute-start(bf16[16,512]{1,0:T(8,128)(2,1)S(1)} %add_convert_fusion.30), channel_id=1, source_target_pairs={{16,0},{17,1},{18,2},{19,3},{20,4},{21,5},{22,6},{23,7},{24,8},{25... | collective-permute-start | bytes 49160 | tf_op jit(solution)/shard_map/ppermute | solution.py:29
  138.5 9.8 %copy-start = (f32[1,128,2048]{2,1,0:T(8,128)S(1)}, f32[1,128,2048]{2,1,0:T(8,128)}, u32[]{:S(2)}) copy-start(f32[1,128,2048]{2,1,0:T(8,128)} %param.8) | copy-start | bytes 3145732
  138.5 12.8 %copy-start.2 = (f32[1,128]{1,0:T(1,128)S(1)}, f32[1,128]{1,0:T(1,128)}, u32[]{:S(2)}) copy-start(f32[1,128]{1,0:T(1,128)} %weight.1) | copy-start | bytes 1540
  138.6 7.1 %collective-permute-start.40 = (bf16[128,512]{1,0:T(8,128)(2,1)S(1)}, bf16[128,512]{1,0:T(8,128)(2,1)S(1)}, u32[]{:S(2)}, u32[]{:S(2)}) collective-permute-start(bf16[128,512]{1,0:T(8,128)(2,1)S(1)} %get-tuple-element.39), channel_id=1, source_target_pairs={{0,1},{1,0},{2,3},{3,2},{4,5},{5,4},{6,7},{7,6},{8,9},{9,8},{10,11... | collective-permute-start | bytes 393224 | tf_op jit(solution)/shard_map/ppermute | solution.py:29
  138.7 9.6 %collective-permute-start.41 = (bf16[128,512]{1,0:T(8,128)(2,1)S(1)}, bf16[128,512]{1,0:T(8,128)(2,1)S(1)}, u32[]{:S(2)}, u32[]{:S(2)}) collective-permute-start(bf16[128,512]{1,0:T(8,128)(2,1)S(1)} %get-tuple-element.38), channel_id=1, source_target_pairs={{0,2},{1,3},{2,0},{3,1},{4,6},{5,7},{6,4},{7,5},{8,10},{9,11},{10,... | collective-permute-start | bytes 393224 | tf_op jit(solution)/shard_map/ppermute | solution.py:29
  140.9 7.4 %collective-permute-start.42 = (bf16[128,512]{1,0:T(8,128)(2,1)S(1)}, bf16[128,512]{1,0:T(8,128)(2,1)S(1)}, u32[]{:S(2)}, u32[]{:S(2)}) collective-permute-start(bf16[128,512]{1,0:T(8,128)(2,1)S(1)} %get-tuple-element.37), channel_id=1, source_target_pairs={{0,3},{1,2},{2,1},{3,0},{4,7},{5,6},{6,5},{7,4},{8,11},{9,10},{10,... | collective-permute-start | bytes 393224 | tf_op jit(solution)/shard_map/ppermute | solution.py:29
  143.4 6.6 %collective-permute-start.45 = (bf16[16,2432]{1,0:T(8,128)(2,1)S(1)}, bf16[16,2432]{1,0:T(8,128)(2,1)S(1)}, u32[]{:S(2)}, u32[]{:S(2)}) collective-permute-start(bf16[16,2432]{1,0:T(8,128)(2,1)S(1)} %get-tuple-element.48), channel_id=1, source_target_pairs={{0,1},{1,0},{2,3},{3,2},{4,5},{5,4},{6,7},{7,6},{8,9},{9,8},{10,11... | collective-permute-start | bytes 233480 | tf_op jit(solution)/shard_map/ppermute | solution.py:29
  143.5 6.5 %collective-permute-start.46 = (bf16[16,2432]{1,0:T(8,128)(2,1)S(1)}, bf16[16,2432]{1,0:T(8,128)(2,1)S(1)}, u32[]{:S(2)}, u32[]{:S(2)}) collective-permute-start(bf16[16,2432]{1,0:T(8,128)(2,1)S(1)} %get-tuple-element.49), channel_id=1, source_target_pairs={{0,2},{1,3},{2,0},{3,1},{4,6},{5,7},{6,4},{7,5},{8,10},{9,11},{10,... | collective-permute-start | bytes 233480 | tf_op jit(solution)/shard_map/ppermute | solution.py:29
  145.7 5.6 %collective-permute-start.47 = (bf16[16,2432]{1,0:T(8,128)(2,1)S(1)}, bf16[16,2432]{1,0:T(8,128)(2,1)S(1)}, u32[]{:S(2)}, u32[]{:S(2)}) collective-permute-start(bf16[16,2432]{1,0:T(8,128)(2,1)S(1)} %get-tuple-element.47), channel_id=1, source_target_pairs={{0,3},{1,2},{2,1},{3,0},{4,7},{5,6},{6,5},{7,4},{8,11},{9,10},{10,... | collective-permute-start | bytes 233480 | tf_op jit(solution)/shard_map/ppermute | solution.py:29
Sparse Core Ops, SparseCore 0:
  9.8 27.9 all-gather.8
  40.1 43.7 all-gather.4
  94.4 38.9 all-gather.6

commit v16 on v15

--- a/solution.py
+++ b/solution.py
@@ -261,6 +261,10 @@
     rest = permuted(
         jnp.concatenate([rounded, theirs], axis=1), lambda p, y, x: (p, other(p, y), x)
     )
+    inner_all = tie(inner_all, rounded)
+    folded = jnp.dot(outer[:, nodes:], inner_all, preferred_element_type=f32).astype(bf16)
+
+    rest = tie(rest, folded)
     following = permuted(
         (mine + rest[:, half:].astype(f32)).astype(bf16),
         lambda p, y, x: (p - 1, y, x),
@@ -281,10 +285,6 @@
             jnp.concatenate([r0, m0, m1, r1], axis=1),
         ),
     )
-    inner_all = tie(inner_all, rounded)
-    folded = jnp.dot(outer[:, nodes:], inner_all, preferred_element_type=f32).astype(bf16)
-
-    lines = tie(lines, folded)
     sweep_line = lax.dynamic_slice(total, (0, out_place * line), (share, line))
     sweep_high = sweep_line.astype(bf16)
     sweep_low = (sweep_line - sweep_high.astype(f32)).astype(bf16)

time: 162 us -> 158 us (0.975)
  the two profiles are of different devices: /device:TPU:224 before, /device:TPU:1 now
where the time goes in v16:
time: 158 us
  waiting for transfers between devices  59.3 us (38%)
  starting transfers between devices  56.2 us (36%)
  matrix products  17.9 us (11%)
  between operations  14.3 us (9%)
  Pallas kernels  4.48 us (3%)
  local copies, waits for them, and re-layouts  3.28 us (2%)
  other arithmetic  2.4 us (2%)
    ppermute x48, starting transfers between devices, permuted(): return lax.ppermute(value, AXES, pairs)  56.1 us
    ppermute x48, waiting for transfers between devices, permuted(): return lax.ppermute(value, AXES, pairs)  47.3 us
    all_gather x3, waiting for transfers between devices, gathered(): lax.all_gather(array, AXES, axis=0, tiled=True, axis_index_groups=gather_...  11.3 us
    dot_general x15, matrix products, shards(): lax.dot_general(previous, block, (((1,), (1,)), ((), ())), preferred_elem...  9.75 us
    pallas_call x4, Pallas kernels, kernel_call(): pl.pallas_call(body, out_shape=out_shapes, in_specs=[pl.BlockSpec(memory_...  4.48 us
    dot_general x1, matrix products, shards(): lax.dot_general(outer[:, :nodes], coupling_in, (((1,), (1,)), ((), ())),...  4.3 us
    dot_general x1, matrix products, shards(): jnp.dot(outer[:, nodes:], inner_all, preferred_element_type=f32)  3.46 us
  transfers between devices with their start and end apart: 51, of which 19 were waited for; matrix products, arithmetic and copies ran while one was open for 14% of the time, Pallas kernels for 2%

profile of v16, /device:TPU:1, one launch (start us, length us, event | category | flops | bytes accessed | tf_op | source)
XLA Modules:
  0.0 157.9 jit_solution(10458653309079968944)
XLA Ops:
  7.2 0.7 all-gather.9.cloned.1.call-update
  8.0 0.8 bitcast_multiply_fusion
  8.8 0.7 broadcast_in_dim.8
  9.4 2.0 %collective-permute-start.1 = (f32[24,128]{1,0:T(8,128)S(1)}, f32[24,128]{1,0:T(8,128)S(1)}, u32[]{:S(2)}, u32[]{:S(2)}) collective-permute-start(f32[24,128]{1,0:T(8,128)S(1)} %get-tuple-element.78), channel_id=1, source_target_pairs={{0,1},{1,0},{2,3},{3,2},{4,5},{5,4},{6,7},{7,6},{8,9},{9,8},{10,11... | collective-permute-start | bytes 36872 | tf_op jit(solution)/shard_map/ppermute | solution.py:29
  11.5 2.5 %collective-permute-start.2 = (f32[24,128]{1,0:T(8,128)S(1)}, f32[24,128]{1,0:T(8,128)S(1)}, u32[]{:S(2)}, u32[]{:S(2)}) collective-permute-start(f32[24,128]{1,0:T(8,128)S(1)} %get-tuple-element.79), channel_id=1, source_target_pairs={{0,2},{1,3},{2,0},{3,1},{4,6},{5,7},{6,4},{7,5},{8,10},{9,11},{10,... | collective-permute-start | bytes 36872 | tf_op jit(solution)/shard_map/ppermute | solution.py:29
  14.0 1.0 copy-done.1
  15.7 3.0 %collective-permute-start = (bf16[128,1024]{1,0:T(8,128)(2,1)S(1)}, bf16[128,1024]{1,0:T(8,128)(2,1)S(1)}, u32[]{:S(2)}, u32[]{:S(2)}) collective-permute-start(bf16[128,1024]{1,0:T(8,128)(2,1)S(1)} %get-tuple-element.20), channel_id=1, source_target_pairs={{0,4},{1,5},{2,6},{3,7},{4,0},{5,1},{6,2},{7,3},{8,12},{9,13},{10,... | collective-permute-start | bytes 786440 | tf_op jit(solution)/shard_map/ppermute | solution.py:29
  18.7 3.7 %collective-permute-done = bf16[128,1024]{1,0:T(8,128)(2,1)S(1)} collective-permute-done((bf16[128,1024]{1,0:T(8,128)(2,1)S(1)}, bf16[128,1024]{1,0:T(8,128)(2,1)S(1)}, u32[]{:S(2)}, u32[]{:S(2)}) %collective-permute-start) | collective-permute-done | bytes 262176 | tf_op jit(solution)/shard_map/ppermute | solution.py:29
  24.0 1.1 pad_maximum_fusion
  25.1 2.6 %collective-permute-start.9 = (bf16[256,1024]{1,0:T(8,128)(2,1)S(1)}, bf16[256,1024]{1,0:T(8,128)(2,1)S(1)}, u32[]{:S(2)}, u32[]{:S(2)}) collective-permute-start(bf16[256,1024]{1,0:T(8,128)(2,1)S(1)} %maximum_select_fusion), channel_id=1, source_target_pairs={{0,3},{1,2},{2,1},{3,0},{4,7},{5,6},{6,5},{7,4},{8,11},{9,10},{10,... | collective-permute-start | bytes 1572872 | tf_op jit(solution)/shard_map/ppermute | solution.py:29
  27.7 16.1 %collective-permute-done.9 = bf16[256,1024]{1,0:T(8,128)(2,1)S(1)} collective-permute-done((bf16[256,1024]{1,0:T(8,128)(2,1)S(1)}, bf16[256,1024]{1,0:T(8,128)(2,1)S(1)}, u32[]{:S(2)}, u32[]{:S(2)}) %collective-permute-start.9) | collective-permute-done | bytes 524320 | tf_op jit(solution)/shard_map/ppermute | solution.py:29
  44.0 2.0 %collective-permute-done.7 = bf16[256,1024]{1,0:T(8,128)(2,1)S(1)} collective-permute-done((bf16[256,1024]{1,0:T(8,128)(2,1)S(1)}, bf16[256,1024]{1,0:T(8,128)(2,1)S(1)}, u32[]{:S(2)}, u32[]{:S(2)}) %collective-permute-start.7) | collective-permute-done | bytes 524320 | tf_op jit(solution)/shard_map/ppermute | solution.py:29
  46.1 1.5 collective-permute-start.8
  47.6 2.8 %collective-permute-start.4 = (f32[1,512]{1,0:T(1,128)S(1)}, f32[1,512]{1,0:T(1,128)S(1)}, u32[]{:S(2)}, u32[]{:S(2)}) collective-permute-start(f32[1,512]{1,0:T(1,128)S(1)} %slice.57), channel_id=1, source_target_pairs={{0,4},{1,5},{2,6},{3,7},{4,0},{5,1},{6,2},{7,3},{8,12},{9,13},{10,... | collective-permute-start | bytes 6152 | tf_op jit(solution)/shard_map/ppermute | solution.py:29
  50.4 1.6 %collective-permute-start.5 = (bf16[16,1024]{1,0:T(8,128)(2,1)S(1)}, bf16[16,1024]{1,0:T(8,128)(2,1)S(1)}, u32[]{:S(2)}, u32[]{:S(2)}) collective-permute-start(bf16[16,1024]{1,0:T(8,128)(2,1)S(1)} %convert_element_type.216), channel_id=1, source_target_pairs={{0,20},{1,21},{2,22},{3,23},{4,16},{5,17},{6,18},{7,19},{8,28},{9,... | collective-permute-start | bytes 98312 | tf_op jit(solution)/shard_map/ppermute | solution.py:29
  52.6 0.7 shard_map.86
  53.3 0.8 collective-permute-done.5
  54.8 8.4 %collective-permute-start.11 = (bf16[16,1024]{1,0:T(8,128)(2,1)S(1)}, bf16[16,1024]{1,0:T(8,128)(2,1)S(1)}, u32[]{:S(2)}, u32[]{:S(2)}) collective-permute-start(bf16[16,1024]{1,0:T(8,128)(2,1)S(1)} %fusion.25), channel_id=1, source_target_pairs={{16,44},{17,45},{18,46},{19,47},{20,40},{21,41},{22,42},{23,43},{2... | collective-permute-start | bytes 98312 | tf_op jit(solution)/shard_map/ppermute | solution.py:29
  63.2 1.3 collective-permute-start.12
  64.5 1.0 collective-permute-done.12
  66.1 1.4 collective-permute-start.14
  67.6 2.6 %collective-permute-done.13 = bf16[16,1024]{1,0:T(8,128)(2,1)S(1)} collective-permute-done((bf16[16,1024]{1,0:T(8,128)(2,1)S(1)}, bf16[16,1024]{1,0:T(8,128)(2,1)S(1)}, u32[]{:S(2)}, u32[]{:S(2)}) %collective-permute-start.13) | collective-permute-done | bytes 32800 | tf_op jit(solution)/shard_map/ppermute | solution.py:29
  70.9 0.7 collective-permute-start.15
  71.5 0.7 collective-permute-start.16
  72.2 0.7 fusion.28
  72.9 1.4 collective-permute-start.18
  74.3 2.6 %collective-permute-done.17 = bf16[16,1024]{1,0:T(8,128)(2,1)S(1)} collective-permute-done((bf16[16,1024]{1,0:T(8,128)(2,1)S(1)}, bf16[16,1024]{1,0:T(8,128)(2,1)S(1)}, u32[]{:S(2)}, u32[]{:S(2)}) %collective-permute-start.17) | collective-permute-done | bytes 32800 | tf_op jit(solution)/shard_map/ppermute | solution.py:29
  77.6 0.7 collective-permute-start.19
  78.3 0.7 collective-permute-start.20
  79.0 0.7 fusion.30
  79.6 1.4 collective-permute-start.22
  81.1 2.6 %collective-permute-done.21 = bf16[16,1024]{1,0:T(8,128)(2,1)S(1)} collective-permute-done((bf16[16,1024]{1,0:T(8,128)(2,1)S(1)}, bf16[16,1024]{1,0:T(8,128)(2,1)S(1)}, u32[]{:S(2)}, u32[]{:S(2)}) %collective-permute-start.21) | collective-permute-done | bytes 32800 | tf_op jit(solution)/shard_map/ppermute | solution.py:29
  83.7 0.6 fusion.31
  84.4 0.7 collective-permute-start.23
  85.0 0.7 collective-permute-start.24
  85.7 0.7 fusion.32
  86.4 1.4 collective-permute-start.26
  87.8 1.9 %collective-permute-done.25 = bf16[16,1024]{1,0:T(8,128)(2,1)S(1)} collective-permute-done((bf16[16,1024]{1,0:T(8,128)(2,1)S(1)}, bf16[16,1024]{1,0:T(8,128)(2,1)S(1)}, u32[]{:S(2)}, u32[]{:S(2)}) %collective-permute-start.25) | collective-permute-done | bytes 32800 | tf_op jit(solution)/shard_map/ppermute | solution.py:29
  90.4 0.7 collective-permute-start.27
  91.1 0.7 collective-permute-start.28
  91.8 4.3 %fusion.7 = bf16[512,512]{1,0:T(8,128)(2,1)} fusion(bf16[512,2048]{1,0:T(8,128)(2,1)} %bitcast.70, bf16[512,4096]{1,0:T(8,128)(2,1)} %all-gather.5.cloned.1.call-done), kind=kOutput, calls=%fused_computation.5 | convolution fusion | flops 1074003968 | bytes 4718592 | tf_op jit(solution)/shard_map/dot_general | solution.py:242
  96.8 1.4 collective-permute-start.30
  98.2 1.9 %collective-permute-done.29 = bf16[16,1024]{1,0:T(8,128)(2,1)S(1)} collective-permute-done((bf16[16,1024]{1,0:T(8,128)(2,1)S(1)}, bf16[16,1024]{1,0:T(8,128)(2,1)S(1)}, u32[]{:S(2)}, u32[]{:S(2)}) %collective-permute-start.29) | collective-permute-done | bytes 32800 | tf_op jit(solution)/shard_map/ppermute | solution.py:29
  100.8 0.7 collective-permute-start.31
  101.5 0.7 collective-permute-start.32
  102.8 1.4 collective-permute-start.34
  104.2 1.9 %collective-permute-done.33 = bf16[16,1024]{1,0:T(8,128)(2,1)S(1)} collective-permute-done((bf16[16,1024]{1,0:T(8,128)(2,1)S(1)}, bf16[16,1024]{1,0:T(8,128)(2,1)S(1)}, u32[]{:S(2)}, u32[]{:S(2)}) %collective-permute-start.33) | collective-permute-done | bytes 32800 | tf_op jit(solution)/shard_map/ppermute | solution.py:29
  106.8 0.7 collective-permute-start.35
  107.5 0.7 collective-permute-start.36
  108.8 1.4 collective-permute-start.38
  110.3 1.9 %collective-permute-done.37 = bf16[16,1024]{1,0:T(8,128)(2,1)S(1)} collective-permute-done((bf16[16,1024]{1,0:T(8,128)(2,1)S(1)}, bf16[16,1024]{1,0:T(8,128)(2,1)S(1)}, u32[]{:S(2)}, u32[]{:S(2)}) %collective-permute-start.37) | collective-permute-done | bytes 32800 | tf_op jit(solution)/shard_map/ppermute | solution.py:29
  112.2 0.7 fusion.40
  113.0 3.8 %collective-permute-done.39 = bf16[16,1024]{1,0:T(8,128)(2,1)S(1)} collective-permute-done((bf16[16,1024]{1,0:T(8,128)(2,1)S(1)}, bf16[16,1024]{1,0:T(8,128)(2,1)S(1)}, u32[]{:S(2)}, u32[]{:S(2)}) %collective-permute-start.39) | collective-permute-done | bytes 32800 | tf_op jit(solution)/shard_map/ppermute | solution.py:29
  117.4 11.3 %all-gather.7.cloned.1.call-done = bf16[2048,512]{1,0:T(8,128)(2,1)} async-done(((bf16[512,512]{1,0:T(8,128)(2,1)}), bf16[2048,512]{1,0:T(8,128)(2,1)}) %all-gather.7.cloned.1.call-update) | async-done | bytes 2097168 | tf_op jit(solution)/shard_map/all_gather | solution.py:133
  128.7 3.5 %fusion.4 = bf16[512,512]{1,0:T(8,128)(2,1)S(1)} fusion(bf16[2048,512]{1,0:T(8,128)(2,1)} %all-gather.7.cloned.1.call-done, bf16[512,4096]{1,0:T(8,128)(2,1)} %all-gather.5.cloned.1.call-done), kind=kOutput, calls=%fused_computation.4 | convolution fusion | flops 1074003968 | bytes 4718592 | tf_op jit(solution)/shard_map/dot_general | solution.py:265
  132.3 4.2 %collective-permute-start.44 = (bf16[16,512]{1,0:T(8,128)(2,1)S(1)}, bf16[16,512]{1,0:T(8,128)(2,1)S(1)}, u32[]{:S(2)}, u32[]{:S(2)}) collective-permute-start(bf16[16,512]{1,0:T(8,128)(2,1)S(1)} %add_convert_fusion.30), channel_id=1, source_target_pairs={{16,0},{17,1},{18,2},{19,3},{20,4},{21,5},{22,6},{23,7},{24,8},{25... | collective-permute-start | bytes 49160 | tf_op jit(solution)/shard_map/ppermute | solution.py:29
  137.0 2.4 %collective-permute-start.41 = (bf16[128,512]{1,0:T(8,128)(2,1)S(1)}, bf16[128,512]{1,0:T(8,128)(2,1)S(1)}, u32[]{:S(2)}, u32[]{:S(2)}) collective-permute-start(bf16[128,512]{1,0:T(8,128)(2,1)S(1)} %get-tuple-element.38), channel_id=1, source_target_pairs={{0,2},{1,3},{2,0},{3,1},{4,6},{5,7},{6,4},{7,5},{8,10},{9,11},{10,... | collective-permute-start | bytes 393224 | tf_op jit(solution)/shard_map/ppermute | solution.py:29
  139.4 1.1 collective-permute-start.42
  140.5 1.1 collective-permute-start.45
  141.7 2.7 %collective-permute-start.46 = (bf16[16,2432]{1,0:T(8,128)(2,1)S(1)}, bf16[16,2432]{1,0:T(8,128)(2,1)S(1)}, u32[]{:S(2)}, u32[]{:S(2)}) collective-permute-start(bf16[16,2432]{1,0:T(8,128)(2,1)S(1)} %get-tuple-element.49), channel_id=1, source_target_pairs={{0,2},{1,3},{2,0},{3,1},{4,6},{5,7},{6,4},{7,5},{8,10},{9,11},{10,... | collective-permute-start | bytes 233480 | tf_op jit(solution)/shard_map/ppermute | solution.py:29
  144.8 1.8 %shard_map.87 = (f32[128,2048]{1,0:T(8,128)}, bf16[128,2048]{1,0:T(8,128)(2,1)S(1)}) custom-call(s32[3]{0:T(128)S(1)} %pad_add_fusion.place, f32[128,2048]{1,0:T(8,128)S(1)} %bitcast.57, bf16[128,512]{1,0:T(8,128)(2,1)S(1)} %get-tuple-element.40.refs_1_, bf16[128,512]{1,0:T(8,128)(2,1)S(1)} %collective-permute-done.40.refs_2_, ...), custom_call_target="tpu_custom_call" | custom-call | bytes 3145728 | tf_op jit(solution)/shard_map/pallas_call | solution.py:58
  146.6 1.7 %collective-permute-done.46.refs_2_ = bf16[16,2432]{1,0:T(8,128)(2,1)S(1)} collective-permute-done((bf16[16,2432]{1,0:T(8,128)(2,1)S(1)}, bf16[16,2432]{1,0:T(8,128)(2,1)S(1)}, u32[]{:S(2)}, u32[]{:S(2)}) %collective-permute-start.46) | collective-permute-done | bytes 77856 | tf_op jit(solution)/shard_map/ppermute | solution.py:29
  148.3 1.7 %collective-permute-done.47.refs_3_ = bf16[16,2432]{1,0:T(8,128)(2,1)S(1)} collective-permute-done((bf16[16,2432]{1,0:T(8,128)(2,1)S(1)}, bf16[16,2432]{1,0:T(8,128)(2,1)S(1)}, u32[]{:S(2)}, u32[]{:S(2)}) %collective-permute-start.47) | collective-permute-done | bytes 77856 | tf_op jit(solution)/shard_map/ppermute | solution.py:29
  150.0 1.5 shard_map.88
  (110 shorter events, 11.8 us)
Async XLA Ops:
  7.2 15.4 %copy-start.3 = (bf16[1,128,2048]{2,1,0:T(8,128)(2,1)S(1)}, bf16[1,128,2048]{2,1,0:T(8,128)(2,1)}, u32[]{:S(2)}) copy-start(bf16[1,128,2048]{2,1,0:T(8,128)(2,1)} %param.7) | copy-start | bytes 1572868
  7.2 84.6 %all-gather.9.cloned.1.call-start = ((), (), s32[]{:S(2)}) async-start(), calls=%async_computation.2 | async-start | bytes 2621440 | tf_op jit(solution)/shard_map/all_gather | solution.py:133
  7.9 83.9 %all-gather.5.cloned.1.call-start = ((), (), s32[]{:S(2)}) async-start(), calls=%async_computation | async-start | bytes 5242880 | tf_op jit(solution)/shard_map/all_gather | solution.py:133
  9.4 9.2 %collective-permute-start.1 = (f32[24,128]{1,0:T(8,128)S(1)}, f32[24,128]{1,0:T(8,128)S(1)}, u32[]{:S(2)}, u32[]{:S(2)}) collective-permute-start(f32[24,128]{1,0:T(8,128)S(1)} %get-tuple-element.78), channel_id=1, source_target_pairs={{0,1},{1,0},{2,3},{3,2},{4,5},{5,4},{6,7},{7,6},{8,9},{9,8},{10,11... | collective-permute-start | bytes 36872 | tf_op jit(solution)/shard_map/ppermute | solution.py:29
  11.5 7.2 %collective-permute-start.2 = (f32[24,128]{1,0:T(8,128)S(1)}, f32[24,128]{1,0:T(8,128)S(1)}, u32[]{:S(2)}, u32[]{:S(2)}) collective-permute-start(f32[24,128]{1,0:T(8,128)S(1)} %get-tuple-element.79), channel_id=1, source_target_pairs={{0,2},{1,3},{2,0},{3,1},{4,6},{5,7},{6,4},{7,5},{8,10},{9,11},{10,... | collective-permute-start | bytes 36872 | tf_op jit(solution)/shard_map/ppermute | solution.py:29
  13.9 4.7 %collective-permute-start.3 = (f32[24,128]{1,0:T(8,128)S(1)}, f32[24,128]{1,0:T(8,128)S(1)}, u32[]{:S(2)}, u32[]{:S(2)}) collective-permute-start(f32[24,128]{1,0:T(8,128)S(1)} %get-tuple-element.80), channel_id=1, source_target_pairs={{0,3},{1,2},{2,1},{3,0},{4,7},{5,6},{6,5},{7,4},{8,11},{9,10},{10,... | collective-permute-start | bytes 36872 | tf_op jit(solution)/shard_map/ppermute | solution.py:29
  14.0 1.0 copy-start.1
  15.7 6.7 %collective-permute-start = (bf16[128,1024]{1,0:T(8,128)(2,1)S(1)}, bf16[128,1024]{1,0:T(8,128)(2,1)S(1)}, u32[]{:S(2)}, u32[]{:S(2)}) collective-permute-start(bf16[128,1024]{1,0:T(8,128)(2,1)S(1)} %get-tuple-element.20), channel_id=1, source_target_pairs={{0,4},{1,5},{2,6},{3,7},{4,0},{5,1},{6,2},{7,3},{8,12},{9,13},{10,... | collective-permute-start | bytes 786440 | tf_op jit(solution)/shard_map/ppermute | solution.py:29
  22.9 1.0 copy-start.4
  25.1 103.7 %all-gather.7.cloned.1.call-start = ((), (), s32[]{:S(2)}) async-start(), calls=%async_computation.1 | async-start | bytes 2621440 | tf_op jit(solution)/shard_map/all_gather | solution.py:133
  25.1 18.8 %collective-permute-start.9 = (bf16[256,1024]{1,0:T(8,128)(2,1)S(1)}, bf16[256,1024]{1,0:T(8,128)(2,1)S(1)}, u32[]{:S(2)}, u32[]{:S(2)}) collective-permute-start(bf16[256,1024]{1,0:T(8,128)(2,1)S(1)} %maximum_select_fusion), channel_id=1, source_target_pairs={{0,3},{1,2},{2,1},{3,0},{4,7},{5,6},{6,5},{7,4},{8,11},{9,10},{10,... | collective-permute-start | bytes 1572872 | tf_op jit(solution)/shard_map/ppermute | solution.py:29
  27.7 18.4 %collective-permute-start.7 = (bf16[256,1024]{1,0:T(8,128)(2,1)S(1)}, bf16[256,1024]{1,0:T(8,128)(2,1)S(1)}, u32[]{:S(2)}, u32[]{:S(2)}) collective-permute-start(bf16[256,1024]{1,0:T(8,128)(2,1)S(1)} %maximum_select_fusion), channel_id=1, source_target_pairs={{0,1},{1,0},{2,3},{3,2},{4,5},{5,4},{6,7},{7,6},{8,9},{9,8},{10,11... | collective-permute-start | bytes 1572872 | tf_op jit(solution)/shard_map/ppermute | solution.py:29
  43.9 8.2 %collective-permute-start.10 = (bf16[128,1024]{1,0:T(8,128)(2,1)S(1)}, bf16[128,1024]{1,0:T(8,128)(2,1)S(1)}, u32[]{:S(2)}, u32[]{:S(2)}) collective-permute-start(bf16[128,1024]{1,0:T(8,128)(2,1)S(1)} %get-tuple-element.42.refs_7_), channel_id=1, source_target_pairs={{0,1},{1,0},{2,3},{3,2},{4,5},{5,4},{6,7},{7,6},{8,9},{9,8},{10,11... | collective-permute-start | bytes 786440 | tf_op jit(solution)/shard_map/ppermute | solution.py:29
  46.1 6.5 %collective-permute-start.8 = (bf16[128,1024]{1,0:T(8,128)(2,1)S(1)}, bf16[128,1024]{1,0:T(8,128)(2,1)S(1)}, u32[]{:S(2)}, u32[]{:S(2)}) collective-permute-start(bf16[128,1024]{1,0:T(8,128)(2,1)S(1)} %get-tuple-element.44.refs_2_), channel_id=1, source_target_pairs={{0,3},{1,2},{2,1},{3,0},{4,7},{5,6},{6,5},{7,4},{8,11},{9,10},{10,... | collective-permute-start | bytes 786440 | tf_op jit(solution)/shard_map/ppermute | solution.py:29
  47.6 4.4 %collective-permute-start.4 = (f32[1,512]{1,0:T(1,128)S(1)}, f32[1,512]{1,0:T(1,128)S(1)}, u32[]{:S(2)}, u32[]{:S(2)}) collective-permute-start(f32[1,512]{1,0:T(1,128)S(1)} %slice.57), channel_id=1, source_target_pairs={{0,4},{1,5},{2,6},{3,7},{4,0},{5,1},{6,2},{7,3},{8,12},{9,13},{10,... | collective-permute-start | bytes 6152 | tf_op jit(solution)/shard_map/ppermute | solution.py:29
  50.4 3.7 %collective-permute-start.5 = (bf16[16,1024]{1,0:T(8,128)(2,1)S(1)}, bf16[16,1024]{1,0:T(8,128)(2,1)S(1)}, u32[]{:S(2)}, u32[]{:S(2)}) collective-permute-start(bf16[16,1024]{1,0:T(8,128)(2,1)S(1)} %convert_element_type.216), channel_id=1, source_target_pairs={{0,20},{1,21},{2,22},{3,23},{4,16},{5,17},{6,18},{7,19},{8,28},{9,... | collective-permute-start | bytes 98312 | tf_op jit(solution)/shard_map/ppermute | solution.py:29
  52.0 2.1 %collective-permute-start.6 = (bf16[16,1024]{1,0:T(8,128)(2,1)S(1)}, bf16[16,1024]{1,0:T(8,128)(2,1)S(1)}, u32[]{:S(2)}, u32[]{:S(2)}) collective-permute-start(bf16[16,1024]{1,0:T(8,128)(2,1)S(1)} %convert_element_type.216), channel_id=1, source_target_pairs={{0,16},{1,17},{2,18},{3,19},{4,20},{5,21},{6,22},{7,23},{8,24},{9,... | collective-permute-start | bytes 98312 | tf_op jit(solution)/shard_map/ppermute | solution.py:29
  54.8 9.7 %collective-permute-start.11 = (bf16[16,1024]{1,0:T(8,128)(2,1)S(1)}, bf16[16,1024]{1,0:T(8,128)(2,1)S(1)}, u32[]{:S(2)}, u32[]{:S(2)}) collective-permute-start(bf16[16,1024]{1,0:T(8,128)(2,1)S(1)} %fusion.25), channel_id=1, source_target_pairs={{16,44},{17,45},{18,46},{19,47},{20,40},{21,41},{22,42},{23,43},{2... | collective-permute-start | bytes 98312 | tf_op jit(solution)/shard_map/ppermute | solution.py:29
  63.2 2.3 %collective-permute-start.12 = (bf16[16,1024]{1,0:T(8,128)(2,1)S(1)}, bf16[16,1024]{1,0:T(8,128)(2,1)S(1)}, u32[]{:S(2)}, u32[]{:S(2)}) collective-permute-start(bf16[16,1024]{1,0:T(8,128)(2,1)S(1)} %fusion.25), channel_id=1, source_target_pairs={{16,32},{17,33},{18,34},{19,35},{20,36},{21,37},{22,38},{23,39},{2... | collective-permute-start | bytes 98312 | tf_op jit(solution)/shard_map/ppermute | solution.py:29
  66.1 4.1 %collective-permute-start.13 = (bf16[16,1024]{1,0:T(8,128)(2,1)S(1)}, bf16[16,1024]{1,0:T(8,128)(2,1)S(1)}, u32[]{:S(2)}, u32[]{:S(2)}) collective-permute-start(bf16[16,1024]{1,0:T(8,128)(2,1)S(1)} %fusion.26), channel_id=1, source_target_pairs={{0,20},{1,21},{2,22},{3,23},{4,16},{5,17},{6,18},{7,19},{8,28},{9,... | collective-permute-start | bytes 98312 | tf_op jit(solution)/shard_map/ppermute | solution.py:29
  66.1 4.1 %collective-permute-start.14 = (bf16[16,1024]{1,0:T(8,128)(2,1)S(1)}, bf16[16,1024]{1,0:T(8,128)(2,1)S(1)}, u32[]{:S(2)}, u32[]{:S(2)}) collective-permute-start(bf16[16,1024]{1,0:T(8,128)(2,1)S(1)} %fusion.26), channel_id=1, source_target_pairs={{0,16},{1,17},{2,18},{3,19},{4,20},{5,21},{6,22},{7,23},{8,24},{9,... | collective-permute-start | bytes 98312 | tf_op jit(solution)/shard_map/ppermute | solution.py:29
  70.9 1.3 collective-permute-start.15
  71.5 0.7 collective-permute-start.16
  72.9 4.1 %collective-permute-start.17 = (bf16[16,1024]{1,0:T(8,128)(2,1)S(1)}, bf16[16,1024]{1,0:T(8,128)(2,1)S(1)}, u32[]{:S(2)}, u32[]{:S(2)}) collective-permute-start(bf16[16,1024]{1,0:T(8,128)(2,1)S(1)} %fusion.28), channel_id=1, source_target_pairs={{0,20},{1,21},{2,22},{3,23},{4,16},{5,17},{6,18},{7,19},{8,28},{9,... | collective-permute-start | bytes 98312 | tf_op jit(solution)/shard_map/ppermute | solution.py:29
  72.9 4.1 %collective-permute-start.18 = (bf16[16,1024]{1,0:T(8,128)(2,1)S(1)}, bf16[16,1024]{1,0:T(8,128)(2,1)S(1)}, u32[]{:S(2)}, u32[]{:S(2)}) collective-permute-start(bf16[16,1024]{1,0:T(8,128)(2,1)S(1)} %fusion.28), channel_id=1, source_target_pairs={{0,16},{1,17},{2,18},{3,19},{4,20},{5,21},{6,22},{7,23},{8,24},{9,... | collective-permute-start | bytes 98312 | tf_op jit(solution)/shard_map/ppermute | solution.py:29
  77.6 1.3 collective-permute-start.19
  78.3 0.7 collective-permute-start.20
  79.6 4.1 %collective-permute-start.21 = (bf16[16,1024]{1,0:T(8,128)(2,1)S(1)}, bf16[16,1024]{1,0:T(8,128)(2,1)S(1)}, u32[]{:S(2)}, u32[]{:S(2)}) collective-permute-start(bf16[16,1024]{1,0:T(8,128)(2,1)S(1)} %fusion.30), channel_id=1, source_target_pairs={{0,20},{1,21},{2,22},{3,23},{4,16},{5,17},{6,18},{7,19},{8,28},{9,... | collective-permute-start | bytes 98312 | tf_op jit(solution)/shard_map/ppermute | solution.py:29
  79.6 4.1 %collective-permute-start.22 = (bf16[16,1024]{1,0:T(8,128)(2,1)S(1)}, bf16[16,1024]{1,0:T(8,128)(2,1)S(1)}, u32[]{:S(2)}, u32[]{:S(2)}) collective-permute-start(bf16[16,1024]{1,0:T(8,128)(2,1)S(1)} %fusion.30), channel_id=1, source_target_pairs={{0,16},{1,17},{2,18},{3,19},{4,20},{5,21},{6,22},{7,23},{8,24},{9,... | collective-permute-start | bytes 98312 | tf_op jit(solution)/shard_map/ppermute | solution.py:29
  84.4 1.3 collective-permute-start.23
  85.0 0.7 collective-permute-start.24
  86.4 3.4 %collective-permute-start.25 = (bf16[16,1024]{1,0:T(8,128)(2,1)S(1)}, bf16[16,1024]{1,0:T(8,128)(2,1)S(1)}, u32[]{:S(2)}, u32[]{:S(2)}) collective-permute-start(bf16[16,1024]{1,0:T(8,128)(2,1)S(1)} %fusion.32), channel_id=1, source_target_pairs={{0,20},{1,21},{2,22},{3,23},{4,16},{5,17},{6,18},{7,19},{8,28},{9,... | collective-permute-start | bytes 98312 | tf_op jit(solution)/shard_map/ppermute | solution.py:29
  86.4 3.4 %collective-permute-start.26 = (bf16[16,1024]{1,0:T(8,128)(2,1)S(1)}, bf16[16,1024]{1,0:T(8,128)(2,1)S(1)}, u32[]{:S(2)}, u32[]{:S(2)}) collective-permute-start(bf16[16,1024]{1,0:T(8,128)(2,1)S(1)} %fusion.32), channel_id=1, source_target_pairs={{0,16},{1,17},{2,18},{3,19},{4,20},{5,21},{6,22},{7,23},{8,24},{9,... | collective-permute-start | bytes 98312 | tf_op jit(solution)/shard_map/ppermute | solution.py:29
  90.4 5.7 %collective-permute-start.27 = (bf16[16,1024]{1,0:T(8,128)(2,1)S(1)}, bf16[16,1024]{1,0:T(8,128)(2,1)S(1)}, u32[]{:S(2)}, u32[]{:S(2)}) collective-permute-start(bf16[16,1024]{1,0:T(8,128)(2,1)S(1)} %fusion.33), channel_id=1, source_target_pairs={{144,172},{145,173},{146,174},{147,175},{148,168},{149,169},{150,1... | collective-permute-start | bytes 98312 | tf_op jit(solution)/shard_map/ppermute | solution.py:29
  91.1 5.1 %collective-permute-start.28 = (bf16[16,1024]{1,0:T(8,128)(2,1)S(1)}, bf16[16,1024]{1,0:T(8,128)(2,1)S(1)}, u32[]{:S(2)}, u32[]{:S(2)}) collective-permute-start(bf16[16,1024]{1,0:T(8,128)(2,1)S(1)} %fusion.33), channel_id=1, source_target_pairs={{144,160},{145,161},{146,162},{147,163},{148,164},{149,165},{150,1... | collective-permute-start | bytes 98312 | tf_op jit(solution)/shard_map/ppermute | solution.py:29
  96.8 3.3 %collective-permute-start.29 = (bf16[16,1024]{1,0:T(8,128)(2,1)S(1)}, bf16[16,1024]{1,0:T(8,128)(2,1)S(1)}, u32[]{:S(2)}, u32[]{:S(2)}) collective-permute-start(bf16[16,1024]{1,0:T(8,128)(2,1)S(1)} %fusion.34), channel_id=1, source_target_pairs={{0,20},{1,21},{2,22},{3,23},{4,16},{5,17},{6,18},{7,19},{8,28},{9,... | collective-permute-start | bytes 98312 | tf_op jit(solution)/shard_map/ppermute | solution.py:29
  96.8 3.3 %collective-permute-start.30 = (bf16[16,1024]{1,0:T(8,128)(2,1)S(1)}, bf16[16,1024]{1,0:T(8,128)(2,1)S(1)}, u32[]{:S(2)}, u32[]{:S(2)}) collective-permute-start(bf16[16,1024]{1,0:T(8,128)(2,1)S(1)} %fusion.34), channel_id=1, source_target_pairs={{0,16},{1,17},{2,18},{3,19},{4,20},{5,21},{6,22},{7,23},{8,24},{9,... | collective-permute-start | bytes 98312 | tf_op jit(solution)/shard_map/ppermute | solution.py:29
  100.8 1.3 collective-permute-start.31
  101.5 0.7 collective-permute-start.32
  102.8 3.4 %collective-permute-start.33 = (bf16[16,1024]{1,0:T(8,128)(2,1)S(1)}, bf16[16,1024]{1,0:T(8,128)(2,1)S(1)}, u32[]{:S(2)}, u32[]{:S(2)}) collective-permute-start(bf16[16,1024]{1,0:T(8,128)(2,1)S(1)} %fusion.36), channel_id=1, source_target_pairs={{0,20},{1,21},{2,22},{3,23},{4,16},{5,17},{6,18},{7,19},{8,28},{9,... | collective-permute-start | bytes 98312 | tf_op jit(solution)/shard_map/ppermute | solution.py:29
  102.8 3.3 %collective-permute-start.34 = (bf16[16,1024]{1,0:T(8,128)(2,1)S(1)}, bf16[16,1024]{1,0:T(8,128)(2,1)S(1)}, u32[]{:S(2)}, u32[]{:S(2)}) collective-permute-start(bf16[16,1024]{1,0:T(8,128)(2,1)S(1)} %fusion.36), channel_id=1, source_target_pairs={{0,16},{1,17},{2,18},{3,19},{4,20},{5,21},{6,22},{7,23},{8,24},{9,... | collective-permute-start | bytes 98312 | tf_op jit(solution)/shard_map/ppermute | solution.py:29
  106.8 1.3 collective-permute-start.35
  107.5 0.7 collective-permute-start.36
  108.8 3.4 %collective-permute-start.37 = (bf16[16,1024]{1,0:T(8,128)(2,1)S(1)}, bf16[16,1024]{1,0:T(8,128)(2,1)S(1)}, u32[]{:S(2)}, u32[]{:S(2)}) collective-permute-start(bf16[16,1024]{1,0:T(8,128)(2,1)S(1)} %fusion.38), channel_id=1, source_target_pairs={{0,20},{1,21},{2,22},{3,23},{4,16},{5,17},{6,18},{7,19},{8,28},{9,... | collective-permute-start | bytes 98312 | tf_op jit(solution)/shard_map/ppermute | solution.py:29
  108.8 3.3 %collective-permute-start.38 = (bf16[16,1024]{1,0:T(8,128)(2,1)S(1)}, bf16[16,1024]{1,0:T(8,128)(2,1)S(1)}, u32[]{:S(2)}, u32[]{:S(2)}) collective-permute-start(bf16[16,1024]{1,0:T(8,128)(2,1)S(1)} %fusion.38), channel_id=1, source_target_pairs={{0,16},{1,17},{2,18},{3,19},{4,20},{5,21},{6,22},{7,23},{8,24},{9,... | collective-permute-start | bytes 98312 | tf_op jit(solution)/shard_map/ppermute | solution.py:29
  112.8 4.0 %collective-permute-start.39 = (bf16[16,1024]{1,0:T(8,128)(2,1)S(1)}, bf16[16,1024]{1,0:T(8,128)(2,1)S(1)}, u32[]{:S(2)}, u32[]{:S(2)}) collective-permute-start(bf16[16,1024]{1,0:T(8,128)(2,1)S(1)} %fusion.40), channel_id=1, source_target_pairs={{0,4},{1,5},{2,6},{3,7},{4,0},{5,1},{6,2},{7,3},{8,12},{9,13},{10,... | collective-permute-start | bytes 98312 | tf_op jit(solution)/shard_map/ppermute | solution.py:29
  117.2 15.0 %collective-permute-start.43 = (bf16[16,1536]{1,0:T(8,128)(2,1)S(1)}, bf16[16,1536]{1,0:T(8,128)(2,1)S(1)}, u32[]{:S(2)}, u32[]{:S(2)}) collective-permute-start(bf16[16,1536]{1,0:T(8,128)(2,1)S(1)} %pad_maximum_fusion.7), channel_id=1, source_target_pairs={{0,12},{1,13},{2,14},{3,15},{4,8},{5,9},{6,10},{7,11},{8,4},{9,5},... | collective-permute-start | bytes 147464 | tf_op jit(solution)/shard_map/ppermute | solution.py:29
  132.2 12.6 %copy-start = (f32[1,128,2048]{2,1,0:T(8,128)S(1)}, f32[1,128,2048]{2,1,0:T(8,128)}, u32[]{:S(2)}) copy-start(f32[1,128,2048]{2,1,0:T(8,128)} %param.8) | copy-start | bytes 3145732
  132.2 17.8 %copy-start.2 = (f32[1,128]{1,0:T(1,128)S(1)}, f32[1,128]{1,0:T(1,128)}, u32[]{:S(2)}) copy-start(f32[1,128]{1,0:T(1,128)} %weight.1) | copy-start | bytes 1540
  132.3 8.2 %collective-permute-start.44 = (bf16[16,512]{1,0:T(8,128)(2,1)S(1)}, bf16[16,512]{1,0:T(8,128)(2,1)S(1)}, u32[]{:S(2)}, u32[]{:S(2)}) collective-permute-start(bf16[16,512]{1,0:T(8,128)(2,1)S(1)} %add_convert_fusion.30), channel_id=1, source_target_pairs={{16,0},{17,1},{18,2},{19,3},{20,4},{21,5},{22,6},{23,7},{24,8},{25... | collective-permute-start | bytes 49160 | tf_op jit(solution)/shard_map/ppermute | solution.py:29
  136.5 7.9 %collective-permute-start.40 = (bf16[128,512]{1,0:T(8,128)(2,1)S(1)}, bf16[128,512]{1,0:T(8,128)(2,1)S(1)}, u32[]{:S(2)}, u32[]{:S(2)}) collective-permute-start(bf16[128,512]{1,0:T(8,128)(2,1)S(1)} %get-tuple-element.39), channel_id=1, source_target_pairs={{0,1},{1,0},{2,3},{3,2},{4,5},{5,4},{6,7},{7,6},{8,9},{9,8},{10,11... | collective-permute-start | bytes 393224 | tf_op jit(solution)/shard_map/ppermute | solution.py:29
  137.0 7.6 %collective-permute-start.41 = (bf16[128,512]{1,0:T(8,128)(2,1)S(1)}, bf16[128,512]{1,0:T(8,128)(2,1)S(1)}, u32[]{:S(2)}, u32[]{:S(2)}) collective-permute-start(bf16[128,512]{1,0:T(8,128)(2,1)S(1)} %get-tuple-element.38), channel_id=1, source_target_pairs={{0,2},{1,3},{2,0},{3,1},{4,6},{5,7},{6,4},{7,5},{8,10},{9,11},{10,... | collective-permute-start | bytes 393224 | tf_op jit(solution)/shard_map/ppermute | solution.py:29
  139.4 5.5 %collective-permute-start.42 = (bf16[128,512]{1,0:T(8,128)(2,1)S(1)}, bf16[128,512]{1,0:T(8,128)(2,1)S(1)}, u32[]{:S(2)}, u32[]{:S(2)}) collective-permute-start(bf16[128,512]{1,0:T(8,128)(2,1)S(1)} %get-tuple-element.37), channel_id=1, source_target_pairs={{0,3},{1,2},{2,1},{3,0},{4,7},{5,6},{6,5},{7,4},{8,11},{9,10},{10,... | collective-permute-start | bytes 393224 | tf_op jit(solution)/shard_map/ppermute | solution.py:29
  140.5 6.0 %collective-permute-start.45 = (bf16[16,2432]{1,0:T(8,128)(2,1)S(1)}, bf16[16,2432]{1,0:T(8,128)(2,1)S(1)}, u32[]{:S(2)}, u32[]{:S(2)}) collective-permute-start(bf16[16,2432]{1,0:T(8,128)(2,1)S(1)} %get-tuple-element.48), channel_id=1, source_target_pairs={{0,1},{1,0},{2,3},{3,2},{4,5},{5,4},{6,7},{7,6},{8,9},{9,8},{10,11... | collective-permute-start | bytes 233480 | tf_op jit(solution)/shard_map/ppermute | solution.py:29
  141.7 6.6 %collective-permute-start.46 = (bf16[16,2432]{1,0:T(8,128)(2,1)S(1)}, bf16[16,2432]{1,0:T(8,128)(2,1)S(1)}, u32[]{:S(2)}, u32[]{:S(2)}) collective-permute-start(bf16[16,2432]{1,0:T(8,128)(2,1)S(1)} %get-tuple-element.49), channel_id=1, source_target_pairs={{0,2},{1,3},{2,0},{3,1},{4,6},{5,7},{6,4},{7,5},{8,10},{9,11},{10,... | collective-permute-start | bytes 233480 | tf_op jit(solution)/shard_map/ppermute | solution.py:29
  144.3 5.6 %collective-permute-start.47 = (bf16[16,2432]{1,0:T(8,128)(2,1)S(1)}, bf16[16,2432]{1,0:T(8,128)(2,1)S(1)}, u32[]{:S(2)}, u32[]{:S(2)}) collective-permute-start(bf16[16,2432]{1,0:T(8,128)(2,1)S(1)} %get-tuple-element.47), channel_id=1, source_target_pairs={{0,3},{1,2},{2,1},{3,0},{4,7},{5,6},{6,5},{7,4},{8,11},{9,10},{10,... | collective-permute-start | bytes 233480 | tf_op jit(solution)/shard_map/ppermute | solution.py:29
Sparse Core Ops, SparseCore 0:
  9.8 40.2 all-gather.8
  52.5 35.4 all-gather.4
  96.2 32.4 all-gather.6

commit v17 on v16

--- a/solution.py
+++ b/solution.py
@@ -267,9 +267,9 @@
     rest = tie(rest, folded)
     following = permuted(
         (mine + rest[:, half:].astype(f32)).astype(bf16),
-        lambda p, y, x: (p - 1, y, x),
-        range(1, PARTITIONS),
-    )
+        lambda p, y, x: ((p - 1) % PARTITIONS, y, x),
+    )
+    following = jnp.where(p < PARTITIONS - 1, following, jnp.zeros_like(following))
 
     m0, m1, r0, r1 = rounded[:, :line], rounded[:, line:], rest[:, :line], rest[:, line:half]
     lines = jnp.where(

time: 158 us -> 158 us (level)
  the two profiles are of different devices: /device:TPU:1 before, /device:TPU:6 now
where the time goes in v17:
time: 158 us; the launch traced here: 157 us
  waiting for transfers between devices  58.4 us (37%)
  starting transfers between devices  56.4 us (36%)
  matrix products  17.9 us (11%)
  between operations  14.3 us (9%)
  Pallas kernels  4.48 us (3%)
  local copies, waits for them, and re-layouts  3.26 us (2%)
  other arithmetic  2.4 us (2%)
    ppermute x48, starting transfers between devices, permuted(): return lax.ppermute(value, AXES, pairs)  56.3 us
    ppermute x48, waiting for transfers between devices, permuted(): return lax.ppermute(value, AXES, pairs)  42.3 us
    all_gather x3, waiting for transfers between devices, gathered(): lax.all_gather(array, AXES, axis=0, tiled=True, axis_index_groups=gather_...  15.4 us
    dot_general x15, matrix products, shards(): lax.dot_general(previous, block, (((1,), (1,)), ((), ())), preferred_elem...  9.75 us
    pallas_call x4, Pallas kernels, kernel_call(): pl.pallas_call(body, out_shape=out_shapes, in_specs=[pl.BlockSpec(memory_...  4.48 us
    dot_general x1, matrix products, shards(): lax.dot_general(outer[:, :nodes], coupling_in, (((1,), (1,)), ((), ())),...  4.3 us
    dot_general x1, matrix products, shards(): jnp.dot(outer[:, nodes:], inner_all, preferred_element_type=f32)  3.46 us
  transfers between devices with their start and end apart: 51, of which 16 were waited for; matrix products, arithmetic and copies ran while one was open for 14% of the time, Pallas kernels for 2%

profile of v17, /device:TPU:6, one launch (start us, length us, event | category | flops | bytes accessed | tf_op | source)
XLA Modules:
  0.0 157.2 jit_solution(361529565283576481)
XLA Ops:
  7.2 0.7 all-gather.9.cloned.1.call-update
  8.0 0.8 bitcast_multiply_fusion
  8.8 0.7 broadcast_in_dim.10
  9.4 0.8 collective-permute-start.1
  10.3 2.8 %collective-permute-start.2 = (f32[24,128]{1,0:T(8,128)S(1)}, f32[24,128]{1,0:T(8,128)S(1)}, u32[]{:S(2)}, u32[]{:S(2)}) collective-permute-start(f32[24,128]{1,0:T(8,128)S(1)} %get-tuple-element.79), channel_id=1, source_target_pairs={{0,2},{1,3},{2,0},{3,1},{4,6},{5,7},{6,4},{7,5},{8,10},{9,11},{10,... | collective-permute-start | bytes 36872 | tf_op jit(solution)/shard_map/ppermute | solution.py:29
  13.1 1.0 collective-permute-start.3
  14.2 1.0 copy-done.1
  15.8 1.7 %collective-permute-start = (bf16[128,1024]{1,0:T(8,128)(2,1)S(1)}, bf16[128,1024]{1,0:T(8,128)(2,1)S(1)}, u32[]{:S(2)}, u32[]{:S(2)}) collective-permute-start(bf16[128,1024]{1,0:T(8,128)(2,1)S(1)} %get-tuple-element.20), channel_id=1, source_target_pairs={{0,4},{1,5},{2,6},{3,7},{4,0},{5,1},{6,2},{7,3},{8,12},{9,13},{10,... | collective-permute-start | bytes 786440 | tf_op jit(solution)/shard_map/ppermute | solution.py:29
  18.0 4.3 %collective-permute-done = bf16[128,1024]{1,0:T(8,128)(2,1)S(1)} collective-permute-done((bf16[128,1024]{1,0:T(8,128)(2,1)S(1)}, bf16[128,1024]{1,0:T(8,128)(2,1)S(1)}, u32[]{:S(2)}, u32[]{:S(2)}) %collective-permute-start) | collective-permute-done | bytes 262176 | tf_op jit(solution)/shard_map/ppermute | solution.py:29
  23.9 1.1 pad_maximum_fusion
  25.0 2.3 %collective-permute-start.9 = (bf16[256,1024]{1,0:T(8,128)(2,1)S(1)}, bf16[256,1024]{1,0:T(8,128)(2,1)S(1)}, u32[]{:S(2)}, u32[]{:S(2)}) collective-permute-start(bf16[256,1024]{1,0:T(8,128)(2,1)S(1)} %maximum_select_fusion), channel_id=1, source_target_pairs={{0,3},{1,2},{2,1},{3,0},{4,7},{5,6},{6,5},{7,4},{8,11},{9,10},{10,... | collective-permute-start | bytes 1572872 | tf_op jit(solution)/shard_map/ppermute | solution.py:29
  27.4 18.2 %collective-permute-done.9 = bf16[256,1024]{1,0:T(8,128)(2,1)S(1)} collective-permute-done((bf16[256,1024]{1,0:T(8,128)(2,1)S(1)}, bf16[256,1024]{1,0:T(8,128)(2,1)S(1)}, u32[]{:S(2)}, u32[]{:S(2)}) %collective-permute-start.9) | collective-permute-done | bytes 524320 | tf_op jit(solution)/shard_map/ppermute | solution.py:29
  45.8 2.7 %collective-permute-start.8 = (bf16[128,1024]{1,0:T(8,128)(2,1)S(1)}, bf16[128,1024]{1,0:T(8,128)(2,1)S(1)}, u32[]{:S(2)}, u32[]{:S(2)}) collective-permute-start(bf16[128,1024]{1,0:T(8,128)(2,1)S(1)} %get-tuple-element.44.refs_2_), channel_id=1, source_target_pairs={{0,3},{1,2},{2,1},{3,0},{4,7},{5,6},{6,5},{7,4},{8,11},{9,10},{10,... | collective-permute-start | bytes 786440 | tf_op jit(solution)/shard_map/ppermute | solution.py:29
  48.6 1.5 collective-permute-start.4
  50.2 0.7 collective-permute-start.6
  50.9 1.3 collective-permute-done.4
  52.3 1.3 collective-permute-done.8.refs_4_
  53.5 0.7 shard_map.86
  54.9 0.7 collective-permute-start.11
  55.6 0.7 collective-permute-start.12
  56.2 0.7 fusion.26
  56.9 6.6 %collective-permute-start.13 = (bf16[16,1024]{1,0:T(8,128)(2,1)S(1)}, bf16[16,1024]{1,0:T(8,128)(2,1)S(1)}, u32[]{:S(2)}, u32[]{:S(2)}) collective-permute-start(bf16[16,1024]{1,0:T(8,128)(2,1)S(1)} %fusion.26), channel_id=1, source_target_pairs={{0,20},{1,21},{2,22},{3,23},{4,16},{5,17},{6,18},{7,19},{8,28},{9,... | collective-permute-start | bytes 98312 | tf_op jit(solution)/shard_map/ppermute | solution.py:29
  64.1 1.1 collective-permute-done.13
  65.8 0.7 collective-permute-start.15
  66.5 0.7 collective-permute-start.16
  67.2 0.7 fusion.28
  67.8 1.9 %collective-permute-start.17 = (bf16[16,1024]{1,0:T(8,128)(2,1)S(1)}, bf16[16,1024]{1,0:T(8,128)(2,1)S(1)}, u32[]{:S(2)}, u32[]{:S(2)}) collective-permute-start(bf16[16,1024]{1,0:T(8,128)(2,1)S(1)} %fusion.28), channel_id=1, source_target_pairs={{0,20},{1,21},{2,22},{3,23},{4,16},{5,17},{6,18},{7,19},{8,28},{9,... | collective-permute-start | bytes 98312 | tf_op jit(solution)/shard_map/ppermute | solution.py:29
  69.7 1.0 collective-permute-start.18
  70.6 1.1 collective-permute-done.17
  72.4 0.7 collective-permute-start.19
  73.1 0.7 collective-permute-start.20
  73.8 0.7 fusion.30
  74.4 2.3 %collective-permute-start.21 = (bf16[16,1024]{1,0:T(8,128)(2,1)S(1)}, bf16[16,1024]{1,0:T(8,128)(2,1)S(1)}, u32[]{:S(2)}, u32[]{:S(2)}) collective-permute-start(bf16[16,1024]{1,0:T(8,128)(2,1)S(1)} %fusion.30), channel_id=1, source_target_pairs={{0,20},{1,21},{2,22},{3,23},{4,16},{5,17},{6,18},{7,19},{8,28},{9,... | collective-permute-start | bytes 98312 | tf_op jit(solution)/shard_map/ppermute | solution.py:29
  77.2 1.5 collective-permute-done.21
  79.4 0.7 collective-permute-start.23
  80.0 0.7 collective-permute-start.24
  81.4 2.3 %collective-permute-start.25 = (bf16[16,1024]{1,0:T(8,128)(2,1)S(1)}, bf16[16,1024]{1,0:T(8,128)(2,1)S(1)}, u32[]{:S(2)}, u32[]{:S(2)}) collective-permute-start(bf16[16,1024]{1,0:T(8,128)(2,1)S(1)} %fusion.32), channel_id=1, source_target_pairs={{0,20},{1,21},{2,22},{3,23},{4,16},{5,17},{6,18},{7,19},{8,28},{9,... | collective-permute-start | bytes 98312 | tf_op jit(solution)/shard_map/ppermute | solution.py:29
  84.0 1.7 %collective-permute-done.25 = bf16[16,1024]{1,0:T(8,128)(2,1)S(1)} collective-permute-done((bf16[16,1024]{1,0:T(8,128)(2,1)S(1)}, bf16[16,1024]{1,0:T(8,128)(2,1)S(1)}, u32[]{:S(2)}, u32[]{:S(2)}) %collective-permute-start.25) | collective-permute-done | bytes 32800 | tf_op jit(solution)/shard_map/ppermute | solution.py:29
  86.3 0.7 collective-permute-start.27
  86.9 0.7 collective-permute-start.28
  87.7 4.3 %fusion.7 = bf16[512,512]{1,0:T(8,128)(2,1)} fusion(bf16[512,2048]{1,0:T(8,128)(2,1)} %bitcast.70, bf16[512,4096]{1,0:T(8,128)(2,1)} %all-gather.5.cloned.1.call-done), kind=kOutput, calls=%fused_computation.5 | convolution fusion | flops 1074003968 | bytes 4718592 | tf_op jit(solution)/shard_map/dot_general | solution.py:242
  92.7 1.4 collective-permute-start.29
  94.4 1.7 %collective-permute-done.29 = bf16[16,1024]{1,0:T(8,128)(2,1)S(1)} collective-permute-done((bf16[16,1024]{1,0:T(8,128)(2,1)S(1)}, bf16[16,1024]{1,0:T(8,128)(2,1)S(1)}, u32[]{:S(2)}, u32[]{:S(2)}) %collective-permute-start.29) | collective-permute-done | bytes 32800 | tf_op jit(solution)/shard_map/ppermute | solution.py:29
  96.7 0.7 collective-permute-start.31
  97.3 0.7 collective-permute-start.32
  98.7 1.4 collective-permute-start.33
  100.4 1.7 %collective-permute-done.33 = bf16[16,1024]{1,0:T(8,128)(2,1)S(1)} collective-permute-done((bf16[16,1024]{1,0:T(8,128)(2,1)S(1)}, bf16[16,1024]{1,0:T(8,128)(2,1)S(1)}, u32[]{:S(2)}, u32[]{:S(2)}) %collective-permute-start.33) | collective-permute-done | bytes 32800 | tf_op jit(solution)/shard_map/ppermute | solution.py:29
  102.7 0.7 collective-permute-start.35
  103.4 0.7 collective-permute-start.36
  104.7 1.4 collective-permute-start.37
  106.6 1.5 collective-permute-done.37
  108.1 0.7 fusion.40
  108.7 1.5 collective-permute-start.39
  110.2 2.4 %collective-permute-done.39 = bf16[16,1024]{1,0:T(8,128)(2,1)S(1)} collective-permute-done((bf16[16,1024]{1,0:T(8,128)(2,1)S(1)}, bf16[16,1024]{1,0:T(8,128)(2,1)S(1)}, u32[]{:S(2)}, u32[]{:S(2)}) %collective-permute-start.39) | collective-permute-done | bytes 32800 | tf_op jit(solution)/shard_map/ppermute | solution.py:29
  113.1 0.9 collective-permute-start.43
  114.0 15.4 %all-gather.7.cloned.1.call-done = bf16[2048,512]{1,0:T(8,128)(2,1)} async-done(((bf16[512,512]{1,0:T(8,128)(2,1)}), bf16[2048,512]{1,0:T(8,128)(2,1)}) %all-gather.7.cloned.1.call-update) | async-done | bytes 2097168 | tf_op jit(solution)/shard_map/all_gather | solution.py:133
  129.4 3.5 %fusion.4 = bf16[512,512]{1,0:T(8,128)(2,1)S(1)} fusion(bf16[2048,512]{1,0:T(8,128)(2,1)} %all-gather.7.cloned.1.call-done, bf16[512,4096]{1,0:T(8,128)(2,1)} %all-gather.5.cloned.1.call-done), kind=kOutput, calls=%fused_computation.4 | convolution fusion | flops 1074003968 | bytes 4718592 | tf_op jit(solution)/shard_map/dot_general | solution.py:265
  133.0 1.8 %collective-permute-start.40 = (bf16[128,512]{1,0:T(8,128)(2,1)S(1)}, bf16[128,512]{1,0:T(8,128)(2,1)S(1)}, u32[]{:S(2)}, u32[]{:S(2)}) collective-permute-start(bf16[128,512]{1,0:T(8,128)(2,1)S(1)} %get-tuple-element.39), channel_id=1, source_target_pairs={{0,1},{1,0},{2,3},{3,2},{4,5},{5,4},{6,7},{7,6},{8,9},{9,8},{10,11... | collective-permute-start | bytes 393224 | tf_op jit(solution)/shard_map/ppermute | solution.py:29
  134.8 3.5 %collective-permute-start.41 = (bf16[128,512]{1,0:T(8,128)(2,1)S(1)}, bf16[128,512]{1,0:T(8,128)(2,1)S(1)}, u32[]{:S(2)}, u32[]{:S(2)}) collective-permute-start(bf16[128,512]{1,0:T(8,128)(2,1)S(1)} %get-tuple-element.38), channel_id=1, source_target_pairs={{0,2},{1,3},{2,0},{3,1},{4,6},{5,7},{6,4},{7,5},{8,10},{9,11},{10,... | collective-permute-start | bytes 393224 | tf_op jit(solution)/shard_map/ppermute | solution.py:29
  138.6 4.7 %collective-permute-start.46 = (bf16[16,2432]{1,0:T(8,128)(2,1)S(1)}, bf16[16,2432]{1,0:T(8,128)(2,1)S(1)}, u32[]{:S(2)}, u32[]{:S(2)}) collective-permute-start(bf16[16,2432]{1,0:T(8,128)(2,1)S(1)} %get-tuple-element.49), channel_id=1, source_target_pairs={{0,2},{1,3},{2,0},{3,1},{4,6},{5,7},{6,4},{7,5},{8,10},{9,11},{10,... | collective-permute-start | bytes 233480 | tf_op jit(solution)/shard_map/ppermute | solution.py:29
  143.3 1.1 collective-permute-done.41.refs_3_
  144.5 3.0 %collective-permute-done.42.refs_4_ = bf16[128,512]{1,0:T(8,128)(2,1)S(1)} collective-permute-done((bf16[128,512]{1,0:T(8,128)(2,1)S(1)}, bf16[128,512]{1,0:T(8,128)(2,1)S(1)}, u32[]{:S(2)}, u32[]{:S(2)}) %collective-permute-start.42) | collective-permute-done | bytes 131104 | tf_op jit(solution)/shard_map/ppermute | solution.py:29
  147.4 1.8 %shard_map.87 = (f32[128,2048]{1,0:T(8,128)}, bf16[128,2048]{1,0:T(8,128)(2,1)S(1)}) custom-call(s32[3]{0:T(128)S(1)} %pad_add_fusion.place, f32[128,2048]{1,0:T(8,128)S(1)} %bitcast.57, bf16[128,512]{1,0:T(8,128)(2,1)S(1)} %get-tuple-element.40.refs_1_, bf16[128,512]{1,0:T(8,128)(2,1)S(1)} %collective-permute-done.40.refs_2_, ...), custom_call_target="tpu_custom_call" | custom-call | bytes 3145728 | tf_op jit(solution)/shard_map/pallas_call | solution.py:58
  149.2 1.5 shard_map.88
  (111 shorter events, 13.6 us)
Async XLA Ops:
  7.2 15.3 %copy-start.3 = (bf16[1,128,2048]{2,1,0:T(8,128)(2,1)S(1)}, bf16[1,128,2048]{2,1,0:T(8,128)(2,1)}, u32[]{:S(2)}) copy-start(bf16[1,128,2048]{2,1,0:T(8,128)(2,1)} %param.7) | copy-start | bytes 1572868
  7.2 80.5 %all-gather.9.cloned.1.call-start = ((), (), s32[]{:S(2)}) async-start(), calls=%async_computation.2 | async-start | bytes 2621440 | tf_op jit(solution)/shard_map/all_gather | solution.py:133
  7.9 79.8 %all-gather.5.cloned.1.call-start = ((), (), s32[]{:S(2)}) async-start(), calls=%async_computation | async-start | bytes 5242880 | tf_op jit(solution)/shard_map/all_gather | solution.py:133
  9.4 8.1 %collective-permute-start.1 = (f32[24,128]{1,0:T(8,128)S(1)}, f32[24,128]{1,0:T(8,128)S(1)}, u32[]{:S(2)}, u32[]{:S(2)}) collective-permute-start(f32[24,128]{1,0:T(8,128)S(1)} %get-tuple-element.78), channel_id=1, source_target_pairs={{0,1},{1,0},{2,3},{3,2},{4,5},{5,4},{6,7},{7,6},{8,9},{9,8},{10,11... | collective-permute-start | bytes 36872 | tf_op jit(solution)/shard_map/ppermute | solution.py:29
  10.3 7.3 %collective-permute-start.2 = (f32[24,128]{1,0:T(8,128)S(1)}, f32[24,128]{1,0:T(8,128)S(1)}, u32[]{:S(2)}, u32[]{:S(2)}) collective-permute-start(f32[24,128]{1,0:T(8,128)S(1)} %get-tuple-element.79), channel_id=1, source_target_pairs={{0,2},{1,3},{2,0},{3,1},{4,6},{5,7},{6,4},{7,5},{8,10},{9,11},{10,... | collective-permute-start | bytes 36872 | tf_op jit(solution)/shard_map/ppermute | solution.py:29
  13.1 4.9 %collective-permute-start.3 = (f32[24,128]{1,0:T(8,128)S(1)}, f32[24,128]{1,0:T(8,128)S(1)}, u32[]{:S(2)}, u32[]{:S(2)}) collective-permute-start(f32[24,128]{1,0:T(8,128)S(1)} %get-tuple-element.80), channel_id=1, source_target_pairs={{0,3},{1,2},{2,1},{3,0},{4,7},{5,6},{6,5},{7,4},{8,11},{9,10},{10,... | collective-permute-start | bytes 36872 | tf_op jit(solution)/shard_map/ppermute | solution.py:29
  14.2 1.0 copy-start.1
  15.8 6.5 %collective-permute-start = (bf16[128,1024]{1,0:T(8,128)(2,1)S(1)}, bf16[128,1024]{1,0:T(8,128)(2,1)S(1)}, u32[]{:S(2)}, u32[]{:S(2)}) collective-permute-start(bf16[128,1024]{1,0:T(8,128)(2,1)S(1)} %get-tuple-element.20), channel_id=1, source_target_pairs={{0,4},{1,5},{2,6},{3,7},{4,0},{5,1},{6,2},{7,3},{8,12},{9,13},{10,... | collective-permute-start | bytes 786440 | tf_op jit(solution)/shard_map/ppermute | solution.py:29
  22.8 1.0 copy-start.4
  24.9 104.4 %all-gather.7.cloned.1.call-start = ((), (), s32[]{:S(2)}) async-start(), calls=%async_computation.1 | async-start | bytes 2621440 | tf_op jit(solution)/shard_map/all_gather | solution.py:133
  25.0 20.6 %collective-permute-start.9 = (bf16[256,1024]{1,0:T(8,128)(2,1)S(1)}, bf16[256,1024]{1,0:T(8,128)(2,1)S(1)}, u32[]{:S(2)}, u32[]{:S(2)}) collective-permute-start(bf16[256,1024]{1,0:T(8,128)(2,1)S(1)} %maximum_select_fusion), channel_id=1, source_target_pairs={{0,3},{1,2},{2,1},{3,0},{4,7},{5,6},{6,5},{7,4},{8,11},{9,10},{10,... | collective-permute-start | bytes 1572872 | tf_op jit(solution)/shard_map/ppermute | solution.py:29
  27.3 18.4 %collective-permute-start.7 = (bf16[256,1024]{1,0:T(8,128)(2,1)S(1)}, bf16[256,1024]{1,0:T(8,128)(2,1)S(1)}, u32[]{:S(2)}, u32[]{:S(2)}) collective-permute-start(bf16[256,1024]{1,0:T(8,128)(2,1)S(1)} %maximum_select_fusion), channel_id=1, source_target_pairs={{0,1},{1,0},{2,3},{3,2},{4,5},{5,4},{6,7},{7,6},{8,9},{9,8},{10,11... | collective-permute-start | bytes 1572872 | tf_op jit(solution)/shard_map/ppermute | solution.py:29
  45.6 6.6 %collective-permute-start.10 = (bf16[128,1024]{1,0:T(8,128)(2,1)S(1)}, bf16[128,1024]{1,0:T(8,128)(2,1)S(1)}, u32[]{:S(2)}, u32[]{:S(2)}) collective-permute-start(bf16[128,1024]{1,0:T(8,128)(2,1)S(1)} %get-tuple-element.42.refs_7_), channel_id=1, source_target_pairs={{0,1},{1,0},{2,3},{3,2},{4,5},{5,4},{6,7},{7,6},{8,9},{9,8},{10,11... | collective-permute-start | bytes 786440 | tf_op jit(solution)/shard_map/ppermute | solution.py:29
  45.8 7.7 %collective-permute-start.8 = (bf16[128,1024]{1,0:T(8,128)(2,1)S(1)}, bf16[128,1024]{1,0:T(8,128)(2,1)S(1)}, u32[]{:S(2)}, u32[]{:S(2)}) collective-permute-start(bf16[128,1024]{1,0:T(8,128)(2,1)S(1)} %get-tuple-element.44.refs_2_), channel_id=1, source_target_pairs={{0,3},{1,2},{2,1},{3,0},{4,7},{5,6},{6,5},{7,4},{8,11},{9,10},{10,... | collective-permute-start | bytes 786440 | tf_op jit(solution)/shard_map/ppermute | solution.py:29
  48.6 3.7 %collective-permute-start.4 = (f32[1,512]{1,0:T(1,128)S(1)}, f32[1,512]{1,0:T(1,128)S(1)}, u32[]{:S(2)}, u32[]{:S(2)}) collective-permute-start(f32[1,512]{1,0:T(1,128)S(1)} %slice.57), channel_id=1, source_target_pairs={{0,4},{1,5},{2,6},{3,7},{4,0},{5,1},{6,2},{7,3},{8,12},{9,13},{10,... | collective-permute-start | bytes 6152 | tf_op jit(solution)/shard_map/ppermute | solution.py:29
  50.1 4.1 %collective-permute-start.5 = (bf16[16,1024]{1,0:T(8,128)(2,1)S(1)}, bf16[16,1024]{1,0:T(8,128)(2,1)S(1)}, u32[]{:S(2)}, u32[]{:S(2)}) collective-permute-start(bf16[16,1024]{1,0:T(8,128)(2,1)S(1)} %convert_element_type.216), channel_id=1, source_target_pairs={{0,20},{1,21},{2,22},{3,23},{4,16},{5,17},{6,18},{7,19},{8,28},{9,... | collective-permute-start | bytes 98312 | tf_op jit(solution)/shard_map/ppermute | solution.py:29
  50.2 4.0 %collective-permute-start.6 = (bf16[16,1024]{1,0:T(8,128)(2,1)S(1)}, bf16[16,1024]{1,0:T(8,128)(2,1)S(1)}, u32[]{:S(2)}, u32[]{:S(2)}) collective-permute-start(bf16[16,1024]{1,0:T(8,128)(2,1)S(1)} %convert_element_type.216), channel_id=1, source_target_pairs={{0,16},{1,17},{2,18},{3,19},{4,20},{5,21},{6,22},{7,23},{8,24},{9,... | collective-permute-start | bytes 98312 | tf_op jit(solution)/shard_map/ppermute | solution.py:29
  54.9 1.3 collective-permute-start.11
  55.6 0.7 collective-permute-start.12
  56.9 8.2 %collective-permute-start.13 = (bf16[16,1024]{1,0:T(8,128)(2,1)S(1)}, bf16[16,1024]{1,0:T(8,128)(2,1)S(1)}, u32[]{:S(2)}, u32[]{:S(2)}) collective-permute-start(bf16[16,1024]{1,0:T(8,128)(2,1)S(1)} %fusion.26), channel_id=1, source_target_pairs={{0,20},{1,21},{2,22},{3,23},{4,16},{5,17},{6,18},{7,19},{8,28},{9,... | collective-permute-start | bytes 98312 | tf_op jit(solution)/shard_map/ppermute | solution.py:29
  63.5 1.6 %collective-permute-start.14 = (bf16[16,1024]{1,0:T(8,128)(2,1)S(1)}, bf16[16,1024]{1,0:T(8,128)(2,1)S(1)}, u32[]{:S(2)}, u32[]{:S(2)}) collective-permute-start(bf16[16,1024]{1,0:T(8,128)(2,1)S(1)} %fusion.26), channel_id=1, source_target_pairs={{0,16},{1,17},{2,18},{3,19},{4,20},{5,21},{6,22},{7,23},{8,24},{9,... | collective-permute-start | bytes 98312 | tf_op jit(solution)/shard_map/ppermute | solution.py:29
  65.8 1.3 collective-permute-start.15
  66.5 0.7 collective-permute-start.16
  67.8 4.0 %collective-permute-start.17 = (bf16[16,1024]{1,0:T(8,128)(2,1)S(1)}, bf16[16,1024]{1,0:T(8,128)(2,1)S(1)}, u32[]{:S(2)}, u32[]{:S(2)}) collective-permute-start(bf16[16,1024]{1,0:T(8,128)(2,1)S(1)} %fusion.28), channel_id=1, source_target_pairs={{0,20},{1,21},{2,22},{3,23},{4,16},{5,17},{6,18},{7,19},{8,28},{9,... | collective-permute-start | bytes 98312 | tf_op jit(solution)/shard_map/ppermute | solution.py:29
  69.7 2.1 %collective-permute-start.18 = (bf16[16,1024]{1,0:T(8,128)(2,1)S(1)}, bf16[16,1024]{1,0:T(8,128)(2,1)S(1)}, u32[]{:S(2)}, u32[]{:S(2)}) collective-permute-start(bf16[16,1024]{1,0:T(8,128)(2,1)S(1)} %fusion.28), channel_id=1, source_target_pairs={{0,16},{1,17},{2,18},{3,19},{4,20},{5,21},{6,22},{7,23},{8,24},{9,... | collective-permute-start | bytes 98312 | tf_op jit(solution)/shard_map/ppermute | solution.py:29
  72.4 1.3 collective-permute-start.19
  73.1 0.7 collective-permute-start.20
  74.4 4.3 %collective-permute-start.21 = (bf16[16,1024]{1,0:T(8,128)(2,1)S(1)}, bf16[16,1024]{1,0:T(8,128)(2,1)S(1)}, u32[]{:S(2)}, u32[]{:S(2)}) collective-permute-start(bf16[16,1024]{1,0:T(8,128)(2,1)S(1)} %fusion.30), channel_id=1, source_target_pairs={{0,20},{1,21},{2,22},{3,23},{4,16},{5,17},{6,18},{7,19},{8,28},{9,... | collective-permute-start | bytes 98312 | tf_op jit(solution)/shard_map/ppermute | solution.py:29
  76.8 2.0 %collective-permute-start.22 = (bf16[16,1024]{1,0:T(8,128)(2,1)S(1)}, bf16[16,1024]{1,0:T(8,128)(2,1)S(1)}, u32[]{:S(2)}, u32[]{:S(2)}) collective-permute-start(bf16[16,1024]{1,0:T(8,128)(2,1)S(1)} %fusion.30), channel_id=1, source_target_pairs={{0,16},{1,17},{2,18},{3,19},{4,20},{5,21},{6,22},{7,23},{8,24},{9,... | collective-permute-start | bytes 98312 | tf_op jit(solution)/shard_map/ppermute | solution.py:29
  79.4 1.3 collective-permute-start.23
  80.0 0.7 collective-permute-start.24
  81.4 4.2 %collective-permute-start.25 = (bf16[16,1024]{1,0:T(8,128)(2,1)S(1)}, bf16[16,1024]{1,0:T(8,128)(2,1)S(1)}, u32[]{:S(2)}, u32[]{:S(2)}) collective-permute-start(bf16[16,1024]{1,0:T(8,128)(2,1)S(1)} %fusion.32), channel_id=1, source_target_pairs={{0,20},{1,21},{2,22},{3,23},{4,16},{5,17},{6,18},{7,19},{8,28},{9,... | collective-permute-start | bytes 98312 | tf_op jit(solution)/shard_map/ppermute | solution.py:29
  83.7 1.9 %collective-permute-start.26 = (bf16[16,1024]{1,0:T(8,128)(2,1)S(1)}, bf16[16,1024]{1,0:T(8,128)(2,1)S(1)}, u32[]{:S(2)}, u32[]{:S(2)}) collective-permute-start(bf16[16,1024]{1,0:T(8,128)(2,1)S(1)} %fusion.32), channel_id=1, source_target_pairs={{0,16},{1,17},{2,18},{3,19},{4,20},{5,21},{6,22},{7,23},{8,24},{9,... | collective-permute-start | bytes 98312 | tf_op jit(solution)/shard_map/ppermute | solution.py:29
  86.3 5.7 %collective-permute-start.27 = (bf16[16,1024]{1,0:T(8,128)(2,1)S(1)}, bf16[16,1024]{1,0:T(8,128)(2,1)S(1)}, u32[]{:S(2)}, u32[]{:S(2)}) collective-permute-start(bf16[16,1024]{1,0:T(8,128)(2,1)S(1)} %fusion.33), channel_id=1, source_target_pairs={{144,172},{145,173},{146,174},{147,175},{148,168},{149,169},{150,1... | collective-permute-start | bytes 98312 | tf_op jit(solution)/shard_map/ppermute | solution.py:29
  86.9 5.1 %collective-permute-start.28 = (bf16[16,1024]{1,0:T(8,128)(2,1)S(1)}, bf16[16,1024]{1,0:T(8,128)(2,1)S(1)}, u32[]{:S(2)}, u32[]{:S(2)}) collective-permute-start(bf16[16,1024]{1,0:T(8,128)(2,1)S(1)} %fusion.33), channel_id=1, source_target_pairs={{144,160},{145,161},{146,162},{147,163},{148,164},{149,165},{150,1... | collective-permute-start | bytes 98312 | tf_op jit(solution)/shard_map/ppermute | solution.py:29
  92.7 3.3 %collective-permute-start.29 = (bf16[16,1024]{1,0:T(8,128)(2,1)S(1)}, bf16[16,1024]{1,0:T(8,128)(2,1)S(1)}, u32[]{:S(2)}, u32[]{:S(2)}) collective-permute-start(bf16[16,1024]{1,0:T(8,128)(2,1)S(1)} %fusion.34), channel_id=1, source_target_pairs={{0,20},{1,21},{2,22},{3,23},{4,16},{5,17},{6,18},{7,19},{8,28},{9,... | collective-permute-start | bytes 98312 | tf_op jit(solution)/shard_map/ppermute | solution.py:29
  94.1 1.9 %collective-permute-start.30 = (bf16[16,1024]{1,0:T(8,128)(2,1)S(1)}, bf16[16,1024]{1,0:T(8,128)(2,1)S(1)}, u32[]{:S(2)}, u32[]{:S(2)}) collective-permute-start(bf16[16,1024]{1,0:T(8,128)(2,1)S(1)} %fusion.34), channel_id=1, source_target_pairs={{0,16},{1,17},{2,18},{3,19},{4,20},{5,21},{6,22},{7,23},{8,24},{9,... | collective-permute-start | bytes 98312 | tf_op jit(solution)/shard_map/ppermute | solution.py:29
  96.7 1.3 collective-permute-start.31
  97.3 0.7 collective-permute-start.32
  98.7 3.4 %collective-permute-start.33 = (bf16[16,1024]{1,0:T(8,128)(2,1)S(1)}, bf16[16,1024]{1,0:T(8,128)(2,1)S(1)}, u32[]{:S(2)}, u32[]{:S(2)}) collective-permute-start(bf16[16,1024]{1,0:T(8,128)(2,1)S(1)} %fusion.36), channel_id=1, source_target_pairs={{0,20},{1,21},{2,22},{3,23},{4,16},{5,17},{6,18},{7,19},{8,28},{9,... | collective-permute-start | bytes 98312 | tf_op jit(solution)/shard_map/ppermute | solution.py:29
  100.1 1.9 %collective-permute-start.34 = (bf16[16,1024]{1,0:T(8,128)(2,1)S(1)}, bf16[16,1024]{1,0:T(8,128)(2,1)S(1)}, u32[]{:S(2)}, u32[]{:S(2)}) collective-permute-start(bf16[16,1024]{1,0:T(8,128)(2,1)S(1)} %fusion.36), channel_id=1, source_target_pairs={{0,16},{1,17},{2,18},{3,19},{4,20},{5,21},{6,22},{7,23},{8,24},{9,... | collective-permute-start | bytes 98312 | tf_op jit(solution)/shard_map/ppermute | solution.py:29
  102.7 1.3 collective-permute-start.35
  103.4 0.7 collective-permute-start.36
  104.7 3.4 %collective-permute-start.37 = (bf16[16,1024]{1,0:T(8,128)(2,1)S(1)}, bf16[16,1024]{1,0:T(8,128)(2,1)S(1)}, u32[]{:S(2)}, u32[]{:S(2)}) collective-permute-start(bf16[16,1024]{1,0:T(8,128)(2,1)S(1)} %fusion.38), channel_id=1, source_target_pairs={{0,20},{1,21},{2,22},{3,23},{4,16},{5,17},{6,18},{7,19},{8,28},{9,... | collective-permute-start | bytes 98312 | tf_op jit(solution)/shard_map/ppermute | solution.py:29
  106.1 1.9 %collective-permute-start.38 = (bf16[16,1024]{1,0:T(8,128)(2,1)S(1)}, bf16[16,1024]{1,0:T(8,128)(2,1)S(1)}, u32[]{:S(2)}, u32[]{:S(2)}) collective-permute-start(bf16[16,1024]{1,0:T(8,128)(2,1)S(1)} %fusion.38), channel_id=1, source_target_pairs={{0,16},{1,17},{2,18},{3,19},{4,20},{5,21},{6,22},{7,23},{8,24},{9,... | collective-permute-start | bytes 98312 | tf_op jit(solution)/shard_map/ppermute | solution.py:29
  108.7 3.9 %collective-permute-start.39 = (bf16[16,1024]{1,0:T(8,128)(2,1)S(1)}, bf16[16,1024]{1,0:T(8,128)(2,1)S(1)}, u32[]{:S(2)}, u32[]{:S(2)}) collective-permute-start(bf16[16,1024]{1,0:T(8,128)(2,1)S(1)} %fusion.40), channel_id=1, source_target_pairs={{0,4},{1,5},{2,6},{3,7},{4,0},{5,1},{6,2},{7,3},{8,12},{9,13},{10,... | collective-permute-start | bytes 98312 | tf_op jit(solution)/shard_map/ppermute | solution.py:29
  113.1 19.8 %collective-permute-start.43 = (bf16[16,1536]{1,0:T(8,128)(2,1)S(1)}, bf16[16,1536]{1,0:T(8,128)(2,1)S(1)}, u32[]{:S(2)}, u32[]{:S(2)}) collective-permute-start(bf16[16,1536]{1,0:T(8,128)(2,1)S(1)} %pad_maximum_fusion.7), channel_id=1, source_target_pairs={{0,12},{1,13},{2,14},{3,15},{4,8},{5,9},{6,10},{7,11},{8,4},{9,5},... | collective-permute-start | bytes 147464 | tf_op jit(solution)/shard_map/ppermute | solution.py:29
  132.8 14.6 %copy-start = (f32[1,128,2048]{2,1,0:T(8,128)S(1)}, f32[1,128,2048]{2,1,0:T(8,128)}, u32[]{:S(2)}) copy-start(f32[1,128,2048]{2,1,0:T(8,128)} %param.8) | copy-start | bytes 3145732
  132.9 16.3 %copy-start.2 = (f32[1,128]{1,0:T(1,128)S(1)}, f32[1,128]{1,0:T(1,128)}, u32[]{:S(2)}) copy-start(f32[1,128]{1,0:T(1,128)} %weight.1) | copy-start | bytes 1540
  132.9 5.5 %collective-permute-start.44 = (bf16[16,512]{1,0:T(8,128)(2,1)S(1)}, bf16[16,512]{1,0:T(8,128)(2,1)S(1)}, u32[]{:S(2)}, u32[]{:S(2)}) collective-permute-start(bf16[16,512]{1,0:T(8,128)(2,1)S(1)} %add_convert_fusion.30), channel_id=1, source_target_pairs={{0,240},{1,241},{2,242},{3,243},{4,244},{5,245},{6,246},{7,247},{8... | collective-permute-start | bytes 49160 | tf_op jit(solution)/shard_map/ppermute | solution.py:29
  133.0 10.2 %collective-permute-start.40 = (bf16[128,512]{1,0:T(8,128)(2,1)S(1)}, bf16[128,512]{1,0:T(8,128)(2,1)S(1)}, u32[]{:S(2)}, u32[]{:S(2)}) collective-permute-start(bf16[128,512]{1,0:T(8,128)(2,1)S(1)} %get-tuple-element.39), channel_id=1, source_target_pairs={{0,1},{1,0},{2,3},{3,2},{4,5},{5,4},{6,7},{7,6},{8,9},{9,8},{10,11... | collective-permute-start | bytes 393224 | tf_op jit(solution)/shard_map/ppermute | solution.py:29
  134.8 9.7 %collective-permute-start.41 = (bf16[128,512]{1,0:T(8,128)(2,1)S(1)}, bf16[128,512]{1,0:T(8,128)(2,1)S(1)}, u32[]{:S(2)}, u32[]{:S(2)}) collective-permute-start(bf16[128,512]{1,0:T(8,128)(2,1)S(1)} %get-tuple-element.38), channel_id=1, source_target_pairs={{0,2},{1,3},{2,0},{3,1},{4,6},{5,7},{6,4},{7,5},{8,10},{9,11},{10,... | collective-permute-start | bytes 393224 | tf_op jit(solution)/shard_map/ppermute | solution.py:29
  138.3 9.1 %collective-permute-start.42 = (bf16[128,512]{1,0:T(8,128)(2,1)S(1)}, bf16[128,512]{1,0:T(8,128)(2,1)S(1)}, u32[]{:S(2)}, u32[]{:S(2)}) collective-permute-start(bf16[128,512]{1,0:T(8,128)(2,1)S(1)} %get-tuple-element.37), channel_id=1, source_target_pairs={{0,3},{1,2},{2,1},{3,0},{4,7},{5,6},{6,5},{7,4},{8,11},{9,10},{10,... | collective-permute-start | bytes 393224 | tf_op jit(solution)/shard_map/ppermute | solution.py:29
  138.5 10.7 %collective-permute-start.45 = (bf16[16,2432]{1,0:T(8,128)(2,1)S(1)}, bf16[16,2432]{1,0:T(8,128)(2,1)S(1)}, u32[]{:S(2)}, u32[]{:S(2)}) collective-permute-start(bf16[16,2432]{1,0:T(8,128)(2,1)S(1)} %get-tuple-element.48), channel_id=1, source_target_pairs={{0,1},{1,0},{2,3},{3,2},{4,5},{5,4},{6,7},{7,6},{8,9},{9,8},{10,11... | collective-permute-start | bytes 233480 | tf_op jit(solution)/shard_map/ppermute | solution.py:29
  138.6 10.6 %collective-permute-start.46 = (bf16[16,2432]{1,0:T(8,128)(2,1)S(1)}, bf16[16,2432]{1,0:T(8,128)(2,1)S(1)}, u32[]{:S(2)}, u32[]{:S(2)}) collective-permute-start(bf16[16,2432]{1,0:T(8,128)(2,1)S(1)} %get-tuple-element.49), channel_id=1, source_target_pairs={{0,2},{1,3},{2,0},{3,1},{4,6},{5,7},{6,4},{7,5},{8,10},{9,11},{10,... | collective-permute-start | bytes 233480 | tf_op jit(solution)/shard_map/ppermute | solution.py:29
  143.2 5.9 %collective-permute-start.47 = (bf16[16,2432]{1,0:T(8,128)(2,1)S(1)}, bf16[16,2432]{1,0:T(8,128)(2,1)S(1)}, u32[]{:S(2)}, u32[]{:S(2)}) collective-permute-start(bf16[16,2432]{1,0:T(8,128)(2,1)S(1)} %get-tuple-element.47), channel_id=1, source_target_pairs={{0,3},{1,2},{2,1},{3,0},{4,7},{5,6},{6,5},{7,4},{8,11},{9,10},{10,... | collective-permute-start | bytes 233480 | tf_op jit(solution)/shard_map/ppermute | solution.py:29
Sparse Core Ops, SparseCore 0:
  9.8 30.3 all-gather.8
  42.6 42.5 all-gather.4
  92.1 37.2 all-gather.6

commit v18 on v17

--- a/solution.py
+++ b/solution.py
@@ -198,14 +198,14 @@
     two = jnp.where(
         out_place == 0, jnp.concatenate([keep, got]), jnp.concatenate([got, keep])
     )
-    coupling_late = tie(coupling_rows, two)
+    left, right = along_x(two, 1), along_x(two, 3)
+    coupling_late = tie(coupling_rows, right)
     turned = jnp.where(
         even,
         coupling_late,
         coupling_late.reshape(rows, SIDE, SIDE, rows).transpose(0, 2, 1, 3).reshape(rows, nodes),
     )
     outer = gathered(jnp.concatenate([inverse_rows, turned], axis=1), True)
-    left, right = along_x(two, 1), along_x(two, 3)
     pieces = [
         two[:rows],
         two[rows:],

time: 158 us -> 171 us (1.082)
  the two profiles are of different devices: /device:TPU:6 before, /device:TPU:224 now
where the time goes in v18:
time: 171 us; the launch traced here: 168 us
  waiting for transfers between devices  81.7 us (48%)
  starting transfers between devices  43.9 us (26%)
  matrix products  17.9 us (10%)
  between operations  14.4 us (8%)
  Pallas kernels  4.48 us (3%)
  local copies, waits for them, and re-layouts  3.25 us (2%)
  other arithmetic  2.4 us (1%)
    ppermute x48, waiting for transfers between devices, permuted(): return lax.ppermute(value, AXES, pairs)  80.9 us
    ppermute x48, starting transfers between devices, permuted(): return lax.ppermute(value, AXES, pairs)  43.8 us
    dot_general x15, matrix products, shards(): lax.dot_general(previous, block, (((1,), (1,)), ((), ())), preferred_elem...  9.78 us
    pallas_call x4, Pallas kernels, kernel_call(): pl.pallas_call(body, out_shape=out_shapes, in_specs=[pl.BlockSpec(memory_...  4.48 us
    dot_general x1, matrix products, shards(): lax.dot_general(outer[:, :nodes], coupling_in, (((1,), (1,)), ((), ())),...  4.3 us
    dot_general x1, matrix products, shards(): jnp.dot(outer[:, nodes:], inner_all, preferred_element_type=f32)  3.47 us
  transfers between devices with their start and end apart: 51, of which 19 were waited for; matrix products, arithmetic and copies ran while one was open for 13% of the time, Pallas kernels for 2%

profile of v18, /device:TPU:224, one launch (start us, length us, event | category | flops | bytes accessed | tf_op | source)
XLA Modules:
  0.0 168.0 jit_solution(11558535774850949070)
XLA Ops:
  7.2 0.7 all-gather.9.cloned.1.call-update
  8.0 0.8 bitcast_multiply_fusion
  8.8 0.7 broadcast_in_dim.10
  9.4 1.5 collective-permute-start.1
  10.9 2.7 %collective-permute-start.2 = (f32[24,128]{1,0:T(8,128)S(1)}, f32[24,128]{1,0:T(8,128)S(1)}, u32[]{:S(2)}, u32[]{:S(2)}) collective-permute-start(f32[24,128]{1,0:T(8,128)S(1)} %get-tuple-element.79), channel_id=1, source_target_pairs={{0,2},{1,3},{2,0},{3,1},{4,6},{5,7},{6,4},{7,5},{8,10},{9,11},{10,... | collective-permute-start | bytes 36872 | tf_op jit(solution)/shard_map/ppermute | solution.py:29
  14.2 1.0 copy-done.1
  15.8 1.7 collective-permute-start
  17.5 1.0 collective-permute-done.3
  18.6 3.7 %collective-permute-done = bf16[128,1024]{1,0:T(8,128)(2,1)S(1)} collective-permute-done((bf16[128,1024]{1,0:T(8,128)(2,1)S(1)}, bf16[128,1024]{1,0:T(8,128)(2,1)S(1)}, u32[]{:S(2)}, u32[]{:S(2)}) %collective-permute-start) | collective-permute-done | bytes 262176 | tf_op jit(solution)/shard_map/ppermute | solution.py:29
  22.4 2.8 %collective-permute-start.4 = (bf16[256,1024]{1,0:T(8,128)(2,1)S(1)}, bf16[256,1024]{1,0:T(8,128)(2,1)S(1)}, u32[]{:S(2)}, u32[]{:S(2)}) collective-permute-start(bf16[256,1024]{1,0:T(8,128)(2,1)S(1)} %maximum_select_fusion), channel_id=1, source_target_pairs={{0,3},{1,2},{2,1},{3,0},{4,7},{5,6},{6,5},{7,4},{8,11},{9,10},{10,... | collective-permute-start | bytes 1572872 | tf_op jit(solution)/shard_map/ppermute | solution.py:29
  25.3 17.3 %collective-permute-done.4 = bf16[256,1024]{1,0:T(8,128)(2,1)S(1)} collective-permute-done((bf16[256,1024]{1,0:T(8,128)(2,1)S(1)}, bf16[256,1024]{1,0:T(8,128)(2,1)S(1)}, u32[]{:S(2)}, u32[]{:S(2)}) %collective-permute-start.4) | collective-permute-done | bytes 524320 | tf_op jit(solution)/shard_map/ppermute | solution.py:29
  44.0 1.1 pad_maximum_fusion
  45.4 2.1 %collective-permute-start.10 = (bf16[128,1024]{1,0:T(8,128)(2,1)S(1)}, bf16[128,1024]{1,0:T(8,128)(2,1)S(1)}, u32[]{:S(2)}, u32[]{:S(2)}) collective-permute-start(bf16[128,1024]{1,0:T(8,128)(2,1)S(1)} %get-tuple-element.42.refs_7_), channel_id=1, source_target_pairs={{0,1},{1,0},{2,3},{3,2},{4,5},{5,4},{6,7},{7,6},{8,9},{9,8},{10,11... | collective-permute-start | bytes 786440 | tf_op jit(solution)/shard_map/ppermute | solution.py:29
  47.5 12.2 %collective-permute-done.8 = bf16[256,1024]{1,0:T(8,128)(2,1)S(1)} collective-permute-done((bf16[256,1024]{1,0:T(8,128)(2,1)S(1)}, bf16[256,1024]{1,0:T(8,128)(2,1)S(1)}, u32[]{:S(2)}, u32[]{:S(2)}) %collective-permute-start.8) | collective-permute-done | bytes 524320 | tf_op jit(solution)/shard_map/ppermute | solution.py:29
  59.7 3.8 %collective-permute-start.9 = (bf16[128,1024]{1,0:T(8,128)(2,1)S(1)}, bf16[128,1024]{1,0:T(8,128)(2,1)S(1)}, u32[]{:S(2)}, u32[]{:S(2)}) collective-permute-start(bf16[128,1024]{1,0:T(8,128)(2,1)S(1)} %get-tuple-element.44.refs_2_), channel_id=1, source_target_pairs={{0,3},{1,2},{2,1},{3,0},{4,7},{5,6},{6,5},{7,4},{8,11},{9,10},{10,... | collective-permute-start | bytes 786440 | tf_op jit(solution)/shard_map/ppermute | solution.py:29
  64.0 1.9 %collective-permute-start.7 = (bf16[16,1024]{1,0:T(8,128)(2,1)S(1)}, bf16[16,1024]{1,0:T(8,128)(2,1)S(1)}, u32[]{:S(2)}, u32[]{:S(2)}) collective-permute-start(bf16[16,1024]{1,0:T(8,128)(2,1)S(1)} %convert_element_type.216), channel_id=1, source_target_pairs={{0,16},{1,17},{2,18},{3,19},{4,20},{5,21},{6,22},{7,23},{8,24},{9,... | collective-permute-start | bytes 98312 | tf_op jit(solution)/shard_map/ppermute | solution.py:29
  65.9 1.4 collective-permute-done.5
  67.2 3.3 %collective-permute-done.9.refs_4_ = bf16[128,1024]{1,0:T(8,128)(2,1)S(1)} collective-permute-done((bf16[128,1024]{1,0:T(8,128)(2,1)S(1)}, bf16[128,1024]{1,0:T(8,128)(2,1)S(1)}, u32[]{:S(2)}, u32[]{:S(2)}) %collective-permute-start.9) | collective-permute-done | bytes 262176 | tf_op jit(solution)/shard_map/ppermute | solution.py:29
  70.5 0.7 shard_map.86
  71.9 0.7 collective-permute-start.11
  72.5 0.7 collective-permute-start.12
  73.2 0.7 fusion.26
  74.0 3.6 %collective-permute-done.13 = bf16[16,1024]{1,0:T(8,128)(2,1)S(1)} collective-permute-done((bf16[16,1024]{1,0:T(8,128)(2,1)S(1)}, bf16[16,1024]{1,0:T(8,128)(2,1)S(1)}, u32[]{:S(2)}, u32[]{:S(2)}) %collective-permute-start.13) | collective-permute-done | bytes 32800 | tf_op jit(solution)/shard_map/ppermute | solution.py:29
  78.2 0.7 collective-permute-start.15
  78.9 0.7 collective-permute-start.16
  79.6 0.7 fusion.28
  80.7 2.9 %collective-permute-done.17 = bf16[16,1024]{1,0:T(8,128)(2,1)S(1)} collective-permute-done((bf16[16,1024]{1,0:T(8,128)(2,1)S(1)}, bf16[16,1024]{1,0:T(8,128)(2,1)S(1)}, u32[]{:S(2)}, u32[]{:S(2)}) %collective-permute-start.17) | collective-permute-done | bytes 32800 | tf_op jit(solution)/shard_map/ppermute | solution.py:29
  83.6 0.7 fusion.29
  84.2 0.7 collective-permute-start.19
  84.9 0.7 collective-permute-start.20
  85.6 0.7 fusion.30
  86.2 0.9 collective-permute-start.21
  87.1 2.5 %collective-permute-done.21 = bf16[16,1024]{1,0:T(8,128)(2,1)S(1)} collective-permute-done((bf16[16,1024]{1,0:T(8,128)(2,1)S(1)}, bf16[16,1024]{1,0:T(8,128)(2,1)S(1)}, u32[]{:S(2)}, u32[]{:S(2)}) %collective-permute-start.21) | collective-permute-done | bytes 32800 | tf_op jit(solution)/shard_map/ppermute | solution.py:29
  90.2 0.7 collective-permute-start.23
  90.9 0.7 collective-permute-start.24
  91.6 0.7 fusion.32
  92.3 0.9 collective-permute-start.25
  93.1 2.5 %collective-permute-done.25 = bf16[16,1024]{1,0:T(8,128)(2,1)S(1)} collective-permute-done((bf16[16,1024]{1,0:T(8,128)(2,1)S(1)}, bf16[16,1024]{1,0:T(8,128)(2,1)S(1)}, u32[]{:S(2)}, u32[]{:S(2)}) %collective-permute-start.25) | collective-permute-done | bytes 32800 | tf_op jit(solution)/shard_map/ppermute | solution.py:29
  96.3 0.7 collective-permute-start.27
  96.9 0.7 collective-permute-start.28
  97.7 4.3 %fusion.7 = bf16[512,512]{1,0:T(8,128)(2,1)} fusion(bf16[512,2048]{1,0:T(8,128)(2,1)} %bitcast.70, bf16[512,4096]{1,0:T(8,128)(2,1)} %all-gather.5.cloned.1.call-done), kind=kOutput, calls=%fused_computation.5 | convolution fusion | flops 1074003968 | bytes 4718592 | tf_op jit(solution)/shard_map/dot_general | solution.py:242
  102.7 0.9 collective-permute-start.29
  103.5 2.5 %collective-permute-done.29 = bf16[16,1024]{1,0:T(8,128)(2,1)S(1)} collective-permute-done((bf16[16,1024]{1,0:T(8,128)(2,1)S(1)}, bf16[16,1024]{1,0:T(8,128)(2,1)S(1)}, u32[]{:S(2)}, u32[]{:S(2)}) %collective-permute-start.29) | collective-permute-done | bytes 32800 | tf_op jit(solution)/shard_map/ppermute | solution.py:29
  106.7 0.7 collective-permute-start.31
  107.3 0.7 collective-permute-start.32
  108.7 0.9 collective-permute-start.33
  109.6 2.5 %collective-permute-done.33 = bf16[16,1024]{1,0:T(8,128)(2,1)S(1)} collective-permute-done((bf16[16,1024]{1,0:T(8,128)(2,1)S(1)}, bf16[16,1024]{1,0:T(8,128)(2,1)S(1)}, u32[]{:S(2)}, u32[]{:S(2)}) %collective-permute-start.33) | collective-permute-done | bytes 32800 | tf_op jit(solution)/shard_map/ppermute | solution.py:29
  112.7 1.3 collective-permute-start.35
  114.0 1.3 collective-permute-start.36
  115.3 14.1 %collective-permute-done.35 = bf16[16,1024]{1,0:T(8,128)(2,1)S(1)} collective-permute-done((bf16[16,1024]{1,0:T(8,128)(2,1)S(1)}, bf16[16,1024]{1,0:T(8,128)(2,1)S(1)}, u32[]{:S(2)}, u32[]{:S(2)}) %collective-permute-start.35) | collective-permute-done | bytes 32800 | tf_op jit(solution)/shard_map/ppermute | solution.py:29
  129.8 0.7 fusion.38
  130.8 3.2 %collective-permute-done.37 = bf16[16,1024]{1,0:T(8,128)(2,1)S(1)} collective-permute-done((bf16[16,1024]{1,0:T(8,128)(2,1)S(1)}, bf16[16,1024]{1,0:T(8,128)(2,1)S(1)}, u32[]{:S(2)}, u32[]{:S(2)}) %collective-permute-start.37) | collective-permute-done | bytes 32800 | tf_op jit(solution)/shard_map/ppermute | solution.py:29
  133.9 0.7 fusion.40
  134.7 4.0 %collective-permute-done.39 = bf16[16,1024]{1,0:T(8,128)(2,1)S(1)} collective-permute-done((bf16[16,1024]{1,0:T(8,128)(2,1)S(1)}, bf16[16,1024]{1,0:T(8,128)(2,1)S(1)}, u32[]{:S(2)}, u32[]{:S(2)}) %collective-permute-start.39) | collective-permute-done | bytes 32800 | tf_op jit(solution)/shard_map/ppermute | solution.py:29
  139.1 1.7 %collective-permute-start.43 = (bf16[16,1536]{1,0:T(8,128)(2,1)S(1)}, bf16[16,1536]{1,0:T(8,128)(2,1)S(1)}, u32[]{:S(2)}, u32[]{:S(2)}) collective-permute-start(bf16[16,1536]{1,0:T(8,128)(2,1)S(1)} %pad_maximum_fusion.7), channel_id=1, source_target_pairs={{0,12},{1,13},{2,14},{3,15},{4,8},{5,9},{6,10},{7,11},{8,4},{9,5},... | collective-permute-start | bytes 147464 | tf_op jit(solution)/shard_map/ppermute | solution.py:29
  140.9 3.5 %fusion.4 = bf16[512,512]{1,0:T(8,128)(2,1)S(1)} fusion(bf16[2048,512]{1,0:T(8,128)(2,1)} %all-gather.7.cloned.1.call-done, bf16[512,4096]{1,0:T(8,128)(2,1)} %all-gather.5.cloned.1.call-done), kind=kOutput, calls=%fused_computation.4 | convolution fusion | flops 1074003968 | bytes 4718592 | tf_op jit(solution)/shard_map/dot_general | solution.py:265
  144.6 2.0 %collective-permute-start.40 = (bf16[128,512]{1,0:T(8,128)(2,1)S(1)}, bf16[128,512]{1,0:T(8,128)(2,1)S(1)}, u32[]{:S(2)}, u32[]{:S(2)}) collective-permute-start(bf16[128,512]{1,0:T(8,128)(2,1)S(1)} %get-tuple-element.39), channel_id=1, source_target_pairs={{0,1},{1,0},{2,3},{3,2},{4,5},{5,4},{6,7},{7,6},{8,9},{9,8},{10,11... | collective-permute-start | bytes 393224 | tf_op jit(solution)/shard_map/ppermute | solution.py:29
  146.6 2.9 %collective-permute-start.41 = (bf16[128,512]{1,0:T(8,128)(2,1)S(1)}, bf16[128,512]{1,0:T(8,128)(2,1)S(1)}, u32[]{:S(2)}, u32[]{:S(2)}) collective-permute-start(bf16[128,512]{1,0:T(8,128)(2,1)S(1)} %get-tuple-element.38), channel_id=1, source_target_pairs={{0,2},{1,3},{2,0},{3,1},{4,6},{5,7},{6,4},{7,5},{8,10},{9,11},{10,... | collective-permute-start | bytes 393224 | tf_op jit(solution)/shard_map/ppermute | solution.py:29
  149.7 0.7 collective-permute-start.45
  150.3 4.1 %collective-permute-start.46 = (bf16[16,2432]{1,0:T(8,128)(2,1)S(1)}, bf16[16,2432]{1,0:T(8,128)(2,1)S(1)}, u32[]{:S(2)}, u32[]{:S(2)}) collective-permute-start(bf16[16,2432]{1,0:T(8,128)(2,1)S(1)} %get-tuple-element.49), channel_id=1, source_target_pairs={{0,2},{1,3},{2,0},{3,1},{4,6},{5,7},{6,4},{7,5},{8,10},{9,11},{10,... | collective-permute-start | bytes 233480 | tf_op jit(solution)/shard_map/ppermute | solution.py:29
  154.5 2.0 %collective-permute-done.42.refs_4_ = bf16[128,512]{1,0:T(8,128)(2,1)S(1)} collective-permute-done((bf16[128,512]{1,0:T(8,128)(2,1)S(1)}, bf16[128,512]{1,0:T(8,128)(2,1)S(1)}, u32[]{:S(2)}, u32[]{:S(2)}) %collective-permute-start.42) | collective-permute-done | bytes 131104 | tf_op jit(solution)/shard_map/ppermute | solution.py:29
  156.5 1.8 %shard_map.87 = (f32[128,2048]{1,0:T(8,128)}, bf16[128,2048]{1,0:T(8,128)(2,1)S(1)}) custom-call(s32[3]{0:T(128)S(1)} %pad_add_fusion.place, f32[128,2048]{1,0:T(8,128)S(1)} %bitcast.57, bf16[128,512]{1,0:T(8,128)(2,1)S(1)} %get-tuple-element.40.refs_1_, bf16[128,512]{1,0:T(8,128)(2,1)S(1)} %collective-permute-done.40.refs_2_, ...), custom_call_target="tpu_custom_call" | custom-call | bytes 3145728 | tf_op jit(solution)/shard_map/pallas_call | solution.py:58
  158.2 1.8 %collective-permute-done.47.refs_3_ = bf16[16,2432]{1,0:T(8,128)(2,1)S(1)} collective-permute-done((bf16[16,2432]{1,0:T(8,128)(2,1)S(1)}, bf16[16,2432]{1,0:T(8,128)(2,1)S(1)}, u32[]{:S(2)}, u32[]{:S(2)}) %collective-permute-start.47) | collective-permute-done | bytes 77856 | tf_op jit(solution)/shard_map/ppermute | solution.py:29
  160.1 1.5 shard_map.88
  (111 shorter events, 11.0 us)
Async XLA Ops:
  7.2 35.5 %copy-start.3 = (bf16[1,128,2048]{2,1,0:T(8,128)(2,1)S(1)}, bf16[1,128,2048]{2,1,0:T(8,128)(2,1)}, u32[]{:S(2)}) copy-start(bf16[1,128,2048]{2,1,0:T(8,128)(2,1)} %param.7) | copy-start | bytes 1572868
  7.2 90.5 %all-gather.9.cloned.1.call-start = ((), (), s32[]{:S(2)}) async-start(), calls=%async_computation.2 | async-start | bytes 2621440 | tf_op jit(solution)/shard_map/all_gather | solution.py:133
  7.9 89.8 %all-gather.5.cloned.1.call-start = ((), (), s32[]{:S(2)}) async-start(), calls=%async_computation | async-start | bytes 5242880 | tf_op jit(solution)/shard_map/all_gather | solution.py:133
  9.4 8.1 %collective-permute-start.1 = (f32[24,128]{1,0:T(8,128)S(1)}, f32[24,128]{1,0:T(8,128)S(1)}, u32[]{:S(2)}, u32[]{:S(2)}) collective-permute-start(f32[24,128]{1,0:T(8,128)S(1)} %get-tuple-element.78), channel_id=1, source_target_pairs={{0,1},{1,0},{2,3},{3,2},{4,5},{5,4},{6,7},{7,6},{8,9},{9,8},{10,11... | collective-permute-start | bytes 36872 | tf_op jit(solution)/shard_map/ppermute | solution.py:29
  10.9 6.6 %collective-permute-start.2 = (f32[24,128]{1,0:T(8,128)S(1)}, f32[24,128]{1,0:T(8,128)S(1)}, u32[]{:S(2)}, u32[]{:S(2)}) collective-permute-start(f32[24,128]{1,0:T(8,128)S(1)} %get-tuple-element.79), channel_id=1, source_target_pairs={{0,2},{1,3},{2,0},{3,1},{4,6},{5,7},{6,4},{7,5},{8,10},{9,11},{10,... | collective-permute-start | bytes 36872 | tf_op jit(solution)/shard_map/ppermute | solution.py:29
  13.6 4.9 %collective-permute-start.3 = (f32[24,128]{1,0:T(8,128)S(1)}, f32[24,128]{1,0:T(8,128)S(1)}, u32[]{:S(2)}, u32[]{:S(2)}) collective-permute-start(f32[24,128]{1,0:T(8,128)S(1)} %get-tuple-element.80), channel_id=1, source_target_pairs={{0,3},{1,2},{2,1},{3,0},{4,7},{5,6},{6,5},{7,4},{8,11},{9,10},{10,... | collective-permute-start | bytes 36872 | tf_op jit(solution)/shard_map/ppermute | solution.py:29
  14.2 1.0 copy-start.1
  15.8 6.5 %collective-permute-start = (bf16[128,1024]{1,0:T(8,128)(2,1)S(1)}, bf16[128,1024]{1,0:T(8,128)(2,1)S(1)}, u32[]{:S(2)}, u32[]{:S(2)}) collective-permute-start(bf16[128,1024]{1,0:T(8,128)(2,1)S(1)} %get-tuple-element.20), channel_id=1, source_target_pairs={{0,4},{1,5},{2,6},{3,7},{4,0},{5,1},{6,2},{7,3},{8,12},{9,13},{10,... | collective-permute-start | bytes 786440 | tf_op jit(solution)/shard_map/ppermute | solution.py:29
  22.4 20.2 %collective-permute-start.4 = (bf16[256,1024]{1,0:T(8,128)(2,1)S(1)}, bf16[256,1024]{1,0:T(8,128)(2,1)S(1)}, u32[]{:S(2)}, u32[]{:S(2)}) collective-permute-start(bf16[256,1024]{1,0:T(8,128)(2,1)S(1)} %maximum_select_fusion), channel_id=1, source_target_pairs={{0,3},{1,2},{2,1},{3,0},{4,7},{5,6},{6,5},{7,4},{8,11},{9,10},{10,... | collective-permute-start | bytes 1572872 | tf_op jit(solution)/shard_map/ppermute | solution.py:29
  43.0 1.0 copy-start.4
  45.1 95.7 %all-gather.7.cloned.1.call-start = ((), (), s32[]{:S(2)}) async-start(), calls=%async_computation.1 | async-start | bytes 2621440 | tf_op jit(solution)/shard_map/all_gather | solution.py:133
  45.2 14.5 %collective-permute-start.8 = (bf16[256,1024]{1,0:T(8,128)(2,1)S(1)}, bf16[256,1024]{1,0:T(8,128)(2,1)S(1)}, u32[]{:S(2)}, u32[]{:S(2)}) collective-permute-start(bf16[256,1024]{1,0:T(8,128)(2,1)S(1)} %maximum_select_fusion), channel_id=1, source_target_pairs={{0,1},{1,0},{2,3},{3,2},{4,5},{5,4},{6,7},{7,6},{8,9},{9,8},{10,11... | collective-permute-start | bytes 1572872 | tf_op jit(solution)/shard_map/ppermute | solution.py:29
  45.4 21.9 %collective-permute-start.10 = (bf16[128,1024]{1,0:T(8,128)(2,1)S(1)}, bf16[128,1024]{1,0:T(8,128)(2,1)S(1)}, u32[]{:S(2)}, u32[]{:S(2)}) collective-permute-start(bf16[128,1024]{1,0:T(8,128)(2,1)S(1)} %get-tuple-element.42.refs_7_), channel_id=1, source_target_pairs={{0,1},{1,0},{2,3},{3,2},{4,5},{5,4},{6,7},{7,6},{8,9},{9,8},{10,11... | collective-permute-start | bytes 786440 | tf_op jit(solution)/shard_map/ppermute | solution.py:29
  59.7 10.8 %collective-permute-start.9 = (bf16[128,1024]{1,0:T(8,128)(2,1)S(1)}, bf16[128,1024]{1,0:T(8,128)(2,1)S(1)}, u32[]{:S(2)}, u32[]{:S(2)}) collective-permute-start(bf16[128,1024]{1,0:T(8,128)(2,1)S(1)} %get-tuple-element.44.refs_2_), channel_id=1, source_target_pairs={{0,3},{1,2},{2,1},{3,0},{4,7},{5,6},{6,5},{7,4},{8,11},{9,10},{10,... | collective-permute-start | bytes 786440 | tf_op jit(solution)/shard_map/ppermute | solution.py:29
  63.5 3.7 %collective-permute-start.5 = (f32[1,512]{1,0:T(1,128)S(1)}, f32[1,512]{1,0:T(1,128)S(1)}, u32[]{:S(2)}, u32[]{:S(2)}) collective-permute-start(f32[1,512]{1,0:T(1,128)S(1)} %slice.57), channel_id=1, source_target_pairs={{0,4},{1,5},{2,6},{3,7},{4,0},{5,1},{6,2},{7,3},{8,12},{9,13},{10,... | collective-permute-start | bytes 6152 | tf_op jit(solution)/shard_map/ppermute | solution.py:29
  63.9 7.3 %collective-permute-start.6 = (bf16[16,1024]{1,0:T(8,128)(2,1)S(1)}, bf16[16,1024]{1,0:T(8,128)(2,1)S(1)}, u32[]{:S(2)}, u32[]{:S(2)}) collective-permute-start(bf16[16,1024]{1,0:T(8,128)(2,1)S(1)} %convert_element_type.216), channel_id=1, source_target_pairs={{0,20},{1,21},{2,22},{3,23},{4,16},{5,17},{6,18},{7,19},{8,28},{9,... | collective-permute-start | bytes 98312 | tf_op jit(solution)/shard_map/ppermute | solution.py:29
  64.0 7.2 %collective-permute-start.7 = (bf16[16,1024]{1,0:T(8,128)(2,1)S(1)}, bf16[16,1024]{1,0:T(8,128)(2,1)S(1)}, u32[]{:S(2)}, u32[]{:S(2)}) collective-permute-start(bf16[16,1024]{1,0:T(8,128)(2,1)S(1)} %convert_element_type.216), channel_id=1, source_target_pairs={{0,16},{1,17},{2,18},{3,19},{4,20},{5,21},{6,22},{7,23},{8,24},{9,... | collective-permute-start | bytes 98312 | tf_op jit(solution)/shard_map/ppermute | solution.py:29
  71.9 1.3 collective-permute-start.11
  72.5 0.7 collective-permute-start.12
  73.9 3.7 %collective-permute-start.13 = (bf16[16,1024]{1,0:T(8,128)(2,1)S(1)}, bf16[16,1024]{1,0:T(8,128)(2,1)S(1)}, u32[]{:S(2)}, u32[]{:S(2)}) collective-permute-start(bf16[16,1024]{1,0:T(8,128)(2,1)S(1)} %fusion.26), channel_id=1, source_target_pairs={{0,20},{1,21},{2,22},{3,23},{4,16},{5,17},{6,18},{7,19},{8,28},{9,... | collective-permute-start | bytes 98312 | tf_op jit(solution)/shard_map/ppermute | solution.py:29
  73.9 3.7 %collective-permute-start.14 = (bf16[16,1024]{1,0:T(8,128)(2,1)S(1)}, bf16[16,1024]{1,0:T(8,128)(2,1)S(1)}, u32[]{:S(2)}, u32[]{:S(2)}) collective-permute-start(bf16[16,1024]{1,0:T(8,128)(2,1)S(1)} %fusion.26), channel_id=1, source_target_pairs={{0,16},{1,17},{2,18},{3,19},{4,20},{5,21},{6,22},{7,23},{8,24},{9,... | collective-permute-start | bytes 98312 | tf_op jit(solution)/shard_map/ppermute | solution.py:29
  78.2 1.3 collective-permute-start.15
  78.9 0.7 collective-permute-start.16
  80.2 3.3 %collective-permute-start.17 = (bf16[16,1024]{1,0:T(8,128)(2,1)S(1)}, bf16[16,1024]{1,0:T(8,128)(2,1)S(1)}, u32[]{:S(2)}, u32[]{:S(2)}) collective-permute-start(bf16[16,1024]{1,0:T(8,128)(2,1)S(1)} %fusion.28), channel_id=1, source_target_pairs={{0,20},{1,21},{2,22},{3,23},{4,16},{5,17},{6,18},{7,19},{8,28},{9,... | collective-permute-start | bytes 98312 | tf_op jit(solution)/shard_map/ppermute | solution.py:29
  80.7 2.9 %collective-permute-start.18 = (bf16[16,1024]{1,0:T(8,128)(2,1)S(1)}, bf16[16,1024]{1,0:T(8,128)(2,1)S(1)}, u32[]{:S(2)}, u32[]{:S(2)}) collective-permute-start(bf16[16,1024]{1,0:T(8,128)(2,1)S(1)} %fusion.28), channel_id=1, source_target_pairs={{0,16},{1,17},{2,18},{3,19},{4,20},{5,21},{6,22},{7,23},{8,24},{9,... | collective-permute-start | bytes 98312 | tf_op jit(solution)/shard_map/ppermute | solution.py:29
  84.2 1.3 collective-permute-start.19
  84.9 0.7 collective-permute-start.20
  86.2 3.3 %collective-permute-start.21 = (bf16[16,1024]{1,0:T(8,128)(2,1)S(1)}, bf16[16,1024]{1,0:T(8,128)(2,1)S(1)}, u32[]{:S(2)}, u32[]{:S(2)}) collective-permute-start(bf16[16,1024]{1,0:T(8,128)(2,1)S(1)} %fusion.30), channel_id=1, source_target_pairs={{0,20},{1,21},{2,22},{3,23},{4,16},{5,17},{6,18},{7,19},{8,28},{9,... | collective-permute-start | bytes 98312 | tf_op jit(solution)/shard_map/ppermute | solution.py:29
  87.1 2.5 %collective-permute-start.22 = (bf16[16,1024]{1,0:T(8,128)(2,1)S(1)}, bf16[16,1024]{1,0:T(8,128)(2,1)S(1)}, u32[]{:S(2)}, u32[]{:S(2)}) collective-permute-start(bf16[16,1024]{1,0:T(8,128)(2,1)S(1)} %fusion.30), channel_id=1, source_target_pairs={{0,16},{1,17},{2,18},{3,19},{4,20},{5,21},{6,22},{7,23},{8,24},{9,... | collective-permute-start | bytes 98312 | tf_op jit(solution)/shard_map/ppermute | solution.py:29
  90.2 1.3 collective-permute-start.23
  90.9 0.7 collective-permute-start.24
  92.3 3.4 %collective-permute-start.25 = (bf16[16,1024]{1,0:T(8,128)(2,1)S(1)}, bf16[16,1024]{1,0:T(8,128)(2,1)S(1)}, u32[]{:S(2)}, u32[]{:S(2)}) collective-permute-start(bf16[16,1024]{1,0:T(8,128)(2,1)S(1)} %fusion.32), channel_id=1, source_target_pairs={{0,20},{1,21},{2,22},{3,23},{4,16},{5,17},{6,18},{7,19},{8,28},{9,... | collective-permute-start | bytes 98312 | tf_op jit(solution)/shard_map/ppermute | solution.py:29
  93.1 2.5 %collective-permute-start.26 = (bf16[16,1024]{1,0:T(8,128)(2,1)S(1)}, bf16[16,1024]{1,0:T(8,128)(2,1)S(1)}, u32[]{:S(2)}, u32[]{:S(2)}) collective-permute-start(bf16[16,1024]{1,0:T(8,128)(2,1)S(1)} %fusion.32), channel_id=1, source_target_pairs={{0,16},{1,17},{2,18},{3,19},{4,20},{5,21},{6,22},{7,23},{8,24},{9,... | collective-permute-start | bytes 98312 | tf_op jit(solution)/shard_map/ppermute | solution.py:29
  96.3 5.7 %collective-permute-start.27 = (bf16[16,1024]{1,0:T(8,128)(2,1)S(1)}, bf16[16,1024]{1,0:T(8,128)(2,1)S(1)}, u32[]{:S(2)}, u32[]{:S(2)}) collective-permute-start(bf16[16,1024]{1,0:T(8,128)(2,1)S(1)} %fusion.33), channel_id=1, source_target_pairs={{144,172},{145,173},{146,174},{147,175},{148,168},{149,169},{150,1... | collective-permute-start | bytes 98312 | tf_op jit(solution)/shard_map/ppermute | solution.py:29
  96.9 5.1 %collective-permute-start.28 = (bf16[16,1024]{1,0:T(8,128)(2,1)S(1)}, bf16[16,1024]{1,0:T(8,128)(2,1)S(1)}, u32[]{:S(2)}, u32[]{:S(2)}) collective-permute-start(bf16[16,1024]{1,0:T(8,128)(2,1)S(1)} %fusion.33), channel_id=1, source_target_pairs={{144,160},{145,161},{146,162},{147,163},{148,164},{149,165},{150,1... | collective-permute-start | bytes 98312 | tf_op jit(solution)/shard_map/ppermute | solution.py:29
  102.7 3.3 %collective-permute-start.29 = (bf16[16,1024]{1,0:T(8,128)(2,1)S(1)}, bf16[16,1024]{1,0:T(8,128)(2,1)S(1)}, u32[]{:S(2)}, u32[]{:S(2)}) collective-permute-start(bf16[16,1024]{1,0:T(8,128)(2,1)S(1)} %fusion.34), channel_id=1, source_target_pairs={{0,20},{1,21},{2,22},{3,23},{4,16},{5,17},{6,18},{7,19},{8,28},{9,... | collective-permute-start | bytes 98312 | tf_op jit(solution)/shard_map/ppermute | solution.py:29
  103.5 2.5 %collective-permute-start.30 = (bf16[16,1024]{1,0:T(8,128)(2,1)S(1)}, bf16[16,1024]{1,0:T(8,128)(2,1)S(1)}, u32[]{:S(2)}, u32[]{:S(2)}) collective-permute-start(bf16[16,1024]{1,0:T(8,128)(2,1)S(1)} %fusion.34), channel_id=1, source_target_pairs={{0,16},{1,17},{2,18},{3,19},{4,20},{5,21},{6,22},{7,23},{8,24},{9,... | collective-permute-start | bytes 98312 | tf_op jit(solution)/shard_map/ppermute | solution.py:29
  106.7 1.3 collective-permute-start.31
  107.3 0.7 collective-permute-start.32
  108.7 3.4 %collective-permute-start.33 = (bf16[16,1024]{1,0:T(8,128)(2,1)S(1)}, bf16[16,1024]{1,0:T(8,128)(2,1)S(1)}, u32[]{:S(2)}, u32[]{:S(2)}) collective-permute-start(bf16[16,1024]{1,0:T(8,128)(2,1)S(1)} %fusion.36), channel_id=1, source_target_pairs={{0,20},{1,21},{2,22},{3,23},{4,16},{5,17},{6,18},{7,19},{8,28},{9,... | collective-permute-start | bytes 98312 | tf_op jit(solution)/shard_map/ppermute | solution.py:29
  109.5 2.5 %collective-permute-start.34 = (bf16[16,1024]{1,0:T(8,128)(2,1)S(1)}, bf16[16,1024]{1,0:T(8,128)(2,1)S(1)}, u32[]{:S(2)}, u32[]{:S(2)}) collective-permute-start(bf16[16,1024]{1,0:T(8,128)(2,1)S(1)} %fusion.36), channel_id=1, source_target_pairs={{0,16},{1,17},{2,18},{3,19},{4,20},{5,21},{6,22},{7,23},{8,24},{9,... | collective-permute-start | bytes 98312 | tf_op jit(solution)/shard_map/ppermute | solution.py:29
  112.7 16.7 %collective-permute-start.35 = (bf16[16,1024]{1,0:T(8,128)(2,1)S(1)}, bf16[16,1024]{1,0:T(8,128)(2,1)S(1)}, u32[]{:S(2)}, u32[]{:S(2)}) collective-permute-start(bf16[16,1024]{1,0:T(8,128)(2,1)S(1)} %fusion.37), channel_id=1, source_target_pairs={{208,236},{209,237},{210,238},{211,239},{212,232},{213,233},{214,2... | collective-permute-start | bytes 98312 | tf_op jit(solution)/shard_map/ppermute | solution.py:29
  114.0 15.8 %collective-permute-start.36 = (bf16[16,1024]{1,0:T(8,128)(2,1)S(1)}, bf16[16,1024]{1,0:T(8,128)(2,1)S(1)}, u32[]{:S(2)}, u32[]{:S(2)}) collective-permute-start(bf16[16,1024]{1,0:T(8,128)(2,1)S(1)} %fusion.37), channel_id=1, source_target_pairs={{208,224},{209,225},{210,226},{211,227},{212,228},{213,229},{214,2... | collective-permute-start | bytes 98312 | tf_op jit(solution)/shard_map/ppermute | solution.py:29
  130.4 3.5 %collective-permute-start.37 = (bf16[16,1024]{1,0:T(8,128)(2,1)S(1)}, bf16[16,1024]{1,0:T(8,128)(2,1)S(1)}, u32[]{:S(2)}, u32[]{:S(2)}) collective-permute-start(bf16[16,1024]{1,0:T(8,128)(2,1)S(1)} %fusion.38), channel_id=1, source_target_pairs={{0,20},{1,21},{2,22},{3,23},{4,16},{5,17},{6,18},{7,19},{8,28},{9,... | collective-permute-start | bytes 98312 | tf_op jit(solution)/shard_map/ppermute | solution.py:29
  130.4 3.5 %collective-permute-start.38 = (bf16[16,1024]{1,0:T(8,128)(2,1)S(1)}, bf16[16,1024]{1,0:T(8,128)(2,1)S(1)}, u32[]{:S(2)}, u32[]{:S(2)}) collective-permute-start(bf16[16,1024]{1,0:T(8,128)(2,1)S(1)} %fusion.38), channel_id=1, source_target_pairs={{0,16},{1,17},{2,18},{3,19},{4,20},{5,21},{6,22},{7,23},{8,24},{9,... | collective-permute-start | bytes 98312 | tf_op jit(solution)/shard_map/ppermute | solution.py:29
  134.6 4.1 %collective-permute-start.39 = (bf16[16,1024]{1,0:T(8,128)(2,1)S(1)}, bf16[16,1024]{1,0:T(8,128)(2,1)S(1)}, u32[]{:S(2)}, u32[]{:S(2)}) collective-permute-start(bf16[16,1024]{1,0:T(8,128)(2,1)S(1)} %fusion.40), channel_id=1, source_target_pairs={{0,4},{1,5},{2,6},{3,7},{4,0},{5,1},{6,2},{7,3},{8,12},{9,13},{10,... | collective-permute-start | bytes 98312 | tf_op jit(solution)/shard_map/ppermute | solution.py:29
  139.1 5.4 %collective-permute-start.43 = (bf16[16,1536]{1,0:T(8,128)(2,1)S(1)}, bf16[16,1536]{1,0:T(8,128)(2,1)S(1)}, u32[]{:S(2)}, u32[]{:S(2)}) collective-permute-start(bf16[16,1536]{1,0:T(8,128)(2,1)S(1)} %pad_maximum_fusion.7), channel_id=1, source_target_pairs={{0,12},{1,13},{2,14},{3,15},{4,8},{5,9},{6,10},{7,11},{8,4},{9,5},... | collective-permute-start | bytes 147464 | tf_op jit(solution)/shard_map/ppermute | solution.py:29
  144.3 12.1 %copy-start = (f32[1,128,2048]{2,1,0:T(8,128)S(1)}, f32[1,128,2048]{2,1,0:T(8,128)}, u32[]{:S(2)}) copy-start(f32[1,128,2048]{2,1,0:T(8,128)} %param.8) | copy-start | bytes 3145732
  144.4 15.7 %copy-start.2 = (f32[1,128]{1,0:T(1,128)S(1)}, f32[1,128]{1,0:T(1,128)}, u32[]{:S(2)}) copy-start(f32[1,128]{1,0:T(1,128)} %weight.1) | copy-start | bytes 1540
  144.5 5.0 %collective-permute-start.44 = (bf16[16,512]{1,0:T(8,128)(2,1)S(1)}, bf16[16,512]{1,0:T(8,128)(2,1)S(1)}, u32[]{:S(2)}, u32[]{:S(2)}) collective-permute-start(bf16[16,512]{1,0:T(8,128)(2,1)S(1)} %add_convert_fusion.30), channel_id=1, source_target_pairs={{0,240},{1,241},{2,242},{3,243},{4,244},{5,245},{6,246},{7,247},{8... | collective-permute-start | bytes 49160 | tf_op jit(solution)/shard_map/ppermute | solution.py:29
  144.6 9.8 %collective-permute-start.40 = (bf16[128,512]{1,0:T(8,128)(2,1)S(1)}, bf16[128,512]{1,0:T(8,128)(2,1)S(1)}, u32[]{:S(2)}, u32[]{:S(2)}) collective-permute-start(bf16[128,512]{1,0:T(8,128)(2,1)S(1)} %get-tuple-element.39), channel_id=1, source_target_pairs={{0,1},{1,0},{2,3},{3,2},{4,5},{5,4},{6,7},{7,6},{8,9},{9,8},{10,11... | collective-permute-start | bytes 393224 | tf_op jit(solution)/shard_map/ppermute | solution.py:29
  146.6 7.9 %collective-permute-start.41 = (bf16[128,512]{1,0:T(8,128)(2,1)S(1)}, bf16[128,512]{1,0:T(8,128)(2,1)S(1)}, u32[]{:S(2)}, u32[]{:S(2)}) collective-permute-start(bf16[128,512]{1,0:T(8,128)(2,1)S(1)} %get-tuple-element.38), channel_id=1, source_target_pairs={{0,2},{1,3},{2,0},{3,1},{4,6},{5,7},{6,4},{7,5},{8,10},{9,11},{10,... | collective-permute-start | bytes 393224 | tf_op jit(solution)/shard_map/ppermute | solution.py:29
  149.5 6.9 %collective-permute-start.42 = (bf16[128,512]{1,0:T(8,128)(2,1)S(1)}, bf16[128,512]{1,0:T(8,128)(2,1)S(1)}, u32[]{:S(2)}, u32[]{:S(2)}) collective-permute-start(bf16[128,512]{1,0:T(8,128)(2,1)S(1)} %get-tuple-element.37), channel_id=1, source_target_pairs={{0,3},{1,2},{2,1},{3,0},{4,7},{5,6},{6,5},{7,4},{8,11},{9,10},{10,... | collective-permute-start | bytes 393224 | tf_op jit(solution)/shard_map/ppermute | solution.py:29
  149.7 8.6 %collective-permute-start.45 = (bf16[16,2432]{1,0:T(8,128)(2,1)S(1)}, bf16[16,2432]{1,0:T(8,128)(2,1)S(1)}, u32[]{:S(2)}, u32[]{:S(2)}) collective-permute-start(bf16[16,2432]{1,0:T(8,128)(2,1)S(1)} %get-tuple-element.48), channel_id=1, source_target_pairs={{0,1},{1,0},{2,3},{3,2},{4,5},{5,4},{6,7},{7,6},{8,9},{9,8},{10,11... | collective-permute-start | bytes 233480 | tf_op jit(solution)/shard_map/ppermute | solution.py:29
  150.3 7.9 %collective-permute-start.46 = (bf16[16,2432]{1,0:T(8,128)(2,1)S(1)}, bf16[16,2432]{1,0:T(8,128)(2,1)S(1)}, u32[]{:S(2)}, u32[]{:S(2)}) collective-permute-start(bf16[16,2432]{1,0:T(8,128)(2,1)S(1)} %get-tuple-element.49), channel_id=1, source_target_pairs={{0,2},{1,3},{2,0},{3,1},{4,6},{5,7},{6,4},{7,5},{8,10},{9,11},{10,... | collective-permute-start | bytes 233480 | tf_op jit(solution)/shard_map/ppermute | solution.py:29
  154.4 5.6 %collective-permute-start.47 = (bf16[16,2432]{1,0:T(8,128)(2,1)S(1)}, bf16[16,2432]{1,0:T(8,128)(2,1)S(1)}, u32[]{:S(2)}, u32[]{:S(2)}) collective-permute-start(bf16[16,2432]{1,0:T(8,128)(2,1)S(1)} %get-tuple-element.47), channel_id=1, source_target_pairs={{0,3},{1,2},{2,1},{3,0},{4,7},{5,6},{6,5},{7,4},{8,11},{9,10},{10,... | collective-permute-start | bytes 233480 | tf_op jit(solution)/shard_map/ppermute | solution.py:29
Sparse Core Ops, SparseCore 0:
  9.8 27.9 all-gather.8
  45.2 39.0 all-gather.4
  102.1 38.5 all-gather.6
